TPU v7x, 32 devices: a whole 2x2x4 slice. The times are simulated.
32 devices in a mesh: rows: 2 (over core), cols: 4 (over y, x), grp: 4 (over z).
Axes of the slice: x: 2, y: 2, z: 4, core: 2. Of those that a mesh axis runs over, the one named last changes fastest.
Arguments:
- inputs: bfloat16 [8, 32, 128, 256], P('grp', 'rows', 'cols'), may hold values from -6 to 6
- w_first: bfloat16 [3, 3, 256, 512], replicated, may hold values from -0.125 to 0.125
- gain_first: float32 [512], replicated, may hold values from 0.4 to 1.6
- shift_first: float32 [512], replicated, may hold values from -3 to 3
- w_second: bfloat16 [3, 3, 512, 512], replicated, may hold values from -0.09375 to 0.09375
- gain_second: float32 [512], replicated, may hold values from 0.4 to 1.6
- shift_second: float32 [512], replicated, may hold values from -3 to 3
- w_proj: bfloat16 [256, 512], replicated, may hold values from -0.375 to 0.375
- gain_proj: float32 [512], replicated, may hold values from 0.4 to 1.6
- shift_proj: float32 [512], replicated, may hold values from -3 to 3
- valid_mask: int32 [8, 16, 64], P('grp', 'rows', 'cols'), may hold values from 0 to 1, as said below
- cotangent: bfloat16 [8, 16, 64, 512], P('grp', 'rows', 'cols'), may hold values from -6 to 6
Outputs:
- block_out: bfloat16 [8, 16, 64, 512], P('grp', 'rows', 'cols')
- grad_inputs: bfloat16 [8, 32, 128, 256], P('grp', 'rows', 'cols')
- grad_w_first: float32 [3, 3, 256, 512], replicated
- grad_gain_first: float32 [512], replicated
- grad_shift_first: float32 [512], replicated
- grad_w_second: float32 [3, 3, 512, 512], replicated
- grad_gain_second: float32 [512], replicated
- grad_shift_second: float32 [512], replicated
- grad_w_proj: float32 [256, 512], replicated
- grad_gain_proj: float32 [512], replicated
- grad_shift_proj: float32 [512], replicated
Inputs may be any that keep to these rules, and one draw needn't show every extreme that they name: `valid_mask`: 1 exactly on square tiles of 7 by 7 pixels on a grid of pitch 8 in groups of even index and of 3 by 3 pixels on a grid of pitch 4 in groups of odd index, the grid offset per group and each tile present or absent; group 0 has all its tiles.
All inputs are finite; a program needn't handle non-finite values.
Results may differ from a plain program's by a relative error of at most 0.006.
Values may be sent and summed in bfloat16 or wider, within the bound.
No kernel may reach another device: no remote copies, remote signals or barrier semaphores. Data moves between devices by JAX's collectives and lax.ppermute only.
A program may use at most 128 MiB of HBM per device.

v0:
```python
import functools

import jax
import jax.numpy as jnp
from jax import lax
from jax.experimental import pallas as pl
from jax.experimental.pallas import tpu as pltpu
from jax.sharding import PartitionSpec as P

epsilon = 1e-05
axes = ("rows", "cols", "grp")
bf16 = jnp.bfloat16
f32 = jnp.float32
inner = 0.7978845608028654
cubic = 0.044715
over = 6
rim = 3


class Refs:
    def __init__(self, named):
        self.__dict__.update(named)


class Copies:
    def __init__(self, names, sources, targets, sems):
        self.jobs = {n: pltpu.make_async_copy(s, t, sems.at[k]) for k, (n, s, t) in enumerate(zip(names, sources, targets))}

    def start(self, *names):
        for name in names:
            self.jobs[name].start()

    def wait(self, *names):
        for name in names:
            self.jobs[name].wait()


def call(body, ins, outs, scratch=None, far_in=(), far_out=(), smem=(), flops=0, moved=0, limit=52):
    scratch = scratch or {}
    far = (*far_in, *far_out)

    def spec(name):
        if name in smem:
            return pl.BlockSpec(memory_space=pltpu.SMEM)
        return pl.BlockSpec(memory_space=pltpu.HBM if name in far else pltpu.VMEM)

    kinds = {**{n: shape(v.shape, v.dtype) for n, v in ins.items()}, **outs}
    names = [*ins, *outs, *far, *scratch]

    def run(*refs):
        given = dict(zip(names, refs)) if not far else None
        if far:
            plain = dict(zip([*ins, *outs], refs))
            rest = refs[len(plain) :]
            buffers = dict(zip(far, rest))
            more = dict(zip(scratch, rest[len(far) : -1]))
            given = {**plain, **buffers, **more}
            sources = [plain[n] if n in far_in else buffers[n] for n in far]
            targets = [buffers[n] if n in far_in else plain[n] for n in far]
            copies = Copies(far, sources, targets, rest[-1])
            copies.start(*far_in)
        else:
            copies = None
        body(Refs(given), copies)

    buffers = [pltpu.VMEM(kinds[n].shape, kinds[n].dtype) for n in far]
    sems = [pltpu.SemaphoreType.DMA((len(far),))] if far else []
    result = pl.pallas_call(
        run,
        out_shape=list(outs.values()),
        in_specs=[spec(n) for n in ins],
        out_specs=[spec(n) for n in outs],
        scratch_shapes=[*buffers, *scratch.values(), *sems],
        compiler_params=pltpu.CompilerParams(vmem_limit_bytes=limit * 1024 * 1024),
        cost_estimate=pl.CostEstimate(flops=0, bytes_accessed=0, transcendentals=0),
    )(*ins.values())
    return dict(zip(outs, result))


def shape(dims, dtype=f32):
    return jax.ShapeDtypeStruct(dims, dtype)


def wide(mask, width):
    return jnp.concatenate([mask] * (width // mask.shape[1]), axis=1)


def matmul(a, b):
    return lax.dot_general(a, b, (((1,), (0,)), ((), ())), preferred_element_type=f32)


def matmul_nt(a, b):
    return lax.dot_general(a, b, (((1,), (1,)), ((), ())), preferred_element_type=f32)


def matmul_tn(a, b):
    return lax.dot_general(a, b, (((0,), (0,)), ((), ())), preferred_element_type=f32)


def gelu_parts(v):
    return jnp.tanh(inner * (v + cubic * v * v * v))


def gelu_slope(v, t):
    return 0.5 * (1.0 + t) + 0.5 * v * (1.0 - t * t) * (inner * (1.0 + 3.0 * cubic * v * v))


def column_sum(v):
    return jnp.sum(v, axis=0, keepdims=True)


def moments(total, squares, pixel_count):
    center = total / pixel_count
    spread = squares / pixel_count - center * center
    return center, lax.rsqrt(spread + epsilon)


def chunks(total, size):
    return [(at, min(size, total - at)) for at in range(0, total, size)]


def assemble(raw, flags, own, top, bot, left, right, first, last, put):
    n_top, n_own, groups = own.n_top, own.n_own, own.groups
    for r in range(first, last):
        for g in range(groups):
            if r < n_top:
                src = jnp.where(flags[0] == 1, top(g, r).astype(f32), 0.0)
            elif r < n_top + n_own:
                src = own(g, r - n_top).astype(f32)
            else:
                src = jnp.where(flags[1] == 1, bot(g, r - n_top - n_own).astype(f32), 0.0)
            line = (r - first) * groups + g
            sides = left(g, r).astype(f32), right(g, r).astype(f32)
            edge, cols = sides[0].shape[0], src.shape[0]
            pieces = ((0, sides[0]), (edge, src), (edge + cols, sides[1]))
            for at, value in pieces:
                for k in range(raw.shape[0]):
                    step = raw.shape[3]
                    raw[k, line, at : at + value.shape[0], :] = value[:, k * step : (k + 1) * step]
            put(r, g, line)


class Rows:
    def __init__(self, read, groups, n_top, n_own):
        self.read, self.groups, self.n_top, self.n_own = read, groups, n_top, n_own

    def __call__(self, g, r):
        return self.read(g, r)


def flat_row(ref, base, n, cols):
    return lambda g, r: ref[base + (g * n + r) * cols : base + (g * n + r + 1) * cols, :]


def flat_pair(ref, base, n, cols, size):
    low, high = flat_row(ref, base, n, cols), flat_row(ref, base + size, n, cols)
    return lambda g, r: jnp.concatenate([low(g, r), high(g, r)], axis=1)


def stats_kernel(r, copies):
    groups, cin = r.x.shape[0], r.x.shape[3]
    rows, S = r.own.shape[1], r.own.shape[2]
    L = groups * S
    width = r.w1.shape[2]
    raw = r.raw
    for n in range(2 * rows + 1):
        for g in range(groups):
            line = n * groups + g
            src = (r.top[g, 0] if n == 0 else r.x[g, n - 1]).astype(f32)
            side = r.lft[g, n].astype(f32)
            for k in range(raw.shape[0]):
                raw[k, line, 7:8, :] = side[:, k * 128 : (k + 1) * 128]
                raw[k, line, 8:, :] = src[:, k * 128 : (k + 1) * 128]
    for out, n_rows, start in ((r.xe, rows, 1), (r.xo, rows + 1, 0)):
        for n in range(n_rows):
            for b in range(3):
                for k in range(raw.shape[0]):
                    parts = [
                        raw[k, (2 * n + start) * groups + g, pl.ds(7 + b, S, stride=2), :]
                        for g in range(groups)
                    ]
                    at = b * cin + k * 128
                    out[n * L : (n + 1) * L, at : at + 128] = jnp.concatenate(
                        parts, axis=0
                    ).astype(bf16)
    mask = jnp.concatenate(
        [r.own[g, i].astype(f32) for i in range(rows) for g in range(groups)], axis=0
    )
    M = rows * L
    z = matmul(r.xo[0:M, :], r.w1[0])
    z += matmul(r.xe[...], r.w1[1])
    z += matmul(r.xo[L : L + M, :], r.w1[2])
    zp = matmul(r.xe[:, cin : 2 * cin], r.wp[...])
    zm, zpm = z * wide(mask, width), zp * wide(mask, width)
    row = jnp.concatenate([column_sum(zm), column_sum(zm * z), column_sum(mask)], axis=1)
    r.spread[...] = jnp.broadcast_to(row[None], r.spread.shape)
    r.psum[...] = jnp.concatenate([column_sum(zpm), column_sum(zpm * zp)], axis=1)


def first_kernel(r, copies):
    groups, cin = r.x.shape[0], r.x.shape[3]
    rows, cols = r.own.shape[1], r.own.shape[2]
    S = cols + 8
    L = groups * S
    raw = r.raw
    end = 16 + r.x.shape[2]
    total_rows = r.x.shape[1] + 2 * over

    def put(n, g, line):
        for k in range(raw.shape[0]):
            raw[k, line, end:, :] = jnp.zeros((raw.shape[2] - end, 128), f32)

    assemble(
        raw,
        r.flags,
        Rows(lambda g, n: r.x[g, n], groups, over, r.x.shape[1]),
        flat_row(r.top, 0, over, r.x.shape[2]),
        flat_row(r.bot, 0, over, r.x.shape[2]),
        lambda g, n: r.lft[g, n],
        lambda g, n: r.rgt[g, n],
        0,
        total_rows,
        put,
    )
    for out, n_rows, start in ((r.xe, rows + 5, 2), (r.xo, rows + 6, 1)):
        for n in range(n_rows):
            for b in range(3):
                for k in range(raw.shape[0]):
                    parts = [
                        raw[k, (2 * n + start) * groups + g, pl.ds(3 + b, S, stride=2), :]
                        for g in range(groups)
                    ]
                    at = b * cin + k * 128
                    out[n * L : (n + 1) * L, at : at + 128] = jnp.concatenate(
                        parts, axis=0
                    ).astype(bf16)
    copies.start("xe", "xo")
    r.ownp[...] = jnp.zeros(r.ownp.shape, f32)
    for i in range(rows):
        for g in range(groups):
            at = (i + 2) * L + g * S + 2
            r.ownp[at : at + cols, :] = r.own[g, i].astype(f32)
    copies.wait("w1", "wp")
    for m0, m in chunks(r.pre1.shape[0], 208):
        z = matmul(r.xo[m0 : m0 + m, :], r.w1[0])
        z += matmul(r.xe[m0 : m0 + m, :], r.w1[1])
        z += matmul(r.xo[L + m0 : L + m0 + m, :], r.w1[2])
        r.pre1[m0 : m0 + m, :] = z
        r.prep[m0 : m0 + m, :] = matmul(r.xe[m0 : m0 + m, cin : 2 * cin], r.wp[...])
        r.keep[m0 : m0 + m, :] = z
    copies.start("keep")
    copies.wait("xe", "xo", "keep")


def rims_kernel(r, copies):
    groups, rows, cols, width = r.cot.shape
    S = cols + 8
    L = groups * S
    base, size = over * groups * 2 * cols, rim * groups * cols
    lanes = slice(width, width + 128)

    def put(n, g, line):
        at = (n - 1) * L + g * S
        r.maskp[at : at + S, :] = r.raw[0, line, 6 : 6 + S, :]

    assemble(
        r.raw,
        r.flags,
        Rows(lambda g, n: r.own[g, n], groups, rim, rows),
        lambda g, n: flat_row(r.top, base + width // 256 * size, rim, cols)(g, n)[:, :128],
        lambda g, n: flat_row(r.bot, base + width // 256 * size, rim, cols)(g, n)[:, :128],
        lambda g, n: r.lft[g, n][:, lanes],
        lambda g, n: r.rgt[g, n][:, lanes],
        1,
        rows + 6,
        put,
    )

    def put_cot(n, g, line):
        at = (n - 2) * L + g * S
        r.cotq[at : at + S, :] = r.field[0, line, 7 : 7 + S, :]

    assemble(
        r.field,
        r.flags,
        Rows(lambda g, n: r.cot[g, n], groups, rim, rows),
        flat_pair(r.top, base, rim, cols, size),
        flat_pair(r.bot, base, rim, cols, size),
        lambda g, n: r.lft[g, n][:, :width],
        lambda g, n: r.rgt[g, n][:, :width],
        2,
        rows + 5,
        put_cot,
    )
    copies.start("cotq")
    copies.wait("cotq")


def second_kernel(r, copies):
    width = r.gain.shape[1]
    t = jnp.sum(r.tot1[...], axis=0)
    n = wide(t[:, 2 * width :], width)
    center, inv = moments(t[:, :width], t[:, width : 2 * width], n)
    r.mom1[...] = jnp.concatenate([center, inv, n, jnp.zeros((5, width), f32)], axis=0)
    scale = inv * r.gain[...]
    M, Q = r.pre1.shape[0], r.pre2.shape[0]
    L = (M - Q) // 2
    for m0, m in chunks(M, 104):
        v = (r.pre1[m0 : m0 + m, :] - center) * scale + r.shift[...]
        mask = wide(r.maskp[m0 : m0 + m, :], width)
        r.hid[m0 : m0 + m, :] = 0.5 * v * (1.0 + gelu_parts(v)) * mask
    r.hid[M:, :] = jnp.zeros((r.hid.shape[0] - M, width), f32)
    for m0, m in chunks(M, 208):
        for b in range(3):
            r.h3[m0 : m0 + m, b * width : (b + 1) * width] = r.hid[m0 + b : m0 + b + m, :].astype(bf16)
    copies.start("h3")
    copies.wait("w2")
    sums = [jnp.zeros((1, width), f32)] * 2
    for m0, m in chunks(Q, 176):
        z = matmul(r.h3[m0 : m0 + m, :], r.w2[0])
        z += matmul(r.h3[L + m0 : L + m0 + m, :], r.w2[1])
        z += matmul(r.h3[2 * L + m0 : 2 * L + m0 + m, :], r.w2[2])
        r.pre2[m0 : m0 + m, :] = z
        zm = z * wide(r.ownp[L + 1 + m0 : L + 1 + m0 + m, :], width)
        sums = [sums[0] + column_sum(zm), sums[1] + column_sum(zm * z)]
    row = jnp.concatenate([*sums, r.psum[...]], axis=1)
    r.spread[...] = jnp.broadcast_to(row[None], r.spread.shape)
    copies.wait("h3")


def third_kernel(r, copies):
    groups, rows, cols, width = r.out.shape
    S = cols + 8
    L = groups * S
    n = r.mom1[2:3, :]
    t = jnp.sum(r.tot2[...], axis=0)
    parts = [t[:, k * width : (k + 1) * width] for k in range(4)]
    (c2, i2), (cp, ip) = moments(parts[0], parts[1], n), moments(parts[2], parts[3], n)
    r.mom2[...] = jnp.concatenate([c2, i2, cp, ip, jnp.zeros((4, width), f32)], axis=0)
    sums = [jnp.zeros((1, width), f32)] * 3
    both_shift = r.shift2[...] + r.shiftp[...]
    copies.wait("cotq")
    for line in range(r.grad.shape[0] // S):
        at = line * S
        shifted = slice(L + 1 + at, L + 1 + at + S)
        n2 = (r.pre2[at : at + S, :] - c2) * i2
        np_ = (r.prep[shifted, :] - cp) * ip
        v = n2 * r.gain2[...] + np_ * r.gainp[...] + both_shift
        mask = wide(r.maskp[shifted, :], width)
        own = wide(r.ownp[shifted, :], width)
        t = gelu_parts(v)
        r.field[at : at + S, :] = 0.5 * v * (1.0 + t) * mask
        g = gelu_slope(v, t) * mask * r.cotq[at : at + S, :]
        r.grad[at : at + S, :] = g
        g = g * own
        new = [column_sum(g * n2), column_sum(g), column_sum(g * np_)]
        sums = [a + b for a, b in zip(sums, new)]
    copies.start("grad")
    for i in range(rows):
        for g in range(groups):
            at = (i + 1) * L + g * S + 1
            r.out[g, i, :, :] = r.field[at : at + cols, :].astype(bf16)
    copies.start("out")
    row = jnp.concatenate(sums, axis=1)
    r.spread[...] = jnp.broadcast_to(row[None], r.spread.shape)
    copies.wait("grad", "out")


def halves(r, source, at, frame, to, rows_w):
    half = r.mine.shape[1]
    bit = r.bits[0] == 1
    for m0, m in chunks(rows_w, 96):
        own = wide(r.ownp[frame + m0 : frame + m0 + m, :], half)
        low = (source[at + m0 : at + m0 + m, :half] * own).astype(bf16)
        high = (source[at + m0 : at + m0 + m, half:] * own).astype(bf16)
        r.mine[to + m0 : to + m0 + m, :] = jnp.where(bit, high, low)
        r.theirs[to + m0 : to + m0 + m, :] = jnp.where(bit, low, high)


def fourth_kernel(r, copies):
    width = r.gain2.shape[1]
    Q = r.pre2.shape[0]
    rows_w = r.gpu.shape[0]
    L = (Q - rows_w) // 3
    n = r.mom1[2:3, :]
    c2, i2, cp, ip = (r.mom2[k : k + 1, :] for k in range(4))
    t3 = jnp.sum(r.tot3[...], axis=0)
    r.sums[...] = t3
    gg2, gs, ggp = (t3[:, k * width : (k + 1) * width] for k in range(3))
    copies.wait("grad")
    for m0, m in chunks(Q, L):
        shifted = slice(L + 1 + m0, L + 1 + m0 + m)
        mask = wide(r.maskp[shifted, :], width) / n
        n2 = (r.pre2[m0 : m0 + m, :] - c2) * i2
        np_ = (r.prep[shifted, :] - cp) * ip
        g = r.grad[m0 : m0 + m, :]
        r.gq[m0 : m0 + m, :] = (r.gain2[...] * i2) * (g - mask * (gs + n2 * gg2))
        r.gpq[m0 : m0 + m, :] = (r.gainp[...] * ip) * (g - mask * (gs + np_ * ggp))
    r.gq[Q:, :] = jnp.zeros((r.gq.shape[0] - Q, width), f32)
    for m0, m in chunks(rows_w, 96):
        r.gpu[m0 : m0 + m, :] = r.gpq[L + 1 + m0 : L + 1 + m0 + m, :].astype(bf16)
    copies.start("gpu")
    halves(r, r.gq, L, 2 * L + 1, 0, rows_w)
    halves(r, r.gpq, L - 1, 2 * L, rows_w, rows_w)
    copies.wait("gpu")


def hidden_kernel(r, copies):
    width = r.gain.shape[1]
    Q = r.gq.shape[0] - 8
    L = (r.keep.shape[0] - Q) // 2
    center, inv = r.mom1[0:1, :], r.mom1[1:2, :]
    for m0, m in chunks(Q, 176):
        for b in range(3):
            r.g3[m0 : m0 + m, b * width : (b + 1) * width] = r.gq[m0 + b : m0 + b + m, :].astype(bf16)
    copies.wait("w2")
    U = r.act.shape[0]
    for m0, m in chunks(U, 144):
        gh = jnp.zeros((m, width), f32)
        for a in range(3):
            for b in range(3):
                gh += matmul_nt(
                    r.g3[L * a + m0 : L * a + m0 + m, b * width : (b + 1) * width],
                    r.w2[2 - a, (2 - b) * width : (3 - b) * width, :],
                )
        r.act[m0 : m0 + m, :] = gh
    copies.wait("keep")
    sums = [jnp.zeros((1, width), f32)] * 2
    for m0, m in chunks(U, L):
        frame = slice(2 * L + 2 + m0, 2 * L + 2 + m0 + m)
        n1 = (r.keep[frame, :] - center) * inv
        v = n1 * r.gain[...] + r.shift[...]
        mask = wide(r.maskp[frame, :], width)
        g = gelu_slope(v, gelu_parts(v)) * mask * r.act[m0 : m0 + m, :]
        r.act[m0 : m0 + m, :] = g
        r.normed[m0 : m0 + m, :] = n1 * mask
        g = g * wide(r.ownp[frame, :], width)
        sums = [sums[0] + column_sum(g * n1), sums[1] + column_sum(g)]
    row = jnp.concatenate(sums, axis=1)
    r.spread[...] = jnp.broadcast_to(row[None], r.spread.shape)


def split_store(bits, acc, rows, unit, sent_a, kept_a, sent_b, kept_b):
    quarter = unit // 4
    for k in range(rows // unit):
        for bit, base, sent, kept in ((1, 0, sent_a, kept_a), (2, 2 * quarter, sent_b, kept_b)):
            keep = pl.multiple_of(k * unit + base + bits[bit] * quarter, quarter)
            send = pl.multiple_of(k * unit + base + (1 - bits[bit]) * quarter, quarter)
            yield k, acc[pl.ds(send, quarter), :].astype(bf16), acc[pl.ds(keep, quarter), :], sent, kept


def weights_second_kernel(r, copies):
    width = r.h3.shape[1] // 3
    cin = r.xe.shape[1] // 3
    rows_w = r.near.shape[0] // 2
    L = (r.h3.shape[0] - rows_w) // 5
    per = 3 * width // cin
    places = r.sent_a, r.kept_a, r.sent_b, r.kept_b
    copies.wait("h3", "h3_far")
    for a in range(3):
        at = L * a + L
        for b in range(3):
            lanes = slice(b * width, (b + 1) * width)
            r.acc[lanes, :] = matmul_tn(r.h3[at : at + rows_w, lanes], r.near[:rows_w, :]) + matmul_tn(
                r.h3_far[at : at + rows_w, lanes], r.far[:rows_w, :]
            )
        for k, s, v, sent, kept in split_store(r.bits, r.acc, 3 * width, cin, *places):
            sent[a * per + k] = s
            kept[a * per + k] = v
    at = 2 * L
    copies.wait("xe", "xe_far")
    r.acc[0:cin, :] = matmul_tn(r.xe[at : at + rows_w, cin : 2 * cin], r.near[rows_w:, :]) + matmul_tn(
        r.xe_far[at : at + rows_w, cin : 2 * cin], r.far[rows_w:, :]
    )
    for k, s, v, sent, kept in split_store(r.bits, r.acc, cin, cin, *places):
        sent[3 * per] = s
        kept[3 * per] = v
    copies.start("kept_a", "kept_b")
    copies.wait("kept_a", "kept_b")


def fifth_kernel(r, copies):
    width = r.gain.shape[1]
    U = r.act.shape[0]
    rows_w = r.mine.shape[0]
    L = U - rows_w
    inv, n = r.mom1[1:2, :], r.mom1[2:3, :]
    t4 = jnp.sum(r.tot4[...], axis=0)
    r.sums[...] = t4
    gg, gs = t4[:, :width] / n, t4[:, width:] / n
    scale = r.gain[...] * inv
    r.gf[0:8, :] = jnp.zeros((8, width), f32)
    r.gf[8 + U :, :] = jnp.zeros((r.gf.shape[0] - 8 - U, width), f32)
    for m0, m in chunks(U, L):
        mask = wide(r.maskp[2 * L + 2 + m0 : 2 * L + 2 + m0 + m, :], width)
        back = mask * gs + r.normed[m0 : m0 + m, :] * gg
        r.gf[8 + m0 : 8 + m0 + m, :] = scale * (r.act[m0 : m0 + m, :] - back)
    halves(r, r.gf, 6, 2 * L, 0, rows_w)
    for m0, m in chunks(U, 144):
        r.gu[m0 : m0 + m, :width] = r.gf[8 + m0 : 8 + m0 + m, :].astype(bf16)
        r.gu[m0 : m0 + m, width:] = r.gf[9 + m0 : 9 + m0 + m, :].astype(bf16)
    copies.start("gu")
    copies.wait("gu")


def weights_first_kernel(r, copies):
    rows_w = r.near.shape[0]
    cin = r.xe.shape[1] // 3
    L = (r.xe.shape[0] - rows_w) // 5
    places = r.sent_a, r.kept_a, r.sent_b, r.kept_b
    copies.wait("xe", "xo", "xe_far", "xo_far")
    for a in range(3):
        source, source_far = (r.xe, r.xe_far) if a == 1 else (r.xo, r.xo_far)
        at = (3 if a == 2 else 2) * L
        r.acc[...] = matmul_tn(source[at : at + rows_w, :], r.near[...]) + matmul_tn(
            source_far[at : at + rows_w, :], r.far[...]
        )
        for k, s, v, sent, kept in split_store(r.bits, r.acc, 3 * cin, cin, *places):
            sent[a * 3 + k] = s
            kept[a * 3 + k] = v
    copies.start("kept_a", "kept_b")
    copies.wait("kept_a", "kept_b")


def inputs_kernel(r, copies):
    width = r.gpu.shape[1]
    groups, rows, cols = r.out.shape[0], r.out.shape[1] // 2, r.out.shape[2] // 2
    cin = r.out.shape[3]
    M = r.gpu.shape[0]
    S = cols + 8
    L = groups * S
    lines = r.lines
    copies.wait("gu", "gpu", "w1", "wp")

    def tap(m0, m, a, b):
        di, dj = (1 if a == 0 else 0), (1 if b == 0 else 0)
        return matmul_nt(
            r.gu[di * L + m0 : di * L + m0 + m, dj * width : (dj + 1) * width],
            r.w1[a, b * cin : (b + 1) * cin, :],
        )

    for m0, m in chunks(M, 2 * L):
        pieces = {
            (0, 0): tap(m0, m, 1, 1) + matmul_nt(r.gpu[m0 : m0 + m, :], r.wp[...]),
            (0, 1): tap(m0, m, 1, 2) + tap(m0, m, 1, 0),
            (1, 0): tap(m0, m, 2, 1) + tap(m0, m, 0, 1),
            (1, 1): tap(m0, m, 2, 2) + tap(m0, m, 2, 0) + tap(m0, m, 0, 2) + tap(m0, m, 0, 0),
        }
        for (ro, co), v in pieces.items():
            for k in range(m // S):
                line = m0 // S + k
                i, g = line // groups, line % groups
                for h in range(lines.shape[0]):
                    lines[h, (2 * i + ro) * groups + g, pl.ds(co, cols, stride=2), :] = v[
                        k * S : k * S + cols, h * 128 : (h + 1) * 128
                    ]
    for n in range(2 * rows):
        for g in range(groups):
            for h in range(lines.shape[0]):
                r.out[g, n, :, h * 128 : (h + 1) * 128] = lines[h, n * groups + g].astype(bf16)
    copies.start("out")
    copies.wait("out")


def widen_kernel(bits, half, *refs):
    refs[-1][...] = half[...].astype(f32)


def widen(half, side, taps, into=None):
    n, m = half.shape[1], half.shape[2]
    step = 3 if taps % 3 == 0 else 1
    block = pl.BlockSpec((step, n, m), lambda t, side: (t, 0, 0))
    placed = pl.BlockSpec((step, n, m), lambda t, side: (t, 0, side[0]))
    more = [] if into is None else [into]
    return pl.pallas_call(
        widen_kernel,
        out_shape=shape((taps, n, 2 * m)),
        grid_spec=pltpu.PrefetchScalarGridSpec(
            num_scalar_prefetch=1,
            grid=(taps // step,),
            in_specs=[block] + [pl.BlockSpec(memory_space=pl.ANY)] * len(more),
            out_specs=placed,
        ),
        input_output_aliases={2: 0} if more else {},
        compiler_params=pltpu.CompilerParams(vmem_limit_bytes=20 * 1024 * 1024),
        cost_estimate=pl.CostEstimate(flops=0, bytes_accessed=taps * n * m * 6, transcendentals=0),
    )(side.reshape(1), half, *more)


def shifted(value, axis, steps):
    count = lax.axis_size(axis)
    first, last = (max(0, -steps), min(count, count - steps))
    return lax.ppermute(value, axis, [(source, source + steps) for source in range(first, last)])


def vertical(cells, cot, own):
    width = cot.shape[3]
    count = lax.axis_size("rows")
    me = lax.axis_index("rows")
    mask = jnp.concatenate([own, own], axis=3)

    def packed(ends):
        parts = [cells[:, ends(over)], *(cot[:, ends(rim), :, k : k + 256] for k in range(0, width, 256)), mask[:, ends(rim)]]
        return jnp.concatenate([part.reshape(-1, 256) for part in parts], axis=0)

    down, up = packed(lambda n: slice(-n, None)), packed(lambda n: slice(0, n))
    flags = jnp.stack([me > 0, me < count - 1]).astype(jnp.int32)
    if count == 2:
        swapped = lax.ppermute(jnp.where(me == 0, down, up), "rows", [(0, 1), (1, 0)])
        return swapped, swapped, flags
    return shifted(down, "rows", 1), shifted(up, "rows", -1), flags


def horizontal(top, mid, bot, flags, edge):
    top = jnp.where(flags[0] == 1, top, jnp.zeros_like(top))
    bot = jnp.where(flags[1] == 1, bot, jnp.zeros_like(bot))
    ends = [
        jnp.concatenate([part[:, :, at] for part in (top, mid, bot)], axis=1)
        for at in (slice(-edge, None), slice(0, edge))
    ]
    return shifted(ends[0], "cols", 1), shifted(ends[1], "cols", -1)


def gather_sum(spread):
    return lax.all_to_all(spread, axes, 0, 0)


def bit_of(axis, step):
    return (lax.axis_index(axis) // step) % 2


def partner(value, axis, step):
    count = lax.axis_size(axis)
    return lax.ppermute(value, axis, [(i, i ^ step) for i in range(count)])


def steps_of(axis):
    count, step, out = lax.axis_size(axis), 1, []
    while step < count:
        out.append((axis, step))
        step *= 2
    return out


def split(total, axis, step):
    n = total.shape[1] // 2
    bit = bit_of(axis, step) == 1
    low, high = total[:, :n], total[:, n:]
    return jnp.where(bit, low, high).astype(bf16), jnp.where(bit, high, low)


def join(value, axis, step, dim=1):
    other = partner(value, axis, step)
    bit = bit_of(axis, step) == 1
    return jnp.concatenate([jnp.where(bit, other, value), jnp.where(bit, value, other)], axis=dim)


class Tree:
    def __init__(self, parts, plane, rest):
        self.sent_a, self.kept_a, self.sent_b, self.kept_b = parts
        self.a, self.b = plane, plane[::-1]
        self.rest = []
        for axis in dict.fromkeys(axis for axis, _ in rest):
            steps = [step for name, step in rest if name == axis]
            self.rest += [(axis, steps[k : k + 2]) for k in range(0, len(steps), 2)]
        self.at = 0

    def start(self):
        self.got = partner(self.sent_a, *self.a[self.at]), partner(self.sent_b, *self.b[self.at])

    def finish(self, before=None):
        total_a = self.kept_a + self.got[0].astype(f32)
        total_b = self.kept_b + self.got[1].astype(f32)
        self.at += 1
        if self.at < len(self.a):
            self.sent_a, self.kept_a = split(total_a, *self.a[self.at])
            self.sent_b, self.kept_b = split(total_b, *self.b[self.at])
            keep = [self.sent_a, self.kept_a, self.sent_b, self.kept_b]
            if before is not None:
                before, *keep = lax.optimization_barrier((before, *keep))
            self.sent_a, self.kept_a, self.sent_b, self.kept_b = keep
        else:
            self.taps = total_a.shape[0]
            self.value = jnp.concatenate([total_a, total_b], axis=0).astype(bf16)
            if before is not None:
                before, self.value = lax.optimization_barrier((before, self.value))
        return before

    def exchange(self, k, part=slice(None)):
        axis, steps = self.rest[k]
        got = [] if part.start is None or part.start == 0 else self.got
        self.got = got + [partner(self.value, axis, m * steps[0]) for m in range(1, 2 ** len(steps))[part]]

    def gathered(self):
        parts = [v.astype(f32) for v in (self.value, *self.got)]
        while len(parts) > 1:
            parts = [parts[k] + parts[k + 1] for k in range(0, len(parts), 2)]
        self.value = parts[0].astype(bf16)

    def join(self):
        a, b = self.value[: self.taps], self.value[self.taps :]
        for at in reversed(range(len(self.a))):
            a, b = join(a, *self.a[at]), join(b, *self.b[at])
        return jnp.concatenate([a, b], axis=1)

    def rest_from(self, k):
        for k in range(k, len(self.rest)):
            self.exchange(k)
            self.gathered()


def on_device(inputs, w_first, gain_first, shift_first, w_second, gain_second, shift_second, w_proj, gain_proj, shift_proj, valid_mask, cotangent):
    groups, rows_in, cols_in, cin = inputs.shape
    rows, cols = rows_in // 2, cols_in // 2
    width = w_first.shape[3]
    half = width // 2
    S = cols + 8
    L = groups * S
    devices = lax.axis_size("rows") * lax.axis_size("cols") * lax.axis_size("grp")
    plane = steps_of("cols")
    core = steps_of("rows")[0]
    rest = steps_of("rows")[1:] + steps_of("grp")
    bits = jnp.stack([bit_of(*core), bit_of(*plane[0]), bit_of(*plane[-1])]).astype(jnp.int32)
    w1 = w_first.reshape(3, 3 * cin, width)
    w2 = w_second.reshape(3, 3 * width, width)
    as_row = lambda v: v.reshape(1, -1)
    own = jnp.broadcast_to(valid_mask.astype(bf16)[..., None], valid_mask.shape + (128,))
    MP, MQ, MU, MW = (rows + 5) * L, (rows + 3) * L, (rows + 1) * L, rows * L
    px = lambda m, k: 2 * m * k * width
    vec = lambda k: shape((1, k * width))
    all_devices = lambda k: shape((devices, 1, k))
    g1, b1, g2, b2, gp, bp = map(
        as_row, (gain_first, shift_first, gain_second, shift_second, gain_proj, shift_proj)
    )

    top1 = shifted(inputs[:, -1:], "rows", 1)
    lft1 = shifted(jnp.concatenate([top1[:, :, -1:], inputs[:, :, -1:]], axis=1), "cols", 1)
    stats = call(
        stats_kernel,
        dict(x=inputs, top=top1, lft=lft1, own=own, w1=w1, wp=w_proj),
        dict(spread=all_devices(2 * width + 128), psum=vec(2)),
        dict(
            raw=pltpu.VMEM((cin // 128, (rows_in + 1) * groups, cols_in + 8, 128), f32),
            xe=pltpu.VMEM((rows * groups * cols, 3 * cin), bf16),
            xo=pltpu.VMEM(((rows + 1) * groups * cols, 3 * cin), bf16),
        ),
        flops=px(rows * groups * cols, 10 * cin),
        moved=4_000_000,
    )
    spread1 = stats["spread"]
    tot1 = gather_sum(spread1)

    wide_inputs, _ = lax.optimization_barrier((inputs, top1))
    top, bot, flags = vertical(wide_inputs, cotangent, own)
    flat = over * groups * cols_in
    lft, rgt = horizontal(
        top[:flat].reshape(groups, over, cols_in, cin), inputs, bot[:flat].reshape(groups, over, cols_in, cin), flags, 8
    )
    first = call(
        first_kernel,
        dict(flags=flags, x=inputs, top=top, bot=bot, lft=lft, rgt=rgt, own=own, w1=w1, wp=w_proj),
        dict(
            pre1=shape((MP, width)),
            prep=shape((MP, width)),
            xe=shape((MP, 3 * cin), bf16),
            xo=shape((MP + L, 3 * cin), bf16),
            keep=shape((MP, width)),
            ownp=shape((MP, 128)),
        ),
        dict(raw=pltpu.VMEM((cin // 128, (rows_in + 12) * groups, cols_in + 24, 128), f32)),
        far_in=("w1", "wp"),
        far_out=("xe", "xo", "keep"),
        smem=("flags",),
        flops=px(MP, 10 * cin),
        moved=10_000_000,
    )
    xe, xo, ownp = first["xe"], first["xo"], first["ownp"]
    piece = rim * groups * cols

    def rows_of(flat_rim):
        parts = [
            flat_rim[flat + k * piece : flat + (k + 1) * piece].reshape(groups, rim, cols, 256)
            for k in range(width // 256 + 1)
        ]
        return jnp.concatenate(parts[:-1] + [parts[-1][..., :128]], axis=3)

    cot_here, _ = lax.optimization_barrier((cotangent, spread1))
    clft, crgt = horizontal(
        rows_of(top), jnp.concatenate([cot_here, own], axis=3), rows_of(bot), flags, 8
    )
    rims = call(
        rims_kernel,
        dict(flags=flags, own=own, cot=cotangent, top=top, bot=bot, lft=clft, rgt=crgt),
        dict(maskp=shape((MP, 128)), cotq=shape((MQ, width))),
        dict(
            raw=pltpu.VMEM((1, (rows + 5) * groups, cols + 16, 128), f32),
            field=pltpu.VMEM((1, (rows + 3) * groups, cols + 16, width), f32),
        ),
        far_out=("cotq",),
        smem=("flags",),
        flops=MQ * width * 4,
        moved=4_000_000,
    )
    maskp = rims["maskp"]
    far_xe, far_xo = partner(xe, *core), partner(xo, *core)

    second = call(
        second_kernel,
        dict(pre1=first["pre1"], tot1=tot1, gain=g1, shift=b1, maskp=maskp, ownp=ownp, psum=stats["psum"], w2=w2),
        dict(h3=shape((MP, 3 * width), bf16), pre2=shape((MQ, width)), spread=all_devices(4 * width), mom1=shape((8, width))),
        dict(hid=pltpu.VMEM((MP + 8, width), f32)),
        far_in=("w2",),
        far_out=("h3",),
        flops=px(MQ, 9 * width),
        moved=10_000_000,
    )
    h3, pre2, mom1 = second["h3"], second["pre2"], second["mom1"]
    tot2 = gather_sum(second["spread"])
    far_h3 = partner(h3, *core)

    third = call(
        third_kernel,
        dict(
            pre2=pre2, prep=first["prep"], mom1=mom1, tot2=tot2, gain2=g2, shift2=b2, gainp=gp, shiftp=bp,
            maskp=maskp, ownp=ownp, cotq=rims["cotq"],
        ),
        dict(
            out=shape((groups, rows, cols, width), bf16),
            grad=shape((MQ, width)),
            spread=all_devices(3 * width),
            mom2=shape((8, width)),
        ),
        dict(field=pltpu.VMEM((MQ, width), f32)),
        far_in=("cotq",),
        far_out=("out", "grad"),
        flops=MQ * width * 60,
        moved=5_000_000,
    )
    mom2 = third["mom2"]
    tot3 = gather_sum(third["spread"])

    fourth = call(
        fourth_kernel,
        dict(
            bits=bits, pre2=pre2, prep=first["prep"], mom1=mom1, mom2=mom2, tot3=tot3, gain2=g2, gainp=gp,
            grad=third["grad"], maskp=maskp, ownp=ownp,
        ),
        dict(
            mine=shape((2 * MW, half), bf16),
            theirs=shape((2 * MW, half), bf16),
            gq=shape((MQ + 8, width)),
            gpu=shape((MW, width), bf16),
            sums=vec(3),
        ),
        dict(gpq=pltpu.VMEM((MQ, width), f32)),
        far_in=("grad",),
        far_out=("gpu",),
        smem=("bits",),
        flops=MQ * width * 40,
        moved=6_000_000,
    )
    far2 = partner(fourth["theirs"], *core)

    def chunk_shapes(taps):
        dims = (taps, cin // 4, half)
        return dict(sent_a=shape(dims, bf16), kept_a=shape(dims), sent_b=shape(dims, bf16), kept_b=shape(dims))

    taps2 = 9 * width // cin + 1
    second_parts = call(
        weights_second_kernel,
        dict(bits=bits, h3=h3, h3_far=far_h3, xe=xe, xe_far=far_xe, near=fourth["mine"], far=far2),
        chunk_shapes(taps2),
        dict(acc=pltpu.VMEM((3 * width, half), f32)),
        far_in=("h3", "h3_far", "xe", "xe_far"),
        far_out=("kept_a", "kept_b"),
        smem=("bits",),
        flops=2 * 9 * width * half * 2 * MW,
        moved=8_000_000,
    ).values()
    gq, *second_parts = lax.optimization_barrier((fourth["gq"], *second_parts))

    tree2 = Tree(second_parts, plane, rest)
    tree2.start()
    hidden = call(
        hidden_kernel,
        dict(w2=w2, keep=first["keep"], mom1=mom1, gain=g1, shift=b1, gq=gq, maskp=maskp, ownp=ownp),
        dict(act=shape((MU, width)), normed=shape((MU, width)), spread=all_devices(2 * width)),
        dict(g3=pltpu.VMEM((MQ, 3 * width), bf16)),
        far_in=("w2", "keep"),
        flops=px(MU, 9 * width),
        moved=10_000_000,
    )
    spread4 = tree2.finish(hidden["spread"])
    tot4 = gather_sum(spread4)
    tree2.start()
    tot4, tree2.got = lax.optimization_barrier((tot4, tree2.got))
    act = tree2.finish(hidden["act"])

    tree2.exchange(0, slice(0, 1))
    fifth = call(
        fifth_kernel,
        dict(
            bits=bits, act=act, normed=hidden["normed"], mom1=mom1, tot4=tot4, gain=g1, maskp=maskp, ownp=ownp
        ),
        dict(
            mine=shape((MW, half), bf16), theirs=shape((MW, half), bf16), gu=shape((MU, 2 * width), bf16), sums=vec(2)
        ),
        dict(gf=pltpu.VMEM((MU + 16, width), f32)),
        far_out=("gu",),
        smem=("bits",),
        flops=MU * width * 20,
        moved=4_000_000,
    )
    far1 = partner(fifth["theirs"], *core)
    first_parts = call(
        weights_first_kernel,
        dict(bits=bits, xe=xe, xo=xo, xe_far=far_xe, xo_far=far_xo, near=fifth["mine"], far=far1),
        chunk_shapes(9),
        dict(acc=pltpu.VMEM((3 * cin, half), f32)),
        far_in=("xe", "xo", "xe_far", "xo_far"),
        far_out=("kept_a", "kept_b"),
        smem=("bits",),
        flops=2 * 9 * cin * half * 2 * MW,
        moved=6_000_000,
    ).values()
    gu, tree2.got, *first_parts = lax.optimization_barrier((fifth["gu"], tree2.got, *first_parts))
    tree2.exchange(0, slice(1, None))
    tree1 = Tree(first_parts, plane, rest)
    tree1.start()
    tree2.got = tree1.finish(tree2.got)
    tree1.start()
    tree1.finish()
    tree2.gathered()
    tree2.rest_from(1)
    grad_inputs = call(
        inputs_kernel,
        dict(gu=gu, gpu=fourth["gpu"], w1=w1, wp=w_proj),
        dict(out=shape((groups, rows_in, cols_in, cin), bf16)),
        dict(lines=pltpu.VMEM((cin // 128, rows_in * groups, cols_in, 128), f32)),
        far_in=("gu", "gpu", "w1", "wp"),
        far_out=("out",),
        flops=px(MW, 10 * cin),
        moved=5_000_000,
    )["out"]
    tree1.exchange(0)
    tree1.gathered()
    tree1.rest_from(1)
    tree1.value, grad_inputs = lax.optimization_barrier((tree1.value, grad_inputs))
    half2 = tree2.join()

    side = bit_of(*core).astype(jnp.int32)
    other2 = partner(half2, *core)
    grad_w2 = widen(other2, 1 - side, taps2 - 1, widen(half2, side, taps2 - 1))
    ends = half2[taps2 - 1], other2[taps2 - 1]
    grad_wp = jnp.concatenate(
        [jnp.where(side == 1, ends[1], ends[0]), jnp.where(side == 1, ends[0], ends[1])], axis=1
    ).astype(f32)
    half1, grad_w2, grad_wp = lax.optimization_barrier((tree1.join(), grad_w2, grad_wp))
    other1 = partner(half1, *core)
    grad_w1 = widen(other1, 1 - side, 9, widen(half1, side, 9))

    s3, s4 = fourth["sums"].reshape(3, width), fifth["sums"].reshape(2, width)
    return (
        third["out"],
        grad_inputs,
        grad_w1.reshape(w_first.shape),
        s4[0],
        s4[1],
        grad_w2.reshape(w_second.shape),
        s3[0],
        s3[1],
        grad_wp,
        s3[2],
        s3[1],
    )


def solution(mesh):
    spread = P("grp", "rows", "cols", None)
    return jax.shard_map(
        on_device,
        mesh=mesh,
        in_specs=(spread,) + (P(),) * 9 + (P("grp", "rows", "cols"), spread),
        out_specs=(spread, spread) + (P(),) * 9,
        check_vma=False,
    )
```

profile of v0, /device:TPU:0, one launch (start us, length us, event | category | flops | bytes accessed | tf_op | source)
XLA Modules:
  0.0 306.6 jit_solution(11839029869726278291)
XLA Ops:
  1.5 2.3 collective-permute-start
  7.0 4.2 %collective-permute-start.4 = (bf16[2,17,1,256]{3,2,1,0:T(2,128)(2,1)S(1)}, bf16[2,17,1,256]{3,2,1,0:T(2,128)(2,1)S(1)}, u32[]{:S(2)}, u32[]{:S(2)}) collective-permute-start(bf16[2,17,1,256]{3,2,1,0:T(2,128)(2,1)S(1)} %pad_maximum_fusion.15), channel_id=1, source_target_pairs={{0,4},{4,8},{8,12},{1,5},{5,9},{9,13},{2,6},{6,10},{10,14},{3,7},{... | collective-permute-start | bytes 52232 | tf_op jit(solution)/shard_map/ppermute | solution.py:593
  13.2 3.2 %shard_map.204 = (f32[32,1,1152]{2,1,0:T(1,128)}, f32[1,1024]{1,0:T(1,128)S(1)}) custom-call(bf16[2,16,32,256]{3,2,1,0:T(8,128)(2,1)S(1)} %copy-done, bf16[2,1,32,256]{3,2,1,0:T(8,128)(2,1)S(1)} %collective-permute-done.refs_1_, bf16[2,17,1,256]{3,2,1,0:T(2,128)(2,1)S(1)} %collective-permute-done.4.refs_2_, ...), custom_call_target="tpu_custom_call" | custom-call | tf_op jit(solution)/shard_map/pallas_call | solution.py:68
  16.4 6.4 %all-to-all-start = ((f32[32,1,1152]{2,1,0:T(1,128)}), f32[32,1,1152]{2,1,0:T(1,128)S(1)}, u32[]{:S(2)}, u32[]{:S(2)}) async-start(f32[32,1,1152]{2,1,0:T(1,128)} %get-tuple-element.86), calls=%async_computation | async-start | bytes 294912 | tf_op jit(solution)/shard_map/all_to_all | solution.py:625
  24.3 4.6 %collective-permute-start.5 = (bf16[2,14,8,640]{3,2,1,0:T(8,128)(2,1)S(1)}, bf16[2,14,8,640]{3,2,1,0:T(8,128)(2,1)S(1)}, u32[]{:S(2)}, u32[]{:S(2)}) collective-permute-start(bf16[2,14,8,640]{3,2,1,0:T(8,128)(2,1)S(1)} %pad_maximum_fusion.9), channel_id=1, source_target_pairs={{0,4},{4,8},{8,12},{1,5},{5,9},{9,13},{2,6},{6,10},{10,14},{3,7},{... | collective-permute-start | bytes 860168 | tf_op jit(solution)/shard_map/ppermute | solution.py:593
  29.0 4.6 %collective-permute-start.2 = (bf16[2,28,8,256]{3,2,1,0:T(8,128)(2,1)S(1)}, bf16[2,28,8,256]{3,2,1,0:T(8,128)(2,1)S(1)}, u32[]{:S(2)}, u32[]{:S(2)}) collective-permute-start(bf16[2,28,8,256]{3,2,1,0:T(8,128)(2,1)S(1)} %pad_maximum_fusion.10), channel_id=1, source_target_pairs={{0,4},{4,8},{8,12},{1,5},{5,9},{9,13},{2,6},{6,10},{10,14},{3,7},{... | collective-permute-start | bytes 688136 | tf_op jit(solution)/shard_map/ppermute | solution.py:593
  34.9 5.1 %collective-permute-done.2.refs_4_ = bf16[2,28,8,256]{3,2,1,0:T(8,128)(2,1)S(1)} collective-permute-done((bf16[2,28,8,256]{3,2,1,0:T(8,128)(2,1)S(1)}, bf16[2,28,8,256]{3,2,1,0:T(8,128)(2,1)S(1)}, u32[]{:S(2)}, u32[]{:S(2)}) %collective-permute-start.2) | collective-permute-done | bytes 229408 | tf_op jit(solution)/shard_map/ppermute | solution.py:593
  40.0 10.6 %collective-permute-done.3.refs_5_ = bf16[2,28,8,256]{3,2,1,0:T(8,128)(2,1)S(1)} collective-permute-done((bf16[2,28,8,256]{3,2,1,0:T(8,128)(2,1)S(1)}, bf16[2,28,8,256]{3,2,1,0:T(8,128)(2,1)S(1)}, u32[]{:S(2)}, u32[]{:S(2)}) %collective-permute-start.3) | collective-permute-done | bytes 229408 | tf_op jit(solution)/shard_map/ppermute | solution.py:593
  50.6 6.9 %shard_map.203 = (f32[624,512]{1,0:T(8,128)}, f32[624,512]{1,0:T(8,128)}, bf16[624,768]{1,0:T(8,128)(2,1)}, bf16[672,768]{1,0:T(8,128)(2,1)}, f32[624,512]{1,0:T(8,128)}, /*index=5*/f32[624,128]{1,0:T(8,128)S(1)}) custom-call(s32[2]{0:T(128)S(1)} %add_convert_fusion.6.refs_0_, bf16[2,16,32,256]{3,2,1,0:T(8,128)(2,1)S(1)} %copy-done, ...), custom_call_target="tpu_custom_call" | custom-call | tf_op jit(solution)/shard_map/pallas_call | solution.py:68
  57.5 1.8 shard_map.205
  59.4 8.2 %shard_map.206 = (bf16[624,1536]{1,0:T(8,128)(2,1)}, f32[528,512]{1,0:T(8,128)}, f32[32,1,2048]{2,1,0:T(1,128)}, f32[8,512]{1,0:T(8,128)S(1)}) custom-call(f32[624,512]{1,0:T(8,128)} %get-tuple-element.85.refs_0_, f32[32,1,1152]{2,1,0:T(1,128)S(1)} %all-to-all-done.refs_1_, f32[1,512]{1,0:T(1,128)S(1)} %bitcast.40, f32[1,512]{1,0:T(1,128)S(1)} %bitcast.43, ...), custom_call_target="tpu_custom_call" | custom-call | tf_op jit(solution)/shard_map/pallas_call | solution.py:68
  67.7 5.0 %all-to-all-start.1 = ((f32[32,1,2048]{2,1,0:T(1,128)}), f32[32,1,2048]{2,1,0:T(1,128)S(1)}, u32[]{:S(2)}, u32[]{:S(2)}) async-start(f32[32,1,2048]{2,1,0:T(1,128)} %get-tuple-element.94), calls=%async_computation.1 | async-start | bytes 524288 | tf_op jit(solution)/shard_map/all_to_all | solution.py:625
  73.1 10.6 %all-to-all-done.1.refs_3_ = f32[32,1,2048]{2,1,0:T(1,128)S(1)} async-done(((f32[32,1,2048]{2,1,0:T(1,128)}), f32[32,1,2048]{2,1,0:T(1,128)S(1)}, u32[]{:S(2)}, u32[]{:S(2)}) %all-to-all-start.1) | async-done | bytes 262176 | tf_op jit(solution)/shard_map/all_to_all | solution.py:625
  83.7 6.4 %shard_map.207 = (bf16[2,8,16,512]{3,2,1,0:T(8,128)(2,1)}, f32[528,512]{1,0:T(8,128)}, f32[32,1,1536]{2,1,0:T(1,128)}, f32[8,512]{1,0:T(8,128)S(1)}) custom-call(f32[528,512]{1,0:T(8,128)} %get-tuple-element.91.refs_0_.refs_1_, f32[624,512]{1,0:T(8,128)} %get-tuple-element.92.refs_1_.refs_2_, f32[8,512]{1,0:T(8,128)S(1)} %get-tuple-element.93.refs_2_.refs_3_, ...), custom_call_target="tpu_custom_call" | custom-call | tf_op jit(solution)/shard_map/pallas_call | solution.py:68
  90.1 2.8 all-to-all-start.2
  93.0 9.1 %all-to-all-done.2.refs_5_ = f32[32,1,1536]{2,1,0:T(1,128)S(1)} async-done(((f32[32,1,1536]{2,1,0:T(1,128)}), f32[32,1,1536]{2,1,0:T(1,128)S(1)}, u32[]{:S(2)}, u32[]{:S(2)}) %all-to-all-start.2) | async-done | bytes 196640 | tf_op jit(solution)/shard_map/all_to_all | solution.py:625
  102.1 5.4 %shard_map.208 = (bf16[768,256]{1,0:T(8,128)(2,1)S(1)}, bf16[768,256]{1,0:T(8,128)(2,1)S(1)}, f32[536,512]{1,0:T(8,128)}, bf16[384,512]{1,0:T(8,128)(2,1)}, f32[1,1536]{1,0:T(1,128)S(1)}) custom-call(s32[3]{0:T(128)S(1)} %pad_add_fusion.refs_0_, f32[528,512]{1,0:T(8,128)} %get-tuple-element.91.refs_0_.refs_1_, f32[624,512]{1,0:T(8,128)} %get-tuple-element.92.refs_1_.refs_2_, ...), custom_call_target="tpu_custom_call" | custom-call | tf_op jit(solution)/shard_map/pallas_call | solution.py:68
  107.6 1.7 collective-permute-done.9.refs_6_
  109.3 8.5 %shard_map.209 = (bf16[19,64,256]{2,1,0:T(8,128)(2,1)S(1)}, f32[19,64,256]{2,1,0:T(8,128)}, bf16[19,64,256]{2,1,0:T(8,128)(2,1)}, f32[19,64,256]{2,1,0:T(8,128)}) custom-call(s32[3]{0:T(128)S(1)} %pad_add_fusion.refs_0_, bf16[624,1536]{1,0:T(8,128)(2,1)} %get-tuple-element.102.refs_1_, bf16[624,1536]{1,0:T(8,128)(2,1)} %collective-permute-done.7.refs_2_, ...), custom_call_target="tpu_custom_call" | custom-call | tf_op jit(solution)/shard_map/pallas_call | solution.py:68
  118.9 10.7 %shard_map.210 = (f32[432,512]{1,0:T(8,128)S(1)}, f32[432,512]{1,0:T(8,128)}, f32[32,1,1024]{2,1,0:T(1,128)}) custom-call(bf16[3,1536,512]{2,1,0:T(8,128)(2,1)} %bitcast.56, f32[624,512]{1,0:T(8,128)} %get-tuple-element.97.refs_1_, f32[8,512]{1,0:T(8,128)S(1)} %get-tuple-element.93.refs_2_.refs_3_, f32[1,512]{1,0:T(1,128)S(1)} %bitcast.41, ...), custom_call_target="tpu_custom_call" | custom-call | tf_op jit(solution)/shard_map/pallas_call | solution.py:68
  129.7 4.3 %collective-permute-done.10 = bf16[19,64,256]{2,1,0:T(8,128)(2,1)S(1)} collective-permute-done((bf16[19,64,256]{2,1,0:T(8,128)(2,1)S(1)}, bf16[19,64,256]{2,1,0:T(8,128)(2,1)S(1)}, u32[]{:S(2)}, u32[]{:S(2)}) %collective-permute-start.10) | collective-permute-done | bytes 622624 | tf_op jit(solution)/shard_map/ppermute | solution.py:634
  137.2 3.1 %all-to-all-start.3 = ((f32[32,1,1024]{2,1,0:T(1,128)}), f32[32,1,1024]{2,1,0:T(1,128)S(1)}, u32[]{:S(2)}, u32[]{:S(2)}) async-start(f32[32,1,1024]{2,1,0:T(1,128)} %get-tuple-element.118), calls=%async_computation.3 | async-start | bytes 262144 | tf_op jit(solution)/shard_map/all_to_all | solution.py:625
  140.4 7.6 %all-to-all-done.3.refs_4_ = f32[32,1,1024]{2,1,0:T(1,128)S(1)} async-done(((f32[32,1,1024]{2,1,0:T(1,128)}), f32[32,1,1024]{2,1,0:T(1,128)S(1)}, u32[]{:S(2)}, u32[]{:S(2)}) %all-to-all-start.3) | async-done | bytes 131104 | tf_op jit(solution)/shard_map/all_to_all | solution.py:625
  150.5 2.9 shard_map.211
  154.9 5.1 %shard_map.212 = (bf16[9,64,256]{2,1,0:T(8,128)(2,1)S(1)}, f32[9,64,256]{2,1,0:T(8,128)S(1)}, bf16[9,64,256]{2,1,0:T(8,128)(2,1)S(1)}, f32[9,64,256]{2,1,0:T(8,128)}) custom-call(s32[3]{0:T(128)S(1)} %pad_add_fusion.refs_0_, bf16[624,768]{1,0:T(8,128)(2,1)} %get-tuple-element.103.refs_3_.refs_1_, bf16[672,768]{1,0:T(8,128)(2,1)} %get-tuple-element.129.refs_2_, ...), custom_call_target="tpu_custom_call" | custom-call | tf_op jit(solution)/shard_map/pallas_call | solution.py:68
  160.0 5.0 %collective-permute-done.14 = bf16[38,32,256]{2,1,0:T(8,128)(2,1)S(1)} collective-permute-done((bf16[38,32,256]{2,1,0:T(8,128)(2,1)S(1)}, bf16[38,32,256]{2,1,0:T(8,128)(2,1)S(1)}, u32[]{:S(2)}, u32[]{:S(2)}) %collective-permute-start.14) | collective-permute-done | bytes 622624 | tf_op jit(solution)/shard_map/ppermute | solution.py:634
  168.9 3.8 %collective-permute-done.19 = bf16[9,64,256]{2,1,0:T(8,128)(2,1)S(1)} collective-permute-done((bf16[9,64,256]{2,1,0:T(8,128)(2,1)S(1)}, bf16[9,64,256]{2,1,0:T(8,128)(2,1)S(1)}, u32[]{:S(2)}, u32[]{:S(2)}) %collective-permute-start.19) | collective-permute-done | bytes 294944 | tf_op jit(solution)/shard_map/ppermute | solution.py:634
  172.8 2.0 collective-permute-done.20
  175.0 10.0 %collective-permute-done.18 = bf16[38,32,256]{2,1,0:T(8,128)(2,1)S(1)} collective-permute-done((bf16[38,32,256]{2,1,0:T(8,128)(2,1)S(1)}, bf16[38,32,256]{2,1,0:T(8,128)(2,1)S(1)}, u32[]{:S(2)}, u32[]{:S(2)}) %collective-permute-start.18) | collective-permute-done | bytes 622624 | tf_op jit(solution)/shard_map/ppermute | solution.py:634
  185.0 35.4 %collective-permute-done.17 = bf16[38,32,256]{2,1,0:T(8,128)(2,1)S(1)} collective-permute-done((bf16[38,32,256]{2,1,0:T(8,128)(2,1)S(1)}, bf16[38,32,256]{2,1,0:T(8,128)(2,1)S(1)}, u32[]{:S(2)}, u32[]{:S(2)}) %collective-permute-start.17) | collective-permute-done | bytes 622624 | tf_op jit(solution)/shard_map/ppermute | solution.py:634
  220.9 1.5 collective-permute-start.30
  223.4 4.8 %collective-permute-done.30 = bf16[19,32,256]{2,1,0:T(8,128)(2,1)S(1)} collective-permute-done((bf16[19,32,256]{2,1,0:T(8,128)(2,1)S(1)}, bf16[19,32,256]{2,1,0:T(8,128)(2,1)S(1)}, u32[]{:S(2)}, u32[]{:S(2)}) %collective-permute-start.30) | collective-permute-done | bytes 311328 | tf_op jit(solution)/shard_map/ppermute | solution.py:634
  231.8 1.6 collective-permute-start.31
  233.9 11.8 %collective-permute-done.21 = bf16[9,32,256]{2,1,0:T(8,128)(2,1)S(1)} collective-permute-done((bf16[9,32,256]{2,1,0:T(8,128)(2,1)S(1)}, bf16[9,32,256]{2,1,0:T(8,128)(2,1)S(1)}, u32[]{:S(2)}, u32[]{:S(2)}) %collective-permute-start.21) | collective-permute-done | bytes 147488 | tf_op jit(solution)/shard_map/ppermute | solution.py:634
  247.9 5.1 %collective-permute-start.23 = (bf16[18,32,256]{2,1,0:T(8,128)(2,1)S(1)}, bf16[18,32,256]{2,1,0:T(8,128)(2,1)S(1)}, u32[]{:S(2)}, u32[]{:S(2)}) collective-permute-start(bf16[18,32,256]{2,1,0:T(8,128)(2,1)S(1)} %pad_maximum_fusion.5), channel_id=1, source_target_pairs={{0,1},{1,0},{2,3},{3,2},{4,5},{5,4},{6,7},{7,6},{8,9},{9,8},{10,11... | collective-permute-start | bytes 884744 | tf_op jit(solution)/shard_map/ppermute | solution.py:634
  253.0 6.2 %shard_map.213 = bf16[2,16,32,256]{3,2,1,0:T(8,128)(2,1)} custom-call(bf16[432,1024]{1,0:T(8,128)(2,1)S(1)} %copy-done.4, bf16[384,512]{1,0:T(8,128)(2,1)S(1)} %copy-done.5, bf16[3,768,512]{2,1,0:T(8,128)(2,1)} %bitcast.54, bf16[256,512]{1,0:T(8,128)(2,1)S(1)} %copy-done.2), custom_call_target="tpu_custom_call" | custom-call | tf_op jit(solution)/shard_map/pallas_call | solution.py:68
  259.2 6.0 %collective-permute-done.24 = bf16[18,32,256]{2,1,0:T(8,128)(2,1)S(1)} collective-permute-done((bf16[18,32,256]{2,1,0:T(8,128)(2,1)S(1)}, bf16[18,32,256]{2,1,0:T(8,128)(2,1)S(1)}, u32[]{:S(2)}, u32[]{:S(2)}) %collective-permute-start.24) | collective-permute-done | bytes 294944 | tf_op jit(solution)/shard_map/ppermute | solution.py:634
  265.2 7.0 %collective-permute-done.25 = bf16[18,32,256]{2,1,0:T(8,128)(2,1)S(1)} collective-permute-done((bf16[18,32,256]{2,1,0:T(8,128)(2,1)S(1)}, bf16[18,32,256]{2,1,0:T(8,128)(2,1)S(1)}, u32[]{:S(2)}, u32[]{:S(2)}) %collective-permute-start.25) | collective-permute-done | bytes 294944 | tf_op jit(solution)/shard_map/ppermute | solution.py:634
  272.4 1.8 collective-permute-start.26
  274.2 1.7 collective-permute-start.28
  275.9 1.9 collective-permute-done.26
  277.8 1.5 collective-permute-done.28
  282.2 1.8 collective-permute-start.27
  283.9 4.6 %collective-permute-done.29 = bf16[9,64,256]{2,1,0:T(8,128)(2,1)} collective-permute-done((bf16[9,64,256]{2,1,0:T(8,128)(2,1)}, bf16[9,64,256]{2,1,0:T(8,128)(2,1)}, u32[]{:S(2)}, u32[]{:S(2)}) %collective-permute-start.29) | collective-permute-done | bytes 294944 | tf_op jit(solution)/shard_map/ppermute | solution.py:634
  291.0 3.1 %shard_map.214.refs_0_ = f32[18,256,512]{2,1,0:T(8,128)} custom-call(s32[1]{0:T(128)} %bitcast.25.bits, bf16[19,256,256]{2,1,0:T(8,128)(2,1)S(1)} %pad_maximum_fusion.half), custom_call_target="tpu_custom_call" | custom-call | bytes 7077888 | tf_op jit(solution)/shard_map/pallas_call | solution.py:575
  295.9 5.3 %shard_map.215 = f32[18,256,512]{2,1,0:T(8,128)} custom-call(s32[1]{0:T(128)} %bitcast.28.bits, bf16[19,256,256]{2,1,0:T(8,128)(2,1)} %collective-permute-done.34.half, f32[18,256,512]{2,1,0:T(8,128)} %shard_map.214.refs_0_), custom_call_target="tpu_custom_call", output_to_operand_aliasing={{}: (2, {})} | custom-call | bytes 7077888 | tf_op jit(solution)/shard_map/pallas_call | solution.py:575
  302.3 1.9 shard_map.216.refs_0_
  304.2 1.9 shard_map.217
  (147 shorter events, 37.1 us)
Async XLA Ops:
  1.5 5.1 %collective-permute-start = (bf16[2,1,32,256]{3,2,1,0:T(8,128)(2,1)S(1)}, bf16[2,1,32,256]{3,2,1,0:T(8,128)(2,1)S(1)}, u32[]{:S(2)}, u32[]{:S(2)}) collective-permute-start(bf16[2,1,32,256]{3,2,1,0:T(8,128)(2,1)S(1)} %slice.160), channel_id=1, source_target_pairs={{0,16},{1,17},{2,18},{3,19},{4,20},{5,21},{6,22},{7,23},{8,24},{9,... | collective-permute-start | bytes 98312 | tf_op jit(solution)/shard_map/ppermute | solution.py:593
  6.8 16.1 %collective-permute-start.1 = (bf16[672,256]{1,0:T(8,128)(2,1)S(1)}, bf16[672,256]{1,0:T(8,128)(2,1)S(1)}, u32[]{:S(2)}, u32[]{:S(2)}) collective-permute-start(bf16[672,256]{1,0:T(8,128)(2,1)S(1)} %maximum_select_fusion), channel_id=1, source_target_pairs={{0,16},{16,0},{1,17},{17,1},{2,18},{18,2},{3,19},{19,3},{4,20},{20... | collective-permute-start | bytes 1032200 | tf_op jit(solution)/shard_map/ppermute | solution.py:609
  7.0 6.1 %collective-permute-start.4 = (bf16[2,17,1,256]{3,2,1,0:T(2,128)(2,1)S(1)}, bf16[2,17,1,256]{3,2,1,0:T(2,128)(2,1)S(1)}, u32[]{:S(2)}, u32[]{:S(2)}) collective-permute-start(bf16[2,17,1,256]{3,2,1,0:T(2,128)(2,1)S(1)} %pad_maximum_fusion.15), channel_id=1, source_target_pairs={{0,4},{4,8},{8,12},{1,5},{5,9},{9,13},{2,6},{6,10},{10,14},{3,7},{... | collective-permute-start | bytes 52232 | tf_op jit(solution)/shard_map/ppermute | solution.py:593
  13.2 9.6 %copy-start.1 = (bf16[2,8,16,512]{3,2,1,0:T(8,128)(2,1)S(1)}, bf16[2,8,16,512]{3,2,1,0:T(8,128)(2,1)}, u32[]{:S(2)}) copy-start(bf16[2,8,16,512]{3,2,1,0:T(8,128)(2,1)} %refs_2_.1) | copy-start | bytes 786436
  16.4 42.9 %all-to-all-start = ((f32[32,1,1152]{2,1,0:T(1,128)}), f32[32,1,1152]{2,1,0:T(1,128)S(1)}, u32[]{:S(2)}, u32[]{:S(2)}) async-start(f32[32,1,1152]{2,1,0:T(1,128)} %get-tuple-element.86), calls=%async_computation | async-start | bytes 294912 | tf_op jit(solution)/shard_map/all_to_all | solution.py:625
  23.0 34.5 %collective-permute-start.6 = (bf16[2,14,8,640]{3,2,1,0:T(8,128)(2,1)S(1)}, bf16[2,14,8,640]{3,2,1,0:T(8,128)(2,1)S(1)}, u32[]{:S(2)}, u32[]{:S(2)}) collective-permute-start(bf16[2,14,8,640]{3,2,1,0:T(8,128)(2,1)S(1)} %fusion.1), channel_id=1, source_target_pairs={{4,0},{8,4},{12,8},{5,1},{9,5},{13,9},{6,2},{10,6},{14,10},{7,3},{... | collective-permute-start | bytes 860168 | tf_op jit(solution)/shard_map/ppermute | solution.py:593
  24.3 33.2 %collective-permute-start.5 = (bf16[2,14,8,640]{3,2,1,0:T(8,128)(2,1)S(1)}, bf16[2,14,8,640]{3,2,1,0:T(8,128)(2,1)S(1)}, u32[]{:S(2)}, u32[]{:S(2)}) collective-permute-start(bf16[2,14,8,640]{3,2,1,0:T(8,128)(2,1)S(1)} %pad_maximum_fusion.9), channel_id=1, source_target_pairs={{0,4},{4,8},{8,12},{1,5},{5,9},{9,13},{2,6},{6,10},{10,14},{3,7},{... | collective-permute-start | bytes 860168 | tf_op jit(solution)/shard_map/ppermute | solution.py:593
  29.0 11.0 %collective-permute-start.2 = (bf16[2,28,8,256]{3,2,1,0:T(8,128)(2,1)S(1)}, bf16[2,28,8,256]{3,2,1,0:T(8,128)(2,1)S(1)}, u32[]{:S(2)}, u32[]{:S(2)}) collective-permute-start(bf16[2,28,8,256]{3,2,1,0:T(8,128)(2,1)S(1)} %pad_maximum_fusion.10), channel_id=1, source_target_pairs={{0,4},{4,8},{8,12},{1,5},{5,9},{9,13},{2,6},{6,10},{10,14},{3,7},{... | collective-permute-start | bytes 688136 | tf_op jit(solution)/shard_map/ppermute | solution.py:593
  33.6 17.0 %collective-permute-start.3 = (bf16[2,28,8,256]{3,2,1,0:T(8,128)(2,1)S(1)}, bf16[2,28,8,256]{3,2,1,0:T(8,128)(2,1)S(1)}, u32[]{:S(2)}, u32[]{:S(2)}) collective-permute-start(bf16[2,28,8,256]{3,2,1,0:T(8,128)(2,1)S(1)} %pad_maximum_fusion.11), channel_id=1, source_target_pairs={{4,0},{8,4},{12,8},{5,1},{9,5},{13,9},{6,2},{10,6},{14,10},{7,3},{... | collective-permute-start | bytes 688136 | tf_op jit(solution)/shard_map/ppermute | solution.py:593
  59.4 13.4 %copy-start.12 = (bf16[624,768]{1,0:T(8,128)(2,1)S(1)}, bf16[624,768]{1,0:T(8,128)(2,1)}, u32[]{:S(2)}) copy-start(bf16[624,768]{1,0:T(8,128)(2,1)} %get-tuple-element.103.refs_3_.refs_1_) | copy-start | bytes 2875396
  59.4 24.3 %copy-start.8 = (f32[512]{0:T(512)S(1)}, f32[512]{0:T(512)}, u32[]{:S(2)}) copy-start(f32[512]{0:T(512)} %param.17) | copy-start | bytes 6148
  59.4 24.3 %copy-start.9 = (f32[512]{0:T(512)S(1)}, f32[512]{0:T(512)}, u32[]{:S(2)}) copy-start(f32[512]{0:T(512)} %param.20) | copy-start | bytes 6148
  59.4 24.3 %copy-start.10 = (f32[512]{0:T(512)S(1)}, f32[512]{0:T(512)}, u32[]{:S(2)}) copy-start(f32[512]{0:T(512)} %param.18) | copy-start | bytes 6148
  59.4 24.3 %copy-start.11 = (f32[512]{0:T(512)S(1)}, f32[512]{0:T(512)}, u32[]{:S(2)}) copy-start(f32[512]{0:T(512)} %param.21) | copy-start | bytes 6148
  67.6 41.7 %collective-permute-start.7 = (bf16[624,1536]{1,0:T(8,128)(2,1)}, bf16[624,1536]{1,0:T(8,128)(2,1)}, u32[]{:S(2)}, u32[]{:S(2)}) collective-permute-start(bf16[624,1536]{1,0:T(8,128)(2,1)} %get-tuple-element.102.refs_1_), channel_id=1, source_target_pairs={{0,16},{16,0},{1,17},{17,1},{2,18},{18,2},{3,19},{19,3},{4,20},{20... | collective-permute-start | bytes 5750792 | tf_op jit(solution)/shard_map/ppermute | solution.py:634
  67.7 16.0 %all-to-all-start.1 = ((f32[32,1,2048]{2,1,0:T(1,128)}), f32[32,1,2048]{2,1,0:T(1,128)S(1)}, u32[]{:S(2)}, u32[]{:S(2)}) async-start(f32[32,1,2048]{2,1,0:T(1,128)} %get-tuple-element.94), calls=%async_computation.1 | async-start | bytes 524288 | tf_op jit(solution)/shard_map/all_to_all | solution.py:625
  72.7 34.9 %collective-permute-start.8 = (bf16[624,768]{1,0:T(8,128)(2,1)S(1)}, bf16[624,768]{1,0:T(8,128)(2,1)}, u32[]{:S(2)}, u32[]{:S(2)}) collective-permute-start(bf16[624,768]{1,0:T(8,128)(2,1)S(1)} %copy-done.12), channel_id=1, source_target_pairs={{0,16},{16,0},{1,17},{17,1},{2,18},{18,2},{3,19},{19,3},{4,20},{20... | collective-permute-start | bytes 2875400 | tf_op jit(solution)/shard_map/ppermute | solution.py:634
  90.1 12.0 %all-to-all-start.2 = ((f32[32,1,1536]{2,1,0:T(1,128)}), f32[32,1,1536]{2,1,0:T(1,128)S(1)}, u32[]{:S(2)}, u32[]{:S(2)}) async-start(f32[32,1,1536]{2,1,0:T(1,128)} %get-tuple-element.99), calls=%async_computation.2 | async-start | bytes 393216 | tf_op jit(solution)/shard_map/all_to_all | solution.py:625
  107.5 1.8 collective-permute-start.9
  117.8 16.1 %collective-permute-start.10 = (bf16[19,64,256]{2,1,0:T(8,128)(2,1)S(1)}, bf16[19,64,256]{2,1,0:T(8,128)(2,1)S(1)}, u32[]{:S(2)}, u32[]{:S(2)}) collective-permute-start(bf16[19,64,256]{2,1,0:T(8,128)(2,1)S(1)} %get-tuple-element.114), channel_id=1, source_target_pairs={{0,4},{4,0},{8,12},{12,8},{1,5},{5,1},{9,13},{13,9},{2,6},{6,2},{1... | collective-permute-start | bytes 1867784 | tf_op jit(solution)/shard_map/ppermute | solution.py:634
  118.8 16.0 %collective-permute-start.11 = (bf16[19,64,256]{2,1,0:T(8,128)(2,1)}, bf16[19,64,256]{2,1,0:T(8,128)(2,1)S(1)}, u32[]{:S(2)}, u32[]{:S(2)}) collective-permute-start(bf16[19,64,256]{2,1,0:T(8,128)(2,1)} %get-tuple-element.116), channel_id=1, source_target_pairs={{0,8},{4,12},{8,0},{12,4},{1,9},{5,13},{9,1},{13,5},{2,10},{6,14},... | collective-permute-start | bytes 1867784 | tf_op jit(solution)/shard_map/ppermute | solution.py:634
  118.9 15.1 %copy-start.15 = (f32[19,64,256]{2,1,0:T(8,128)S(1)}, f32[19,64,256]{2,1,0:T(8,128)}, u32[]{:S(2)}) copy-start(f32[19,64,256]{2,1,0:T(8,128)} %get-tuple-element.113) | copy-start | bytes 3735556
  135.8 12.2 %collective-permute-start.12 = (bf16[19,32,256]{2,1,0:T(8,128)(2,1)S(1)}, bf16[19,32,256]{2,1,0:T(8,128)(2,1)S(1)}, u32[]{:S(2)}, u32[]{:S(2)}) collective-permute-start(bf16[19,32,256]{2,1,0:T(8,128)(2,1)S(1)} %select_convert_fusion.1), channel_id=1, source_target_pairs={{0,8},{4,12},{8,0},{12,4},{1,9},{5,13},{9,1},{13,5},{2,10},{6,14},... | collective-permute-start | bytes 933896 | tf_op jit(solution)/shard_map/ppermute | solution.py:634
  136.8 11.2 %collective-permute-start.13 = (bf16[19,32,256]{2,1,0:T(8,128)(2,1)S(1)}, bf16[19,32,256]{2,1,0:T(8,128)(2,1)}, u32[]{:S(2)}, u32[]{:S(2)}) collective-permute-start(bf16[19,32,256]{2,1,0:T(8,128)(2,1)S(1)} %select_convert_fusion), channel_id=1, source_target_pairs={{0,4},{4,0},{8,12},{12,8},{1,5},{5,1},{9,13},{13,9},{2,6},{6,2},{1... | collective-permute-start | bytes 933896 | tf_op jit(solution)/shard_map/ppermute | solution.py:634
  137.2 10.8 %all-to-all-start.3 = ((f32[32,1,1024]{2,1,0:T(1,128)}), f32[32,1,1024]{2,1,0:T(1,128)S(1)}, u32[]{:S(2)}, u32[]{:S(2)}) async-start(f32[32,1,1024]{2,1,0:T(1,128)} %get-tuple-element.118), calls=%async_computation.3 | async-start | bytes 262144 | tf_op jit(solution)/shard_map/all_to_all | solution.py:625
  140.3 13.1 %collective-permute-start.15 = (bf16[672,768]{1,0:T(8,128)(2,1)}, bf16[672,768]{1,0:T(8,128)(2,1)}, u32[]{:S(2)}, u32[]{:S(2)}) collective-permute-start(bf16[672,768]{1,0:T(8,128)(2,1)} %get-tuple-element.129.refs_2_), channel_id=1, source_target_pairs={{0,16},{16,0},{1,17},{17,1},{2,18},{18,2},{3,19},{19,3},{4,20},{20... | collective-permute-start | bytes 3096584 | tf_op jit(solution)/shard_map/ppermute | solution.py:634
  149.3 15.7 %collective-permute-start.14 = (bf16[38,32,256]{2,1,0:T(8,128)(2,1)S(1)}, bf16[38,32,256]{2,1,0:T(8,128)(2,1)S(1)}, u32[]{:S(2)}, u32[]{:S(2)}) collective-permute-start(bf16[38,32,256]{2,1,0:T(8,128)(2,1)S(1)} %pad_maximum_fusion.2), channel_id=1, source_target_pairs={{0,1},{1,0},{2,3},{3,2},{4,5},{5,4},{6,7},{7,6},{8,9},{9,8},{10,11... | collective-permute-start | bytes 1867784 | tf_op jit(solution)/shard_map/ppermute | solution.py:634
  153.4 1.5 collective-permute-start.16
  160.0 14.8 %copy-start.16 = (f32[9,64,256]{2,1,0:T(8,128)S(1)}, f32[9,64,256]{2,1,0:T(8,128)}, u32[]{:S(2)}) copy-start(f32[9,64,256]{2,1,0:T(8,128)} %get-tuple-element.139) | copy-start | bytes 1769476
  165.0 7.7 %collective-permute-start.19 = (bf16[9,64,256]{2,1,0:T(8,128)(2,1)S(1)}, bf16[9,64,256]{2,1,0:T(8,128)(2,1)S(1)}, u32[]{:S(2)}, u32[]{:S(2)}) collective-permute-start(bf16[9,64,256]{2,1,0:T(8,128)(2,1)S(1)} %get-tuple-element.138), channel_id=1, source_target_pairs={{0,4},{4,0},{8,12},{12,8},{1,5},{5,1},{9,13},{13,9},{2,6},{6,2},{1... | collective-permute-start | bytes 884744 | tf_op jit(solution)/shard_map/ppermute | solution.py:634
  166.2 18.8 %collective-permute-start.18 = (bf16[38,32,256]{2,1,0:T(8,128)(2,1)S(1)}, bf16[38,32,256]{2,1,0:T(8,128)(2,1)S(1)}, u32[]{:S(2)}, u32[]{:S(2)}) collective-permute-start(bf16[38,32,256]{2,1,0:T(8,128)(2,1)S(1)} %pad_maximum_fusion.2), channel_id=1, source_target_pairs={{0,3},{1,2},{2,1},{3,0},{4,7},{5,6},{6,5},{7,4},{8,11},{9,10},{10,... | collective-permute-start | bytes 1867784 | tf_op jit(solution)/shard_map/ppermute | solution.py:634
  167.4 53.0 %collective-permute-start.17 = (bf16[38,32,256]{2,1,0:T(8,128)(2,1)S(1)}, bf16[38,32,256]{2,1,0:T(8,128)(2,1)S(1)}, u32[]{:S(2)}, u32[]{:S(2)}) collective-permute-start(bf16[38,32,256]{2,1,0:T(8,128)(2,1)S(1)} %pad_maximum_fusion.2), channel_id=1, source_target_pairs={{0,2},{1,3},{2,0},{3,1},{4,6},{5,7},{6,4},{7,5},{8,10},{9,11},{10,... | collective-permute-start | bytes 1867784 | tf_op jit(solution)/shard_map/ppermute | solution.py:634
  168.1 6.7 %collective-permute-start.20 = (bf16[9,64,256]{2,1,0:T(8,128)(2,1)S(1)}, bf16[9,64,256]{2,1,0:T(8,128)(2,1)S(1)}, u32[]{:S(2)}, u32[]{:S(2)}) collective-permute-start(bf16[9,64,256]{2,1,0:T(8,128)(2,1)S(1)} %get-tuple-element.140), channel_id=1, source_target_pairs={{0,8},{4,12},{8,0},{12,4},{1,9},{5,13},{9,1},{13,5},{2,10},{6,14},... | collective-permute-start | bytes 884744 | tf_op jit(solution)/shard_map/ppermute | solution.py:634
  220.9 7.3 %collective-permute-start.30 = (bf16[19,32,256]{2,1,0:T(8,128)(2,1)S(1)}, bf16[19,32,256]{2,1,0:T(8,128)(2,1)S(1)}, u32[]{:S(2)}, u32[]{:S(2)}) collective-permute-start(bf16[19,32,256]{2,1,0:T(8,128)(2,1)S(1)} %get-tuple-element.169), channel_id=1, source_target_pairs={{0,8},{4,12},{8,0},{12,4},{1,9},{5,13},{9,1},{13,5},{2,10},{6,14},... | collective-permute-start | bytes 933896 | tf_op jit(solution)/shard_map/ppermute | solution.py:634
  222.4 7.1 %collective-permute-start.32 = (bf16[19,32,256]{2,1,0:T(8,128)(2,1)S(1)}, bf16[19,32,256]{2,1,0:T(8,128)(2,1)S(1)}, u32[]{:S(2)}, u32[]{:S(2)}) collective-permute-start(bf16[19,32,256]{2,1,0:T(8,128)(2,1)S(1)} %get-tuple-element.170), channel_id=1, source_target_pairs={{0,4},{4,0},{8,12},{12,8},{1,5},{5,1},{9,13},{13,9},{2,6},{6,2},{1... | collective-permute-start | bytes 933896 | tf_op jit(solution)/shard_map/ppermute | solution.py:634
  229.6 16.1 %collective-permute-start.33 = (bf16[19,64,256]{2,1,0:T(8,128)(2,1)S(1)}, bf16[19,64,256]{2,1,0:T(8,128)(2,1)S(1)}, u32[]{:S(2)}, u32[]{:S(2)}) collective-permute-start(bf16[19,64,256]{2,1,0:T(8,128)(2,1)S(1)} %pad_maximum_fusion.4), channel_id=1, source_target_pairs={{0,8},{4,12},{8,0},{12,4},{1,9},{5,13},{9,1},{13,5},{2,10},{6,14},... | collective-permute-start | bytes 1867784 | tf_op jit(solution)/shard_map/ppermute | solution.py:634
  230.4 15.3 %collective-permute-start.21 = (bf16[9,32,256]{2,1,0:T(8,128)(2,1)S(1)}, bf16[9,32,256]{2,1,0:T(8,128)(2,1)S(1)}, u32[]{:S(2)}, u32[]{:S(2)}) collective-permute-start(bf16[9,32,256]{2,1,0:T(8,128)(2,1)S(1)} %select_convert_fusion.3), channel_id=1, source_target_pairs={{0,8},{4,12},{8,0},{12,4},{1,9},{5,13},{9,1},{13,5},{2,10},{6,14},... | collective-permute-start | bytes 442376 | tf_op jit(solution)/shard_map/ppermute | solution.py:634
  231.8 14.4 %collective-permute-start.31 = (bf16[19,64,256]{2,1,0:T(8,128)(2,1)S(1)}, bf16[19,64,256]{2,1,0:T(8,128)(2,1)S(1)}, u32[]{:S(2)}, u32[]{:S(2)}) collective-permute-start(bf16[19,64,256]{2,1,0:T(8,128)(2,1)S(1)} %pad_maximum_fusion.3), channel_id=1, source_target_pairs={{0,4},{4,0},{8,12},{12,8},{1,5},{5,1},{9,13},{13,9},{2,6},{6,2},{1... | collective-permute-start | bytes 1867784 | tf_op jit(solution)/shard_map/ppermute | solution.py:634
  233.4 14.3 %collective-permute-start.22 = (bf16[9,32,256]{2,1,0:T(8,128)(2,1)S(1)}, bf16[9,32,256]{2,1,0:T(8,128)(2,1)S(1)}, u32[]{:S(2)}, u32[]{:S(2)}) collective-permute-start(bf16[9,32,256]{2,1,0:T(8,128)(2,1)S(1)} %select_convert_fusion.2), channel_id=1, source_target_pairs={{0,4},{4,0},{8,12},{12,8},{1,5},{5,1},{9,13},{13,9},{2,6},{6,2},{1... | collective-permute-start | bytes 442376 | tf_op jit(solution)/shard_map/ppermute | solution.py:634
  247.0 47.1 %collective-permute-start.34 = (bf16[19,256,256]{2,1,0:T(8,128)(2,1)S(1)}, bf16[19,256,256]{2,1,0:T(8,128)(2,1)}, u32[]{:S(2)}, u32[]{:S(2)}) collective-permute-start(bf16[19,256,256]{2,1,0:T(8,128)(2,1)S(1)} %pad_maximum_fusion.half), channel_id=1, source_target_pairs={{0,16},{16,0},{1,17},{17,1},{2,18},{18,2},{3,19},{19,3},{4,20},{20... | collective-permute-start | bytes 7471112 | tf_op jit(solution)/shard_map/ppermute | solution.py:634
  247.8 17.4 %collective-permute-start.24 = (bf16[18,32,256]{2,1,0:T(8,128)(2,1)S(1)}, bf16[18,32,256]{2,1,0:T(8,128)(2,1)S(1)}, u32[]{:S(2)}, u32[]{:S(2)}) collective-permute-start(bf16[18,32,256]{2,1,0:T(8,128)(2,1)S(1)} %pad_maximum_fusion.5), channel_id=1, source_target_pairs={{0,2},{1,3},{2,0},{3,1},{4,6},{5,7},{6,4},{7,5},{8,10},{9,11},{10,... | collective-permute-start | bytes 884744 | tf_op jit(solution)/shard_map/ppermute | solution.py:634
  247.9 17.3 %collective-permute-start.23 = (bf16[18,32,256]{2,1,0:T(8,128)(2,1)S(1)}, bf16[18,32,256]{2,1,0:T(8,128)(2,1)S(1)}, u32[]{:S(2)}, u32[]{:S(2)}) collective-permute-start(bf16[18,32,256]{2,1,0:T(8,128)(2,1)S(1)} %pad_maximum_fusion.5), channel_id=1, source_target_pairs={{0,1},{1,0},{2,3},{3,2},{4,5},{5,4},{6,7},{7,6},{8,9},{9,8},{10,11... | collective-permute-start | bytes 884744 | tf_op jit(solution)/shard_map/ppermute | solution.py:634
  252.9 19.2 %collective-permute-start.25 = (bf16[18,32,256]{2,1,0:T(8,128)(2,1)S(1)}, bf16[18,32,256]{2,1,0:T(8,128)(2,1)S(1)}, u32[]{:S(2)}, u32[]{:S(2)}) collective-permute-start(bf16[18,32,256]{2,1,0:T(8,128)(2,1)S(1)} %pad_maximum_fusion.5), channel_id=1, source_target_pairs={{0,3},{1,2},{2,1},{3,0},{4,7},{5,6},{6,5},{7,4},{8,11},{9,10},{10,... | collective-permute-start | bytes 884744 | tf_op jit(solution)/shard_map/ppermute | solution.py:634
  272.4 5.4 %collective-permute-start.26 = (bf16[9,32,256]{2,1,0:T(8,128)(2,1)S(1)}, bf16[9,32,256]{2,1,0:T(8,128)(2,1)S(1)}, u32[]{:S(2)}, u32[]{:S(2)}) collective-permute-start(bf16[9,32,256]{2,1,0:T(8,128)(2,1)S(1)} %get-tuple-element.190), channel_id=1, source_target_pairs={{0,8},{4,12},{8,0},{12,4},{1,9},{5,13},{9,1},{13,5},{2,10},{6,14},... | collective-permute-start | bytes 442376 | tf_op jit(solution)/shard_map/ppermute | solution.py:634
  274.2 5.1 %collective-permute-start.28 = (bf16[9,32,256]{2,1,0:T(8,128)(2,1)S(1)}, bf16[9,32,256]{2,1,0:T(8,128)(2,1)S(1)}, u32[]{:S(2)}, u32[]{:S(2)}) collective-permute-start(bf16[9,32,256]{2,1,0:T(8,128)(2,1)S(1)} %get-tuple-element.191), channel_id=1, source_target_pairs={{0,4},{4,0},{8,12},{12,8},{1,5},{5,1},{9,13},{13,9},{2,6},{6,2},{1... | collective-permute-start | bytes 442376 | tf_op jit(solution)/shard_map/ppermute | solution.py:634
  280.8 7.7 %collective-permute-start.29 = (bf16[9,64,256]{2,1,0:T(8,128)(2,1)}, bf16[9,64,256]{2,1,0:T(8,128)(2,1)}, u32[]{:S(2)}, u32[]{:S(2)}) collective-permute-start(bf16[9,64,256]{2,1,0:T(8,128)(2,1)} %pad_maximum_fusion.7), channel_id=1, source_target_pairs={{0,8},{4,12},{8,0},{12,4},{1,9},{5,13},{9,1},{13,5},{2,10},{6,14},... | collective-permute-start | bytes 884744 | tf_op jit(solution)/shard_map/ppermute | solution.py:634
  282.2 7.7 %collective-permute-start.27 = (bf16[9,64,256]{2,1,0:T(8,128)(2,1)}, bf16[9,64,256]{2,1,0:T(8,128)(2,1)}, u32[]{:S(2)}, u32[]{:S(2)}) collective-permute-start(bf16[9,64,256]{2,1,0:T(8,128)(2,1)} %pad_maximum_fusion.6), channel_id=1, source_target_pairs={{0,4},{4,0},{8,12},{12,8},{1,5},{5,1},{9,13},{13,9},{2,6},{6,2},{1... | collective-permute-start | bytes 884744 | tf_op jit(solution)/shard_map/ppermute | solution.py:634
  301.1 3.0 collective-permute-start.35
  (10 other events, 40.6 us)
where the time goes:
time: 310 us; the launch traced here: 307 us
  waiting for transfers between devices  147 us (47%)
  Pallas kernels  77.4 us (25%)
  starting transfers between devices  61.6 us (20%)
  other arithmetic  11 us (4%)
  local copies, waits for them, and re-layouts  6.8 us (2%)
    ppermute x29, waiting for transfers between devices, partner(): return lax.ppermute(value, axis, [(i, i ^ step) for i in range(count)])  104 us
    pallas_call x11, Pallas kernels, call(): pl.pallas_call(run, out_shape=list(outs.values()), in_specs=[spec(n) for...  65.4 us
    all_to_all x4, waiting for transfers between devices, gather_sum(): return lax.all_to_all(spread, axes, 0, 0)  27.3 us
    ppermute x29, starting transfers between devices, partner(): return lax.ppermute(value, axis, [(i, i ^ step) for i in range(count)])  26 us
    ppermute x6, starting transfers between devices, shifted(): lax.ppermute(value, axis, [(source, source + steps) for source in range(f...  18.3 us
    all_to_all x4, starting transfers between devices, gather_sum(): return lax.all_to_all(spread, axes, 0, 0)  17.2 us
    ppermute x6, waiting for transfers between devices, shifted(): lax.ppermute(value, axis, [(source, source + steps) for source in range(f...  15.7 us
    pallas_call x4, Pallas kernels, widen(): pl.pallas_call(widen_kernel, out_shape=shape((taps, n, 2 * m)), grid_spec...  12.1 us
  transfers between devices with their start and end apart: 40, of which 25 were waited for; matrix products, arithmetic and copies ran while one was open for 4% of the time, Pallas kernels for 17%

commit v1 on v0

--- a/solution.py
+++ b/solution.py
@@ -35,7 +35,7 @@
             self.jobs[name].wait()
 
 
-def call(body, ins, outs, scratch=None, far_in=(), far_out=(), smem=(), flops=0, moved=0, limit=52):
+def call(body, ins, outs, scratch=None, far_in=(), far_out=(), smem=(), limit=52):
     scratch = scratch or {}
     far = (*far_in, *far_out)
 
@@ -119,42 +119,101 @@
     return [(at, min(size, total - at)) for at in range(0, total, size)]
 
 
-def assemble(raw, flags, own, top, bot, left, right, first, last, put):
-    n_top, n_own, groups = own.n_top, own.n_own, own.groups
-    for r in range(first, last):
+def strided(ref, k, first, count, step):
+    return ref[k, pl.ds(first, count, stride=step), :]
+
+
+def vertical_kernel(r, copies):
+    groups, width = r.x.shape[0], r.cot.shape[3]
+    rows, cols = r.own.shape[1], r.own.shape[2]
+
+    def pack(out, input_row, row, pick):
+        at = 0
         for g in range(groups):
-            if r < n_top:
-                src = jnp.where(flags[0] == 1, top(g, r).astype(f32), 0.0)
-            elif r < n_top + n_own:
-                src = own(g, r - n_top).astype(f32)
-            else:
-                src = jnp.where(flags[1] == 1, bot(g, r - n_top - n_own).astype(f32), 0.0)
-            line = (r - first) * groups + g
-            sides = left(g, r).astype(f32), right(g, r).astype(f32)
-            edge, cols = sides[0].shape[0], src.shape[0]
-            pieces = ((0, sides[0]), (edge, src), (edge + cols, sides[1]))
-            for at, value in pieces:
-                for k in range(raw.shape[0]):
-                    step = raw.shape[3]
-                    raw[k, line, at : at + value.shape[0], :] = value[:, k * step : (k + 1) * step]
-            put(r, g, line)
-
-
-class Rows:
-    def __init__(self, read, groups, n_top, n_own):
-        self.read, self.groups, self.n_top, self.n_own = read, groups, n_top, n_own
-
-    def __call__(self, g, r):
-        return self.read(g, r)
-
-
-def flat_row(ref, base, n, cols):
-    return lambda g, r: ref[base + (g * n + r) * cols : base + (g * n + r + 1) * cols, :]
-
-
-def flat_pair(ref, base, n, cols, size):
-    low, high = flat_row(ref, base, n, cols), flat_row(ref, base + size, n, cols)
-    return lambda g, r: jnp.concatenate([low(g, r), high(g, r)], axis=1)
+            for n in range(over):
+                value = r.x[g, input_row(n)]
+                out[at : at + 2 * cols, :] = pick(value, r.x[g, n])
+                at += 2 * cols
+        for k in range(0, width, 256):
+            for g in range(groups):
+                for n in range(rim):
+                    lanes = slice(k, k + 256)
+                    out[at : at + cols, :] = pick(r.cot[g, row(n), :, lanes], r.cot[g, n, :, lanes])
+                    at += cols
+        for g in range(groups):
+            for n in range(rim):
+                out[at : at + cols, :] = pick(wide(r.own[g, row(n)], 256), wide(r.own[g, n], 256))
+                at += cols
+
+    last = r.x.shape[1] - over
+    if hasattr(r, "up"):
+        pack(r.down, lambda n: last + n, lambda n: rows - rim + n, lambda tail, head: tail)
+        pack(r.up, lambda n: last + n, lambda n: rows - rim + n, lambda tail, head: head)
+    else:
+        bottom = r.flags[0] == 1
+        pack(r.down, lambda n: last + n, lambda n: rows - rim + n, lambda tail, head: jnp.where(bottom, head, tail))
+
+
+def rim_rows(r, own, n_own, n_rim, base, cols, split):
+    groups = own.shape[0]
+    size = groups * n_rim * cols
+
+    def flat(ref, g, n):
+        at = [base + k * size + (g * n_rim + n) * cols for k in range(split)]
+        return jnp.concatenate([ref[p : p + cols, :] for p in at], axis=1).astype(f32)
+
+    def read(g, n):
+        if n < n_rim:
+            return jnp.where(r.flags[0] == 1, flat(r.top, g, n), 0.0)
+        if n < n_rim + n_own:
+            return own[g, n - n_rim].astype(f32)
+        return jnp.where(r.flags[1] == 1, flat(r.bot, g, n - n_rim - n_own), 0.0)
+
+    return read
+
+
+def fields(r):
+    groups, width = r.x.shape[0], r.cot.shape[3]
+    rows, cols = r.own.shape[1], r.own.shape[2]
+    base = over * groups * 2 * cols
+    piece = rim * groups * cols
+    blocks = width // 256
+    x = rim_rows(r, r.x, 2 * rows, over, 0, 2 * cols, 1)
+    mask = rim_rows(r, r.own, rows, rim, base + blocks * piece, cols, 1)
+    cot = rim_rows(r, r.cot, rows, rim, base, cols, blocks)
+    return x, lambda g, n: mask(g, n)[:, :128], cot
+
+
+def strips_kernel(r, copies):
+    groups, width = r.x.shape[0], r.cot.shape[3]
+    rows, cols = r.own.shape[1], r.own.shape[2]
+    x, mask, cot = fields(r)
+    lines = (2 * rows + 2 * over) * groups, (rows + 2 * rim) * groups, (rows + 3) * groups
+    for raw, read, first, count, w in (
+        (r.raw_x, x, 0, lines[0], 2 * cols),
+        (r.raw_m, mask, 0, lines[1], cols),
+        (r.raw_c, cot, 2, lines[2], cols),
+    ):
+        for at in range(count):
+            value = read(at % groups, at // groups + first)
+            for k in range(raw.shape[0]):
+                raw[k, at * w : (at + 1) * w, :] = value[:, k * 128 : (k + 1) * 128]
+    for out, x0, m0, c0 in ((r.right, 2 * cols - over, cols - rim, cols - 2), (r.left, 0, 0, 0)):
+        pieces = []
+        for c in range(over):
+            pieces.append([strided(r.raw_x, k, x0 + c, lines[0], 2 * cols) for k in range(2)])
+        for c in range(0, rim + 1, 2):
+            pieces.append([strided(r.raw_m, 0, m0 + min(c + k, rim - 1), lines[1], cols) for k in range(2)])
+        for c in range(2):
+            for h in range(0, width // 128, 2):
+                pieces.append([strided(r.raw_c, h + k, c0 + c, lines[2], cols) for k in range(2)])
+        at = 0
+        for low, high in pieces:
+            r.flat[at : at + low.shape[0], :] = jnp.concatenate([low, high], axis=1)
+            at += low.shape[0]
+        if at < r.flat.shape[0]:
+            r.flat[at:, :] = jnp.zeros((r.flat.shape[0] - at, 256), f32)
+        out[...] = r.flat[...].astype(bf16)
 
 
 def stats_kernel(r, copies):
@@ -192,49 +251,73 @@
     z += matmul(r.xo[L : L + M, :], r.w1[2])
     zp = matmul(r.xe[:, cin : 2 * cin], r.wp[...])
     zm, zpm = z * wide(mask, width), zp * wide(mask, width)
-    row = jnp.concatenate([column_sum(zm), column_sum(zm * z), column_sum(mask)], axis=1)
+    row = jnp.concatenate(
+        [column_sum(zm), column_sum(zm * z), column_sum(zpm), column_sum(zpm * zp), column_sum(mask)], axis=1
+    )
     r.spread[...] = jnp.broadcast_to(row[None], r.spread.shape)
-    r.psum[...] = jnp.concatenate([column_sum(zpm), column_sum(zpm * zp)], axis=1)
 
 
 def first_kernel(r, copies):
-    groups, cin = r.x.shape[0], r.x.shape[3]
+    groups, cin, width = r.x.shape[0], r.x.shape[3], r.cot.shape[3]
     rows, cols = r.own.shape[1], r.own.shape[2]
     S = cols + 8
     L = groups * S
-    raw = r.raw
-    end = 16 + r.x.shape[2]
-    total_rows = r.x.shape[1] + 2 * over
-
-    def put(n, g, line):
-        for k in range(raw.shape[0]):
-            raw[k, line, end:, :] = jnp.zeros((raw.shape[2] - end, 128), f32)
-
-    assemble(
-        raw,
-        r.flags,
-        Rows(lambda g, n: r.x[g, n], groups, over, r.x.shape[1]),
-        flat_row(r.top, 0, over, r.x.shape[2]),
-        flat_row(r.bot, 0, over, r.x.shape[2]),
-        lambda g, n: r.lft[g, n],
-        lambda g, n: r.rgt[g, n],
-        0,
-        total_rows,
-        put,
-    )
+    W = 2 * cols + 24
+    V = cols + 16
+    x, mask, cot = fields(r)
+    lines = (2 * rows + 2 * over) * groups, (rows + 2 * rim) * groups, (rows + 3) * groups
+    tail = jnp.zeros((W - 8 - 2 * cols, 128), f32)
+    r.raw_m[...] = jnp.zeros(r.raw_m.shape, f32)
+    r.raw_c[...] = jnp.zeros(r.raw_c.shape, f32)
+    for at in range(lines[0]):
+        value = x(at % groups, at // groups)
+        for k in range(r.raw_x.shape[0]):
+            r.raw_x[k, at * W + 8 : at * W + 8 + 2 * cols, :] = value[:, k * 128 : (k + 1) * 128]
+            r.raw_x[k, at * W + 8 + 2 * cols : (at + 1) * W, :] = tail
+    for strip, x0, m0, c0 in ((r.lft, 8 - over, 8 - rim, 6), (r.rgt, 8 + 2 * cols, 8 + cols, 8 + cols)):
+        r.flat[...] = strip[...].astype(f32)
+        at = 0
+        for c in range(over):
+            for k in range(2):
+                r.raw_x[k, pl.ds(x0 + c, lines[0], stride=W), :] = r.flat[at : at + lines[0], k * 128 : (k + 1) * 128]
+            at += lines[0]
+        for c in range(0, rim + 1, 2):
+            for k in range(2):
+                if c + k < rim:
+                    r.raw_m[0, pl.ds(m0 + c + k, lines[1], stride=V), :] = r.flat[
+                        at : at + lines[1], k * 128 : (k + 1) * 128
+                    ]
+            at += lines[1]
+        for c in range(2):
+            for h in range(0, width // 128, 2):
+                for k in range(2):
+                    r.raw_c[h + k, pl.ds(c0 + c, lines[2], stride=V), :] = r.flat[
+                        at : at + lines[2], k * 128 : (k + 1) * 128
+                    ]
+                at += lines[2]
     for out, n_rows, start in ((r.xe, rows + 5, 2), (r.xo, rows + 6, 1)):
         for n in range(n_rows):
             for b in range(3):
-                for k in range(raw.shape[0]):
+                for k in range(r.raw_x.shape[0]):
                     parts = [
-                        raw[k, (2 * n + start) * groups + g, pl.ds(3 + b, S, stride=2), :]
-                        for g in range(groups)
+                        strided(r.raw_x, k, ((2 * n + start) * groups + g) * W + 3 + b, S, 2) for g in range(groups)
                     ]
                     at = b * cin + k * 128
-                    out[n * L : (n + 1) * L, at : at + 128] = jnp.concatenate(
-                        parts, axis=0
-                    ).astype(bf16)
+                    out[n * L : (n + 1) * L, at : at + 128] = jnp.concatenate(parts, axis=0).astype(bf16)
     copies.start("xe", "xo")
+    for at in range(lines[1]):
+        r.raw_m[0, at * V + 8 : at * V + 8 + cols, :] = mask(at % groups, at // groups)
+    for n in range(1, rows + 6):
+        for g in range(groups):
+            to, at = (n - 1) * L + g * S, (n * groups + g) * V
+            r.maskp[to : to + S, :] = r.raw_m[0, at + 6 : at + 6 + S, :]
+    for at in range(lines[2]):
+        value = cot(at % groups, at // groups + 2)
+        for k in range(r.raw_c.shape[0]):
+            lanes = slice(k * 128, (k + 1) * 128)
+            r.raw_c[k, at * V + 8 : at * V + 8 + cols, :] = value[:, lanes]
+            r.cotq[at * S : (at + 1) * S, lanes] = r.raw_c[k, at * V + 7 : at * V + 7 + S, :]
+    copies.start("cotq")
     r.ownp[...] = jnp.zeros(r.ownp.shape, f32)
     for i in range(rows):
         for g in range(groups):
@@ -249,59 +332,16 @@
         r.prep[m0 : m0 + m, :] = matmul(r.xe[m0 : m0 + m, cin : 2 * cin], r.wp[...])
         r.keep[m0 : m0 + m, :] = z
     copies.start("keep")
-    copies.wait("xe", "xo", "keep")
-
-
-def rims_kernel(r, copies):
-    groups, rows, cols, width = r.cot.shape
-    S = cols + 8
-    L = groups * S
-    base, size = over * groups * 2 * cols, rim * groups * cols
-    lanes = slice(width, width + 128)
-
-    def put(n, g, line):
-        at = (n - 1) * L + g * S
-        r.maskp[at : at + S, :] = r.raw[0, line, 6 : 6 + S, :]
-
-    assemble(
-        r.raw,
-        r.flags,
-        Rows(lambda g, n: r.own[g, n], groups, rim, rows),
-        lambda g, n: flat_row(r.top, base + width // 256 * size, rim, cols)(g, n)[:, :128],
-        lambda g, n: flat_row(r.bot, base + width // 256 * size, rim, cols)(g, n)[:, :128],
-        lambda g, n: r.lft[g, n][:, lanes],
-        lambda g, n: r.rgt[g, n][:, lanes],
-        1,
-        rows + 6,
-        put,
-    )
-
-    def put_cot(n, g, line):
-        at = (n - 2) * L + g * S
-        r.cotq[at : at + S, :] = r.field[0, line, 7 : 7 + S, :]
-
-    assemble(
-        r.field,
-        r.flags,
-        Rows(lambda g, n: r.cot[g, n], groups, rim, rows),
-        flat_pair(r.top, base, rim, cols, size),
-        flat_pair(r.bot, base, rim, cols, size),
-        lambda g, n: r.lft[g, n][:, :width],
-        lambda g, n: r.rgt[g, n][:, :width],
-        2,
-        rows + 5,
-        put_cot,
-    )
-    copies.start("cotq")
-    copies.wait("cotq")
+    copies.wait("xe", "xo", "keep", "cotq")
 
 
 def second_kernel(r, copies):
     width = r.gain.shape[1]
     t = jnp.sum(r.tot1[...], axis=0)
-    n = wide(t[:, 2 * width :], width)
+    n = wide(t[:, 4 * width :], width)
     center, inv = moments(t[:, :width], t[:, width : 2 * width], n)
-    r.mom1[...] = jnp.concatenate([center, inv, n, jnp.zeros((5, width), f32)], axis=0)
+    proj = moments(t[:, 2 * width : 3 * width], t[:, 3 * width : 4 * width], n)
+    r.mom1[...] = jnp.concatenate([center, inv, n, *proj, jnp.zeros((3, width), f32)], axis=0)
     scale = inv * r.gain[...]
     M, Q = r.pre1.shape[0], r.pre2.shape[0]
     L = (M - Q) // 2
@@ -323,7 +363,7 @@
         r.pre2[m0 : m0 + m, :] = z
         zm = z * wide(r.ownp[L + 1 + m0 : L + 1 + m0 + m, :], width)
         sums = [sums[0] + column_sum(zm), sums[1] + column_sum(zm * z)]
-    row = jnp.concatenate([*sums, r.psum[...]], axis=1)
+    row = jnp.concatenate(sums, axis=1)
     r.spread[...] = jnp.broadcast_to(row[None], r.spread.shape)
     copies.wait("h3")
 
@@ -334,8 +374,8 @@
     L = groups * S
     n = r.mom1[2:3, :]
     t = jnp.sum(r.tot2[...], axis=0)
-    parts = [t[:, k * width : (k + 1) * width] for k in range(4)]
-    (c2, i2), (cp, ip) = moments(parts[0], parts[1], n), moments(parts[2], parts[3], n)
+    c2, i2 = moments(t[:, :width], t[:, width:], n)
+    cp, ip = r.mom1[3:4, :], r.mom1[4:5, :]
     r.mom2[...] = jnp.concatenate([c2, i2, cp, ip, jnp.zeros((4, width), f32)], axis=0)
     sums = [jnp.zeros((1, width), f32)] * 3
     both_shift = r.shift2[...] + r.shiftp[...]
@@ -583,7 +623,7 @@
         ),
         input_output_aliases={2: 0} if more else {},
         compiler_params=pltpu.CompilerParams(vmem_limit_bytes=20 * 1024 * 1024),
-        cost_estimate=pl.CostEstimate(flops=0, bytes_accessed=taps * n * m * 6, transcendentals=0),
+        cost_estimate=pl.CostEstimate(flops=0, bytes_accessed=0, transcendentals=0),
     )(side.reshape(1), half, *more)
 
 
@@ -591,34 +631,6 @@
     count = lax.axis_size(axis)
     first, last = (max(0, -steps), min(count, count - steps))
     return lax.ppermute(value, axis, [(source, source + steps) for source in range(first, last)])
-
-
-def vertical(cells, cot, own):
-    width = cot.shape[3]
-    count = lax.axis_size("rows")
-    me = lax.axis_index("rows")
-    mask = jnp.concatenate([own, own], axis=3)
-
-    def packed(ends):
-        parts = [cells[:, ends(over)], *(cot[:, ends(rim), :, k : k + 256] for k in range(0, width, 256)), mask[:, ends(rim)]]
-        return jnp.concatenate([part.reshape(-1, 256) for part in parts], axis=0)
-
-    down, up = packed(lambda n: slice(-n, None)), packed(lambda n: slice(0, n))
-    flags = jnp.stack([me > 0, me < count - 1]).astype(jnp.int32)
-    if count == 2:
-        swapped = lax.ppermute(jnp.where(me == 0, down, up), "rows", [(0, 1), (1, 0)])
-        return swapped, swapped, flags
-    return shifted(down, "rows", 1), shifted(up, "rows", -1), flags
-
-
-def horizontal(top, mid, bot, flags, edge):
-    top = jnp.where(flags[0] == 1, top, jnp.zeros_like(top))
-    bot = jnp.where(flags[1] == 1, bot, jnp.zeros_like(bot))
-    ends = [
-        jnp.concatenate([part[:, :, at] for part in (top, mid, bot)], axis=1)
-        for at in (slice(-edge, None), slice(0, edge))
-    ]
-    return shifted(ends[0], "cols", 1), shifted(ends[1], "cols", -1)
 
 
 def gather_sum(spread):
@@ -649,64 +661,76 @@
     return jnp.where(bit, low, high).astype(bf16), jnp.where(bit, high, low)
 
 
-def join(value, axis, step, dim=1):
-    other = partner(value, axis, step)
+def joined(value, other, axis, step, dim=1):
     bit = bit_of(axis, step) == 1
     return jnp.concatenate([jnp.where(bit, other, value), jnp.where(bit, value, other)], axis=dim)
 
 
 class Tree:
-    def __init__(self, parts, plane, rest):
+    def __init__(self, parts, plane, rest, core):
         self.sent_a, self.kept_a, self.sent_b, self.kept_b = parts
-        self.a, self.b = plane, plane[::-1]
-        self.rest = []
-        for axis in dict.fromkeys(axis for axis, _ in rest):
-            steps = [step for name, step in rest if name == axis]
-            self.rest += [(axis, steps[k : k + 2]) for k in range(0, len(steps), 2)]
-        self.at = 0
+        self.a, self.b, self.rest, self.core = plane, plane[::-1], rest, core
+        p, n = len(plane), len(rest)
+        self.stages = [("plane", k) for k in range(p)] + [("rest", k) for k in range(n)]
+        self.stages += [("rest_join", k) for k in reversed(range(n))] + [("plane_join", k) for k in reversed(range(p))]
+        self.stages += [("core", 0)]
+
+    def next(self):
+        return self.stages[0] if self.stages else None
 
     def start(self):
-        self.got = partner(self.sent_a, *self.a[self.at]), partner(self.sent_b, *self.b[self.at])
+        kind, k = self.stages[0]
+        if kind == "plane":
+            self.got = partner(self.sent_a, *self.a[k]), partner(self.sent_b, *self.b[k])
+        elif kind == "rest":
+            self.got = (partner(self.sent, *self.rest[k]),)
+        elif kind == "rest_join":
+            self.got = (partner(self.value, *self.rest[k]),)
+        elif kind == "plane_join":
+            self.got = partner(self.value_a, *self.a[k]), partner(self.value_b, *self.b[k])
+        else:
+            self.got = (partner(self.value, *self.core),)
 
     def finish(self, before=None):
-        total_a = self.kept_a + self.got[0].astype(f32)
-        total_b = self.kept_b + self.got[1].astype(f32)
-        self.at += 1
-        if self.at < len(self.a):
-            self.sent_a, self.kept_a = split(total_a, *self.a[self.at])
-            self.sent_b, self.kept_b = split(total_b, *self.b[self.at])
-            keep = [self.sent_a, self.kept_a, self.sent_b, self.kept_b]
-            if before is not None:
-                before, *keep = lax.optimization_barrier((before, *keep))
-            self.sent_a, self.kept_a, self.sent_b, self.kept_b = keep
+        kind, k = self.stages.pop(0)
+        if kind == "plane":
+            total_a = self.kept_a + self.got[0].astype(f32)
+            total_b = self.kept_b + self.got[1].astype(f32)
+            if k + 1 < len(self.a):
+                self.sent_a, self.kept_a = split(total_a, *self.a[k + 1])
+                self.sent_b, self.kept_b = split(total_b, *self.b[k + 1])
+                keep = self.sent_a, self.kept_a, self.sent_b, self.kept_b
+                if before is not None:
+                    before, keep = lax.optimization_barrier((before, keep))
+                self.sent_a, self.kept_a, self.sent_b, self.kept_b = keep
+            else:
+                self.taps = total_a.shape[0]
+                self.split_rest(jnp.concatenate([total_a, total_b], axis=0), 0)
+        elif kind == "rest":
+            self.split_rest(self.kept + self.got[0].astype(f32), k + 1)
+        elif kind == "rest_join":
+            self.value = joined(self.value, self.got[0], *self.rest[k])
+            self.value_a, self.value_b = self.value[: self.taps], self.value[self.taps :]
+        elif kind == "plane_join":
+            self.value_a = joined(self.value_a, self.got[0], *self.a[k])
+            self.value_b = joined(self.value_b, self.got[1], *self.b[k])
+            self.value = jnp.concatenate([self.value_a, self.value_b], axis=1)
+        return before
+
+    def split_rest(self, total, k):
+        if k < len(self.rest):
+            self.sent, self.kept = split(total, *self.rest[k])
         else:
-            self.taps = total_a.shape[0]
-            self.value = jnp.concatenate([total_a, total_b], axis=0).astype(bf16)
-            if before is not None:
-                before, self.value = lax.optimization_barrier((before, self.value))
-        return before
-
-    def exchange(self, k, part=slice(None)):
-        axis, steps = self.rest[k]
-        got = [] if part.start is None or part.start == 0 else self.got
-        self.got = got + [partner(self.value, axis, m * steps[0]) for m in range(1, 2 ** len(steps))[part]]
-
-    def gathered(self):
-        parts = [v.astype(f32) for v in (self.value, *self.got)]
-        while len(parts) > 1:
-            parts = [parts[k] + parts[k + 1] for k in range(0, len(parts), 2)]
-        self.value = parts[0].astype(bf16)
-
-    def join(self):
-        a, b = self.value[: self.taps], self.value[self.taps :]
-        for at in reversed(range(len(self.a))):
-            a, b = join(a, *self.a[at]), join(b, *self.b[at])
-        return jnp.concatenate([a, b], axis=1)
-
-    def rest_from(self, k):
-        for k in range(k, len(self.rest)):
-            self.exchange(k)
-            self.gathered()
+            self.value = total.astype(bf16)
+
+
+def lockstep(*trees):
+    for t in trees:
+        t.start()
+    got = lax.optimization_barrier([t.got for t in trees])
+    for t, g in zip(trees, got):
+        t.got = g
+        t.finish()
 
 
 def on_device(inputs, w_first, gain_first, shift_first, w_second, gain_second, shift_second, w_proj, gain_proj, shift_proj, valid_mask, cotangent):
@@ -738,27 +762,48 @@
     stats = call(
         stats_kernel,
         dict(x=inputs, top=top1, lft=lft1, own=own, w1=w1, wp=w_proj),
-        dict(spread=all_devices(2 * width + 128), psum=vec(2)),
+        dict(spread=all_devices(4 * width + 128)),
         dict(
             raw=pltpu.VMEM((cin // 128, (rows_in + 1) * groups, cols_in + 8, 128), f32),
             xe=pltpu.VMEM((rows * groups * cols, 3 * cin), bf16),
             xo=pltpu.VMEM(((rows + 1) * groups * cols, 3 * cin), bf16),
         ),
-        flops=px(rows * groups * cols, 10 * cin),
-        moved=4_000_000,
-    )
-    spread1 = stats["spread"]
-    tot1 = gather_sum(spread1)
-
-    wide_inputs, _ = lax.optimization_barrier((inputs, top1))
-    top, bot, flags = vertical(wide_inputs, cotangent, own)
-    flat = over * groups * cols_in
-    lft, rgt = horizontal(
-        top[:flat].reshape(groups, over, cols_in, cin), inputs, bot[:flat].reshape(groups, over, cols_in, cin), flags, 8
-    )
+    )
+    tot1 = gather_sum(stats["spread"])
+
+    me, count = lax.axis_index("rows"), lax.axis_size("rows")
+    flags = jnp.stack([me > 0, me < count - 1]).astype(jnp.int32)
+    flat_rows = shape((over * groups * cols_in + (width // 256 + 1) * rim * groups * cols, 256), bf16)
+    packed = call(
+        vertical_kernel,
+        dict(flags=flags, x=inputs, cot=cotangent, own=own),
+        dict(down=flat_rows) if count == 2 else dict(down=flat_rows, up=flat_rows),
+        smem=("flags",),
+    )
+    if count == 2:
+        top = bot = lax.ppermute(packed["down"], "rows", [(0, 1), (1, 0)])
+    else:
+        top, bot = shifted(packed["down"], "rows", 1), shifted(packed["up"], "rows", -1)
+    lines = (rows_in + 2 * over) * groups, (rows + 2 * rim) * groups, (rows + 3) * groups
+    n_strip = over * lines[0] + (rim + 1) // 2 * lines[1] + width // 128 * lines[2]
+    n_strip = -(-n_strip // 16) * 16
+    near = dict(flags=flags, x=inputs, cot=cotangent, own=own, top=top, bot=bot)
+    strips = call(
+        strips_kernel,
+        near,
+        dict(right=shape((n_strip, 256), bf16), left=shape((n_strip, 256), bf16)),
+        dict(
+            raw_x=pltpu.VMEM((cin // 128, lines[0] * cols_in, 128), f32),
+            raw_m=pltpu.VMEM((1, lines[1] * cols, 128), f32),
+            raw_c=pltpu.VMEM((width // 128, lines[2] * cols, 128), f32),
+            flat=pltpu.VMEM((n_strip, 256), f32),
+        ),
+        smem=("flags",),
+    )
+    lft, rgt = shifted(strips["right"], "cols", 1), shifted(strips["left"], "cols", -1)
     first = call(
         first_kernel,
-        dict(flags=flags, x=inputs, top=top, bot=bot, lft=lft, rgt=rgt, own=own, w1=w1, wp=w_proj),
+        dict(**near, lft=lft, rgt=rgt, w1=w1, wp=w_proj),
         dict(
             pre1=shape((MP, width)),
             prep=shape((MP, width)),
@@ -766,53 +811,29 @@
             xo=shape((MP + L, 3 * cin), bf16),
             keep=shape((MP, width)),
             ownp=shape((MP, 128)),
-        ),
-        dict(raw=pltpu.VMEM((cin // 128, (rows_in + 12) * groups, cols_in + 24, 128), f32)),
+            maskp=shape((MP, 128)),
+            cotq=shape((MQ, width)),
+        ),
+        dict(
+            raw_x=pltpu.VMEM((cin // 128, lines[0] * (cols_in + 24), 128), f32),
+            raw_m=pltpu.VMEM((1, lines[1] * (cols + 16), 128), f32),
+            raw_c=pltpu.VMEM((width // 128, lines[2] * (cols + 16), 128), f32),
+            flat=pltpu.VMEM((n_strip, 256), f32),
+        ),
         far_in=("w1", "wp"),
-        far_out=("xe", "xo", "keep"),
+        far_out=("xe", "xo", "keep", "cotq"),
         smem=("flags",),
-        flops=px(MP, 10 * cin),
-        moved=10_000_000,
-    )
-    xe, xo, ownp = first["xe"], first["xo"], first["ownp"]
-    piece = rim * groups * cols
-
-    def rows_of(flat_rim):
-        parts = [
-            flat_rim[flat + k * piece : flat + (k + 1) * piece].reshape(groups, rim, cols, 256)
-            for k in range(width // 256 + 1)
-        ]
-        return jnp.concatenate(parts[:-1] + [parts[-1][..., :128]], axis=3)
-
-    cot_here, _ = lax.optimization_barrier((cotangent, spread1))
-    clft, crgt = horizontal(
-        rows_of(top), jnp.concatenate([cot_here, own], axis=3), rows_of(bot), flags, 8
-    )
-    rims = call(
-        rims_kernel,
-        dict(flags=flags, own=own, cot=cotangent, top=top, bot=bot, lft=clft, rgt=crgt),
-        dict(maskp=shape((MP, 128)), cotq=shape((MQ, width))),
-        dict(
-            raw=pltpu.VMEM((1, (rows + 5) * groups, cols + 16, 128), f32),
-            field=pltpu.VMEM((1, (rows + 3) * groups, cols + 16, width), f32),
-        ),
-        far_out=("cotq",),
-        smem=("flags",),
-        flops=MQ * width * 4,
-        moved=4_000_000,
-    )
-    maskp = rims["maskp"]
+    )
+    xe, xo, ownp, maskp = first["xe"], first["xo"], first["ownp"], first["maskp"]
     far_xe, far_xo = partner(xe, *core), partner(xo, *core)
 
     second = call(
         second_kernel,
-        dict(pre1=first["pre1"], tot1=tot1, gain=g1, shift=b1, maskp=maskp, ownp=ownp, psum=stats["psum"], w2=w2),
-        dict(h3=shape((MP, 3 * width), bf16), pre2=shape((MQ, width)), spread=all_devices(4 * width), mom1=shape((8, width))),
+        dict(pre1=first["pre1"], tot1=tot1, gain=g1, shift=b1, maskp=maskp, ownp=ownp, w2=w2),
+        dict(h3=shape((MP, 3 * width), bf16), pre2=shape((MQ, width)), spread=all_devices(2 * width), mom1=shape((8, width))),
         dict(hid=pltpu.VMEM((MP + 8, width), f32)),
         far_in=("w2",),
         far_out=("h3",),
-        flops=px(MQ, 9 * width),
-        moved=10_000_000,
     )
     h3, pre2, mom1 = second["h3"], second["pre2"], second["mom1"]
     tot2 = gather_sum(second["spread"])
@@ -822,7 +843,7 @@
         third_kernel,
         dict(
             pre2=pre2, prep=first["prep"], mom1=mom1, tot2=tot2, gain2=g2, shift2=b2, gainp=gp, shiftp=bp,
-            maskp=maskp, ownp=ownp, cotq=rims["cotq"],
+            maskp=maskp, ownp=ownp, cotq=first["cotq"],
         ),
         dict(
             out=shape((groups, rows, cols, width), bf16),
@@ -833,8 +854,6 @@
         dict(field=pltpu.VMEM((MQ, width), f32)),
         far_in=("cotq",),
         far_out=("out", "grad"),
-        flops=MQ * width * 60,
-        moved=5_000_000,
     )
     mom2 = third["mom2"]
     tot3 = gather_sum(third["spread"])
@@ -856,8 +875,6 @@
         far_in=("grad",),
         far_out=("gpu",),
         smem=("bits",),
-        flops=MQ * width * 40,
-        moved=6_000_000,
     )
     far2 = partner(fourth["theirs"], *core)
 
@@ -874,12 +891,10 @@
         far_in=("h3", "h3_far", "xe", "xe_far"),
         far_out=("kept_a", "kept_b"),
         smem=("bits",),
-        flops=2 * 9 * width * half * 2 * MW,
-        moved=8_000_000,
     ).values()
     gq, *second_parts = lax.optimization_barrier((fourth["gq"], *second_parts))
 
-    tree2 = Tree(second_parts, plane, rest)
+    tree2 = Tree(second_parts, plane, rest, core)
     tree2.start()
     hidden = call(
         hidden_kernel,
@@ -887,8 +902,6 @@
         dict(act=shape((MU, width)), normed=shape((MU, width)), spread=all_devices(2 * width)),
         dict(g3=pltpu.VMEM((MQ, 3 * width), bf16)),
         far_in=("w2", "keep"),
-        flops=px(MU, 9 * width),
-        moved=10_000_000,
     )
     spread4 = tree2.finish(hidden["spread"])
     tot4 = gather_sum(spread4)
@@ -896,7 +909,7 @@
     tot4, tree2.got = lax.optimization_barrier((tot4, tree2.got))
     act = tree2.finish(hidden["act"])
 
-    tree2.exchange(0, slice(0, 1))
+    tree2.start()
     fifth = call(
         fifth_kernel,
         dict(
@@ -908,8 +921,6 @@
         dict(gf=pltpu.VMEM((MU + 16, width), f32)),
         far_out=("gu",),
         smem=("bits",),
-        flops=MU * width * 20,
-        moved=4_000_000,
     )
     far1 = partner(fifth["theirs"], *core)
     first_parts = call(
@@ -920,18 +931,11 @@
         far_in=("xe", "xo", "xe_far", "xo_far"),
         far_out=("kept_a", "kept_b"),
         smem=("bits",),
-        flops=2 * 9 * cin * half * 2 * MW,
-        moved=6_000_000,
     ).values()
     gu, tree2.got, *first_parts = lax.optimization_barrier((fifth["gu"], tree2.got, *first_parts))
-    tree2.exchange(0, slice(1, None))
-    tree1 = Tree(first_parts, plane, rest)
-    tree1.start()
-    tree2.got = tree1.finish(tree2.got)
-    tree1.start()
-    tree1.finish()
-    tree2.gathered()
-    tree2.rest_from(1)
+    tree2.finish()
+    tree1 = Tree(first_parts, plane, rest, core)
+
     grad_inputs = call(
         inputs_kernel,
         dict(gu=gu, gpu=fourth["gpu"], w1=w1, wp=w_proj),
@@ -939,25 +943,33 @@
         dict(lines=pltpu.VMEM((cin // 128, rows_in * groups, cols_in, 128), f32)),
         far_in=("gu", "gpu", "w1", "wp"),
         far_out=("out",),
-        flops=px(MW, 10 * cin),
-        moved=5_000_000,
     )["out"]
-    tree1.exchange(0)
-    tree1.gathered()
-    tree1.rest_from(1)
-    tree1.value, grad_inputs = lax.optimization_barrier((tree1.value, grad_inputs))
-    half2 = tree2.join()
-
     side = bit_of(*core).astype(jnp.int32)
-    other2 = partner(half2, *core)
+    while tree2.next() != ("plane_join", 0):
+        lockstep(tree2, tree1)
+    tree2.start()
+    while tree1.next()[0] != "rest_join" or tree1.next()[1] > 0:
+        tree1.start()
+        tree1.finish()
+    tree1.start()
+    tree1.got, tree2.got, grad_inputs = lax.optimization_barrier((tree1.got, tree2.got, grad_inputs))
+    tree1.finish()
+    tree2.finish()
+    half2 = tree2.value
+    lockstep(tree2, tree1)
+    other2 = tree2.got[0]
     grad_w2 = widen(other2, 1 - side, taps2 - 1, widen(half2, side, taps2 - 1))
     ends = half2[taps2 - 1], other2[taps2 - 1]
     grad_wp = jnp.concatenate(
         [jnp.where(side == 1, ends[1], ends[0]), jnp.where(side == 1, ends[0], ends[1])], axis=1
     ).astype(f32)
-    half1, grad_w2, grad_wp = lax.optimization_barrier((tree1.join(), grad_w2, grad_wp))
-    other1 = partner(half1, *core)
-    grad_w1 = widen(other1, 1 - side, 9, widen(half1, side, 9))
+    while tree1.next()[0] != "core":
+        tree1.start()
+        tree1.got, grad_w2, grad_wp = lax.optimization_barrier((tree1.got, grad_w2, grad_wp))
+        tree1.finish()
+    half1 = tree1.value
+    tree1.start()
+    grad_w1 = widen(tree1.got[0], 1 - side, 9, widen(half1, side, 9))
 
     s3, s4 = fourth["sums"].reshape(3, width), fifth["sums"].reshape(2, width)
     return (

time: 310 us -> 232 us (0.75)
  waiting for transfers between devices: 147 us -> 86.1 us
  starting transfers between devices: 61.6 us -> 49.6 us
    ppermute x29 -> x31, waiting for transfers between devices: 104 us -> 47.7 us  [partner(): return lax.ppermute(value, axis, [(i, i ^ step) for i in range(count)])]
    ppermute x6 -> x4, starting transfers between devices: 18.3 us -> 11.6 us  [shifted(): lax.ppermute(value, axis, [(source, source + steps) for source in range(f...]
    ppermute x29 -> x31, starting transfers between devices: 26 us -> 21.4 us  [partner(): return lax.ppermute(value, axis, [(i, i ^ step) for i in range(count)])]
    ppermute x6 -> x4, waiting for transfers between devices: 15.7 us -> 14 us  [shifted(): lax.ppermute(value, axis, [(source, source + steps) for source in range(f...]
    pallas_call x11 -> x12, Pallas kernels: 65.4 us -> 65.9 us  [call(): pl.pallas_call(run, out_shape=list(outs.values()), in_specs=[spec(n) for...]
  transfers between devices with their start and end apart: 40 -> 40, of which waited for: 25 -> 21; matrix products, arithmetic and copies ran while one was open for 4% -> 3% of each run, Pallas kernels for 17% -> 26%
where the time goes in v1:
time: 232 us; the launch traced here: 230 us
  waiting for transfers between devices  86.1 us (37%)
  Pallas kernels  78 us (34%)
  starting transfers between devices  49.6 us (21%)
  other arithmetic  9.23 us (4%)
  local copies, waits for them, and re-layouts  5.85 us (3%)
    pallas_call x12, Pallas kernels, call(): pl.pallas_call(run, out_shape=list(outs.values()), in_specs=[spec(n) for...  65.9 us
    ppermute x31, waiting for transfers between devices, partner(): return lax.ppermute(value, axis, [(i, i ^ step) for i in range(count)])  47.7 us
    all_to_all x4, waiting for transfers between devices, gather_sum(): return lax.all_to_all(spread, axes, 0, 0)  24.4 us
    ppermute x31, starting transfers between devices, partner(): return lax.ppermute(value, axis, [(i, i ^ step) for i in range(count)])  21.4 us
    all_to_all x4, starting transfers between devices, gather_sum(): return lax.all_to_all(spread, axes, 0, 0)  16.6 us
    ppermute x4, waiting for transfers between devices, shifted(): lax.ppermute(value, axis, [(source, source + steps) for source in range(f...  14 us
    pallas_call x4, Pallas kernels, widen(): pl.pallas_call(widen_kernel, out_shape=shape((taps, n, 2 * m)), grid_spec...  12 us
    ppermute x4, starting transfers between devices, shifted(): lax.ppermute(value, axis, [(source, source + steps) for source in range(f...  11.6 us
  transfers between devices with their start and end apart: 40, of which 21 were waited for; matrix products, arithmetic and copies ran while one was open for 3% of the time, Pallas kernels for 26%

profile of v1, /device:TPU:0, one launch (start us, length us, event | category | flops | bytes accessed | tf_op | source)
XLA Modules:
  0.0 230.3 jit_solution(4633362420794074061)
XLA Ops:
  1.4 2.3 %collective-permute-start.3 = (bf16[2,1,32,256]{3,2,1,0:T(8,128)(2,1)S(1)}, bf16[2,1,32,256]{3,2,1,0:T(8,128)(2,1)S(1)}, u32[]{:S(2)}, u32[]{:S(2)}) collective-permute-start(bf16[2,1,32,256]{3,2,1,0:T(8,128)(2,1)S(1)} %slice.96), channel_id=1, source_target_pairs={{0,16},{1,17},{2,18},{3,19},{4,20},{5,21},{6,22},{7,23},{8,24},{9,... | collective-permute-start | bytes 98312 | tf_op jit(solution)/shard_map/ppermute | solution.py:633
  7.5 4.2 %collective-permute-start.4 = (bf16[2,17,1,256]{3,2,1,0:T(2,128)(2,1)S(1)}, bf16[2,17,1,256]{3,2,1,0:T(2,128)(2,1)S(1)}, u32[]{:S(2)}, u32[]{:S(2)}) collective-permute-start(bf16[2,17,1,256]{3,2,1,0:T(2,128)(2,1)S(1)} %pad_maximum_fusion.12), channel_id=1, source_target_pairs={{0,4},{4,8},{8,12},{1,5},{5,9},{9,13},{2,6},{6,10},{10,14},{3,7},{... | collective-permute-start | bytes 52232 | tf_op jit(solution)/shard_map/ppermute | solution.py:633
  11.7 1.6 collective-permute-done.4.refs_2_
  13.3 3.4 %shard_map.206 = f32[32,1,2176]{2,1,0:T(1,128)} custom-call(bf16[2,16,32,256]{3,2,1,0:T(8,128)(2,1)S(1)} %copy-done.1, bf16[2,1,32,256]{3,2,1,0:T(8,128)(2,1)S(1)} %collective-permute-done.3.refs_1_, bf16[2,17,1,256]{3,2,1,0:T(2,128)(2,1)S(1)} %collective-permute-done.4.refs_2_, bf16[2,8,16,128]{3,2,1,0:T(8,128)(2,1)S(1)} %broadcast_in_dim.2.refs_3_, ...), custom_call_target="tpu_custom_call" | custom-call | tf_op jit(solution)/shard_map/pallas_call | solution.py:68
  16.6 6.7 %all-to-all-start = ((f32[32,1,2176]{2,1,0:T(1,128)}), f32[32,1,2176]{2,1,0:T(1,128)S(1)}, u32[]{:S(2)}, u32[]{:S(2)}) async-start(f32[32,1,2176]{2,1,0:T(1,128)} %shard_map.206), calls=%async_computation | async-start | bytes 557056 | tf_op jit(solution)/shard_map/all_to_all | solution.py:637
  23.4 1.3 shard_map.204
  24.6 3.7 %collective-permute-start.1 = (bf16[480,256]{1,0:T(8,128)(2,1)S(1)}, bf16[480,256]{1,0:T(8,128)(2,1)S(1)}, u32[]{:S(2)}, u32[]{:S(2)}) collective-permute-start(bf16[480,256]{1,0:T(8,128)(2,1)S(1)} %get-tuple-element.90), channel_id=1, source_target_pairs={{0,4},{4,8},{8,12},{1,5},{5,9},{9,13},{2,6},{6,10},{10,14},{3,7},{... | collective-permute-start | bytes 737288 | tf_op jit(solution)/shard_map/ppermute | solution.py:633
  28.4 1.3 collective-permute-start.2
  29.7 5.2 %collective-permute-done.1.refs_6_ = bf16[480,256]{1,0:T(8,128)(2,1)S(1)} collective-permute-done((bf16[480,256]{1,0:T(8,128)(2,1)S(1)}, bf16[480,256]{1,0:T(8,128)(2,1)S(1)}, u32[]{:S(2)}, u32[]{:S(2)}) %collective-permute-start.1) | collective-permute-done | bytes 245792 | tf_op jit(solution)/shard_map/ppermute | solution.py:633
  34.8 7.2 %collective-permute-done.2.refs_7_ = bf16[480,256]{1,0:T(8,128)(2,1)S(1)} collective-permute-done((bf16[480,256]{1,0:T(8,128)(2,1)S(1)}, bf16[480,256]{1,0:T(8,128)(2,1)S(1)}, u32[]{:S(2)}, u32[]{:S(2)}) %collective-permute-start.2) | collective-permute-done | bytes 245792 | tf_op jit(solution)/shard_map/ppermute | solution.py:633
  42.1 7.4 %shard_map.205 = (f32[624,512]{1,0:T(8,128)}, f32[624,512]{1,0:T(8,128)}, bf16[624,768]{1,0:T(8,128)(2,1)}, bf16[672,768]{1,0:T(8,128)(2,1)}, f32[624,512]{1,0:T...) custom-call(s32[2]{0:T(128)S(1)} %add_convert_fusion.2.refs_0_, ...), custom_call_target="tpu_custom_call" | custom-call | tf_op jit(solution)/shard_map/pallas_call | solution.py:68
  49.6 8.0 %shard_map.207 = (bf16[624,1536]{1,0:T(8,128)(2,1)}, f32[528,512]{1,0:T(8,128)}, f32[32,1,1024]{2,1,0:T(1,128)}, f32[8,512]{1,0:T(8,128)S(1)}) custom-call(f32[624,512]{1,0:T(8,128)} %get-tuple-element.92.refs_0_, f32[32,1,2176]{2,1,0:T(1,128)S(1)} %all-to-all-done.refs_1_, f32[1,512]{1,0:T(1,128)S(1)} %bitcast.25, f32[1,512]{1,0:T(1,128)S(1)} %bitcast.32, ...), custom_call_target="tpu_custom_call" | custom-call | tf_op jit(solution)/shard_map/pallas_call | solution.py:68
  57.7 3.8 %all-to-all-start.1 = ((f32[32,1,1024]{2,1,0:T(1,128)}), f32[32,1,1024]{2,1,0:T(1,128)S(1)}, u32[]{:S(2)}, u32[]{:S(2)}) async-start(f32[32,1,1024]{2,1,0:T(1,128)} %get-tuple-element.98), calls=%async_computation.1 | async-start | bytes 262144 | tf_op jit(solution)/shard_map/all_to_all | solution.py:637
  61.8 7.6 %all-to-all-done.1.refs_3_ = f32[32,1,1024]{2,1,0:T(1,128)S(1)} async-done(((f32[32,1,1024]{2,1,0:T(1,128)}), f32[32,1,1024]{2,1,0:T(1,128)S(1)}, u32[]{:S(2)}, u32[]{:S(2)}) %all-to-all-start.1) | async-done | bytes 131104 | tf_op jit(solution)/shard_map/all_to_all | solution.py:637
  69.4 6.4 %shard_map.208 = (bf16[2,8,16,512]{3,2,1,0:T(8,128)(2,1)}, f32[528,512]{1,0:T(8,128)}, f32[32,1,1536]{2,1,0:T(1,128)}, f32[8,512]{1,0:T(8,128)S(1)}) custom-call(f32[528,512]{1,0:T(8,128)} %get-tuple-element.95.refs_0_.refs_1_, f32[624,512]{1,0:T(8,128)} %get-tuple-element.96.refs_1_.refs_2_, f32[8,512]{1,0:T(8,128)S(1)} %get-tuple-element.97.refs_2_.refs_3_, ...), custom_call_target="tpu_custom_call" | custom-call | tf_op jit(solution)/shard_map/pallas_call | solution.py:68
  75.8 2.8 %all-to-all-start.2 = ((f32[32,1,1536]{2,1,0:T(1,128)}), f32[32,1,1536]{2,1,0:T(1,128)S(1)}, u32[]{:S(2)}, u32[]{:S(2)}) async-start(f32[32,1,1536]{2,1,0:T(1,128)} %get-tuple-element.103), calls=%async_computation.2 | async-start | bytes 393216 | tf_op jit(solution)/shard_map/all_to_all | solution.py:637
  78.7 9.1 %all-to-all-done.2.refs_5_ = f32[32,1,1536]{2,1,0:T(1,128)S(1)} async-done(((f32[32,1,1536]{2,1,0:T(1,128)}), f32[32,1,1536]{2,1,0:T(1,128)S(1)}, u32[]{:S(2)}, u32[]{:S(2)}) %all-to-all-start.2) | async-done | bytes 196640 | tf_op jit(solution)/shard_map/all_to_all | solution.py:637
  87.8 5.4 %shard_map.209 = (bf16[768,256]{1,0:T(8,128)(2,1)S(1)}, bf16[768,256]{1,0:T(8,128)(2,1)S(1)}, f32[536,512]{1,0:T(8,128)}, bf16[384,512]{1,0:T(8,128)(2,1)}, f32[1,1536]{1,0:T(1,128)S(1)}) custom-call(s32[3]{0:T(128)S(1)} %pad_add_fusion.refs_0_, f32[528,512]{1,0:T(8,128)} %get-tuple-element.95.refs_0_.refs_1_, f32[624,512]{1,0:T(8,128)} %get-tuple-element.96.refs_1_.refs_2_, ...), custom_call_target="tpu_custom_call" | custom-call | tf_op jit(solution)/shard_map/pallas_call | solution.py:68
  93.3 1.7 collective-permute-done.7.refs_6_
  95.0 8.5 %shard_map.210 = (bf16[19,64,256]{2,1,0:T(8,128)(2,1)S(1)}, f32[19,64,256]{2,1,0:T(8,128)}, bf16[19,64,256]{2,1,0:T(8,128)(2,1)}, f32[19,64,256]{2,1,0:T(8,128)}) custom-call(s32[3]{0:T(128)S(1)} %pad_add_fusion.refs_0_, bf16[624,1536]{1,0:T(8,128)(2,1)} %get-tuple-element.106.refs_1_, bf16[624,1536]{1,0:T(8,128)(2,1)} %collective-permute-done.5.refs_2_, ...), custom_call_target="tpu_custom_call" | custom-call | tf_op jit(solution)/shard_map/pallas_call | solution.py:68
  104.6 10.8 %shard_map.211 = (f32[432,512]{1,0:T(8,128)S(1)}, f32[432,512]{1,0:T(8,128)}, f32[32,1,1024]{2,1,0:T(1,128)}) custom-call(bf16[3,1536,512]{2,1,0:T(8,128)(2,1)} %bitcast.41, f32[624,512]{1,0:T(8,128)} %get-tuple-element.101.refs_1_, f32[8,512]{1,0:T(8,128)S(1)} %get-tuple-element.97.refs_2_.refs_3_, f32[1,512]{1,0:T(1,128)S(1)} %bitcast.26, ...), custom_call_target="tpu_custom_call" | custom-call | tf_op jit(solution)/shard_map/pallas_call | solution.py:68
  115.4 4.5 %collective-permute-done.9 = bf16[19,64,256]{2,1,0:T(8,128)(2,1)S(1)} collective-permute-done((bf16[19,64,256]{2,1,0:T(8,128)(2,1)}, bf16[19,64,256]{2,1,0:T(8,128)(2,1)S(1)}, u32[]{:S(2)}, u32[]{:S(2)}) %collective-permute-start.9) | collective-permute-done | bytes 622624 | tf_op jit(solution)/shard_map/ppermute | solution.py:646
  123.8 3.4 %all-to-all-start.3 = ((f32[32,1,1024]{2,1,0:T(1,128)}), f32[32,1,1024]{2,1,0:T(1,128)S(1)}, u32[]{:S(2)}, u32[]{:S(2)}) async-start(f32[32,1,1024]{2,1,0:T(1,128)} %get-tuple-element.122), calls=%async_computation.3 | async-start | bytes 262144 | tf_op jit(solution)/shard_map/all_to_all | solution.py:637
  127.2 7.7 %all-to-all-done.3.refs_4_ = f32[32,1,1024]{2,1,0:T(1,128)S(1)} async-done(((f32[32,1,1024]{2,1,0:T(1,128)}), f32[32,1,1024]{2,1,0:T(1,128)S(1)}, u32[]{:S(2)}, u32[]{:S(2)}) %all-to-all-start.3) | async-done | bytes 131104 | tf_op jit(solution)/shard_map/all_to_all | solution.py:637
  134.9 1.4 convert_add_fusion.3
  138.2 2.9 %shard_map.212 = (bf16[384,256]{1,0:T(8,128)(2,1)S(1)}, bf16[384,256]{1,0:T(8,128)(2,1)S(1)}, bf16[432,1024]{1,0:T(8,128)(2,1)}, f32[1,1024]{1,0:T(1,128)S(1)}) custom-call(s32[3]{0:T(128)S(1)} %pad_add_fusion.refs_0_, f32[432,512]{1,0:T(8,128)} %copy-done.6, f32[432,512]{1,0:T(8,128)} %get-tuple-element.116.refs_2_, ...), custom_call_target="tpu_custom_call" | custom-call | tf_op jit(solution)/shard_map/pallas_call | solution.py:68
  141.2 1.4 collective-permute-done.14.refs_6_
  142.6 5.1 %shard_map.213 = (bf16[9,64,256]{2,1,0:T(8,128)(2,1)S(1)}, f32[9,64,256]{2,1,0:T(8,128)S(1)}, bf16[9,64,256]{2,1,0:T(8,128)(2,1)S(1)}, f32[9,64,256]{2,1,0:T(8,128)}) custom-call(s32[3]{0:T(128)S(1)} %pad_add_fusion.refs_0_, bf16[624,768]{1,0:T(8,128)(2,1)} %get-tuple-element.107.refs_3_.refs_1_, bf16[672,768]{1,0:T(8,128)(2,1)} %get-tuple-element.131.refs_2_, ...), custom_call_target="tpu_custom_call" | custom-call | tf_op jit(solution)/shard_map/pallas_call | solution.py:68
  149.0 1.4 collective-permute-start.15
  150.4 8.5 %collective-permute-done.15 = bf16[38,8,256]{2,1,0:T(8,128)(2,1)S(1)} collective-permute-done((bf16[38,8,256]{2,1,0:T(8,128)(2,1)S(1)}, bf16[38,8,256]{2,1,0:T(8,128)(2,1)S(1)}, u32[]{:S(2)}, u32[]{:S(2)}) %collective-permute-start.15) | collective-permute-done | bytes 155680 | tf_op jit(solution)/shard_map/ppermute | solution.py:646
  159.0 1.7 collective-permute-start.20
  161.0 1.4 collective-permute-start.19
  162.4 1.9 collective-permute-done.20
  164.3 1.9 collective-permute-done.19
  166.2 3.3 %collective-permute-done.18 = bf16[38,8,256]{2,1,0:T(8,128)(2,1)S(1)} collective-permute-done((bf16[38,8,256]{2,1,0:T(8,128)(2,1)S(1)}, bf16[38,8,256]{2,1,0:T(8,128)(2,1)S(1)}, u32[]{:S(2)}, u32[]{:S(2)}) %collective-permute-start.18) | collective-permute-done | bytes 155680 | tf_op jit(solution)/shard_map/ppermute | solution.py:646
  169.8 2.1 collective-permute-start.22
  171.9 10.2 %collective-permute-done.22 = bf16[18,16,256]{2,1,0:T(8,128)(2,1)S(1)} collective-permute-done((bf16[18,16,256]{2,1,0:T(8,128)(2,1)S(1)}, bf16[18,16,256]{2,1,0:T(8,128)(2,1)S(1)}, u32[]{:S(2)}, u32[]{:S(2)}) %collective-permute-start.22) | collective-permute-done | bytes 147488 | tf_op jit(solution)/shard_map/ppermute | solution.py:646
  182.4 1.2 collective-permute-start.23
  183.9 1.2 collective-permute-start.25
  185.1 4.7 %collective-permute-done.25 = bf16[18,8,256]{2,1,0:T(8,128)(2,1)S(1)} collective-permute-done((bf16[18,8,256]{2,1,0:T(8,128)(2,1)S(1)}, bf16[18,8,256]{2,1,0:T(8,128)(2,1)S(1)}, u32[]{:S(2)}, u32[]{:S(2)}) %collective-permute-start.25) | collective-permute-done | bytes 73760 | tf_op jit(solution)/shard_map/ppermute | solution.py:646
  193.3 1.2 collective-permute-start.26
  194.5 5.0 %collective-permute-done.26 = bf16[18,8,256]{2,1,0:T(8,128)(2,1)S(1)} collective-permute-done((bf16[18,8,256]{2,1,0:T(8,128)(2,1)S(1)}, bf16[18,8,256]{2,1,0:T(8,128)(2,1)S(1)}, u32[]{:S(2)}, u32[]{:S(2)}) %collective-permute-start.26) | collective-permute-done | bytes 73760 | tf_op jit(solution)/shard_map/ppermute | solution.py:646
  199.7 6.2 %shard_map.214 = bf16[2,16,32,256]{3,2,1,0:T(8,128)(2,1)} custom-call(bf16[432,1024]{1,0:T(8,128)(2,1)S(1)} %copy-done.7, bf16[384,512]{1,0:T(8,128)(2,1)S(1)} %copy-done.8, bf16[3,768,512]{2,1,0:T(8,128)(2,1)} %bitcast.39, bf16[256,512]{1,0:T(8,128)(2,1)S(1)} %copy-done.3), custom_call_target="tpu_custom_call" | custom-call | tf_op jit(solution)/shard_map/pallas_call | solution.py:68
  208.0 1.2 collective-permute-start.31
  210.2 3.0 %shard_map.215.refs_0_ = f32[18,256,512]{2,1,0:T(8,128)} custom-call(s32[1]{0:T(128)} %bitcast.10.bits, bf16[19,256,256]{2,1,0:T(8,128)(2,1)S(1)} %pad_maximum_fusion.half), custom_call_target="tpu_custom_call" | custom-call | tf_op jit(solution)/shard_map/pallas_call | solution.py:615
  217.3 5.3 %shard_map.216 = f32[18,256,512]{2,1,0:T(8,128)} custom-call(s32[1]{0:T(128)} %bitcast.13.bits, bf16[19,256,256]{2,1,0:T(8,128)(2,1)} %collective-permute-done.30.half, f32[18,256,512]{2,1,0:T(8,128)} %shard_map.215.refs_0_), custom_call_target="tpu_custom_call", output_to_operand_aliasing={{}: (2, {})} | custom-call | tf_op jit(solution)/shard_map/pallas_call | solution.py:615
  226.0 1.9 shard_map.217.refs_0_
  227.8 1.9 shard_map.218
  (144 shorter events, 29.0 us)
Async XLA Ops:
  1.4 6.0 %collective-permute-start.3 = (bf16[2,1,32,256]{3,2,1,0:T(8,128)(2,1)S(1)}, bf16[2,1,32,256]{3,2,1,0:T(8,128)(2,1)S(1)}, u32[]{:S(2)}, u32[]{:S(2)}) collective-permute-start(bf16[2,1,32,256]{3,2,1,0:T(8,128)(2,1)S(1)} %slice.96), channel_id=1, source_target_pairs={{0,16},{1,17},{2,18},{3,19},{4,20},{5,21},{6,22},{7,23},{8,24},{9,... | collective-permute-start | bytes 98312 | tf_op jit(solution)/shard_map/ppermute | solution.py:633
  7.2 16.1 %collective-permute-start = (bf16[672,256]{1,0:T(8,128)(2,1)S(1)}, bf16[672,256]{1,0:T(8,128)(2,1)S(1)}, u32[]{:S(2)}, u32[]{:S(2)}) collective-permute-start(bf16[672,256]{1,0:T(8,128)(2,1)S(1)} %shard_map.203), channel_id=1, source_target_pairs={{0,16},{16,0},{1,17},{17,1},{2,18},{18,2},{3,19},{19,3},{4,20},{20... | collective-permute-start | bytes 1032200 | tf_op jit(solution)/shard_map/ppermute | solution.py:784
  7.5 5.8 %collective-permute-start.4 = (bf16[2,17,1,256]{3,2,1,0:T(2,128)(2,1)S(1)}, bf16[2,17,1,256]{3,2,1,0:T(2,128)(2,1)S(1)}, u32[]{:S(2)}, u32[]{:S(2)}) collective-permute-start(bf16[2,17,1,256]{3,2,1,0:T(2,128)(2,1)S(1)} %pad_maximum_fusion.12), channel_id=1, source_target_pairs={{0,4},{4,8},{8,12},{1,5},{5,9},{9,13},{2,6},{6,10},{10,14},{3,7},{... | collective-permute-start | bytes 52232 | tf_op jit(solution)/shard_map/ppermute | solution.py:633
  16.6 32.9 %all-to-all-start = ((f32[32,1,2176]{2,1,0:T(1,128)}), f32[32,1,2176]{2,1,0:T(1,128)S(1)}, u32[]{:S(2)}, u32[]{:S(2)}) async-start(f32[32,1,2176]{2,1,0:T(1,128)} %shard_map.206), calls=%async_computation | async-start | bytes 557056 | tf_op jit(solution)/shard_map/all_to_all | solution.py:637
  23.3 18.7 %copy-start.2 = (bf16[672,256]{1,0:T(8,128)(2,1)}, bf16[672,256]{1,0:T(8,128)(2,1)S(1)}, u32[]{:S(2)}) copy-start(bf16[672,256]{1,0:T(8,128)(2,1)S(1)} %collective-permute-done.refs_4_.refs_5_) | copy-start | bytes 1032196
  24.6 10.2 %collective-permute-start.1 = (bf16[480,256]{1,0:T(8,128)(2,1)S(1)}, bf16[480,256]{1,0:T(8,128)(2,1)S(1)}, u32[]{:S(2)}, u32[]{:S(2)}) collective-permute-start(bf16[480,256]{1,0:T(8,128)(2,1)S(1)} %get-tuple-element.90), channel_id=1, source_target_pairs={{0,4},{4,8},{8,12},{1,5},{5,9},{9,13},{2,6},{6,10},{10,14},{3,7},{... | collective-permute-start | bytes 737288 | tf_op jit(solution)/shard_map/ppermute | solution.py:633
  28.3 21.2 %copy-start.9 = (f32[512]{0:T(512)S(1)}, f32[512]{0:T(512)}, u32[]{:S(2)}) copy-start(f32[512]{0:T(512)} %param.14) | copy-start | bytes 6148
  28.3 21.2 %copy-start.12 = (f32[512]{0:T(512)S(1)}, f32[512]{0:T(512)}, u32[]{:S(2)}) copy-start(f32[512]{0:T(512)} %param.15) | copy-start | bytes 6148
  28.4 13.7 %collective-permute-start.2 = (bf16[480,256]{1,0:T(8,128)(2,1)S(1)}, bf16[480,256]{1,0:T(8,128)(2,1)S(1)}, u32[]{:S(2)}, u32[]{:S(2)}) collective-permute-start(bf16[480,256]{1,0:T(8,128)(2,1)S(1)} %get-tuple-element.91), channel_id=1, source_target_pairs={{4,0},{8,4},{12,8},{5,1},{9,5},{13,9},{6,2},{10,6},{14,10},{7,3},{... | collective-permute-start | bytes 737288 | tf_op jit(solution)/shard_map/ppermute | solution.py:633
  49.5 19.8 %copy-start.10 = (f32[512]{0:T(512)S(1)}, f32[512]{0:T(512)}, u32[]{:S(2)}) copy-start(f32[512]{0:T(512)} %param.17) | copy-start | bytes 6148
  49.6 19.8 %copy-start.11 = (f32[512]{0:T(512)S(1)}, f32[512]{0:T(512)}, u32[]{:S(2)}) copy-start(f32[512]{0:T(512)} %param.20) | copy-start | bytes 6148
  49.6 19.8 %copy-start.13 = (f32[512]{0:T(512)S(1)}, f32[512]{0:T(512)}, u32[]{:S(2)}) copy-start(f32[512]{0:T(512)} %param.18) | copy-start | bytes 6148
  49.6 19.8 %copy-start.14 = (f32[512]{0:T(512)S(1)}, f32[512]{0:T(512)}, u32[]{:S(2)}) copy-start(f32[512]{0:T(512)} %param.21) | copy-start | bytes 6148
  57.6 37.4 %collective-permute-start.5 = (bf16[624,1536]{1,0:T(8,128)(2,1)}, bf16[624,1536]{1,0:T(8,128)(2,1)}, u32[]{:S(2)}, u32[]{:S(2)}) collective-permute-start(bf16[624,1536]{1,0:T(8,128)(2,1)} %get-tuple-element.106.refs_1_), channel_id=1, source_target_pairs={{0,16},{16,0},{1,17},{17,1},{2,18},{18,2},{3,19},{19,3},{4,20},{20... | collective-permute-start | bytes 5750792 | tf_op jit(solution)/shard_map/ppermute | solution.py:646
  57.7 11.7 %all-to-all-start.1 = ((f32[32,1,1024]{2,1,0:T(1,128)}), f32[32,1,1024]{2,1,0:T(1,128)S(1)}, u32[]{:S(2)}, u32[]{:S(2)}) async-start(f32[32,1,1024]{2,1,0:T(1,128)} %get-tuple-element.98), calls=%async_computation.1 | async-start | bytes 262144 | tf_op jit(solution)/shard_map/all_to_all | solution.py:637
  61.5 31.8 %collective-permute-start.6 = (bf16[624,768]{1,0:T(8,128)(2,1)S(1)}, bf16[624,768]{1,0:T(8,128)(2,1)}, u32[]{:S(2)}, u32[]{:S(2)}) collective-permute-start(bf16[624,768]{1,0:T(8,128)(2,1)S(1)} %copy-done.15), channel_id=1, source_target_pairs={{0,16},{16,0},{1,17},{17,1},{2,18},{18,2},{3,19},{19,3},{4,20},{20... | collective-permute-start | bytes 2875400 | tf_op jit(solution)/shard_map/ppermute | solution.py:646
  75.8 12.0 %all-to-all-start.2 = ((f32[32,1,1536]{2,1,0:T(1,128)}), f32[32,1,1536]{2,1,0:T(1,128)S(1)}, u32[]{:S(2)}, u32[]{:S(2)}) async-start(f32[32,1,1536]{2,1,0:T(1,128)} %get-tuple-element.103), calls=%async_computation.2 | async-start | bytes 393216 | tf_op jit(solution)/shard_map/all_to_all | solution.py:637
  93.2 1.8 collective-permute-start.7
  103.6 16.3 %collective-permute-start.9 = (bf16[19,64,256]{2,1,0:T(8,128)(2,1)}, bf16[19,64,256]{2,1,0:T(8,128)(2,1)S(1)}, u32[]{:S(2)}, u32[]{:S(2)}) collective-permute-start(bf16[19,64,256]{2,1,0:T(8,128)(2,1)} %get-tuple-element.121), channel_id=1, source_target_pairs={{0,8},{4,12},{8,0},{12,4},{1,9},{5,13},{9,1},{13,5},{2,10},{6,14},... | collective-permute-start | bytes 1867784 | tf_op jit(solution)/shard_map/ppermute | solution.py:646
  104.5 15.8 %collective-permute-start.8 = (bf16[19,64,256]{2,1,0:T(8,128)(2,1)S(1)}, bf16[19,64,256]{2,1,0:T(8,128)(2,1)S(1)}, u32[]{:S(2)}, u32[]{:S(2)}) collective-permute-start(bf16[19,64,256]{2,1,0:T(8,128)(2,1)S(1)} %get-tuple-element.119), channel_id=1, source_target_pairs={{0,4},{4,0},{8,12},{12,8},{1,5},{5,1},{9,13},{13,9},{2,6},{6,2},{1... | collective-permute-start | bytes 1867784 | tf_op jit(solution)/shard_map/ppermute | solution.py:646
  104.6 15.3 %copy-start.17 = (f32[19,64,256]{2,1,0:T(8,128)S(1)}, f32[19,64,256]{2,1,0:T(8,128)}, u32[]{:S(2)}) copy-start(f32[19,64,256]{2,1,0:T(8,128)} %get-tuple-element.120) | copy-start | bytes 3735556
  122.6 12.3 %collective-permute-start.10 = (bf16[19,32,256]{2,1,0:T(8,128)(2,1)S(1)}, bf16[19,32,256]{2,1,0:T(8,128)(2,1)S(1)}, u32[]{:S(2)}, u32[]{:S(2)}) collective-permute-start(bf16[19,32,256]{2,1,0:T(8,128)(2,1)S(1)} %select_convert_fusion.2), channel_id=1, source_target_pairs={{0,8},{4,12},{8,0},{12,4},{1,9},{5,13},{9,1},{13,5},{2,10},{6,14},... | collective-permute-start | bytes 933896 | tf_op jit(solution)/shard_map/ppermute | solution.py:646
  123.5 11.4 %collective-permute-start.11 = (bf16[19,32,256]{2,1,0:T(8,128)(2,1)S(1)}, bf16[19,32,256]{2,1,0:T(8,128)(2,1)}, u32[]{:S(2)}, u32[]{:S(2)}) collective-permute-start(bf16[19,32,256]{2,1,0:T(8,128)(2,1)S(1)} %select_convert_fusion.1), channel_id=1, source_target_pairs={{0,4},{4,0},{8,12},{12,8},{1,5},{5,1},{9,13},{13,9},{2,6},{6,2},{1... | collective-permute-start | bytes 933896 | tf_op jit(solution)/shard_map/ppermute | solution.py:646
  123.8 17.4 %collective-permute-start.13 = (bf16[672,768]{1,0:T(8,128)(2,1)}, bf16[672,768]{1,0:T(8,128)(2,1)}, u32[]{:S(2)}, u32[]{:S(2)}) collective-permute-start(bf16[672,768]{1,0:T(8,128)(2,1)} %get-tuple-element.131.refs_2_), channel_id=1, source_target_pairs={{0,16},{16,0},{1,17},{17,1},{2,18},{18,2},{3,19},{19,3},{4,20},{20... | collective-permute-start | bytes 3096584 | tf_op jit(solution)/shard_map/ppermute | solution.py:646
  123.8 11.1 %all-to-all-start.3 = ((f32[32,1,1024]{2,1,0:T(1,128)}), f32[32,1,1024]{2,1,0:T(1,128)S(1)}, u32[]{:S(2)}, u32[]{:S(2)}) async-start(f32[32,1,1024]{2,1,0:T(1,128)} %get-tuple-element.122), calls=%async_computation.3 | async-start | bytes 262144 | tf_op jit(solution)/shard_map/all_to_all | solution.py:637
  137.1 10.6 %collective-permute-start.12 = (bf16[38,16,256]{2,1,0:T(8,128)(2,1)}, bf16[38,16,256]{2,1,0:T(8,128)(2,1)S(1)}, u32[]{:S(2)}, u32[]{:S(2)}) collective-permute-start(bf16[38,16,256]{2,1,0:T(8,128)(2,1)} %select_convert_fusion), channel_id=1, source_target_pairs={{0,1},{1,0},{2,3},{3,2},{4,5},{5,4},{6,7},{7,6},{8,9},{9,8},{10,11... | collective-permute-start | bytes 933896 | tf_op jit(solution)/shard_map/ppermute | solution.py:646
  141.1 1.5 collective-permute-start.14
  147.9 11.0 %collective-permute-start.16 = (bf16[9,64,256]{2,1,0:T(8,128)(2,1)S(1)}, bf16[9,64,256]{2,1,0:T(8,128)(2,1)S(1)}, u32[]{:S(2)}, u32[]{:S(2)}) collective-permute-start(bf16[9,64,256]{2,1,0:T(8,128)(2,1)S(1)} %get-tuple-element.140), channel_id=1, source_target_pairs={{0,4},{4,0},{8,12},{12,8},{1,5},{5,1},{9,13},{13,9},{2,6},{6,2},{1... | collective-permute-start | bytes 884744 | tf_op jit(solution)/shard_map/ppermute | solution.py:646
  148.7 10.2 %collective-permute-start.17 = (bf16[9,64,256]{2,1,0:T(8,128)(2,1)S(1)}, bf16[9,64,256]{2,1,0:T(8,128)(2,1)S(1)}, u32[]{:S(2)}, u32[]{:S(2)}) collective-permute-start(bf16[9,64,256]{2,1,0:T(8,128)(2,1)S(1)} %get-tuple-element.141), channel_id=1, source_target_pairs={{0,8},{4,12},{8,0},{12,4},{1,9},{5,13},{9,1},{13,5},{2,10},{6,14},... | collective-permute-start | bytes 884744 | tf_op jit(solution)/shard_map/ppermute | solution.py:646
  149.0 9.9 %collective-permute-start.15 = (bf16[38,8,256]{2,1,0:T(8,128)(2,1)S(1)}, bf16[38,8,256]{2,1,0:T(8,128)(2,1)S(1)}, u32[]{:S(2)}, u32[]{:S(2)}) collective-permute-start(bf16[38,8,256]{2,1,0:T(8,128)(2,1)S(1)} %select_convert_fusion.3), channel_id=1, source_target_pairs={{0,2},{1,3},{2,0},{3,1},{4,6},{5,7},{6,4},{7,5},{8,10},{9,11},{10,... | collective-permute-start | bytes 466952 | tf_op jit(solution)/shard_map/ppermute | solution.py:646
  159.0 5.3 %collective-permute-start.20 = (bf16[9,32,256]{2,1,0:T(8,128)(2,1)S(1)}, bf16[9,32,256]{2,1,0:T(8,128)(2,1)S(1)}, u32[]{:S(2)}, u32[]{:S(2)}) collective-permute-start(bf16[9,32,256]{2,1,0:T(8,128)(2,1)S(1)} %select_convert_fusion.5), channel_id=1, source_target_pairs={{0,4},{4,0},{8,12},{12,8},{1,5},{5,1},{9,13},{13,9},{2,6},{6,2},{1... | collective-permute-start | bytes 442376 | tf_op jit(solution)/shard_map/ppermute | solution.py:646
  160.8 8.7 %collective-permute-start.18 = (bf16[38,8,256]{2,1,0:T(8,128)(2,1)S(1)}, bf16[38,8,256]{2,1,0:T(8,128)(2,1)S(1)}, u32[]{:S(2)}, u32[]{:S(2)}) collective-permute-start(bf16[38,8,256]{2,1,0:T(8,128)(2,1)S(1)} %add_convert_fusion), channel_id=1, source_target_pairs={{0,2},{1,3},{2,0},{3,1},{4,6},{5,7},{6,4},{7,5},{8,10},{9,11},{10,... | collective-permute-start | bytes 466952 | tf_op jit(solution)/shard_map/ppermute | solution.py:646
  161.0 5.2 %collective-permute-start.19 = (bf16[9,32,256]{2,1,0:T(8,128)(2,1)S(1)}, bf16[9,32,256]{2,1,0:T(8,128)(2,1)S(1)}, u32[]{:S(2)}, u32[]{:S(2)}) collective-permute-start(bf16[9,32,256]{2,1,0:T(8,128)(2,1)S(1)} %select_convert_fusion.6), channel_id=1, source_target_pairs={{0,8},{4,12},{8,0},{12,4},{1,9},{5,13},{9,1},{13,5},{2,10},{6,14},... | collective-permute-start | bytes 442376 | tf_op jit(solution)/shard_map/ppermute | solution.py:646
  169.6 12.5 %collective-permute-start.21 = (bf16[38,16,256]{2,1,0:T(8,128)(2,1)S(1)}, bf16[38,16,256]{2,1,0:T(8,128)(2,1)S(1)}, u32[]{:S(2)}, u32[]{:S(2)}) collective-permute-start(bf16[38,16,256]{2,1,0:T(8,128)(2,1)S(1)} %pad_maximum_fusion.6), channel_id=1, source_target_pairs={{0,1},{1,0},{2,3},{3,2},{4,5},{5,4},{6,7},{7,6},{8,9},{9,8},{10,11... | collective-permute-start | bytes 933896 | tf_op jit(solution)/shard_map/ppermute | solution.py:646
  169.8 12.3 %collective-permute-start.22 = (bf16[18,16,256]{2,1,0:T(8,128)(2,1)S(1)}, bf16[18,16,256]{2,1,0:T(8,128)(2,1)S(1)}, u32[]{:S(2)}, u32[]{:S(2)}) collective-permute-start(bf16[18,16,256]{2,1,0:T(8,128)(2,1)S(1)} %select_convert_fusion.4), channel_id=1, source_target_pairs={{0,1},{1,0},{2,3},{3,2},{4,5},{5,4},{6,7},{7,6},{8,9},{9,8},{10,11... | collective-permute-start | bytes 442376 | tf_op jit(solution)/shard_map/ppermute | solution.py:646
  182.4 8.5 %collective-permute-start.23 = (bf16[19,32,256]{2,1,0:T(8,128)(2,1)S(1)}, bf16[19,32,256]{2,1,0:T(8,128)(2,1)S(1)}, u32[]{:S(2)}, u32[]{:S(2)}) collective-permute-start(bf16[19,32,256]{2,1,0:T(8,128)(2,1)S(1)} %get-tuple-element.180), channel_id=1, source_target_pairs={{0,8},{4,12},{8,0},{12,4},{1,9},{5,13},{9,1},{13,5},{2,10},{6,14},... | collective-permute-start | bytes 933896 | tf_op jit(solution)/shard_map/ppermute | solution.py:646
  183.6 8.2 %collective-permute-start.24 = (bf16[19,32,256]{2,1,0:T(8,128)(2,1)S(1)}, bf16[19,32,256]{2,1,0:T(8,128)(2,1)S(1)}, u32[]{:S(2)}, u32[]{:S(2)}) collective-permute-start(bf16[19,32,256]{2,1,0:T(8,128)(2,1)S(1)} %get-tuple-element.179), channel_id=1, source_target_pairs={{0,4},{4,0},{8,12},{12,8},{1,5},{5,1},{9,13},{13,9},{2,6},{6,2},{1... | collective-permute-start | bytes 933896 | tf_op jit(solution)/shard_map/ppermute | solution.py:646
  183.9 5.8 %collective-permute-start.25 = (bf16[18,8,256]{2,1,0:T(8,128)(2,1)S(1)}, bf16[18,8,256]{2,1,0:T(8,128)(2,1)S(1)}, u32[]{:S(2)}, u32[]{:S(2)}) collective-permute-start(bf16[18,8,256]{2,1,0:T(8,128)(2,1)S(1)} %select_convert_fusion.7), channel_id=1, source_target_pairs={{0,2},{1,3},{2,0},{3,1},{4,6},{5,7},{6,4},{7,5},{8,10},{9,11},{10,... | collective-permute-start | bytes 221192 | tf_op jit(solution)/shard_map/ppermute | solution.py:646
  191.8 14.1 %collective-permute-start.29 = (bf16[19,64,256]{2,1,0:T(8,128)(2,1)S(1)}, bf16[19,64,256]{2,1,0:T(8,128)(2,1)S(1)}, u32[]{:S(2)}, u32[]{:S(2)}) collective-permute-start(bf16[19,64,256]{2,1,0:T(8,128)(2,1)S(1)} %pad_maximum_fusion.4), channel_id=1, source_target_pairs={{0,8},{4,12},{8,0},{12,4},{1,9},{5,13},{9,1},{13,5},{2,10},{6,14},... | collective-permute-start | bytes 1867784 | tf_op jit(solution)/shard_map/ppermute | solution.py:646
  192.9 13.7 %collective-permute-start.28 = (bf16[19,64,256]{2,1,0:T(8,128)(2,1)S(1)}, bf16[19,64,256]{2,1,0:T(8,128)(2,1)S(1)}, u32[]{:S(2)}, u32[]{:S(2)}) collective-permute-start(bf16[19,64,256]{2,1,0:T(8,128)(2,1)S(1)} %pad_maximum_fusion.3), channel_id=1, source_target_pairs={{0,4},{4,0},{8,12},{12,8},{1,5},{5,1},{9,13},{13,9},{2,6},{6,2},{1... | collective-permute-start | bytes 1867784 | tf_op jit(solution)/shard_map/ppermute | solution.py:646
  193.3 6.2 %collective-permute-start.26 = (bf16[18,8,256]{2,1,0:T(8,128)(2,1)S(1)}, bf16[18,8,256]{2,1,0:T(8,128)(2,1)S(1)}, u32[]{:S(2)}, u32[]{:S(2)}) collective-permute-start(bf16[18,8,256]{2,1,0:T(8,128)(2,1)S(1)} %add_convert_fusion.1), channel_id=1, source_target_pairs={{0,2},{1,3},{2,0},{3,1},{4,6},{5,7},{6,4},{7,5},{8,10},{9,11},{10,... | collective-permute-start | bytes 221192 | tf_op jit(solution)/shard_map/ppermute | solution.py:646
  199.6 6.3 %collective-permute-start.27 = (bf16[18,16,256]{2,1,0:T(8,128)(2,1)S(1)}, bf16[18,16,256]{2,1,0:T(8,128)(2,1)S(1)}, u32[]{:S(2)}, u32[]{:S(2)}) collective-permute-start(bf16[18,16,256]{2,1,0:T(8,128)(2,1)S(1)} %pad_maximum_fusion.11), channel_id=1, source_target_pairs={{0,1},{1,0},{2,3},{3,2},{4,5},{5,4},{6,7},{7,6},{8,9},{9,8},{10,11... | collective-permute-start | bytes 442376 | tf_op jit(solution)/shard_map/ppermute | solution.py:646
  207.8 7.3 %collective-permute-start.30 = (bf16[19,256,256]{2,1,0:T(8,128)(2,1)S(1)}, bf16[19,256,256]{2,1,0:T(8,128)(2,1)}, u32[]{:S(2)}, u32[]{:S(2)}) collective-permute-start(bf16[19,256,256]{2,1,0:T(8,128)(2,1)S(1)} %pad_maximum_fusion.half), channel_id=1, source_target_pairs={{0,16},{16,0},{1,17},{17,1},{2,18},{18,2},{3,19},{19,3},{4,20},{20... | collective-permute-start | bytes 7471112 | tf_op jit(solution)/shard_map/ppermute | solution.py:646
  208.0 6.3 %collective-permute-start.31 = (bf16[9,32,256]{2,1,0:T(8,128)(2,1)S(1)}, bf16[9,32,256]{2,1,0:T(8,128)(2,1)S(1)}, u32[]{:S(2)}, u32[]{:S(2)}) collective-permute-start(bf16[9,32,256]{2,1,0:T(8,128)(2,1)S(1)} %get-tuple-element.194), channel_id=1, source_target_pairs={{0,8},{4,12},{8,0},{12,4},{1,9},{5,13},{9,1},{13,5},{2,10},{6,14},... | collective-permute-start | bytes 442376 | tf_op jit(solution)/shard_map/ppermute | solution.py:646
  209.1 6.0 %collective-permute-start.32 = (bf16[9,32,256]{2,1,0:T(8,128)(2,1)S(1)}, bf16[9,32,256]{2,1,0:T(8,128)(2,1)S(1)}, u32[]{:S(2)}, u32[]{:S(2)}) collective-permute-start(bf16[9,32,256]{2,1,0:T(8,128)(2,1)S(1)} %get-tuple-element.193), channel_id=1, source_target_pairs={{0,4},{4,0},{8,12},{12,8},{1,5},{5,1},{9,13},{13,9},{2,6},{6,2},{1... | collective-permute-start | bytes 442376 | tf_op jit(solution)/shard_map/ppermute | solution.py:646
  215.2 9.2 %collective-permute-start.34 = (bf16[9,64,256]{2,1,0:T(8,128)(2,1)S(1)}, bf16[9,64,256]{2,1,0:T(8,128)(2,1)S(1)}, u32[]{:S(2)}, u32[]{:S(2)}) collective-permute-start(bf16[9,64,256]{2,1,0:T(8,128)(2,1)S(1)} %pad_maximum_fusion.9), channel_id=1, source_target_pairs={{0,8},{4,12},{8,0},{12,4},{1,9},{5,13},{9,1},{13,5},{2,10},{6,14},... | collective-permute-start | bytes 884744 | tf_op jit(solution)/shard_map/ppermute | solution.py:646
  216.2 8.2 %collective-permute-start.33 = (bf16[9,64,256]{2,1,0:T(8,128)(2,1)S(1)}, bf16[9,64,256]{2,1,0:T(8,128)(2,1)S(1)}, u32[]{:S(2)}, u32[]{:S(2)}) collective-permute-start(bf16[9,64,256]{2,1,0:T(8,128)(2,1)S(1)} %pad_maximum_fusion.8), channel_id=1, source_target_pairs={{0,4},{4,0},{8,12},{12,8},{1,5},{5,1},{9,13},{13,9},{2,6},{6,2},{1... | collective-permute-start | bytes 884744 | tf_op jit(solution)/shard_map/ppermute | solution.py:646
  224.7 3.1 %collective-permute-start.35 = (bf16[9,256,256]{2,1,0:T(8,128)(2,1)S(1)}, bf16[9,256,256]{2,1,0:T(8,128)(2,1)S(1)}, u32[]{:S(2)}, u32[]{:S(2)}) collective-permute-start(bf16[9,256,256]{2,1,0:T(8,128)(2,1)S(1)} %pad_maximum_fusion.1.half), channel_id=1, source_target_pairs={{0,16},{16,0},{1,17},{17,1},{2,18},{18,2},{3,19},{19,3},{4,20},{20... | collective-permute-start | bytes 3538952 | tf_op jit(solution)/shard_map/ppermute | solution.py:646
  (12 other events, 72.3 us)

commit v2 on v1

--- a/solution.py
+++ b/solution.py
@@ -23,21 +23,47 @@
 
 
 class Copies:
-    def __init__(self, names, sources, targets, sems):
-        self.jobs = {n: pltpu.make_async_copy(s, t, sems.at[k]) for k, (n, s, t) in enumerate(zip(names, sources, targets))}
+    def __init__(self, parts, pairs, sems):
+        self.jobs = {}
+        for k, (name, index) in enumerate(parts):
+            source, target = pairs[name]
+            if index:
+                source, target = source.at[index[1]], target.at[index[1]]
+            self.jobs.setdefault(name, []).append(pltpu.make_async_copy(source, target, sems.at[k]))
 
     def start(self, *names):
-        for name in names:
-            self.jobs[name].start()
+        for name, *which in map(named, names):
+            for job in self.jobs[name][slice(*which) if which else slice(None)]:
+                job.start()
 
     def wait(self, *names):
-        for name in names:
-            self.jobs[name].wait()
-
-
-def call(body, ins, outs, scratch=None, far_in=(), far_out=(), smem=(), limit=52):
-    scratch = scratch or {}
+        for name, *which in map(named, names):
+            for job in self.jobs[name][slice(*which) if which else slice(None)]:
+                job.wait()
+
+
+def named(name):
+    return (name,) if isinstance(name, str) else (name[0], name[1], name[1] + 1)
+
+
+def row_parts(total, count):
+    size = total // count
+    return [(k, (pl.ds(k * size, size),)) for k in range(count)]
+
+
+def end_parts(total, size):
+    return [(k, (slice(None), pl.ds(at, size))) for k, at in enumerate((0, total - size))]
+
+
+def lane_parts(total, count):
+    size = total // count
+    return [(k, (slice(None), pl.ds(k * size, size))) for k in range(count)]
+
+
+def call(body, ins, outs, scratch=None, far_in=(), far_out=(), smem=(), parts=None, limit=52, cost=0):
+    scratch, parts = scratch or {}, parts or {}
     far = (*far_in, *far_out)
+    jobs = [(name, index) for name in far for index in parts.get(name, [None])]
 
     def spec(name):
         if name in smem:
@@ -45,26 +71,21 @@
         return pl.BlockSpec(memory_space=pltpu.HBM if name in far else pltpu.VMEM)
 
     kinds = {**{n: shape(v.shape, v.dtype) for n, v in ins.items()}, **outs}
-    names = [*ins, *outs, *far, *scratch]
 
     def run(*refs):
-        given = dict(zip(names, refs)) if not far else None
+        plain = dict(zip([*ins, *outs], refs))
+        rest = refs[len(plain) :]
+        buffers = dict(zip(far, rest))
+        more = dict(zip(scratch, rest[len(far) :]))
+        copies = None
         if far:
-            plain = dict(zip([*ins, *outs], refs))
-            rest = refs[len(plain) :]
-            buffers = dict(zip(far, rest))
-            more = dict(zip(scratch, rest[len(far) : -1]))
-            given = {**plain, **buffers, **more}
-            sources = [plain[n] if n in far_in else buffers[n] for n in far]
-            targets = [buffers[n] if n in far_in else plain[n] for n in far]
-            copies = Copies(far, sources, targets, rest[-1])
+            pairs = {n: (plain[n], buffers[n]) if n in far_in else (buffers[n], plain[n]) for n in far}
+            copies = Copies(jobs, pairs, rest[-1])
             copies.start(*far_in)
-        else:
-            copies = None
-        body(Refs(given), copies)
+        body(Refs({**plain, **buffers, **more}), copies)
 
     buffers = [pltpu.VMEM(kinds[n].shape, kinds[n].dtype) for n in far]
-    sems = [pltpu.SemaphoreType.DMA((len(far),))] if far else []
+    sems = [pltpu.SemaphoreType.DMA((len(jobs),))] if far else []
     result = pl.pallas_call(
         run,
         out_shape=list(outs.values()),
@@ -72,7 +93,7 @@
         out_specs=[spec(n) for n in outs],
         scratch_shapes=[*buffers, *scratch.values(), *sems],
         compiler_params=pltpu.CompilerParams(vmem_limit_bytes=limit * 1024 * 1024),
-        cost_estimate=pl.CostEstimate(flops=0, bytes_accessed=0, transcendentals=0),
+        cost_estimate=pl.CostEstimate(flops=cost, bytes_accessed=0, transcendentals=0),
     )(*ins.values())
     return dict(zip(outs, result))
 
@@ -146,6 +167,7 @@
                 at += cols
 
     last = r.x.shape[1] - over
+    copies.wait("x", "cot")
     if hasattr(r, "up"):
         pack(r.down, lambda n: last + n, lambda n: rows - rim + n, lambda tail, head: tail)
         pack(r.up, lambda n: last + n, lambda n: rows - rim + n, lambda tail, head: head)
@@ -324,15 +346,15 @@
             at = (i + 2) * L + g * S + 2
             r.ownp[at : at + cols, :] = r.own[g, i].astype(f32)
     copies.wait("w1", "wp")
-    for m0, m in chunks(r.pre1.shape[0], 208):
+    for k, (m0, m) in enumerate(chunks(r.pre1.shape[0], r.pre1.shape[0] // 3)):
         z = matmul(r.xo[m0 : m0 + m, :], r.w1[0])
         z += matmul(r.xe[m0 : m0 + m, :], r.w1[1])
         z += matmul(r.xo[L + m0 : L + m0 + m, :], r.w1[2])
         r.pre1[m0 : m0 + m, :] = z
+        copies.start(("pre1", k))
         r.prep[m0 : m0 + m, :] = matmul(r.xe[m0 : m0 + m, cin : 2 * cin], r.wp[...])
-        r.keep[m0 : m0 + m, :] = z
-    copies.start("keep")
-    copies.wait("xe", "xo", "keep", "cotq")
+        copies.start(("prep", k))
+    copies.wait("xe", "xo", "pre1", "prep", "cotq")
 
 
 def second_kernel(r, copies):
@@ -345,6 +367,7 @@
     scale = inv * r.gain[...]
     M, Q = r.pre1.shape[0], r.pre2.shape[0]
     L = (M - Q) // 2
+    copies.wait("pre1")
     for m0, m in chunks(M, 104):
         v = (r.pre1[m0 : m0 + m, :] - center) * scale + r.shift[...]
         mask = wide(r.maskp[m0 : m0 + m, :], width)
@@ -356,16 +379,17 @@
     copies.start("h3")
     copies.wait("w2")
     sums = [jnp.zeros((1, width), f32)] * 2
-    for m0, m in chunks(Q, 176):
+    for k, (m0, m) in enumerate(chunks(Q, Q // 3)):
         z = matmul(r.h3[m0 : m0 + m, :], r.w2[0])
         z += matmul(r.h3[L + m0 : L + m0 + m, :], r.w2[1])
         z += matmul(r.h3[2 * L + m0 : 2 * L + m0 + m, :], r.w2[2])
         r.pre2[m0 : m0 + m, :] = z
+        copies.start(("pre2", k))
         zm = z * wide(r.ownp[L + 1 + m0 : L + 1 + m0 + m, :], width)
         sums = [sums[0] + column_sum(zm), sums[1] + column_sum(zm * z)]
     row = jnp.concatenate(sums, axis=1)
     r.spread[...] = jnp.broadcast_to(row[None], r.spread.shape)
-    copies.wait("h3")
+    copies.wait("h3", "pre2")
 
 
 def third_kernel(r, copies):
@@ -379,8 +403,9 @@
     r.mom2[...] = jnp.concatenate([c2, i2, cp, ip, jnp.zeros((4, width), f32)], axis=0)
     sums = [jnp.zeros((1, width), f32)] * 3
     both_shift = r.shift2[...] + r.shiftp[...]
-    copies.wait("cotq")
-    for line in range(r.grad.shape[0] // S):
+    copies.wait("pre2", "prep", "cotq")
+    total = r.grad.shape[0] // S
+    for line in range(total):
         at = line * S
         shifted = slice(L + 1 + at, L + 1 + at + S)
         n2 = (r.pre2[at : at + S, :] - c2) * i2
@@ -395,7 +420,8 @@
         g = g * own
         new = [column_sum(g * n2), column_sum(g), column_sum(g * np_)]
         sums = [a + b for a, b in zip(sums, new)]
-    copies.start("grad")
+        if (line + 1) % (total // 2) == 0:
+            copies.start(("grad", (line + 1) // (total // 2) - 1))
     for i in range(rows):
         for g in range(groups):
             at = (i + 1) * L + g * S + 1
@@ -425,9 +451,9 @@
     n = r.mom1[2:3, :]
     c2, i2, cp, ip = (r.mom2[k : k + 1, :] for k in range(4))
     t3 = jnp.sum(r.tot3[...], axis=0)
-    r.sums[...] = t3
     gg2, gs, ggp = (t3[:, k * width : (k + 1) * width] for k in range(3))
-    copies.wait("grad")
+    r.gain_second[...], r.shift_second[...], r.gain_proj[...], r.shift_proj[...] = gg2, gs, ggp, gs
+    copies.wait("grad", "pre2", "prep")
     for m0, m in chunks(Q, L):
         shifted = slice(L + 1 + m0, L + 1 + m0 + m)
         mask = wide(r.maskp[shifted, :], width) / n
@@ -437,12 +463,13 @@
         r.gq[m0 : m0 + m, :] = (r.gain2[...] * i2) * (g - mask * (gs + n2 * gg2))
         r.gpq[m0 : m0 + m, :] = (r.gainp[...] * ip) * (g - mask * (gs + np_ * ggp))
     r.gq[Q:, :] = jnp.zeros((r.gq.shape[0] - Q, width), f32)
+    copies.start("gq")
     for m0, m in chunks(rows_w, 96):
         r.gpu[m0 : m0 + m, :] = r.gpq[L + 1 + m0 : L + 1 + m0 + m, :].astype(bf16)
     copies.start("gpu")
     halves(r, r.gq, L, 2 * L + 1, 0, rows_w)
     halves(r, r.gpq, L - 1, 2 * L, rows_w, rows_w)
-    copies.wait("gpu")
+    copies.wait("gpu", "gq")
 
 
 def hidden_kernel(r, copies):
@@ -450,20 +477,20 @@
     Q = r.gq.shape[0] - 8
     L = (r.keep.shape[0] - Q) // 2
     center, inv = r.mom1[0:1, :], r.mom1[1:2, :]
+    copies.wait("gq")
     for m0, m in chunks(Q, 176):
         for b in range(3):
             r.g3[m0 : m0 + m, b * width : (b + 1) * width] = r.gq[m0 + b : m0 + b + m, :].astype(bf16)
-    copies.wait("w2")
     U = r.act.shape[0]
-    for m0, m in chunks(U, 144):
-        gh = jnp.zeros((m, width), f32)
-        for a in range(3):
-            for b in range(3):
-                gh += matmul_nt(
-                    r.g3[L * a + m0 : L * a + m0 + m, b * width : (b + 1) * width],
-                    r.w2[2 - a, (2 - b) * width : (3 - b) * width, :],
-                )
-        r.act[m0 : m0 + m, :] = gh
+    for a in range(3):
+        copies.wait(("w2", a))
+        gh = jnp.zeros((U, width), f32)
+        for b in range(3):
+            gh += matmul_nt(
+                r.g3[L * a : L * a + U, b * width : (b + 1) * width],
+                r.w2[2 - a, (2 - b) * width : (3 - b) * width, :],
+            )
+        r.act[...] = gh if a == 0 else r.act[...] + gh
     copies.wait("keep")
     sums = [jnp.zeros((1, width), f32)] * 2
     for m0, m in chunks(U, L):
@@ -480,13 +507,14 @@
     r.spread[...] = jnp.broadcast_to(row[None], r.spread.shape)
 
 
-def split_store(bits, acc, rows, unit, sent_a, kept_a, sent_b, kept_b):
+def split_store(r, rows, unit, first):
     quarter = unit // 4
     for k in range(rows // unit):
-        for bit, base, sent, kept in ((1, 0, sent_a, kept_a), (2, 2 * quarter, sent_b, kept_b)):
-            keep = pl.multiple_of(k * unit + base + bits[bit] * quarter, quarter)
-            send = pl.multiple_of(k * unit + base + (1 - bits[bit]) * quarter, quarter)
-            yield k, acc[pl.ds(send, quarter), :].astype(bf16), acc[pl.ds(keep, quarter), :], sent, kept
+        for bit, base, sent, kept in ((1, 0, r.sent_a, r.kept_a), (2, 2 * quarter, r.sent_b, r.kept_b)):
+            keep = pl.multiple_of(k * unit + base + r.bits[bit] * quarter, quarter)
+            send = pl.multiple_of(k * unit + base + (1 - r.bits[bit]) * quarter, quarter)
+            sent[first + k] = r.acc[pl.ds(send, quarter), :].astype(bf16)
+            kept[first + k] = r.acc[pl.ds(keep, quarter), :]
 
 
 def weights_second_kernel(r, copies):
@@ -494,71 +522,70 @@
     cin = r.xe.shape[1] // 3
     rows_w = r.near.shape[0] // 2
     L = (r.h3.shape[0] - rows_w) // 5
-    per = 3 * width // cin
-    places = r.sent_a, r.kept_a, r.sent_b, r.kept_b
-    copies.wait("h3", "h3_far")
-    for a in range(3):
-        at = L * a + L
-        for b in range(3):
-            lanes = slice(b * width, (b + 1) * width)
-            r.acc[lanes, :] = matmul_tn(r.h3[at : at + rows_w, lanes], r.near[:rows_w, :]) + matmul_tn(
+    per = width // cin
+    for b in range(3):
+        lanes = slice(b * width, (b + 1) * width)
+        copies.wait(("h3", b), ("h3_far", b))
+        for a in range(3):
+            at = L * a + L
+            r.acc[...] = matmul_tn(r.h3[at : at + rows_w, lanes], r.near[:rows_w, :]) + matmul_tn(
                 r.h3_far[at : at + rows_w, lanes], r.far[:rows_w, :]
             )
-        for k, s, v, sent, kept in split_store(r.bits, r.acc, 3 * width, cin, *places):
-            sent[a * per + k] = s
-            kept[a * per + k] = v
+            split_store(r, width, cin, (3 * b + a) * per)
+        copies.start(("kept_a", b), ("kept_b", b))
     at = 2 * L
     copies.wait("xe", "xe_far")
-    r.acc[0:cin, :] = matmul_tn(r.xe[at : at + rows_w, cin : 2 * cin], r.near[rows_w:, :]) + matmul_tn(
-        r.xe_far[at : at + rows_w, cin : 2 * cin], r.far[rows_w:, :]
-    )
-    for k, s, v, sent, kept in split_store(r.bits, r.acc, cin, cin, *places):
-        sent[3 * per] = s
-        kept[3 * per] = v
-    copies.start("kept_a", "kept_b")
+    middle = slice(cin, 2 * cin)
+    r.acc[0:cin, :] = matmul_tn(r.xe[at : at + rows_w, middle], r.near[rows_w:, :]) + matmul_tn(
+        r.xe_far[at : at + rows_w, middle], r.far[rows_w:, :]
+    )
+    split_store(r, cin, cin, 9 * per)
+    copies.start(("kept_a", 3), ("kept_b", 3))
     copies.wait("kept_a", "kept_b")
 
 
-def fifth_kernel(r, copies):
+def first_back(r, gg, gs, count):
     width = r.gain.shape[1]
     U = r.act.shape[0]
-    rows_w = r.mine.shape[0]
-    L = U - rows_w
+    L = U - r.rows_w
     inv, n = r.mom1[1:2, :], r.mom1[2:3, :]
-    t4 = jnp.sum(r.tot4[...], axis=0)
-    r.sums[...] = t4
-    gg, gs = t4[:, :width] / n, t4[:, width:] / n
+    gg, gs = gg / n, gs / n
     scale = r.gain[...] * inv
     r.gf[0:8, :] = jnp.zeros((8, width), f32)
-    r.gf[8 + U :, :] = jnp.zeros((r.gf.shape[0] - 8 - U, width), f32)
-    for m0, m in chunks(U, L):
+    r.gf[8 + count :, :] = jnp.zeros((r.gf.shape[0] - 8 - count, width), f32)
+    for m0, m in chunks(count, L):
         mask = wide(r.maskp[2 * L + 2 + m0 : 2 * L + 2 + m0 + m, :], width)
         back = mask * gs + r.normed[m0 : m0 + m, :] * gg
         r.gf[8 + m0 : 8 + m0 + m, :] = scale * (r.act[m0 : m0 + m, :] - back)
-    halves(r, r.gf, 6, 2 * L, 0, rows_w)
-    for m0, m in chunks(U, 144):
-        r.gu[m0 : m0 + m, :width] = r.gf[8 + m0 : 8 + m0 + m, :].astype(bf16)
-        r.gu[m0 : m0 + m, width:] = r.gf[9 + m0 : 9 + m0 + m, :].astype(bf16)
-    copies.start("gu")
-    copies.wait("gu")
+
+
+def fifth_kernel(r, copies):
+    width = r.gain.shape[1]
+    r.rows_w = r.mine.shape[0]
+    L = r.act.shape[0] - r.rows_w
+    t4 = jnp.sum(r.tot4[...], axis=0)
+    r.gain_first[...], r.shift_first[...] = t4[:, :width], t4[:, width:]
+    first_back(r, t4[:, :width], t4[:, width:], r.rows_w)
+    halves(r, r.gf, 6, 2 * L, 0, r.rows_w)
 
 
 def weights_first_kernel(r, copies):
     rows_w = r.near.shape[0]
     cin = r.xe.shape[1] // 3
     L = (r.xe.shape[0] - rows_w) // 5
-    places = r.sent_a, r.kept_a, r.sent_b, r.kept_b
-    copies.wait("xe", "xo", "xe_far", "xo_far")
-    for a in range(3):
+    copies.wait("xe", "xe_far")
+    for k, a in enumerate((1, 0, 2)):
+        if k == 1:
+            copies.wait("xo", "xo_far")
         source, source_far = (r.xe, r.xe_far) if a == 1 else (r.xo, r.xo_far)
         at = (3 if a == 2 else 2) * L
-        r.acc[...] = matmul_tn(source[at : at + rows_w, :], r.near[...]) + matmul_tn(
-            source_far[at : at + rows_w, :], r.far[...]
-        )
-        for k, s, v, sent, kept in split_store(r.bits, r.acc, 3 * cin, cin, *places):
-            sent[a * 3 + k] = s
-            kept[a * 3 + k] = v
-    copies.start("kept_a", "kept_b")
+        for b in range(3):
+            lanes = slice(b * cin, (b + 1) * cin)
+            r.acc[lanes, :] = matmul_tn(source[at : at + rows_w, lanes], r.near[...]) + matmul_tn(
+                source_far[at : at + rows_w, lanes], r.far[...]
+            )
+        split_store(r, 3 * cin, cin, a * 3)
+        copies.start(("kept_a", a), ("kept_b", a))
     copies.wait("kept_a", "kept_b")
 
 
@@ -570,7 +597,14 @@
     S = cols + 8
     L = groups * S
     lines = r.lines
-    copies.wait("gu", "gpu", "w1", "wp")
+    U = r.act.shape[0]
+    r.rows_w = M
+    copies.wait("act", "normed")
+    first_back(r, r.gg[...], r.gs[...], U)
+    for m0, m in chunks(U, 144):
+        r.gu[m0 : m0 + m, :width] = r.gf[8 + m0 : 8 + m0 + m, :].astype(bf16)
+        r.gu[m0 : m0 + m, width:] = r.gf[9 + m0 : 9 + m0 + m, :].astype(bf16)
+    copies.wait("gpu", "w1", "wp")
 
     def tap(m0, m, a, b):
         di, dj = (1 if a == 0 else 0), (1 if b == 0 else 0)
@@ -602,29 +636,85 @@
     copies.wait("out")
 
 
-def widen_kernel(bits, half, *refs):
-    refs[-1][...] = half[...].astype(f32)
-
-
-def widen(half, side, taps, into=None):
-    n, m = half.shape[1], half.shape[2]
-    step = 3 if taps % 3 == 0 else 1
-    block = pl.BlockSpec((step, n, m), lambda t, side: (t, 0, 0))
-    placed = pl.BlockSpec((step, n, m), lambda t, side: (t, 0, side[0]))
-    more = [] if into is None else [into]
+def widen(half, side, taps, per, swapped, into=None):
+    total, n, m = half.shape
+    extra = total - taps * per
+    order = [(t % 3 * 3 + t // 3) if swapped else t for t in range(taps)]
+    jobs = [(t * per, per, 0, order[t] * per) for t in range(taps)] + [(taps * per, 1, 1, 0)] * extra
+    more = list(into or [])
+
+    def body(side_ref, half_ref, *refs):
+        outs = refs[len(more) : len(more) + 1 + extra]
+        narrow, full, sems = refs[len(more) + 1 + extra :]
+        lanes = pl.ds(pl.multiple_of(side_ref[0] * m, m), m)
+        reads = [
+            pltpu.make_async_copy(half_ref.at[pl.ds(at, size)], narrow.at[pl.ds(at, size)], sems.at[0, k])
+            for k, (at, size, _, _) in enumerate(jobs)
+        ]
+        writes = [
+            pltpu.make_async_copy(full.at[pl.ds(at, size)], outs[which].at[pl.ds(to, size), :, lanes], sems.at[1, k])
+            for k, (at, size, which, to) in enumerate(jobs)
+        ]
+        for read in reads:
+            read.start()
+        for k, (at, size, _, _) in enumerate(jobs):
+            reads[k].wait()
+            full[at : at + size] = narrow[at : at + size].astype(f32)
+            writes[k].start()
+        for write in writes:
+            write.wait()
+
+    hbm = pl.BlockSpec(memory_space=pltpu.HBM)
     return pl.pallas_call(
-        widen_kernel,
-        out_shape=shape((taps, n, 2 * m)),
-        grid_spec=pltpu.PrefetchScalarGridSpec(
-            num_scalar_prefetch=1,
-            grid=(taps // step,),
-            in_specs=[block] + [pl.BlockSpec(memory_space=pl.ANY)] * len(more),
-            out_specs=placed,
-        ),
-        input_output_aliases={2: 0} if more else {},
+        body,
+        out_shape=[shape((taps * per, n, 2 * m))] + [shape((1, n, 2 * m))] * extra,
+        in_specs=[pl.BlockSpec(memory_space=pltpu.SMEM)] + [hbm] * (1 + len(more)),
+        out_specs=[hbm] * (1 + extra),
+        scratch_shapes=[
+            pltpu.VMEM((total, n, m), bf16),
+            pltpu.VMEM((total, n, m), f32),
+            pltpu.SemaphoreType.DMA((2, len(jobs))),
+        ],
+        input_output_aliases={2 + k: k for k in range(len(more))},
         compiler_params=pltpu.CompilerParams(vmem_limit_bytes=20 * 1024 * 1024),
         cost_estimate=pl.CostEstimate(flops=0, bytes_accessed=0, transcendentals=0),
     )(side.reshape(1), half, *more)
+
+
+def halve_kernel(r, copies):
+    for p in range(r.count):
+        kept, got = getattr(r, f"kept{p}"), getattr(r, f"got{p}")
+        copies.wait(f"kept{p}", f"got{p}")
+        to_send, to_keep = getattr(r, f"sent{p}"), getattr(r, f"left{p}")
+        bit = r.bits[r.steps[p]] == 1
+        h = kept.shape[1] // 2
+        for t in range(kept.shape[0]):
+            total = kept[t] + got[t].astype(f32)
+            low, high = total[:h], total[h:]
+            to_send[t] = jnp.where(bit, low, high).astype(bf16)
+            to_keep[t] = jnp.where(bit, high, low)
+        copies.start(f"sent{p}", f"left{p}")
+    copies.wait(*(name for name in copies.jobs if name[:4] in ("sent", "left")))
+
+
+def halve(bits, pairs, steps, cost):
+    ins = dict(bits=bits)
+    for p, (kept, got) in enumerate(pairs):
+        ins[f"kept{p}"], ins[f"got{p}"] = kept, got
+    taps, n, m = pairs[0][0].shape
+    dims = (taps, n // 2, m)
+    names = [str(p) for p in range(len(pairs))]
+    outs = {}
+    for name in names:
+        outs["sent" + name], outs["left" + name] = shape(dims, bf16), shape(dims)
+
+    def body(r, copies):
+        r.count, r.steps = len(pairs), steps
+        halve_kernel(r, copies)
+
+    far_in = tuple(n for n in ins if n != "bits")
+    out = call(body, ins, outs, far_in=far_in, far_out=tuple(outs), smem=("bits",), cost=cost, limit=60)
+    return [(out["sent" + name], out["left" + name]) for name in names]
 
 
 def shifted(value, axis, steps):
@@ -667,7 +757,8 @@
 
 
 class Tree:
-    def __init__(self, parts, plane, rest, core):
+    def __init__(self, parts, bits, plane, rest, core):
+        self.bits, self.place = bits, {step: k for k, step in enumerate([core, *plane, *rest])}
         self.sent_a, self.kept_a, self.sent_b, self.kept_b = parts
         self.a, self.b, self.rest, self.core = plane, plane[::-1], rest, core
         p, n = len(plane), len(rest)
@@ -691,18 +782,19 @@
         else:
             self.got = (partner(self.value, *self.core),)
 
-    def finish(self, before=None):
+    def finish(self, cost=0):
         kind, k = self.stages.pop(0)
         if kind == "plane":
-            total_a = self.kept_a + self.got[0].astype(f32)
-            total_b = self.kept_b + self.got[1].astype(f32)
-            if k + 1 < len(self.a):
-                self.sent_a, self.kept_a = split(total_a, *self.a[k + 1])
-                self.sent_b, self.kept_b = split(total_b, *self.b[k + 1])
-                keep = self.sent_a, self.kept_a, self.sent_b, self.kept_b
-                if before is not None:
-                    before, keep = lax.optimization_barrier((before, keep))
-                self.sent_a, self.kept_a, self.sent_b, self.kept_b = keep
+            pairs = [(self.kept_a, self.got[0]), (self.kept_b, self.got[1])]
+            nexts = [order[k + 1] for order in (self.a, self.b) if k + 1 < len(order)]
+            if nexts and cost:
+                pairs = halve(self.bits, pairs, [self.place[step] for step in nexts], cost)
+                (self.sent_a, self.kept_a), (self.sent_b, self.kept_b) = pairs
+                return
+            total_a, total_b = (kept + got.astype(f32) for kept, got in pairs)
+            if nexts:
+                self.sent_a, self.kept_a = split(total_a, *nexts[0])
+                self.sent_b, self.kept_b = split(total_b, *nexts[1])
             else:
                 self.taps = total_a.shape[0]
                 self.split_rest(jnp.concatenate([total_a, total_b], axis=0), 0)
@@ -715,7 +807,6 @@
             self.value_a = joined(self.value_a, self.got[0], *self.a[k])
             self.value_b = joined(self.value_b, self.got[1], *self.b[k])
             self.value = jnp.concatenate([self.value_a, self.value_b], axis=1)
-        return before
 
     def split_rest(self, total, k):
         if k < len(self.rest):
@@ -724,13 +815,14 @@
             self.value = total.astype(bf16)
 
 
-def lockstep(*trees):
+def lockstep(*trees, beside=()):
     for t in trees:
         t.start()
-    got = lax.optimization_barrier([t.got for t in trees])
+    got, beside = lax.optimization_barrier(([t.got for t in trees], beside))
     for t, g in zip(trees, got):
         t.got = g
         t.finish()
+    return beside
 
 
 def on_device(inputs, w_first, gain_first, shift_first, w_second, gain_second, shift_second, w_proj, gain_proj, shift_proj, valid_mask, cotangent):
@@ -744,7 +836,7 @@
     plane = steps_of("cols")
     core = steps_of("rows")[0]
     rest = steps_of("rows")[1:] + steps_of("grp")
-    bits = jnp.stack([bit_of(*core), bit_of(*plane[0]), bit_of(*plane[-1])]).astype(jnp.int32)
+    bits = jnp.stack([bit_of(*step) for step in (core, *plane, *rest)]).astype(jnp.int32)
     w1 = w_first.reshape(3, 3 * cin, width)
     w2 = w_second.reshape(3, 3 * width, width)
     as_row = lambda v: v.reshape(1, -1)
@@ -758,19 +850,6 @@
     )
 
     top1 = shifted(inputs[:, -1:], "rows", 1)
-    lft1 = shifted(jnp.concatenate([top1[:, :, -1:], inputs[:, :, -1:]], axis=1), "cols", 1)
-    stats = call(
-        stats_kernel,
-        dict(x=inputs, top=top1, lft=lft1, own=own, w1=w1, wp=w_proj),
-        dict(spread=all_devices(4 * width + 128)),
-        dict(
-            raw=pltpu.VMEM((cin // 128, (rows_in + 1) * groups, cols_in + 8, 128), f32),
-            xe=pltpu.VMEM((rows * groups * cols, 3 * cin), bf16),
-            xo=pltpu.VMEM(((rows + 1) * groups * cols, 3 * cin), bf16),
-        ),
-    )
-    tot1 = gather_sum(stats["spread"])
-
     me, count = lax.axis_index("rows"), lax.axis_size("rows")
     flags = jnp.stack([me > 0, me < count - 1]).astype(jnp.int32)
     flat_rows = shape((over * groups * cols_in + (width // 256 + 1) * rim * groups * cols, 256), bf16)
@@ -778,12 +857,16 @@
         vertical_kernel,
         dict(flags=flags, x=inputs, cot=cotangent, own=own),
         dict(down=flat_rows) if count == 2 else dict(down=flat_rows, up=flat_rows),
+        far_in=("x", "cot"),
         smem=("flags",),
+        parts=dict(x=end_parts(rows_in, over), cot=end_parts(rows, rim)),
     )
     if count == 2:
         top = bot = lax.ppermute(packed["down"], "rows", [(0, 1), (1, 0)])
     else:
         top, bot = shifted(packed["down"], "rows", 1), shifted(packed["up"], "rows", -1)
+    lft1 = shifted(jnp.concatenate([top1[:, :, -1:], inputs[:, :, -1:]], axis=1), "cols", 1)
+    (top, bot), lft1 = lax.optimization_barrier(((top, bot), lft1))
     lines = (rows_in + 2 * over) * groups, (rows + 2 * rim) * groups, (rows + 3) * groups
     n_strip = over * lines[0] + (rim + 1) // 2 * lines[1] + width // 128 * lines[2]
     n_strip = -(-n_strip // 16) * 16
@@ -801,6 +884,19 @@
         smem=("flags",),
     )
     lft, rgt = shifted(strips["right"], "cols", 1), shifted(strips["left"], "cols", -1)
+    lft1, _ = lax.optimization_barrier((lft1, strips["right"]))
+    stats = call(
+        stats_kernel,
+        dict(x=inputs, top=top1, lft=lft1, own=own, w1=w1, wp=w_proj),
+        dict(spread=all_devices(4 * width + 128)),
+        dict(
+            raw=pltpu.VMEM((cin // 128, (rows_in + 1) * groups, cols_in + 8, 128), f32),
+            xe=pltpu.VMEM((rows * groups * cols, 3 * cin), bf16),
+            xo=pltpu.VMEM(((rows + 1) * groups * cols, 3 * cin), bf16),
+        ),
+    )
+    tot1 = gather_sum(stats["spread"])
+
     first = call(
         first_kernel,
         dict(**near, lft=lft, rgt=rgt, w1=w1, wp=w_proj),
@@ -809,7 +905,6 @@
             prep=shape((MP, width)),
             xe=shape((MP, 3 * cin), bf16),
             xo=shape((MP + L, 3 * cin), bf16),
-            keep=shape((MP, width)),
             ownp=shape((MP, 128)),
             maskp=shape((MP, 128)),
             cotq=shape((MQ, width)),
@@ -821,8 +916,10 @@
             flat=pltpu.VMEM((n_strip, 256), f32),
         ),
         far_in=("w1", "wp"),
-        far_out=("xe", "xo", "keep", "cotq"),
+        far_out=("xe", "xo", "pre1", "prep", "cotq"),
         smem=("flags",),
+        cost=20000000000,
+        parts=dict(pre1=row_parts(MP, 3), prep=row_parts(MP, 3)),
     )
     xe, xo, ownp, maskp = first["xe"], first["xo"], first["ownp"], first["maskp"]
     far_xe, far_xo = partner(xe, *core), partner(xo, *core)
@@ -832,8 +929,9 @@
         dict(pre1=first["pre1"], tot1=tot1, gain=g1, shift=b1, maskp=maskp, ownp=ownp, w2=w2),
         dict(h3=shape((MP, 3 * width), bf16), pre2=shape((MQ, width)), spread=all_devices(2 * width), mom1=shape((8, width))),
         dict(hid=pltpu.VMEM((MP + 8, width), f32)),
-        far_in=("w2",),
-        far_out=("h3",),
+        far_in=("pre1", "w2"),
+        far_out=("h3", "pre2"),
+        parts=dict(pre2=row_parts(MQ, 3)),
     )
     h3, pre2, mom1 = second["h3"], second["pre2"], second["mom1"]
     tot2 = gather_sum(second["spread"])
@@ -852,8 +950,9 @@
             mom2=shape((8, width)),
         ),
         dict(field=pltpu.VMEM((MQ, width), f32)),
-        far_in=("cotq",),
+        far_in=("pre2", "prep", "cotq"),
         far_out=("out", "grad"),
+        parts=dict(grad=row_parts(MQ, 2)),
     )
     mom2 = third["mom2"]
     tot3 = gather_sum(third["spread"])
@@ -869,11 +968,14 @@
             theirs=shape((2 * MW, half), bf16),
             gq=shape((MQ + 8, width)),
             gpu=shape((MW, width), bf16),
-            sums=vec(3),
+            gain_second=vec(1),
+            shift_second=vec(1),
+            gain_proj=vec(1),
+            shift_proj=vec(1),
         ),
         dict(gpq=pltpu.VMEM((MQ, width), f32)),
-        far_in=("grad",),
-        far_out=("gpu",),
+        far_in=("pre2", "prep", "grad"),
+        far_out=("gpu", "gq"),
         smem=("bits",),
     )
     far2 = partner(fourth["theirs"], *core)
@@ -882,44 +984,44 @@
         dims = (taps, cin // 4, half)
         return dict(sent_a=shape(dims, bf16), kept_a=shape(dims), sent_b=shape(dims, bf16), kept_b=shape(dims))
 
-    taps2 = 9 * width // cin + 1
+    per = width // cin
+    taps2 = 9 * per + 1
     second_parts = call(
         weights_second_kernel,
         dict(bits=bits, h3=h3, h3_far=far_h3, xe=xe, xe_far=far_xe, near=fourth["mine"], far=far2),
         chunk_shapes(taps2),
-        dict(acc=pltpu.VMEM((3 * width, half), f32)),
+        dict(acc=pltpu.VMEM((width, half), f32)),
         far_in=("h3", "h3_far", "xe", "xe_far"),
         far_out=("kept_a", "kept_b"),
         smem=("bits",),
+        parts=dict(
+            h3=lane_parts(3 * width, 3),
+            h3_far=lane_parts(3 * width, 3),
+            kept_a=row_parts(taps2 - 1, 3) + [(3, (pl.ds(taps2 - 1, 1),))],
+            kept_b=row_parts(taps2 - 1, 3) + [(3, (pl.ds(taps2 - 1, 1),))],
+        ),
     ).values()
     gq, *second_parts = lax.optimization_barrier((fourth["gq"], *second_parts))
 
-    tree2 = Tree(second_parts, plane, rest, core)
+    tree2 = Tree(second_parts, bits, plane, rest, core)
     tree2.start()
     hidden = call(
         hidden_kernel,
-        dict(w2=w2, keep=first["keep"], mom1=mom1, gain=g1, shift=b1, gq=gq, maskp=maskp, ownp=ownp),
+        dict(gq=gq, w2=w2, keep=first["pre1"], mom1=mom1, gain=g1, shift=b1, maskp=maskp, ownp=ownp),
         dict(act=shape((MU, width)), normed=shape((MU, width)), spread=all_devices(2 * width)),
         dict(g3=pltpu.VMEM((MQ, 3 * width), bf16)),
-        far_in=("w2", "keep"),
-    )
-    spread4 = tree2.finish(hidden["spread"])
-    tot4 = gather_sum(spread4)
-    tree2.start()
-    tot4, tree2.got = lax.optimization_barrier((tot4, tree2.got))
-    act = tree2.finish(hidden["act"])
-
+        far_in=("gq", "w2", "keep"),
+        parts=dict(w2=[(k, (pl.ds(2 - k, 1),)) for k in range(3)]),
+    )
+    tot4 = gather_sum(hidden["spread"])
+    tree2.finish(20000000000)
+    act, tree2.sent_a, tree2.sent_b = lax.optimization_barrier((hidden["act"], tree2.sent_a, tree2.sent_b))
     tree2.start()
     fifth = call(
         fifth_kernel,
-        dict(
-            bits=bits, act=act, normed=hidden["normed"], mom1=mom1, tot4=tot4, gain=g1, maskp=maskp, ownp=ownp
-        ),
-        dict(
-            mine=shape((MW, half), bf16), theirs=shape((MW, half), bf16), gu=shape((MU, 2 * width), bf16), sums=vec(2)
-        ),
+        dict(bits=bits, act=act, normed=hidden["normed"], mom1=mom1, tot4=tot4, gain=g1, maskp=maskp, ownp=ownp),
+        dict(mine=shape((MW, half), bf16), theirs=shape((MW, half), bf16), gain_first=vec(1), shift_first=vec(1)),
         dict(gf=pltpu.VMEM((MU + 16, width), f32)),
-        far_out=("gu",),
         smem=("bits",),
     )
     far1 = partner(fifth["theirs"], *core)
@@ -928,62 +1030,65 @@
         dict(bits=bits, xe=xe, xo=xo, xe_far=far_xe, xo_far=far_xo, near=fifth["mine"], far=far1),
         chunk_shapes(9),
         dict(acc=pltpu.VMEM((3 * cin, half), f32)),
-        far_in=("xe", "xo", "xe_far", "xo_far"),
+        far_in=("xe", "xe_far", "xo", "xo_far"),
         far_out=("kept_a", "kept_b"),
         smem=("bits",),
+        parts=dict(kept_a=row_parts(9, 3), kept_b=row_parts(9, 3)),
     ).values()
-    gu, tree2.got, *first_parts = lax.optimization_barrier((fifth["gu"], tree2.got, *first_parts))
+    tree2.got, *first_parts = lax.optimization_barrier((tree2.got, *first_parts))
     tree2.finish()
-    tree1 = Tree(first_parts, plane, rest, core)
+    tree1 = Tree(first_parts, bits, plane, rest, core)
 
     grad_inputs = call(
         inputs_kernel,
-        dict(gu=gu, gpu=fourth["gpu"], w1=w1, wp=w_proj),
+        dict(
+            act=act, normed=hidden["normed"], gpu=fourth["gpu"], w1=w1, wp=w_proj, mom1=mom1, gain=g1, maskp=maskp,
+            gg=fifth["gain_first"], gs=fifth["shift_first"],
+        ),
         dict(out=shape((groups, rows_in, cols_in, cin), bf16)),
-        dict(lines=pltpu.VMEM((cin // 128, rows_in * groups, cols_in, 128), f32)),
-        far_in=("gu", "gpu", "w1", "wp"),
+        dict(
+            lines=pltpu.VMEM((cin // 128, rows_in * groups, cols_in, 128), f32),
+            gf=pltpu.VMEM((MU + 16, width), f32),
+            gu=pltpu.VMEM((MU, 2 * width), bf16),
+        ),
+        far_in=("act", "normed", "gpu", "w1", "wp"),
         far_out=("out",),
+        cost=10000000000,
     )["out"]
     side = bit_of(*core).astype(jnp.int32)
+    grad_inputs = lockstep(tree2, tree1, beside=grad_inputs)
     while tree2.next() != ("plane_join", 0):
         lockstep(tree2, tree1)
     tree2.start()
-    while tree1.next()[0] != "rest_join" or tree1.next()[1] > 0:
+    while tree1.next() != ("plane_join", 0):
         tree1.start()
-        tree1.finish()
+        if tree1.next() != ("plane_join", 1):
+            tree1.finish()
+        else:
+            tree1.got, tree2.got = lax.optimization_barrier((tree1.got, tree2.got))
+            tree1.finish()
+    tree2.finish()
+    tree2.start()
     tree1.start()
-    tree1.got, tree2.got, grad_inputs = lax.optimization_barrier((tree1.got, tree2.got, grad_inputs))
+    grad_second = widen(tree2.got[0], 1 - side, 9, per, True, widen(tree2.value, side, 9, per, True))
+    tree1.got, grad_second = lax.optimization_barrier((tree1.got, grad_second))
+    grad_w2, grad_wp = grad_second
     tree1.finish()
-    tree2.finish()
-    half2 = tree2.value
-    lockstep(tree2, tree1)
-    other2 = tree2.got[0]
-    grad_w2 = widen(other2, 1 - side, taps2 - 1, widen(half2, side, taps2 - 1))
-    ends = half2[taps2 - 1], other2[taps2 - 1]
-    grad_wp = jnp.concatenate(
-        [jnp.where(side == 1, ends[1], ends[0]), jnp.where(side == 1, ends[0], ends[1])], axis=1
-    ).astype(f32)
-    while tree1.next()[0] != "core":
-        tree1.start()
-        tree1.got, grad_w2, grad_wp = lax.optimization_barrier((tree1.got, grad_w2, grad_wp))
-        tree1.finish()
-    half1 = tree1.value
     tree1.start()
-    grad_w1 = widen(tree1.got[0], 1 - side, 9, widen(half1, side, 9))
-
-    s3, s4 = fourth["sums"].reshape(3, width), fifth["sums"].reshape(2, width)
+    (grad_w1,) = widen(tree1.got[0], 1 - side, 3, 3, False, widen(tree1.value, side, 3, 3, False))
+
     return (
         third["out"],
         grad_inputs,
         grad_w1.reshape(w_first.shape),
-        s4[0],
-        s4[1],
+        fifth["gain_first"].reshape(width),
+        fifth["shift_first"].reshape(width),
         grad_w2.reshape(w_second.shape),
-        s3[0],
-        s3[1],
-        grad_wp,
-        s3[2],
-        s3[1],
+        fourth["gain_second"].reshape(width),
+        fourth["shift_second"].reshape(width),
+        grad_wp.reshape(w_proj.shape),
+        fourth["gain_proj"].reshape(width),
+        fourth["shift_proj"].reshape(width),
     )
 
 

time: 232 us -> 215 us (0.927)
  waiting for transfers between devices: 86.1 us -> 77.1 us
  Pallas kernels: 78 us -> 71.5 us
  starting transfers between devices: 49.6 us -> 54.6 us
  other arithmetic: 9.23 us -> 6.58 us
  local copies, waits for them, and re-layouts: 5.85 us -> 3.23 us
    ppermute x4, waiting for transfers between devices: 14 us -> 2.46 us  [shifted(): lax.ppermute(value, axis, [(source, source + steps) for source in range(f...]
    ppermute x31, waiting for transfers between devices: 47.7 us -> 52.5 us  [partner(): return lax.ppermute(value, axis, [(i, i ^ step) for i in range(count)])]
    pallas_call x12 -> x13, Pallas kernels: 65.9 us -> 61.2 us  [call(): pl.pallas_call(run, out_shape=list(outs.values()), in_specs=[spec(n) for...]
    ppermute x31, starting transfers between devices: 21.4 us -> 24.9 us  [partner(): return lax.ppermute(value, axis, [(i, i ^ step) for i in range(count)])]
  transfers between devices with their start and end apart: 40 -> 40, of which waited for: 21 -> 26; matrix products, arithmetic and copies ran while one was open for 3% -> 1% of each run, Pallas kernels for 26% -> 24%
where the time goes in v2:
time: 215 us
  waiting for transfers between devices  77.1 us (36%)
  Pallas kernels  71.5 us (33%)
  starting transfers between devices  54.6 us (25%)
  other arithmetic  6.58 us (3%)
  local copies, waits for them, and re-layouts  3.23 us (2%)
    pallas_call x13, Pallas kernels, call(): pl.pallas_call(run, out_shape=list(outs.values()), in_specs=[spec(n) for...  61.2 us
    ppermute x31, waiting for transfers between devices, partner(): return lax.ppermute(value, axis, [(i, i ^ step) for i in range(count)])  52.5 us
    ppermute x31, starting transfers between devices, partner(): return lax.ppermute(value, axis, [(i, i ^ step) for i in range(count)])  24.9 us
    all_to_all x4, waiting for transfers between devices, gather_sum(): return lax.all_to_all(spread, axes, 0, 0)  22.1 us
    all_to_all x4, starting transfers between devices, gather_sum(): return lax.all_to_all(spread, axes, 0, 0)  16.8 us
    ppermute x4, starting transfers between devices, shifted(): lax.ppermute(value, axis, [(source, source + steps) for source in range(f...  12.3 us
    pallas_call x4, Pallas kernels, widen(): pl.pallas_call(body, out_shape=[shape((taps * per, n, 2 * m))] + [shape((...  10.3 us
  transfers between devices with their start and end apart: 40, of which 26 were waited for; matrix products, arithmetic and copies ran while one was open for 1% of the time, Pallas kernels for 24%

profile of v2, /device:TPU:0, one launch (start us, length us, event | category | flops | bytes accessed | tf_op | source)
XLA Modules:
  0.0 214.6 jit_solution(10351591191531077571)
XLA Ops:
  5.1 2.0 collective-permute-start.1
  7.9 4.8 %collective-permute-start.2 = (bf16[2,17,1,256]{3,2,1,0:T(2,128)(2,1)S(1)}, bf16[2,17,1,256]{3,2,1,0:T(2,128)(2,1)S(1)}, u32[]{:S(2)}, u32[]{:S(2)}) collective-permute-start(bf16[2,17,1,256]{3,2,1,0:T(2,128)(2,1)S(1)} %pad_maximum_fusion.12), channel_id=1, source_target_pairs={{0,4},{4,8},{8,12},{1,5},{5,9},{9,13},{2,6},{6,10},{10,14},{3,7},{... | collective-permute-start | bytes 52232 | tf_op jit(solution)/shard_map/ppermute | solution.py:723
  12.8 1.6 collective-permute-done.2.refs_2_
  15.7 4.2 %collective-permute-start.3 = (bf16[480,256]{1,0:T(8,128)(2,1)S(1)}, bf16[480,256]{1,0:T(8,128)(2,1)S(1)}, u32[]{:S(2)}, u32[]{:S(2)}) collective-permute-start(bf16[480,256]{1,0:T(8,128)(2,1)S(1)} %get-tuple-element.101), channel_id=1, source_target_pairs={{0,4},{4,8},{8,12},{1,5},{5,9},{9,13},{2,6},{6,10},{10,14},{3,7},{... | collective-permute-start | bytes 737288 | tf_op jit(solution)/shard_map/ppermute | solution.py:723
  21.2 3.3 %shard_map.206 = f32[32,1,2176]{2,1,0:T(1,128)} custom-call(bf16[2,16,32,256]{3,2,1,0:T(8,128)(2,1)S(1)} %copy-done.1, bf16[2,1,32,256]{3,2,1,0:T(8,128)(2,1)S(1)} %collective-permute-done.1.refs_1_, bf16[2,17,1,256]{3,2,1,0:T(2,128)(2,1)S(1)} %collective-permute-done.2.refs_2_, bf16[2,8,16,128]{3,2,1,0:T(8,128)(2,1)S(1)} %broadcast_in_dim.2.refs_3_, ...), custom_call_target="tpu_custom_call" | custom-call | tf_op jit(solution)/shard_map/pallas_call | solution.py:89
  24.6 7.9 %all-to-all-start = ((f32[32,1,2176]{2,1,0:T(1,128)}), f32[32,1,2176]{2,1,0:T(1,128)S(1)}, u32[]{:S(2)}, u32[]{:S(2)}) async-start(f32[32,1,2176]{2,1,0:T(1,128)} %shard_map.206), calls=%async_computation | async-start | bytes 557056 | tf_op jit(solution)/shard_map/all_to_all | solution.py:727
  32.6 5.8 %shard_map.205 = (f32[624,512]{1,0:T(8,128)}, f32[624,512]{1,0:T(8,128)}, bf16[624,768]{1,0:T(8,128)(2,1)}, bf16[672,768]{1,0:T(8,128)(2,1)}, f32[624,128]{1,0:T...) custom-call(s32[2]{0:T(128)S(1)} %add_convert_fusion.2.refs_0_, bf16[2,16,32,256]{3,2,1,0:T(8,128)(2,1)} %refs_0_.1, ...), custom_call_target="tpu_custom_call" | custom-call | flops 20000000000 | tf_op jit(solution)/shard_map/pallas_call | solution.py:89
  38.4 5.4 %all-to-all-done.refs_1_ = f32[32,1,2176]{2,1,0:T(1,128)S(1)} async-done(((f32[32,1,2176]{2,1,0:T(1,128)}), f32[32,1,2176]{2,1,0:T(1,128)S(1)}, u32[]{:S(2)}, u32[]{:S(2)}) %all-to-all-start) | async-done | bytes 278560 | tf_op jit(solution)/shard_map/all_to_all | solution.py:727
  43.8 7.0 %shard_map.207 = (bf16[624,1536]{1,0:T(8,128)(2,1)}, f32[528,512]{1,0:T(8,128)}, f32[32,1,1024]{2,1,0:T(1,128)}, f32[8,512]{1,0:T(8,128)S(1)}) custom-call(f32[624,512]{1,0:T(8,128)} %get-tuple-element.103.refs_0_.refs_2_, f32[32,1,2176]{2,1,0:T(1,128)S(1)} %all-to-all-done.refs_1_, f32[1,512]{1,0:T(1,128)S(1)} %bitcast.25, f32[1,512]{1,0:T(1,128)S(1)} %bitcast.33, ...), custom_call_target="tpu_custom_call" | custom-call | tf_op jit(solution)/shard_map/pallas_call | solution.py:89
  50.9 2.6 %all-to-all-start.1 = ((f32[32,1,1024]{2,1,0:T(1,128)}), f32[32,1,1024]{2,1,0:T(1,128)S(1)}, u32[]{:S(2)}, u32[]{:S(2)}) async-start(f32[32,1,1024]{2,1,0:T(1,128)} %get-tuple-element.111), calls=%async_computation.1 | async-start | bytes 262144 | tf_op jit(solution)/shard_map/all_to_all | solution.py:727
  53.8 7.6 %all-to-all-done.1.refs_3_ = f32[32,1,1024]{2,1,0:T(1,128)S(1)} async-done(((f32[32,1,1024]{2,1,0:T(1,128)}), f32[32,1,1024]{2,1,0:T(1,128)S(1)}, u32[]{:S(2)}, u32[]{:S(2)}) %all-to-all-start.1) | async-done | bytes 131104 | tf_op jit(solution)/shard_map/all_to_all | solution.py:727
  61.4 5.3 %shard_map.208 = (bf16[2,8,16,512]{3,2,1,0:T(8,128)(2,1)}, f32[528,512]{1,0:T(8,128)}, f32[32,1,1536]{2,1,0:T(1,128)}, f32[8,512]{1,0:T(8,128)S(1)}) custom-call(f32[528,512]{1,0:T(8,128)} %get-tuple-element.108.refs_0_.refs_1_, f32[624,512]{1,0:T(8,128)} %get-tuple-element.109.refs_1_.refs_2_, f32[8,512]{1,0:T(8,128)S(1)} %get-tuple-element.110.refs_2_.refs_3_.refs_5_, ...), custom_call_target="tpu_custom_call" | custom-call | tf_op jit(solution)/shard_map/pallas_call | solution.py:89
  66.7 2.8 %all-to-all-start.2 = ((f32[32,1,1536]{2,1,0:T(1,128)}), f32[32,1,1536]{2,1,0:T(1,128)S(1)}, u32[]{:S(2)}, u32[]{:S(2)}) async-start(f32[32,1,1536]{2,1,0:T(1,128)} %get-tuple-element.115), calls=%async_computation.2 | async-start | bytes 393216 | tf_op jit(solution)/shard_map/all_to_all | solution.py:727
  69.7 9.1 %all-to-all-done.2.refs_5_ = f32[32,1,1536]{2,1,0:T(1,128)S(1)} async-done(((f32[32,1,1536]{2,1,0:T(1,128)}), f32[32,1,1536]{2,1,0:T(1,128)S(1)}, u32[]{:S(2)}, u32[]{:S(2)}) %all-to-all-start.2) | async-done | bytes 196640 | tf_op jit(solution)/shard_map/all_to_all | solution.py:727
  78.7 4.9 %shard_map.209 = (bf16[768,256]{1,0:T(8,128)(2,1)S(1)}, bf16[768,256]{1,0:T(8,128)(2,1)S(1)}, f32[536,512]{1,0:T(8,128)}, bf16[384,512]{1,0:T(8,128)(2,1)}, f32[...) custom-call(s32[5]{0:T(128)S(1)} %stack.35.refs_0_, ...), custom_call_target="tpu_custom_call" | custom-call | tf_op jit(solution)/shard_map/pallas_call | solution.py:89
  83.7 1.7 collective-permute-done.7.refs_6_
  85.4 8.1 %shard_map.210 = (bf16[19,64,256]{2,1,0:T(8,128)(2,1)S(1)}, f32[19,64,256]{2,1,0:T(8,128)}, bf16[19,64,256]{2,1,0:T(8,128)(2,1)}, f32[19,64,256]{2,1,0:T(8,128)}) custom-call(s32[5]{0:T(128)S(1)} %stack.35.refs_0_, bf16[624,1536]{1,0:T(8,128)(2,1)} %get-tuple-element.118.refs_1_, bf16[624,1536]{1,0:T(8,128)(2,1)} %collective-permute-done.5.refs_2_, ...), custom_call_target="tpu_custom_call" | custom-call | tf_op jit(solution)/shard_map/pallas_call | solution.py:89
  94.6 6.5 %shard_map.212 = (f32[432,512]{1,0:T(8,128)S(1)}, f32[432,512]{1,0:T(8,128)}, f32[32,1,1024]{2,1,0:T(1,128)}) custom-call(f32[536,512]{1,0:T(8,128)} %get-tuple-element.131.refs_0_, bf16[3,1536,512]{2,1,0:T(8,128)(2,1)} %bitcast.40, f32[624,512]{1,0:T(8,128)} %get-tuple-element.103.refs_0_.refs_2_, f32[8,512]{1,0:T(8,128)S(1)} %get-tuple-element.110.refs_2_.refs_3_.refs_5_, ...), custom_call_target="tpu_custom_call" | custom-call | tf_op jit(solution)/shard_map/pallas_call | solution.py:89
  102.0 3.5 %all-to-all-start.3 = ((f32[32,1,1024]{2,1,0:T(1,128)}), f32[32,1,1024]{2,1,0:T(1,128)S(1)}, u32[]{:S(2)}, u32[]{:S(2)}) async-start(f32[32,1,1024]{2,1,0:T(1,128)} %get-tuple-element.140), calls=%async_computation.3 | async-start | bytes 262144 | tf_op jit(solution)/shard_map/all_to_all | solution.py:727
  105.6 4.7 %collective-permute-done.8.refs_2_ = bf16[19,64,256]{2,1,0:T(8,128)(2,1)} collective-permute-done((bf16[19,64,256]{2,1,0:T(8,128)(2,1)S(1)}, bf16[19,64,256]{2,1,0:T(8,128)(2,1)}, u32[]{:S(2)}, u32[]{:S(2)}) %collective-permute-start.8) | collective-permute-done | bytes 622624 | tf_op jit(solution)/shard_map/ppermute | solution.py:736
  111.3 3.8 %shard_map.211 = (bf16[19,32,256]{2,1,0:T(8,128)(2,1)}, f32[19,32,256]{2,1,0:T(8,128)}, bf16[19,32,256]{2,1,0:T(8,128)(2,1)}, f32[19,32,256]{2,1,0:T(8,128)}) custom-call(s32[5]{0:T(128)} %copy-done.9, f32[19,64,256]{2,1,0:T(8,128)} %get-tuple-element.126.refs_1_, bf16[19,64,256]{2,1,0:T(8,128)(2,1)} %collective-permute-done.8.refs_2_, ...), custom_call_target="tpu_custom_call" | custom-call | flops 20000000000 | tf_op jit(solution)/shard_map/pallas_call | solution.py:89
  115.4 2.0 collective-permute-start.11
  117.4 2.2 %shard_map.213 = (bf16[384,256]{1,0:T(8,128)(2,1)S(1)}, bf16[384,256]{1,0:T(8,128)(2,1)S(1)}, f32[1,512]{1,0:T(1,128)}, f32[1,512]{1,0:T(1,128)}) custom-call(s32[5]{0:T(128)S(1)} %copy-done.10, f32[432,512]{1,0:T(8,128)} %copy-done.5, f32[432,512]{1,0:T(8,128)} %get-tuple-element.139.refs_2_.refs_1_, ...), custom_call_target="tpu_custom_call" | custom-call | tf_op jit(solution)/shard_map/pallas_call | solution.py:89
  119.6 1.4 collective-permute-done.13.refs_6_
  121.0 5.7 %shard_map.214 = (bf16[9,64,256]{2,1,0:T(8,128)(2,1)S(1)}, f32[9,64,256]{2,1,0:T(8,128)S(1)}, bf16[9,64,256]{2,1,0:T(8,128)(2,1)S(1)}, f32[9,64,256]{2,1,0:T(8,128)}) custom-call(s32[5]{0:T(128)S(1)} %copy-done.10, bf16[624,768]{1,0:T(8,128)(2,1)} %get-tuple-element.119.refs_3_.refs_1_, bf16[672,768]{1,0:T(8,128)(2,1)} %get-tuple-element.137.refs_2_, ...), custom_call_target="tpu_custom_call" | custom-call | tf_op jit(solution)/shard_map/pallas_call | solution.py:89
  129.3 6.4 %shard_map.215 = bf16[2,16,32,256]{3,2,1,0:T(8,128)(2,1)} custom-call(f32[432,512]{1,0:T(8,128)S(1)} %copy-done.6, f32[432,512]{1,0:T(8,128)} %get-tuple-element.139.refs_2_.refs_1_, bf16[384,512]{1,0:T(8,128)(2,1)S(1)} %copy-done.16, bf16[3,768,512]{2,1,0:T(8,128)(2,1)} %bitcast.45, bf16[256,512]{1,0:T(8,128)(2,1)S(1)} %copy-done.7, ...), custom_call_target="tpu_custom_call" | custom-call | flops 10000000000 | tf_op jit(solution)/shard_map/pallas_call | solution.py:89
  136.8 1.8 collective-permute-start.19
  139.0 1.5 collective-permute-start.18
  140.5 1.5 collective-permute-done.19
  142.0 2.2 %collective-permute-done.18 = bf16[9,32,256]{2,1,0:T(8,128)(2,1)S(1)} collective-permute-done((bf16[9,32,256]{2,1,0:T(8,128)(2,1)S(1)}, bf16[9,32,256]{2,1,0:T(8,128)(2,1)S(1)}, u32[]{:S(2)}, u32[]{:S(2)}) %collective-permute-start.18) | collective-permute-done | bytes 147488 | tf_op jit(solution)/shard_map/ppermute | solution.py:736
  144.2 3.2 %collective-permute-done.17 = bf16[38,8,256]{2,1,0:T(8,128)(2,1)S(1)} collective-permute-done((bf16[38,8,256]{2,1,0:T(8,128)(2,1)S(1)}, bf16[38,8,256]{2,1,0:T(8,128)(2,1)S(1)}, u32[]{:S(2)}, u32[]{:S(2)}) %collective-permute-start.17) | collective-permute-done | bytes 155680 | tf_op jit(solution)/shard_map/ppermute | solution.py:736
  147.8 1.7 collective-permute-start.21
  149.5 6.7 %collective-permute-done.21 = bf16[18,16,256]{2,1,0:T(8,128)(2,1)S(1)} collective-permute-done((bf16[18,16,256]{2,1,0:T(8,128)(2,1)S(1)}, bf16[18,16,256]{2,1,0:T(8,128)(2,1)S(1)}, u32[]{:S(2)}, u32[]{:S(2)}) %collective-permute-start.21) | collective-permute-done | bytes 147488 | tf_op jit(solution)/shard_map/ppermute | solution.py:736
  156.5 2.8 %collective-permute-start.23 = (bf16[18,8,256]{2,1,0:T(8,128)(2,1)S(1)}, bf16[18,8,256]{2,1,0:T(8,128)(2,1)S(1)}, u32[]{:S(2)}, u32[]{:S(2)}) collective-permute-start(bf16[18,8,256]{2,1,0:T(8,128)(2,1)S(1)} %select_convert_fusion.5), channel_id=1, source_target_pairs={{0,2},{1,3},{2,0},{3,1},{4,6},{5,7},{6,4},{7,5},{8,10},{9,11},{10,... | collective-permute-start | bytes 221192 | tf_op jit(solution)/shard_map/ppermute | solution.py:736
  159.2 5.0 %collective-permute-done.23 = bf16[18,8,256]{2,1,0:T(8,128)(2,1)S(1)} collective-permute-done((bf16[18,8,256]{2,1,0:T(8,128)(2,1)S(1)}, bf16[18,8,256]{2,1,0:T(8,128)(2,1)S(1)}, u32[]{:S(2)}, u32[]{:S(2)}) %collective-permute-start.23) | collective-permute-done | bytes 73760 | tf_op jit(solution)/shard_map/ppermute | solution.py:736
  164.3 2.2 %collective-permute-done.22 = bf16[38,16,256]{2,1,0:T(8,128)(2,1)S(1)} collective-permute-done((bf16[38,16,256]{2,1,0:T(8,128)(2,1)S(1)}, bf16[38,16,256]{2,1,0:T(8,128)(2,1)S(1)}, u32[]{:S(2)}, u32[]{:S(2)}) %collective-permute-start.22) | collective-permute-done | bytes 311328 | tf_op jit(solution)/shard_map/ppermute | solution.py:736
  166.7 1.5 collective-permute-start.24
  170.3 4.1 %collective-permute-done.26 = bf16[18,8,256]{2,1,0:T(8,128)(2,1)S(1)} collective-permute-done((bf16[18,8,256]{2,1,0:T(8,128)(2,1)S(1)}, bf16[18,8,256]{2,1,0:T(8,128)(2,1)S(1)}, u32[]{:S(2)}, u32[]{:S(2)}) %collective-permute-start.26) | collective-permute-done | bytes 73760 | tf_op jit(solution)/shard_map/ppermute | solution.py:736
  174.6 1.5 collective-permute-done.25
  176.7 2.0 collective-permute-start.27
  179.1 2.8 %collective-permute-done.27 = bf16[18,16,256]{2,1,0:T(8,128)(2,1)S(1)} collective-permute-done((bf16[18,16,256]{2,1,0:T(8,128)(2,1)S(1)}, bf16[18,16,256]{2,1,0:T(8,128)(2,1)S(1)}, u32[]{:S(2)}, u32[]{:S(2)}) %collective-permute-start.27) | collective-permute-done | bytes 147488 | tf_op jit(solution)/shard_map/ppermute | solution.py:736
  182.0 1.7 collective-permute-start.28
  184.5 8.5 %collective-permute-done.28 = bf16[9,32,256]{2,1,0:T(8,128)(2,1)S(1)} collective-permute-done((bf16[9,32,256]{2,1,0:T(8,128)(2,1)S(1)}, bf16[9,32,256]{2,1,0:T(8,128)(2,1)S(1)}, u32[]{:S(2)}, u32[]{:S(2)}) %collective-permute-start.28) | collective-permute-done | bytes 147488 | tf_op jit(solution)/shard_map/ppermute | solution.py:736
  193.0 2.1 collective-permute-done.29
  199.2 2.8 %shard_map.216 = (f32[18,256,512]{2,1,0:T(8,128)}, f32[1,256,512]{2,1,0:T(8,128)}) custom-call(s32[1]{0:T(128)} %bitcast.10.side_ref, bf16[19,256,256]{2,1,0:T(8,128)(2,1)S(1)} %pad_maximum_fusion.half_ref), custom_call_target="tpu_custom_call" | custom-call | tf_op jit(solution)/shard_map/pallas_call | solution.py:668
  202.0 3.4 %shard_map.217 = (f32[18,256,512]{2,1,0:T(8,128)}, f32[1,256,512]{2,1,0:T(8,128)}) custom-call(s32[1]{0:T(128)} %bitcast.15.side_ref, bf16[19,256,256]{2,1,0:T(8,128)(2,1)} %collective-permute-done.34.half_ref, f32[18,256,512]{2,1,0:T(8,128)} %get-tuple-element.175.refs_0_, ...), custom_call_target="tpu_custom_call", output_to_operand_aliasing={{0}: (2, {}), {1}: (3, {})} | custom-call | tf_op jit(solution)/shard_map/pallas_call | solution.py:668
  209.5 2.1 shard_map.218.refs_0_
  212.4 2.1 shard_map.219
  (142 shorter events, 29.6 us)
Async XLA Ops:
  3.5 17.7 %copy-start.1 = (bf16[2,16,32,256]{3,2,1,0:T(8,128)(2,1)S(1)}, bf16[2,16,32,256]{3,2,1,0:T(8,128)(2,1)}, u32[]{:S(2)}) copy-start(bf16[2,16,32,256]{3,2,1,0:T(8,128)(2,1)} %refs_0_.1) | copy-start | bytes 1572868
  3.5 17.7 %copy-start.7 = (bf16[256,512]{1,0:T(8,128)(2,1)S(1)}, bf16[256,512]{1,0:T(8,128)(2,1)}, u32[]{:S(2)}) copy-start(bf16[256,512]{1,0:T(8,128)(2,1)} %refs_4_.1) | copy-start | bytes 786436
  4.5 9.8 %collective-permute-start = (bf16[672,256]{1,0:T(8,128)(2,1)S(1)}, bf16[672,256]{1,0:T(8,128)(2,1)S(1)}, u32[]{:S(2)}, u32[]{:S(2)}) collective-permute-start(bf16[672,256]{1,0:T(8,128)(2,1)S(1)} %shard_map.203), channel_id=1, source_target_pairs={{0,16},{16,0},{1,17},{17,1},{2,18},{18,2},{3,19},{19,3},{4,20},{20... | collective-permute-start | bytes 1032200 | tf_op jit(solution)/shard_map/ppermute | solution.py:865
  5.1 2.8 %collective-permute-start.1 = (bf16[2,1,32,256]{3,2,1,0:T(8,128)(2,1)S(1)}, bf16[2,1,32,256]{3,2,1,0:T(8,128)(2,1)S(1)}, u32[]{:S(2)}, u32[]{:S(2)}) collective-permute-start(bf16[2,1,32,256]{3,2,1,0:T(8,128)(2,1)S(1)} %slice.57), channel_id=1, source_target_pairs={{0,16},{1,17},{2,18},{3,19},{4,20},{5,21},{6,22},{7,23},{8,24},{9,... | collective-permute-start | bytes 98312 | tf_op jit(solution)/shard_map/ppermute | solution.py:723
  7.9 6.4 %collective-permute-start.2 = (bf16[2,17,1,256]{3,2,1,0:T(2,128)(2,1)S(1)}, bf16[2,17,1,256]{3,2,1,0:T(2,128)(2,1)S(1)}, u32[]{:S(2)}, u32[]{:S(2)}) collective-permute-start(bf16[2,17,1,256]{3,2,1,0:T(2,128)(2,1)S(1)} %pad_maximum_fusion.12), channel_id=1, source_target_pairs={{0,4},{4,8},{8,12},{1,5},{5,9},{9,13},{2,6},{6,10},{10,14},{3,7},{... | collective-permute-start | bytes 52232 | tf_op jit(solution)/shard_map/ppermute | solution.py:723
  15.7 16.8 %collective-permute-start.3 = (bf16[480,256]{1,0:T(8,128)(2,1)S(1)}, bf16[480,256]{1,0:T(8,128)(2,1)S(1)}, u32[]{:S(2)}, u32[]{:S(2)}) collective-permute-start(bf16[480,256]{1,0:T(8,128)(2,1)S(1)} %get-tuple-element.101), channel_id=1, source_target_pairs={{0,4},{4,8},{8,12},{1,5},{5,9},{9,13},{2,6},{6,10},{10,14},{3,7},{... | collective-permute-start | bytes 737288 | tf_op jit(solution)/shard_map/ppermute | solution.py:723
  19.9 12.7 %collective-permute-start.4 = (bf16[480,256]{1,0:T(8,128)(2,1)S(1)}, bf16[480,256]{1,0:T(8,128)(2,1)S(1)}, u32[]{:S(2)}, u32[]{:S(2)}) collective-permute-start(bf16[480,256]{1,0:T(8,128)(2,1)S(1)} %get-tuple-element.102), channel_id=1, source_target_pairs={{4,0},{8,4},{12,8},{5,1},{9,5},{13,9},{6,2},{10,6},{14,10},{7,3},{... | collective-permute-start | bytes 737288 | tf_op jit(solution)/shard_map/ppermute | solution.py:723
  24.6 19.2 %all-to-all-start = ((f32[32,1,2176]{2,1,0:T(1,128)}), f32[32,1,2176]{2,1,0:T(1,128)S(1)}, u32[]{:S(2)}, u32[]{:S(2)}) async-start(f32[32,1,2176]{2,1,0:T(1,128)} %shard_map.206), calls=%async_computation | async-start | bytes 557056 | tf_op jit(solution)/shard_map/all_to_all | solution.py:727
  43.8 17.6 %copy-start.11 = (f32[512]{0:T(512)S(1)}, f32[512]{0:T(512)}, u32[]{:S(2)}) copy-start(f32[512]{0:T(512)} %param.17) | copy-start | bytes 6148
  43.8 17.6 %copy-start.12 = (f32[512]{0:T(512)S(1)}, f32[512]{0:T(512)}, u32[]{:S(2)}) copy-start(f32[512]{0:T(512)} %param.20) | copy-start | bytes 6148
  43.8 17.6 %copy-start.14 = (f32[512]{0:T(512)S(1)}, f32[512]{0:T(512)}, u32[]{:S(2)}) copy-start(f32[512]{0:T(512)} %param.18) | copy-start | bytes 6148
  43.8 17.6 %copy-start.15 = (f32[512]{0:T(512)S(1)}, f32[512]{0:T(512)}, u32[]{:S(2)}) copy-start(f32[512]{0:T(512)} %param.21) | copy-start | bytes 6148
  50.8 34.6 %collective-permute-start.5 = (bf16[624,1536]{1,0:T(8,128)(2,1)}, bf16[624,1536]{1,0:T(8,128)(2,1)}, u32[]{:S(2)}, u32[]{:S(2)}) collective-permute-start(bf16[624,1536]{1,0:T(8,128)(2,1)} %get-tuple-element.118.refs_1_), channel_id=1, source_target_pairs={{0,16},{16,0},{1,17},{17,1},{2,18},{18,2},{3,19},{19,3},{4,20},{20... | collective-permute-start | bytes 5750792 | tf_op jit(solution)/shard_map/ppermute | solution.py:736
  50.9 10.5 %all-to-all-start.1 = ((f32[32,1,1024]{2,1,0:T(1,128)}), f32[32,1,1024]{2,1,0:T(1,128)S(1)}, u32[]{:S(2)}, u32[]{:S(2)}) async-start(f32[32,1,1024]{2,1,0:T(1,128)} %get-tuple-element.111), calls=%async_computation.1 | async-start | bytes 262144 | tf_op jit(solution)/shard_map/all_to_all | solution.py:727
  53.5 30.2 %collective-permute-start.6 = (bf16[624,768]{1,0:T(8,128)(2,1)S(1)}, bf16[624,768]{1,0:T(8,128)(2,1)}, u32[]{:S(2)}, u32[]{:S(2)}) collective-permute-start(bf16[624,768]{1,0:T(8,128)(2,1)S(1)} %copy-done.19), channel_id=1, source_target_pairs={{0,16},{16,0},{1,17},{17,1},{2,18},{18,2},{3,19},{19,3},{4,20},{20... | collective-permute-start | bytes 2875400 | tf_op jit(solution)/shard_map/ppermute | solution.py:736
  66.7 12.0 %all-to-all-start.2 = ((f32[32,1,1536]{2,1,0:T(1,128)}), f32[32,1,1536]{2,1,0:T(1,128)S(1)}, u32[]{:S(2)}, u32[]{:S(2)}) async-start(f32[32,1,1536]{2,1,0:T(1,128)} %get-tuple-element.115), calls=%async_computation.2 | async-start | bytes 393216 | tf_op jit(solution)/shard_map/all_to_all | solution.py:727
  69.7 15.8 %copy-start.9 = (s32[5]{0:T(128)}, s32[5]{0:T(128)S(1)}, u32[]{:S(2)}) copy-start(s32[5]{0:T(128)S(1)} %stack.35.refs_0_) | copy-start | bytes 64
  83.6 1.8 collective-permute-start.7
  93.5 16.8 %collective-permute-start.8 = (bf16[19,64,256]{2,1,0:T(8,128)(2,1)S(1)}, bf16[19,64,256]{2,1,0:T(8,128)(2,1)}, u32[]{:S(2)}, u32[]{:S(2)}) collective-permute-start(bf16[19,64,256]{2,1,0:T(8,128)(2,1)S(1)} %get-tuple-element.127), channel_id=1, source_target_pairs={{0,4},{4,0},{8,12},{12,8},{1,5},{5,1},{9,13},{13,9},{2,6},{6,2},{1... | collective-permute-start | bytes 1867784 | tf_op jit(solution)/shard_map/ppermute | solution.py:736
  94.4 16.9 %collective-permute-start.9 = (bf16[19,64,256]{2,1,0:T(8,128)(2,1)}, bf16[19,64,256]{2,1,0:T(8,128)(2,1)}, u32[]{:S(2)}, u32[]{:S(2)}) collective-permute-start(bf16[19,64,256]{2,1,0:T(8,128)(2,1)} %get-tuple-element.129), channel_id=1, source_target_pairs={{0,8},{4,12},{8,0},{12,4},{1,9},{5,13},{9,1},{13,5},{2,10},{6,14},... | collective-permute-start | bytes 1867784 | tf_op jit(solution)/shard_map/ppermute | solution.py:736
  94.6 25.0 %collective-permute-start.12 = (bf16[672,768]{1,0:T(8,128)(2,1)S(1)}, bf16[672,768]{1,0:T(8,128)(2,1)}, u32[]{:S(2)}, u32[]{:S(2)}) collective-permute-start(bf16[672,768]{1,0:T(8,128)(2,1)S(1)} %copy-done.20), channel_id=1, source_target_pairs={{0,16},{16,0},{1,17},{17,1},{2,18},{18,2},{3,19},{19,3},{4,20},{20... | collective-permute-start | bytes 3096584 | tf_op jit(solution)/shard_map/ppermute | solution.py:736
  102.0 15.3 %all-to-all-start.3 = ((f32[32,1,1024]{2,1,0:T(1,128)}), f32[32,1,1024]{2,1,0:T(1,128)S(1)}, u32[]{:S(2)}, u32[]{:S(2)}) async-start(f32[32,1,1024]{2,1,0:T(1,128)} %get-tuple-element.140), calls=%async_computation.3 | async-start | bytes 262144 | tf_op jit(solution)/shard_map/all_to_all | solution.py:727
  105.6 11.8 %copy-start.10 = (s32[5]{0:T(128)S(1)}, s32[5]{0:T(128)}, u32[]{:S(2)}) copy-start(s32[5]{0:T(128)} %copy-done.9) | copy-start | bytes 64
  115.1 11.6 %collective-permute-start.10 = (bf16[19,32,256]{2,1,0:T(8,128)(2,1)}, bf16[19,32,256]{2,1,0:T(8,128)(2,1)S(1)}, u32[]{:S(2)}, u32[]{:S(2)}) collective-permute-start(bf16[19,32,256]{2,1,0:T(8,128)(2,1)} %get-tuple-element.135), channel_id=1, source_target_pairs={{0,8},{4,12},{8,0},{12,4},{1,9},{5,13},{9,1},{13,5},{2,10},{6,14},... | collective-permute-start | bytes 933896 | tf_op jit(solution)/shard_map/ppermute | solution.py:736
  115.4 11.4 %collective-permute-start.11 = (bf16[19,32,256]{2,1,0:T(8,128)(2,1)}, bf16[19,32,256]{2,1,0:T(8,128)(2,1)S(1)}, u32[]{:S(2)}, u32[]{:S(2)}) collective-permute-start(bf16[19,32,256]{2,1,0:T(8,128)(2,1)} %get-tuple-element.136), channel_id=1, source_target_pairs={{0,4},{4,0},{8,12},{12,8},{1,5},{5,1},{9,13},{13,9},{2,6},{6,2},{1... | collective-permute-start | bytes 933896 | tf_op jit(solution)/shard_map/ppermute | solution.py:736
  119.6 1.4 collective-permute-start.13
  127.2 9.5 %collective-permute-start.14 = (bf16[38,16,256]{2,1,0:T(8,128)(2,1)S(1)}, bf16[38,16,256]{2,1,0:T(8,128)(2,1)S(1)}, u32[]{:S(2)}, u32[]{:S(2)}) collective-permute-start(bf16[38,16,256]{2,1,0:T(8,128)(2,1)S(1)} %select_convert_fusion), channel_id=1, source_target_pairs={{0,1},{1,0},{2,3},{3,2},{4,5},{5,4},{6,7},{7,6},{8,9},{9,8},{10,11... | collective-permute-start | bytes 933896 | tf_op jit(solution)/shard_map/ppermute | solution.py:736
  127.9 8.8 %collective-permute-start.15 = (bf16[9,64,256]{2,1,0:T(8,128)(2,1)S(1)}, bf16[9,64,256]{2,1,0:T(8,128)(2,1)S(1)}, u32[]{:S(2)}, u32[]{:S(2)}) collective-permute-start(bf16[9,64,256]{2,1,0:T(8,128)(2,1)S(1)} %get-tuple-element.150), channel_id=1, source_target_pairs={{0,4},{4,0},{8,12},{12,8},{1,5},{5,1},{9,13},{13,9},{2,6},{6,2},{1... | collective-permute-start | bytes 884744 | tf_op jit(solution)/shard_map/ppermute | solution.py:736
  128.0 8.7 %collective-permute-start.16 = (bf16[9,64,256]{2,1,0:T(8,128)(2,1)S(1)}, bf16[9,64,256]{2,1,0:T(8,128)(2,1)S(1)}, u32[]{:S(2)}, u32[]{:S(2)}) collective-permute-start(bf16[9,64,256]{2,1,0:T(8,128)(2,1)S(1)} %get-tuple-element.151), channel_id=1, source_target_pairs={{0,8},{4,12},{8,0},{12,4},{1,9},{5,13},{9,1},{13,5},{2,10},{6,14},... | collective-permute-start | bytes 884744 | tf_op jit(solution)/shard_map/ppermute | solution.py:736
  136.8 5.2 %collective-permute-start.19 = (bf16[9,32,256]{2,1,0:T(8,128)(2,1)S(1)}, bf16[9,32,256]{2,1,0:T(8,128)(2,1)S(1)}, u32[]{:S(2)}, u32[]{:S(2)}) collective-permute-start(bf16[9,32,256]{2,1,0:T(8,128)(2,1)S(1)} %select_convert_fusion.3), channel_id=1, source_target_pairs={{0,4},{4,0},{8,12},{12,8},{1,5},{5,1},{9,13},{13,9},{2,6},{6,2},{1... | collective-permute-start | bytes 442376 | tf_op jit(solution)/shard_map/ppermute | solution.py:736
  138.8 8.6 %collective-permute-start.17 = (bf16[38,8,256]{2,1,0:T(8,128)(2,1)S(1)}, bf16[38,8,256]{2,1,0:T(8,128)(2,1)S(1)}, u32[]{:S(2)}, u32[]{:S(2)}) collective-permute-start(bf16[38,8,256]{2,1,0:T(8,128)(2,1)S(1)} %select_convert_fusion.1), channel_id=1, source_target_pairs={{0,2},{1,3},{2,0},{3,1},{4,6},{5,7},{6,4},{7,5},{8,10},{9,11},{10,... | collective-permute-start | bytes 466952 | tf_op jit(solution)/shard_map/ppermute | solution.py:736
  139.0 5.2 %collective-permute-start.18 = (bf16[9,32,256]{2,1,0:T(8,128)(2,1)S(1)}, bf16[9,32,256]{2,1,0:T(8,128)(2,1)S(1)}, u32[]{:S(2)}, u32[]{:S(2)}) collective-permute-start(bf16[9,32,256]{2,1,0:T(8,128)(2,1)S(1)} %select_convert_fusion.4), channel_id=1, source_target_pairs={{0,8},{4,12},{8,0},{12,4},{1,9},{5,13},{9,1},{13,5},{2,10},{6,14},... | collective-permute-start | bytes 442376 | tf_op jit(solution)/shard_map/ppermute | solution.py:736
  147.6 8.6 %collective-permute-start.20 = (bf16[38,8,256]{2,1,0:T(8,128)(2,1)S(1)}, bf16[38,8,256]{2,1,0:T(8,128)(2,1)S(1)}, u32[]{:S(2)}, u32[]{:S(2)}) collective-permute-start(bf16[38,8,256]{2,1,0:T(8,128)(2,1)S(1)} %add_convert_fusion), channel_id=1, source_target_pairs={{0,2},{1,3},{2,0},{3,1},{4,6},{5,7},{6,4},{7,5},{8,10},{9,11},{10,... | collective-permute-start | bytes 466952 | tf_op jit(solution)/shard_map/ppermute | solution.py:736
  147.8 8.4 %collective-permute-start.21 = (bf16[18,16,256]{2,1,0:T(8,128)(2,1)S(1)}, bf16[18,16,256]{2,1,0:T(8,128)(2,1)S(1)}, u32[]{:S(2)}, u32[]{:S(2)}) collective-permute-start(bf16[18,16,256]{2,1,0:T(8,128)(2,1)S(1)} %select_convert_fusion.2), channel_id=1, source_target_pairs={{0,1},{1,0},{2,3},{3,2},{4,5},{5,4},{6,7},{7,6},{8,9},{9,8},{10,11... | collective-permute-start | bytes 442376 | tf_op jit(solution)/shard_map/ppermute | solution.py:736
  156.3 10.2 %collective-permute-start.22 = (bf16[38,16,256]{2,1,0:T(8,128)(2,1)S(1)}, bf16[38,16,256]{2,1,0:T(8,128)(2,1)S(1)}, u32[]{:S(2)}, u32[]{:S(2)}) collective-permute-start(bf16[38,16,256]{2,1,0:T(8,128)(2,1)S(1)} %pad_maximum_fusion.6), channel_id=1, source_target_pairs={{0,1},{1,0},{2,3},{3,2},{4,5},{5,4},{6,7},{7,6},{8,9},{9,8},{10,11... | collective-permute-start | bytes 933896 | tf_op jit(solution)/shard_map/ppermute | solution.py:736
  156.5 7.8 %collective-permute-start.23 = (bf16[18,8,256]{2,1,0:T(8,128)(2,1)S(1)}, bf16[18,8,256]{2,1,0:T(8,128)(2,1)S(1)}, u32[]{:S(2)}, u32[]{:S(2)}) collective-permute-start(bf16[18,8,256]{2,1,0:T(8,128)(2,1)S(1)} %select_convert_fusion.5), channel_id=1, source_target_pairs={{0,2},{1,3},{2,0},{3,1},{4,6},{5,7},{6,4},{7,5},{8,10},{9,11},{10,... | collective-permute-start | bytes 221192 | tf_op jit(solution)/shard_map/ppermute | solution.py:736
  166.7 7.9 %collective-permute-start.24 = (bf16[19,32,256]{2,1,0:T(8,128)(2,1)S(1)}, bf16[19,32,256]{2,1,0:T(8,128)(2,1)S(1)}, u32[]{:S(2)}, u32[]{:S(2)}) collective-permute-start(bf16[19,32,256]{2,1,0:T(8,128)(2,1)S(1)} %get-tuple-element.196), channel_id=1, source_target_pairs={{0,8},{4,12},{8,0},{12,4},{1,9},{5,13},{9,1},{13,5},{2,10},{6,14},... | collective-permute-start | bytes 933896 | tf_op jit(solution)/shard_map/ppermute | solution.py:736
  168.2 7.9 %collective-permute-start.25 = (bf16[19,32,256]{2,1,0:T(8,128)(2,1)S(1)}, bf16[19,32,256]{2,1,0:T(8,128)(2,1)S(1)}, u32[]{:S(2)}, u32[]{:S(2)}) collective-permute-start(bf16[19,32,256]{2,1,0:T(8,128)(2,1)S(1)} %get-tuple-element.195), channel_id=1, source_target_pairs={{0,4},{4,0},{8,12},{12,8},{1,5},{5,1},{9,13},{13,9},{2,6},{6,2},{1... | collective-permute-start | bytes 933896 | tf_op jit(solution)/shard_map/ppermute | solution.py:736
  169.1 5.3 %collective-permute-start.26 = (bf16[18,8,256]{2,1,0:T(8,128)(2,1)S(1)}, bf16[18,8,256]{2,1,0:T(8,128)(2,1)S(1)}, u32[]{:S(2)}, u32[]{:S(2)}) collective-permute-start(bf16[18,8,256]{2,1,0:T(8,128)(2,1)S(1)} %add_convert_fusion.1), channel_id=1, source_target_pairs={{0,2},{1,3},{2,0},{3,1},{4,6},{5,7},{6,4},{7,5},{8,10},{9,11},{10,... | collective-permute-start | bytes 221192 | tf_op jit(solution)/shard_map/ppermute | solution.py:736
  176.2 19.0 %collective-permute-start.31 = (bf16[19,64,256]{2,1,0:T(8,128)(2,1)S(1)}, bf16[19,64,256]{2,1,0:T(8,128)(2,1)S(1)}, u32[]{:S(2)}, u32[]{:S(2)}) collective-permute-start(bf16[19,64,256]{2,1,0:T(8,128)(2,1)S(1)} %pad_maximum_fusion.4), channel_id=1, source_target_pairs={{0,8},{4,12},{8,0},{12,4},{1,9},{5,13},{9,1},{13,5},{2,10},{6,14},... | collective-permute-start | bytes 1867784 | tf_op jit(solution)/shard_map/ppermute | solution.py:736
  176.7 5.2 %collective-permute-start.27 = (bf16[18,16,256]{2,1,0:T(8,128)(2,1)S(1)}, bf16[18,16,256]{2,1,0:T(8,128)(2,1)S(1)}, u32[]{:S(2)}, u32[]{:S(2)}) collective-permute-start(bf16[18,16,256]{2,1,0:T(8,128)(2,1)S(1)} %pad_maximum_fusion.11), channel_id=1, source_target_pairs={{0,1},{1,0},{2,3},{3,2},{4,5},{5,4},{6,7},{7,6},{8,9},{9,8},{10,11... | collective-permute-start | bytes 442376 | tf_op jit(solution)/shard_map/ppermute | solution.py:736
  178.7 16.4 %collective-permute-start.30 = (bf16[19,64,256]{2,1,0:T(8,128)(2,1)S(1)}, bf16[19,64,256]{2,1,0:T(8,128)(2,1)S(1)}, u32[]{:S(2)}, u32[]{:S(2)}) collective-permute-start(bf16[19,64,256]{2,1,0:T(8,128)(2,1)S(1)} %pad_maximum_fusion.3), channel_id=1, source_target_pairs={{0,4},{4,0},{8,12},{12,8},{1,5},{5,1},{9,13},{13,9},{2,6},{6,2},{1... | collective-permute-start | bytes 1867784 | tf_op jit(solution)/shard_map/ppermute | solution.py:736
  182.0 11.0 %collective-permute-start.28 = (bf16[9,32,256]{2,1,0:T(8,128)(2,1)S(1)}, bf16[9,32,256]{2,1,0:T(8,128)(2,1)S(1)}, u32[]{:S(2)}, u32[]{:S(2)}) collective-permute-start(bf16[9,32,256]{2,1,0:T(8,128)(2,1)S(1)} %get-tuple-element.210), channel_id=1, source_target_pairs={{0,8},{4,12},{8,0},{12,4},{1,9},{5,13},{9,1},{13,5},{2,10},{6,14},... | collective-permute-start | bytes 442376 | tf_op jit(solution)/shard_map/ppermute | solution.py:736
  183.7 11.4 %collective-permute-start.29 = (bf16[9,32,256]{2,1,0:T(8,128)(2,1)S(1)}, bf16[9,32,256]{2,1,0:T(8,128)(2,1)S(1)}, u32[]{:S(2)}, u32[]{:S(2)}) collective-permute-start(bf16[9,32,256]{2,1,0:T(8,128)(2,1)S(1)} %get-tuple-element.209), channel_id=1, source_target_pairs={{0,4},{4,0},{8,12},{12,8},{1,5},{5,1},{9,13},{13,9},{2,6},{6,2},{1... | collective-permute-start | bytes 442376 | tf_op jit(solution)/shard_map/ppermute | solution.py:736
  196.2 5.7 %collective-permute-start.34 = (bf16[19,256,256]{2,1,0:T(8,128)(2,1)S(1)}, bf16[19,256,256]{2,1,0:T(8,128)(2,1)}, u32[]{:S(2)}, u32[]{:S(2)}) collective-permute-start(bf16[19,256,256]{2,1,0:T(8,128)(2,1)S(1)} %pad_maximum_fusion.half_ref), channel_id=1, source_target_pairs={{0,16},{16,0},{1,17},{17,1},{2,18},{18,2},{3,19},{19,3},{4,20},{20... | collective-permute-start | bytes 7471112 | tf_op jit(solution)/shard_map/ppermute | solution.py:736
  196.4 9.6 %collective-permute-start.33 = (bf16[9,64,256]{2,1,0:T(8,128)(2,1)S(1)}, bf16[9,64,256]{2,1,0:T(8,128)(2,1)}, u32[]{:S(2)}, u32[]{:S(2)}) collective-permute-start(bf16[9,64,256]{2,1,0:T(8,128)(2,1)S(1)} %pad_maximum_fusion.9), channel_id=1, source_target_pairs={{0,8},{4,12},{8,0},{12,4},{1,9},{5,13},{9,1},{13,5},{2,10},{6,14},... | collective-permute-start | bytes 884744 | tf_op jit(solution)/shard_map/ppermute | solution.py:736
  197.8 9.4 %collective-permute-start.32 = (bf16[9,64,256]{2,1,0:T(8,128)(2,1)}, bf16[9,64,256]{2,1,0:T(8,128)(2,1)}, u32[]{:S(2)}, u32[]{:S(2)}) collective-permute-start(bf16[9,64,256]{2,1,0:T(8,128)(2,1)} %pad_maximum_fusion.8), channel_id=1, source_target_pairs={{0,4},{4,0},{8,12},{12,8},{1,5},{5,1},{9,13},{13,9},{2,6},{6,2},{1... | collective-permute-start | bytes 884744 | tf_op jit(solution)/shard_map/ppermute | solution.py:736
  209.5 2.9 %collective-permute-start.35 = (bf16[9,256,256]{2,1,0:T(8,128)(2,1)S(1)}, bf16[9,256,256]{2,1,0:T(8,128)(2,1)S(1)}, u32[]{:S(2)}, u32[]{:S(2)}) collective-permute-start(bf16[9,256,256]{2,1,0:T(8,128)(2,1)S(1)} %pad_maximum_fusion.1.half_ref), channel_id=1, source_target_pairs={{0,16},{16,0},{1,17},{17,1},{2,18},{18,2},{3,19},{19,3},{4,20},{20... | collective-permute-start | bytes 3538952 | tf_op jit(solution)/shard_map/ppermute | solution.py:736
  (16 other events, 94.8 us)

commit v3 on v2

--- a/solution.py
+++ b/solution.py
@@ -507,40 +507,48 @@
     r.spread[...] = jnp.broadcast_to(row[None], r.spread.shape)
 
 
-def split_store(r, rows, unit, first):
+def split_store(r, rows, lanes, unit, first):
     quarter = unit // 4
     for k in range(rows // unit):
         for bit, base, sent, kept in ((1, 0, r.sent_a, r.kept_a), (2, 2 * quarter, r.sent_b, r.kept_b)):
             keep = pl.multiple_of(k * unit + base + r.bits[bit] * quarter, quarter)
             send = pl.multiple_of(k * unit + base + (1 - r.bits[bit]) * quarter, quarter)
-            sent[first + k] = r.acc[pl.ds(send, quarter), :].astype(bf16)
-            kept[first + k] = r.acc[pl.ds(keep, quarter), :]
+            sent[first + k] = r.acc[pl.ds(send, quarter), lanes].astype(bf16)
+            kept[first + k] = r.acc[pl.ds(keep, quarter), lanes]
+
+
+def beside(out, grad, offsets):
+    rows_w, half = grad.shape
+    out[...] = jnp.zeros(out.shape, bf16)
+    for k, at in enumerate(offsets):
+        out[at : at + rows_w, k * half : (k + 1) * half] = grad
 
 
 def weights_second_kernel(r, copies):
     width = r.h3.shape[1] // 3
+    half = r.near.shape[1]
     cin = r.xe.shape[1] // 3
     rows_w = r.near.shape[0] // 2
     L = (r.h3.shape[0] - rows_w) // 5
     per = width // cin
+    beside(r.g_near, r.near[:rows_w, :], (0, L, 2 * L))
+    beside(r.g_far, r.far[:rows_w, :], (0, L, 2 * L))
+    window = slice(L, L + rows_w + 2 * L)
     for b in range(3):
         lanes = slice(b * width, (b + 1) * width)
         copies.wait(("h3", b), ("h3_far", b))
+        r.acc[...] = matmul_tn(r.h3[window, lanes], r.g_near[...]) + matmul_tn(r.h3_far[window, lanes], r.g_far[...])
         for a in range(3):
-            at = L * a + L
-            r.acc[...] = matmul_tn(r.h3[at : at + rows_w, lanes], r.near[:rows_w, :]) + matmul_tn(
-                r.h3_far[at : at + rows_w, lanes], r.far[:rows_w, :]
-            )
-            split_store(r, width, cin, (3 * b + a) * per)
-        copies.start(("kept_a", b), ("kept_b", b))
+            split_store(r, width, slice(a * half, (a + 1) * half), cin, (3 * a + b) * per)
+            copies.start(("kept_a", 3 * a + b), ("kept_b", 3 * a + b))
     at = 2 * L
     copies.wait("xe", "xe_far")
     middle = slice(cin, 2 * cin)
-    r.acc[0:cin, :] = matmul_tn(r.xe[at : at + rows_w, middle], r.near[rows_w:, :]) + matmul_tn(
+    r.acc[0:cin, 0:half] = matmul_tn(r.xe[at : at + rows_w, middle], r.near[rows_w:, :]) + matmul_tn(
         r.xe_far[at : at + rows_w, middle], r.far[rows_w:, :]
     )
-    split_store(r, cin, cin, 9 * per)
-    copies.start(("kept_a", 3), ("kept_b", 3))
+    split_store(r, cin, slice(0, half), cin, 9 * per)
+    copies.start(("kept_a", 9), ("kept_b", 9))
     copies.wait("kept_a", "kept_b")
 
 
@@ -570,21 +578,21 @@
 
 
 def weights_first_kernel(r, copies):
-    rows_w = r.near.shape[0]
+    rows_w, half = r.near.shape
     cin = r.xe.shape[1] // 3
     L = (r.xe.shape[0] - rows_w) // 5
+    beside(r.g_near, r.near[...], (0, L))
+    beside(r.g_far, r.far[...], (0, L))
     copies.wait("xe", "xe_far")
-    for k, a in enumerate((1, 0, 2)):
-        if k == 1:
-            copies.wait("xo", "xo_far")
-        source, source_far = (r.xe, r.xe_far) if a == 1 else (r.xo, r.xo_far)
-        at = (3 if a == 2 else 2) * L
-        for b in range(3):
-            lanes = slice(b * cin, (b + 1) * cin)
-            r.acc[lanes, :] = matmul_tn(source[at : at + rows_w, lanes], r.near[...]) + matmul_tn(
-                source_far[at : at + rows_w, lanes], r.far[...]
-            )
-        split_store(r, 3 * cin, cin, a * 3)
+    window = slice(2 * L, 2 * L + rows_w)
+    r.acc[:, :half] = matmul_tn(r.xe[window, :], r.near[...]) + matmul_tn(r.xe_far[window, :], r.far[...])
+    split_store(r, 3 * cin, slice(0, half), cin, 3)
+    copies.start(("kept_a", 1), ("kept_b", 1))
+    copies.wait("xo", "xo_far")
+    window = slice(2 * L, 3 * L + rows_w)
+    r.acc[...] = matmul_tn(r.xo[window, :], r.g_near[...]) + matmul_tn(r.xo_far[window, :], r.g_far[...])
+    for k, a in enumerate((0, 2)):
+        split_store(r, 3 * cin, slice(k * half, (k + 1) * half), cin, 3 * a)
         copies.start(("kept_a", a), ("kept_b", a))
     copies.wait("kept_a", "kept_b")
 
@@ -636,49 +644,51 @@
     copies.wait("out")
 
 
-def widen(half, side, taps, per, swapped, into=None):
-    total, n, m = half.shape
-    extra = total - taps * per
-    order = [(t % 3 * 3 + t // 3) if swapped else t for t in range(taps)]
-    jobs = [(t * per, per, 0, order[t] * per) for t in range(taps)] + [(taps * per, 1, 1, 0)] * extra
+def place(pieces, spots, groups, like, into=None):
+    total, h, m = pieces[0].shape
+    extra = len(like) - 1
+    size = like[0][0] // groups
+    jobs = [(t * size, size, 0, t * size) for t in range(groups)] + [(groups * size, 1, 1, 0)] * extra
     more = list(into or [])
-
-    def body(side_ref, half_ref, *refs):
-        outs = refs[len(more) : len(more) + 1 + extra]
-        narrow, full, sems = refs[len(more) + 1 + extra :]
-        lanes = pl.ds(pl.multiple_of(side_ref[0] * m, m), m)
-        reads = [
-            pltpu.make_async_copy(half_ref.at[pl.ds(at, size)], narrow.at[pl.ds(at, size)], sems.at[0, k])
-            for k, (at, size, _, _) in enumerate(jobs)
-        ]
-        writes = [
-            pltpu.make_async_copy(full.at[pl.ds(at, size)], outs[which].at[pl.ds(to, size), :, lanes], sems.at[1, k])
-            for k, (at, size, which, to) in enumerate(jobs)
-        ]
+    n = len(pieces)
+
+    def body(spots_ref, *refs):
+        sources, outs = refs[:n], refs[n + len(more) : n + len(more) + 1 + extra]
+        narrow, full, sems = refs[n + len(more) + 1 + extra :]
+        reads, writes = [], []
+        for p in range(n):
+            rows = pl.ds(pl.multiple_of(spots_ref[2 * p] * h, h), h)
+            lanes = pl.ds(pl.multiple_of(spots_ref[2 * p + 1] * m, m), m)
+            for k, (at, size, which, to) in enumerate(jobs):
+                units = pl.ds(at, size)
+                reads.append(pltpu.make_async_copy(sources[p].at[units], narrow.at[p, units], sems.at[0, p, k]))
+                target = outs[which].at[pl.ds(to, size), rows, lanes]
+                writes.append(pltpu.make_async_copy(full.at[p, units], target, sems.at[1, p, k]))
         for read in reads:
             read.start()
-        for k, (at, size, _, _) in enumerate(jobs):
-            reads[k].wait()
-            full[at : at + size] = narrow[at : at + size].astype(f32)
-            writes[k].start()
+        for p in range(n):
+            for k, (at, size, _, _) in enumerate(jobs):
+                reads[p * len(jobs) + k].wait()
+                full[p, at : at + size] = narrow[p, at : at + size].astype(f32)
+                writes[p * len(jobs) + k].start()
         for write in writes:
             write.wait()
 
     hbm = pl.BlockSpec(memory_space=pltpu.HBM)
     return pl.pallas_call(
         body,
-        out_shape=[shape((taps * per, n, 2 * m))] + [shape((1, n, 2 * m))] * extra,
-        in_specs=[pl.BlockSpec(memory_space=pltpu.SMEM)] + [hbm] * (1 + len(more)),
+        out_shape=[shape(dims) for dims in like],
+        in_specs=[pl.BlockSpec(memory_space=pltpu.SMEM)] + [hbm] * (n + len(more)),
         out_specs=[hbm] * (1 + extra),
         scratch_shapes=[
-            pltpu.VMEM((total, n, m), bf16),
-            pltpu.VMEM((total, n, m), f32),
-            pltpu.SemaphoreType.DMA((2, len(jobs))),
+            pltpu.VMEM((n, total, h, m), bf16),
+            pltpu.VMEM((n, total, h, m), f32),
+            pltpu.SemaphoreType.DMA((2, n, len(jobs))),
         ],
-        input_output_aliases={2 + k: k for k in range(len(more))},
-        compiler_params=pltpu.CompilerParams(vmem_limit_bytes=20 * 1024 * 1024),
-        cost_estimate=pl.CostEstimate(flops=0, bytes_accessed=0, transcendentals=0),
-    )(side.reshape(1), half, *more)
+        input_output_aliases={1 + n + k: k for k in range(len(more))},
+        compiler_params=pltpu.CompilerParams(vmem_limit_bytes=60 * 1024 * 1024),
+        cost_estimate=pl.CostEstimate(flops=20000000000, bytes_accessed=0, transcendentals=0),
+    )(spots, *pieces, *more)
 
 
 def halve_kernel(r, copies):
@@ -764,7 +774,6 @@
         p, n = len(plane), len(rest)
         self.stages = [("plane", k) for k in range(p)] + [("rest", k) for k in range(n)]
         self.stages += [("rest_join", k) for k in reversed(range(n))] + [("plane_join", k) for k in reversed(range(p))]
-        self.stages += [("core", 0)]
 
     def next(self):
         return self.stages[0] if self.stages else None
@@ -779,8 +788,6 @@
             self.got = (partner(self.value, *self.rest[k]),)
         elif kind == "plane_join":
             self.got = partner(self.value_a, *self.a[k]), partner(self.value_b, *self.b[k])
-        else:
-            self.got = (partner(self.value, *self.core),)
 
     def finish(self, cost=0):
         kind, k = self.stages.pop(0)
@@ -806,7 +813,6 @@
         elif kind == "plane_join":
             self.value_a = joined(self.value_a, self.got[0], *self.a[k])
             self.value_b = joined(self.value_b, self.got[1], *self.b[k])
-            self.value = jnp.concatenate([self.value_a, self.value_b], axis=1)
 
     def split_rest(self, total, k):
         if k < len(self.rest):
@@ -990,15 +996,19 @@
         weights_second_kernel,
         dict(bits=bits, h3=h3, h3_far=far_h3, xe=xe, xe_far=far_xe, near=fourth["mine"], far=far2),
         chunk_shapes(taps2),
-        dict(acc=pltpu.VMEM((width, half), f32)),
+        dict(
+            acc=pltpu.VMEM((width, 3 * half), f32),
+            g_near=pltpu.VMEM((MW + 2 * L, 3 * half), bf16),
+            g_far=pltpu.VMEM((MW + 2 * L, 3 * half), bf16),
+        ),
         far_in=("h3", "h3_far", "xe", "xe_far"),
         far_out=("kept_a", "kept_b"),
         smem=("bits",),
         parts=dict(
             h3=lane_parts(3 * width, 3),
             h3_far=lane_parts(3 * width, 3),
-            kept_a=row_parts(taps2 - 1, 3) + [(3, (pl.ds(taps2 - 1, 1),))],
-            kept_b=row_parts(taps2 - 1, 3) + [(3, (pl.ds(taps2 - 1, 1),))],
+            kept_a=row_parts(taps2 - 1, 9) + [(9, (pl.ds(taps2 - 1, 1),))],
+            kept_b=row_parts(taps2 - 1, 9) + [(9, (pl.ds(taps2 - 1, 1),))],
         ),
     ).values()
     gq, *second_parts = lax.optimization_barrier((fourth["gq"], *second_parts))
@@ -1014,22 +1024,27 @@
         parts=dict(w2=[(k, (pl.ds(2 - k, 1),)) for k in range(3)]),
     )
     tot4 = gather_sum(hidden["spread"])
-    tree2.finish(20000000000)
-    act, tree2.sent_a, tree2.sent_b = lax.optimization_barrier((hidden["act"], tree2.sent_a, tree2.sent_b))
-    tree2.start()
     fifth = call(
         fifth_kernel,
-        dict(bits=bits, act=act, normed=hidden["normed"], mom1=mom1, tot4=tot4, gain=g1, maskp=maskp, ownp=ownp),
+        dict(bits=bits, act=hidden["act"], normed=hidden["normed"], mom1=mom1, tot4=tot4, gain=g1, maskp=maskp, ownp=ownp),
         dict(mine=shape((MW, half), bf16), theirs=shape((MW, half), bf16), gain_first=vec(1), shift_first=vec(1)),
         dict(gf=pltpu.VMEM((MU + 16, width), f32)),
         smem=("bits",),
     )
-    far1 = partner(fifth["theirs"], *core)
+    tree2.got, theirs = lax.optimization_barrier((tree2.got, fifth["theirs"]))
+    far1 = partner(theirs, *core)
+    tree2.finish(20000000000)
+    near1, tree2.sent_a, tree2.sent_b = lax.optimization_barrier((fifth["mine"], tree2.sent_a, tree2.sent_b))
+    tree2.start()
     first_parts = call(
         weights_first_kernel,
-        dict(bits=bits, xe=xe, xo=xo, xe_far=far_xe, xo_far=far_xo, near=fifth["mine"], far=far1),
+        dict(bits=bits, xe=xe, xo=xo, xe_far=far_xe, xo_far=far_xo, near=near1, far=far1),
         chunk_shapes(9),
-        dict(acc=pltpu.VMEM((3 * cin, half), f32)),
+        dict(
+            acc=pltpu.VMEM((3 * cin, 2 * half), f32),
+            g_near=pltpu.VMEM((MW + L, 2 * half), bf16),
+            g_far=pltpu.VMEM((MW + L, 2 * half), bf16),
+        ),
         far_in=("xe", "xe_far", "xo", "xo_far"),
         far_out=("kept_a", "kept_b"),
         smem=("bits",),
@@ -1042,7 +1057,7 @@
     grad_inputs = call(
         inputs_kernel,
         dict(
-            act=act, normed=hidden["normed"], gpu=fourth["gpu"], w1=w1, wp=w_proj, mom1=mom1, gain=g1, maskp=maskp,
+            act=hidden["act"], normed=hidden["normed"], gpu=fourth["gpu"], w1=w1, wp=w_proj, mom1=mom1, gain=g1, maskp=maskp,
             gg=fifth["gain_first"], gs=fifth["shift_first"],
         ),
         dict(out=shape((groups, rows_in, cols_in, cin), bf16)),
@@ -1055,27 +1070,36 @@
         far_out=("out",),
         cost=10000000000,
     )["out"]
-    side = bit_of(*core).astype(jnp.int32)
     grad_inputs = lockstep(tree2, tree1, beside=grad_inputs)
     while tree2.next() != ("plane_join", 0):
         lockstep(tree2, tree1)
+
+    side, low, high = (bits[tree2.place[step]] for step in (core, plane[0], plane[-1]))
+    own_spots = jnp.stack([low, side, 2 + high, side, low, 1 - side, 2 + high, 1 - side])
+    far_spots = jnp.stack([1 - low, side, 3 - high, side, 1 - low, 1 - side, 3 - high, 1 - side])
+    swap = lambda values: [partner(v, *core) for v in values]
+    first_dims = [(9, cin, width)]
+    second_dims = [(9 * per, cin, width), (1, cin, width)]
+
     tree2.start()
+    own2 = [tree2.value_a, tree2.value_b]
+    own2 += swap(own2)
     while tree1.next() != ("plane_join", 0):
         tree1.start()
         if tree1.next() != ("plane_join", 1):
             tree1.finish()
         else:
-            tree1.got, tree2.got = lax.optimization_barrier((tree1.got, tree2.got))
+            placed2 = place(own2, own_spots, 3, second_dims)
+            tree1.got, tree2.got, placed2 = lax.optimization_barrier((tree1.got, tree2.got, placed2))
             tree1.finish()
-    tree2.finish()
-    tree2.start()
     tree1.start()
-    grad_second = widen(tree2.got[0], 1 - side, 9, per, True, widen(tree2.value, side, 9, per, True))
-    tree1.got, grad_second = lax.optimization_barrier((tree1.got, grad_second))
-    grad_w2, grad_wp = grad_second
-    tree1.finish()
-    tree1.start()
-    (grad_w1,) = widen(tree1.got[0], 1 - side, 3, 3, False, widen(tree1.value, side, 3, 3, False))
+    own1 = [tree1.value_a, tree1.value_b]
+    own1 += swap(own1)
+    far2 = [*tree2.got, *swap(tree2.got)]
+    placed1 = place(own1, own_spots, 3, first_dims)
+    grad_w2, grad_wp = place(far2, far_spots, 3, second_dims, placed2)
+    tree1.got, grad_w2, grad_wp, placed1 = lax.optimization_barrier((tree1.got, grad_w2, grad_wp, placed1))
+    (grad_w1,) = place([*tree1.got, *swap(tree1.got)], far_spots, 3, first_dims, placed1)
 
     return (
         third["out"],

time: 215 us -> 221 us (1.028)
  Pallas kernels: 71.5 us -> 76.7 us
  local copies, waits for them, and re-layouts: 3.23 us -> 6.49 us
  other arithmetic: 6.58 us -> 3.54 us
  waiting for transfers between devices: 77.1 us -> 74.8 us
    ppermute x31 -> x37, waiting for transfers between devices: 52.5 us -> 42.7 us  [partner(): return lax.ppermute(value, axis, [(i, i ^ step) for i in range(count)])]
    all_to_all x4, waiting for transfers between devices: 22.1 us -> 29.6 us  [gather_sum(): return lax.all_to_all(spread, axes, 0, 0)]
    pallas_call x4, Pallas kernels: 10.3 us -> 14.6 us  [place(): pl.pallas_call(body, out_shape=[shape(dims) for dims in like], in_specs=[...]
    select_n x10 -> x6, other arithmetic: 2.91 us -> 0.19 us  [joined(): jnp.where(bit, other, value)]
    unnamed x48 -> x72, local copies, waits for them, and re-layouts: 3 us -> 5.05 us
    ppermute x31 -> x37, starting transfers between devices: 24.9 us -> 26.8 us  [partner(): return lax.ppermute(value, axis, [(i, i ^ step) for i in range(count)])]
  transfers between devices with their start and end apart: 40 -> 46, of which waited for: 26 -> 24; matrix products, arithmetic and copies ran while one was open for 1% -> 1% of each run, Pallas kernels for 24% -> 25%
where the time goes in v3:
time: 221 us; the launch traced here: 220 us
  Pallas kernels  76.7 us (35%)
  waiting for transfers between devices  74.8 us (34%)
  starting transfers between devices  56.3 us (25%)
  local copies, waits for them, and re-layouts  6.49 us (3%)
  other arithmetic  3.54 us (2%)
    pallas_call x13, Pallas kernels, call(): pl.pallas_call(run, out_shape=list(outs.values()), in_specs=[spec(n) for...  62.1 us
    ppermute x37, waiting for transfers between devices, partner(): return lax.ppermute(value, axis, [(i, i ^ step) for i in range(count)])  42.7 us
    all_to_all x4, waiting for transfers between devices, gather_sum(): return lax.all_to_all(spread, axes, 0, 0)  29.6 us
    ppermute x37, starting transfers between devices, partner(): return lax.ppermute(value, axis, [(i, i ^ step) for i in range(count)])  26.8 us
    all_to_all x4, starting transfers between devices, gather_sum(): return lax.all_to_all(spread, axes, 0, 0)  16.7 us
    pallas_call x4, Pallas kernels, place(): pl.pallas_call(body, out_shape=[shape(dims) for dims in like], in_specs=[...  14.6 us
    ppermute x4, starting transfers between devices, shifted(): lax.ppermute(value, axis, [(source, source + steps) for source in range(f...  12.3 us
    unnamed x72, local copies, waits for them, and re-layouts  5.05 us
  transfers between devices with their start and end apart: 46, of which 24 were waited for; matrix products, arithmetic and copies ran while one was open for 1% of the time, Pallas kernels for 25%

profile of v3, /device:TPU:0, one launch (start us, length us, event | category | flops | bytes accessed | tf_op | source)
XLA Modules:
  0.0 219.6 jit_solution(15956349303106051809)
XLA Ops:
  5.1 2.0 collective-permute-start.1
  7.9 4.8 %collective-permute-start.2 = (bf16[2,17,1,256]{3,2,1,0:T(2,128)(2,1)S(1)}, bf16[2,17,1,256]{3,2,1,0:T(2,128)(2,1)S(1)}, u32[]{:S(2)}, u32[]{:S(2)}) collective-permute-start(bf16[2,17,1,256]{3,2,1,0:T(2,128)(2,1)S(1)} %pad_maximum_fusion.10), channel_id=1, source_target_pairs={{0,4},{4,8},{8,12},{1,5},{5,9},{9,13},{2,6},{6,10},{10,14},{3,7},{... | collective-permute-start | bytes 52232 | tf_op jit(solution)/shard_map/ppermute | solution.py:733
  12.8 1.6 collective-permute-done.2.refs_2_
  14.4 1.3 shard_map.204
  15.7 4.2 %collective-permute-start.3 = (bf16[480,256]{1,0:T(8,128)(2,1)S(1)}, bf16[480,256]{1,0:T(8,128)(2,1)S(1)}, u32[]{:S(2)}, u32[]{:S(2)}) collective-permute-start(bf16[480,256]{1,0:T(8,128)(2,1)S(1)} %get-tuple-element.107), channel_id=1, source_target_pairs={{0,4},{4,8},{8,12},{1,5},{5,9},{9,13},{2,6},{6,10},{10,14},{3,7},{... | collective-permute-start | bytes 737288 | tf_op jit(solution)/shard_map/ppermute | solution.py:733
  19.9 1.3 collective-permute-start.4
  21.2 3.4 %shard_map.206 = f32[32,1,2176]{2,1,0:T(1,128)} custom-call(bf16[2,16,32,256]{3,2,1,0:T(8,128)(2,1)S(1)} %copy-done.1, bf16[2,1,32,256]{3,2,1,0:T(8,128)(2,1)S(1)} %collective-permute-done.1.refs_1_, bf16[2,17,1,256]{3,2,1,0:T(2,128)(2,1)S(1)} %collective-permute-done.2.refs_2_, bf16[2,8,16,128]{3,2,1,0:T(8,128)(2,1)S(1)} %broadcast_in_dim.2.refs_3_, ...), custom_call_target="tpu_custom_call" | custom-call | tf_op jit(solution)/shard_map/pallas_call | solution.py:89
  24.6 7.9 %all-to-all-start = ((f32[32,1,2176]{2,1,0:T(1,128)}), f32[32,1,2176]{2,1,0:T(1,128)S(1)}, u32[]{:S(2)}, u32[]{:S(2)}) async-start(f32[32,1,2176]{2,1,0:T(1,128)} %shard_map.206), calls=%async_computation | async-start | bytes 557056 | tf_op jit(solution)/shard_map/all_to_all | solution.py:737
  32.6 5.8 %shard_map.205 = (f32[624,512]{1,0:T(8,128)}, f32[624,512]{1,0:T(8,128)}, bf16[624,768]{1,0:T(8,128)(2,1)}, bf16[672,768]{1,0:T(8,128)(2,1)}, f32[624,128]{1,0:T...) custom-call(s32[2]{0:T(128)S(1)} %add_convert_fusion.2.refs_0_, bf16[2,16,32,256]{3,2,1,0:T(8,128)(2,1)} %refs_0_.1, ...), custom_call_target="tpu_custom_call" | custom-call | flops 20000000000 | tf_op jit(solution)/shard_map/pallas_call | solution.py:89
  38.4 5.4 %all-to-all-done.refs_1_ = f32[32,1,2176]{2,1,0:T(1,128)S(1)} async-done(((f32[32,1,2176]{2,1,0:T(1,128)}), f32[32,1,2176]{2,1,0:T(1,128)S(1)}, u32[]{:S(2)}, u32[]{:S(2)}) %all-to-all-start) | async-done | bytes 278560 | tf_op jit(solution)/shard_map/all_to_all | solution.py:737
  43.8 7.0 %shard_map.207 = (bf16[624,1536]{1,0:T(8,128)(2,1)}, f32[528,512]{1,0:T(8,128)}, f32[32,1,1024]{2,1,0:T(1,128)}, f32[8,512]{1,0:T(8,128)S(1)}) custom-call(f32[624,512]{1,0:T(8,128)} %get-tuple-element.109.refs_0_.refs_2_, f32[32,1,2176]{2,1,0:T(1,128)S(1)} %all-to-all-done.refs_1_, f32[1,512]{1,0:T(1,128)S(1)} %bitcast.28, f32[1,512]{1,0:T(1,128)S(1)} %bitcast.36, ...), custom_call_target="tpu_custom_call" | custom-call | tf_op jit(solution)/shard_map/pallas_call | solution.py:89
  50.9 2.6 %all-to-all-start.1 = ((f32[32,1,1024]{2,1,0:T(1,128)}), f32[32,1,1024]{2,1,0:T(1,128)S(1)}, u32[]{:S(2)}, u32[]{:S(2)}) async-start(f32[32,1,1024]{2,1,0:T(1,128)} %get-tuple-element.117), calls=%async_computation.1 | async-start | bytes 262144 | tf_op jit(solution)/shard_map/all_to_all | solution.py:737
  53.8 7.6 %all-to-all-done.1.refs_3_ = f32[32,1,1024]{2,1,0:T(1,128)S(1)} async-done(((f32[32,1,1024]{2,1,0:T(1,128)}), f32[32,1,1024]{2,1,0:T(1,128)S(1)}, u32[]{:S(2)}, u32[]{:S(2)}) %all-to-all-start.1) | async-done | bytes 131104 | tf_op jit(solution)/shard_map/all_to_all | solution.py:737
  61.4 5.3 %shard_map.208 = (bf16[2,8,16,512]{3,2,1,0:T(8,128)(2,1)}, f32[528,512]{1,0:T(8,128)}, f32[32,1,1536]{2,1,0:T(1,128)}, f32[8,512]{1,0:T(8,128)S(1)}) custom-call(f32[528,512]{1,0:T(8,128)} %get-tuple-element.114.refs_0_.refs_1_, f32[624,512]{1,0:T(8,128)} %get-tuple-element.115.refs_1_.refs_2_, f32[8,512]{1,0:T(8,128)S(1)} %get-tuple-element.116.refs_2_.refs_3_.refs_5_, ...), custom_call_target="tpu_custom_call" | custom-call | tf_op jit(solution)/shard_map/pallas_call | solution.py:89
  66.7 2.8 %all-to-all-start.2 = ((f32[32,1,1536]{2,1,0:T(1,128)}), f32[32,1,1536]{2,1,0:T(1,128)S(1)}, u32[]{:S(2)}, u32[]{:S(2)}) async-start(f32[32,1,1536]{2,1,0:T(1,128)} %get-tuple-element.121), calls=%async_computation.2 | async-start | bytes 393216 | tf_op jit(solution)/shard_map/all_to_all | solution.py:737
  69.7 9.1 %all-to-all-done.2.refs_5_ = f32[32,1,1536]{2,1,0:T(1,128)S(1)} async-done(((f32[32,1,1536]{2,1,0:T(1,128)}), f32[32,1,1536]{2,1,0:T(1,128)S(1)}, u32[]{:S(2)}, u32[]{:S(2)}) %all-to-all-start.2) | async-done | bytes 196640 | tf_op jit(solution)/shard_map/all_to_all | solution.py:737
  78.7 4.9 %shard_map.209 = (bf16[768,256]{1,0:T(8,128)(2,1)S(1)}, bf16[768,256]{1,0:T(8,128)(2,1)S(1)}, f32[536,512]{1,0:T(8,128)}, bf16[384,512]{1,0:T(8,128)(2,1)}, f32[...) custom-call(s32[5]{0:T(128)S(1)} %stack.59.refs_0_, ...), custom_call_target="tpu_custom_call" | custom-call | tf_op jit(solution)/shard_map/pallas_call | solution.py:89
  83.7 1.7 collective-permute-done.7.refs_6_
  85.4 8.4 %shard_map.210 = (bf16[19,64,256]{2,1,0:T(8,128)(2,1)S(1)}, f32[19,64,256]{2,1,0:T(8,128)}, bf16[19,64,256]{2,1,0:T(8,128)(2,1)}, f32[19,64,256]{2,1,0:T(8,128)}) custom-call(s32[5]{0:T(128)S(1)} %stack.59.refs_0_, bf16[624,1536]{1,0:T(8,128)(2,1)} %get-tuple-element.124.refs_1_, bf16[624,1536]{1,0:T(8,128)(2,1)} %collective-permute-done.5.refs_2_, ...), custom_call_target="tpu_custom_call" | custom-call | tf_op jit(solution)/shard_map/pallas_call | solution.py:89
  94.9 6.6 %shard_map.211 = (f32[432,512]{1,0:T(8,128)S(1)}, f32[432,512]{1,0:T(8,128)}, f32[32,1,1024]{2,1,0:T(1,128)}) custom-call(f32[536,512]{1,0:T(8,128)} %get-tuple-element.135.refs_0_, bf16[3,1536,512]{2,1,0:T(8,128)(2,1)} %bitcast.43, f32[624,512]{1,0:T(8,128)} %get-tuple-element.109.refs_0_.refs_2_, f32[8,512]{1,0:T(8,128)S(1)} %get-tuple-element.116.refs_2_.refs_3_.refs_5_, ...), custom_call_target="tpu_custom_call" | custom-call | tf_op jit(solution)/shard_map/pallas_call | solution.py:89
  102.4 3.4 %all-to-all-start.3 = ((f32[32,1,1024]{2,1,0:T(1,128)}), f32[32,1,1024]{2,1,0:T(1,128)S(1)}, u32[]{:S(2)}, u32[]{:S(2)}) async-start(f32[32,1,1024]{2,1,0:T(1,128)} %get-tuple-element.138), calls=%async_computation.3 | async-start | bytes 262144 | tf_op jit(solution)/shard_map/all_to_all | solution.py:737
  105.9 7.6 %all-to-all-done.3.refs_4_ = f32[32,1,1024]{2,1,0:T(1,128)S(1)} async-done(((f32[32,1,1024]{2,1,0:T(1,128)}), f32[32,1,1024]{2,1,0:T(1,128)S(1)}, u32[]{:S(2)}, u32[]{:S(2)}) %all-to-all-start.3) | async-done | bytes 131104 | tf_op jit(solution)/shard_map/all_to_all | solution.py:737
  113.5 2.2 %shard_map.212 = (bf16[384,256]{1,0:T(8,128)(2,1)S(1)}, bf16[384,256]{1,0:T(8,128)(2,1)S(1)}, f32[1,512]{1,0:T(1,128)}, f32[1,512]{1,0:T(1,128)}) custom-call(s32[5]{0:T(128)S(1)} %stack.59.refs_0_, f32[432,512]{1,0:T(8,128)} %copy-done.5, f32[432,512]{1,0:T(8,128)} %get-tuple-element.137.refs_2_.refs_1_, ...), custom_call_target="tpu_custom_call" | custom-call | tf_op jit(solution)/shard_map/pallas_call | solution.py:89
  115.8 3.9 %shard_map.213 = (bf16[19,32,256]{2,1,0:T(8,128)(2,1)}, f32[19,32,256]{2,1,0:T(8,128)}, bf16[19,32,256]{2,1,0:T(8,128)(2,1)}, f32[19,32,256]{2,1,0:T(8,128)}) custom-call(s32[5]{0:T(128)} %copy-done.9, f32[19,64,256]{2,1,0:T(8,128)} %get-tuple-element.132.refs_1_, bf16[19,64,256]{2,1,0:T(8,128)(2,1)} %collective-permute-done.8.refs_2_, ...), custom_call_target="tpu_custom_call" | custom-call | flops 20000000000 | tf_op jit(solution)/shard_map/pallas_call | solution.py:89
  121.3 1.4 collective-permute-done.13.refs_6_
  122.7 6.1 %shard_map.214 = (bf16[9,64,256]{2,1,0:T(8,128)(2,1)S(1)}, f32[9,64,256]{2,1,0:T(8,128)S(1)}, bf16[9,64,256]{2,1,0:T(8,128)(2,1)S(1)}, f32[9,64,256]{2,1,0:T(8,128)}) custom-call(s32[5]{0:T(128)S(1)} %copy-done.10, bf16[624,768]{1,0:T(8,128)(2,1)} %get-tuple-element.125.refs_3_.refs_1_, bf16[672,768]{1,0:T(8,128)(2,1)} %get-tuple-element.149.refs_2_, ...), custom_call_target="tpu_custom_call" | custom-call | tf_op jit(solution)/shard_map/pallas_call | solution.py:89
  132.6 1.3 collective-permute-start.16
  133.9 6.4 %shard_map.215 = bf16[2,16,32,256]{3,2,1,0:T(8,128)(2,1)} custom-call(f32[432,512]{1,0:T(8,128)S(1)} %copy-done.6, f32[432,512]{1,0:T(8,128)} %get-tuple-element.137.refs_2_.refs_1_, bf16[384,512]{1,0:T(8,128)(2,1)S(1)} %copy-done.16, bf16[3,768,512]{2,1,0:T(8,128)(2,1)} %bitcast.46, bf16[256,512]{1,0:T(8,128)(2,1)S(1)} %copy-done.7, ...), custom_call_target="tpu_custom_call" | custom-call | flops 10000000000 | tf_op jit(solution)/shard_map/pallas_call | solution.py:89
  142.2 1.4 collective-permute-start.18
  143.7 1.2 collective-permute-start.19
  144.9 2.5 %collective-permute-done.18 = bf16[9,32,256]{2,1,0:T(8,128)(2,1)S(1)} collective-permute-done((bf16[9,32,256]{2,1,0:T(8,128)(2,1)S(1)}, bf16[9,32,256]{2,1,0:T(8,128)(2,1)S(1)}, u32[]{:S(2)}, u32[]{:S(2)}) %collective-permute-start.18) | collective-permute-done | bytes 147488 | tf_op jit(solution)/shard_map/ppermute | solution.py:746
  147.4 1.5 collective-permute-done.19
  148.9 1.2 collective-permute-done.17
  152.6 6.6 %collective-permute-done.21 = bf16[18,16,256]{2,1,0:T(8,128)(2,1)S(1)} collective-permute-done((bf16[18,16,256]{2,1,0:T(8,128)(2,1)S(1)}, bf16[18,16,256]{2,1,0:T(8,128)(2,1)S(1)}, u32[]{:S(2)}, u32[]{:S(2)}) %collective-permute-start.21) | collective-permute-done | bytes 147488 | tf_op jit(solution)/shard_map/ppermute | solution.py:746
  159.4 2.7 %collective-permute-start.23 = (bf16[18,8,256]{2,1,0:T(8,128)(2,1)S(1)}, bf16[18,8,256]{2,1,0:T(8,128)(2,1)S(1)}, u32[]{:S(2)}, u32[]{:S(2)}) collective-permute-start(bf16[18,8,256]{2,1,0:T(8,128)(2,1)S(1)} %select_convert_fusion.5), channel_id=1, source_target_pairs={{0,2},{1,3},{2,0},{3,1},{4,6},{5,7},{6,4},{7,5},{8,10},{9,11},{10,... | collective-permute-start | bytes 221192 | tf_op jit(solution)/shard_map/ppermute | solution.py:746
  162.1 4.8 %collective-permute-done.23 = bf16[18,8,256]{2,1,0:T(8,128)(2,1)S(1)} collective-permute-done((bf16[18,8,256]{2,1,0:T(8,128)(2,1)S(1)}, bf16[18,8,256]{2,1,0:T(8,128)(2,1)S(1)}, u32[]{:S(2)}, u32[]{:S(2)}) %collective-permute-start.23) | collective-permute-done | bytes 73760 | tf_op jit(solution)/shard_map/ppermute | solution.py:746
  167.0 2.2 collective-permute-done.22
  170.7 1.3 collective-permute-start.26
  172.0 4.1 %collective-permute-done.26 = bf16[18,8,256]{2,1,0:T(8,128)(2,1)S(1)} collective-permute-done((bf16[18,8,256]{2,1,0:T(8,128)(2,1)S(1)}, bf16[18,8,256]{2,1,0:T(8,128)(2,1)S(1)}, u32[]{:S(2)}, u32[]{:S(2)}) %collective-permute-start.26) | collective-permute-done | bytes 73760 | tf_op jit(solution)/shard_map/ppermute | solution.py:746
  176.1 1.3 collective-permute-done.24
  178.6 2.3 %collective-permute-start.27 = (bf16[18,16,256]{2,1,0:T(8,128)(2,1)S(1)}, bf16[18,16,256]{2,1,0:T(8,128)(2,1)S(1)}, u32[]{:S(2)}, u32[]{:S(2)}) collective-permute-start(bf16[18,16,256]{2,1,0:T(8,128)(2,1)S(1)} %pad_maximum_fusion.9), channel_id=1, source_target_pairs={{0,1},{1,0},{2,3},{3,2},{4,5},{5,4},{6,7},{7,6},{8,9},{9,8},{10,11... | collective-permute-start | bytes 442376 | tf_op jit(solution)/shard_map/ppermute | solution.py:746
  182.4 2.5 %collective-permute-done.27 = bf16[18,16,256]{2,1,0:T(8,128)(2,1)S(1)} collective-permute-done((bf16[18,16,256]{2,1,0:T(8,128)(2,1)S(1)}, bf16[18,16,256]{2,1,0:T(8,128)(2,1)S(1)}, u32[]{:S(2)}, u32[]{:S(2)}) %collective-permute-start.27) | collective-permute-done | bytes 147488 | tf_op jit(solution)/shard_map/ppermute | solution.py:746
  186.3 4.1 %shard_map.216 = (f32[18,256,512]{2,1,0:T(8,128)}, f32[1,256,512]{2,1,0:T(8,128)}) custom-call(s32[8]{0:T(128)} %stack.65.spots_ref, bf16[19,64,256]{2,1,0:T(8,128)(2,1)} %copy-done.21, bf16[19,64,256]{2,1,0:T(8,128)(2,1)} %copy-done.22, bf16[19,64,256]{2,1,0:T(8,128)(2,1)} %collective-permute-done.32.refs_2_, ...), custom_call_target="tpu_custom_call" | custom-call | flops 20000000000 | tf_op jit(solution)/shard_map/pallas_call | solution.py:678
  190.5 9.8 %collective-permute-done.28 = bf16[9,32,256]{2,1,0:T(8,128)(2,1)S(1)} collective-permute-done((bf16[9,32,256]{2,1,0:T(8,128)(2,1)S(1)}, bf16[9,32,256]{2,1,0:T(8,128)(2,1)S(1)}, u32[]{:S(2)}, u32[]{:S(2)}) %collective-permute-start.28) | collective-permute-done | bytes 147488 | tf_op jit(solution)/shard_map/ppermute | solution.py:746
  201.7 1.7 collective-permute-start.34
  204.8 3.2 %shard_map.218.refs_4_ = f32[9,256,512]{2,1,0:T(8,128)} custom-call(s32[8]{0:T(128)} %stack.65.spots_ref, bf16[9,64,256]{2,1,0:T(8,128)(2,1)} %copy-done.26, bf16[9,64,256]{2,1,0:T(8,128)(2,1)} %copy-done.27, bf16[9,64,256]{2,1,0:T(8,128)(2,1)} %copy-done.33, bf16[9,64,256]{2,1,0:T(8,128)(2,1)} %collective-permute-done.39.refs_3_), custom_call_target="tpu_custom_call" | custom-call | flops 20000000000 | tf_op jit(solution)/shard_map/pallas_call | solution.py:678
  208.9 4.1 %shard_map.217 = (f32[18,256,512]{2,1,0:T(8,128)}, f32[1,256,512]{2,1,0:T(8,128)}) custom-call(s32[8]{0:T(128)} %stack.63.spots_ref, bf16[19,64,256]{2,1,0:T(8,128)(2,1)} %copy-done.28, bf16[19,64,256]{2,1,0:T(8,128)(2,1)} %copy-done.29, bf16[19,64,256]{2,1,0:T(8,128)(2,1)} %copy-done.30, ...), custom_call_target="tpu_custom_call", output_to_operand_aliasing={{0}: (5, {}), {1}: (6, {})} | custom-call | flops 20000000000 | tf_op jit(solution)/shard_map/pallas_call | solution.py:678
  216.3 3.2 %shard_map.219 = f32[9,256,512]{2,1,0:T(8,128)} custom-call(s32[8]{0:T(128)} %stack.63.spots_ref, bf16[9,64,256]{2,1,0:T(8,128)(2,1)} %copy-done.31, bf16[9,64,256]{2,1,0:T(8,128)(2,1)} %copy-done.32, bf16[9,64,256]{2,1,0:T(8,128)(2,1)} %copy-done.34, bf16[9,64,256]{2,1,0:T(8,128)(2,1)} %copy-done.35, ...), custom_call_target="tpu_custom_call", output_to_operand_aliasing={{}: (5, {})} | custom-call | flops 20000000000 | tf_op jit(solution)/shard_map/pallas_call | solution.py:678
  (174 shorter events, 30.6 us)
Async XLA Ops:
  3.5 17.7 %copy-start.7 = (bf16[256,512]{1,0:T(8,128)(2,1)S(1)}, bf16[256,512]{1,0:T(8,128)(2,1)}, u32[]{:S(2)}) copy-start(bf16[256,512]{1,0:T(8,128)(2,1)} %refs_4_.1) | copy-start | bytes 786436
  4.5 9.8 %collective-permute-start = (bf16[672,256]{1,0:T(8,128)(2,1)S(1)}, bf16[672,256]{1,0:T(8,128)(2,1)S(1)}, u32[]{:S(2)}, u32[]{:S(2)}) collective-permute-start(bf16[672,256]{1,0:T(8,128)(2,1)S(1)} %shard_map.203), channel_id=1, source_target_pairs={{0,16},{16,0},{1,17},{17,1},{2,18},{18,2},{3,19},{19,3},{4,20},{20... | collective-permute-start | bytes 1032200 | tf_op jit(solution)/shard_map/ppermute | solution.py:871
  5.1 2.8 %collective-permute-start.1 = (bf16[2,1,32,256]{3,2,1,0:T(8,128)(2,1)S(1)}, bf16[2,1,32,256]{3,2,1,0:T(8,128)(2,1)S(1)}, u32[]{:S(2)}, u32[]{:S(2)}) collective-permute-start(bf16[2,1,32,256]{3,2,1,0:T(8,128)(2,1)S(1)} %slice.57), channel_id=1, source_target_pairs={{0,16},{1,17},{2,18},{3,19},{4,20},{5,21},{6,22},{7,23},{8,24},{9,... | collective-permute-start | bytes 98312 | tf_op jit(solution)/shard_map/ppermute | solution.py:733
  7.9 6.4 %collective-permute-start.2 = (bf16[2,17,1,256]{3,2,1,0:T(2,128)(2,1)S(1)}, bf16[2,17,1,256]{3,2,1,0:T(2,128)(2,1)S(1)}, u32[]{:S(2)}, u32[]{:S(2)}) collective-permute-start(bf16[2,17,1,256]{3,2,1,0:T(2,128)(2,1)S(1)} %pad_maximum_fusion.10), channel_id=1, source_target_pairs={{0,4},{4,8},{8,12},{1,5},{5,9},{9,13},{2,6},{6,10},{10,14},{3,7},{... | collective-permute-start | bytes 52232 | tf_op jit(solution)/shard_map/ppermute | solution.py:733
  15.7 16.8 %collective-permute-start.3 = (bf16[480,256]{1,0:T(8,128)(2,1)S(1)}, bf16[480,256]{1,0:T(8,128)(2,1)S(1)}, u32[]{:S(2)}, u32[]{:S(2)}) collective-permute-start(bf16[480,256]{1,0:T(8,128)(2,1)S(1)} %get-tuple-element.107), channel_id=1, source_target_pairs={{0,4},{4,8},{8,12},{1,5},{5,9},{9,13},{2,6},{6,10},{10,14},{3,7},{... | collective-permute-start | bytes 737288 | tf_op jit(solution)/shard_map/ppermute | solution.py:733
  19.9 12.7 %collective-permute-start.4 = (bf16[480,256]{1,0:T(8,128)(2,1)S(1)}, bf16[480,256]{1,0:T(8,128)(2,1)S(1)}, u32[]{:S(2)}, u32[]{:S(2)}) collective-permute-start(bf16[480,256]{1,0:T(8,128)(2,1)S(1)} %get-tuple-element.108), channel_id=1, source_target_pairs={{4,0},{8,4},{12,8},{5,1},{9,5},{13,9},{6,2},{10,6},{14,10},{7,3},{... | collective-permute-start | bytes 737288 | tf_op jit(solution)/shard_map/ppermute | solution.py:733
  24.6 19.1 %all-to-all-start = ((f32[32,1,2176]{2,1,0:T(1,128)}), f32[32,1,2176]{2,1,0:T(1,128)S(1)}, u32[]{:S(2)}, u32[]{:S(2)}) async-start(f32[32,1,2176]{2,1,0:T(1,128)} %shard_map.206), calls=%async_computation | async-start | bytes 557056 | tf_op jit(solution)/shard_map/all_to_all | solution.py:737
  50.8 34.6 %collective-permute-start.5 = (bf16[624,1536]{1,0:T(8,128)(2,1)}, bf16[624,1536]{1,0:T(8,128)(2,1)}, u32[]{:S(2)}, u32[]{:S(2)}) collective-permute-start(bf16[624,1536]{1,0:T(8,128)(2,1)} %get-tuple-element.124.refs_1_), channel_id=1, source_target_pairs={{0,16},{16,0},{1,17},{17,1},{2,18},{18,2},{3,19},{19,3},{4,20},{20... | collective-permute-start | bytes 5750792 | tf_op jit(solution)/shard_map/ppermute | solution.py:746
  50.9 10.5 %all-to-all-start.1 = ((f32[32,1,1024]{2,1,0:T(1,128)}), f32[32,1,1024]{2,1,0:T(1,128)S(1)}, u32[]{:S(2)}, u32[]{:S(2)}) async-start(f32[32,1,1024]{2,1,0:T(1,128)} %get-tuple-element.117), calls=%async_computation.1 | async-start | bytes 262144 | tf_op jit(solution)/shard_map/all_to_all | solution.py:737
  53.5 30.2 %collective-permute-start.6 = (bf16[624,768]{1,0:T(8,128)(2,1)S(1)}, bf16[624,768]{1,0:T(8,128)(2,1)}, u32[]{:S(2)}, u32[]{:S(2)}) collective-permute-start(bf16[624,768]{1,0:T(8,128)(2,1)S(1)} %copy-done.19), channel_id=1, source_target_pairs={{0,16},{16,0},{1,17},{17,1},{2,18},{18,2},{3,19},{19,3},{4,20},{20... | collective-permute-start | bytes 2875400 | tf_op jit(solution)/shard_map/ppermute | solution.py:746
  66.7 12.0 %all-to-all-start.2 = ((f32[32,1,1536]{2,1,0:T(1,128)}), f32[32,1,1536]{2,1,0:T(1,128)S(1)}, u32[]{:S(2)}, u32[]{:S(2)}) async-start(f32[32,1,1536]{2,1,0:T(1,128)} %get-tuple-element.121), calls=%async_computation.2 | async-start | bytes 393216 | tf_op jit(solution)/shard_map/all_to_all | solution.py:737
  69.7 43.8 %copy-start.9 = (s32[5]{0:T(128)}, s32[5]{0:T(128)S(1)}, u32[]{:S(2)}) copy-start(s32[5]{0:T(128)S(1)} %stack.59.refs_0_) | copy-start | bytes 64
  83.6 1.8 collective-permute-start.7
  93.8 21.9 %collective-permute-start.8 = (bf16[19,64,256]{2,1,0:T(8,128)(2,1)S(1)}, bf16[19,64,256]{2,1,0:T(8,128)(2,1)}, u32[]{:S(2)}, u32[]{:S(2)}) collective-permute-start(bf16[19,64,256]{2,1,0:T(8,128)(2,1)S(1)} %get-tuple-element.133), channel_id=1, source_target_pairs={{0,4},{4,0},{8,12},{12,8},{1,5},{5,1},{9,13},{13,9},{2,6},{6,2},{1... | collective-permute-start | bytes 1867784 | tf_op jit(solution)/shard_map/ppermute | solution.py:746
  94.8 21.0 %collective-permute-start.9 = (bf16[19,64,256]{2,1,0:T(8,128)(2,1)}, bf16[19,64,256]{2,1,0:T(8,128)(2,1)}, u32[]{:S(2)}, u32[]{:S(2)}) collective-permute-start(bf16[19,64,256]{2,1,0:T(8,128)(2,1)} %get-tuple-element.134), channel_id=1, source_target_pairs={{0,8},{4,12},{8,0},{12,4},{1,9},{5,13},{9,1},{13,5},{2,10},{6,14},... | collective-permute-start | bytes 1867784 | tf_op jit(solution)/shard_map/ppermute | solution.py:746
  102.4 11.1 %all-to-all-start.3 = ((f32[32,1,1024]{2,1,0:T(1,128)}), f32[32,1,1024]{2,1,0:T(1,128)S(1)}, u32[]{:S(2)}, u32[]{:S(2)}) async-start(f32[32,1,1024]{2,1,0:T(1,128)} %get-tuple-element.138), calls=%async_computation.3 | async-start | bytes 262144 | tf_op jit(solution)/shard_map/all_to_all | solution.py:737
  105.8 15.5 %collective-permute-start.12 = (bf16[672,768]{1,0:T(8,128)(2,1)S(1)}, bf16[672,768]{1,0:T(8,128)(2,1)}, u32[]{:S(2)}, u32[]{:S(2)}) collective-permute-start(bf16[672,768]{1,0:T(8,128)(2,1)S(1)} %copy-done.20), channel_id=1, source_target_pairs={{0,16},{16,0},{1,17},{17,1},{2,18},{18,2},{3,19},{19,3},{4,20},{20... | collective-permute-start | bytes 3096584 | tf_op jit(solution)/shard_map/ppermute | solution.py:746
  119.6 9.2 %collective-permute-start.10 = (bf16[19,32,256]{2,1,0:T(8,128)(2,1)}, bf16[19,32,256]{2,1,0:T(8,128)(2,1)S(1)}, u32[]{:S(2)}, u32[]{:S(2)}) collective-permute-start(bf16[19,32,256]{2,1,0:T(8,128)(2,1)} %get-tuple-element.147), channel_id=1, source_target_pairs={{0,8},{4,12},{8,0},{12,4},{1,9},{5,13},{9,1},{13,5},{2,10},{6,14},... | collective-permute-start | bytes 933896 | tf_op jit(solution)/shard_map/ppermute | solution.py:746
  120.4 8.9 %collective-permute-start.11 = (bf16[19,32,256]{2,1,0:T(8,128)(2,1)}, bf16[19,32,256]{2,1,0:T(8,128)(2,1)}, u32[]{:S(2)}, u32[]{:S(2)}) collective-permute-start(bf16[19,32,256]{2,1,0:T(8,128)(2,1)} %get-tuple-element.148), channel_id=1, source_target_pairs={{0,4},{4,0},{8,12},{12,8},{1,5},{5,1},{9,13},{13,9},{2,6},{6,2},{1... | collective-permute-start | bytes 933896 | tf_op jit(solution)/shard_map/ppermute | solution.py:746
  121.3 1.4 collective-permute-start.13
  130.8 10.3 %collective-permute-start.14 = (bf16[38,16,256]{2,1,0:T(8,128)(2,1)S(1)}, bf16[38,16,256]{2,1,0:T(8,128)(2,1)S(1)}, u32[]{:S(2)}, u32[]{:S(2)}) collective-permute-start(bf16[38,16,256]{2,1,0:T(8,128)(2,1)S(1)} %select_convert_fusion), channel_id=1, source_target_pairs={{0,1},{1,0},{2,3},{3,2},{4,5},{5,4},{6,7},{7,6},{8,9},{9,8},{10,11... | collective-permute-start | bytes 933896 | tf_op jit(solution)/shard_map/ppermute | solution.py:746
  132.0 8.3 %collective-permute-start.15 = (bf16[9,64,256]{2,1,0:T(8,128)(2,1)S(1)}, bf16[9,64,256]{2,1,0:T(8,128)(2,1)S(1)}, u32[]{:S(2)}, u32[]{:S(2)}) collective-permute-start(bf16[9,64,256]{2,1,0:T(8,128)(2,1)S(1)} %get-tuple-element.159), channel_id=1, source_target_pairs={{0,4},{4,0},{8,12},{12,8},{1,5},{5,1},{9,13},{13,9},{2,6},{6,2},{1... | collective-permute-start | bytes 884744 | tf_op jit(solution)/shard_map/ppermute | solution.py:746
  132.6 8.4 %collective-permute-start.16 = (bf16[9,64,256]{2,1,0:T(8,128)(2,1)S(1)}, bf16[9,64,256]{2,1,0:T(8,128)(2,1)S(1)}, u32[]{:S(2)}, u32[]{:S(2)}) collective-permute-start(bf16[9,64,256]{2,1,0:T(8,128)(2,1)S(1)} %get-tuple-element.160), channel_id=1, source_target_pairs={{0,8},{4,12},{8,0},{12,4},{1,9},{5,13},{9,1},{13,5},{2,10},{6,14},... | collective-permute-start | bytes 884744 | tf_op jit(solution)/shard_map/ppermute | solution.py:746
  141.2 8.8 %collective-permute-start.17 = (bf16[38,8,256]{2,1,0:T(8,128)(2,1)S(1)}, bf16[38,8,256]{2,1,0:T(8,128)(2,1)S(1)}, u32[]{:S(2)}, u32[]{:S(2)}) collective-permute-start(bf16[38,8,256]{2,1,0:T(8,128)(2,1)S(1)} %select_convert_fusion.1), channel_id=1, source_target_pairs={{0,2},{1,3},{2,0},{3,1},{4,6},{5,7},{6,4},{7,5},{8,10},{9,11},{10,... | collective-permute-start | bytes 466952 | tf_op jit(solution)/shard_map/ppermute | solution.py:746
  142.2 5.2 %collective-permute-start.18 = (bf16[9,32,256]{2,1,0:T(8,128)(2,1)S(1)}, bf16[9,32,256]{2,1,0:T(8,128)(2,1)S(1)}, u32[]{:S(2)}, u32[]{:S(2)}) collective-permute-start(bf16[9,32,256]{2,1,0:T(8,128)(2,1)S(1)} %select_convert_fusion.4), channel_id=1, source_target_pairs={{0,8},{4,12},{8,0},{12,4},{1,9},{5,13},{9,1},{13,5},{2,10},{6,14},... | collective-permute-start | bytes 442376 | tf_op jit(solution)/shard_map/ppermute | solution.py:746
  143.7 5.2 %collective-permute-start.19 = (bf16[9,32,256]{2,1,0:T(8,128)(2,1)S(1)}, bf16[9,32,256]{2,1,0:T(8,128)(2,1)S(1)}, u32[]{:S(2)}, u32[]{:S(2)}) collective-permute-start(bf16[9,32,256]{2,1,0:T(8,128)(2,1)S(1)} %select_convert_fusion.3), channel_id=1, source_target_pairs={{0,4},{4,0},{8,12},{12,8},{1,5},{5,1},{9,13},{13,9},{2,6},{6,2},{1... | collective-permute-start | bytes 442376 | tf_op jit(solution)/shard_map/ppermute | solution.py:746
  150.2 9.0 %collective-permute-start.20 = (bf16[38,8,256]{2,1,0:T(8,128)(2,1)S(1)}, bf16[38,8,256]{2,1,0:T(8,128)(2,1)S(1)}, u32[]{:S(2)}, u32[]{:S(2)}) collective-permute-start(bf16[38,8,256]{2,1,0:T(8,128)(2,1)S(1)} %add_convert_fusion), channel_id=1, source_target_pairs={{0,2},{1,3},{2,0},{3,1},{4,6},{5,7},{6,4},{7,5},{8,10},{9,11},{10,... | collective-permute-start | bytes 466952 | tf_op jit(solution)/shard_map/ppermute | solution.py:746
  151.4 7.8 %collective-permute-start.21 = (bf16[18,16,256]{2,1,0:T(8,128)(2,1)S(1)}, bf16[18,16,256]{2,1,0:T(8,128)(2,1)S(1)}, u32[]{:S(2)}, u32[]{:S(2)}) collective-permute-start(bf16[18,16,256]{2,1,0:T(8,128)(2,1)S(1)} %select_convert_fusion.2), channel_id=1, source_target_pairs={{0,1},{1,0},{2,3},{3,2},{4,5},{5,4},{6,7},{7,6},{8,9},{9,8},{10,11... | collective-permute-start | bytes 442376 | tf_op jit(solution)/shard_map/ppermute | solution.py:746
  159.3 9.9 %collective-permute-start.22 = (bf16[38,16,256]{2,1,0:T(8,128)(2,1)S(1)}, bf16[38,16,256]{2,1,0:T(8,128)(2,1)S(1)}, u32[]{:S(2)}, u32[]{:S(2)}) collective-permute-start(bf16[38,16,256]{2,1,0:T(8,128)(2,1)S(1)} %pad_maximum_fusion.4), channel_id=1, source_target_pairs={{0,1},{1,0},{2,3},{3,2},{4,5},{5,4},{6,7},{7,6},{8,9},{9,8},{10,11... | collective-permute-start | bytes 933896 | tf_op jit(solution)/shard_map/ppermute | solution.py:746
  159.4 7.5 %collective-permute-start.23 = (bf16[18,8,256]{2,1,0:T(8,128)(2,1)S(1)}, bf16[18,8,256]{2,1,0:T(8,128)(2,1)S(1)}, u32[]{:S(2)}, u32[]{:S(2)}) collective-permute-start(bf16[18,8,256]{2,1,0:T(8,128)(2,1)S(1)} %select_convert_fusion.5), channel_id=1, source_target_pairs={{0,2},{1,3},{2,0},{3,1},{4,6},{5,7},{6,4},{7,5},{8,10},{9,11},{10,... | collective-permute-start | bytes 221192 | tf_op jit(solution)/shard_map/ppermute | solution.py:746
  169.4 8.0 %collective-permute-start.24 = (bf16[19,32,256]{2,1,0:T(8,128)(2,1)S(1)}, bf16[19,32,256]{2,1,0:T(8,128)(2,1)S(1)}, u32[]{:S(2)}, u32[]{:S(2)}) collective-permute-start(bf16[19,32,256]{2,1,0:T(8,128)(2,1)S(1)} %get-tuple-element.204), channel_id=1, source_target_pairs={{0,8},{4,12},{8,0},{12,4},{1,9},{5,13},{9,1},{13,5},{2,10},{6,14},... | collective-permute-start | bytes 933896 | tf_op jit(solution)/shard_map/ppermute | solution.py:746
  170.4 7.3 %collective-permute-start.25 = (bf16[19,32,256]{2,1,0:T(8,128)(2,1)S(1)}, bf16[19,32,256]{2,1,0:T(8,128)(2,1)S(1)}, u32[]{:S(2)}, u32[]{:S(2)}) collective-permute-start(bf16[19,32,256]{2,1,0:T(8,128)(2,1)S(1)} %get-tuple-element.203), channel_id=1, source_target_pairs={{0,4},{4,0},{8,12},{12,8},{1,5},{5,1},{9,13},{13,9},{2,6},{6,2},{1... | collective-permute-start | bytes 933896 | tf_op jit(solution)/shard_map/ppermute | solution.py:746
  170.7 5.3 %collective-permute-start.26 = (bf16[18,8,256]{2,1,0:T(8,128)(2,1)S(1)}, bf16[18,8,256]{2,1,0:T(8,128)(2,1)S(1)}, u32[]{:S(2)}, u32[]{:S(2)}) collective-permute-start(bf16[18,8,256]{2,1,0:T(8,128)(2,1)S(1)} %add_convert_fusion.1), channel_id=1, source_target_pairs={{0,2},{1,3},{2,0},{3,1},{4,6},{5,7},{6,4},{7,5},{8,10},{9,11},{10,... | collective-permute-start | bytes 221192 | tf_op jit(solution)/shard_map/ppermute | solution.py:746
  177.8 8.2 %collective-permute-start.32 = (bf16[19,64,256]{2,1,0:T(8,128)(2,1)S(1)}, bf16[19,64,256]{2,1,0:T(8,128)(2,1)}, u32[]{:S(2)}, u32[]{:S(2)}) collective-permute-start(bf16[19,64,256]{2,1,0:T(8,128)(2,1)S(1)} %pad_maximum_fusion.1.refs_0_), channel_id=1, source_target_pairs={{0,16},{16,0},{1,17},{17,1},{2,18},{18,2},{3,19},{19,3},{4,20},{20... | collective-permute-start | bytes 1867784 | tf_op jit(solution)/shard_map/ppermute | solution.py:746
  178.0 8.4 %collective-permute-start.33 = (bf16[19,64,256]{2,1,0:T(8,128)(2,1)S(1)}, bf16[19,64,256]{2,1,0:T(8,128)(2,1)}, u32[]{:S(2)}, u32[]{:S(2)}) collective-permute-start(bf16[19,64,256]{2,1,0:T(8,128)(2,1)S(1)} %pad_maximum_fusion.2.refs_1_), channel_id=1, source_target_pairs={{0,16},{16,0},{1,17},{17,1},{2,18},{18,2},{3,19},{19,3},{4,20},{20... | collective-permute-start | bytes 1867784 | tf_op jit(solution)/shard_map/ppermute | solution.py:746
  178.6 6.3 %collective-permute-start.27 = (bf16[18,16,256]{2,1,0:T(8,128)(2,1)S(1)}, bf16[18,16,256]{2,1,0:T(8,128)(2,1)S(1)}, u32[]{:S(2)}, u32[]{:S(2)}) collective-permute-start(bf16[18,16,256]{2,1,0:T(8,128)(2,1)S(1)} %pad_maximum_fusion.9), channel_id=1, source_target_pairs={{0,1},{1,0},{2,3},{3,2},{4,5},{5,4},{6,7},{7,6},{8,9},{9,8},{10,11... | collective-permute-start | bytes 442376 | tf_op jit(solution)/shard_map/ppermute | solution.py:746
  181.4 18.8 %collective-permute-start.30 = (bf16[19,64,256]{2,1,0:T(8,128)(2,1)S(1)}, bf16[19,64,256]{2,1,0:T(8,128)(2,1)S(1)}, u32[]{:S(2)}, u32[]{:S(2)}) collective-permute-start(bf16[19,64,256]{2,1,0:T(8,128)(2,1)S(1)} %pad_maximum_fusion.1.refs_0_), channel_id=1, source_target_pairs={{0,4},{4,0},{8,12},{12,8},{1,5},{5,1},{9,13},{13,9},{2,6},{6,2},{1... | collective-permute-start | bytes 1867784 | tf_op jit(solution)/shard_map/ppermute | solution.py:746
  181.7 18.6 %collective-permute-start.31 = (bf16[19,64,256]{2,1,0:T(8,128)(2,1)S(1)}, bf16[19,64,256]{2,1,0:T(8,128)(2,1)S(1)}, u32[]{:S(2)}, u32[]{:S(2)}) collective-permute-start(bf16[19,64,256]{2,1,0:T(8,128)(2,1)S(1)} %pad_maximum_fusion.2.refs_1_), channel_id=1, source_target_pairs={{0,8},{4,12},{8,0},{12,4},{1,9},{5,13},{9,1},{13,5},{2,10},{6,14},... | collective-permute-start | bytes 1867784 | tf_op jit(solution)/shard_map/ppermute | solution.py:746
  185.0 15.3 %collective-permute-start.28 = (bf16[9,32,256]{2,1,0:T(8,128)(2,1)S(1)}, bf16[9,32,256]{2,1,0:T(8,128)(2,1)S(1)}, u32[]{:S(2)}, u32[]{:S(2)}) collective-permute-start(bf16[9,32,256]{2,1,0:T(8,128)(2,1)S(1)} %get-tuple-element.214), channel_id=1, source_target_pairs={{0,8},{4,12},{8,0},{12,4},{1,9},{5,13},{9,1},{13,5},{2,10},{6,14},... | collective-permute-start | bytes 442376 | tf_op jit(solution)/shard_map/ppermute | solution.py:746
  186.1 14.2 %collective-permute-start.29 = (bf16[9,32,256]{2,1,0:T(8,128)(2,1)S(1)}, bf16[9,32,256]{2,1,0:T(8,128)(2,1)S(1)}, u32[]{:S(2)}, u32[]{:S(2)}) collective-permute-start(bf16[9,32,256]{2,1,0:T(8,128)(2,1)S(1)} %get-tuple-element.213), channel_id=1, source_target_pairs={{0,4},{4,0},{8,12},{12,8},{1,5},{5,1},{9,13},{13,9},{2,6},{6,2},{1... | collective-permute-start | bytes 442376 | tf_op jit(solution)/shard_map/ppermute | solution.py:746
  200.4 3.7 %collective-permute-start.38 = (bf16[9,64,256]{2,1,0:T(8,128)(2,1)S(1)}, bf16[9,64,256]{2,1,0:T(8,128)(2,1)S(1)}, u32[]{:S(2)}, u32[]{:S(2)}) collective-permute-start(bf16[9,64,256]{2,1,0:T(8,128)(2,1)S(1)} %pad_maximum_fusion.6.refs_0_), channel_id=1, source_target_pairs={{0,16},{16,0},{1,17},{17,1},{2,18},{18,2},{3,19},{19,3},{4,20},{20... | collective-permute-start | bytes 884744 | tf_op jit(solution)/shard_map/ppermute | solution.py:746
  200.5 4.1 %collective-permute-start.39 = (bf16[9,64,256]{2,1,0:T(8,128)(2,1)S(1)}, bf16[9,64,256]{2,1,0:T(8,128)(2,1)}, u32[]{:S(2)}, u32[]{:S(2)}) collective-permute-start(bf16[9,64,256]{2,1,0:T(8,128)(2,1)S(1)} %pad_maximum_fusion.7.refs_1_), channel_id=1, source_target_pairs={{0,16},{16,0},{1,17},{17,1},{2,18},{18,2},{3,19},{19,3},{4,20},{20... | collective-permute-start | bytes 884744 | tf_op jit(solution)/shard_map/ppermute | solution.py:746
  201.7 11.3 %collective-permute-start.34 = (bf16[9,64,256]{2,1,0:T(8,128)(2,1)S(1)}, bf16[9,64,256]{2,1,0:T(8,128)(2,1)S(1)}, u32[]{:S(2)}, u32[]{:S(2)}) collective-permute-start(bf16[9,64,256]{2,1,0:T(8,128)(2,1)S(1)} %pad_maximum_fusion.6.refs_0_), channel_id=1, source_target_pairs={{0,4},{4,0},{8,12},{12,8},{1,5},{5,1},{9,13},{13,9},{2,6},{6,2},{1... | collective-permute-start | bytes 884744 | tf_op jit(solution)/shard_map/ppermute | solution.py:746
  203.4 9.6 %collective-permute-start.35 = (bf16[9,64,256]{2,1,0:T(8,128)(2,1)S(1)}, bf16[9,64,256]{2,1,0:T(8,128)(2,1)S(1)}, u32[]{:S(2)}, u32[]{:S(2)}) collective-permute-start(bf16[9,64,256]{2,1,0:T(8,128)(2,1)S(1)} %pad_maximum_fusion.7.refs_1_), channel_id=1, source_target_pairs={{0,8},{4,12},{8,0},{12,4},{1,9},{5,13},{9,1},{13,5},{2,10},{6,14},... | collective-permute-start | bytes 884744 | tf_op jit(solution)/shard_map/ppermute | solution.py:746
  204.1 3.9 %collective-permute-start.36 = (bf16[19,64,256]{2,1,0:T(8,128)(2,1)S(1)}, bf16[19,64,256]{2,1,0:T(8,128)(2,1)S(1)}, u32[]{:S(2)}, u32[]{:S(2)}) collective-permute-start(bf16[19,64,256]{2,1,0:T(8,128)(2,1)S(1)} %collective-permute-done.30.refs_0_), channel_id=1, source_target_pairs={{0,16},{16,0},{1,17},{17,1},{2,18},{18,2},{3,19},{19,3},{4,20},{20... | collective-permute-start | bytes 1867784 | tf_op jit(solution)/shard_map/ppermute | solution.py:746
  204.1 3.9 %collective-permute-start.37 = (bf16[19,64,256]{2,1,0:T(8,128)(2,1)S(1)}, bf16[19,64,256]{2,1,0:T(8,128)(2,1)}, u32[]{:S(2)}, u32[]{:S(2)}) collective-permute-start(bf16[19,64,256]{2,1,0:T(8,128)(2,1)S(1)} %collective-permute-done.31.refs_1_), channel_id=1, source_target_pairs={{0,16},{16,0},{1,17},{17,1},{2,18},{18,2},{3,19},{19,3},{4,20},{20... | collective-permute-start | bytes 1867784 | tf_op jit(solution)/shard_map/ppermute | solution.py:746
  213.0 1.8 collective-permute-start.40
  213.6 1.6 collective-permute-start.41
  (34 other events, 242.5 us)

commit v4 on v2

--- a/solution.py
+++ b/solution.py
@@ -14,6 +14,7 @@
 inner = 0.7978845608028654
 cubic = 0.044715
 over = 6
+CHUNKS = "sent_a", "kept_a", "sent_b", "kept_b"
 rim = 3
 
 
@@ -36,6 +37,12 @@
             for job in self.jobs[name][slice(*which) if which else slice(None)]:
                 job.start()
 
+    def start_all(self, names):
+        for k in range(max((len(self.jobs[n]) for n in names), default=0)):
+            for n in names:
+                if k < len(self.jobs[n]):
+                    self.jobs[n][k].start()
+
     def wait(self, *names):
         for name, *which in map(named, names):
             for job in self.jobs[name][slice(*which) if which else slice(None)]:
@@ -55,9 +62,13 @@
     return [(k, (slice(None), pl.ds(at, size))) for k, at in enumerate((0, total - size))]
 
 
-def lane_parts(total, count):
+def cuts(*at):
+    return [(k, (pl.ds(a, b - a),)) for k, (a, b) in enumerate(zip(at, at[1:]))]
+
+
+def lane_parts(total, count, rows=slice(None)):
     size = total // count
-    return [(k, (slice(None), pl.ds(k * size, size))) for k in range(count)]
+    return [(k, (rows, pl.ds(k * size, size))) for k in range(count)]
 
 
 def call(body, ins, outs, scratch=None, far_in=(), far_out=(), smem=(), parts=None, limit=52, cost=0):
@@ -81,7 +92,7 @@
         if far:
             pairs = {n: (plain[n], buffers[n]) if n in far_in else (buffers[n], plain[n]) for n in far}
             copies = Copies(jobs, pairs, rest[-1])
-            copies.start(*far_in)
+            copies.start_all(far_in)
         body(Refs({**plain, **buffers, **more}), copies)
 
     buffers = [pltpu.VMEM(kinds[n].shape, kinds[n].dtype) for n in far]
@@ -277,6 +288,8 @@
         [column_sum(zm), column_sum(zm * z), column_sum(zpm), column_sum(zpm * zp), column_sum(mask)], axis=1
     )
     r.spread[...] = jnp.broadcast_to(row[None], r.spread.shape)
+    copies.start("spread")
+    copies.wait("spread")
 
 
 def first_kernel(r, copies):
@@ -389,7 +402,8 @@
         sums = [sums[0] + column_sum(zm), sums[1] + column_sum(zm * z)]
     row = jnp.concatenate(sums, axis=1)
     r.spread[...] = jnp.broadcast_to(row[None], r.spread.shape)
-    copies.wait("h3", "pre2")
+    copies.start("spread")
+    copies.wait("h3", "pre2", "spread")
 
 
 def third_kernel(r, copies):
@@ -403,9 +417,11 @@
     r.mom2[...] = jnp.concatenate([c2, i2, cp, ip, jnp.zeros((4, width), f32)], axis=0)
     sums = [jnp.zeros((1, width), f32)] * 3
     both_shift = r.shift2[...] + r.shiftp[...]
-    copies.wait("pre2", "prep", "cotq")
     total = r.grad.shape[0] // S
     for line in range(total):
+        if line % (total // 2) == 0:
+            k = line // (total // 2)
+            copies.wait(("pre2", k), ("prep", k), ("cotq", k))
         at = line * S
         shifted = slice(L + 1 + at, L + 1 + at + S)
         n2 = (r.pre2[at : at + S, :] - c2) * i2
@@ -422,14 +438,15 @@
         sums = [a + b for a, b in zip(sums, new)]
         if (line + 1) % (total // 2) == 0:
             copies.start(("grad", (line + 1) // (total // 2) - 1))
+    row = jnp.concatenate(sums, axis=1)
+    r.spread[...] = jnp.broadcast_to(row[None], r.spread.shape)
+    copies.start("spread")
     for i in range(rows):
         for g in range(groups):
             at = (i + 1) * L + g * S + 1
             r.out[g, i, :, :] = r.field[at : at + cols, :].astype(bf16)
     copies.start("out")
-    row = jnp.concatenate(sums, axis=1)
-    r.spread[...] = jnp.broadcast_to(row[None], r.spread.shape)
-    copies.wait("grad", "out")
+    copies.wait("grad", "out", "spread")
 
 
 def halves(r, source, at, frame, to, rows_w):
@@ -453,8 +470,12 @@
     t3 = jnp.sum(r.tot3[...], axis=0)
     gg2, gs, ggp = (t3[:, k * width : (k + 1) * width] for k in range(3))
     r.gain_second[...], r.shift_second[...], r.gain_proj[...], r.shift_proj[...] = gg2, gs, ggp, gs
-    copies.wait("grad", "pre2", "prep")
+    tiny = "gain_second", "shift_second", "gain_proj", "shift_proj"
+    copies.start(*tiny)
     for m0, m in chunks(Q, L):
+        if m0 in (0, 6 * L):
+            k = m0 // (6 * L)
+            copies.wait(("grad", k), ("pre2", k), ("prep", k))
         shifted = slice(L + 1 + m0, L + 1 + m0 + m)
         mask = wide(r.maskp[shifted, :], width) / n
         n2 = (r.pre2[m0 : m0 + m, :] - c2) * i2
@@ -469,7 +490,7 @@
     copies.start("gpu")
     halves(r, r.gq, L, 2 * L + 1, 0, rows_w)
     halves(r, r.gpq, L - 1, 2 * L, rows_w, rows_w)
-    copies.wait("gpu", "gq")
+    copies.wait("gpu", "gq", *tiny)
 
 
 def hidden_kernel(r, copies):
@@ -493,7 +514,7 @@
         r.act[...] = gh if a == 0 else r.act[...] + gh
     copies.wait("keep")
     sums = [jnp.zeros((1, width), f32)] * 2
-    for m0, m in chunks(U, L):
+    for k, (m0, m) in enumerate(chunks(U, L)):
         frame = slice(2 * L + 2 + m0, 2 * L + 2 + m0 + m)
         n1 = (r.keep[frame, :] - center) * inv
         v = n1 * r.gain[...] + r.shift[...]
@@ -501,10 +522,14 @@
         g = gelu_slope(v, gelu_parts(v)) * mask * r.act[m0 : m0 + m, :]
         r.act[m0 : m0 + m, :] = g
         r.normed[m0 : m0 + m, :] = n1 * mask
+        if k % 3 == 2:
+            copies.start(("act", k // 3), ("normed", k // 3))
         g = g * wide(r.ownp[frame, :], width)
         sums = [sums[0] + column_sum(g * n1), sums[1] + column_sum(g)]
     row = jnp.concatenate(sums, axis=1)
     r.spread[...] = jnp.broadcast_to(row[None], r.spread.shape)
+    copies.start("spread")
+    copies.wait("act", "normed", "spread")
 
 
 def split_store(r, rows, unit, first):
@@ -532,7 +557,7 @@
                 r.h3_far[at : at + rows_w, lanes], r.far[:rows_w, :]
             )
             split_store(r, width, cin, (3 * b + a) * per)
-        copies.start(("kept_a", b), ("kept_b", b))
+        copies.start(*((name, b) for name in CHUNKS))
     at = 2 * L
     copies.wait("xe", "xe_far")
     middle = slice(cin, 2 * cin)
@@ -540,8 +565,8 @@
         r.xe_far[at : at + rows_w, middle], r.far[rows_w:, :]
     )
     split_store(r, cin, cin, 9 * per)
-    copies.start(("kept_a", 3), ("kept_b", 3))
-    copies.wait("kept_a", "kept_b")
+    copies.start(*((name, 3) for name in CHUNKS))
+    copies.wait(*CHUNKS)
 
 
 def first_back(r, gg, gs, count):
@@ -565,8 +590,11 @@
     L = r.act.shape[0] - r.rows_w
     t4 = jnp.sum(r.tot4[...], axis=0)
     r.gain_first[...], r.shift_first[...] = t4[:, :width], t4[:, width:]
+    copies.start("gain_first", "shift_first")
+    copies.wait("act", "normed")
     first_back(r, t4[:, :width], t4[:, width:], r.rows_w)
     halves(r, r.gf, 6, 2 * L, 0, r.rows_w)
+    copies.wait("gain_first", "shift_first")
 
 
 def weights_first_kernel(r, copies):
@@ -585,8 +613,8 @@
                 source_far[at : at + rows_w, lanes], r.far[...]
             )
         split_store(r, 3 * cin, cin, a * 3)
-        copies.start(("kept_a", a), ("kept_b", a))
-    copies.wait("kept_a", "kept_b")
+        copies.start(*((name, a) for name in CHUNKS))
+    copies.wait(*CHUNKS)
 
 
 def inputs_kernel(r, copies):
@@ -894,6 +922,7 @@
             xe=pltpu.VMEM((rows * groups * cols, 3 * cin), bf16),
             xo=pltpu.VMEM(((rows + 1) * groups * cols, 3 * cin), bf16),
         ),
+        far_out=("spread",),
     )
     tot1 = gather_sum(stats["spread"])
 
@@ -930,7 +959,7 @@
         dict(h3=shape((MP, 3 * width), bf16), pre2=shape((MQ, width)), spread=all_devices(2 * width), mom1=shape((8, width))),
         dict(hid=pltpu.VMEM((MP + 8, width), f32)),
         far_in=("pre1", "w2"),
-        far_out=("h3", "pre2"),
+        far_out=("h3", "pre2", "spread"),
         parts=dict(pre2=row_parts(MQ, 3)),
     )
     h3, pre2, mom1 = second["h3"], second["pre2"], second["mom1"]
@@ -951,8 +980,10 @@
         ),
         dict(field=pltpu.VMEM((MQ, width), f32)),
         far_in=("pre2", "prep", "cotq"),
-        far_out=("out", "grad"),
-        parts=dict(grad=row_parts(MQ, 2)),
+        far_out=("grad", "spread", "out"),
+        parts=dict(
+            grad=row_parts(MQ, 2), pre2=row_parts(MQ, 2), cotq=row_parts(MQ, 2), prep=cuts(L, L + MQ // 2 + 8, L + MQ + 8)
+        ),
     )
     mom2 = third["mom2"]
     tot3 = gather_sum(third["spread"])
@@ -975,7 +1006,8 @@
         ),
         dict(gpq=pltpu.VMEM((MQ, width), f32)),
         far_in=("pre2", "prep", "grad"),
-        far_out=("gpu", "gq"),
+        far_out=("gpu", "gq", "gain_second", "shift_second", "gain_proj", "shift_proj"),
+        parts=dict(grad=cuts(0, 6 * L, MQ), pre2=cuts(0, 6 * L, MQ), prep=cuts(L, 7 * L + 8, L + MQ + 8)),
         smem=("bits",),
     )
     far2 = partner(fourth["theirs"], *core)
@@ -992,13 +1024,14 @@
         chunk_shapes(taps2),
         dict(acc=pltpu.VMEM((width, half), f32)),
         far_in=("h3", "h3_far", "xe", "xe_far"),
-        far_out=("kept_a", "kept_b"),
+        far_out=CHUNKS,
         smem=("bits",),
         parts=dict(
-            h3=lane_parts(3 * width, 3),
-            h3_far=lane_parts(3 * width, 3),
-            kept_a=row_parts(taps2 - 1, 3) + [(3, (pl.ds(taps2 - 1, 1),))],
-            kept_b=row_parts(taps2 - 1, 3) + [(3, (pl.ds(taps2 - 1, 1),))],
+            h3=lane_parts(3 * width, 3, pl.ds(L, MW + 2 * L)),
+            h3_far=lane_parts(3 * width, 3, pl.ds(L, MW + 2 * L)),
+            xe=[(0, (pl.ds(2 * L, MW), pl.ds(cin, cin)))],
+            xe_far=[(0, (pl.ds(2 * L, MW), pl.ds(cin, cin)))],
+            **{name: row_parts(taps2 - 1, 3) + [(3, (pl.ds(taps2 - 1, 1),))] for name in CHUNKS},
         ),
     ).values()
     gq, *second_parts = lax.optimization_barrier((fourth["gq"], *second_parts))
@@ -1011,7 +1044,13 @@
         dict(act=shape((MU, width)), normed=shape((MU, width)), spread=all_devices(2 * width)),
         dict(g3=pltpu.VMEM((MQ, 3 * width), bf16)),
         far_in=("gq", "w2", "keep"),
-        parts=dict(w2=[(k, (pl.ds(2 - k, 1),)) for k in range(3)]),
+        far_out=("act", "normed", "spread"),
+        parts=dict(
+            w2=[(k, (pl.ds(2 - k, 1),)) for k in range(3)],
+            keep=cuts(2 * L, 2 * L + MU + 8),
+            act=row_parts(MU, 3),
+            normed=row_parts(MU, 3),
+        ),
     )
     tot4 = gather_sum(hidden["spread"])
     tree2.finish(20000000000)
@@ -1022,7 +1061,10 @@
         dict(bits=bits, act=act, normed=hidden["normed"], mom1=mom1, tot4=tot4, gain=g1, maskp=maskp, ownp=ownp),
         dict(mine=shape((MW, half), bf16), theirs=shape((MW, half), bf16), gain_first=vec(1), shift_first=vec(1)),
         dict(gf=pltpu.VMEM((MU + 16, width), f32)),
+        far_in=("act", "normed"),
+        far_out=("gain_first", "shift_first"),
         smem=("bits",),
+        parts=dict(act=cuts(0, MW), normed=cuts(0, MW)),
     )
     far1 = partner(fifth["theirs"], *core)
     first_parts = call(
@@ -1031,9 +1073,15 @@
         chunk_shapes(9),
         dict(acc=pltpu.VMEM((3 * cin, half), f32)),
         far_in=("xe", "xe_far", "xo", "xo_far"),
-        far_out=("kept_a", "kept_b"),
+        far_out=CHUNKS,
         smem=("bits",),
-        parts=dict(kept_a=row_parts(9, 3), kept_b=row_parts(9, 3)),
+        parts=dict(
+            xe=cuts(2 * L, 2 * L + MW),
+            xe_far=cuts(2 * L, 2 * L + MW),
+            xo=cuts(2 * L, 3 * L + MW),
+            xo_far=cuts(2 * L, 3 * L + MW),
+            **{name: row_parts(9, 3) for name in CHUNKS},
+        ),
     ).values()
     tree2.got, *first_parts = lax.optimization_barrier((tree2.got, *first_parts))
     tree2.finish()

time: 215 us -> 213 us (level)
  Pallas kernels: 71.5 us -> 69 us
    pallas_call x13, Pallas kernels: 61.2 us -> 58.7 us  [call(): pl.pallas_call(run, out_shape=list(outs.values()), in_specs=[spec(n) for...]
  transfers between devices with their start and end apart: 40 -> 40, of which waited for: 26 -> 25; matrix products, arithmetic and copies ran while one was open for 1% -> 1% of each run, Pallas kernels for 24% -> 24%
where the time goes in v4:
time: 213 us; the launch traced here: 212 us
  waiting for transfers between devices  76.9 us (36%)
  Pallas kernels  69 us (32%)
  starting transfers between devices  54.8 us (26%)
  other arithmetic  6.58 us (3%)
  local copies, waits for them, and re-layouts  3.23 us (2%)
    pallas_call x13, Pallas kernels, call(): pl.pallas_call(run, out_shape=list(outs.values()), in_specs=[spec(n) for...  58.7 us
    ppermute x31, waiting for transfers between devices, partner(): return lax.ppermute(value, axis, [(i, i ^ step) for i in range(count)])  52.4 us
    ppermute x31, starting transfers between devices, partner(): return lax.ppermute(value, axis, [(i, i ^ step) for i in range(count)])  25.2 us
    all_to_all x4, waiting for transfers between devices, gather_sum(): return lax.all_to_all(spread, axes, 0, 0)  22.1 us
    all_to_all x4, starting transfers between devices, gather_sum(): return lax.all_to_all(spread, axes, 0, 0)  16.8 us
    ppermute x4, starting transfers between devices, shifted(): lax.ppermute(value, axis, [(source, source + steps) for source in range(f...  12.3 us
    pallas_call x4, Pallas kernels, widen(): pl.pallas_call(body, out_shape=[shape((taps * per, n, 2 * m))] + [shape((...  10.3 us
  transfers between devices with their start and end apart: 40, of which 25 were waited for; matrix products, arithmetic and copies ran while one was open for 1% of the time, Pallas kernels for 24%

profile of v4, /device:TPU:0, one launch (start us, length us, event | category | flops | bytes accessed | tf_op | source)
XLA Modules:
  0.0 212.2 jit_solution(79079643023770753)
XLA Ops:
  5.1 2.0 collective-permute-start.1
  7.9 4.8 %collective-permute-start.2 = (bf16[2,17,1,256]{3,2,1,0:T(2,128)(2,1)S(1)}, bf16[2,17,1,256]{3,2,1,0:T(2,128)(2,1)S(1)}, u32[]{:S(2)}, u32[]{:S(2)}) collective-permute-start(bf16[2,17,1,256]{3,2,1,0:T(2,128)(2,1)S(1)} %pad_maximum_fusion.12), channel_id=1, source_target_pairs={{0,4},{4,8},{8,12},{1,5},{5,9},{9,13},{2,6},{6,10},{10,14},{3,7},{... | collective-permute-start | bytes 52232 | tf_op jit(solution)/shard_map/ppermute | solution.py:751
  12.8 1.6 collective-permute-done.2.refs_2_
  15.7 4.2 %collective-permute-start.3 = (bf16[480,256]{1,0:T(8,128)(2,1)S(1)}, bf16[480,256]{1,0:T(8,128)(2,1)S(1)}, u32[]{:S(2)}, u32[]{:S(2)}) collective-permute-start(bf16[480,256]{1,0:T(8,128)(2,1)S(1)} %get-tuple-element.101), channel_id=1, source_target_pairs={{0,4},{4,8},{8,12},{1,5},{5,9},{9,13},{2,6},{6,10},{10,14},{3,7},{... | collective-permute-start | bytes 737288 | tf_op jit(solution)/shard_map/ppermute | solution.py:751
  21.2 3.4 %shard_map.206 = f32[32,1,2176]{2,1,0:T(1,128)} custom-call(bf16[2,16,32,256]{3,2,1,0:T(8,128)(2,1)S(1)} %copy-done.1, bf16[2,1,32,256]{3,2,1,0:T(8,128)(2,1)S(1)} %collective-permute-done.1.refs_1_, bf16[2,17,1,256]{3,2,1,0:T(2,128)(2,1)S(1)} %collective-permute-done.2.refs_2_, bf16[2,8,16,128]{3,2,1,0:T(8,128)(2,1)S(1)} %broadcast_in_dim.2.refs_3_, ...), custom_call_target="tpu_custom_call" | custom-call | tf_op jit(solution)/shard_map/pallas_call | solution.py:100
  24.6 7.9 %all-to-all-start = ((f32[32,1,2176]{2,1,0:T(1,128)}), f32[32,1,2176]{2,1,0:T(1,128)S(1)}, u32[]{:S(2)}, u32[]{:S(2)}) async-start(f32[32,1,2176]{2,1,0:T(1,128)} %shard_map.206), calls=%async_computation | async-start | bytes 557056 | tf_op jit(solution)/shard_map/all_to_all | solution.py:755
  32.6 5.8 %shard_map.205 = (f32[624,512]{1,0:T(8,128)}, f32[624,512]{1,0:T(8,128)}, bf16[624,768]{1,0:T(8,128)(2,1)}, bf16[672,768]{1,0:T(8,128)(2,1)}, f32[624,128]{1,0:T...) custom-call(s32[2]{0:T(128)S(1)} %add_convert_fusion.2.refs_0_, bf16[2,16,32,256]{3,2,1,0:T(8,128)(2,1)} %refs_0_.1, ...), custom_call_target="tpu_custom_call" | custom-call | flops 20000000000 | tf_op jit(solution)/shard_map/pallas_call | solution.py:100
  38.4 5.4 %all-to-all-done.refs_1_ = f32[32,1,2176]{2,1,0:T(1,128)S(1)} async-done(((f32[32,1,2176]{2,1,0:T(1,128)}), f32[32,1,2176]{2,1,0:T(1,128)S(1)}, u32[]{:S(2)}, u32[]{:S(2)}) %all-to-all-start) | async-done | bytes 278560 | tf_op jit(solution)/shard_map/all_to_all | solution.py:755
  43.8 6.3 %shard_map.207 = (bf16[624,1536]{1,0:T(8,128)(2,1)}, f32[528,512]{1,0:T(8,128)}, f32[32,1,1024]{2,1,0:T(1,128)}, f32[8,512]{1,0:T(8,128)S(1)}) custom-call(f32[624,512]{1,0:T(8,128)} %get-tuple-element.103.refs_0_.refs_2_, f32[32,1,2176]{2,1,0:T(1,128)S(1)} %all-to-all-done.refs_1_, f32[1,512]{1,0:T(1,128)S(1)} %bitcast.25, f32[1,512]{1,0:T(1,128)S(1)} %bitcast.33, ...), custom_call_target="tpu_custom_call" | custom-call | tf_op jit(solution)/shard_map/pallas_call | solution.py:100
  50.2 2.6 %all-to-all-start.1 = ((f32[32,1,1024]{2,1,0:T(1,128)}), f32[32,1,1024]{2,1,0:T(1,128)S(1)}, u32[]{:S(2)}, u32[]{:S(2)}) async-start(f32[32,1,1024]{2,1,0:T(1,128)} %get-tuple-element.111), calls=%async_computation.1 | async-start | bytes 262144 | tf_op jit(solution)/shard_map/all_to_all | solution.py:755
  53.1 7.6 %all-to-all-done.1.refs_3_ = f32[32,1,1024]{2,1,0:T(1,128)S(1)} async-done(((f32[32,1,1024]{2,1,0:T(1,128)}), f32[32,1,1024]{2,1,0:T(1,128)S(1)}, u32[]{:S(2)}, u32[]{:S(2)}) %all-to-all-start.1) | async-done | bytes 131104 | tf_op jit(solution)/shard_map/all_to_all | solution.py:755
  60.8 4.2 %shard_map.208 = (bf16[2,8,16,512]{3,2,1,0:T(8,128)(2,1)}, f32[528,512]{1,0:T(8,128)}, f32[32,1,1536]{2,1,0:T(1,128)}, f32[8,512]{1,0:T(8,128)S(1)}) custom-call(f32[528,512]{1,0:T(8,128)} %get-tuple-element.108.refs_0_.refs_1_, f32[624,512]{1,0:T(8,128)} %get-tuple-element.109.refs_1_.refs_2_, f32[8,512]{1,0:T(8,128)S(1)} %get-tuple-element.110.refs_2_.refs_3_.refs_5_, ...), custom_call_target="tpu_custom_call" | custom-call | tf_op jit(solution)/shard_map/pallas_call | solution.py:100
  65.0 2.8 %all-to-all-start.2 = ((f32[32,1,1536]{2,1,0:T(1,128)}), f32[32,1,1536]{2,1,0:T(1,128)S(1)}, u32[]{:S(2)}, u32[]{:S(2)}) async-start(f32[32,1,1536]{2,1,0:T(1,128)} %get-tuple-element.115), calls=%async_computation.2 | async-start | bytes 393216 | tf_op jit(solution)/shard_map/all_to_all | solution.py:755
  67.9 9.1 %all-to-all-done.2.refs_5_ = f32[32,1,1536]{2,1,0:T(1,128)S(1)} async-done(((f32[32,1,1536]{2,1,0:T(1,128)}), f32[32,1,1536]{2,1,0:T(1,128)S(1)}, u32[]{:S(2)}, u32[]{:S(2)}) %all-to-all-start.2) | async-done | bytes 196640 | tf_op jit(solution)/shard_map/all_to_all | solution.py:755
  77.0 3.9 %shard_map.209 = (bf16[768,256]{1,0:T(8,128)(2,1)S(1)}, bf16[768,256]{1,0:T(8,128)(2,1)S(1)}, f32[536,512]{1,0:T(8,128)}, bf16[384,512]{1,0:T(8,128)(2,1)}, f32[...) custom-call(s32[5]{0:T(128)S(1)} %stack.35.refs_0_, ...), custom_call_target="tpu_custom_call" | custom-call | tf_op jit(solution)/shard_map/pallas_call | solution.py:100
  81.0 1.7 collective-permute-done.7.refs_6_
  82.7 7.6 %shard_map.210 = (bf16[19,64,256]{2,1,0:T(8,128)(2,1)S(1)}, f32[19,64,256]{2,1,0:T(8,128)}, bf16[19,64,256]{2,1,0:T(8,128)(2,1)}, f32[19,64,256]{2,1,0:T(8,128)}) custom-call(s32[5]{0:T(128)S(1)} %stack.35.refs_0_, bf16[624,1536]{1,0:T(8,128)(2,1)} %get-tuple-element.118.refs_1_, bf16[624,1536]{1,0:T(8,128)(2,1)} %collective-permute-done.5.refs_2_, ...), custom_call_target="tpu_custom_call" | custom-call | tf_op jit(solution)/shard_map/pallas_call | solution.py:100
  91.4 6.6 %shard_map.212 = (f32[432,512]{1,0:T(8,128)S(1)}, f32[432,512]{1,0:T(8,128)}, f32[32,1,1024]{2,1,0:T(1,128)}) custom-call(f32[536,512]{1,0:T(8,128)} %get-tuple-element.131.refs_0_, bf16[3,1536,512]{2,1,0:T(8,128)(2,1)} %bitcast.40, f32[624,512]{1,0:T(8,128)} %get-tuple-element.103.refs_0_.refs_2_, f32[8,512]{1,0:T(8,128)S(1)} %get-tuple-element.110.refs_2_.refs_3_.refs_5_, ...), custom_call_target="tpu_custom_call" | custom-call | tf_op jit(solution)/shard_map/pallas_call | solution.py:100
  98.9 3.5 %all-to-all-start.3 = ((f32[32,1,1024]{2,1,0:T(1,128)}), f32[32,1,1024]{2,1,0:T(1,128)S(1)}, u32[]{:S(2)}, u32[]{:S(2)}) async-start(f32[32,1,1024]{2,1,0:T(1,128)} %get-tuple-element.140), calls=%async_computation.3 | async-start | bytes 262144 | tf_op jit(solution)/shard_map/all_to_all | solution.py:755
  102.5 4.6 %collective-permute-done.8.refs_2_ = bf16[19,64,256]{2,1,0:T(8,128)(2,1)} collective-permute-done((bf16[19,64,256]{2,1,0:T(8,128)(2,1)S(1)}, bf16[19,64,256]{2,1,0:T(8,128)(2,1)}, u32[]{:S(2)}, u32[]{:S(2)}) %collective-permute-start.8) | collective-permute-done | bytes 622624 | tf_op jit(solution)/shard_map/ppermute | solution.py:764
  108.2 3.8 %shard_map.211 = (bf16[19,32,256]{2,1,0:T(8,128)(2,1)}, f32[19,32,256]{2,1,0:T(8,128)}, bf16[19,32,256]{2,1,0:T(8,128)(2,1)}, f32[19,32,256]{2,1,0:T(8,128)}) custom-call(s32[5]{0:T(128)} %copy-done.9, f32[19,64,256]{2,1,0:T(8,128)} %get-tuple-element.126.refs_1_, bf16[19,64,256]{2,1,0:T(8,128)(2,1)} %collective-permute-done.8.refs_2_, ...), custom_call_target="tpu_custom_call" | custom-call | flops 20000000000 | tf_op jit(solution)/shard_map/pallas_call | solution.py:100
  112.2 1.9 collective-permute-start.11
  114.2 2.2 %shard_map.213 = (bf16[384,256]{1,0:T(8,128)(2,1)S(1)}, bf16[384,256]{1,0:T(8,128)(2,1)S(1)}, f32[1,512]{1,0:T(1,128)}, f32[1,512]{1,0:T(1,128)}) custom-call(s32[5]{0:T(128)S(1)} %copy-done.10, f32[432,512]{1,0:T(8,128)} %copy-done.5, f32[432,512]{1,0:T(8,128)} %get-tuple-element.139.refs_2_.refs_1_, ...), custom_call_target="tpu_custom_call" | custom-call | tf_op jit(solution)/shard_map/pallas_call | solution.py:100
  117.9 6.3 %shard_map.214 = (bf16[9,64,256]{2,1,0:T(8,128)(2,1)S(1)}, f32[9,64,256]{2,1,0:T(8,128)S(1)}, bf16[9,64,256]{2,1,0:T(8,128)(2,1)S(1)}, f32[9,64,256]{2,1,0:T(8,128)}) custom-call(s32[5]{0:T(128)S(1)} %copy-done.10, bf16[624,768]{1,0:T(8,128)(2,1)} %get-tuple-element.119.refs_3_.refs_1_, bf16[672,768]{1,0:T(8,128)(2,1)} %get-tuple-element.137.refs_2_, ...), custom_call_target="tpu_custom_call" | custom-call | tf_op jit(solution)/shard_map/pallas_call | solution.py:100
  126.8 6.4 %shard_map.215 = bf16[2,16,32,256]{3,2,1,0:T(8,128)(2,1)} custom-call(f32[432,512]{1,0:T(8,128)S(1)} %copy-done.6, f32[432,512]{1,0:T(8,128)} %get-tuple-element.139.refs_2_.refs_1_, bf16[384,512]{1,0:T(8,128)(2,1)S(1)} %copy-done.16, bf16[3,768,512]{2,1,0:T(8,128)(2,1)} %bitcast.45, bf16[256,512]{1,0:T(8,128)(2,1)S(1)} %copy-done.7, ...), custom_call_target="tpu_custom_call" | custom-call | flops 10000000000 | tf_op jit(solution)/shard_map/pallas_call | solution.py:100
  134.3 1.8 collective-permute-start.19
  136.5 1.4 collective-permute-start.18
  138.0 1.6 collective-permute-done.19
  139.5 2.2 %collective-permute-done.18 = bf16[9,32,256]{2,1,0:T(8,128)(2,1)S(1)} collective-permute-done((bf16[9,32,256]{2,1,0:T(8,128)(2,1)S(1)}, bf16[9,32,256]{2,1,0:T(8,128)(2,1)S(1)}, u32[]{:S(2)}, u32[]{:S(2)}) %collective-permute-start.18) | collective-permute-done | bytes 147488 | tf_op jit(solution)/shard_map/ppermute | solution.py:764
  141.8 3.2 %collective-permute-done.17 = bf16[38,8,256]{2,1,0:T(8,128)(2,1)S(1)} collective-permute-done((bf16[38,8,256]{2,1,0:T(8,128)(2,1)S(1)}, bf16[38,8,256]{2,1,0:T(8,128)(2,1)S(1)}, u32[]{:S(2)}, u32[]{:S(2)}) %collective-permute-start.17) | collective-permute-done | bytes 155680 | tf_op jit(solution)/shard_map/ppermute | solution.py:764
  145.3 1.7 collective-permute-start.21
  147.0 6.8 %collective-permute-done.21 = bf16[18,16,256]{2,1,0:T(8,128)(2,1)S(1)} collective-permute-done((bf16[18,16,256]{2,1,0:T(8,128)(2,1)S(1)}, bf16[18,16,256]{2,1,0:T(8,128)(2,1)S(1)}, u32[]{:S(2)}, u32[]{:S(2)}) %collective-permute-start.21) | collective-permute-done | bytes 147488 | tf_op jit(solution)/shard_map/ppermute | solution.py:764
  154.0 2.7 %collective-permute-start.23 = (bf16[18,8,256]{2,1,0:T(8,128)(2,1)S(1)}, bf16[18,8,256]{2,1,0:T(8,128)(2,1)S(1)}, u32[]{:S(2)}, u32[]{:S(2)}) collective-permute-start(bf16[18,8,256]{2,1,0:T(8,128)(2,1)S(1)} %select_convert_fusion.5), channel_id=1, source_target_pairs={{0,2},{1,3},{2,0},{3,1},{4,6},{5,7},{6,4},{7,5},{8,10},{9,11},{10,... | collective-permute-start | bytes 221192 | tf_op jit(solution)/shard_map/ppermute | solution.py:764
  156.7 4.9 %collective-permute-done.23 = bf16[18,8,256]{2,1,0:T(8,128)(2,1)S(1)} collective-permute-done((bf16[18,8,256]{2,1,0:T(8,128)(2,1)S(1)}, bf16[18,8,256]{2,1,0:T(8,128)(2,1)S(1)}, u32[]{:S(2)}, u32[]{:S(2)}) %collective-permute-start.23) | collective-permute-done | bytes 73760 | tf_op jit(solution)/shard_map/ppermute | solution.py:764
  161.6 2.2 %collective-permute-done.22 = bf16[38,16,256]{2,1,0:T(8,128)(2,1)S(1)} collective-permute-done((bf16[38,16,256]{2,1,0:T(8,128)(2,1)S(1)}, bf16[38,16,256]{2,1,0:T(8,128)(2,1)S(1)}, u32[]{:S(2)}, u32[]{:S(2)}) %collective-permute-start.22) | collective-permute-done | bytes 311328 | tf_op jit(solution)/shard_map/ppermute | solution.py:764
  164.1 1.6 collective-permute-start.24
  167.8 4.1 %collective-permute-done.26 = bf16[18,8,256]{2,1,0:T(8,128)(2,1)S(1)} collective-permute-done((bf16[18,8,256]{2,1,0:T(8,128)(2,1)S(1)}, bf16[18,8,256]{2,1,0:T(8,128)(2,1)S(1)}, u32[]{:S(2)}, u32[]{:S(2)}) %collective-permute-start.26) | collective-permute-done | bytes 73760 | tf_op jit(solution)/shard_map/ppermute | solution.py:764
  172.1 1.5 collective-permute-done.25
  174.1 1.9 collective-permute-start.27
  176.6 2.7 %collective-permute-done.27 = bf16[18,16,256]{2,1,0:T(8,128)(2,1)S(1)} collective-permute-done((bf16[18,16,256]{2,1,0:T(8,128)(2,1)S(1)}, bf16[18,16,256]{2,1,0:T(8,128)(2,1)S(1)}, u32[]{:S(2)}, u32[]{:S(2)}) %collective-permute-start.27) | collective-permute-done | bytes 147488 | tf_op jit(solution)/shard_map/ppermute | solution.py:764
  179.5 1.7 collective-permute-start.28
  181.9 8.6 %collective-permute-done.28 = bf16[9,32,256]{2,1,0:T(8,128)(2,1)S(1)} collective-permute-done((bf16[9,32,256]{2,1,0:T(8,128)(2,1)S(1)}, bf16[9,32,256]{2,1,0:T(8,128)(2,1)S(1)}, u32[]{:S(2)}, u32[]{:S(2)}) %collective-permute-start.28) | collective-permute-done | bytes 147488 | tf_op jit(solution)/shard_map/ppermute | solution.py:764
  190.5 2.0 collective-permute-done.29
  196.7 2.8 %shard_map.216 = (f32[18,256,512]{2,1,0:T(8,128)}, f32[1,256,512]{2,1,0:T(8,128)}) custom-call(s32[1]{0:T(128)} %bitcast.10.side_ref, bf16[19,256,256]{2,1,0:T(8,128)(2,1)S(1)} %pad_maximum_fusion.half_ref), custom_call_target="tpu_custom_call" | custom-call | tf_op jit(solution)/shard_map/pallas_call | solution.py:696
  199.5 3.4 %shard_map.217 = (f32[18,256,512]{2,1,0:T(8,128)}, f32[1,256,512]{2,1,0:T(8,128)}) custom-call(s32[1]{0:T(128)} %bitcast.15.side_ref, bf16[19,256,256]{2,1,0:T(8,128)(2,1)} %collective-permute-done.34.half_ref, f32[18,256,512]{2,1,0:T(8,128)} %get-tuple-element.175.refs_0_, ...), custom_call_target="tpu_custom_call", output_to_operand_aliasing={{0}: (2, {}), {1}: (3, {})} | custom-call | tf_op jit(solution)/shard_map/pallas_call | solution.py:696
  203.3 1.5 collective-permute-done.32
  207.1 2.1 shard_map.218.refs_0_
  210.0 2.1 shard_map.219
  (142 shorter events, 30.0 us)
Async XLA Ops:
  3.5 17.7 %copy-start.1 = (bf16[2,16,32,256]{3,2,1,0:T(8,128)(2,1)S(1)}, bf16[2,16,32,256]{3,2,1,0:T(8,128)(2,1)}, u32[]{:S(2)}) copy-start(bf16[2,16,32,256]{3,2,1,0:T(8,128)(2,1)} %refs_0_.1) | copy-start | bytes 1572868
  3.5 17.7 %copy-start.7 = (bf16[256,512]{1,0:T(8,128)(2,1)S(1)}, bf16[256,512]{1,0:T(8,128)(2,1)}, u32[]{:S(2)}) copy-start(bf16[256,512]{1,0:T(8,128)(2,1)} %refs_4_.1) | copy-start | bytes 786436
  4.5 9.8 %collective-permute-start = (bf16[672,256]{1,0:T(8,128)(2,1)S(1)}, bf16[672,256]{1,0:T(8,128)(2,1)S(1)}, u32[]{:S(2)}, u32[]{:S(2)}) collective-permute-start(bf16[672,256]{1,0:T(8,128)(2,1)S(1)} %shard_map.203), channel_id=1, source_target_pairs={{0,16},{16,0},{1,17},{17,1},{2,18},{18,2},{3,19},{19,3},{4,20},{20... | collective-permute-start | bytes 1032200 | tf_op jit(solution)/shard_map/ppermute | solution.py:893
  5.1 2.8 %collective-permute-start.1 = (bf16[2,1,32,256]{3,2,1,0:T(8,128)(2,1)S(1)}, bf16[2,1,32,256]{3,2,1,0:T(8,128)(2,1)S(1)}, u32[]{:S(2)}, u32[]{:S(2)}) collective-permute-start(bf16[2,1,32,256]{3,2,1,0:T(8,128)(2,1)S(1)} %slice.57), channel_id=1, source_target_pairs={{0,16},{1,17},{2,18},{3,19},{4,20},{5,21},{6,22},{7,23},{8,24},{9,... | collective-permute-start | bytes 98312 | tf_op jit(solution)/shard_map/ppermute | solution.py:751
  7.9 6.4 %collective-permute-start.2 = (bf16[2,17,1,256]{3,2,1,0:T(2,128)(2,1)S(1)}, bf16[2,17,1,256]{3,2,1,0:T(2,128)(2,1)S(1)}, u32[]{:S(2)}, u32[]{:S(2)}) collective-permute-start(bf16[2,17,1,256]{3,2,1,0:T(2,128)(2,1)S(1)} %pad_maximum_fusion.12), channel_id=1, source_target_pairs={{0,4},{4,8},{8,12},{1,5},{5,9},{9,13},{2,6},{6,10},{10,14},{3,7},{... | collective-permute-start | bytes 52232 | tf_op jit(solution)/shard_map/ppermute | solution.py:751
  15.7 16.9 %collective-permute-start.3 = (bf16[480,256]{1,0:T(8,128)(2,1)S(1)}, bf16[480,256]{1,0:T(8,128)(2,1)S(1)}, u32[]{:S(2)}, u32[]{:S(2)}) collective-permute-start(bf16[480,256]{1,0:T(8,128)(2,1)S(1)} %get-tuple-element.101), channel_id=1, source_target_pairs={{0,4},{4,8},{8,12},{1,5},{5,9},{9,13},{2,6},{6,10},{10,14},{3,7},{... | collective-permute-start | bytes 737288 | tf_op jit(solution)/shard_map/ppermute | solution.py:751
  19.9 12.7 %collective-permute-start.4 = (bf16[480,256]{1,0:T(8,128)(2,1)S(1)}, bf16[480,256]{1,0:T(8,128)(2,1)S(1)}, u32[]{:S(2)}, u32[]{:S(2)}) collective-permute-start(bf16[480,256]{1,0:T(8,128)(2,1)S(1)} %get-tuple-element.102), channel_id=1, source_target_pairs={{4,0},{8,4},{12,8},{5,1},{9,5},{13,9},{6,2},{10,6},{14,10},{7,3},{... | collective-permute-start | bytes 737288 | tf_op jit(solution)/shard_map/ppermute | solution.py:751
  24.6 19.2 %all-to-all-start = ((f32[32,1,2176]{2,1,0:T(1,128)}), f32[32,1,2176]{2,1,0:T(1,128)S(1)}, u32[]{:S(2)}, u32[]{:S(2)}) async-start(f32[32,1,2176]{2,1,0:T(1,128)} %shard_map.206), calls=%async_computation | async-start | bytes 557056 | tf_op jit(solution)/shard_map/all_to_all | solution.py:755
  43.8 17.0 %copy-start.11 = (f32[512]{0:T(512)S(1)}, f32[512]{0:T(512)}, u32[]{:S(2)}) copy-start(f32[512]{0:T(512)} %param.17) | copy-start | bytes 6148
  43.8 17.0 %copy-start.12 = (f32[512]{0:T(512)S(1)}, f32[512]{0:T(512)}, u32[]{:S(2)}) copy-start(f32[512]{0:T(512)} %param.20) | copy-start | bytes 6148
  43.8 17.0 %copy-start.14 = (f32[512]{0:T(512)S(1)}, f32[512]{0:T(512)}, u32[]{:S(2)}) copy-start(f32[512]{0:T(512)} %param.18) | copy-start | bytes 6148
  43.8 17.0 %copy-start.15 = (f32[512]{0:T(512)S(1)}, f32[512]{0:T(512)}, u32[]{:S(2)}) copy-start(f32[512]{0:T(512)} %param.21) | copy-start | bytes 6148
  50.2 32.5 %collective-permute-start.5 = (bf16[624,1536]{1,0:T(8,128)(2,1)}, bf16[624,1536]{1,0:T(8,128)(2,1)}, u32[]{:S(2)}, u32[]{:S(2)}) collective-permute-start(bf16[624,1536]{1,0:T(8,128)(2,1)} %get-tuple-element.118.refs_1_), channel_id=1, source_target_pairs={{0,16},{16,0},{1,17},{17,1},{2,18},{18,2},{3,19},{19,3},{4,20},{20... | collective-permute-start | bytes 5750792 | tf_op jit(solution)/shard_map/ppermute | solution.py:764
  50.2 10.5 %all-to-all-start.1 = ((f32[32,1,1024]{2,1,0:T(1,128)}), f32[32,1,1024]{2,1,0:T(1,128)S(1)}, u32[]{:S(2)}, u32[]{:S(2)}) async-start(f32[32,1,1024]{2,1,0:T(1,128)} %get-tuple-element.111), calls=%async_computation.1 | async-start | bytes 262144 | tf_op jit(solution)/shard_map/all_to_all | solution.py:755
  52.9 28.1 %collective-permute-start.6 = (bf16[624,768]{1,0:T(8,128)(2,1)S(1)}, bf16[624,768]{1,0:T(8,128)(2,1)}, u32[]{:S(2)}, u32[]{:S(2)}) collective-permute-start(bf16[624,768]{1,0:T(8,128)(2,1)S(1)} %copy-done.19), channel_id=1, source_target_pairs={{0,16},{16,0},{1,17},{17,1},{2,18},{18,2},{3,19},{19,3},{4,20},{20... | collective-permute-start | bytes 2875400 | tf_op jit(solution)/shard_map/ppermute | solution.py:764
  65.0 12.0 %all-to-all-start.2 = ((f32[32,1,1536]{2,1,0:T(1,128)}), f32[32,1,1536]{2,1,0:T(1,128)S(1)}, u32[]{:S(2)}, u32[]{:S(2)}) async-start(f32[32,1,1536]{2,1,0:T(1,128)} %get-tuple-element.115), calls=%async_computation.2 | async-start | bytes 393216 | tf_op jit(solution)/shard_map/all_to_all | solution.py:755
  67.9 14.8 %copy-start.9 = (s32[5]{0:T(128)}, s32[5]{0:T(128)S(1)}, u32[]{:S(2)}) copy-start(s32[5]{0:T(128)S(1)} %stack.35.refs_0_) | copy-start | bytes 64
  80.9 1.8 collective-permute-start.7
  90.3 16.8 %collective-permute-start.8 = (bf16[19,64,256]{2,1,0:T(8,128)(2,1)S(1)}, bf16[19,64,256]{2,1,0:T(8,128)(2,1)}, u32[]{:S(2)}, u32[]{:S(2)}) collective-permute-start(bf16[19,64,256]{2,1,0:T(8,128)(2,1)S(1)} %get-tuple-element.127), channel_id=1, source_target_pairs={{0,4},{4,0},{8,12},{12,8},{1,5},{5,1},{9,13},{13,9},{2,6},{6,2},{1... | collective-permute-start | bytes 1867784 | tf_op jit(solution)/shard_map/ppermute | solution.py:764
  91.3 16.9 %collective-permute-start.9 = (bf16[19,64,256]{2,1,0:T(8,128)(2,1)}, bf16[19,64,256]{2,1,0:T(8,128)(2,1)}, u32[]{:S(2)}, u32[]{:S(2)}) collective-permute-start(bf16[19,64,256]{2,1,0:T(8,128)(2,1)} %get-tuple-element.129), channel_id=1, source_target_pairs={{0,8},{4,12},{8,0},{12,4},{1,9},{5,13},{9,1},{13,5},{2,10},{6,14},... | collective-permute-start | bytes 1867784 | tf_op jit(solution)/shard_map/ppermute | solution.py:764
  91.4 25.1 %collective-permute-start.12 = (bf16[672,768]{1,0:T(8,128)(2,1)S(1)}, bf16[672,768]{1,0:T(8,128)(2,1)}, u32[]{:S(2)}, u32[]{:S(2)}) collective-permute-start(bf16[672,768]{1,0:T(8,128)(2,1)S(1)} %copy-done.20), channel_id=1, source_target_pairs={{0,16},{16,0},{1,17},{17,1},{2,18},{18,2},{3,19},{19,3},{4,20},{20... | collective-permute-start | bytes 3096584 | tf_op jit(solution)/shard_map/ppermute | solution.py:764
  98.9 15.2 %all-to-all-start.3 = ((f32[32,1,1024]{2,1,0:T(1,128)}), f32[32,1,1024]{2,1,0:T(1,128)S(1)}, u32[]{:S(2)}, u32[]{:S(2)}) async-start(f32[32,1,1024]{2,1,0:T(1,128)} %get-tuple-element.140), calls=%async_computation.3 | async-start | bytes 262144 | tf_op jit(solution)/shard_map/all_to_all | solution.py:755
  102.5 11.7 %copy-start.10 = (s32[5]{0:T(128)S(1)}, s32[5]{0:T(128)}, u32[]{:S(2)}) copy-start(s32[5]{0:T(128)} %copy-done.9) | copy-start | bytes 64
  112.0 12.2 %collective-permute-start.10 = (bf16[19,32,256]{2,1,0:T(8,128)(2,1)}, bf16[19,32,256]{2,1,0:T(8,128)(2,1)S(1)}, u32[]{:S(2)}, u32[]{:S(2)}) collective-permute-start(bf16[19,32,256]{2,1,0:T(8,128)(2,1)} %get-tuple-element.135), channel_id=1, source_target_pairs={{0,8},{4,12},{8,0},{12,4},{1,9},{5,13},{9,1},{13,5},{2,10},{6,14},... | collective-permute-start | bytes 933896 | tf_op jit(solution)/shard_map/ppermute | solution.py:764
  112.2 12.0 %collective-permute-start.11 = (bf16[19,32,256]{2,1,0:T(8,128)(2,1)}, bf16[19,32,256]{2,1,0:T(8,128)(2,1)S(1)}, u32[]{:S(2)}, u32[]{:S(2)}) collective-permute-start(bf16[19,32,256]{2,1,0:T(8,128)(2,1)} %get-tuple-element.136), channel_id=1, source_target_pairs={{0,4},{4,0},{8,12},{12,8},{1,5},{5,1},{9,13},{13,9},{2,6},{6,2},{1... | collective-permute-start | bytes 933896 | tf_op jit(solution)/shard_map/ppermute | solution.py:764
  116.4 1.5 collective-permute-start.13
  124.7 9.6 %collective-permute-start.14 = (bf16[38,16,256]{2,1,0:T(8,128)(2,1)S(1)}, bf16[38,16,256]{2,1,0:T(8,128)(2,1)S(1)}, u32[]{:S(2)}, u32[]{:S(2)}) collective-permute-start(bf16[38,16,256]{2,1,0:T(8,128)(2,1)S(1)} %select_convert_fusion), channel_id=1, source_target_pairs={{0,1},{1,0},{2,3},{3,2},{4,5},{5,4},{6,7},{7,6},{8,9},{9,8},{10,11... | collective-permute-start | bytes 933896 | tf_op jit(solution)/shard_map/ppermute | solution.py:764
  125.4 8.8 %collective-permute-start.15 = (bf16[9,64,256]{2,1,0:T(8,128)(2,1)S(1)}, bf16[9,64,256]{2,1,0:T(8,128)(2,1)S(1)}, u32[]{:S(2)}, u32[]{:S(2)}) collective-permute-start(bf16[9,64,256]{2,1,0:T(8,128)(2,1)S(1)} %get-tuple-element.150), channel_id=1, source_target_pairs={{0,4},{4,0},{8,12},{12,8},{1,5},{5,1},{9,13},{13,9},{2,6},{6,2},{1... | collective-permute-start | bytes 884744 | tf_op jit(solution)/shard_map/ppermute | solution.py:764
  125.5 8.7 %collective-permute-start.16 = (bf16[9,64,256]{2,1,0:T(8,128)(2,1)S(1)}, bf16[9,64,256]{2,1,0:T(8,128)(2,1)S(1)}, u32[]{:S(2)}, u32[]{:S(2)}) collective-permute-start(bf16[9,64,256]{2,1,0:T(8,128)(2,1)S(1)} %get-tuple-element.151), channel_id=1, source_target_pairs={{0,8},{4,12},{8,0},{12,4},{1,9},{5,13},{9,1},{13,5},{2,10},{6,14},... | collective-permute-start | bytes 884744 | tf_op jit(solution)/shard_map/ppermute | solution.py:764
  134.3 5.2 %collective-permute-start.19 = (bf16[9,32,256]{2,1,0:T(8,128)(2,1)S(1)}, bf16[9,32,256]{2,1,0:T(8,128)(2,1)S(1)}, u32[]{:S(2)}, u32[]{:S(2)}) collective-permute-start(bf16[9,32,256]{2,1,0:T(8,128)(2,1)S(1)} %select_convert_fusion.3), channel_id=1, source_target_pairs={{0,4},{4,0},{8,12},{12,8},{1,5},{5,1},{9,13},{13,9},{2,6},{6,2},{1... | collective-permute-start | bytes 442376 | tf_op jit(solution)/shard_map/ppermute | solution.py:764
  136.4 8.6 %collective-permute-start.17 = (bf16[38,8,256]{2,1,0:T(8,128)(2,1)S(1)}, bf16[38,8,256]{2,1,0:T(8,128)(2,1)S(1)}, u32[]{:S(2)}, u32[]{:S(2)}) collective-permute-start(bf16[38,8,256]{2,1,0:T(8,128)(2,1)S(1)} %select_convert_fusion.1), channel_id=1, source_target_pairs={{0,2},{1,3},{2,0},{3,1},{4,6},{5,7},{6,4},{7,5},{8,10},{9,11},{10,... | collective-permute-start | bytes 466952 | tf_op jit(solution)/shard_map/ppermute | solution.py:764
  136.5 5.2 %collective-permute-start.18 = (bf16[9,32,256]{2,1,0:T(8,128)(2,1)S(1)}, bf16[9,32,256]{2,1,0:T(8,128)(2,1)S(1)}, u32[]{:S(2)}, u32[]{:S(2)}) collective-permute-start(bf16[9,32,256]{2,1,0:T(8,128)(2,1)S(1)} %select_convert_fusion.4), channel_id=1, source_target_pairs={{0,8},{4,12},{8,0},{12,4},{1,9},{5,13},{9,1},{13,5},{2,10},{6,14},... | collective-permute-start | bytes 442376 | tf_op jit(solution)/shard_map/ppermute | solution.py:764
  145.2 8.6 %collective-permute-start.20 = (bf16[38,8,256]{2,1,0:T(8,128)(2,1)S(1)}, bf16[38,8,256]{2,1,0:T(8,128)(2,1)S(1)}, u32[]{:S(2)}, u32[]{:S(2)}) collective-permute-start(bf16[38,8,256]{2,1,0:T(8,128)(2,1)S(1)} %add_convert_fusion), channel_id=1, source_target_pairs={{0,2},{1,3},{2,0},{3,1},{4,6},{5,7},{6,4},{7,5},{8,10},{9,11},{10,... | collective-permute-start | bytes 466952 | tf_op jit(solution)/shard_map/ppermute | solution.py:764
  145.3 8.4 %collective-permute-start.21 = (bf16[18,16,256]{2,1,0:T(8,128)(2,1)S(1)}, bf16[18,16,256]{2,1,0:T(8,128)(2,1)S(1)}, u32[]{:S(2)}, u32[]{:S(2)}) collective-permute-start(bf16[18,16,256]{2,1,0:T(8,128)(2,1)S(1)} %select_convert_fusion.2), channel_id=1, source_target_pairs={{0,1},{1,0},{2,3},{3,2},{4,5},{5,4},{6,7},{7,6},{8,9},{9,8},{10,11... | collective-permute-start | bytes 442376 | tf_op jit(solution)/shard_map/ppermute | solution.py:764
  153.8 10.0 %collective-permute-start.22 = (bf16[38,16,256]{2,1,0:T(8,128)(2,1)S(1)}, bf16[38,16,256]{2,1,0:T(8,128)(2,1)S(1)}, u32[]{:S(2)}, u32[]{:S(2)}) collective-permute-start(bf16[38,16,256]{2,1,0:T(8,128)(2,1)S(1)} %pad_maximum_fusion.6), channel_id=1, source_target_pairs={{0,1},{1,0},{2,3},{3,2},{4,5},{5,4},{6,7},{7,6},{8,9},{9,8},{10,11... | collective-permute-start | bytes 933896 | tf_op jit(solution)/shard_map/ppermute | solution.py:764
  154.0 7.6 %collective-permute-start.23 = (bf16[18,8,256]{2,1,0:T(8,128)(2,1)S(1)}, bf16[18,8,256]{2,1,0:T(8,128)(2,1)S(1)}, u32[]{:S(2)}, u32[]{:S(2)}) collective-permute-start(bf16[18,8,256]{2,1,0:T(8,128)(2,1)S(1)} %select_convert_fusion.5), channel_id=1, source_target_pairs={{0,2},{1,3},{2,0},{3,1},{4,6},{5,7},{6,4},{7,5},{8,10},{9,11},{10,... | collective-permute-start | bytes 221192 | tf_op jit(solution)/shard_map/ppermute | solution.py:764
  164.1 8.0 %collective-permute-start.24 = (bf16[19,32,256]{2,1,0:T(8,128)(2,1)S(1)}, bf16[19,32,256]{2,1,0:T(8,128)(2,1)S(1)}, u32[]{:S(2)}, u32[]{:S(2)}) collective-permute-start(bf16[19,32,256]{2,1,0:T(8,128)(2,1)S(1)} %get-tuple-element.196), channel_id=1, source_target_pairs={{0,8},{4,12},{8,0},{12,4},{1,9},{5,13},{9,1},{13,5},{2,10},{6,14},... | collective-permute-start | bytes 933896 | tf_op jit(solution)/shard_map/ppermute | solution.py:764
  165.7 7.9 %collective-permute-start.25 = (bf16[19,32,256]{2,1,0:T(8,128)(2,1)S(1)}, bf16[19,32,256]{2,1,0:T(8,128)(2,1)S(1)}, u32[]{:S(2)}, u32[]{:S(2)}) collective-permute-start(bf16[19,32,256]{2,1,0:T(8,128)(2,1)S(1)} %get-tuple-element.195), channel_id=1, source_target_pairs={{0,4},{4,0},{8,12},{12,8},{1,5},{5,1},{9,13},{13,9},{2,6},{6,2},{1... | collective-permute-start | bytes 933896 | tf_op jit(solution)/shard_map/ppermute | solution.py:764
  166.5 5.3 %collective-permute-start.26 = (bf16[18,8,256]{2,1,0:T(8,128)(2,1)S(1)}, bf16[18,8,256]{2,1,0:T(8,128)(2,1)S(1)}, u32[]{:S(2)}, u32[]{:S(2)}) collective-permute-start(bf16[18,8,256]{2,1,0:T(8,128)(2,1)S(1)} %add_convert_fusion.1), channel_id=1, source_target_pairs={{0,2},{1,3},{2,0},{3,1},{4,6},{5,7},{6,4},{7,5},{8,10},{9,11},{10,... | collective-permute-start | bytes 221192 | tf_op jit(solution)/shard_map/ppermute | solution.py:764
  173.6 18.9 %collective-permute-start.31 = (bf16[19,64,256]{2,1,0:T(8,128)(2,1)S(1)}, bf16[19,64,256]{2,1,0:T(8,128)(2,1)S(1)}, u32[]{:S(2)}, u32[]{:S(2)}) collective-permute-start(bf16[19,64,256]{2,1,0:T(8,128)(2,1)S(1)} %pad_maximum_fusion.4), channel_id=1, source_target_pairs={{0,8},{4,12},{8,0},{12,4},{1,9},{5,13},{9,1},{13,5},{2,10},{6,14},... | collective-permute-start | bytes 1867784 | tf_op jit(solution)/shard_map/ppermute | solution.py:764
  174.1 5.2 %collective-permute-start.27 = (bf16[18,16,256]{2,1,0:T(8,128)(2,1)S(1)}, bf16[18,16,256]{2,1,0:T(8,128)(2,1)S(1)}, u32[]{:S(2)}, u32[]{:S(2)}) collective-permute-start(bf16[18,16,256]{2,1,0:T(8,128)(2,1)S(1)} %pad_maximum_fusion.11), channel_id=1, source_target_pairs={{0,1},{1,0},{2,3},{3,2},{4,5},{5,4},{6,7},{7,6},{8,9},{9,8},{10,11... | collective-permute-start | bytes 442376 | tf_op jit(solution)/shard_map/ppermute | solution.py:764
  176.1 16.3 %collective-permute-start.30 = (bf16[19,64,256]{2,1,0:T(8,128)(2,1)S(1)}, bf16[19,64,256]{2,1,0:T(8,128)(2,1)S(1)}, u32[]{:S(2)}, u32[]{:S(2)}) collective-permute-start(bf16[19,64,256]{2,1,0:T(8,128)(2,1)S(1)} %pad_maximum_fusion.3), channel_id=1, source_target_pairs={{0,4},{4,0},{8,12},{12,8},{1,5},{5,1},{9,13},{13,9},{2,6},{6,2},{1... | collective-permute-start | bytes 1867784 | tf_op jit(solution)/shard_map/ppermute | solution.py:764
  179.5 11.0 %collective-permute-start.28 = (bf16[9,32,256]{2,1,0:T(8,128)(2,1)S(1)}, bf16[9,32,256]{2,1,0:T(8,128)(2,1)S(1)}, u32[]{:S(2)}, u32[]{:S(2)}) collective-permute-start(bf16[9,32,256]{2,1,0:T(8,128)(2,1)S(1)} %get-tuple-element.210), channel_id=1, source_target_pairs={{0,8},{4,12},{8,0},{12,4},{1,9},{5,13},{9,1},{13,5},{2,10},{6,14},... | collective-permute-start | bytes 442376 | tf_op jit(solution)/shard_map/ppermute | solution.py:764
  181.2 11.3 %collective-permute-start.29 = (bf16[9,32,256]{2,1,0:T(8,128)(2,1)S(1)}, bf16[9,32,256]{2,1,0:T(8,128)(2,1)S(1)}, u32[]{:S(2)}, u32[]{:S(2)}) collective-permute-start(bf16[9,32,256]{2,1,0:T(8,128)(2,1)S(1)} %get-tuple-element.209), channel_id=1, source_target_pairs={{0,4},{4,0},{8,12},{12,8},{1,5},{5,1},{9,13},{13,9},{2,6},{6,2},{1... | collective-permute-start | bytes 442376 | tf_op jit(solution)/shard_map/ppermute | solution.py:764
  193.6 5.9 %collective-permute-start.34 = (bf16[19,256,256]{2,1,0:T(8,128)(2,1)S(1)}, bf16[19,256,256]{2,1,0:T(8,128)(2,1)}, u32[]{:S(2)}, u32[]{:S(2)}) collective-permute-start(bf16[19,256,256]{2,1,0:T(8,128)(2,1)S(1)} %pad_maximum_fusion.half_ref), channel_id=1, source_target_pairs={{0,16},{16,0},{1,17},{17,1},{2,18},{18,2},{3,19},{19,3},{4,20},{20... | collective-permute-start | bytes 7471112 | tf_op jit(solution)/shard_map/ppermute | solution.py:764
  193.7 9.6 %collective-permute-start.33 = (bf16[9,64,256]{2,1,0:T(8,128)(2,1)S(1)}, bf16[9,64,256]{2,1,0:T(8,128)(2,1)}, u32[]{:S(2)}, u32[]{:S(2)}) collective-permute-start(bf16[9,64,256]{2,1,0:T(8,128)(2,1)S(1)} %pad_maximum_fusion.9), channel_id=1, source_target_pairs={{0,8},{4,12},{8,0},{12,4},{1,9},{5,13},{9,1},{13,5},{2,10},{6,14},... | collective-permute-start | bytes 884744 | tf_op jit(solution)/shard_map/ppermute | solution.py:764
  195.4 9.4 %collective-permute-start.32 = (bf16[9,64,256]{2,1,0:T(8,128)(2,1)}, bf16[9,64,256]{2,1,0:T(8,128)(2,1)}, u32[]{:S(2)}, u32[]{:S(2)}) collective-permute-start(bf16[9,64,256]{2,1,0:T(8,128)(2,1)} %pad_maximum_fusion.8), channel_id=1, source_target_pairs={{0,4},{4,0},{8,12},{12,8},{1,5},{5,1},{9,13},{13,9},{2,6},{6,2},{1... | collective-permute-start | bytes 884744 | tf_op jit(solution)/shard_map/ppermute | solution.py:764
  207.1 2.9 %collective-permute-start.35 = (bf16[9,256,256]{2,1,0:T(8,128)(2,1)S(1)}, bf16[9,256,256]{2,1,0:T(8,128)(2,1)S(1)}, u32[]{:S(2)}, u32[]{:S(2)}) collective-permute-start(bf16[9,256,256]{2,1,0:T(8,128)(2,1)S(1)} %pad_maximum_fusion.1.half_ref), channel_id=1, source_target_pairs={{0,16},{16,0},{1,17},{17,1},{2,18},{18,2},{3,19},{19,3},{4,20},{20... | collective-permute-start | bytes 3538952 | tf_op jit(solution)/shard_map/ppermute | solution.py:764
  (16 other events, 95.0 us)

commit v5 on v4

--- a/solution.py
+++ b/solution.py
@@ -16,6 +16,14 @@
 over = 6
 CHUNKS = "sent_a", "kept_a", "sent_b", "kept_b"
 rim = 3
+
+
+class Names:
+    def __getattr__(self, name):
+        return name
+
+
+N = Names()
 
 
 class Refs:
@@ -178,8 +186,8 @@
                 at += cols
 
     last = r.x.shape[1] - over
-    copies.wait("x", "cot")
-    if hasattr(r, "up"):
+    copies.wait(N.x, N.cot)
+    if hasattr(r, N.up):
         pack(r.down, lambda n: last + n, lambda n: rows - rim + n, lambda tail, head: tail)
         pack(r.up, lambda n: last + n, lambda n: rows - rim + n, lambda tail, head: head)
     else:
@@ -288,8 +296,8 @@
         [column_sum(zm), column_sum(zm * z), column_sum(zpm), column_sum(zpm * zp), column_sum(mask)], axis=1
     )
     r.spread[...] = jnp.broadcast_to(row[None], r.spread.shape)
-    copies.start("spread")
-    copies.wait("spread")
+    copies.start(N.spread)
+    copies.wait(N.spread)
 
 
 def first_kernel(r, copies):
@@ -339,7 +347,7 @@
                     ]
                     at = b * cin + k * 128
                     out[n * L : (n + 1) * L, at : at + 128] = jnp.concatenate(parts, axis=0).astype(bf16)
-    copies.start("xe", "xo")
+    copies.start(N.xe, N.xo)
     for at in range(lines[1]):
         r.raw_m[0, at * V + 8 : at * V + 8 + cols, :] = mask(at % groups, at // groups)
     for n in range(1, rows + 6):
@@ -352,22 +360,22 @@
             lanes = slice(k * 128, (k + 1) * 128)
             r.raw_c[k, at * V + 8 : at * V + 8 + cols, :] = value[:, lanes]
             r.cotq[at * S : (at + 1) * S, lanes] = r.raw_c[k, at * V + 7 : at * V + 7 + S, :]
-    copies.start("cotq")
+    copies.start(N.cotq)
     r.ownp[...] = jnp.zeros(r.ownp.shape, f32)
     for i in range(rows):
         for g in range(groups):
             at = (i + 2) * L + g * S + 2
             r.ownp[at : at + cols, :] = r.own[g, i].astype(f32)
-    copies.wait("w1", "wp")
+    copies.wait(N.w1, N.wp)
     for k, (m0, m) in enumerate(chunks(r.pre1.shape[0], r.pre1.shape[0] // 3)):
         z = matmul(r.xo[m0 : m0 + m, :], r.w1[0])
         z += matmul(r.xe[m0 : m0 + m, :], r.w1[1])
         z += matmul(r.xo[L + m0 : L + m0 + m, :], r.w1[2])
         r.pre1[m0 : m0 + m, :] = z
-        copies.start(("pre1", k))
+        copies.start((N.pre1, k))
         r.prep[m0 : m0 + m, :] = matmul(r.xe[m0 : m0 + m, cin : 2 * cin], r.wp[...])
-        copies.start(("prep", k))
-    copies.wait("xe", "xo", "pre1", "prep", "cotq")
+        copies.start((N.prep, k))
+    copies.wait(N.xe, N.xo, N.pre1, N.prep, N.cotq)
 
 
 def second_kernel(r, copies):
@@ -380,7 +388,7 @@
     scale = inv * r.gain[...]
     M, Q = r.pre1.shape[0], r.pre2.shape[0]
     L = (M - Q) // 2
-    copies.wait("pre1")
+    copies.wait(N.pre1)
     for m0, m in chunks(M, 104):
         v = (r.pre1[m0 : m0 + m, :] - center) * scale + r.shift[...]
         mask = wide(r.maskp[m0 : m0 + m, :], width)
@@ -389,21 +397,35 @@
     for m0, m in chunks(M, 208):
         for b in range(3):
             r.h3[m0 : m0 + m, b * width : (b + 1) * width] = r.hid[m0 + b : m0 + b + m, :].astype(bf16)
-    copies.start("h3")
-    copies.wait("w2")
+    copies.start(N.h3)
+    copies.wait(N.w2)
     sums = [jnp.zeros((1, width), f32)] * 2
     for k, (m0, m) in enumerate(chunks(Q, Q // 3)):
         z = matmul(r.h3[m0 : m0 + m, :], r.w2[0])
         z += matmul(r.h3[L + m0 : L + m0 + m, :], r.w2[1])
         z += matmul(r.h3[2 * L + m0 : 2 * L + m0 + m, :], r.w2[2])
         r.pre2[m0 : m0 + m, :] = z
-        copies.start(("pre2", k))
+        copies.start((N.pre2, k))
         zm = z * wide(r.ownp[L + 1 + m0 : L + 1 + m0 + m, :], width)
         sums = [sums[0] + column_sum(zm), sums[1] + column_sum(zm * z)]
     row = jnp.concatenate(sums, axis=1)
     r.spread[...] = jnp.broadcast_to(row[None], r.spread.shape)
-    copies.start("spread")
-    copies.wait("h3", "pre2", "spread")
+    copies.start(N.spread)
+    copies.wait(N.h3, N.pre2, N.spread)
+
+
+def part(r, at, *fields):
+    bit = r.bits[0] == 1
+    for k, field in enumerate(fields):
+        half = field.shape[1] // 2
+        low, high = field[:, :half], field[:, half:]
+        r.mine[k, at : at + field.shape[0], :] = jnp.where(bit, high, low)
+        r.theirs[k, at : at + field.shape[0], :] = jnp.where(bit, low, high)
+
+
+def mine_of(r, row):
+    half = row.shape[1] // 2
+    return jnp.where(r.bits[0] == 1, row[:, half:], row[:, :half])
 
 
 def third_kernel(r, copies):
@@ -421,7 +443,7 @@
     for line in range(total):
         if line % (total // 2) == 0:
             k = line // (total // 2)
-            copies.wait(("pre2", k), ("prep", k), ("cotq", k))
+            copies.wait((N.pre2, k), (N.prep, k), (N.cotq, k))
         at = line * S
         shifted = slice(L + 1 + at, L + 1 + at + S)
         n2 = (r.pre2[at : at + S, :] - c2) * i2
@@ -434,30 +456,21 @@
         g = gelu_slope(v, t) * mask * r.cotq[at : at + S, :]
         r.grad[at : at + S, :] = g
         g = g * own
+        if L <= at < L + r.mine.shape[1]:
+            part(r, at - L, g, n2 * own, np_ * own)
         new = [column_sum(g * n2), column_sum(g), column_sum(g * np_)]
         sums = [a + b for a, b in zip(sums, new)]
         if (line + 1) % (total // 2) == 0:
-            copies.start(("grad", (line + 1) // (total // 2) - 1))
+            copies.start((N.grad, (line + 1) // (total // 2) - 1))
     row = jnp.concatenate(sums, axis=1)
     r.spread[...] = jnp.broadcast_to(row[None], r.spread.shape)
-    copies.start("spread")
+    copies.start(N.spread, N.mine, N.theirs)
     for i in range(rows):
         for g in range(groups):
             at = (i + 1) * L + g * S + 1
             r.out[g, i, :, :] = r.field[at : at + cols, :].astype(bf16)
-    copies.start("out")
-    copies.wait("grad", "out", "spread")
-
-
-def halves(r, source, at, frame, to, rows_w):
-    half = r.mine.shape[1]
-    bit = r.bits[0] == 1
-    for m0, m in chunks(rows_w, 96):
-        own = wide(r.ownp[frame + m0 : frame + m0 + m, :], half)
-        low = (source[at + m0 : at + m0 + m, :half] * own).astype(bf16)
-        high = (source[at + m0 : at + m0 + m, half:] * own).astype(bf16)
-        r.mine[to + m0 : to + m0 + m, :] = jnp.where(bit, high, low)
-        r.theirs[to + m0 : to + m0 + m, :] = jnp.where(bit, low, high)
+    copies.start(N.out)
+    copies.wait(N.grad, N.out, N.spread, N.mine, N.theirs)
 
 
 def fourth_kernel(r, copies):
@@ -470,12 +483,12 @@
     t3 = jnp.sum(r.tot3[...], axis=0)
     gg2, gs, ggp = (t3[:, k * width : (k + 1) * width] for k in range(3))
     r.gain_second[...], r.shift_second[...], r.gain_proj[...], r.shift_proj[...] = gg2, gs, ggp, gs
-    tiny = "gain_second", "shift_second", "gain_proj", "shift_proj"
+    tiny = N.gain_second, N.shift_second, N.gain_proj, N.shift_proj
     copies.start(*tiny)
     for m0, m in chunks(Q, L):
         if m0 in (0, 6 * L):
             k = m0 // (6 * L)
-            copies.wait(("grad", k), ("pre2", k), ("prep", k))
+            copies.wait((N.grad, k), (N.pre2, k), (N.prep, k))
         shifted = slice(L + 1 + m0, L + 1 + m0 + m)
         mask = wide(r.maskp[shifted, :], width) / n
         n2 = (r.pre2[m0 : m0 + m, :] - c2) * i2
@@ -484,13 +497,11 @@
         r.gq[m0 : m0 + m, :] = (r.gain2[...] * i2) * (g - mask * (gs + n2 * gg2))
         r.gpq[m0 : m0 + m, :] = (r.gainp[...] * ip) * (g - mask * (gs + np_ * ggp))
     r.gq[Q:, :] = jnp.zeros((r.gq.shape[0] - Q, width), f32)
-    copies.start("gq")
+    copies.start(N.gq)
     for m0, m in chunks(rows_w, 96):
         r.gpu[m0 : m0 + m, :] = r.gpq[L + 1 + m0 : L + 1 + m0 + m, :].astype(bf16)
-    copies.start("gpu")
-    halves(r, r.gq, L, 2 * L + 1, 0, rows_w)
-    halves(r, r.gpq, L - 1, 2 * L, rows_w, rows_w)
-    copies.wait("gpu", "gq", *tiny)
+    copies.start(N.gpu)
+    copies.wait(N.gpu, N.gq, *tiny)
 
 
 def hidden_kernel(r, copies):
@@ -498,13 +509,13 @@
     Q = r.gq.shape[0] - 8
     L = (r.keep.shape[0] - Q) // 2
     center, inv = r.mom1[0:1, :], r.mom1[1:2, :]
-    copies.wait("gq")
+    copies.wait(N.gq)
     for m0, m in chunks(Q, 176):
         for b in range(3):
             r.g3[m0 : m0 + m, b * width : (b + 1) * width] = r.gq[m0 + b : m0 + b + m, :].astype(bf16)
     U = r.act.shape[0]
     for a in range(3):
-        copies.wait(("w2", a))
+        copies.wait((N.w2, a))
         gh = jnp.zeros((U, width), f32)
         for b in range(3):
             gh += matmul_nt(
@@ -512,7 +523,7 @@
                 r.w2[2 - a, (2 - b) * width : (3 - b) * width, :],
             )
         r.act[...] = gh if a == 0 else r.act[...] + gh
-    copies.wait("keep")
+    copies.wait(N.keep)
     sums = [jnp.zeros((1, width), f32)] * 2
     for k, (m0, m) in enumerate(chunks(U, L)):
         frame = slice(2 * L + 2 + m0, 2 * L + 2 + m0 + m)
@@ -523,13 +534,16 @@
         r.act[m0 : m0 + m, :] = g
         r.normed[m0 : m0 + m, :] = n1 * mask
         if k % 3 == 2:
-            copies.start(("act", k // 3), ("normed", k // 3))
-        g = g * wide(r.ownp[frame, :], width)
+            copies.start((N.act, k // 3), (N.normed, k // 3))
+        own = wide(r.ownp[frame, :], width)
+        g = g * own
+        if m0 < r.mine.shape[1]:
+            part(r, m0, g, n1 * own)
         sums = [sums[0] + column_sum(g * n1), sums[1] + column_sum(g)]
     row = jnp.concatenate(sums, axis=1)
     r.spread[...] = jnp.broadcast_to(row[None], r.spread.shape)
-    copies.start("spread")
-    copies.wait("act", "normed", "spread")
+    copies.start(N.spread, N.mine, N.theirs)
+    copies.wait(N.act, N.normed, N.spread, N.mine, N.theirs)
 
 
 def split_store(r, rows, unit, first):
@@ -545,12 +559,30 @@
 def weights_second_kernel(r, copies):
     width = r.h3.shape[1] // 3
     cin = r.xe.shape[1] // 3
-    rows_w = r.near.shape[0] // 2
+    rows_w = r.mine.shape[1]
     L = (r.h3.shape[0] - rows_w) // 5
     per = width // cin
+    t3 = jnp.sum(r.tot3[...], axis=0)
+    n = mine_of(r, r.mom1[2:3, :])
+    gg2, gs, ggp = (mine_of(r, t3[:, k * width : (k + 1) * width]) / n for k in range(3))
+    scale2, scalep = mine_of(r, r.gain2[...] * r.mom2[1:2, :]), mine_of(r, r.gainp[...] * r.mom2[3:4, :])
+    half = scale2.shape[1]
+    for source, name, own, out in ((r.mine, N.mine, r.ownp, r.near), (r.far3, N.far3, r.ownp_far, r.far)):
+        copies.wait(name)
+        r.pad[:, 0:8, :] = jnp.zeros((3, 8, half), f32)
+        r.pad[:, 8:, :] = source[...]
+        for m0, m in chunks(rows_w, 96):
+            mask = wide(own[2 * L + 1 + m0 : 2 * L + 1 + m0 + m, :], half)
+            rows = slice(8 + m0, 8 + m0 + m)
+            back = mask * gs + r.pad[1, rows, :] * gg2
+            out[m0 : m0 + m, :] = (scale2 * (r.pad[0, rows, :] - back)).astype(bf16)
+            mask = wide(own[2 * L + m0 : 2 * L + m0 + m, :], half)
+            rows = slice(7 + m0, 7 + m0 + m)
+            back = mask * gs + r.pad[2, rows, :] * ggp
+            out[rows_w + m0 : rows_w + m0 + m, :] = (scalep * (r.pad[0, rows, :] - back)).astype(bf16)
     for b in range(3):
         lanes = slice(b * width, (b + 1) * width)
-        copies.wait(("h3", b), ("h3_far", b))
+        copies.wait((N.h3, b), (N.h3_far, b))
         for a in range(3):
             at = L * a + L
             r.acc[...] = matmul_tn(r.h3[at : at + rows_w, lanes], r.near[:rows_w, :]) + matmul_tn(
@@ -559,7 +591,7 @@
             split_store(r, width, cin, (3 * b + a) * per)
         copies.start(*((name, b) for name in CHUNKS))
     at = 2 * L
-    copies.wait("xe", "xe_far")
+    copies.wait(N.xe, N.xe_far)
     middle = slice(cin, 2 * cin)
     r.acc[0:cin, :] = matmul_tn(r.xe[at : at + rows_w, middle], r.near[rows_w:, :]) + matmul_tn(
         r.xe_far[at : at + rows_w, middle], r.far[rows_w:, :]
@@ -584,27 +616,31 @@
         r.gf[8 + m0 : 8 + m0 + m, :] = scale * (r.act[m0 : m0 + m, :] - back)
 
 
-def fifth_kernel(r, copies):
+def weights_first_kernel(r, copies):
+    rows_w = r.mine.shape[1]
+    cin = r.xe.shape[1] // 3
+    L = (r.xe.shape[0] - rows_w) // 5
     width = r.gain.shape[1]
-    r.rows_w = r.mine.shape[0]
-    L = r.act.shape[0] - r.rows_w
     t4 = jnp.sum(r.tot4[...], axis=0)
     r.gain_first[...], r.shift_first[...] = t4[:, :width], t4[:, width:]
-    copies.start("gain_first", "shift_first")
-    copies.wait("act", "normed")
-    first_back(r, t4[:, :width], t4[:, width:], r.rows_w)
-    halves(r, r.gf, 6, 2 * L, 0, r.rows_w)
-    copies.wait("gain_first", "shift_first")
-
-
-def weights_first_kernel(r, copies):
-    rows_w = r.near.shape[0]
-    cin = r.xe.shape[1] // 3
-    L = (r.xe.shape[0] - rows_w) // 5
-    copies.wait("xe", "xe_far")
+    copies.start(N.gain_first, N.shift_first)
+    n = mine_of(r, r.mom1[2:3, :])
+    gg, gs = mine_of(r, t4[:, :width]) / n, mine_of(r, t4[:, width:]) / n
+    scale = mine_of(r, r.gain[...] * r.mom1[1:2, :])
+    half = scale.shape[1]
+    for source, name, own, out in ((r.mine, N.mine, r.ownp, r.near), (r.far4, N.far4, r.ownp_far, r.far)):
+        copies.wait(name)
+        r.pad[:, 0:8, :] = jnp.zeros((2, 8, half), f32)
+        r.pad[:, 8:, :] = source[...]
+        for m0, m in chunks(rows_w, 96):
+            mask = wide(own[2 * L + m0 : 2 * L + m0 + m, :], half)
+            rows = slice(6 + m0, 6 + m0 + m)
+            back = mask * gs + r.pad[1, rows, :] * gg
+            out[m0 : m0 + m, :] = (scale * (r.pad[0, rows, :] - back)).astype(bf16)
+    copies.wait(N.xe, N.xe_far)
     for k, a in enumerate((1, 0, 2)):
         if k == 1:
-            copies.wait("xo", "xo_far")
+            copies.wait(N.xo, N.xo_far)
         source, source_far = (r.xe, r.xe_far) if a == 1 else (r.xo, r.xo_far)
         at = (3 if a == 2 else 2) * L
         for b in range(3):
@@ -614,7 +650,7 @@
             )
         split_store(r, 3 * cin, cin, a * 3)
         copies.start(*((name, a) for name in CHUNKS))
-    copies.wait(*CHUNKS)
+    copies.wait(N.gain_first, N.shift_first, *CHUNKS)
 
 
 def inputs_kernel(r, copies):
@@ -627,12 +663,12 @@
     lines = r.lines
     U = r.act.shape[0]
     r.rows_w = M
-    copies.wait("act", "normed")
+    copies.wait(N.act, N.normed)
     first_back(r, r.gg[...], r.gs[...], U)
     for m0, m in chunks(U, 144):
         r.gu[m0 : m0 + m, :width] = r.gf[8 + m0 : 8 + m0 + m, :].astype(bf16)
         r.gu[m0 : m0 + m, width:] = r.gf[9 + m0 : 9 + m0 + m, :].astype(bf16)
-    copies.wait("gpu", "w1", "wp")
+    copies.wait(N.gpu, N.w1, N.wp)
 
     def tap(m0, m, a, b):
         di, dj = (1 if a == 0 else 0), (1 if b == 0 else 0)
@@ -660,8 +696,8 @@
         for g in range(groups):
             for h in range(lines.shape[0]):
                 r.out[g, n, :, h * 128 : (h + 1) * 128] = lines[h, n * groups + g].astype(bf16)
-    copies.start("out")
-    copies.wait("out")
+    copies.start(N.out)
+    copies.wait(N.out)
 
 
 def widen(half, side, taps, per, swapped, into=None):
@@ -722,7 +758,7 @@
             to_send[t] = jnp.where(bit, low, high).astype(bf16)
             to_keep[t] = jnp.where(bit, high, low)
         copies.start(f"sent{p}", f"left{p}")
-    copies.wait(*(name for name in copies.jobs if name[:4] in ("sent", "left")))
+    copies.wait(*(name for name in copies.jobs if name[:4] in (N.sent, N.left)))
 
 
 def halve(bits, pairs, steps, cost):
@@ -734,15 +770,15 @@
     names = [str(p) for p in range(len(pairs))]
     outs = {}
     for name in names:
-        outs["sent" + name], outs["left" + name] = shape(dims, bf16), shape(dims)
+        outs[N.sent + name], outs[N.left + name] = shape(dims, bf16), shape(dims)
 
     def body(r, copies):
         r.count, r.steps = len(pairs), steps
         halve_kernel(r, copies)
 
-    far_in = tuple(n for n in ins if n != "bits")
-    out = call(body, ins, outs, far_in=far_in, far_out=tuple(outs), smem=("bits",), cost=cost, limit=60)
-    return [(out["sent" + name], out["left" + name]) for name in names]
+    far_in = tuple(n for n in ins if n != N.bits)
+    out = call(body, ins, outs, far_in=far_in, far_out=tuple(outs), smem=(N.bits,), cost=cost, limit=60)
+    return [(out[N.sent + name], out[N.left + name]) for name in names]
 
 
 def shifted(value, axis, steps):
@@ -790,29 +826,29 @@
         self.sent_a, self.kept_a, self.sent_b, self.kept_b = parts
         self.a, self.b, self.rest, self.core = plane, plane[::-1], rest, core
         p, n = len(plane), len(rest)
-        self.stages = [("plane", k) for k in range(p)] + [("rest", k) for k in range(n)]
-        self.stages += [("rest_join", k) for k in reversed(range(n))] + [("plane_join", k) for k in reversed(range(p))]
-        self.stages += [("core", 0)]
+        self.stages = [(N.plane, k) for k in range(p)] + [(N.rest, k) for k in range(n)]
+        self.stages += [(N.rest_join, k) for k in reversed(range(n))] + [(N.plane_join, k) for k in reversed(range(p))]
+        self.stages += [(N.core, 0)]
 
     def next(self):
         return self.stages[0] if self.stages else None
 
     def start(self):
         kind, k = self.stages[0]
-        if kind == "plane":
+        if kind == N.plane:
             self.got = partner(self.sent_a, *self.a[k]), partner(self.sent_b, *self.b[k])
-        elif kind == "rest":
+        elif kind == N.rest:
             self.got = (partner(self.sent, *self.rest[k]),)
-        elif kind == "rest_join":
+        elif kind == N.rest_join:
             self.got = (partner(self.value, *self.rest[k]),)
-        elif kind == "plane_join":
+        elif kind == N.plane_join:
             self.got = partner(self.value_a, *self.a[k]), partner(self.value_b, *self.b[k])
         else:
             self.got = (partner(self.value, *self.core),)
 
     def finish(self, cost=0):
         kind, k = self.stages.pop(0)
-        if kind == "plane":
+        if kind == N.plane:
             pairs = [(self.kept_a, self.got[0]), (self.kept_b, self.got[1])]
             nexts = [order[k + 1] for order in (self.a, self.b) if k + 1 < len(order)]
             if nexts and cost:
@@ -826,12 +862,12 @@
             else:
                 self.taps = total_a.shape[0]
                 self.split_rest(jnp.concatenate([total_a, total_b], axis=0), 0)
-        elif kind == "rest":
+        elif kind == N.rest:
             self.split_rest(self.kept + self.got[0].astype(f32), k + 1)
-        elif kind == "rest_join":
+        elif kind == N.rest_join:
             self.value = joined(self.value, self.got[0], *self.rest[k])
             self.value_a, self.value_b = self.value[: self.taps], self.value[self.taps :]
-        elif kind == "plane_join":
+        elif kind == N.plane_join:
             self.value_a = joined(self.value_a, self.got[0], *self.a[k])
             self.value_b = joined(self.value_b, self.got[1], *self.b[k])
             self.value = jnp.concatenate([self.value_a, self.value_b], axis=1)
@@ -860,10 +896,10 @@
     half = width // 2
     S = cols + 8
     L = groups * S
-    devices = lax.axis_size("rows") * lax.axis_size("cols") * lax.axis_size("grp")
-    plane = steps_of("cols")
-    core = steps_of("rows")[0]
-    rest = steps_of("rows")[1:] + steps_of("grp")
+    devices = lax.axis_size(N.rows) * lax.axis_size(N.cols) * lax.axis_size(N.grp)
+    plane = steps_of(N.cols)
+    core = steps_of(N.rows)[0]
+    rest = steps_of(N.rows)[1:] + steps_of(N.grp)
     bits = jnp.stack([bit_of(*step) for step in (core, *plane, *rest)]).astype(jnp.int32)
     w1 = w_first.reshape(3, 3 * cin, width)
     w2 = w_second.reshape(3, 3 * width, width)
@@ -877,23 +913,23 @@
         as_row, (gain_first, shift_first, gain_second, shift_second, gain_proj, shift_proj)
     )
 
-    top1 = shifted(inputs[:, -1:], "rows", 1)
-    me, count = lax.axis_index("rows"), lax.axis_size("rows")
+    top1 = shifted(inputs[:, -1:], N.rows, 1)
+    me, count = lax.axis_index(N.rows), lax.axis_size(N.rows)
     flags = jnp.stack([me > 0, me < count - 1]).astype(jnp.int32)
     flat_rows = shape((over * groups * cols_in + (width // 256 + 1) * rim * groups * cols, 256), bf16)
     packed = call(
         vertical_kernel,
         dict(flags=flags, x=inputs, cot=cotangent, own=own),
         dict(down=flat_rows) if count == 2 else dict(down=flat_rows, up=flat_rows),
-        far_in=("x", "cot"),
-        smem=("flags",),
+        far_in=(N.x, N.cot),
+        smem=(N.flags,),
         parts=dict(x=end_parts(rows_in, over), cot=end_parts(rows, rim)),
     )
     if count == 2:
         top = bot = lax.ppermute(packed["down"], "rows", [(0, 1), (1, 0)])
     else:
-        top, bot = shifted(packed["down"], "rows", 1), shifted(packed["up"], "rows", -1)
-    lft1 = shifted(jnp.concatenate([top1[:, :, -1:], inputs[:, :, -1:]], axis=1), "cols", 1)
+        top, bot = shifted(packed[N.down], N.rows, 1), shifted(packed[N.up], N.rows, -1)
+    lft1 = shifted(jnp.concatenate([top1[:, :, -1:], inputs[:, :, -1:]], axis=1), N.cols, 1)
     (top, bot), lft1 = lax.optimization_barrier(((top, bot), lft1))
     lines = (rows_in + 2 * over) * groups, (rows + 2 * rim) * groups, (rows + 3) * groups
     n_strip = over * lines[0] + (rim + 1) // 2 * lines[1] + width // 128 * lines[2]
@@ -909,10 +945,10 @@
             raw_c=pltpu.VMEM((width // 128, lines[2] * cols, 128), f32),
             flat=pltpu.VMEM((n_strip, 256), f32),
         ),
-        smem=("flags",),
-    )
-    lft, rgt = shifted(strips["right"], "cols", 1), shifted(strips["left"], "cols", -1)
-    lft1, _ = lax.optimization_barrier((lft1, strips["right"]))
+        smem=(N.flags,),
+    )
+    lft, rgt = shifted(strips[N.right], N.cols, 1), shifted(strips[N.left], N.cols, -1)
+    lft1, _ = lax.optimization_barrier((lft1, strips[N.right]))
     stats = call(
         stats_kernel,
         dict(x=inputs, top=top1, lft=lft1, own=own, w1=w1, wp=w_proj),
@@ -922,9 +958,9 @@
             xe=pltpu.VMEM((rows * groups * cols, 3 * cin), bf16),
             xo=pltpu.VMEM(((rows + 1) * groups * cols, 3 * cin), bf16),
         ),
-        far_out=("spread",),
-    )
-    tot1 = gather_sum(stats["spread"])
+        far_out=(N.spread,),
+    )
+    tot1 = gather_sum(stats[N.spread])
 
     first = call(
         first_kernel,
@@ -944,59 +980,93 @@
             raw_c=pltpu.VMEM((width // 128, lines[2] * (cols + 16), 128), f32),
             flat=pltpu.VMEM((n_strip, 256), f32),
         ),
-        far_in=("w1", "wp"),
-        far_out=("xe", "xo", "pre1", "prep", "cotq"),
-        smem=("flags",),
+        far_in=(N.w1, N.wp),
+        far_out=(N.xe, N.xo, N.pre1, N.prep, N.cotq),
+        smem=(N.flags,),
         cost=20000000000,
         parts=dict(pre1=row_parts(MP, 3), prep=row_parts(MP, 3)),
     )
-    xe, xo, ownp, maskp = first["xe"], first["xo"], first["ownp"], first["maskp"]
-    far_xe, far_xo = partner(xe, *core), partner(xo, *core)
+    xe, xo, ownp, maskp = first[N.xe], first[N.xo], first[N.ownp], first[N.maskp]
+    far_xe, far_xo, ownp_far = partner(xe, *core), partner(xo, *core), partner(ownp, *core)
 
     second = call(
         second_kernel,
-        dict(pre1=first["pre1"], tot1=tot1, gain=g1, shift=b1, maskp=maskp, ownp=ownp, w2=w2),
+        dict(pre1=first[N.pre1], tot1=tot1, gain=g1, shift=b1, maskp=maskp, ownp=ownp, w2=w2),
         dict(h3=shape((MP, 3 * width), bf16), pre2=shape((MQ, width)), spread=all_devices(2 * width), mom1=shape((8, width))),
         dict(hid=pltpu.VMEM((MP + 8, width), f32)),
-        far_in=("pre1", "w2"),
-        far_out=("h3", "pre2", "spread"),
+        far_in=(N.pre1, N.w2),
+        far_out=(N.h3, N.pre2, N.spread),
         parts=dict(pre2=row_parts(MQ, 3)),
     )
-    h3, pre2, mom1 = second["h3"], second["pre2"], second["mom1"]
-    tot2 = gather_sum(second["spread"])
+    h3, pre2, mom1 = second[N.h3], second[N.pre2], second[N.mom1]
+    tot2 = gather_sum(second[N.spread])
     far_h3 = partner(h3, *core)
 
     third = call(
         third_kernel,
         dict(
-            pre2=pre2, prep=first["prep"], mom1=mom1, tot2=tot2, gain2=g2, shift2=b2, gainp=gp, shiftp=bp,
-            maskp=maskp, ownp=ownp, cotq=first["cotq"],
+            bits=bits, pre2=pre2, prep=first[N.prep], mom1=mom1, tot2=tot2, gain2=g2, shift2=b2, gainp=gp, shiftp=bp,
+            maskp=maskp, ownp=ownp, cotq=first[N.cotq],
         ),
         dict(
             out=shape((groups, rows, cols, width), bf16),
             grad=shape((MQ, width)),
             spread=all_devices(3 * width),
             mom2=shape((8, width)),
+            mine=shape((3, MW, half)),
+            theirs=shape((3, MW, half)),
         ),
         dict(field=pltpu.VMEM((MQ, width), f32)),
-        far_in=("pre2", "prep", "cotq"),
-        far_out=("grad", "spread", "out"),
+        far_in=(N.pre2, N.prep, N.cotq),
+        far_out=(N.grad, N.spread, N.mine, N.theirs, N.out),
+        smem=(N.bits,),
         parts=dict(
             grad=row_parts(MQ, 2), pre2=row_parts(MQ, 2), cotq=row_parts(MQ, 2), prep=cuts(L, L + MQ // 2 + 8, L + MQ + 8)
         ),
     )
-    mom2 = third["mom2"]
-    tot3 = gather_sum(third["spread"])
-
+    mom2 = third[N.mom2]
+    tot3 = gather_sum(third[N.spread])
+
+    def chunk_shapes(taps):
+        dims = (taps, cin // 4, half)
+        return dict(sent_a=shape(dims, bf16), kept_a=shape(dims), sent_b=shape(dims, bf16), kept_b=shape(dims))
+
+    per = width // cin
+    taps2 = 9 * per + 1
+    second_parts = call(
+        weights_second_kernel,
+        dict(
+            bits=bits, mine=third[N.mine], far3=partner(third[N.theirs], *core), h3=h3, h3_far=far_h3, xe=xe, xe_far=far_xe,
+            tot3=tot3, mom1=mom1, mom2=mom2, gain2=g2, gainp=gp, ownp=ownp, ownp_far=ownp_far,
+        ),
+        chunk_shapes(taps2),
+        dict(
+            acc=pltpu.VMEM((width, half), f32),
+            pad=pltpu.VMEM((3, MW + 8, half), f32),
+            near=pltpu.VMEM((2 * MW, half), bf16),
+            far=pltpu.VMEM((2 * MW, half), bf16),
+        ),
+        far_in=(N.mine, N.far3, N.h3, N.h3_far, N.xe, N.xe_far),
+        far_out=CHUNKS,
+        smem=(N.bits,),
+        parts=dict(
+            h3=lane_parts(3 * width, 3, pl.ds(L, MW + 2 * L)),
+            h3_far=lane_parts(3 * width, 3, pl.ds(L, MW + 2 * L)),
+            xe=[(0, (pl.ds(2 * L, MW), pl.ds(cin, cin)))],
+            xe_far=[(0, (pl.ds(2 * L, MW), pl.ds(cin, cin)))],
+            **{name: row_parts(taps2 - 1, 3) + [(3, (pl.ds(taps2 - 1, 1),))] for name in CHUNKS},
+        ),
+    ).values()
+    grad, *second_parts = lax.optimization_barrier((third[N.grad], *second_parts))
+    tree2 = Tree(second_parts, bits, plane, rest, core)
+    tree2.start()
     fourth = call(
         fourth_kernel,
         dict(
-            bits=bits, pre2=pre2, prep=first["prep"], mom1=mom1, mom2=mom2, tot3=tot3, gain2=g2, gainp=gp,
-            grad=third["grad"], maskp=maskp, ownp=ownp,
-        ),
-        dict(
-            mine=shape((2 * MW, half), bf16),
-            theirs=shape((2 * MW, half), bf16),
+            pre2=pre2, prep=first[N.prep], mom1=mom1, mom2=mom2, tot3=tot3, gain2=g2, gainp=gp,
+            grad=grad, maskp=maskp, ownp=ownp,
+        ),
+        dict(
             gq=shape((MQ + 8, width)),
             gpu=shape((MW, width), bf16),
             gain_second=vec(1),
@@ -1005,46 +1075,22 @@
             shift_proj=vec(1),
         ),
         dict(gpq=pltpu.VMEM((MQ, width), f32)),
-        far_in=("pre2", "prep", "grad"),
-        far_out=("gpu", "gq", "gain_second", "shift_second", "gain_proj", "shift_proj"),
+        far_in=(N.pre2, N.prep, N.grad),
+        far_out=(N.gpu, N.gq, N.gain_second, N.shift_second, N.gain_proj, N.shift_proj),
         parts=dict(grad=cuts(0, 6 * L, MQ), pre2=cuts(0, 6 * L, MQ), prep=cuts(L, 7 * L + 8, L + MQ + 8)),
-        smem=("bits",),
-    )
-    far2 = partner(fourth["theirs"], *core)
-
-    def chunk_shapes(taps):
-        dims = (taps, cin // 4, half)
-        return dict(sent_a=shape(dims, bf16), kept_a=shape(dims), sent_b=shape(dims, bf16), kept_b=shape(dims))
-
-    per = width // cin
-    taps2 = 9 * per + 1
-    second_parts = call(
-        weights_second_kernel,
-        dict(bits=bits, h3=h3, h3_far=far_h3, xe=xe, xe_far=far_xe, near=fourth["mine"], far=far2),
-        chunk_shapes(taps2),
-        dict(acc=pltpu.VMEM((width, half), f32)),
-        far_in=("h3", "h3_far", "xe", "xe_far"),
-        far_out=CHUNKS,
-        smem=("bits",),
-        parts=dict(
-            h3=lane_parts(3 * width, 3, pl.ds(L, MW + 2 * L)),
-            h3_far=lane_parts(3 * width, 3, pl.ds(L, MW + 2 * L)),
-            xe=[(0, (pl.ds(2 * L, MW), pl.ds(cin, cin)))],
-            xe_far=[(0, (pl.ds(2 * L, MW), pl.ds(cin, cin)))],
-            **{name: row_parts(taps2 - 1, 3) + [(3, (pl.ds(taps2 - 1, 1),))] for name in CHUNKS},
-        ),
-    ).values()
-    gq, *second_parts = lax.optimization_barrier((fourth["gq"], *second_parts))
-
-    tree2 = Tree(second_parts, bits, plane, rest, core)
-    tree2.start()
+    )
     hidden = call(
         hidden_kernel,
-        dict(gq=gq, w2=w2, keep=first["pre1"], mom1=mom1, gain=g1, shift=b1, maskp=maskp, ownp=ownp),
-        dict(act=shape((MU, width)), normed=shape((MU, width)), spread=all_devices(2 * width)),
+        dict(bits=bits, gq=fourth[N.gq], w2=w2, keep=first[N.pre1], mom1=mom1, gain=g1, shift=b1, maskp=maskp, ownp=ownp),
+        dict(
+            act=shape((MU, width)), normed=shape((MU, width)), spread=all_devices(2 * width),
+            mine=shape((2, MW, half)), theirs=shape((2, MW, half)),
+        ),
         dict(g3=pltpu.VMEM((MQ, 3 * width), bf16)),
-        far_in=("gq", "w2", "keep"),
-        far_out=("act", "normed", "spread"),
+        far_in=(N.gq, N.w2, N.keep),
+        far_out=(N.act, N.normed, N.spread, N.mine, N.theirs),
+        smem=(N.bits,),
+        limit=60,
         parts=dict(
             w2=[(k, (pl.ds(2 - k, 1),)) for k in range(3)],
             keep=cuts(2 * L, 2 * L + MU + 8),
@@ -1052,29 +1098,27 @@
             normed=row_parts(MU, 3),
         ),
     )
-    tot4 = gather_sum(hidden["spread"])
+    tot4 = gather_sum(hidden[N.spread])
     tree2.finish(20000000000)
-    act, tree2.sent_a, tree2.sent_b = lax.optimization_barrier((hidden["act"], tree2.sent_a, tree2.sent_b))
+    near1, tree2.sent_a, tree2.sent_b = lax.optimization_barrier((hidden[N.mine], tree2.sent_a, tree2.sent_b))
     tree2.start()
     fifth = call(
-        fifth_kernel,
-        dict(bits=bits, act=act, normed=hidden["normed"], mom1=mom1, tot4=tot4, gain=g1, maskp=maskp, ownp=ownp),
-        dict(mine=shape((MW, half), bf16), theirs=shape((MW, half), bf16), gain_first=vec(1), shift_first=vec(1)),
-        dict(gf=pltpu.VMEM((MU + 16, width), f32)),
-        far_in=("act", "normed"),
-        far_out=("gain_first", "shift_first"),
-        smem=("bits",),
-        parts=dict(act=cuts(0, MW), normed=cuts(0, MW)),
-    )
-    far1 = partner(fifth["theirs"], *core)
-    first_parts = call(
         weights_first_kernel,
-        dict(bits=bits, xe=xe, xo=xo, xe_far=far_xe, xo_far=far_xo, near=fifth["mine"], far=far1),
-        chunk_shapes(9),
-        dict(acc=pltpu.VMEM((3 * cin, half), f32)),
-        far_in=("xe", "xe_far", "xo", "xo_far"),
-        far_out=CHUNKS,
-        smem=("bits",),
+        dict(
+            bits=bits, mine=near1, far4=partner(hidden[N.theirs], *core), xe=xe, xe_far=far_xe, xo=xo, xo_far=far_xo,
+            tot4=tot4, mom1=mom1, gain=g1, ownp=ownp, ownp_far=ownp_far,
+        ),
+        dict(**chunk_shapes(9), gain_first=vec(1), shift_first=vec(1)),
+        dict(
+            acc=pltpu.VMEM((3 * cin, half), f32),
+            pad=pltpu.VMEM((2, MW + 8, half), f32),
+            near=pltpu.VMEM((MW, half), bf16),
+            far=pltpu.VMEM((MW, half), bf16),
+        ),
+        far_in=(N.mine, N.far4, N.xe, N.xe_far, N.xo, N.xo_far),
+        cost=20000000000,
+        far_out=(*CHUNKS, N.gain_first, N.shift_first),
+        smem=(N.bits,),
         parts=dict(
             xe=cuts(2 * L, 2 * L + MW),
             xe_far=cuts(2 * L, 2 * L + MW),
@@ -1082,7 +1126,8 @@
             xo_far=cuts(2 * L, 3 * L + MW),
             **{name: row_parts(9, 3) for name in CHUNKS},
         ),
-    ).values()
+    )
+    first_parts = [fifth[name] for name in CHUNKS]
     tree2.got, *first_parts = lax.optimization_barrier((tree2.got, *first_parts))
     tree2.finish()
     tree1 = Tree(first_parts, bits, plane, rest, core)
@@ -1090,8 +1135,8 @@
     grad_inputs = call(
         inputs_kernel,
         dict(
-            act=act, normed=hidden["normed"], gpu=fourth["gpu"], w1=w1, wp=w_proj, mom1=mom1, gain=g1, maskp=maskp,
-            gg=fifth["gain_first"], gs=fifth["shift_first"],
+            act=hidden[N.act], normed=hidden[N.normed], gpu=fourth[N.gpu], w1=w1, wp=w_proj, mom1=mom1, gain=g1, maskp=maskp,
+            gg=fifth[N.gain_first], gs=fifth[N.shift_first],
         ),
         dict(out=shape((groups, rows_in, cols_in, cin), bf16)),
         dict(
@@ -1099,18 +1144,18 @@
             gf=pltpu.VMEM((MU + 16, width), f32),
             gu=pltpu.VMEM((MU, 2 * width), bf16),
         ),
-        far_in=("act", "normed", "gpu", "w1", "wp"),
-        far_out=("out",),
+        far_in=(N.act, N.normed, N.gpu, N.w1, N.wp),
+        far_out=(N.out,),
         cost=10000000000,
-    )["out"]
+    )[N.out]
     side = bit_of(*core).astype(jnp.int32)
     grad_inputs = lockstep(tree2, tree1, beside=grad_inputs)
-    while tree2.next() != ("plane_join", 0):
+    while tree2.next() != (N.plane_join, 0):
         lockstep(tree2, tree1)
     tree2.start()
-    while tree1.next() != ("plane_join", 0):
+    while tree1.next() != (N.plane_join, 0):
         tree1.start()
-        if tree1.next() != ("plane_join", 1):
+        if tree1.next() != (N.plane_join, 1):
             tree1.finish()
         else:
             tree1.got, tree2.got = lax.optimization_barrier((tree1.got, tree2.got))
@@ -1126,17 +1171,17 @@
     (grad_w1,) = widen(tree1.got[0], 1 - side, 3, 3, False, widen(tree1.value, side, 3, 3, False))
 
     return (
-        third["out"],
+        third[N.out],
         grad_inputs,
         grad_w1.reshape(w_first.shape),
-        fifth["gain_first"].reshape(width),
-        fifth["shift_first"].reshape(width),
+        fifth[N.gain_first].reshape(width),
+        fifth[N.shift_first].reshape(width),
         grad_w2.reshape(w_second.shape),
-        fourth["gain_second"].reshape(width),
-        fourth["shift_second"].reshape(width),
+        fourth[N.gain_second].reshape(width),
+        fourth[N.shift_second].reshape(width),
         grad_wp.reshape(w_proj.shape),
-        fourth["gain_proj"].reshape(width),
-        fourth["shift_proj"].reshape(width),
+        fourth[N.gain_proj].reshape(width),
+        fourth[N.shift_proj].reshape(width),
     )
 
 

time: 213 us -> 209 us (0.981)
  waiting for transfers between devices: 76.9 us -> 59.2 us
  starting transfers between devices: 54.8 us -> 64 us
    ppermute x31 -> x32, waiting for transfers between devices: 52.4 us -> 36 us  [partner(): return lax.ppermute(value, axis, [(i, i ^ step) for i in range(count)])]
    ppermute x31 -> x32, starting transfers between devices: 25.2 us -> 34.5 us  [partner(): return lax.ppermute(value, axis, [(i, i ^ step) for i in range(count)])]
    pallas_call x13 -> x12, Pallas kernels: 58.7 us -> 60.4 us  [call(): pl.pallas_call(run, out_shape=list(outs.values()), in_specs=[spec(n) for...]
  transfers between devices with their start and end apart: 40 -> 41, of which waited for: 25 -> 21; matrix products, arithmetic and copies ran while one was open for 1% -> 1% of each run, Pallas kernels for 24% -> 25%
where the time goes in v5:
time: 209 us; the launch traced here: 208 us
  Pallas kernels  70.7 us (34%)
  starting transfers between devices  64 us (31%)
  waiting for transfers between devices  59.2 us (28%)
  other arithmetic  7.84 us (4%)
  local copies, waits for them, and re-layouts  4.25 us (2%)
    pallas_call x12, Pallas kernels, call(): pl.pallas_call(run, out_shape=list(outs.values()), in_specs=[spec(n) for...  60.4 us
    ppermute x32, waiting for transfers between devices, partner(): return lax.ppermute(value, axis, [(i, i ^ step) for i in range(count)])  36 us
    ppermute x32, starting transfers between devices, partner(): return lax.ppermute(value, axis, [(i, i ^ step) for i in range(count)])  34.5 us
    all_to_all x4, waiting for transfers between devices, gather_sum(): return lax.all_to_all(spread, axes, 0, 0)  20.8 us
    all_to_all x4, starting transfers between devices, gather_sum(): return lax.all_to_all(spread, axes, 0, 0)  16.7 us
    ppermute x4, starting transfers between devices, shifted(): lax.ppermute(value, axis, [(source, source + steps) for source in range(f...  12.3 us
    pallas_call x4, Pallas kernels, widen(): pl.pallas_call(body, out_shape=[shape((taps * per, n, 2 * m))] + [shape((...  10.3 us
  transfers between devices with their start and end apart: 41, of which 21 were waited for; matrix products, arithmetic and copies ran while one was open for 1% of the time, Pallas kernels for 25%

profile of v5, /device:TPU:0, one launch (start us, length us, event | category | flops | bytes accessed | tf_op | source)
XLA Modules:
  0.0 207.7 jit_solution(15266613448648787659)
XLA Ops:
  5.1 2.0 collective-permute-start.1
  7.9 4.8 %collective-permute-start.2 = (bf16[2,17,1,256]{3,2,1,0:T(2,128)(2,1)S(1)}, bf16[2,17,1,256]{3,2,1,0:T(2,128)(2,1)S(1)}, u32[]{:S(2)}, u32[]{:S(2)}) collective-permute-start(bf16[2,17,1,256]{3,2,1,0:T(2,128)(2,1)S(1)} %pad_maximum_fusion.12), channel_id=1, source_target_pairs={{0,4},{4,8},{8,12},{1,5},{5,9},{9,13},{2,6},{6,10},{10,14},{3,7},{... | collective-permute-start | bytes 52232 | tf_op jit(solution)/shard_map/ppermute | solution.py:787
  12.8 1.6 collective-permute-done.2.refs_2_
  15.7 4.2 %collective-permute-start.3 = (bf16[480,256]{1,0:T(8,128)(2,1)S(1)}, bf16[480,256]{1,0:T(8,128)(2,1)S(1)}, u32[]{:S(2)}, u32[]{:S(2)}) collective-permute-start(bf16[480,256]{1,0:T(8,128)(2,1)S(1)} %get-tuple-element.101), channel_id=1, source_target_pairs={{0,4},{4,8},{8,12},{1,5},{5,9},{9,13},{2,6},{6,10},{10,14},{3,7},{... | collective-permute-start | bytes 737288 | tf_op jit(solution)/shard_map/ppermute | solution.py:787
  19.9 1.3 collective-permute-start.4
  21.2 3.4 %shard_map.206 = f32[32,1,2176]{2,1,0:T(1,128)} custom-call(bf16[2,16,32,256]{3,2,1,0:T(8,128)(2,1)S(1)} %copy-done.3, bf16[2,1,32,256]{3,2,1,0:T(8,128)(2,1)S(1)} %collective-permute-done.1.refs_1_, bf16[2,17,1,256]{3,2,1,0:T(2,128)(2,1)S(1)} %collective-permute-done.2.refs_2_, bf16[2,8,16,128]{3,2,1,0:T(8,128)(2,1)S(1)} %broadcast_in_dim.2.refs_3_, ...), custom_call_target="tpu_custom_call" | custom-call | tf_op jit(solution)/shard_map/pallas_call | solution.py:108
  24.6 7.9 %all-to-all-start = ((f32[32,1,2176]{2,1,0:T(1,128)}), f32[32,1,2176]{2,1,0:T(1,128)S(1)}, u32[]{:S(2)}, u32[]{:S(2)}) async-start(f32[32,1,2176]{2,1,0:T(1,128)} %shard_map.206), calls=%async_computation | async-start | bytes 557056 | tf_op jit(solution)/shard_map/all_to_all | solution.py:791
  32.6 5.7 %shard_map.205 = (f32[624,512]{1,0:T(8,128)}, f32[624,512]{1,0:T(8,128)}, bf16[624,768]{1,0:T(8,128)(2,1)}, bf16[672,768]{1,0:T(8,128)(2,1)}, f32[624,128]{1,0:T...) custom-call(s32[2]{0:T(128)S(1)} %add_convert_fusion.2.refs_0_, bf16[2,16,32,256]{3,2,1,0:T(8,128)(2,1)} %refs_0_.1, ...), custom_call_target="tpu_custom_call" | custom-call | flops 20000000000 | tf_op jit(solution)/shard_map/pallas_call | solution.py:108
  38.3 5.5 %all-to-all-done.refs_1_ = f32[32,1,2176]{2,1,0:T(1,128)S(1)} async-done(((f32[32,1,2176]{2,1,0:T(1,128)}), f32[32,1,2176]{2,1,0:T(1,128)S(1)}, u32[]{:S(2)}, u32[]{:S(2)}) %all-to-all-start) | async-done | bytes 278560 | tf_op jit(solution)/shard_map/all_to_all | solution.py:791
  43.8 6.3 %shard_map.207 = (bf16[624,1536]{1,0:T(8,128)(2,1)}, f32[528,512]{1,0:T(8,128)}, f32[32,1,1024]{2,1,0:T(1,128)}, f32[8,512]{1,0:T(8,128)S(1)}) custom-call(f32[624,512]{1,0:T(8,128)} %get-tuple-element.103.refs_0_.refs_3_, f32[32,1,2176]{2,1,0:T(1,128)S(1)} %all-to-all-done.refs_1_, f32[1,512]{1,0:T(1,128)S(1)} %bitcast.34, f32[1,512]{1,0:T(1,128)S(1)} %bitcast.32, ...), custom_call_target="tpu_custom_call" | custom-call | tf_op jit(solution)/shard_map/pallas_call | solution.py:108
  50.2 2.6 %all-to-all-start.1 = ((f32[32,1,1024]{2,1,0:T(1,128)}), f32[32,1,1024]{2,1,0:T(1,128)S(1)}, u32[]{:S(2)}, u32[]{:S(2)}) async-start(f32[32,1,1024]{2,1,0:T(1,128)} %get-tuple-element.111), calls=%async_computation.1 | async-start | bytes 262144 | tf_op jit(solution)/shard_map/all_to_all | solution.py:791
  53.0 7.7 %all-to-all-done.1.refs_4_ = f32[32,1,1024]{2,1,0:T(1,128)S(1)} async-done(((f32[32,1,1024]{2,1,0:T(1,128)}), f32[32,1,1024]{2,1,0:T(1,128)S(1)}, u32[]{:S(2)}, u32[]{:S(2)}) %all-to-all-start.1) | async-done | bytes 131104 | tf_op jit(solution)/shard_map/all_to_all | solution.py:791
  60.7 5.8 %shard_map.208 = (bf16[2,8,16,512]{3,2,1,0:T(8,128)(2,1)}, f32[528,512]{1,0:T(8,128)}, f32[32,1,1536]{2,1,0:T(1,128)}, f32[8,512]{1,0:T(8,128)S(1)}, f32[3,384,256]{2,1,0:T(8,128)}, /*index=5*/f32[3,384,256]{2,1,0:T(8,128)}) custom-call(s32[5]{0:T(128)S(1)} %stack.32.refs_0_, f32[528,512]{1,0:T(8,128)} %get-tuple-element.108.refs_1_.refs_0_, ...), custom_call_target="tpu_custom_call" | custom-call | tf_op jit(solution)/shard_map/pallas_call | solution.py:108
  67.1 2.8 %all-to-all-start.2 = ((f32[32,1,1536]{2,1,0:T(1,128)}), f32[32,1,1536]{2,1,0:T(1,128)S(1)}, u32[]{:S(2)}, u32[]{:S(2)}) async-start(f32[32,1,1536]{2,1,0:T(1,128)} %get-tuple-element.119), calls=%async_computation.2 | async-start | bytes 393216 | tf_op jit(solution)/shard_map/all_to_all | solution.py:791
  70.0 1.6 collective-permute-done.8.refs_13_.refs_11_
  71.6 7.5 %all-to-all-done.2.refs_7_.refs_4_ = f32[32,1,1536]{2,1,0:T(1,128)S(1)} async-done(((f32[32,1,1536]{2,1,0:T(1,128)}), f32[32,1,1536]{2,1,0:T(1,128)S(1)}, u32[]{:S(2)}, u32[]{:S(2)}) %all-to-all-start.2) | async-done | bytes 196640 | tf_op jit(solution)/shard_map/all_to_all | solution.py:791
  80.2 8.4 %shard_map.209 = (bf16[19,64,256]{2,1,0:T(8,128)(2,1)S(1)}, f32[19,64,256]{2,1,0:T(8,128)}, bf16[19,64,256]{2,1,0:T(8,128)(2,1)}, f32[19,64,256]{2,1,0:T(8,128)}) custom-call(s32[5]{0:T(128)S(1)} %stack.32.refs_0_, f32[3,384,256]{2,1,0:T(8,128)} %get-tuple-element.115.refs_1_, f32[3,384,256]{2,1,0:T(8,128)} %copy-done.24, ...), custom_call_target="tpu_custom_call" | custom-call | tf_op jit(solution)/shard_map/pallas_call | solution.py:108
  89.8 3.2 %shard_map.211 = (f32[536,512]{1,0:T(8,128)}, bf16[384,512]{1,0:T(8,128)(2,1)S(1)}, f32[1,512]{1,0:T(1,128)}, f32[1,512]{1,0:T(1,128)}, f32[1,512]{1,0:T(1,128)}, /*index=5*/f32[1,512]{1,0:T(1,128)}) custom-call(f32[528,512]{1,0:T(8,128)} %get-tuple-element.108.refs_1_.refs_0_, f32[624,512]{1,0:T(8,128)} %get-tuple-element.109.refs_2_.refs_1_, ...), custom_call_target="tpu_custom_call" | custom-call | tf_op jit(solution)/shard_map/pallas_call | solution.py:108
  93.0 8.3 %shard_map.212 = (f32[432,512]{1,0:T(8,128)}, f32[432,512]{1,0:T(8,128)}, f32[32,1,1024]{2,1,0:T(1,128)}, f32[2,384,256]{2,1,0:T(8,128)}, f32[2,384,256]{2,1,0:T(8,128)}) custom-call(s32[5]{0:T(128)} %copy-done.17, f32[536,512]{1,0:T(8,128)} %get-tuple-element.131.refs_1_, bf16[3,1536,512]{2,1,0:T(8,128)(2,1)} %bitcast.42, ...), custom_call_target="tpu_custom_call" | custom-call | tf_op jit(solution)/shard_map/pallas_call | solution.py:108
  101.8 3.4 %all-to-all-start.3 = ((f32[32,1,1024]{2,1,0:T(1,128)}), f32[32,1,1024]{2,1,0:T(1,128)S(1)}, u32[]{:S(2)}, u32[]{:S(2)}) async-start(f32[32,1,1024]{2,1,0:T(1,128)} %get-tuple-element.140), calls=%async_computation.3 | async-start | bytes 262144 | tf_op jit(solution)/shard_map/all_to_all | solution.py:791
  106.2 3.8 %shard_map.210 = (bf16[19,32,256]{2,1,0:T(8,128)(2,1)}, f32[19,32,256]{2,1,0:T(8,128)}, bf16[19,32,256]{2,1,0:T(8,128)(2,1)}, f32[19,32,256]{2,1,0:T(8,128)}) custom-call(s32[5]{0:T(128)} %copy-done.17, f32[19,64,256]{2,1,0:T(8,128)} %get-tuple-element.125.refs_1_, bf16[19,64,256]{2,1,0:T(8,128)(2,1)} %collective-permute-done.9.refs_2_, ...), custom_call_target="tpu_custom_call" | custom-call | flops 20000000000 | tf_op jit(solution)/shard_map/pallas_call | solution.py:108
  110.0 1.6 collective-permute-start.11
  111.6 1.5 collective-permute-start.12
  113.1 6.9 %shard_map.213 = (bf16[9,64,256]{2,1,0:T(8,128)(2,1)S(1)}, f32[9,64,256]{2,1,0:T(8,128)S(1)}, bf16[9,64,256]{2,1,0:T(8,128)(2,1)S(1)}, f32[9,64,256]{2,1,0:T(8,1...) custom-call(s32[5]{0:T(128)S(1)} %copy-done.18, f32[2,384,256]{2,1,0:T(8,128)} %get-tuple-element.137.refs_1_, ...), custom_call_target="tpu_custom_call" | custom-call | flops 20000000000 | tf_op jit(solution)/shard_map/pallas_call | solution.py:108
  121.0 1.5 convert_add_fusion.1
  122.7 1.5 collective-permute-start.15
  124.3 1.5 collective-permute-start.16
  126.3 6.4 %shard_map.214 = bf16[2,16,32,256]{3,2,1,0:T(8,128)(2,1)} custom-call(f32[432,512]{1,0:T(8,128)S(1)} %copy-done.21, f32[432,512]{1,0:T(8,128)} %get-tuple-element.151.refs_1_, bf16[384,512]{1,0:T(8,128)(2,1)S(1)} %get-tuple-element.152.refs_2_, bf16[3,768,512]{2,1,0:T(8,128)(2,1)} %bitcast.47, bf16[256,512]{1,0:T(8,128)(2,1)S(1)} %copy-done.11, ...), custom_call_target="tpu_custom_call" | custom-call | flops 10000000000 | tf_op jit(solution)/shard_map/pallas_call | solution.py:108
  134.0 2.5 %collective-permute-start.18 = (bf16[38,8,256]{2,1,0:T(8,128)(2,1)S(1)}, bf16[38,8,256]{2,1,0:T(8,128)(2,1)S(1)}, u32[]{:S(2)}, u32[]{:S(2)}) collective-permute-start(bf16[38,8,256]{2,1,0:T(8,128)(2,1)S(1)} %select_convert_fusion.1), channel_id=1, source_target_pairs={{0,2},{1,3},{2,0},{3,1},{4,6},{5,7},{6,4},{7,5},{8,10},{9,11},{10,... | collective-permute-start | bytes 466952 | tf_op jit(solution)/shard_map/ppermute | solution.py:800
  138.4 3.4 %collective-permute-done.19 = bf16[9,32,256]{2,1,0:T(8,128)(2,1)S(1)} collective-permute-done((bf16[9,32,256]{2,1,0:T(8,128)(2,1)S(1)}, bf16[9,32,256]{2,1,0:T(8,128)(2,1)S(1)}, u32[]{:S(2)}, u32[]{:S(2)}) %collective-permute-start.19) | collective-permute-done | bytes 147488 | tf_op jit(solution)/shard_map/ppermute | solution.py:800
  143.0 4.5 %collective-permute-start.22 = (bf16[18,16,256]{2,1,0:T(8,128)(2,1)S(1)}, bf16[18,16,256]{2,1,0:T(8,128)(2,1)S(1)}, u32[]{:S(2)}, u32[]{:S(2)}) collective-permute-start(bf16[18,16,256]{2,1,0:T(8,128)(2,1)S(1)} %select_convert_fusion.2), channel_id=1, source_target_pairs={{0,1},{1,0},{2,3},{3,2},{4,5},{5,4},{6,7},{7,6},{8,9},{9,8},{10,11... | collective-permute-start | bytes 442376 | tf_op jit(solution)/shard_map/ppermute | solution.py:800
  147.6 5.5 %collective-permute-done.22 = bf16[18,16,256]{2,1,0:T(8,128)(2,1)S(1)} collective-permute-done((bf16[18,16,256]{2,1,0:T(8,128)(2,1)S(1)}, bf16[18,16,256]{2,1,0:T(8,128)(2,1)S(1)}, u32[]{:S(2)}, u32[]{:S(2)}) %collective-permute-start.22) | collective-permute-done | bytes 147488 | tf_op jit(solution)/shard_map/ppermute | solution.py:800
  154.5 2.5 %collective-permute-start.24 = (bf16[18,8,256]{2,1,0:T(8,128)(2,1)S(1)}, bf16[18,8,256]{2,1,0:T(8,128)(2,1)S(1)}, u32[]{:S(2)}, u32[]{:S(2)}) collective-permute-start(bf16[18,8,256]{2,1,0:T(8,128)(2,1)S(1)} %select_convert_fusion.5), channel_id=1, source_target_pairs={{0,2},{1,3},{2,0},{3,1},{4,6},{5,7},{6,4},{7,5},{8,10},{9,11},{10,... | collective-permute-start | bytes 221192 | tf_op jit(solution)/shard_map/ppermute | solution.py:800
  157.1 3.4 %collective-permute-done.24 = bf16[18,8,256]{2,1,0:T(8,128)(2,1)S(1)} collective-permute-done((bf16[18,8,256]{2,1,0:T(8,128)(2,1)S(1)}, bf16[18,8,256]{2,1,0:T(8,128)(2,1)S(1)}, u32[]{:S(2)}, u32[]{:S(2)}) %collective-permute-start.24) | collective-permute-done | bytes 73760 | tf_op jit(solution)/shard_map/ppermute | solution.py:800
  163.2 2.2 %collective-permute-start.27 = (bf16[18,8,256]{2,1,0:T(8,128)(2,1)S(1)}, bf16[18,8,256]{2,1,0:T(8,128)(2,1)S(1)}, u32[]{:S(2)}, u32[]{:S(2)}) collective-permute-start(bf16[18,8,256]{2,1,0:T(8,128)(2,1)S(1)} %add_convert_fusion.1), channel_id=1, source_target_pairs={{0,2},{1,3},{2,0},{3,1},{4,6},{5,7},{6,4},{7,5},{8,10},{9,11},{10,... | collective-permute-start | bytes 221192 | tf_op jit(solution)/shard_map/ppermute | solution.py:800
  165.4 3.1 %collective-permute-done.27 = bf16[18,8,256]{2,1,0:T(8,128)(2,1)S(1)} collective-permute-done((bf16[18,8,256]{2,1,0:T(8,128)(2,1)S(1)}, bf16[18,8,256]{2,1,0:T(8,128)(2,1)S(1)}, u32[]{:S(2)}, u32[]{:S(2)}) %collective-permute-start.27) | collective-permute-done | bytes 73760 | tf_op jit(solution)/shard_map/ppermute | solution.py:800
  168.5 3.7 %collective-permute-done.25 = bf16[19,32,256]{2,1,0:T(8,128)(2,1)S(1)} collective-permute-done((bf16[19,32,256]{2,1,0:T(8,128)(2,1)S(1)}, bf16[19,32,256]{2,1,0:T(8,128)(2,1)S(1)}, u32[]{:S(2)}, u32[]{:S(2)}) %collective-permute-start.25) | collective-permute-done | bytes 311328 | tf_op jit(solution)/shard_map/ppermute | solution.py:800
  172.3 1.5 collective-permute-start.32
  173.9 2.6 %collective-permute-start.28 = (bf16[18,16,256]{2,1,0:T(8,128)(2,1)S(1)}, bf16[18,16,256]{2,1,0:T(8,128)(2,1)S(1)}, u32[]{:S(2)}, u32[]{:S(2)}) collective-permute-start(bf16[18,16,256]{2,1,0:T(8,128)(2,1)S(1)} %pad_maximum_fusion.11), channel_id=1, source_target_pairs={{0,1},{1,0},{2,3},{3,2},{4,5},{5,4},{6,7},{7,6},{8,9},{9,8},{10,11... | collective-permute-start | bytes 442376 | tf_op jit(solution)/shard_map/ppermute | solution.py:800
  176.6 1.3 collective-permute-start.31
  177.9 1.7 collective-permute-done.28
  179.9 1.3 collective-permute-start.30
  181.2 3.8 %collective-permute-done.29 = bf16[9,32,256]{2,1,0:T(8,128)(2,1)S(1)} collective-permute-done((bf16[9,32,256]{2,1,0:T(8,128)(2,1)S(1)}, bf16[9,32,256]{2,1,0:T(8,128)(2,1)S(1)}, u32[]{:S(2)}, u32[]{:S(2)}) %collective-permute-start.29) | collective-permute-done | bytes 147488 | tf_op jit(solution)/shard_map/ppermute | solution.py:800
  185.0 3.5 %collective-permute-done.30 = bf16[9,32,256]{2,1,0:T(8,128)(2,1)S(1)} collective-permute-done((bf16[9,32,256]{2,1,0:T(8,128)(2,1)S(1)}, bf16[9,32,256]{2,1,0:T(8,128)(2,1)S(1)}, u32[]{:S(2)}, u32[]{:S(2)}) %collective-permute-start.30) | collective-permute-done | bytes 147488 | tf_op jit(solution)/shard_map/ppermute | solution.py:800
  191.9 2.8 %shard_map.215 = (f32[18,256,512]{2,1,0:T(8,128)}, f32[1,256,512]{2,1,0:T(8,128)}) custom-call(s32[1]{0:T(128)} %bitcast.side_ref, bf16[19,256,256]{2,1,0:T(8,128)(2,1)S(1)} %pad_maximum_fusion.half_ref), custom_call_target="tpu_custom_call" | custom-call | tf_op jit(solution)/shard_map/pallas_call | solution.py:732
  194.7 3.4 %shard_map.216 = (f32[18,256,512]{2,1,0:T(8,128)}, f32[1,256,512]{2,1,0:T(8,128)}) custom-call(s32[1]{0:T(128)} %bitcast.15.side_ref, bf16[19,256,256]{2,1,0:T(8,128)(2,1)} %collective-permute-done.35.half_ref, f32[18,256,512]{2,1,0:T(8,128)} %get-tuple-element.175.refs_0_, ...), custom_call_target="tpu_custom_call", output_to_operand_aliasing={{0}: (2, {}), {1}: (3, {})} | custom-call | tf_op jit(solution)/shard_map/pallas_call | solution.py:732
  202.6 2.1 shard_map.217.refs_0_
  205.4 2.1 shard_map.218
  (151 shorter events, 30.4 us)
Async XLA Ops:
  3.5 17.7 %copy-start.3 = (bf16[2,16,32,256]{3,2,1,0:T(8,128)(2,1)S(1)}, bf16[2,16,32,256]{3,2,1,0:T(8,128)(2,1)}, u32[]{:S(2)}) copy-start(bf16[2,16,32,256]{3,2,1,0:T(8,128)(2,1)} %refs_0_.1) | copy-start | bytes 1572868
  3.5 17.7 %copy-start.11 = (bf16[256,512]{1,0:T(8,128)(2,1)S(1)}, bf16[256,512]{1,0:T(8,128)(2,1)}, u32[]{:S(2)}) copy-start(bf16[256,512]{1,0:T(8,128)(2,1)} %refs_4_.1) | copy-start | bytes 786436
  4.5 9.8 %collective-permute-start = (bf16[672,256]{1,0:T(8,128)(2,1)S(1)}, bf16[672,256]{1,0:T(8,128)(2,1)S(1)}, u32[]{:S(2)}, u32[]{:S(2)}) collective-permute-start(bf16[672,256]{1,0:T(8,128)(2,1)S(1)} %shard_map.203), channel_id=1, source_target_pairs={{0,16},{16,0},{1,17},{17,1},{2,18},{18,2},{3,19},{19,3},{4,20},{20... | collective-permute-start | bytes 1032200 | tf_op jit(solution)/shard_map/ppermute | solution.py:929
  5.1 2.8 %collective-permute-start.1 = (bf16[2,1,32,256]{3,2,1,0:T(8,128)(2,1)S(1)}, bf16[2,1,32,256]{3,2,1,0:T(8,128)(2,1)S(1)}, u32[]{:S(2)}, u32[]{:S(2)}) collective-permute-start(bf16[2,1,32,256]{3,2,1,0:T(8,128)(2,1)S(1)} %slice.57), channel_id=1, source_target_pairs={{0,16},{1,17},{2,18},{3,19},{4,20},{5,21},{6,22},{7,23},{8,24},{9,... | collective-permute-start | bytes 98312 | tf_op jit(solution)/shard_map/ppermute | solution.py:787
  7.9 6.4 %collective-permute-start.2 = (bf16[2,17,1,256]{3,2,1,0:T(2,128)(2,1)S(1)}, bf16[2,17,1,256]{3,2,1,0:T(2,128)(2,1)S(1)}, u32[]{:S(2)}, u32[]{:S(2)}) collective-permute-start(bf16[2,17,1,256]{3,2,1,0:T(2,128)(2,1)S(1)} %pad_maximum_fusion.12), channel_id=1, source_target_pairs={{0,4},{4,8},{8,12},{1,5},{5,9},{9,13},{2,6},{6,10},{10,14},{3,7},{... | collective-permute-start | bytes 52232 | tf_op jit(solution)/shard_map/ppermute | solution.py:787
  15.7 16.9 %collective-permute-start.3 = (bf16[480,256]{1,0:T(8,128)(2,1)S(1)}, bf16[480,256]{1,0:T(8,128)(2,1)S(1)}, u32[]{:S(2)}, u32[]{:S(2)}) collective-permute-start(bf16[480,256]{1,0:T(8,128)(2,1)S(1)} %get-tuple-element.101), channel_id=1, source_target_pairs={{0,4},{4,8},{8,12},{1,5},{5,9},{9,13},{2,6},{6,10},{10,14},{3,7},{... | collective-permute-start | bytes 737288 | tf_op jit(solution)/shard_map/ppermute | solution.py:787
  19.9 12.7 %collective-permute-start.4 = (bf16[480,256]{1,0:T(8,128)(2,1)S(1)}, bf16[480,256]{1,0:T(8,128)(2,1)S(1)}, u32[]{:S(2)}, u32[]{:S(2)}) collective-permute-start(bf16[480,256]{1,0:T(8,128)(2,1)S(1)} %get-tuple-element.102), channel_id=1, source_target_pairs={{4,0},{8,4},{12,8},{5,1},{9,5},{13,9},{6,2},{10,6},{14,10},{7,3},{... | collective-permute-start | bytes 737288 | tf_op jit(solution)/shard_map/ppermute | solution.py:787
  24.6 19.2 %all-to-all-start = ((f32[32,1,2176]{2,1,0:T(1,128)}), f32[32,1,2176]{2,1,0:T(1,128)S(1)}, u32[]{:S(2)}, u32[]{:S(2)}) async-start(f32[32,1,2176]{2,1,0:T(1,128)} %shard_map.206), calls=%async_computation | async-start | bytes 557056 | tf_op jit(solution)/shard_map/all_to_all | solution.py:791
  38.3 51.5 %copy-start = (f32[624,128]{1,0:T(8,128)}, f32[624,128]{1,0:T(8,128)S(1)}, u32[]{:S(2)}) copy-start(f32[624,128]{1,0:T(8,128)S(1)} %get-tuple-element.107.refs_5_.refs_10_.refs_12_.refs_9_.refs_8_) | copy-start | bytes 958468
  38.3 51.5 %copy-start.4 = (f32[624,128]{1,0:T(8,128)}, f32[624,128]{1,0:T(8,128)S(1)}, u32[]{:S(2)}) copy-start(f32[624,128]{1,0:T(8,128)S(1)} %get-tuple-element.106.refs_4_.refs_9_.refs_8_.refs_7_) | copy-start | bytes 958468
  43.8 16.9 %copy-start.13 = (f32[512]{0:T(512)S(1)}, f32[512]{0:T(512)}, u32[]{:S(2)}) copy-start(f32[512]{0:T(512)} %param.20) | copy-start | bytes 6148
  50.1 39.6 %copy-start.9 = (f32[8,512]{1,0:T(8,128)}, f32[8,512]{1,0:T(8,128)S(1)}, u32[]{:S(2)}) copy-start(f32[8,512]{1,0:T(8,128)S(1)} %get-tuple-element.110.refs_3_.refs_8_.refs_2_.refs_4_.refs_5_) | copy-start | bytes 49156
  50.1 29.0 %collective-permute-start.6 = (bf16[624,1536]{1,0:T(8,128)(2,1)}, bf16[624,1536]{1,0:T(8,128)(2,1)}, u32[]{:S(2)}, u32[]{:S(2)}) collective-permute-start(bf16[624,1536]{1,0:T(8,128)(2,1)} %get-tuple-element.117.refs_3_), channel_id=1, source_target_pairs={{0,16},{16,0},{1,17},{17,1},{2,18},{18,2},{3,19},{19,3},{4,20},{20... | collective-permute-start | bytes 5750792 | tf_op jit(solution)/shard_map/ppermute | solution.py:800
  50.2 10.5 %all-to-all-start.1 = ((f32[32,1,1024]{2,1,0:T(1,128)}), f32[32,1,1024]{2,1,0:T(1,128)S(1)}, u32[]{:S(2)}, u32[]{:S(2)}) async-start(f32[32,1,1024]{2,1,0:T(1,128)} %get-tuple-element.111), calls=%async_computation.1 | async-start | bytes 262144 | tf_op jit(solution)/shard_map/all_to_all | solution.py:791
  53.0 27.3 %copy-start.17 = (s32[5]{0:T(128)}, s32[5]{0:T(128)S(1)}, u32[]{:S(2)}) copy-start(s32[5]{0:T(128)S(1)} %stack.32.refs_0_) | copy-start | bytes 64
  66.5 12.6 %collective-permute-start.5 = (f32[3,384,256]{2,1,0:T(8,128)}, f32[3,384,256]{2,1,0:T(8,128)S(1)}, u32[]{:S(2)}, u32[]{:S(2)}) collective-permute-start(f32[3,384,256]{2,1,0:T(8,128)} %get-tuple-element.116), channel_id=1, source_target_pairs={{0,16},{16,0},{1,17},{17,1},{2,18},{18,2},{3,19},{19,3},{4,20},{20... | collective-permute-start | bytes 3538952 | tf_op jit(solution)/shard_map/ppermute | solution.py:800
  66.6 12.5 %collective-permute-start.7 = (bf16[624,768]{1,0:T(8,128)(2,1)}, bf16[624,768]{1,0:T(8,128)(2,1)}, u32[]{:S(2)}, u32[]{:S(2)}) collective-permute-start(bf16[624,768]{1,0:T(8,128)(2,1)} %get-tuple-element.118.refs_5_.refs_3_), channel_id=1, source_target_pairs={{0,16},{16,0},{1,17},{17,1},{2,18},{18,2},{3,19},{19,3},{4,20},{20... | collective-permute-start | bytes 2875400 | tf_op jit(solution)/shard_map/ppermute | solution.py:800
  67.1 12.0 %all-to-all-start.2 = ((f32[32,1,1536]{2,1,0:T(1,128)}), f32[32,1,1536]{2,1,0:T(1,128)S(1)}, u32[]{:S(2)}, u32[]{:S(2)}) async-start(f32[32,1,1536]{2,1,0:T(1,128)} %get-tuple-element.119), calls=%async_computation.2 | async-start | bytes 393216 | tf_op jit(solution)/shard_map/all_to_all | solution.py:791
  69.9 1.7 collective-permute-start.8
  88.7 16.7 %collective-permute-start.10 = (bf16[19,64,256]{2,1,0:T(8,128)(2,1)}, bf16[19,64,256]{2,1,0:T(8,128)(2,1)S(1)}, u32[]{:S(2)}, u32[]{:S(2)}) collective-permute-start(bf16[19,64,256]{2,1,0:T(8,128)(2,1)} %get-tuple-element.128), channel_id=1, source_target_pairs={{0,8},{4,12},{8,0},{12,4},{1,9},{5,13},{9,1},{13,5},{2,10},{6,14},... | collective-permute-start | bytes 1867784 | tf_op jit(solution)/shard_map/ppermute | solution.py:800
  89.6 15.7 %collective-permute-start.9 = (bf16[19,64,256]{2,1,0:T(8,128)(2,1)S(1)}, bf16[19,64,256]{2,1,0:T(8,128)(2,1)}, u32[]{:S(2)}, u32[]{:S(2)}) collective-permute-start(bf16[19,64,256]{2,1,0:T(8,128)(2,1)S(1)} %get-tuple-element.126), channel_id=1, source_target_pairs={{0,4},{4,0},{8,12},{12,8},{1,5},{5,1},{9,13},{13,9},{2,6},{6,2},{1... | collective-permute-start | bytes 1867784 | tf_op jit(solution)/shard_map/ppermute | solution.py:800
  89.7 23.3 %collective-permute-start.14 = (bf16[672,768]{1,0:T(8,128)(2,1)}, bf16[672,768]{1,0:T(8,128)(2,1)}, u32[]{:S(2)}, u32[]{:S(2)}) collective-permute-start(bf16[672,768]{1,0:T(8,128)(2,1)} %get-tuple-element.139.refs_5_), channel_id=1, source_target_pairs={{0,16},{16,0},{1,17},{17,1},{2,18},{18,2},{3,19},{19,3},{4,20},{20... | collective-permute-start | bytes 3096584 | tf_op jit(solution)/shard_map/ppermute | solution.py:800
  101.3 11.8 %collective-permute-start.13 = (f32[2,384,256]{2,1,0:T(8,128)}, f32[2,384,256]{2,1,0:T(8,128)}, u32[]{:S(2)}, u32[]{:S(2)}) collective-permute-start(f32[2,384,256]{2,1,0:T(8,128)} %get-tuple-element.138), channel_id=1, source_target_pairs={{0,16},{16,0},{1,17},{17,1},{2,18},{18,2},{3,19},{19,3},{4,20},{20... | collective-permute-start | bytes 2359304 | tf_op jit(solution)/shard_map/ppermute | solution.py:800
  101.8 11.2 %all-to-all-start.3 = ((f32[32,1,1024]{2,1,0:T(1,128)}), f32[32,1,1024]{2,1,0:T(1,128)S(1)}, u32[]{:S(2)}, u32[]{:S(2)}) async-start(f32[32,1,1024]{2,1,0:T(1,128)} %get-tuple-element.140), calls=%async_computation.3 | async-start | bytes 262144 | tf_op jit(solution)/shard_map/all_to_all | solution.py:791
  110.0 10.0 %collective-permute-start.11 = (bf16[19,32,256]{2,1,0:T(8,128)(2,1)}, bf16[19,32,256]{2,1,0:T(8,128)(2,1)}, u32[]{:S(2)}, u32[]{:S(2)}) collective-permute-start(bf16[19,32,256]{2,1,0:T(8,128)(2,1)} %get-tuple-element.135), channel_id=1, source_target_pairs={{0,8},{4,12},{8,0},{12,4},{1,9},{5,13},{9,1},{13,5},{2,10},{6,14},... | collective-permute-start | bytes 933896 | tf_op jit(solution)/shard_map/ppermute | solution.py:800
  111.6 9.4 %collective-permute-start.12 = (bf16[19,32,256]{2,1,0:T(8,128)(2,1)}, bf16[19,32,256]{2,1,0:T(8,128)(2,1)}, u32[]{:S(2)}, u32[]{:S(2)}) collective-permute-start(bf16[19,32,256]{2,1,0:T(8,128)(2,1)} %get-tuple-element.136), channel_id=1, source_target_pairs={{0,4},{4,0},{8,12},{12,8},{1,5},{5,1},{9,13},{13,9},{2,6},{6,2},{1... | collective-permute-start | bytes 933896 | tf_op jit(solution)/shard_map/ppermute | solution.py:800
  122.7 10.4 %collective-permute-start.15 = (bf16[38,16,256]{2,1,0:T(8,128)(2,1)S(1)}, bf16[38,16,256]{2,1,0:T(8,128)(2,1)S(1)}, u32[]{:S(2)}, u32[]{:S(2)}) collective-permute-start(bf16[38,16,256]{2,1,0:T(8,128)(2,1)S(1)} %select_convert_fusion), channel_id=1, source_target_pairs={{0,1},{1,0},{2,3},{3,2},{4,5},{5,4},{6,7},{7,6},{8,9},{9,8},{10,11... | collective-permute-start | bytes 933896 | tf_op jit(solution)/shard_map/ppermute | solution.py:800
  124.3 8.4 %collective-permute-start.16 = (bf16[9,64,256]{2,1,0:T(8,128)(2,1)S(1)}, bf16[9,64,256]{2,1,0:T(8,128)(2,1)S(1)}, u32[]{:S(2)}, u32[]{:S(2)}) collective-permute-start(bf16[9,64,256]{2,1,0:T(8,128)(2,1)S(1)} %get-tuple-element.148), channel_id=1, source_target_pairs={{0,4},{4,0},{8,12},{12,8},{1,5},{5,1},{9,13},{13,9},{2,6},{6,2},{1... | collective-permute-start | bytes 884744 | tf_op jit(solution)/shard_map/ppermute | solution.py:800
  125.7 7.4 %collective-permute-start.17 = (bf16[9,64,256]{2,1,0:T(8,128)(2,1)S(1)}, bf16[9,64,256]{2,1,0:T(8,128)(2,1)S(1)}, u32[]{:S(2)}, u32[]{:S(2)}) collective-permute-start(bf16[9,64,256]{2,1,0:T(8,128)(2,1)S(1)} %get-tuple-element.149), channel_id=1, source_target_pairs={{0,8},{4,12},{8,0},{12,4},{1,9},{5,13},{9,1},{13,5},{2,10},{6,14},... | collective-permute-start | bytes 884744 | tf_op jit(solution)/shard_map/ppermute | solution.py:800
  133.2 5.2 %collective-permute-start.20 = (bf16[9,32,256]{2,1,0:T(8,128)(2,1)S(1)}, bf16[9,32,256]{2,1,0:T(8,128)(2,1)S(1)}, u32[]{:S(2)}, u32[]{:S(2)}) collective-permute-start(bf16[9,32,256]{2,1,0:T(8,128)(2,1)S(1)} %select_convert_fusion.3), channel_id=1, source_target_pairs={{0,4},{4,0},{8,12},{12,8},{1,5},{5,1},{9,13},{13,9},{2,6},{6,2},{1... | collective-permute-start | bytes 442376 | tf_op jit(solution)/shard_map/ppermute | solution.py:800
  134.0 7.9 %collective-permute-start.18 = (bf16[38,8,256]{2,1,0:T(8,128)(2,1)S(1)}, bf16[38,8,256]{2,1,0:T(8,128)(2,1)S(1)}, u32[]{:S(2)}, u32[]{:S(2)}) collective-permute-start(bf16[38,8,256]{2,1,0:T(8,128)(2,1)S(1)} %select_convert_fusion.1), channel_id=1, source_target_pairs={{0,2},{1,3},{2,0},{3,1},{4,6},{5,7},{6,4},{7,5},{8,10},{9,11},{10,... | collective-permute-start | bytes 466952 | tf_op jit(solution)/shard_map/ppermute | solution.py:800
  136.6 5.2 %collective-permute-start.19 = (bf16[9,32,256]{2,1,0:T(8,128)(2,1)S(1)}, bf16[9,32,256]{2,1,0:T(8,128)(2,1)S(1)}, u32[]{:S(2)}, u32[]{:S(2)}) collective-permute-start(bf16[9,32,256]{2,1,0:T(8,128)(2,1)S(1)} %select_convert_fusion.4), channel_id=1, source_target_pairs={{0,8},{4,12},{8,0},{12,4},{1,9},{5,13},{9,1},{13,5},{2,10},{6,14},... | collective-permute-start | bytes 442376 | tf_op jit(solution)/shard_map/ppermute | solution.py:800
  142.1 11.0 %collective-permute-start.21 = (bf16[38,8,256]{2,1,0:T(8,128)(2,1)S(1)}, bf16[38,8,256]{2,1,0:T(8,128)(2,1)S(1)}, u32[]{:S(2)}, u32[]{:S(2)}) collective-permute-start(bf16[38,8,256]{2,1,0:T(8,128)(2,1)S(1)} %add_convert_fusion), channel_id=1, source_target_pairs={{0,2},{1,3},{2,0},{3,1},{4,6},{5,7},{6,4},{7,5},{8,10},{9,11},{10,... | collective-permute-start | bytes 466952 | tf_op jit(solution)/shard_map/ppermute | solution.py:800
  143.0 10.0 %collective-permute-start.22 = (bf16[18,16,256]{2,1,0:T(8,128)(2,1)S(1)}, bf16[18,16,256]{2,1,0:T(8,128)(2,1)S(1)}, u32[]{:S(2)}, u32[]{:S(2)}) collective-permute-start(bf16[18,16,256]{2,1,0:T(8,128)(2,1)S(1)} %select_convert_fusion.2), channel_id=1, source_target_pairs={{0,1},{1,0},{2,3},{3,2},{4,5},{5,4},{6,7},{7,6},{8,9},{9,8},{10,11... | collective-permute-start | bytes 442376 | tf_op jit(solution)/shard_map/ppermute | solution.py:800
  153.1 8.5 %collective-permute-start.23 = (bf16[38,16,256]{2,1,0:T(8,128)(2,1)S(1)}, bf16[38,16,256]{2,1,0:T(8,128)(2,1)S(1)}, u32[]{:S(2)}, u32[]{:S(2)}) collective-permute-start(bf16[38,16,256]{2,1,0:T(8,128)(2,1)S(1)} %pad_maximum_fusion.6), channel_id=1, source_target_pairs={{0,1},{1,0},{2,3},{3,2},{4,5},{5,4},{6,7},{7,6},{8,9},{9,8},{10,11... | collective-permute-start | bytes 933896 | tf_op jit(solution)/shard_map/ppermute | solution.py:800
  154.5 5.9 %collective-permute-start.24 = (bf16[18,8,256]{2,1,0:T(8,128)(2,1)S(1)}, bf16[18,8,256]{2,1,0:T(8,128)(2,1)S(1)}, u32[]{:S(2)}, u32[]{:S(2)}) collective-permute-start(bf16[18,8,256]{2,1,0:T(8,128)(2,1)S(1)} %select_convert_fusion.5), channel_id=1, source_target_pairs={{0,2},{1,3},{2,0},{3,1},{4,6},{5,7},{6,4},{7,5},{8,10},{9,11},{10,... | collective-permute-start | bytes 221192 | tf_op jit(solution)/shard_map/ppermute | solution.py:800
  161.9 10.3 %collective-permute-start.25 = (bf16[19,32,256]{2,1,0:T(8,128)(2,1)S(1)}, bf16[19,32,256]{2,1,0:T(8,128)(2,1)S(1)}, u32[]{:S(2)}, u32[]{:S(2)}) collective-permute-start(bf16[19,32,256]{2,1,0:T(8,128)(2,1)S(1)} %get-tuple-element.196), channel_id=1, source_target_pairs={{0,8},{4,12},{8,0},{12,4},{1,9},{5,13},{9,1},{13,5},{2,10},{6,14},... | collective-permute-start | bytes 933896 | tf_op jit(solution)/shard_map/ppermute | solution.py:800
  162.0 10.2 %collective-permute-start.26 = (bf16[19,32,256]{2,1,0:T(8,128)(2,1)S(1)}, bf16[19,32,256]{2,1,0:T(8,128)(2,1)S(1)}, u32[]{:S(2)}, u32[]{:S(2)}) collective-permute-start(bf16[19,32,256]{2,1,0:T(8,128)(2,1)S(1)} %get-tuple-element.195), channel_id=1, source_target_pairs={{0,4},{4,0},{8,12},{12,8},{1,5},{5,1},{9,13},{13,9},{2,6},{6,2},{1... | collective-permute-start | bytes 933896 | tf_op jit(solution)/shard_map/ppermute | solution.py:800
  163.2 5.3 %collective-permute-start.27 = (bf16[18,8,256]{2,1,0:T(8,128)(2,1)S(1)}, bf16[18,8,256]{2,1,0:T(8,128)(2,1)S(1)}, u32[]{:S(2)}, u32[]{:S(2)}) collective-permute-start(bf16[18,8,256]{2,1,0:T(8,128)(2,1)S(1)} %add_convert_fusion.1), channel_id=1, source_target_pairs={{0,2},{1,3},{2,0},{3,1},{4,6},{5,7},{6,4},{7,5},{8,10},{9,11},{10,... | collective-permute-start | bytes 221192 | tf_op jit(solution)/shard_map/ppermute | solution.py:800
  172.3 16.1 %collective-permute-start.32 = (bf16[19,64,256]{2,1,0:T(8,128)(2,1)S(1)}, bf16[19,64,256]{2,1,0:T(8,128)(2,1)S(1)}, u32[]{:S(2)}, u32[]{:S(2)}) collective-permute-start(bf16[19,64,256]{2,1,0:T(8,128)(2,1)S(1)} %pad_maximum_fusion.4), channel_id=1, source_target_pairs={{0,8},{4,12},{8,0},{12,4},{1,9},{5,13},{9,1},{13,5},{2,10},{6,14},... | collective-permute-start | bytes 1867784 | tf_op jit(solution)/shard_map/ppermute | solution.py:800
  173.9 5.7 %collective-permute-start.28 = (bf16[18,16,256]{2,1,0:T(8,128)(2,1)S(1)}, bf16[18,16,256]{2,1,0:T(8,128)(2,1)S(1)}, u32[]{:S(2)}, u32[]{:S(2)}) collective-permute-start(bf16[18,16,256]{2,1,0:T(8,128)(2,1)S(1)} %pad_maximum_fusion.11), channel_id=1, source_target_pairs={{0,1},{1,0},{2,3},{3,2},{4,5},{5,4},{6,7},{7,6},{8,9},{9,8},{10,11... | collective-permute-start | bytes 442376 | tf_op jit(solution)/shard_map/ppermute | solution.py:800
  176.6 11.9 %collective-permute-start.31 = (bf16[19,64,256]{2,1,0:T(8,128)(2,1)S(1)}, bf16[19,64,256]{2,1,0:T(8,128)(2,1)S(1)}, u32[]{:S(2)}, u32[]{:S(2)}) collective-permute-start(bf16[19,64,256]{2,1,0:T(8,128)(2,1)S(1)} %pad_maximum_fusion.3), channel_id=1, source_target_pairs={{0,4},{4,0},{8,12},{12,8},{1,5},{5,1},{9,13},{13,9},{2,6},{6,2},{1... | collective-permute-start | bytes 1867784 | tf_op jit(solution)/shard_map/ppermute | solution.py:800
  179.8 5.2 %collective-permute-start.29 = (bf16[9,32,256]{2,1,0:T(8,128)(2,1)S(1)}, bf16[9,32,256]{2,1,0:T(8,128)(2,1)S(1)}, u32[]{:S(2)}, u32[]{:S(2)}) collective-permute-start(bf16[9,32,256]{2,1,0:T(8,128)(2,1)S(1)} %get-tuple-element.210), channel_id=1, source_target_pairs={{0,8},{4,12},{8,0},{12,4},{1,9},{5,13},{9,1},{13,5},{2,10},{6,14},... | collective-permute-start | bytes 442376 | tf_op jit(solution)/shard_map/ppermute | solution.py:800
  179.9 8.6 %collective-permute-start.30 = (bf16[9,32,256]{2,1,0:T(8,128)(2,1)S(1)}, bf16[9,32,256]{2,1,0:T(8,128)(2,1)S(1)}, u32[]{:S(2)}, u32[]{:S(2)}) collective-permute-start(bf16[9,32,256]{2,1,0:T(8,128)(2,1)S(1)} %get-tuple-element.209), channel_id=1, source_target_pairs={{0,4},{4,0},{8,12},{12,8},{1,5},{5,1},{9,13},{13,9},{2,6},{6,2},{1... | collective-permute-start | bytes 442376 | tf_op jit(solution)/shard_map/ppermute | solution.py:800
  189.6 5.1 %collective-permute-start.35 = (bf16[19,256,256]{2,1,0:T(8,128)(2,1)S(1)}, bf16[19,256,256]{2,1,0:T(8,128)(2,1)}, u32[]{:S(2)}, u32[]{:S(2)}) collective-permute-start(bf16[19,256,256]{2,1,0:T(8,128)(2,1)S(1)} %pad_maximum_fusion.half_ref), channel_id=1, source_target_pairs={{0,16},{16,0},{1,17},{17,1},{2,18},{18,2},{3,19},{19,3},{4,20},{20... | collective-permute-start | bytes 7471112 | tf_op jit(solution)/shard_map/ppermute | solution.py:800
  189.7 9.6 %collective-permute-start.34 = (bf16[9,64,256]{2,1,0:T(8,128)(2,1)S(1)}, bf16[9,64,256]{2,1,0:T(8,128)(2,1)}, u32[]{:S(2)}, u32[]{:S(2)}) collective-permute-start(bf16[9,64,256]{2,1,0:T(8,128)(2,1)S(1)} %pad_maximum_fusion.9), channel_id=1, source_target_pairs={{0,8},{4,12},{8,0},{12,4},{1,9},{5,13},{9,1},{13,5},{2,10},{6,14},... | collective-permute-start | bytes 884744 | tf_op jit(solution)/shard_map/ppermute | solution.py:800
  190.6 9.7 %collective-permute-start.33 = (bf16[9,64,256]{2,1,0:T(8,128)(2,1)}, bf16[9,64,256]{2,1,0:T(8,128)(2,1)}, u32[]{:S(2)}, u32[]{:S(2)}) collective-permute-start(bf16[9,64,256]{2,1,0:T(8,128)(2,1)} %pad_maximum_fusion.8), channel_id=1, source_target_pairs={{0,4},{4,0},{8,12},{12,8},{1,5},{5,1},{9,13},{13,9},{2,6},{6,2},{1... | collective-permute-start | bytes 884744 | tf_op jit(solution)/shard_map/ppermute | solution.py:800
  202.5 2.9 %collective-permute-start.36 = (bf16[9,256,256]{2,1,0:T(8,128)(2,1)S(1)}, bf16[9,256,256]{2,1,0:T(8,128)(2,1)S(1)}, u32[]{:S(2)}, u32[]{:S(2)}) collective-permute-start(bf16[9,256,256]{2,1,0:T(8,128)(2,1)S(1)} %pad_maximum_fusion.1.half_ref), channel_id=1, source_target_pairs={{0,16},{16,0},{1,17},{17,1},{2,18},{18,2},{3,19},{19,3},{4,20},{20... | collective-permute-start | bytes 3538952 | tf_op jit(solution)/shard_map/ppermute | solution.py:800
  (21 other events, 162.8 us)

commit v6 on v5

--- a/solution.py
+++ b/solution.py
@@ -64,6 +64,11 @@
 def row_parts(total, count):
     size = total // count
     return [(k, (pl.ds(k * size, size),)) for k in range(count)]
+
+
+def middle_parts(total, count):
+    size = total // count
+    return [(k, (slice(None), pl.ds(k * size, size))) for k in range(count)]
 
 
 def end_parts(total, size):
@@ -414,9 +419,9 @@
     copies.wait(N.h3, N.pre2, N.spread)
 
 
-def part(r, at, *fields):
+def part(r, at, *fields, first=0):
     bit = r.bits[0] == 1
-    for k, field in enumerate(fields):
+    for k, field in enumerate(fields, first):
         half = field.shape[1] // 2
         low, high = field[:, :half], field[:, half:]
         r.mine[k, at : at + field.shape[0], :] = jnp.where(bit, high, low)
@@ -458,13 +463,15 @@
         g = g * own
         if L <= at < L + r.mine.shape[1]:
             part(r, at - L, g, n2 * own, np_ * own)
+            if at - L + S == r.mine.shape[1] // 2:
+                copies.start((N.mine, 0), (N.theirs, 0))
         new = [column_sum(g * n2), column_sum(g), column_sum(g * np_)]
         sums = [a + b for a, b in zip(sums, new)]
         if (line + 1) % (total // 2) == 0:
             copies.start((N.grad, (line + 1) // (total // 2) - 1))
     row = jnp.concatenate(sums, axis=1)
     r.spread[...] = jnp.broadcast_to(row[None], r.spread.shape)
-    copies.start(N.spread, N.mine, N.theirs)
+    copies.start(N.spread, (N.mine, 1), (N.theirs, 1))
     for i in range(rows):
         for g in range(groups):
             at = (i + 1) * L + g * S + 1
@@ -474,11 +481,10 @@
 
 
 def fourth_kernel(r, copies):
-    width = r.gain2.shape[1]
-    Q = r.pre2.shape[0]
-    rows_w = r.gpu.shape[0]
-    L = (Q - rows_w) // 3
-    n = r.mom1[2:3, :]
+    width = r.gain.shape[1]
+    Q, U, rows_w = r.pre2.shape[0], r.act.shape[0], r.gpu.shape[0]
+    L = U - rows_w
+    center, inv, n = (r.mom1[k : k + 1, :] for k in range(3))
     c2, i2, cp, ip = (r.mom2[k : k + 1, :] for k in range(4))
     t3 = jnp.sum(r.tot3[...], axis=0)
     gg2, gs, ggp = (t3[:, k * width : (k + 1) * width] for k in range(3))
@@ -487,33 +493,26 @@
     copies.start(*tiny)
     for m0, m in chunks(Q, L):
         if m0 in (0, 6 * L):
-            k = m0 // (6 * L)
-            copies.wait((N.grad, k), (N.pre2, k), (N.prep, k))
-        shifted = slice(L + 1 + m0, L + 1 + m0 + m)
-        mask = wide(r.maskp[shifted, :], width) / n
+            copies.wait((N.grad, m0 // (6 * L)), (N.pre2, m0 // (6 * L)))
+        mask = wide(r.maskp[L + 1 + m0 : L + 1 + m0 + m, :], width) / n
         n2 = (r.pre2[m0 : m0 + m, :] - c2) * i2
-        np_ = (r.prep[shifted, :] - cp) * ip
-        g = r.grad[m0 : m0 + m, :]
-        r.gq[m0 : m0 + m, :] = (r.gain2[...] * i2) * (g - mask * (gs + n2 * gg2))
-        r.gpq[m0 : m0 + m, :] = (r.gainp[...] * ip) * (g - mask * (gs + np_ * ggp))
+        back = mask * (gs + n2 * gg2)
+        r.gq[m0 : m0 + m, :] = (r.gain2[...] * i2) * (r.grad[m0 : m0 + m, :] - back)
     r.gq[Q:, :] = jnp.zeros((r.gq.shape[0] - Q, width), f32)
-    copies.start(N.gq)
-    for m0, m in chunks(rows_w, 96):
-        r.gpu[m0 : m0 + m, :] = r.gpq[L + 1 + m0 : L + 1 + m0 + m, :].astype(bf16)
-    copies.start(N.gpu)
-    copies.wait(N.gpu, N.gq, *tiny)
-
-
-def hidden_kernel(r, copies):
-    width = r.gain.shape[1]
-    Q = r.gq.shape[0] - 8
-    L = (r.keep.shape[0] - Q) // 2
-    center, inv = r.mom1[0:1, :], r.mom1[1:2, :]
-    copies.wait(N.gq)
     for m0, m in chunks(Q, 176):
         for b in range(3):
             r.g3[m0 : m0 + m, b * width : (b + 1) * width] = r.gq[m0 + b : m0 + b + m, :].astype(bf16)
-    U = r.act.shape[0]
+    copies.wait(N.keep)
+    for m0, m in chunks(U, L):
+        frame = slice(2 * L + 2 + m0, 2 * L + 2 + m0 + m)
+        n1 = (r.keep[frame, :] - center) * inv
+        v = n1 * r.gain[...] + r.shift[...]
+        mask = wide(r.maskp[frame, :], width)
+        r.act[m0 : m0 + m, :] = gelu_slope(v, gelu_parts(v)) * mask
+        r.normed[m0 : m0 + m, :] = n1 * mask
+        if m0 < rows_w:
+            part(r, m0, n1 * wide(r.ownp[frame, :], width), first=1)
+    copies.start(N.normed, (N.mine, 1), (N.theirs, 1))
     for a in range(3):
         copies.wait((N.w2, a))
         gh = jnp.zeros((U, width), f32)
@@ -522,28 +521,26 @@
                 r.g3[L * a : L * a + U, b * width : (b + 1) * width],
                 r.w2[2 - a, (2 - b) * width : (3 - b) * width, :],
             )
-        r.act[...] = gh if a == 0 else r.act[...] + gh
-    copies.wait(N.keep)
+        r.gh[...] = gh if a == 0 else r.gh[...] + gh
     sums = [jnp.zeros((1, width), f32)] * 2
-    for k, (m0, m) in enumerate(chunks(U, L)):
-        frame = slice(2 * L + 2 + m0, 2 * L + 2 + m0 + m)
-        n1 = (r.keep[frame, :] - center) * inv
-        v = n1 * r.gain[...] + r.shift[...]
-        mask = wide(r.maskp[frame, :], width)
-        g = gelu_slope(v, gelu_parts(v)) * mask * r.act[m0 : m0 + m, :]
+    for m0, m in chunks(U, L):
+        g = r.act[m0 : m0 + m, :] * r.gh[m0 : m0 + m, :]
         r.act[m0 : m0 + m, :] = g
-        r.normed[m0 : m0 + m, :] = n1 * mask
-        if k % 3 == 2:
-            copies.start((N.act, k // 3), (N.normed, k // 3))
-        own = wide(r.ownp[frame, :], width)
-        g = g * own
-        if m0 < r.mine.shape[1]:
-            part(r, m0, g, n1 * own)
-        sums = [sums[0] + column_sum(g * n1), sums[1] + column_sum(g)]
+        g = g * wide(r.ownp[2 * L + 2 + m0 : 2 * L + 2 + m0 + m, :], width)
+        if m0 < rows_w:
+            part(r, m0, g)
+        sums = [sums[0] + column_sum(g * r.normed[m0 : m0 + m, :]), sums[1] + column_sum(g)]
     row = jnp.concatenate(sums, axis=1)
     r.spread[...] = jnp.broadcast_to(row[None], r.spread.shape)
-    copies.start(N.spread, N.mine, N.theirs)
-    copies.wait(N.act, N.normed, N.spread, N.mine, N.theirs)
+    copies.start(N.spread, (N.mine, 0), (N.theirs, 0), N.act)
+    copies.wait(N.prep)
+    for m0, m in chunks(rows_w, L):
+        frame = slice(2 * L + 2 + m0, 2 * L + 2 + m0 + m)
+        mask = wide(r.maskp[frame, :], width) / n
+        back = mask * (gs + (r.prep[frame, :] - cp) * ip * ggp)
+        r.gpu[m0 : m0 + m, :] = ((r.gainp[...] * ip) * (r.grad[L + 1 + m0 : L + 1 + m0 + m, :] - back)).astype(bf16)
+    copies.start(N.gpu)
+    copies.wait(N.normed, N.mine, N.theirs, N.spread, N.act, N.gpu, *tiny)
 
 
 def split_store(r, rows, unit, first):
@@ -1000,7 +997,7 @@
     )
     h3, pre2, mom1 = second[N.h3], second[N.pre2], second[N.mom1]
     tot2 = gather_sum(second[N.spread])
-    far_h3 = partner(h3, *core)
+    tot2, far_h3 = lax.optimization_barrier((tot2, partner(h3, *core)))
 
     third = call(
         third_kernel,
@@ -1021,6 +1018,7 @@
         far_out=(N.grad, N.spread, N.mine, N.theirs, N.out),
         smem=(N.bits,),
         parts=dict(
+            mine=middle_parts(MW, 2), theirs=middle_parts(MW, 2),
             grad=row_parts(MQ, 2), pre2=row_parts(MQ, 2), cotq=row_parts(MQ, 2), prep=cuts(L, L + MQ // 2 + 8, L + MQ + 8)
         ),
     )
@@ -1060,42 +1058,36 @@
     grad, *second_parts = lax.optimization_barrier((third[N.grad], *second_parts))
     tree2 = Tree(second_parts, bits, plane, rest, core)
     tree2.start()
-    fourth = call(
+    hidden = call(
         fourth_kernel,
         dict(
-            pre2=pre2, prep=first[N.prep], mom1=mom1, mom2=mom2, tot3=tot3, gain2=g2, gainp=gp,
-            grad=grad, maskp=maskp, ownp=ownp,
-        ),
-        dict(
-            gq=shape((MQ + 8, width)),
-            gpu=shape((MW, width), bf16),
-            gain_second=vec(1),
-            shift_second=vec(1),
-            gain_proj=vec(1),
-            shift_proj=vec(1),
-        ),
-        dict(gpq=pltpu.VMEM((MQ, width), f32)),
-        far_in=(N.pre2, N.prep, N.grad),
-        far_out=(N.gpu, N.gq, N.gain_second, N.shift_second, N.gain_proj, N.shift_proj),
-        parts=dict(grad=cuts(0, 6 * L, MQ), pre2=cuts(0, 6 * L, MQ), prep=cuts(L, 7 * L + 8, L + MQ + 8)),
-    )
-    hidden = call(
-        hidden_kernel,
-        dict(bits=bits, gq=fourth[N.gq], w2=w2, keep=first[N.pre1], mom1=mom1, gain=g1, shift=b1, maskp=maskp, ownp=ownp),
+            bits=bits, grad=grad, pre2=pre2, keep=first[N.pre1], w2=w2, prep=first[N.prep], mom1=mom1, mom2=mom2, tot3=tot3,
+            gain=g1, shift=b1, gain2=g2, gainp=gp, maskp=maskp, ownp=ownp,
+        ),
         dict(
             act=shape((MU, width)), normed=shape((MU, width)), spread=all_devices(2 * width),
-            mine=shape((2, MW, half)), theirs=shape((2, MW, half)),
-        ),
-        dict(g3=pltpu.VMEM((MQ, 3 * width), bf16)),
-        far_in=(N.gq, N.w2, N.keep),
-        far_out=(N.act, N.normed, N.spread, N.mine, N.theirs),
+            mine=shape((2, MW, half)), theirs=shape((2, MW, half)), gpu=shape((MW, width), bf16),
+            gain_second=vec(1), shift_second=vec(1), gain_proj=vec(1), shift_proj=vec(1),
+        ),
+        dict(
+            gq=pltpu.VMEM((MQ + 8, width), f32),
+            g3=pltpu.VMEM((MQ, 3 * width), bf16),
+            gh=pltpu.VMEM((MU, width), f32),
+        ),
+        far_in=(N.grad, N.pre2, N.keep, N.w2, N.prep),
+        far_out=(
+            N.act, N.normed, N.spread, N.mine, N.theirs, N.gpu, N.gain_second, N.shift_second, N.gain_proj, N.shift_proj
+        ),
         smem=(N.bits,),
-        limit=60,
+        limit=52,
         parts=dict(
+            grad=cuts(0, 6 * L, MQ),
+            pre2=cuts(0, 6 * L, MQ),
+            keep=cuts(2 * L, 2 * L + MU + 8),
             w2=[(k, (pl.ds(2 - k, 1),)) for k in range(3)],
-            keep=cuts(2 * L, 2 * L + MU + 8),
-            act=row_parts(MU, 3),
-            normed=row_parts(MU, 3),
+            prep=cuts(2 * L, 2 * L + MW + 8),
+            mine=row_parts(2, 2),
+            theirs=row_parts(2, 2),
         ),
     )
     tot4 = gather_sum(hidden[N.spread])
@@ -1135,7 +1127,7 @@
     grad_inputs = call(
         inputs_kernel,
         dict(
-            act=hidden[N.act], normed=hidden[N.normed], gpu=fourth[N.gpu], w1=w1, wp=w_proj, mom1=mom1, gain=g1, maskp=maskp,
+            act=hidden[N.act], normed=hidden[N.normed], gpu=hidden[N.gpu], w1=w1, wp=w_proj, mom1=mom1, gain=g1, maskp=maskp,
             gg=fifth[N.gain_first], gs=fifth[N.shift_first],
         ),
         dict(out=shape((groups, rows_in, cols_in, cin), bf16)),
@@ -1177,11 +1169,11 @@
         fifth[N.gain_first].reshape(width),
         fifth[N.shift_first].reshape(width),
         grad_w2.reshape(w_second.shape),
-        fourth[N.gain_second].reshape(width),
-        fourth[N.shift_second].reshape(width),
+        hidden[N.gain_second].reshape(width),
+        hidden[N.shift_second].reshape(width),
         grad_wp.reshape(w_proj.shape),
-        fourth[N.gain_proj].reshape(width),
-        fourth[N.shift_proj].reshape(width),
+        hidden[N.gain_proj].reshape(width),
+        hidden[N.shift_proj].reshape(width),
     )
 
 

time: 209 us -> 206 us (0.986)
  Pallas kernels: 70.7 us -> 67.4 us
    pallas_call x12 -> x11, Pallas kernels: 60.4 us -> 57.1 us  [call(): pl.pallas_call(run, out_shape=list(outs.values()), in_specs=[spec(n) for...]
  transfers between devices with their start and end apart: 41 -> 41, of which waited for: 21 -> 24; matrix products, arithmetic and copies ran while one was open for 1% -> 1% of each run, Pallas kernels for 25% -> 21%
where the time goes in v6:
time: 206 us; the launch traced here: 205 us
  Pallas kernels  67.4 us (33%)
  starting transfers between devices  65.7 us (32%)
  waiting for transfers between devices  58.6 us (28%)
  other arithmetic  7.78 us (4%)
  local copies, waits for them, and re-layouts  3.74 us (2%)
    pallas_call x11, Pallas kernels, call(): pl.pallas_call(run, out_shape=list(outs.values()), in_specs=[spec(n) for...  57.1 us
    ppermute x32, starting transfers between devices, partner(): return lax.ppermute(value, axis, [(i, i ^ step) for i in range(count)])  36.2 us
    ppermute x32, waiting for transfers between devices, partner(): return lax.ppermute(value, axis, [(i, i ^ step) for i in range(count)])  35.4 us
    all_to_all x4, waiting for transfers between devices, gather_sum(): return lax.all_to_all(spread, axes, 0, 0)  20.8 us
    all_to_all x4, starting transfers between devices, gather_sum(): return lax.all_to_all(spread, axes, 0, 0)  16.7 us
    ppermute x4, starting transfers between devices, shifted(): lax.ppermute(value, axis, [(source, source + steps) for source in range(f...  12.3 us
    pallas_call x4, Pallas kernels, widen(): pl.pallas_call(body, out_shape=[shape((taps * per, n, 2 * m))] + [shape((...  10.3 us
  transfers between devices with their start and end apart: 41, of which 24 were waited for; matrix products, arithmetic and copies ran while one was open for 1% of the time, Pallas kernels for 21%

profile of v6, /device:TPU:0, one launch (start us, length us, event | category | flops | bytes accessed | tf_op | source)
XLA Modules:
  0.0 204.9 jit_solution(15416848852095232336)
XLA Ops:
  5.1 2.0 collective-permute-start.1
  7.9 4.8 %collective-permute-start.2 = (bf16[2,17,1,256]{3,2,1,0:T(2,128)(2,1)S(1)}, bf16[2,17,1,256]{3,2,1,0:T(2,128)(2,1)S(1)}, u32[]{:S(2)}, u32[]{:S(2)}) collective-permute-start(bf16[2,17,1,256]{3,2,1,0:T(2,128)(2,1)S(1)} %pad_maximum_fusion.12), channel_id=1, source_target_pairs={{0,4},{4,8},{8,12},{1,5},{5,9},{9,13},{2,6},{6,10},{10,14},{3,7},{... | collective-permute-start | bytes 52232 | tf_op jit(solution)/shard_map/ppermute | solution.py:784
  12.8 1.6 collective-permute-done.2.refs_2_
  15.7 4.2 %collective-permute-start.3 = (bf16[480,256]{1,0:T(8,128)(2,1)S(1)}, bf16[480,256]{1,0:T(8,128)(2,1)S(1)}, u32[]{:S(2)}, u32[]{:S(2)}) collective-permute-start(bf16[480,256]{1,0:T(8,128)(2,1)S(1)} %get-tuple-element.102), channel_id=1, source_target_pairs={{0,4},{4,8},{8,12},{1,5},{5,9},{9,13},{2,6},{6,10},{10,14},{3,7},{... | collective-permute-start | bytes 737288 | tf_op jit(solution)/shard_map/ppermute | solution.py:784
  21.2 3.4 %shard_map.206 = f32[32,1,2176]{2,1,0:T(1,128)} custom-call(bf16[2,16,32,256]{3,2,1,0:T(8,128)(2,1)S(1)} %copy-done.1, bf16[2,1,32,256]{3,2,1,0:T(8,128)(2,1)S(1)} %collective-permute-done.1.refs_1_, bf16[2,17,1,256]{3,2,1,0:T(2,128)(2,1)S(1)} %collective-permute-done.2.refs_2_, bf16[2,8,16,128]{3,2,1,0:T(8,128)(2,1)S(1)} %broadcast_in_dim.2.refs_3_, ...), custom_call_target="tpu_custom_call" | custom-call | tf_op jit(solution)/shard_map/pallas_call | solution.py:113
  24.6 7.9 %all-to-all-start = ((f32[32,1,2176]{2,1,0:T(1,128)}), f32[32,1,2176]{2,1,0:T(1,128)S(1)}, u32[]{:S(2)}, u32[]{:S(2)}) async-start(f32[32,1,2176]{2,1,0:T(1,128)} %shard_map.206), calls=%async_computation | async-start | bytes 557056 | tf_op jit(solution)/shard_map/all_to_all | solution.py:788
  32.6 5.7 %shard_map.205 = (f32[624,512]{1,0:T(8,128)}, f32[624,512]{1,0:T(8,128)}, bf16[624,768]{1,0:T(8,128)(2,1)}, bf16[672,768]{1,0:T(8,128)(2,1)}, f32[624,128]{1,0:T...) custom-call(s32[2]{0:T(128)S(1)} %add_convert_fusion.2.refs_0_, bf16[2,16,32,256]{3,2,1,0:T(8,128)(2,1)} %refs_0_.1, ...), custom_call_target="tpu_custom_call" | custom-call | flops 20000000000 | tf_op jit(solution)/shard_map/pallas_call | solution.py:113
  38.3 5.5 %all-to-all-done.refs_1_ = f32[32,1,2176]{2,1,0:T(1,128)S(1)} async-done(((f32[32,1,2176]{2,1,0:T(1,128)}), f32[32,1,2176]{2,1,0:T(1,128)S(1)}, u32[]{:S(2)}, u32[]{:S(2)}) %all-to-all-start) | async-done | bytes 278560 | tf_op jit(solution)/shard_map/all_to_all | solution.py:788
  43.8 6.3 %shard_map.207 = (bf16[624,1536]{1,0:T(8,128)(2,1)}, f32[528,512]{1,0:T(8,128)}, f32[32,1,1024]{2,1,0:T(1,128)}, f32[8,512]{1,0:T(8,128)S(1)}) custom-call(f32[624,512]{1,0:T(8,128)} %get-tuple-element.104.refs_0_.refs_3_, f32[32,1,2176]{2,1,0:T(1,128)S(1)} %all-to-all-done.refs_1_, f32[1,512]{1,0:T(1,128)S(1)} %bitcast.33, f32[1,512]{1,0:T(1,128)S(1)} %bitcast.31, ...), custom_call_target="tpu_custom_call" | custom-call | tf_op jit(solution)/shard_map/pallas_call | solution.py:113
  50.2 2.6 %all-to-all-start.1 = ((f32[32,1,1024]{2,1,0:T(1,128)}), f32[32,1,1024]{2,1,0:T(1,128)S(1)}, u32[]{:S(2)}, u32[]{:S(2)}) async-start(f32[32,1,1024]{2,1,0:T(1,128)} %get-tuple-element.112), calls=%async_computation.1 | async-start | bytes 262144 | tf_op jit(solution)/shard_map/all_to_all | solution.py:788
  53.0 7.7 %all-to-all-done.1.refs_4_ = f32[32,1,1024]{2,1,0:T(1,128)S(1)} async-done(((f32[32,1,1024]{2,1,0:T(1,128)}), f32[32,1,1024]{2,1,0:T(1,128)S(1)}, u32[]{:S(2)}, u32[]{:S(2)}) %all-to-all-start.1) | async-done | bytes 131104 | tf_op jit(solution)/shard_map/all_to_all | solution.py:788
  60.7 5.5 %shard_map.208 = (bf16[2,8,16,512]{3,2,1,0:T(8,128)(2,1)}, f32[528,512]{1,0:T(8,128)}, f32[32,1,1536]{2,1,0:T(1,128)}, f32[8,512]{1,0:T(8,128)S(1)}, f32[3,384,256]{2,1,0:T(8,128)}, /*index=5*/f32[3,384,256]{2,1,0:T(8,128)}) custom-call(s32[5]{0:T(128)S(1)} %stack.32.refs_0_, f32[528,512]{1,0:T(8,128)} %get-tuple-element.109.refs_1_.refs_2_, ...), custom_call_target="tpu_custom_call" | custom-call | tf_op jit(solution)/shard_map/pallas_call | solution.py:113
  66.8 2.8 %all-to-all-start.2 = ((f32[32,1,1536]{2,1,0:T(1,128)}), f32[32,1,1536]{2,1,0:T(1,128)S(1)}, u32[]{:S(2)}, u32[]{:S(2)}) async-start(f32[32,1,1536]{2,1,0:T(1,128)} %get-tuple-element.122), calls=%async_computation.2 | async-start | bytes 393216 | tf_op jit(solution)/shard_map/all_to_all | solution.py:788
  69.7 1.6 collective-permute-done.8.refs_13_.refs_11_
  71.3 7.5 %all-to-all-done.2.refs_7_.refs_8_ = f32[32,1,1536]{2,1,0:T(1,128)S(1)} async-done(((f32[32,1,1536]{2,1,0:T(1,128)}), f32[32,1,1536]{2,1,0:T(1,128)S(1)}, u32[]{:S(2)}, u32[]{:S(2)}) %all-to-all-start.2) | async-done | bytes 196640 | tf_op jit(solution)/shard_map/all_to_all | solution.py:788
  80.0 8.4 %shard_map.209 = (bf16[19,64,256]{2,1,0:T(8,128)(2,1)S(1)}, f32[19,64,256]{2,1,0:T(8,128)}, bf16[19,64,256]{2,1,0:T(8,128)(2,1)}, f32[19,64,256]{2,1,0:T(8,128)}) custom-call(s32[5]{0:T(128)S(1)} %stack.32.refs_0_, f32[3,384,256]{2,1,0:T(8,128)} %get-tuple-element.118.refs_1_, f32[3,384,256]{2,1,0:T(8,128)} %copy-done.18, ...), custom_call_target="tpu_custom_call" | custom-call | tf_op jit(solution)/shard_map/pallas_call | solution.py:113
  89.5 8.6 %shard_map.211 = (f32[432,512]{1,0:T(8,128)}, f32[432,512]{1,0:T(8,128)}, f32[32,1,1024]{2,1,0:T(1,128)}, f32[2,384,256]{2,1,0:T(8,128)}, f32[2,384,256]{2,1,0:T...) custom-call(s32[5]{0:T(128)S(1)} %stack.32.refs_0_, ...), custom_call_target="tpu_custom_call" | custom-call | tf_op jit(solution)/shard_map/pallas_call | solution.py:113
  98.6 3.4 %all-to-all-start.3 = ((f32[32,1,1024]{2,1,0:T(1,128)}), f32[32,1,1024]{2,1,0:T(1,128)S(1)}, u32[]{:S(2)}, u32[]{:S(2)}) async-start(f32[32,1,1024]{2,1,0:T(1,128)} %get-tuple-element.142), calls=%async_computation.3 | async-start | bytes 262144 | tf_op jit(solution)/shard_map/all_to_all | solution.py:788
  102.1 1.9 collective-permute-done.10.refs_4_
  104.9 3.8 %shard_map.210 = (bf16[19,32,256]{2,1,0:T(8,128)(2,1)}, f32[19,32,256]{2,1,0:T(8,128)}, bf16[19,32,256]{2,1,0:T(8,128)(2,1)}, f32[19,32,256]{2,1,0:T(8,128)}) custom-call(s32[5]{0:T(128)} %copy-done.10, f32[19,64,256]{2,1,0:T(8,128)} %get-tuple-element.128.refs_1_, bf16[19,64,256]{2,1,0:T(8,128)(2,1)} %collective-permute-done.9.refs_2_, ...), custom_call_target="tpu_custom_call" | custom-call | flops 20000000000 | tf_op jit(solution)/shard_map/pallas_call | solution.py:113
  110.6 6.9 %shard_map.212 = (bf16[9,64,256]{2,1,0:T(8,128)(2,1)S(1)}, f32[9,64,256]{2,1,0:T(8,128)S(1)}, bf16[9,64,256]{2,1,0:T(8,128)(2,1)S(1)}, f32[9,64,256]{2,1,0:T(8,1...) custom-call(s32[5]{0:T(128)S(1)} %copy-done.11, f32[2,384,256]{2,1,0:T(8,128)} %get-tuple-element.139.refs_1_, ...), custom_call_target="tpu_custom_call" | custom-call | flops 20000000000 | tf_op jit(solution)/shard_map/pallas_call | solution.py:113
  117.9 1.4 convert_add_fusion.1
  119.4 1.5 collective-permute-start.15
  121.0 1.5 collective-permute-start.16
  123.0 6.4 %shard_map.213 = bf16[2,16,32,256]{3,2,1,0:T(8,128)(2,1)} custom-call(f32[432,512]{1,0:T(8,128)S(1)} %copy-done.14, f32[432,512]{1,0:T(8,128)} %get-tuple-element.153.refs_1_, bf16[384,512]{1,0:T(8,128)(2,1)S(1)} %get-tuple-element.154.refs_2_, bf16[3,768,512]{2,1,0:T(8,128)(2,1)} %bitcast.47, bf16[256,512]{1,0:T(8,128)(2,1)S(1)} %copy-done.5, ...), custom_call_target="tpu_custom_call" | custom-call | flops 10000000000 | tf_op jit(solution)/shard_map/pallas_call | solution.py:113
  131.5 1.8 collective-permute-start.18
  135.1 3.5 %collective-permute-done.19 = bf16[9,32,256]{2,1,0:T(8,128)(2,1)S(1)} collective-permute-done((bf16[9,32,256]{2,1,0:T(8,128)(2,1)S(1)}, bf16[9,32,256]{2,1,0:T(8,128)(2,1)S(1)}, u32[]{:S(2)}, u32[]{:S(2)}) %collective-permute-start.19) | collective-permute-done | bytes 147488 | tf_op jit(solution)/shard_map/ppermute | solution.py:797
  140.1 4.1 %collective-permute-start.22 = (bf16[18,16,256]{2,1,0:T(8,128)(2,1)S(1)}, bf16[18,16,256]{2,1,0:T(8,128)(2,1)S(1)}, u32[]{:S(2)}, u32[]{:S(2)}) collective-permute-start(bf16[18,16,256]{2,1,0:T(8,128)(2,1)S(1)} %select_convert_fusion.2), channel_id=1, source_target_pairs={{0,1},{1,0},{2,3},{3,2},{4,5},{5,4},{6,7},{7,6},{8,9},{9,8},{10,11... | collective-permute-start | bytes 442376 | tf_op jit(solution)/shard_map/ppermute | solution.py:797
  144.1 5.5 %collective-permute-done.22 = bf16[18,16,256]{2,1,0:T(8,128)(2,1)S(1)} collective-permute-done((bf16[18,16,256]{2,1,0:T(8,128)(2,1)S(1)}, bf16[18,16,256]{2,1,0:T(8,128)(2,1)S(1)}, u32[]{:S(2)}, u32[]{:S(2)}) %collective-permute-start.22) | collective-permute-done | bytes 147488 | tf_op jit(solution)/shard_map/ppermute | solution.py:797
  149.7 1.4 collective-permute-start.23
  151.1 2.5 %collective-permute-start.24 = (bf16[18,8,256]{2,1,0:T(8,128)(2,1)S(1)}, bf16[18,8,256]{2,1,0:T(8,128)(2,1)S(1)}, u32[]{:S(2)}, u32[]{:S(2)}) collective-permute-start(bf16[18,8,256]{2,1,0:T(8,128)(2,1)S(1)} %select_convert_fusion.5), channel_id=1, source_target_pairs={{0,2},{1,3},{2,0},{3,1},{4,6},{5,7},{6,4},{7,5},{8,10},{9,11},{10,... | collective-permute-start | bytes 221192 | tf_op jit(solution)/shard_map/ppermute | solution.py:797
  153.6 3.4 %collective-permute-done.24 = bf16[18,8,256]{2,1,0:T(8,128)(2,1)S(1)} collective-permute-done((bf16[18,8,256]{2,1,0:T(8,128)(2,1)S(1)}, bf16[18,8,256]{2,1,0:T(8,128)(2,1)S(1)}, u32[]{:S(2)}, u32[]{:S(2)}) %collective-permute-start.24) | collective-permute-done | bytes 73760 | tf_op jit(solution)/shard_map/ppermute | solution.py:797
  159.5 1.5 collective-permute-start.26
  161.1 2.3 %collective-permute-start.27 = (bf16[18,8,256]{2,1,0:T(8,128)(2,1)S(1)}, bf16[18,8,256]{2,1,0:T(8,128)(2,1)S(1)}, u32[]{:S(2)}, u32[]{:S(2)}) collective-permute-start(bf16[18,8,256]{2,1,0:T(8,128)(2,1)S(1)} %add_convert_fusion.1), channel_id=1, source_target_pairs={{0,2},{1,3},{2,0},{3,1},{4,6},{5,7},{6,4},{7,5},{8,10},{9,11},{10,... | collective-permute-start | bytes 221192 | tf_op jit(solution)/shard_map/ppermute | solution.py:797
  163.4 3.0 %collective-permute-done.27 = bf16[18,8,256]{2,1,0:T(8,128)(2,1)S(1)} collective-permute-done((bf16[18,8,256]{2,1,0:T(8,128)(2,1)S(1)}, bf16[18,8,256]{2,1,0:T(8,128)(2,1)S(1)}, u32[]{:S(2)}, u32[]{:S(2)}) %collective-permute-start.27) | collective-permute-done | bytes 73760 | tf_op jit(solution)/shard_map/ppermute | solution.py:797
  166.4 2.4 %collective-permute-done.25 = bf16[19,32,256]{2,1,0:T(8,128)(2,1)S(1)} collective-permute-done((bf16[19,32,256]{2,1,0:T(8,128)(2,1)S(1)}, bf16[19,32,256]{2,1,0:T(8,128)(2,1)S(1)}, u32[]{:S(2)}, u32[]{:S(2)}) %collective-permute-start.25) | collective-permute-done | bytes 311328 | tf_op jit(solution)/shard_map/ppermute | solution.py:797
  170.3 3.0 %collective-permute-start.28 = (bf16[18,16,256]{2,1,0:T(8,128)(2,1)S(1)}, bf16[18,16,256]{2,1,0:T(8,128)(2,1)S(1)}, u32[]{:S(2)}, u32[]{:S(2)}) collective-permute-start(bf16[18,16,256]{2,1,0:T(8,128)(2,1)S(1)} %pad_maximum_fusion.11), channel_id=1, source_target_pairs={{0,1},{1,0},{2,3},{3,2},{4,5},{5,4},{6,7},{7,6},{8,9},{9,8},{10,11... | collective-permute-start | bytes 442376 | tf_op jit(solution)/shard_map/ppermute | solution.py:797
  173.3 1.5 collective-permute-start.31
  174.8 1.6 collective-permute-done.28
  177.3 1.8 collective-permute-start.30
  179.1 2.6 %collective-permute-done.29 = bf16[9,32,256]{2,1,0:T(8,128)(2,1)S(1)} collective-permute-done((bf16[9,32,256]{2,1,0:T(8,128)(2,1)S(1)}, bf16[9,32,256]{2,1,0:T(8,128)(2,1)S(1)}, u32[]{:S(2)}, u32[]{:S(2)}) %collective-permute-start.29) | collective-permute-done | bytes 147488 | tf_op jit(solution)/shard_map/ppermute | solution.py:797
  181.7 3.5 %collective-permute-done.30 = bf16[9,32,256]{2,1,0:T(8,128)(2,1)S(1)} collective-permute-done((bf16[9,32,256]{2,1,0:T(8,128)(2,1)S(1)}, bf16[9,32,256]{2,1,0:T(8,128)(2,1)S(1)}, u32[]{:S(2)}, u32[]{:S(2)}) %collective-permute-start.30) | collective-permute-done | bytes 147488 | tf_op jit(solution)/shard_map/ppermute | solution.py:797
  187.8 2.0 collective-permute-start.33
  189.8 2.8 %shard_map.214 = (f32[18,256,512]{2,1,0:T(8,128)}, f32[1,256,512]{2,1,0:T(8,128)}) custom-call(s32[1]{0:T(128)} %bitcast.side_ref, bf16[19,256,256]{2,1,0:T(8,128)(2,1)S(1)} %pad_maximum_fusion.half_ref), custom_call_target="tpu_custom_call" | custom-call | tf_op jit(solution)/shard_map/pallas_call | solution.py:729
  192.6 3.4 %shard_map.215 = (f32[18,256,512]{2,1,0:T(8,128)}, f32[1,256,512]{2,1,0:T(8,128)}) custom-call(s32[1]{0:T(128)} %bitcast.15.side_ref, bf16[19,256,256]{2,1,0:T(8,128)(2,1)} %collective-permute-done.35.half_ref, f32[18,256,512]{2,1,0:T(8,128)} %get-tuple-element.177.refs_0_, ...), custom_call_target="tpu_custom_call", output_to_operand_aliasing={{0}: (2, {}), {1}: (3, {})} | custom-call | tf_op jit(solution)/shard_map/pallas_call | solution.py:729
  196.0 1.5 collective-permute-done.33
  199.8 2.1 %shard_map.216.refs_0_ = f32[9,256,512]{2,1,0:T(8,128)} custom-call(s32[1]{0:T(128)} %bitcast.side_ref, bf16[9,256,256]{2,1,0:T(8,128)(2,1)S(1)} %pad_maximum_fusion.1.half_ref), custom_call_target="tpu_custom_call" | custom-call | tf_op jit(solution)/shard_map/pallas_call | solution.py:729
  202.7 2.1 %shard_map.217 = f32[9,256,512]{2,1,0:T(8,128)} custom-call(s32[1]{0:T(128)} %bitcast.15.side_ref, bf16[9,256,256]{2,1,0:T(8,128)(2,1)S(1)} %collective-permute-done.36.half_ref, f32[9,256,512]{2,1,0:T(8,128)} %shard_map.216.refs_0_), custom_call_target="tpu_custom_call", output_to_operand_aliasing={{}: (2, {})} | custom-call | tf_op jit(solution)/shard_map/pallas_call | solution.py:729
  (138 shorter events, 31.5 us)
Async XLA Ops:
  3.5 17.7 %copy-start.1 = (bf16[2,16,32,256]{3,2,1,0:T(8,128)(2,1)S(1)}, bf16[2,16,32,256]{3,2,1,0:T(8,128)(2,1)}, u32[]{:S(2)}) copy-start(bf16[2,16,32,256]{3,2,1,0:T(8,128)(2,1)} %refs_0_.1) | copy-start | bytes 1572868
  3.5 17.7 %copy-start.5 = (bf16[256,512]{1,0:T(8,128)(2,1)S(1)}, bf16[256,512]{1,0:T(8,128)(2,1)}, u32[]{:S(2)}) copy-start(bf16[256,512]{1,0:T(8,128)(2,1)} %refs_4_.1) | copy-start | bytes 786436
  4.5 9.8 %collective-permute-start = (bf16[672,256]{1,0:T(8,128)(2,1)S(1)}, bf16[672,256]{1,0:T(8,128)(2,1)S(1)}, u32[]{:S(2)}, u32[]{:S(2)}) collective-permute-start(bf16[672,256]{1,0:T(8,128)(2,1)S(1)} %shard_map.203), channel_id=1, source_target_pairs={{0,16},{16,0},{1,17},{17,1},{2,18},{18,2},{3,19},{19,3},{4,20},{20... | collective-permute-start | bytes 1032200 | tf_op jit(solution)/shard_map/ppermute | solution.py:926
  5.1 2.8 %collective-permute-start.1 = (bf16[2,1,32,256]{3,2,1,0:T(8,128)(2,1)S(1)}, bf16[2,1,32,256]{3,2,1,0:T(8,128)(2,1)S(1)}, u32[]{:S(2)}, u32[]{:S(2)}) collective-permute-start(bf16[2,1,32,256]{3,2,1,0:T(8,128)(2,1)S(1)} %slice.57), channel_id=1, source_target_pairs={{0,16},{1,17},{2,18},{3,19},{4,20},{5,21},{6,22},{7,23},{8,24},{9,... | collective-permute-start | bytes 98312 | tf_op jit(solution)/shard_map/ppermute | solution.py:784
  7.9 6.4 %collective-permute-start.2 = (bf16[2,17,1,256]{3,2,1,0:T(2,128)(2,1)S(1)}, bf16[2,17,1,256]{3,2,1,0:T(2,128)(2,1)S(1)}, u32[]{:S(2)}, u32[]{:S(2)}) collective-permute-start(bf16[2,17,1,256]{3,2,1,0:T(2,128)(2,1)S(1)} %pad_maximum_fusion.12), channel_id=1, source_target_pairs={{0,4},{4,8},{8,12},{1,5},{5,9},{9,13},{2,6},{6,10},{10,14},{3,7},{... | collective-permute-start | bytes 52232 | tf_op jit(solution)/shard_map/ppermute | solution.py:784
  15.7 16.9 %collective-permute-start.3 = (bf16[480,256]{1,0:T(8,128)(2,1)S(1)}, bf16[480,256]{1,0:T(8,128)(2,1)S(1)}, u32[]{:S(2)}, u32[]{:S(2)}) collective-permute-start(bf16[480,256]{1,0:T(8,128)(2,1)S(1)} %get-tuple-element.102), channel_id=1, source_target_pairs={{0,4},{4,8},{8,12},{1,5},{5,9},{9,13},{2,6},{6,10},{10,14},{3,7},{... | collective-permute-start | bytes 737288 | tf_op jit(solution)/shard_map/ppermute | solution.py:784
  19.9 12.7 %collective-permute-start.4 = (bf16[480,256]{1,0:T(8,128)(2,1)S(1)}, bf16[480,256]{1,0:T(8,128)(2,1)S(1)}, u32[]{:S(2)}, u32[]{:S(2)}) collective-permute-start(bf16[480,256]{1,0:T(8,128)(2,1)S(1)} %get-tuple-element.103), channel_id=1, source_target_pairs={{4,0},{8,4},{12,8},{5,1},{9,5},{13,9},{6,2},{10,6},{14,10},{7,3},{... | collective-permute-start | bytes 737288 | tf_op jit(solution)/shard_map/ppermute | solution.py:784
  24.6 19.2 %all-to-all-start = ((f32[32,1,2176]{2,1,0:T(1,128)}), f32[32,1,2176]{2,1,0:T(1,128)S(1)}, u32[]{:S(2)}, u32[]{:S(2)}) async-start(f32[32,1,2176]{2,1,0:T(1,128)} %shard_map.206), calls=%async_computation | async-start | bytes 557056 | tf_op jit(solution)/shard_map/all_to_all | solution.py:788
  43.8 16.9 %copy-start.6 = (f32[512]{0:T(512)S(1)}, f32[512]{0:T(512)}, u32[]{:S(2)}) copy-start(f32[512]{0:T(512)} %param.17) | copy-start | bytes 6148
  43.8 16.9 %copy-start.7 = (f32[512]{0:T(512)S(1)}, f32[512]{0:T(512)}, u32[]{:S(2)}) copy-start(f32[512]{0:T(512)} %param.20) | copy-start | bytes 6148
  43.8 16.9 %copy-start.12 = (f32[512]{0:T(512)S(1)}, f32[512]{0:T(512)}, u32[]{:S(2)}) copy-start(f32[512]{0:T(512)} %param.18) | copy-start | bytes 6148
  43.8 16.9 %copy-start.13 = (f32[512]{0:T(512)S(1)}, f32[512]{0:T(512)}, u32[]{:S(2)}) copy-start(f32[512]{0:T(512)} %param.21) | copy-start | bytes 6148
  50.1 10.6 %collective-permute-start.5 = (bf16[624,1536]{1,0:T(8,128)(2,1)}, bf16[624,1536]{1,0:T(8,128)(2,1)S(1)}, u32[]{:S(2)}, u32[]{:S(2)}) collective-permute-start(bf16[624,1536]{1,0:T(8,128)(2,1)} %get-tuple-element.113.refs_3_), channel_id=1, source_target_pairs={{0,16},{16,0},{1,17},{17,1},{2,18},{18,2},{3,19},{19,3},{4,20},{20... | collective-permute-start | bytes 5750792 | tf_op jit(solution)/shard_map/ppermute | solution.py:797
  50.2 10.5 %all-to-all-start.1 = ((f32[32,1,1024]{2,1,0:T(1,128)}), f32[32,1,1024]{2,1,0:T(1,128)S(1)}, u32[]{:S(2)}, u32[]{:S(2)}) async-start(f32[32,1,1024]{2,1,0:T(1,128)} %get-tuple-element.112), calls=%async_computation.1 | async-start | bytes 262144 | tf_op jit(solution)/shard_map/all_to_all | solution.py:788
  52.9 36.5 %copy-start.10 = (s32[5]{0:T(128)}, s32[5]{0:T(128)S(1)}, u32[]{:S(2)}) copy-start(s32[5]{0:T(128)S(1)} %stack.32.refs_0_) | copy-start | bytes 64
  66.3 12.6 %collective-permute-start.6 = (f32[3,384,256]{2,1,0:T(8,128)}, f32[3,384,256]{2,1,0:T(8,128)S(1)}, u32[]{:S(2)}, u32[]{:S(2)}) collective-permute-start(f32[3,384,256]{2,1,0:T(8,128)} %get-tuple-element.119), channel_id=1, source_target_pairs={{0,16},{16,0},{1,17},{17,1},{2,18},{18,2},{3,19},{19,3},{4,20},{20... | collective-permute-start | bytes 3538952 | tf_op jit(solution)/shard_map/ppermute | solution.py:797
  66.3 5.0 %collective-permute-start.7 = (bf16[624,768]{1,0:T(8,128)(2,1)}, bf16[624,768]{1,0:T(8,128)(2,1)}, u32[]{:S(2)}, u32[]{:S(2)}) collective-permute-start(bf16[624,768]{1,0:T(8,128)(2,1)} %get-tuple-element.121.refs_5_.refs_3_), channel_id=1, source_target_pairs={{0,16},{16,0},{1,17},{17,1},{2,18},{18,2},{3,19},{19,3},{4,20},{20... | collective-permute-start | bytes 2875400 | tf_op jit(solution)/shard_map/ppermute | solution.py:797
  66.8 12.0 %all-to-all-start.2 = ((f32[32,1,1536]{2,1,0:T(1,128)}), f32[32,1,1536]{2,1,0:T(1,128)S(1)}, u32[]{:S(2)}, u32[]{:S(2)}) async-start(f32[32,1,1536]{2,1,0:T(1,128)} %get-tuple-element.122), calls=%async_computation.2 | async-start | bytes 393216 | tf_op jit(solution)/shard_map/all_to_all | solution.py:788
  69.6 1.7 collective-permute-start.8
  88.4 15.6 %collective-permute-start.10 = (bf16[19,64,256]{2,1,0:T(8,128)(2,1)}, bf16[19,64,256]{2,1,0:T(8,128)(2,1)S(1)}, u32[]{:S(2)}, u32[]{:S(2)}) collective-permute-start(bf16[19,64,256]{2,1,0:T(8,128)(2,1)} %get-tuple-element.131), channel_id=1, source_target_pairs={{0,8},{4,12},{8,0},{12,4},{1,9},{5,13},{9,1},{13,5},{2,10},{6,14},... | collective-permute-start | bytes 1867784 | tf_op jit(solution)/shard_map/ppermute | solution.py:797
  89.3 15.2 %collective-permute-start.9 = (bf16[19,64,256]{2,1,0:T(8,128)(2,1)S(1)}, bf16[19,64,256]{2,1,0:T(8,128)(2,1)}, u32[]{:S(2)}, u32[]{:S(2)}) collective-permute-start(bf16[19,64,256]{2,1,0:T(8,128)(2,1)S(1)} %get-tuple-element.129), channel_id=1, source_target_pairs={{0,4},{4,0},{8,12},{12,8},{1,5},{5,1},{9,13},{13,9},{2,6},{6,2},{1... | collective-permute-start | bytes 1867784 | tf_op jit(solution)/shard_map/ppermute | solution.py:797
  89.4 21.1 %collective-permute-start.14 = (bf16[672,768]{1,0:T(8,128)(2,1)}, bf16[672,768]{1,0:T(8,128)(2,1)}, u32[]{:S(2)}, u32[]{:S(2)}) collective-permute-start(bf16[672,768]{1,0:T(8,128)(2,1)} %get-tuple-element.141.refs_5_), channel_id=1, source_target_pairs={{0,16},{16,0},{1,17},{17,1},{2,18},{18,2},{3,19},{19,3},{4,20},{20... | collective-permute-start | bytes 3096584 | tf_op jit(solution)/shard_map/ppermute | solution.py:797
  98.1 12.6 %collective-permute-start.13 = (f32[2,384,256]{2,1,0:T(8,128)}, f32[2,384,256]{2,1,0:T(8,128)}, u32[]{:S(2)}, u32[]{:S(2)}) collective-permute-start(f32[2,384,256]{2,1,0:T(8,128)} %get-tuple-element.140), channel_id=1, source_target_pairs={{0,16},{16,0},{1,17},{17,1},{2,18},{18,2},{3,19},{19,3},{4,20},{20... | collective-permute-start | bytes 2359304 | tf_op jit(solution)/shard_map/ppermute | solution.py:797
  98.6 12.0 %all-to-all-start.3 = ((f32[32,1,1024]{2,1,0:T(1,128)}), f32[32,1,1024]{2,1,0:T(1,128)S(1)}, u32[]{:S(2)}, u32[]{:S(2)}) async-start(f32[32,1,1024]{2,1,0:T(1,128)} %get-tuple-element.142), calls=%async_computation.3 | async-start | bytes 262144 | tf_op jit(solution)/shard_map/all_to_all | solution.py:788
  108.7 8.8 %collective-permute-start.11 = (bf16[19,32,256]{2,1,0:T(8,128)(2,1)}, bf16[19,32,256]{2,1,0:T(8,128)(2,1)S(1)}, u32[]{:S(2)}, u32[]{:S(2)}) collective-permute-start(bf16[19,32,256]{2,1,0:T(8,128)(2,1)} %get-tuple-element.137), channel_id=1, source_target_pairs={{0,8},{4,12},{8,0},{12,4},{1,9},{5,13},{9,1},{13,5},{2,10},{6,14},... | collective-permute-start | bytes 933896 | tf_op jit(solution)/shard_map/ppermute | solution.py:797
  109.7 8.2 %collective-permute-start.12 = (bf16[19,32,256]{2,1,0:T(8,128)(2,1)}, bf16[19,32,256]{2,1,0:T(8,128)(2,1)}, u32[]{:S(2)}, u32[]{:S(2)}) collective-permute-start(bf16[19,32,256]{2,1,0:T(8,128)(2,1)} %get-tuple-element.138), channel_id=1, source_target_pairs={{0,4},{4,0},{8,12},{12,8},{1,5},{5,1},{9,13},{13,9},{2,6},{6,2},{1... | collective-permute-start | bytes 933896 | tf_op jit(solution)/shard_map/ppermute | solution.py:797
  119.4 10.4 %collective-permute-start.15 = (bf16[38,16,256]{2,1,0:T(8,128)(2,1)S(1)}, bf16[38,16,256]{2,1,0:T(8,128)(2,1)S(1)}, u32[]{:S(2)}, u32[]{:S(2)}) collective-permute-start(bf16[38,16,256]{2,1,0:T(8,128)(2,1)S(1)} %select_convert_fusion), channel_id=1, source_target_pairs={{0,1},{1,0},{2,3},{3,2},{4,5},{5,4},{6,7},{7,6},{8,9},{9,8},{10,11... | collective-permute-start | bytes 933896 | tf_op jit(solution)/shard_map/ppermute | solution.py:797
  121.0 8.4 %collective-permute-start.16 = (bf16[9,64,256]{2,1,0:T(8,128)(2,1)S(1)}, bf16[9,64,256]{2,1,0:T(8,128)(2,1)S(1)}, u32[]{:S(2)}, u32[]{:S(2)}) collective-permute-start(bf16[9,64,256]{2,1,0:T(8,128)(2,1)S(1)} %get-tuple-element.150), channel_id=1, source_target_pairs={{0,4},{4,0},{8,12},{12,8},{1,5},{5,1},{9,13},{13,9},{2,6},{6,2},{1... | collective-permute-start | bytes 884744 | tf_op jit(solution)/shard_map/ppermute | solution.py:797
  122.4 7.4 %collective-permute-start.17 = (bf16[9,64,256]{2,1,0:T(8,128)(2,1)S(1)}, bf16[9,64,256]{2,1,0:T(8,128)(2,1)S(1)}, u32[]{:S(2)}, u32[]{:S(2)}) collective-permute-start(bf16[9,64,256]{2,1,0:T(8,128)(2,1)S(1)} %get-tuple-element.151), channel_id=1, source_target_pairs={{0,8},{4,12},{8,0},{12,4},{1,9},{5,13},{9,1},{13,5},{2,10},{6,14},... | collective-permute-start | bytes 884744 | tf_op jit(solution)/shard_map/ppermute | solution.py:797
  129.9 5.2 %collective-permute-start.20 = (bf16[9,32,256]{2,1,0:T(8,128)(2,1)S(1)}, bf16[9,32,256]{2,1,0:T(8,128)(2,1)S(1)}, u32[]{:S(2)}, u32[]{:S(2)}) collective-permute-start(bf16[9,32,256]{2,1,0:T(8,128)(2,1)S(1)} %select_convert_fusion.3), channel_id=1, source_target_pairs={{0,4},{4,0},{8,12},{12,8},{1,5},{5,1},{9,13},{13,9},{2,6},{6,2},{1... | collective-permute-start | bytes 442376 | tf_op jit(solution)/shard_map/ppermute | solution.py:797
  131.5 7.4 %collective-permute-start.18 = (bf16[38,8,256]{2,1,0:T(8,128)(2,1)S(1)}, bf16[38,8,256]{2,1,0:T(8,128)(2,1)S(1)}, u32[]{:S(2)}, u32[]{:S(2)}) collective-permute-start(bf16[38,8,256]{2,1,0:T(8,128)(2,1)S(1)} %select_convert_fusion.1), channel_id=1, source_target_pairs={{0,2},{1,3},{2,0},{3,1},{4,6},{5,7},{6,4},{7,5},{8,10},{9,11},{10,... | collective-permute-start | bytes 466952 | tf_op jit(solution)/shard_map/ppermute | solution.py:797
  133.4 5.2 %collective-permute-start.19 = (bf16[9,32,256]{2,1,0:T(8,128)(2,1)S(1)}, bf16[9,32,256]{2,1,0:T(8,128)(2,1)S(1)}, u32[]{:S(2)}, u32[]{:S(2)}) collective-permute-start(bf16[9,32,256]{2,1,0:T(8,128)(2,1)S(1)} %select_convert_fusion.4), channel_id=1, source_target_pairs={{0,8},{4,12},{8,0},{12,4},{1,9},{5,13},{9,1},{13,5},{2,10},{6,14},... | collective-permute-start | bytes 442376 | tf_op jit(solution)/shard_map/ppermute | solution.py:797
  139.0 10.6 %collective-permute-start.21 = (bf16[38,8,256]{2,1,0:T(8,128)(2,1)S(1)}, bf16[38,8,256]{2,1,0:T(8,128)(2,1)S(1)}, u32[]{:S(2)}, u32[]{:S(2)}) collective-permute-start(bf16[38,8,256]{2,1,0:T(8,128)(2,1)S(1)} %add_convert_fusion), channel_id=1, source_target_pairs={{0,2},{1,3},{2,0},{3,1},{4,6},{5,7},{6,4},{7,5},{8,10},{9,11},{10,... | collective-permute-start | bytes 466952 | tf_op jit(solution)/shard_map/ppermute | solution.py:797
  140.1 9.5 %collective-permute-start.22 = (bf16[18,16,256]{2,1,0:T(8,128)(2,1)S(1)}, bf16[18,16,256]{2,1,0:T(8,128)(2,1)S(1)}, u32[]{:S(2)}, u32[]{:S(2)}) collective-permute-start(bf16[18,16,256]{2,1,0:T(8,128)(2,1)S(1)} %select_convert_fusion.2), channel_id=1, source_target_pairs={{0,1},{1,0},{2,3},{3,2},{4,5},{5,4},{6,7},{7,6},{8,9},{9,8},{10,11... | collective-permute-start | bytes 442376 | tf_op jit(solution)/shard_map/ppermute | solution.py:797
  149.7 8.5 %collective-permute-start.23 = (bf16[38,16,256]{2,1,0:T(8,128)(2,1)S(1)}, bf16[38,16,256]{2,1,0:T(8,128)(2,1)S(1)}, u32[]{:S(2)}, u32[]{:S(2)}) collective-permute-start(bf16[38,16,256]{2,1,0:T(8,128)(2,1)S(1)} %pad_maximum_fusion.6), channel_id=1, source_target_pairs={{0,1},{1,0},{2,3},{3,2},{4,5},{5,4},{6,7},{7,6},{8,9},{9,8},{10,11... | collective-permute-start | bytes 933896 | tf_op jit(solution)/shard_map/ppermute | solution.py:797
  151.1 5.9 %collective-permute-start.24 = (bf16[18,8,256]{2,1,0:T(8,128)(2,1)S(1)}, bf16[18,8,256]{2,1,0:T(8,128)(2,1)S(1)}, u32[]{:S(2)}, u32[]{:S(2)}) collective-permute-start(bf16[18,8,256]{2,1,0:T(8,128)(2,1)S(1)} %select_convert_fusion.5), channel_id=1, source_target_pairs={{0,2},{1,3},{2,0},{3,1},{4,6},{5,7},{6,4},{7,5},{8,10},{9,11},{10,... | collective-permute-start | bytes 221192 | tf_op jit(solution)/shard_map/ppermute | solution.py:797
  158.5 10.3 %collective-permute-start.25 = (bf16[19,32,256]{2,1,0:T(8,128)(2,1)S(1)}, bf16[19,32,256]{2,1,0:T(8,128)(2,1)S(1)}, u32[]{:S(2)}, u32[]{:S(2)}) collective-permute-start(bf16[19,32,256]{2,1,0:T(8,128)(2,1)S(1)} %get-tuple-element.198), channel_id=1, source_target_pairs={{0,8},{4,12},{8,0},{12,4},{1,9},{5,13},{9,1},{13,5},{2,10},{6,14},... | collective-permute-start | bytes 933896 | tf_op jit(solution)/shard_map/ppermute | solution.py:797
  159.5 10.1 %collective-permute-start.26 = (bf16[19,32,256]{2,1,0:T(8,128)(2,1)S(1)}, bf16[19,32,256]{2,1,0:T(8,128)(2,1)S(1)}, u32[]{:S(2)}, u32[]{:S(2)}) collective-permute-start(bf16[19,32,256]{2,1,0:T(8,128)(2,1)S(1)} %get-tuple-element.197), channel_id=1, source_target_pairs={{0,4},{4,0},{8,12},{12,8},{1,5},{5,1},{9,13},{13,9},{2,6},{6,2},{1... | collective-permute-start | bytes 933896 | tf_op jit(solution)/shard_map/ppermute | solution.py:797
  161.1 5.3 %collective-permute-start.27 = (bf16[18,8,256]{2,1,0:T(8,128)(2,1)S(1)}, bf16[18,8,256]{2,1,0:T(8,128)(2,1)S(1)}, u32[]{:S(2)}, u32[]{:S(2)}) collective-permute-start(bf16[18,8,256]{2,1,0:T(8,128)(2,1)S(1)} %add_convert_fusion.1), channel_id=1, source_target_pairs={{0,2},{1,3},{2,0},{3,1},{4,6},{5,7},{6,4},{7,5},{8,10},{9,11},{10,... | collective-permute-start | bytes 221192 | tf_op jit(solution)/shard_map/ppermute | solution.py:797
  169.7 15.4 %collective-permute-start.32 = (bf16[19,64,256]{2,1,0:T(8,128)(2,1)S(1)}, bf16[19,64,256]{2,1,0:T(8,128)(2,1)S(1)}, u32[]{:S(2)}, u32[]{:S(2)}) collective-permute-start(bf16[19,64,256]{2,1,0:T(8,128)(2,1)S(1)} %pad_maximum_fusion.4), channel_id=1, source_target_pairs={{0,8},{4,12},{8,0},{12,4},{1,9},{5,13},{9,1},{13,5},{2,10},{6,14},... | collective-permute-start | bytes 1867784 | tf_op jit(solution)/shard_map/ppermute | solution.py:797
  170.3 6.1 %collective-permute-start.28 = (bf16[18,16,256]{2,1,0:T(8,128)(2,1)S(1)}, bf16[18,16,256]{2,1,0:T(8,128)(2,1)S(1)}, u32[]{:S(2)}, u32[]{:S(2)}) collective-permute-start(bf16[18,16,256]{2,1,0:T(8,128)(2,1)S(1)} %pad_maximum_fusion.11), channel_id=1, source_target_pairs={{0,1},{1,0},{2,3},{3,2},{4,5},{5,4},{6,7},{7,6},{8,9},{9,8},{10,11... | collective-permute-start | bytes 442376 | tf_op jit(solution)/shard_map/ppermute | solution.py:797
  173.3 11.9 %collective-permute-start.31 = (bf16[19,64,256]{2,1,0:T(8,128)(2,1)S(1)}, bf16[19,64,256]{2,1,0:T(8,128)(2,1)S(1)}, u32[]{:S(2)}, u32[]{:S(2)}) collective-permute-start(bf16[19,64,256]{2,1,0:T(8,128)(2,1)S(1)} %pad_maximum_fusion.3), channel_id=1, source_target_pairs={{0,4},{4,0},{8,12},{12,8},{1,5},{5,1},{9,13},{13,9},{2,6},{6,2},{1... | collective-permute-start | bytes 1867784 | tf_op jit(solution)/shard_map/ppermute | solution.py:797
  176.5 5.2 %collective-permute-start.29 = (bf16[9,32,256]{2,1,0:T(8,128)(2,1)S(1)}, bf16[9,32,256]{2,1,0:T(8,128)(2,1)S(1)}, u32[]{:S(2)}, u32[]{:S(2)}) collective-permute-start(bf16[9,32,256]{2,1,0:T(8,128)(2,1)S(1)} %get-tuple-element.212), channel_id=1, source_target_pairs={{0,8},{4,12},{8,0},{12,4},{1,9},{5,13},{9,1},{13,5},{2,10},{6,14},... | collective-permute-start | bytes 442376 | tf_op jit(solution)/shard_map/ppermute | solution.py:797
  177.3 7.9 %collective-permute-start.30 = (bf16[9,32,256]{2,1,0:T(8,128)(2,1)S(1)}, bf16[9,32,256]{2,1,0:T(8,128)(2,1)S(1)}, u32[]{:S(2)}, u32[]{:S(2)}) collective-permute-start(bf16[9,32,256]{2,1,0:T(8,128)(2,1)S(1)} %get-tuple-element.211), channel_id=1, source_target_pairs={{0,4},{4,0},{8,12},{12,8},{1,5},{5,1},{9,13},{13,9},{2,6},{6,2},{1... | collective-permute-start | bytes 442376 | tf_op jit(solution)/shard_map/ppermute | solution.py:797
  186.3 6.3 %collective-permute-start.35 = (bf16[19,256,256]{2,1,0:T(8,128)(2,1)S(1)}, bf16[19,256,256]{2,1,0:T(8,128)(2,1)}, u32[]{:S(2)}, u32[]{:S(2)}) collective-permute-start(bf16[19,256,256]{2,1,0:T(8,128)(2,1)S(1)} %pad_maximum_fusion.half_ref), channel_id=1, source_target_pairs={{0,16},{16,0},{1,17},{17,1},{2,18},{18,2},{3,19},{19,3},{4,20},{20... | collective-permute-start | bytes 7471112 | tf_op jit(solution)/shard_map/ppermute | solution.py:797
  186.4 9.6 %collective-permute-start.34 = (bf16[9,64,256]{2,1,0:T(8,128)(2,1)S(1)}, bf16[9,64,256]{2,1,0:T(8,128)(2,1)}, u32[]{:S(2)}, u32[]{:S(2)}) collective-permute-start(bf16[9,64,256]{2,1,0:T(8,128)(2,1)S(1)} %pad_maximum_fusion.9), channel_id=1, source_target_pairs={{0,8},{4,12},{8,0},{12,4},{1,9},{5,13},{9,1},{13,5},{2,10},{6,14},... | collective-permute-start | bytes 884744 | tf_op jit(solution)/shard_map/ppermute | solution.py:797
  187.8 9.7 %collective-permute-start.33 = (bf16[9,64,256]{2,1,0:T(8,128)(2,1)}, bf16[9,64,256]{2,1,0:T(8,128)(2,1)}, u32[]{:S(2)}, u32[]{:S(2)}) collective-permute-start(bf16[9,64,256]{2,1,0:T(8,128)(2,1)} %pad_maximum_fusion.8), channel_id=1, source_target_pairs={{0,4},{4,0},{8,12},{12,8},{1,5},{5,1},{9,13},{13,9},{2,6},{6,2},{1... | collective-permute-start | bytes 884744 | tf_op jit(solution)/shard_map/ppermute | solution.py:797
  199.8 2.9 %collective-permute-start.36 = (bf16[9,256,256]{2,1,0:T(8,128)(2,1)S(1)}, bf16[9,256,256]{2,1,0:T(8,128)(2,1)S(1)}, u32[]{:S(2)}, u32[]{:S(2)}) collective-permute-start(bf16[9,256,256]{2,1,0:T(8,128)(2,1)S(1)} %pad_maximum_fusion.1.half_ref), channel_id=1, source_target_pairs={{0,16},{16,0},{1,17},{17,1},{2,18},{18,2},{3,19},{19,3},{4,20},{20... | collective-permute-start | bytes 3538952 | tf_op jit(solution)/shard_map/ppermute | solution.py:797
  (15 other events, 89.5 us)

commit v7 on v6

--- a/solution.py
+++ b/solution.py
@@ -84,7 +84,7 @@
     return [(k, (rows, pl.ds(k * size, size))) for k in range(count)]
 
 
-def call(body, ins, outs, scratch=None, far_in=(), far_out=(), smem=(), parts=None, limit=52, cost=0):
+def call(body, ins, outs, scratch=None, far_in=(), far_out=(), smem=(), parts=None, limit=52, cost=0, anywhere=()):
     scratch, parts = scratch or {}, parts or {}
     far = (*far_in, *far_out)
     jobs = [(name, index) for name in far for index in parts.get(name, [None])]
@@ -92,6 +92,8 @@
     def spec(name):
         if name in smem:
             return pl.BlockSpec(memory_space=pltpu.SMEM)
+        if name in anywhere:
+            return pl.BlockSpec(memory_space=pl.ANY)
         return pl.BlockSpec(memory_space=pltpu.HBM if name in far else pltpu.VMEM)
 
     kinds = {**{n: shape(v.shape, v.dtype) for n, v in ins.items()}, **outs}
@@ -697,23 +699,32 @@
     copies.wait(N.out)
 
 
-def widen(half, side, taps, per, swapped, into=None):
+def widen(half, spots, side, taps, per, swapped, into=None):
     total, n, m = half.shape
     extra = total - taps * per
     order = [(t % 3 * 3 + t // 3) if swapped else t for t in range(taps)]
     jobs = [(t * per, per, 0, order[t] * per) for t in range(taps)] + [(taps * per, 1, 1, 0)] * extra
     more = list(into or [])
 
-    def body(side_ref, half_ref, *refs):
+    def body(spots_ref, half_ref, *refs):
         outs = refs[len(more) : len(more) + 1 + extra]
         narrow, full, sems = refs[len(more) + 1 + extra :]
-        lanes = pl.ds(pl.multiple_of(side_ref[0] * m, m), m)
+        lanes = pl.ds(pl.multiple_of(spots_ref[4] * m, m), m)
+        h = n // 4
+        places = [pl.ds(pl.multiple_of(spots_ref[q] * h, h), h) for q in range(4)]
         reads = [
             pltpu.make_async_copy(half_ref.at[pl.ds(at, size)], narrow.at[pl.ds(at, size)], sems.at[0, k])
             for k, (at, size, _, _) in enumerate(jobs)
         ]
         writes = [
-            pltpu.make_async_copy(full.at[pl.ds(at, size)], outs[which].at[pl.ds(to, size), :, lanes], sems.at[1, k])
+            [
+                pltpu.make_async_copy(
+                    full.at[pl.ds(at, size), pl.ds(q * h, h)],
+                    outs[which].at[pl.ds(to, size), places[q], lanes],
+                    sems.at[1 + q, k],
+                )
+                for q in range(4)
+            ]
             for k, (at, size, which, to) in enumerate(jobs)
         ]
         for read in reads:
@@ -721,8 +732,9 @@
         for k, (at, size, _, _) in enumerate(jobs):
             reads[k].wait()
             full[at : at + size] = narrow[at : at + size].astype(f32)
-            writes[k].start()
-        for write in writes:
+            for write in writes[k]:
+                write.start()
+        for write in sum(writes, []):
             write.wait()
 
     hbm = pl.BlockSpec(memory_space=pltpu.HBM)
@@ -734,12 +746,12 @@
         scratch_shapes=[
             pltpu.VMEM((total, n, m), bf16),
             pltpu.VMEM((total, n, m), f32),
-            pltpu.SemaphoreType.DMA((2, len(jobs))),
+            pltpu.SemaphoreType.DMA((5, len(jobs))),
         ],
         input_output_aliases={2 + k: k for k in range(len(more))},
         compiler_params=pltpu.CompilerParams(vmem_limit_bytes=20 * 1024 * 1024),
         cost_estimate=pl.CostEstimate(flops=0, bytes_accessed=0, transcendentals=0),
-    )(side.reshape(1), half, *more)
+    )(jnp.concatenate([spots, side.reshape(1)]), half, *more)
 
 
 def halve_kernel(r, copies):
@@ -774,7 +786,7 @@
         halve_kernel(r, copies)
 
     far_in = tuple(n for n in ins if n != N.bits)
-    out = call(body, ins, outs, far_in=far_in, far_out=tuple(outs), smem=(N.bits,), cost=cost, limit=60)
+    out = call(body, ins, outs, far_in=far_in, far_out=tuple(outs), smem=(N.bits,), cost=cost, limit=60, anywhere=(N.got0, N.got1))
     return [(out[N.sent + name], out[N.left + name]) for name in names]
 
 
@@ -864,10 +876,12 @@
         elif kind == N.rest_join:
             self.value = joined(self.value, self.got[0], *self.rest[k])
             self.value_a, self.value_b = self.value[: self.taps], self.value[self.taps :]
-        elif kind == N.plane_join:
+        elif kind == N.plane_join and k > 0:
             self.value_a = joined(self.value_a, self.got[0], *self.a[k])
             self.value_b = joined(self.value_b, self.got[1], *self.b[k])
-            self.value = jnp.concatenate([self.value_a, self.value_b], axis=1)
+        elif kind == N.plane_join:
+            pieces = self.value_a, self.got[0], self.value_b, self.got[1]
+            self.value = jnp.concatenate(pieces, axis=1)
 
     def split_rest(self, total, k):
         if k < len(self.rest):
@@ -984,7 +998,7 @@
         parts=dict(pre1=row_parts(MP, 3), prep=row_parts(MP, 3)),
     )
     xe, xo, ownp, maskp = first[N.xe], first[N.xo], first[N.ownp], first[N.maskp]
-    far_xe, far_xo, ownp_far = partner(xe, *core), partner(xo, *core), partner(ownp, *core)
+    far_xe, far_xo = partner(xe, *core), partner(xo, *core)
 
     second = call(
         second_kernel,
@@ -1024,6 +1038,8 @@
     )
     mom2 = third[N.mom2]
     tot3 = gather_sum(third[N.spread])
+    ownp_here, far3 = lax.optimization_barrier((ownp, partner(third[N.theirs], *core)))
+    ownp_far = partner(ownp_here, *core)
 
     def chunk_shapes(taps):
         dims = (taps, cin // 4, half)
@@ -1034,7 +1050,7 @@
     second_parts = call(
         weights_second_kernel,
         dict(
-            bits=bits, mine=third[N.mine], far3=partner(third[N.theirs], *core), h3=h3, h3_far=far_h3, xe=xe, xe_far=far_xe,
+            bits=bits, mine=third[N.mine], far3=far3, h3=h3, h3_far=far_h3, xe=xe, xe_far=far_xe,
             tot3=tot3, mom1=mom1, mom2=mom2, gain2=g2, gainp=gp, ownp=ownp, ownp_far=ownp_far,
         ),
         chunk_shapes(taps2),
@@ -1045,6 +1061,7 @@
             far=pltpu.VMEM((2 * MW, half), bf16),
         ),
         far_in=(N.mine, N.far3, N.h3, N.h3_far, N.xe, N.xe_far),
+        anywhere=(N.far3,),
         far_out=CHUNKS,
         smem=(N.bits,),
         parts=dict(
@@ -1108,6 +1125,7 @@
             far=pltpu.VMEM((MW, half), bf16),
         ),
         far_in=(N.mine, N.far4, N.xe, N.xe_far, N.xo, N.xo_far),
+        anywhere=(N.far4,),
         cost=20000000000,
         far_out=(*CHUNKS, N.gain_first, N.shift_first),
         smem=(N.bits,),
@@ -1140,7 +1158,8 @@
         far_out=(N.out,),
         cost=10000000000,
     )[N.out]
-    side = bit_of(*core).astype(jnp.int32)
+    side, low, high = (bits[tree2.place[step]] for step in (core, plane[0], plane[-1]))
+    spots = jnp.stack([low, 1 - low, 2 + high, 3 - high])
     grad_inputs = lockstep(tree2, tree1, beside=grad_inputs)
     while tree2.next() != (N.plane_join, 0):
         lockstep(tree2, tree1)
@@ -1155,12 +1174,12 @@
     tree2.finish()
     tree2.start()
     tree1.start()
-    grad_second = widen(tree2.got[0], 1 - side, 9, per, True, widen(tree2.value, side, 9, per, True))
+    grad_second = widen(tree2.got[0], spots, 1 - side, 9, per, True, widen(tree2.value, spots, side, 9, per, True))
     tree1.got, grad_second = lax.optimization_barrier((tree1.got, grad_second))
     grad_w2, grad_wp = grad_second
     tree1.finish()
     tree1.start()
-    (grad_w1,) = widen(tree1.got[0], 1 - side, 3, 3, False, widen(tree1.value, side, 3, 3, False))
+    (grad_w1,) = widen(tree1.got[0], spots, 1 - side, 3, 3, False, widen(tree1.value, spots, side, 3, 3, False))
 
     return (
         third[N.out],

time: 206 us -> 208 us (level)
  Pallas kernels: 67.4 us -> 70.7 us
  local copies, waits for them, and re-layouts: 3.74 us -> 6.73 us
  waiting for transfers between devices: 58.6 us -> 56.1 us
    pallas_call x4, Pallas kernels: 10.3 us -> 13.5 us  [widen(): pl.pallas_call(body, out_shape=[shape((taps * per, n, 2 * m))] + [shape((...]
    ppermute x32, waiting for transfers between devices: 35.4 us -> 32.5 us  [partner(): return lax.ppermute(value, axis, [(i, i ^ step) for i in range(count)])]
    select_n x10 -> x4, other arithmetic: 2.91 us -> 0.11 us  [joined(): jnp.where(bit, other, value)]
    unnamed x44 -> x50, local copies, waits for them, and re-layouts: 3.51 us -> 5.55 us
  transfers between devices with their start and end apart: 41 -> 41, of which waited for: 24 -> 23; matrix products, arithmetic and copies ran while one was open for 1% -> 2% of each run, Pallas kernels for 21% -> 22%
where the time goes in v7:
time: 208 us; the launch traced here: 207 us
  Pallas kernels  70.7 us (34%)
  starting transfers between devices  65.9 us (32%)
  waiting for transfers between devices  56.1 us (27%)
  local copies, waits for them, and re-layouts  6.73 us (3%)
  other arithmetic  6.04 us (3%)
    pallas_call x11, Pallas kernels, call(): pl.pallas_call(run, out_shape=list(outs.values()), in_specs=[spec(n) for...  57.1 us
    ppermute x32, starting transfers between devices, partner(): return lax.ppermute(value, axis, [(i, i ^ step) for i in range(count)])  36.4 us
    ppermute x32, waiting for transfers between devices, partner(): return lax.ppermute(value, axis, [(i, i ^ step) for i in range(count)])  32.5 us
    all_to_all x4, waiting for transfers between devices, gather_sum(): return lax.all_to_all(spread, axes, 0, 0)  21.2 us
    all_to_all x4, starting transfers between devices, gather_sum(): return lax.all_to_all(spread, axes, 0, 0)  16.7 us
    pallas_call x4, Pallas kernels, widen(): pl.pallas_call(body, out_shape=[shape((taps * per, n, 2 * m))] + [shape((...  13.5 us
    ppermute x4, starting transfers between devices, shifted(): lax.ppermute(value, axis, [(source, source + steps) for source in range(f...  12.3 us
    unnamed x50, local copies, waits for them, and re-layouts  5.55 us
  transfers between devices with their start and end apart: 41, of which 23 were waited for; matrix products, arithmetic and copies ran while one was open for 2% of the time, Pallas kernels for 22%

profile of v7, /device:TPU:0, one launch (start us, length us, event | category | flops | bytes accessed | tf_op | source)
XLA Modules:
  0.0 207.1 jit_solution(13658467048655390249)
XLA Ops:
  5.1 2.0 collective-permute-start.1
  7.9 4.8 %collective-permute-start.2 = (bf16[2,17,1,256]{3,2,1,0:T(2,128)(2,1)S(1)}, bf16[2,17,1,256]{3,2,1,0:T(2,128)(2,1)S(1)}, u32[]{:S(2)}, u32[]{:S(2)}) collective-permute-start(bf16[2,17,1,256]{3,2,1,0:T(2,128)(2,1)S(1)} %pad_maximum_fusion.10), channel_id=1, source_target_pairs={{0,4},{4,8},{8,12},{1,5},{5,9},{9,13},{2,6},{6,10},{10,14},{3,7},{... | collective-permute-start | bytes 52232 | tf_op jit(solution)/shard_map/ppermute | solution.py:796
  12.8 1.6 collective-permute-done.2.refs_2_
  15.7 4.2 %collective-permute-start.3 = (bf16[480,256]{1,0:T(8,128)(2,1)S(1)}, bf16[480,256]{1,0:T(8,128)(2,1)S(1)}, u32[]{:S(2)}, u32[]{:S(2)}) collective-permute-start(bf16[480,256]{1,0:T(8,128)(2,1)S(1)} %get-tuple-element.104), channel_id=1, source_target_pairs={{0,4},{4,8},{8,12},{1,5},{5,9},{9,13},{2,6},{6,10},{10,14},{3,7},{... | collective-permute-start | bytes 737288 | tf_op jit(solution)/shard_map/ppermute | solution.py:796
  21.2 3.4 %shard_map.206 = f32[32,1,2176]{2,1,0:T(1,128)} custom-call(bf16[2,16,32,256]{3,2,1,0:T(8,128)(2,1)S(1)} %copy-done.1, bf16[2,1,32,256]{3,2,1,0:T(8,128)(2,1)S(1)} %collective-permute-done.1.refs_1_, bf16[2,17,1,256]{3,2,1,0:T(2,128)(2,1)S(1)} %collective-permute-done.2.refs_2_, bf16[2,8,16,128]{3,2,1,0:T(8,128)(2,1)S(1)} %broadcast_in_dim.2.refs_3_, ...), custom_call_target="tpu_custom_call" | custom-call | tf_op jit(solution)/shard_map/pallas_call | solution.py:115
  24.6 7.9 %all-to-all-start = ((f32[32,1,2176]{2,1,0:T(1,128)}), f32[32,1,2176]{2,1,0:T(1,128)S(1)}, u32[]{:S(2)}, u32[]{:S(2)}) async-start(f32[32,1,2176]{2,1,0:T(1,128)} %shard_map.206), calls=%async_computation | async-start | bytes 557056 | tf_op jit(solution)/shard_map/all_to_all | solution.py:800
  32.6 5.7 %shard_map.205 = (f32[624,512]{1,0:T(8,128)}, f32[624,512]{1,0:T(8,128)}, bf16[624,768]{1,0:T(8,128)(2,1)}, bf16[672,768]{1,0:T(8,128)(2,1)}, f32[624,128]{1,0:T...) custom-call(s32[2]{0:T(128)S(1)} %add_convert_fusion.2.refs_0_, bf16[2,16,32,256]{3,2,1,0:T(8,128)(2,1)} %refs_0_.1, ...), custom_call_target="tpu_custom_call" | custom-call | flops 20000000000 | tf_op jit(solution)/shard_map/pallas_call | solution.py:115
  38.3 5.5 %all-to-all-done.refs_1_ = f32[32,1,2176]{2,1,0:T(1,128)S(1)} async-done(((f32[32,1,2176]{2,1,0:T(1,128)}), f32[32,1,2176]{2,1,0:T(1,128)S(1)}, u32[]{:S(2)}, u32[]{:S(2)}) %all-to-all-start) | async-done | bytes 278560 | tf_op jit(solution)/shard_map/all_to_all | solution.py:800
  43.8 6.3 %shard_map.207 = (bf16[624,1536]{1,0:T(8,128)(2,1)}, f32[528,512]{1,0:T(8,128)}, f32[32,1,1024]{2,1,0:T(1,128)}, f32[8,512]{1,0:T(8,128)S(1)}) custom-call(f32[624,512]{1,0:T(8,128)} %get-tuple-element.106.refs_0_.refs_3_, f32[32,1,2176]{2,1,0:T(1,128)S(1)} %all-to-all-done.refs_1_, f32[1,512]{1,0:T(1,128)S(1)} %bitcast.36, f32[1,512]{1,0:T(1,128)S(1)} %bitcast.34, ...), custom_call_target="tpu_custom_call" | custom-call | tf_op jit(solution)/shard_map/pallas_call | solution.py:115
  50.2 2.6 %all-to-all-start.1 = ((f32[32,1,1024]{2,1,0:T(1,128)}), f32[32,1,1024]{2,1,0:T(1,128)S(1)}, u32[]{:S(2)}, u32[]{:S(2)}) async-start(f32[32,1,1024]{2,1,0:T(1,128)} %get-tuple-element.114), calls=%async_computation.1 | async-start | bytes 262144 | tf_op jit(solution)/shard_map/all_to_all | solution.py:800
  53.0 7.7 %all-to-all-done.1.refs_4_ = f32[32,1,1024]{2,1,0:T(1,128)S(1)} async-done(((f32[32,1,1024]{2,1,0:T(1,128)}), f32[32,1,1024]{2,1,0:T(1,128)S(1)}, u32[]{:S(2)}, u32[]{:S(2)}) %all-to-all-start.1) | async-done | bytes 131104 | tf_op jit(solution)/shard_map/all_to_all | solution.py:800
  60.7 5.5 %shard_map.208 = (bf16[2,8,16,512]{3,2,1,0:T(8,128)(2,1)}, f32[528,512]{1,0:T(8,128)}, f32[32,1,1536]{2,1,0:T(1,128)}, f32[8,512]{1,0:T(8,128)S(1)}, f32[3,384,256]{2,1,0:T(8,128)}, /*index=5*/f32[3,384,256]{2,1,0:T(8,128)}) custom-call(s32[5]{0:T(128)S(1)} %stack.42.refs_0_, f32[528,512]{1,0:T(8,128)} %get-tuple-element.111.refs_1_.refs_2_, ...), custom_call_target="tpu_custom_call" | custom-call | tf_op jit(solution)/shard_map/pallas_call | solution.py:115
  66.8 2.8 %all-to-all-start.2 = ((f32[32,1,1536]{2,1,0:T(1,128)}), f32[32,1,1536]{2,1,0:T(1,128)S(1)}, u32[]{:S(2)}, u32[]{:S(2)}) async-start(f32[32,1,1536]{2,1,0:T(1,128)} %get-tuple-element.125), calls=%async_computation.2 | async-start | bytes 393216 | tf_op jit(solution)/shard_map/all_to_all | solution.py:800
  70.9 8.0 %all-to-all-done.2.refs_7_.refs_8_ = f32[32,1,1536]{2,1,0:T(1,128)S(1)} async-done(((f32[32,1,1536]{2,1,0:T(1,128)}), f32[32,1,1536]{2,1,0:T(1,128)S(1)}, u32[]{:S(2)}, u32[]{:S(2)}) %all-to-all-start.2) | async-done | bytes 196640 | tf_op jit(solution)/shard_map/all_to_all | solution.py:800
  78.8 8.4 %shard_map.209 = (bf16[19,64,256]{2,1,0:T(8,128)(2,1)S(1)}, f32[19,64,256]{2,1,0:T(8,128)}, bf16[19,64,256]{2,1,0:T(8,128)(2,1)}, f32[19,64,256]{2,1,0:T(8,128)}) custom-call(s32[5]{0:T(128)S(1)} %stack.42.refs_0_, f32[3,384,256]{2,1,0:T(8,128)} %get-tuple-element.120.refs_1_, f32[3,384,256]{2,1,0:T(8,128)} %copy-done.18, ...), custom_call_target="tpu_custom_call" | custom-call | tf_op jit(solution)/shard_map/pallas_call | solution.py:115
  88.3 8.6 %shard_map.211 = (f32[432,512]{1,0:T(8,128)}, f32[432,512]{1,0:T(8,128)}, f32[32,1,1024]{2,1,0:T(1,128)}, f32[2,384,256]{2,1,0:T(8,128)}, f32[2,384,256]{2,1,0:T...) custom-call(s32[5]{0:T(128)S(1)} %stack.42.refs_0_, ...), custom_call_target="tpu_custom_call" | custom-call | tf_op jit(solution)/shard_map/pallas_call | solution.py:115
  97.5 3.4 %all-to-all-start.3 = ((f32[32,1,1024]{2,1,0:T(1,128)}), f32[32,1,1024]{2,1,0:T(1,128)S(1)}, u32[]{:S(2)}, u32[]{:S(2)}) async-start(f32[32,1,1024]{2,1,0:T(1,128)} %get-tuple-element.146), calls=%async_computation.3 | async-start | bytes 262144 | tf_op jit(solution)/shard_map/all_to_all | solution.py:800
  101.0 1.9 collective-permute-done.10.refs_4_
  103.7 3.8 %shard_map.210 = (bf16[19,32,256]{2,1,0:T(8,128)(2,1)}, f32[19,32,256]{2,1,0:T(8,128)}, bf16[19,32,256]{2,1,0:T(8,128)(2,1)}, f32[19,32,256]{2,1,0:T(8,128)}) custom-call(s32[5]{0:T(128)} %copy-done.10, f32[19,64,256]{2,1,0:T(8,128)} %get-tuple-element.132.refs_1_, bf16[19,64,256]{2,1,0:T(8,128)(2,1)} %collective-permute-done.9.refs_2_, ...), custom_call_target="tpu_custom_call" | custom-call | flops 20000000000 | tf_op jit(solution)/shard_map/pallas_call | solution.py:115
  109.5 6.9 %shard_map.212 = (bf16[9,64,256]{2,1,0:T(8,128)(2,1)S(1)}, f32[9,64,256]{2,1,0:T(8,128)S(1)}, bf16[9,64,256]{2,1,0:T(8,128)(2,1)S(1)}, f32[9,64,256]{2,1,0:T(8,1...) custom-call(s32[5]{0:T(128)S(1)} %copy-done.11, f32[2,384,256]{2,1,0:T(8,128)} %get-tuple-element.143.refs_1_, ...), custom_call_target="tpu_custom_call" | custom-call | flops 20000000000 | tf_op jit(solution)/shard_map/pallas_call | solution.py:115
  116.7 1.4 convert_add_fusion.1
  118.3 1.5 collective-permute-start.15
  119.8 1.5 collective-permute-start.16
  121.9 6.4 %shard_map.213 = bf16[2,16,32,256]{3,2,1,0:T(8,128)(2,1)} custom-call(f32[432,512]{1,0:T(8,128)S(1)} %copy-done.14, f32[432,512]{1,0:T(8,128)} %get-tuple-element.157.refs_1_, bf16[384,512]{1,0:T(8,128)(2,1)S(1)} %get-tuple-element.158.refs_2_, bf16[3,768,512]{2,1,0:T(8,128)(2,1)} %bitcast.50, bf16[256,512]{1,0:T(8,128)(2,1)S(1)} %copy-done.5, ...), custom_call_target="tpu_custom_call" | custom-call | flops 10000000000 | tf_op jit(solution)/shard_map/pallas_call | solution.py:115
  128.8 1.3 collective-permute-start.20
  130.3 1.8 collective-permute-start.18
  134.0 3.5 %collective-permute-done.19 = bf16[9,32,256]{2,1,0:T(8,128)(2,1)S(1)} collective-permute-done((bf16[9,32,256]{2,1,0:T(8,128)(2,1)S(1)}, bf16[9,32,256]{2,1,0:T(8,128)(2,1)S(1)}, u32[]{:S(2)}, u32[]{:S(2)}) %collective-permute-start.19) | collective-permute-done | bytes 147488 | tf_op jit(solution)/shard_map/ppermute | solution.py:809
  138.9 4.1 %collective-permute-start.22 = (bf16[18,16,256]{2,1,0:T(8,128)(2,1)S(1)}, bf16[18,16,256]{2,1,0:T(8,128)(2,1)S(1)}, u32[]{:S(2)}, u32[]{:S(2)}) collective-permute-start(bf16[18,16,256]{2,1,0:T(8,128)(2,1)S(1)} %select_convert_fusion.2), channel_id=1, source_target_pairs={{0,1},{1,0},{2,3},{3,2},{4,5},{5,4},{6,7},{7,6},{8,9},{9,8},{10,11... | collective-permute-start | bytes 442376 | tf_op jit(solution)/shard_map/ppermute | solution.py:809
  143.0 5.5 %collective-permute-done.22 = bf16[18,16,256]{2,1,0:T(8,128)(2,1)S(1)} collective-permute-done((bf16[18,16,256]{2,1,0:T(8,128)(2,1)S(1)}, bf16[18,16,256]{2,1,0:T(8,128)(2,1)S(1)}, u32[]{:S(2)}, u32[]{:S(2)}) %collective-permute-start.22) | collective-permute-done | bytes 147488 | tf_op jit(solution)/shard_map/ppermute | solution.py:809
  148.5 1.4 collective-permute-start.23
  150.0 2.5 %collective-permute-start.24 = (bf16[18,8,256]{2,1,0:T(8,128)(2,1)S(1)}, bf16[18,8,256]{2,1,0:T(8,128)(2,1)S(1)}, u32[]{:S(2)}, u32[]{:S(2)}) collective-permute-start(bf16[18,8,256]{2,1,0:T(8,128)(2,1)S(1)} %select_convert_fusion.5), channel_id=1, source_target_pairs={{0,2},{1,3},{2,0},{3,1},{4,6},{5,7},{6,4},{7,5},{8,10},{9,11},{10,... | collective-permute-start | bytes 221192 | tf_op jit(solution)/shard_map/ppermute | solution.py:809
  152.5 3.4 %collective-permute-done.24 = bf16[18,8,256]{2,1,0:T(8,128)(2,1)S(1)} collective-permute-done((bf16[18,8,256]{2,1,0:T(8,128)(2,1)S(1)}, bf16[18,8,256]{2,1,0:T(8,128)(2,1)S(1)}, u32[]{:S(2)}, u32[]{:S(2)}) %collective-permute-start.24) | collective-permute-done | bytes 73760 | tf_op jit(solution)/shard_map/ppermute | solution.py:809
  158.4 1.5 collective-permute-start.26
  160.0 2.3 %collective-permute-start.27 = (bf16[18,8,256]{2,1,0:T(8,128)(2,1)S(1)}, bf16[18,8,256]{2,1,0:T(8,128)(2,1)S(1)}, u32[]{:S(2)}, u32[]{:S(2)}) collective-permute-start(bf16[18,8,256]{2,1,0:T(8,128)(2,1)S(1)} %add_convert_fusion.1), channel_id=1, source_target_pairs={{0,2},{1,3},{2,0},{3,1},{4,6},{5,7},{6,4},{7,5},{8,10},{9,11},{10,... | collective-permute-start | bytes 221192 | tf_op jit(solution)/shard_map/ppermute | solution.py:809
  162.3 3.0 %collective-permute-done.27 = bf16[18,8,256]{2,1,0:T(8,128)(2,1)S(1)} collective-permute-done((bf16[18,8,256]{2,1,0:T(8,128)(2,1)S(1)}, bf16[18,8,256]{2,1,0:T(8,128)(2,1)S(1)}, u32[]{:S(2)}, u32[]{:S(2)}) %collective-permute-start.27) | collective-permute-done | bytes 73760 | tf_op jit(solution)/shard_map/ppermute | solution.py:809
  165.3 2.4 %collective-permute-done.25 = bf16[19,32,256]{2,1,0:T(8,128)(2,1)S(1)} collective-permute-done((bf16[19,32,256]{2,1,0:T(8,128)(2,1)S(1)}, bf16[19,32,256]{2,1,0:T(8,128)(2,1)S(1)}, u32[]{:S(2)}, u32[]{:S(2)}) %collective-permute-start.25) | collective-permute-done | bytes 311328 | tf_op jit(solution)/shard_map/ppermute | solution.py:809
  169.2 3.1 %collective-permute-start.28 = (bf16[18,16,256]{2,1,0:T(8,128)(2,1)S(1)}, bf16[18,16,256]{2,1,0:T(8,128)(2,1)S(1)}, u32[]{:S(2)}, u32[]{:S(2)}) collective-permute-start(bf16[18,16,256]{2,1,0:T(8,128)(2,1)S(1)} %pad_maximum_fusion.9), channel_id=1, source_target_pairs={{0,1},{1,0},{2,3},{3,2},{4,5},{5,4},{6,7},{7,6},{8,9},{9,8},{10,11... | collective-permute-start | bytes 442376 | tf_op jit(solution)/shard_map/ppermute | solution.py:809
  172.3 1.5 collective-permute-start.31
  173.8 1.6 collective-permute-done.28
  176.2 2.0 collective-permute-start.30
  178.2 2.6 %collective-permute-done.29 = bf16[9,32,256]{2,1,0:T(8,128)(2,1)S(1)} collective-permute-done((bf16[9,32,256]{2,1,0:T(8,128)(2,1)S(1)}, bf16[9,32,256]{2,1,0:T(8,128)(2,1)S(1)}, u32[]{:S(2)}, u32[]{:S(2)}) %collective-permute-start.29) | collective-permute-done | bytes 147488 | tf_op jit(solution)/shard_map/ppermute | solution.py:809
  180.7 3.5 %collective-permute-done.30 = bf16[9,32,256]{2,1,0:T(8,128)(2,1)S(1)} collective-permute-done((bf16[9,32,256]{2,1,0:T(8,128)(2,1)S(1)}, bf16[9,32,256]{2,1,0:T(8,128)(2,1)S(1)}, u32[]{:S(2)}, u32[]{:S(2)}) %collective-permute-start.30) | collective-permute-done | bytes 147488 | tf_op jit(solution)/shard_map/ppermute | solution.py:809
  187.3 2.0 collective-permute-start.33
  189.5 3.6 %shard_map.214 = (f32[18,256,512]{2,1,0:T(8,128)}, f32[1,256,512]{2,1,0:T(8,128)}) custom-call(s32[5]{0:T(128)S(1)} %concatenate.66.spots_ref, bf16[19,256,256]{2,1,0:T(8,128)(2,1)S(1)} %constant_dynamic-update-slice_fusion.half_ref), custom_call_target="tpu_custom_call" | custom-call | tf_op jit(solution)/shard_map/pallas_call | solution.py:741
  193.1 4.2 %shard_map.215 = (f32[18,256,512]{2,1,0:T(8,128)}, f32[1,256,512]{2,1,0:T(8,128)}) custom-call(s32[5]{0:T(128)S(1)} %concatenate.55.spots_ref, bf16[19,256,256]{2,1,0:T(8,128)(2,1)} %collective-permute-done.35.half_ref, f32[18,256,512]{2,1,0:T(8,128)} %get-tuple-element.181.refs_0_, ...), custom_call_target="tpu_custom_call", output_to_operand_aliasing={{0}: (2, {}), {1}: (3, {})} | custom-call | tf_op jit(solution)/shard_map/pallas_call | solution.py:741
  197.3 1.7 constant_dynamic-update-slice_fusion.9
  201.1 3.1 %shard_map.216.refs_0_ = f32[9,256,512]{2,1,0:T(8,128)} custom-call(s32[5]{0:T(128)S(1)} %concatenate.66.spots_ref, bf16[9,256,256]{2,1,0:T(8,128)(2,1)} %constant_dynamic-update-slice_fusion.6.half_ref), custom_call_target="tpu_custom_call" | custom-call | tf_op jit(solution)/shard_map/pallas_call | solution.py:741
  204.2 2.7 %shard_map.217 = f32[9,256,512]{2,1,0:T(8,128)} custom-call(s32[5]{0:T(128)S(1)} %concatenate.55.spots_ref, bf16[9,256,256]{2,1,0:T(8,128)(2,1)S(1)} %collective-permute-done.36.half_ref, f32[9,256,512]{2,1,0:T(8,128)} %shard_map.216.refs_0_), custom_call_target="tpu_custom_call", output_to_operand_aliasing={{}: (2, {})} | custom-call | tf_op jit(solution)/shard_map/pallas_call | solution.py:741
  (144 shorter events, 29.7 us)
Async XLA Ops:
  3.5 17.7 %copy-start.1 = (bf16[2,16,32,256]{3,2,1,0:T(8,128)(2,1)S(1)}, bf16[2,16,32,256]{3,2,1,0:T(8,128)(2,1)}, u32[]{:S(2)}) copy-start(bf16[2,16,32,256]{3,2,1,0:T(8,128)(2,1)} %refs_0_.1) | copy-start | bytes 1572868
  3.5 17.7 %copy-start.5 = (bf16[256,512]{1,0:T(8,128)(2,1)S(1)}, bf16[256,512]{1,0:T(8,128)(2,1)}, u32[]{:S(2)}) copy-start(bf16[256,512]{1,0:T(8,128)(2,1)} %refs_4_.1) | copy-start | bytes 786436
  4.5 9.8 %collective-permute-start = (bf16[672,256]{1,0:T(8,128)(2,1)S(1)}, bf16[672,256]{1,0:T(8,128)(2,1)S(1)}, u32[]{:S(2)}, u32[]{:S(2)}) collective-permute-start(bf16[672,256]{1,0:T(8,128)(2,1)S(1)} %shard_map.203), channel_id=1, source_target_pairs={{0,16},{16,0},{1,17},{17,1},{2,18},{18,2},{3,19},{19,3},{4,20},{20... | collective-permute-start | bytes 1032200 | tf_op jit(solution)/shard_map/ppermute | solution.py:940
  5.1 2.8 %collective-permute-start.1 = (bf16[2,1,32,256]{3,2,1,0:T(8,128)(2,1)S(1)}, bf16[2,1,32,256]{3,2,1,0:T(8,128)(2,1)S(1)}, u32[]{:S(2)}, u32[]{:S(2)}) collective-permute-start(bf16[2,1,32,256]{3,2,1,0:T(8,128)(2,1)S(1)} %slice.57), channel_id=1, source_target_pairs={{0,16},{1,17},{2,18},{3,19},{4,20},{5,21},{6,22},{7,23},{8,24},{9,... | collective-permute-start | bytes 98312 | tf_op jit(solution)/shard_map/ppermute | solution.py:796
  7.9 6.4 %collective-permute-start.2 = (bf16[2,17,1,256]{3,2,1,0:T(2,128)(2,1)S(1)}, bf16[2,17,1,256]{3,2,1,0:T(2,128)(2,1)S(1)}, u32[]{:S(2)}, u32[]{:S(2)}) collective-permute-start(bf16[2,17,1,256]{3,2,1,0:T(2,128)(2,1)S(1)} %pad_maximum_fusion.10), channel_id=1, source_target_pairs={{0,4},{4,8},{8,12},{1,5},{5,9},{9,13},{2,6},{6,10},{10,14},{3,7},{... | collective-permute-start | bytes 52232 | tf_op jit(solution)/shard_map/ppermute | solution.py:796
  15.7 16.9 %collective-permute-start.3 = (bf16[480,256]{1,0:T(8,128)(2,1)S(1)}, bf16[480,256]{1,0:T(8,128)(2,1)S(1)}, u32[]{:S(2)}, u32[]{:S(2)}) collective-permute-start(bf16[480,256]{1,0:T(8,128)(2,1)S(1)} %get-tuple-element.104), channel_id=1, source_target_pairs={{0,4},{4,8},{8,12},{1,5},{5,9},{9,13},{2,6},{6,10},{10,14},{3,7},{... | collective-permute-start | bytes 737288 | tf_op jit(solution)/shard_map/ppermute | solution.py:796
  19.9 12.7 %collective-permute-start.4 = (bf16[480,256]{1,0:T(8,128)(2,1)S(1)}, bf16[480,256]{1,0:T(8,128)(2,1)S(1)}, u32[]{:S(2)}, u32[]{:S(2)}) collective-permute-start(bf16[480,256]{1,0:T(8,128)(2,1)S(1)} %get-tuple-element.105), channel_id=1, source_target_pairs={{4,0},{8,4},{12,8},{5,1},{9,5},{13,9},{6,2},{10,6},{14,10},{7,3},{... | collective-permute-start | bytes 737288 | tf_op jit(solution)/shard_map/ppermute | solution.py:796
  24.6 19.2 %all-to-all-start = ((f32[32,1,2176]{2,1,0:T(1,128)}), f32[32,1,2176]{2,1,0:T(1,128)S(1)}, u32[]{:S(2)}, u32[]{:S(2)}) async-start(f32[32,1,2176]{2,1,0:T(1,128)} %shard_map.206), calls=%async_computation | async-start | bytes 557056 | tf_op jit(solution)/shard_map/all_to_all | solution.py:800
  43.8 16.9 %copy-start.6 = (f32[512]{0:T(512)S(1)}, f32[512]{0:T(512)}, u32[]{:S(2)}) copy-start(f32[512]{0:T(512)} %param.17) | copy-start | bytes 6148
  43.8 16.9 %copy-start.7 = (f32[512]{0:T(512)S(1)}, f32[512]{0:T(512)}, u32[]{:S(2)}) copy-start(f32[512]{0:T(512)} %param.20) | copy-start | bytes 6148
  43.8 16.9 %copy-start.12 = (f32[512]{0:T(512)S(1)}, f32[512]{0:T(512)}, u32[]{:S(2)}) copy-start(f32[512]{0:T(512)} %param.18) | copy-start | bytes 6148
  43.8 16.9 %copy-start.13 = (f32[512]{0:T(512)S(1)}, f32[512]{0:T(512)}, u32[]{:S(2)}) copy-start(f32[512]{0:T(512)} %param.21) | copy-start | bytes 6148
  50.1 10.6 %collective-permute-start.5 = (bf16[624,1536]{1,0:T(8,128)(2,1)}, bf16[624,1536]{1,0:T(8,128)(2,1)S(1)}, u32[]{:S(2)}, u32[]{:S(2)}) collective-permute-start(bf16[624,1536]{1,0:T(8,128)(2,1)} %get-tuple-element.115.refs_3_), channel_id=1, source_target_pairs={{0,16},{16,0},{1,17},{17,1},{2,18},{18,2},{3,19},{19,3},{4,20},{20... | collective-permute-start | bytes 5750792 | tf_op jit(solution)/shard_map/ppermute | solution.py:809
  50.2 10.5 %all-to-all-start.1 = ((f32[32,1,1024]{2,1,0:T(1,128)}), f32[32,1,1024]{2,1,0:T(1,128)S(1)}, u32[]{:S(2)}, u32[]{:S(2)}) async-start(f32[32,1,1024]{2,1,0:T(1,128)} %get-tuple-element.114), calls=%async_computation.1 | async-start | bytes 262144 | tf_op jit(solution)/shard_map/all_to_all | solution.py:800
  52.9 35.4 %copy-start.10 = (s32[5]{0:T(128)}, s32[5]{0:T(128)S(1)}, u32[]{:S(2)}) copy-start(s32[5]{0:T(128)S(1)} %stack.42.refs_0_) | copy-start | bytes 64
  66.3 4.0 %collective-permute-start.6 = (f32[3,384,256]{2,1,0:T(8,128)}, f32[3,384,256]{2,1,0:T(8,128)S(1)}, u32[]{:S(2)}, u32[]{:S(2)}) collective-permute-start(f32[3,384,256]{2,1,0:T(8,128)} %get-tuple-element.121), channel_id=1, source_target_pairs={{0,16},{16,0},{1,17},{17,1},{2,18},{18,2},{3,19},{19,3},{4,20},{20... | collective-permute-start | bytes 3538952 | tf_op jit(solution)/shard_map/ppermute | solution.py:809
  66.3 4.5 %collective-permute-start.7 = (bf16[624,768]{1,0:T(8,128)(2,1)}, bf16[624,768]{1,0:T(8,128)(2,1)}, u32[]{:S(2)}, u32[]{:S(2)}) collective-permute-start(bf16[624,768]{1,0:T(8,128)(2,1)} %get-tuple-element.124.refs_5_.refs_3_), channel_id=1, source_target_pairs={{0,16},{16,0},{1,17},{17,1},{2,18},{18,2},{3,19},{19,3},{4,20},{20... | collective-permute-start | bytes 2875400 | tf_op jit(solution)/shard_map/ppermute | solution.py:809
  66.8 12.0 %all-to-all-start.2 = ((f32[32,1,1536]{2,1,0:T(1,128)}), f32[32,1,1536]{2,1,0:T(1,128)S(1)}, u32[]{:S(2)}, u32[]{:S(2)}) async-start(f32[32,1,1536]{2,1,0:T(1,128)} %get-tuple-element.125), calls=%async_computation.2 | async-start | bytes 393216 | tf_op jit(solution)/shard_map/all_to_all | solution.py:800
  70.3 8.6 %collective-permute-start.8 = (f32[624,128]{1,0:T(8,128)S(1)}, f32[624,128]{1,0:T(8,128)S(1)}, u32[]{:S(2)}, u32[]{:S(2)}) collective-permute-start(f32[624,128]{1,0:T(8,128)S(1)} %get-tuple-element.127.refs_5_.refs_10_.refs_12_.refs_14_), channel_id=1, source_target_pairs={{0,16},{16,0},{1,17},{17,1},{2,18},{18,2},{3,19},{19,3},{4,20},{20... | collective-permute-start | bytes 958472 | tf_op jit(solution)/shard_map/ppermute | solution.py:809
  87.3 15.6 %collective-permute-start.10 = (bf16[19,64,256]{2,1,0:T(8,128)(2,1)}, bf16[19,64,256]{2,1,0:T(8,128)(2,1)S(1)}, u32[]{:S(2)}, u32[]{:S(2)}) collective-permute-start(bf16[19,64,256]{2,1,0:T(8,128)(2,1)} %get-tuple-element.135), channel_id=1, source_target_pairs={{0,8},{4,12},{8,0},{12,4},{1,9},{5,13},{9,1},{13,5},{2,10},{6,14},... | collective-permute-start | bytes 1867784 | tf_op jit(solution)/shard_map/ppermute | solution.py:809
  88.2 15.2 %collective-permute-start.9 = (bf16[19,64,256]{2,1,0:T(8,128)(2,1)S(1)}, bf16[19,64,256]{2,1,0:T(8,128)(2,1)}, u32[]{:S(2)}, u32[]{:S(2)}) collective-permute-start(bf16[19,64,256]{2,1,0:T(8,128)(2,1)S(1)} %get-tuple-element.133), channel_id=1, source_target_pairs={{0,4},{4,0},{8,12},{12,8},{1,5},{5,1},{9,13},{13,9},{2,6},{6,2},{1... | collective-permute-start | bytes 1867784 | tf_op jit(solution)/shard_map/ppermute | solution.py:809
  88.3 21.1 %collective-permute-start.14 = (bf16[672,768]{1,0:T(8,128)(2,1)}, bf16[672,768]{1,0:T(8,128)(2,1)}, u32[]{:S(2)}, u32[]{:S(2)}) collective-permute-start(bf16[672,768]{1,0:T(8,128)(2,1)} %get-tuple-element.145.refs_5_), channel_id=1, source_target_pairs={{0,16},{16,0},{1,17},{17,1},{2,18},{18,2},{3,19},{19,3},{4,20},{20... | collective-permute-start | bytes 3096584 | tf_op jit(solution)/shard_map/ppermute | solution.py:809
  97.0 12.5 %collective-permute-start.13 = (f32[2,384,256]{2,1,0:T(8,128)}, f32[2,384,256]{2,1,0:T(8,128)}, u32[]{:S(2)}, u32[]{:S(2)}) collective-permute-start(f32[2,384,256]{2,1,0:T(8,128)} %get-tuple-element.144), channel_id=1, source_target_pairs={{0,16},{16,0},{1,17},{17,1},{2,18},{18,2},{3,19},{19,3},{4,20},{20... | collective-permute-start | bytes 2359304 | tf_op jit(solution)/shard_map/ppermute | solution.py:809
  97.5 12.0 %all-to-all-start.3 = ((f32[32,1,1024]{2,1,0:T(1,128)}), f32[32,1,1024]{2,1,0:T(1,128)S(1)}, u32[]{:S(2)}, u32[]{:S(2)}) async-start(f32[32,1,1024]{2,1,0:T(1,128)} %get-tuple-element.146), calls=%async_computation.3 | async-start | bytes 262144 | tf_op jit(solution)/shard_map/all_to_all | solution.py:800
  107.5 8.8 %collective-permute-start.11 = (bf16[19,32,256]{2,1,0:T(8,128)(2,1)}, bf16[19,32,256]{2,1,0:T(8,128)(2,1)S(1)}, u32[]{:S(2)}, u32[]{:S(2)}) collective-permute-start(bf16[19,32,256]{2,1,0:T(8,128)(2,1)} %get-tuple-element.141), channel_id=1, source_target_pairs={{0,8},{4,12},{8,0},{12,4},{1,9},{5,13},{9,1},{13,5},{2,10},{6,14},... | collective-permute-start | bytes 933896 | tf_op jit(solution)/shard_map/ppermute | solution.py:809
  108.6 8.2 %collective-permute-start.12 = (bf16[19,32,256]{2,1,0:T(8,128)(2,1)}, bf16[19,32,256]{2,1,0:T(8,128)(2,1)}, u32[]{:S(2)}, u32[]{:S(2)}) collective-permute-start(bf16[19,32,256]{2,1,0:T(8,128)(2,1)} %get-tuple-element.142), channel_id=1, source_target_pairs={{0,4},{4,0},{8,12},{12,8},{1,5},{5,1},{9,13},{13,9},{2,6},{6,2},{1... | collective-permute-start | bytes 933896 | tf_op jit(solution)/shard_map/ppermute | solution.py:809
  118.3 10.4 %collective-permute-start.15 = (bf16[38,16,256]{2,1,0:T(8,128)(2,1)S(1)}, bf16[38,16,256]{2,1,0:T(8,128)(2,1)S(1)}, u32[]{:S(2)}, u32[]{:S(2)}) collective-permute-start(bf16[38,16,256]{2,1,0:T(8,128)(2,1)S(1)} %select_convert_fusion), channel_id=1, source_target_pairs={{0,1},{1,0},{2,3},{3,2},{4,5},{5,4},{6,7},{7,6},{8,9},{9,8},{10,11... | collective-permute-start | bytes 933896 | tf_op jit(solution)/shard_map/ppermute | solution.py:809
  119.8 8.4 %collective-permute-start.16 = (bf16[9,64,256]{2,1,0:T(8,128)(2,1)S(1)}, bf16[9,64,256]{2,1,0:T(8,128)(2,1)S(1)}, u32[]{:S(2)}, u32[]{:S(2)}) collective-permute-start(bf16[9,64,256]{2,1,0:T(8,128)(2,1)S(1)} %get-tuple-element.154), channel_id=1, source_target_pairs={{0,4},{4,0},{8,12},{12,8},{1,5},{5,1},{9,13},{13,9},{2,6},{6,2},{1... | collective-permute-start | bytes 884744 | tf_op jit(solution)/shard_map/ppermute | solution.py:809
  121.3 7.4 %collective-permute-start.17 = (bf16[9,64,256]{2,1,0:T(8,128)(2,1)S(1)}, bf16[9,64,256]{2,1,0:T(8,128)(2,1)S(1)}, u32[]{:S(2)}, u32[]{:S(2)}) collective-permute-start(bf16[9,64,256]{2,1,0:T(8,128)(2,1)S(1)} %get-tuple-element.155), channel_id=1, source_target_pairs={{0,8},{4,12},{8,0},{12,4},{1,9},{5,13},{9,1},{13,5},{2,10},{6,14},... | collective-permute-start | bytes 884744 | tf_op jit(solution)/shard_map/ppermute | solution.py:809
  128.8 5.2 %collective-permute-start.20 = (bf16[9,32,256]{2,1,0:T(8,128)(2,1)S(1)}, bf16[9,32,256]{2,1,0:T(8,128)(2,1)S(1)}, u32[]{:S(2)}, u32[]{:S(2)}) collective-permute-start(bf16[9,32,256]{2,1,0:T(8,128)(2,1)S(1)} %select_convert_fusion.3), channel_id=1, source_target_pairs={{0,4},{4,0},{8,12},{12,8},{1,5},{5,1},{9,13},{13,9},{2,6},{6,2},{1... | collective-permute-start | bytes 442376 | tf_op jit(solution)/shard_map/ppermute | solution.py:809
  130.3 7.4 %collective-permute-start.18 = (bf16[38,8,256]{2,1,0:T(8,128)(2,1)S(1)}, bf16[38,8,256]{2,1,0:T(8,128)(2,1)S(1)}, u32[]{:S(2)}, u32[]{:S(2)}) collective-permute-start(bf16[38,8,256]{2,1,0:T(8,128)(2,1)S(1)} %select_convert_fusion.1), channel_id=1, source_target_pairs={{0,2},{1,3},{2,0},{3,1},{4,6},{5,7},{6,4},{7,5},{8,10},{9,11},{10,... | collective-permute-start | bytes 466952 | tf_op jit(solution)/shard_map/ppermute | solution.py:809
  132.2 5.2 %collective-permute-start.19 = (bf16[9,32,256]{2,1,0:T(8,128)(2,1)S(1)}, bf16[9,32,256]{2,1,0:T(8,128)(2,1)S(1)}, u32[]{:S(2)}, u32[]{:S(2)}) collective-permute-start(bf16[9,32,256]{2,1,0:T(8,128)(2,1)S(1)} %select_convert_fusion.4), channel_id=1, source_target_pairs={{0,8},{4,12},{8,0},{12,4},{1,9},{5,13},{9,1},{13,5},{2,10},{6,14},... | collective-permute-start | bytes 442376 | tf_op jit(solution)/shard_map/ppermute | solution.py:809
  137.9 10.6 %collective-permute-start.21 = (bf16[38,8,256]{2,1,0:T(8,128)(2,1)S(1)}, bf16[38,8,256]{2,1,0:T(8,128)(2,1)S(1)}, u32[]{:S(2)}, u32[]{:S(2)}) collective-permute-start(bf16[38,8,256]{2,1,0:T(8,128)(2,1)S(1)} %add_convert_fusion), channel_id=1, source_target_pairs={{0,2},{1,3},{2,0},{3,1},{4,6},{5,7},{6,4},{7,5},{8,10},{9,11},{10,... | collective-permute-start | bytes 466952 | tf_op jit(solution)/shard_map/ppermute | solution.py:809
  138.9 9.5 %collective-permute-start.22 = (bf16[18,16,256]{2,1,0:T(8,128)(2,1)S(1)}, bf16[18,16,256]{2,1,0:T(8,128)(2,1)S(1)}, u32[]{:S(2)}, u32[]{:S(2)}) collective-permute-start(bf16[18,16,256]{2,1,0:T(8,128)(2,1)S(1)} %select_convert_fusion.2), channel_id=1, source_target_pairs={{0,1},{1,0},{2,3},{3,2},{4,5},{5,4},{6,7},{7,6},{8,9},{9,8},{10,11... | collective-permute-start | bytes 442376 | tf_op jit(solution)/shard_map/ppermute | solution.py:809
  148.5 8.5 %collective-permute-start.23 = (bf16[38,16,256]{2,1,0:T(8,128)(2,1)S(1)}, bf16[38,16,256]{2,1,0:T(8,128)(2,1)S(1)}, u32[]{:S(2)}, u32[]{:S(2)}) collective-permute-start(bf16[38,16,256]{2,1,0:T(8,128)(2,1)S(1)} %pad_maximum_fusion.4), channel_id=1, source_target_pairs={{0,1},{1,0},{2,3},{3,2},{4,5},{5,4},{6,7},{7,6},{8,9},{9,8},{10,11... | collective-permute-start | bytes 933896 | tf_op jit(solution)/shard_map/ppermute | solution.py:809
  150.0 5.9 %collective-permute-start.24 = (bf16[18,8,256]{2,1,0:T(8,128)(2,1)S(1)}, bf16[18,8,256]{2,1,0:T(8,128)(2,1)S(1)}, u32[]{:S(2)}, u32[]{:S(2)}) collective-permute-start(bf16[18,8,256]{2,1,0:T(8,128)(2,1)S(1)} %select_convert_fusion.5), channel_id=1, source_target_pairs={{0,2},{1,3},{2,0},{3,1},{4,6},{5,7},{6,4},{7,5},{8,10},{9,11},{10,... | collective-permute-start | bytes 221192 | tf_op jit(solution)/shard_map/ppermute | solution.py:809
  157.3 10.3 %collective-permute-start.25 = (bf16[19,32,256]{2,1,0:T(8,128)(2,1)S(1)}, bf16[19,32,256]{2,1,0:T(8,128)(2,1)S(1)}, u32[]{:S(2)}, u32[]{:S(2)}) collective-permute-start(bf16[19,32,256]{2,1,0:T(8,128)(2,1)S(1)} %get-tuple-element.204), channel_id=1, source_target_pairs={{0,8},{4,12},{8,0},{12,4},{1,9},{5,13},{9,1},{13,5},{2,10},{6,14},... | collective-permute-start | bytes 933896 | tf_op jit(solution)/shard_map/ppermute | solution.py:809
  158.4 9.9 %collective-permute-start.26 = (bf16[19,32,256]{2,1,0:T(8,128)(2,1)S(1)}, bf16[19,32,256]{2,1,0:T(8,128)(2,1)S(1)}, u32[]{:S(2)}, u32[]{:S(2)}) collective-permute-start(bf16[19,32,256]{2,1,0:T(8,128)(2,1)S(1)} %get-tuple-element.203), channel_id=1, source_target_pairs={{0,4},{4,0},{8,12},{12,8},{1,5},{5,1},{9,13},{13,9},{2,6},{6,2},{1... | collective-permute-start | bytes 933896 | tf_op jit(solution)/shard_map/ppermute | solution.py:809
  160.0 5.3 %collective-permute-start.27 = (bf16[18,8,256]{2,1,0:T(8,128)(2,1)S(1)}, bf16[18,8,256]{2,1,0:T(8,128)(2,1)S(1)}, u32[]{:S(2)}, u32[]{:S(2)}) collective-permute-start(bf16[18,8,256]{2,1,0:T(8,128)(2,1)S(1)} %add_convert_fusion.1), channel_id=1, source_target_pairs={{0,2},{1,3},{2,0},{3,1},{4,6},{5,7},{6,4},{7,5},{8,10},{9,11},{10,... | collective-permute-start | bytes 221192 | tf_op jit(solution)/shard_map/ppermute | solution.py:809
  168.4 15.8 %collective-permute-start.32 = (bf16[19,64,256]{2,1,0:T(8,128)(2,1)S(1)}, bf16[19,64,256]{2,1,0:T(8,128)(2,1)S(1)}, u32[]{:S(2)}, u32[]{:S(2)}) collective-permute-start(bf16[19,64,256]{2,1,0:T(8,128)(2,1)S(1)} %pad_maximum_fusion.2), channel_id=1, source_target_pairs={{0,8},{4,12},{8,0},{12,4},{1,9},{5,13},{9,1},{13,5},{2,10},{6,14},... | collective-permute-start | bytes 1867784 | tf_op jit(solution)/shard_map/ppermute | solution.py:809
  169.2 6.2 %collective-permute-start.28 = (bf16[18,16,256]{2,1,0:T(8,128)(2,1)S(1)}, bf16[18,16,256]{2,1,0:T(8,128)(2,1)S(1)}, u32[]{:S(2)}, u32[]{:S(2)}) collective-permute-start(bf16[18,16,256]{2,1,0:T(8,128)(2,1)S(1)} %pad_maximum_fusion.9), channel_id=1, source_target_pairs={{0,1},{1,0},{2,3},{3,2},{4,5},{5,4},{6,7},{7,6},{8,9},{9,8},{10,11... | collective-permute-start | bytes 442376 | tf_op jit(solution)/shard_map/ppermute | solution.py:809
  172.3 11.9 %collective-permute-start.31 = (bf16[19,64,256]{2,1,0:T(8,128)(2,1)S(1)}, bf16[19,64,256]{2,1,0:T(8,128)(2,1)S(1)}, u32[]{:S(2)}, u32[]{:S(2)}) collective-permute-start(bf16[19,64,256]{2,1,0:T(8,128)(2,1)S(1)} %pad_maximum_fusion.1), channel_id=1, source_target_pairs={{0,4},{4,0},{8,12},{12,8},{1,5},{5,1},{9,13},{13,9},{2,6},{6,2},{1... | collective-permute-start | bytes 1867784 | tf_op jit(solution)/shard_map/ppermute | solution.py:809
  175.5 5.2 %collective-permute-start.29 = (bf16[9,32,256]{2,1,0:T(8,128)(2,1)S(1)}, bf16[9,32,256]{2,1,0:T(8,128)(2,1)S(1)}, u32[]{:S(2)}, u32[]{:S(2)}) collective-permute-start(bf16[9,32,256]{2,1,0:T(8,128)(2,1)S(1)} %get-tuple-element.212), channel_id=1, source_target_pairs={{0,8},{4,12},{8,0},{12,4},{1,9},{5,13},{9,1},{13,5},{2,10},{6,14},... | collective-permute-start | bytes 442376 | tf_op jit(solution)/shard_map/ppermute | solution.py:809
  176.2 8.0 %collective-permute-start.30 = (bf16[9,32,256]{2,1,0:T(8,128)(2,1)S(1)}, bf16[9,32,256]{2,1,0:T(8,128)(2,1)S(1)}, u32[]{:S(2)}, u32[]{:S(2)}) collective-permute-start(bf16[9,32,256]{2,1,0:T(8,128)(2,1)S(1)} %get-tuple-element.211), channel_id=1, source_target_pairs={{0,4},{4,0},{8,12},{12,8},{1,5},{5,1},{9,13},{13,9},{2,6},{6,2},{1... | collective-permute-start | bytes 442376 | tf_op jit(solution)/shard_map/ppermute | solution.py:809
  184.4 8.7 %collective-permute-start.35 = (bf16[19,256,256]{2,1,0:T(8,128)(2,1)S(1)}, bf16[19,256,256]{2,1,0:T(8,128)(2,1)}, u32[]{:S(2)}, u32[]{:S(2)}) collective-permute-start(bf16[19,256,256]{2,1,0:T(8,128)(2,1)S(1)} %constant_dynamic-update-slice_fusion.half_ref), channel_id=1, source_target_pairs={{0,16},{16,0},{1,17},{17,1},{2,18},{18,2},{3,19},{19,3},{4,20},{20... | collective-permute-start | bytes 7471112 | tf_op jit(solution)/shard_map/ppermute | solution.py:809
  184.5 12.8 %collective-permute-start.34 = (bf16[9,64,256]{2,1,0:T(8,128)(2,1)S(1)}, bf16[9,64,256]{2,1,0:T(8,128)(2,1)S(1)}, u32[]{:S(2)}, u32[]{:S(2)}) collective-permute-start(bf16[9,64,256]{2,1,0:T(8,128)(2,1)S(1)} %pad_maximum_fusion.7), channel_id=1, source_target_pairs={{0,8},{4,12},{8,0},{12,4},{1,9},{5,13},{9,1},{13,5},{2,10},{6,14},... | collective-permute-start | bytes 884744 | tf_op jit(solution)/shard_map/ppermute | solution.py:809
  187.3 10.0 %collective-permute-start.33 = (bf16[9,64,256]{2,1,0:T(8,128)(2,1)}, bf16[9,64,256]{2,1,0:T(8,128)(2,1)}, u32[]{:S(2)}, u32[]{:S(2)}) collective-permute-start(bf16[9,64,256]{2,1,0:T(8,128)(2,1)} %pad_maximum_fusion.6), channel_id=1, source_target_pairs={{0,4},{4,0},{8,12},{12,8},{1,5},{5,1},{9,13},{13,9},{2,6},{6,2},{1... | collective-permute-start | bytes 884744 | tf_op jit(solution)/shard_map/ppermute | solution.py:809
  201.1 3.1 %collective-permute-start.36 = (bf16[9,256,256]{2,1,0:T(8,128)(2,1)}, bf16[9,256,256]{2,1,0:T(8,128)(2,1)S(1)}, u32[]{:S(2)}, u32[]{:S(2)}) collective-permute-start(bf16[9,256,256]{2,1,0:T(8,128)(2,1)} %constant_dynamic-update-slice_fusion.6.half_ref), channel_id=1, source_target_pairs={{0,16},{16,0},{1,17},{17,1},{2,18},{18,2},{3,19},{19,3},{4,20},{20... | collective-permute-start | bytes 3538952 | tf_op jit(solution)/shard_map/ppermute | solution.py:809
  (15 other events, 96.9 us)

commit v8 on v6

--- a/solution.py
+++ b/solution.py
@@ -292,6 +292,7 @@
         [r.own[g, i].astype(f32) for i in range(rows) for g in range(groups)], axis=0
     )
     M = rows * L
+    copies.wait(N.w1)
     z = matmul(r.xo[0:M, :], r.w1[0])
     z += matmul(r.xe[...], r.w1[1])
     z += matmul(r.xo[L : L + M, :], r.w1[2])
@@ -955,6 +956,7 @@
             xe=pltpu.VMEM((rows * groups * cols, 3 * cin), bf16),
             xo=pltpu.VMEM(((rows + 1) * groups * cols, 3 * cin), bf16),
         ),
+        far_in=(N.w1,),
         far_out=(N.spread,),
     )
     tot1 = gather_sum(stats[N.spread])
@@ -984,7 +986,7 @@
         parts=dict(pre1=row_parts(MP, 3), prep=row_parts(MP, 3)),
     )
     xe, xo, ownp, maskp = first[N.xe], first[N.xo], first[N.ownp], first[N.maskp]
-    far_xe, far_xo, ownp_far = partner(xe, *core), partner(xo, *core), partner(ownp, *core)
+    far_xe, far_xo = partner(xe, *core), partner(xo, *core)
 
     second = call(
         second_kernel,
@@ -1024,6 +1026,8 @@
     )
     mom2 = third[N.mom2]
     tot3 = gather_sum(third[N.spread])
+    ownp_here, far3 = lax.optimization_barrier((ownp, partner(third[N.theirs], *core)))
+    ownp_far = partner(ownp_here, *core)
 
     def chunk_shapes(taps):
         dims = (taps, cin // 4, half)
@@ -1034,7 +1038,7 @@
     second_parts = call(
         weights_second_kernel,
         dict(
-            bits=bits, mine=third[N.mine], far3=partner(third[N.theirs], *core), h3=h3, h3_far=far_h3, xe=xe, xe_far=far_xe,
+            bits=bits, mine=third[N.mine], far3=far3, h3=h3, h3_far=far_h3, xe=xe, xe_far=far_xe,
             tot3=tot3, mom1=mom1, mom2=mom2, gain2=g2, gainp=gp, ownp=ownp, ownp_far=ownp_far,
         ),
         chunk_shapes(taps2),

time: 206 us -> 205 us (level)
  transfers between devices with their start and end apart: 41 -> 41, of which waited for: 24 -> 26; matrix products, arithmetic and copies ran while one was open for 1% -> 1% of each run, Pallas kernels for 21% -> 21%
where the time goes in v8:
time: 205 us; the launch traced here: 204 us
  Pallas kernels  67.4 us (33%)
  starting transfers between devices  65.8 us (32%)
  waiting for transfers between devices  58.6 us (29%)
  other arithmetic  7.78 us (4%)
  local copies, waits for them, and re-layouts  2.63 us (1%)
    pallas_call x11, Pallas kernels, call(): pl.pallas_call(run, out_shape=list(outs.values()), in_specs=[spec(n) for...  57.1 us
    ppermute x32, starting transfers between devices, partner(): return lax.ppermute(value, axis, [(i, i ^ step) for i in range(count)])  36.3 us
    ppermute x32, waiting for transfers between devices, partner(): return lax.ppermute(value, axis, [(i, i ^ step) for i in range(count)])  34.9 us
    all_to_all x4, waiting for transfers between devices, gather_sum(): return lax.all_to_all(spread, axes, 0, 0)  21.2 us
    all_to_all x4, starting transfers between devices, gather_sum(): return lax.all_to_all(spread, axes, 0, 0)  16.7 us
    ppermute x4, starting transfers between devices, shifted(): lax.ppermute(value, axis, [(source, source + steps) for source in range(f...  12.3 us
    pallas_call x4, Pallas kernels, widen(): pl.pallas_call(body, out_shape=[shape((taps * per, n, 2 * m))] + [shape((...  10.3 us
  transfers between devices with their start and end apart: 41, of which 26 were waited for; matrix products, arithmetic and copies ran while one was open for 1% of the time, Pallas kernels for 21%

profile of v8, /device:TPU:0, one launch (start us, length us, event | category | flops | bytes accessed | tf_op | source)
XLA Modules:
  0.0 203.7 jit_solution(3947693282088125716)
XLA Ops:
  5.1 2.0 collective-permute-start.1
  7.9 4.8 %collective-permute-start.2 = (bf16[2,17,1,256]{3,2,1,0:T(2,128)(2,1)S(1)}, bf16[2,17,1,256]{3,2,1,0:T(2,128)(2,1)S(1)}, u32[]{:S(2)}, u32[]{:S(2)}) collective-permute-start(bf16[2,17,1,256]{3,2,1,0:T(2,128)(2,1)S(1)} %pad_maximum_fusion.12), channel_id=1, source_target_pairs={{0,4},{4,8},{8,12},{1,5},{5,9},{9,13},{2,6},{6,10},{10,14},{3,7},{... | collective-permute-start | bytes 52232 | tf_op jit(solution)/shard_map/ppermute | solution.py:785
  12.8 1.6 collective-permute-done.2.refs_2_
  15.7 4.2 %collective-permute-start.3 = (bf16[480,256]{1,0:T(8,128)(2,1)S(1)}, bf16[480,256]{1,0:T(8,128)(2,1)S(1)}, u32[]{:S(2)}, u32[]{:S(2)}) collective-permute-start(bf16[480,256]{1,0:T(8,128)(2,1)S(1)} %get-tuple-element.104), channel_id=1, source_target_pairs={{0,4},{4,8},{8,12},{1,5},{5,9},{9,13},{2,6},{6,10},{10,14},{3,7},{... | collective-permute-start | bytes 737288 | tf_op jit(solution)/shard_map/ppermute | solution.py:785
  21.2 3.3 %shard_map.206 = f32[32,1,2176]{2,1,0:T(1,128)} custom-call(bf16[2,16,32,256]{3,2,1,0:T(8,128)(2,1)S(1)} %copy-done.1, bf16[2,1,32,256]{3,2,1,0:T(8,128)(2,1)S(1)} %collective-permute-done.1.refs_1_, bf16[2,17,1,256]{3,2,1,0:T(2,128)(2,1)S(1)} %collective-permute-done.2.refs_2_, bf16[2,8,16,128]{3,2,1,0:T(8,128)(2,1)S(1)} %broadcast_in_dim.2.refs_3_, ...), custom_call_target="tpu_custom_call" | custom-call | tf_op jit(solution)/shard_map/pallas_call | solution.py:113
  24.6 7.9 %all-to-all-start = ((f32[32,1,2176]{2,1,0:T(1,128)}), f32[32,1,2176]{2,1,0:T(1,128)S(1)}, u32[]{:S(2)}, u32[]{:S(2)}) async-start(f32[32,1,2176]{2,1,0:T(1,128)} %shard_map.206), calls=%async_computation | async-start | bytes 557056 | tf_op jit(solution)/shard_map/all_to_all | solution.py:789
  32.6 5.7 %shard_map.205 = (f32[624,512]{1,0:T(8,128)}, f32[624,512]{1,0:T(8,128)}, bf16[624,768]{1,0:T(8,128)(2,1)}, bf16[672,768]{1,0:T(8,128)(2,1)}, f32[624,128]{1,0:T...) custom-call(s32[2]{0:T(128)S(1)} %add_convert_fusion.2.refs_0_, bf16[2,16,32,256]{3,2,1,0:T(8,128)(2,1)} %refs_0_.1, ...), custom_call_target="tpu_custom_call" | custom-call | flops 20000000000 | tf_op jit(solution)/shard_map/pallas_call | solution.py:113
  38.3 5.5 %all-to-all-done.refs_1_ = f32[32,1,2176]{2,1,0:T(1,128)S(1)} async-done(((f32[32,1,2176]{2,1,0:T(1,128)}), f32[32,1,2176]{2,1,0:T(1,128)S(1)}, u32[]{:S(2)}, u32[]{:S(2)}) %all-to-all-start) | async-done | bytes 278560 | tf_op jit(solution)/shard_map/all_to_all | solution.py:789
  43.8 6.3 %shard_map.207 = (bf16[624,1536]{1,0:T(8,128)(2,1)}, f32[528,512]{1,0:T(8,128)}, f32[32,1,1024]{2,1,0:T(1,128)}, f32[8,512]{1,0:T(8,128)S(1)}) custom-call(f32[624,512]{1,0:T(8,128)} %get-tuple-element.106.refs_0_.refs_3_, f32[32,1,2176]{2,1,0:T(1,128)S(1)} %all-to-all-done.refs_1_, f32[1,512]{1,0:T(1,128)S(1)} %bitcast.33, f32[1,512]{1,0:T(1,128)S(1)} %bitcast.31, ...), custom_call_target="tpu_custom_call" | custom-call | tf_op jit(solution)/shard_map/pallas_call | solution.py:113
  50.1 2.6 %all-to-all-start.1 = ((f32[32,1,1024]{2,1,0:T(1,128)}), f32[32,1,1024]{2,1,0:T(1,128)S(1)}, u32[]{:S(2)}, u32[]{:S(2)}) async-start(f32[32,1,1024]{2,1,0:T(1,128)} %get-tuple-element.114), calls=%async_computation.1 | async-start | bytes 262144 | tf_op jit(solution)/shard_map/all_to_all | solution.py:789
  52.9 7.7 %all-to-all-done.1.refs_4_ = f32[32,1,1024]{2,1,0:T(1,128)S(1)} async-done(((f32[32,1,1024]{2,1,0:T(1,128)}), f32[32,1,1024]{2,1,0:T(1,128)S(1)}, u32[]{:S(2)}, u32[]{:S(2)}) %all-to-all-start.1) | async-done | bytes 131104 | tf_op jit(solution)/shard_map/all_to_all | solution.py:789
  60.7 5.5 %shard_map.208 = (bf16[2,8,16,512]{3,2,1,0:T(8,128)(2,1)}, f32[528,512]{1,0:T(8,128)}, f32[32,1,1536]{2,1,0:T(1,128)}, f32[8,512]{1,0:T(8,128)S(1)}, f32[3,384,256]{2,1,0:T(8,128)}, /*index=5*/f32[3,384,256]{2,1,0:T(8,128)}) custom-call(s32[5]{0:T(128)S(1)} %stack.32.refs_0_, f32[528,512]{1,0:T(8,128)} %get-tuple-element.111.refs_1_.refs_2_, ...), custom_call_target="tpu_custom_call" | custom-call | tf_op jit(solution)/shard_map/pallas_call | solution.py:113
  66.8 2.8 %all-to-all-start.2 = ((f32[32,1,1536]{2,1,0:T(1,128)}), f32[32,1,1536]{2,1,0:T(1,128)S(1)}, u32[]{:S(2)}, u32[]{:S(2)}) async-start(f32[32,1,1536]{2,1,0:T(1,128)} %get-tuple-element.125), calls=%async_computation.2 | async-start | bytes 393216 | tf_op jit(solution)/shard_map/all_to_all | solution.py:789
  70.8 8.0 %all-to-all-done.2.refs_7_.refs_8_ = f32[32,1,1536]{2,1,0:T(1,128)S(1)} async-done(((f32[32,1,1536]{2,1,0:T(1,128)}), f32[32,1,1536]{2,1,0:T(1,128)S(1)}, u32[]{:S(2)}, u32[]{:S(2)}) %all-to-all-start.2) | async-done | bytes 196640 | tf_op jit(solution)/shard_map/all_to_all | solution.py:789
  78.8 8.4 %shard_map.209 = (bf16[19,64,256]{2,1,0:T(8,128)(2,1)S(1)}, f32[19,64,256]{2,1,0:T(8,128)}, bf16[19,64,256]{2,1,0:T(8,128)(2,1)}, f32[19,64,256]{2,1,0:T(8,128)}) custom-call(s32[5]{0:T(128)S(1)} %stack.32.refs_0_, f32[3,384,256]{2,1,0:T(8,128)} %get-tuple-element.120.refs_1_, f32[3,384,256]{2,1,0:T(8,128)} %copy-done.18, ...), custom_call_target="tpu_custom_call" | custom-call | tf_op jit(solution)/shard_map/pallas_call | solution.py:113
  88.3 8.6 %shard_map.211 = (f32[432,512]{1,0:T(8,128)}, f32[432,512]{1,0:T(8,128)}, f32[32,1,1024]{2,1,0:T(1,128)}, f32[2,384,256]{2,1,0:T(8,128)}, f32[2,384,256]{2,1,0:T...) custom-call(s32[5]{0:T(128)S(1)} %stack.32.refs_0_, ...), custom_call_target="tpu_custom_call" | custom-call | tf_op jit(solution)/shard_map/pallas_call | solution.py:113
  97.5 3.4 %all-to-all-start.3 = ((f32[32,1,1024]{2,1,0:T(1,128)}), f32[32,1,1024]{2,1,0:T(1,128)S(1)}, u32[]{:S(2)}, u32[]{:S(2)}) async-start(f32[32,1,1024]{2,1,0:T(1,128)} %get-tuple-element.146), calls=%async_computation.3 | async-start | bytes 262144 | tf_op jit(solution)/shard_map/all_to_all | solution.py:789
  100.9 1.9 collective-permute-done.10.refs_4_
  103.7 3.8 %shard_map.210 = (bf16[19,32,256]{2,1,0:T(8,128)(2,1)}, f32[19,32,256]{2,1,0:T(8,128)}, bf16[19,32,256]{2,1,0:T(8,128)(2,1)}, f32[19,32,256]{2,1,0:T(8,128)}) custom-call(s32[5]{0:T(128)} %copy-done.10, f32[19,64,256]{2,1,0:T(8,128)} %get-tuple-element.132.refs_1_, bf16[19,64,256]{2,1,0:T(8,128)(2,1)} %collective-permute-done.9.refs_2_, ...), custom_call_target="tpu_custom_call" | custom-call | flops 20000000000 | tf_op jit(solution)/shard_map/pallas_call | solution.py:113
  109.5 6.9 %shard_map.212 = (bf16[9,64,256]{2,1,0:T(8,128)(2,1)S(1)}, f32[9,64,256]{2,1,0:T(8,128)S(1)}, bf16[9,64,256]{2,1,0:T(8,128)(2,1)S(1)}, f32[9,64,256]{2,1,0:T(8,1...) custom-call(s32[5]{0:T(128)S(1)} %copy-done.11, f32[2,384,256]{2,1,0:T(8,128)} %get-tuple-element.143.refs_1_, ...), custom_call_target="tpu_custom_call" | custom-call | flops 20000000000 | tf_op jit(solution)/shard_map/pallas_call | solution.py:113
  116.7 1.4 convert_add_fusion.1
  118.3 1.5 collective-permute-start.15
  119.8 1.5 collective-permute-start.16
  121.8 6.4 %shard_map.213 = bf16[2,16,32,256]{3,2,1,0:T(8,128)(2,1)} custom-call(f32[432,512]{1,0:T(8,128)S(1)} %copy-done.14, f32[432,512]{1,0:T(8,128)} %get-tuple-element.157.refs_1_, bf16[384,512]{1,0:T(8,128)(2,1)S(1)} %get-tuple-element.158.refs_2_, bf16[3,768,512]{2,1,0:T(8,128)(2,1)} %bitcast.47, bf16[256,512]{1,0:T(8,128)(2,1)S(1)} %copy-done.5, ...), custom_call_target="tpu_custom_call" | custom-call | flops 10000000000 | tf_op jit(solution)/shard_map/pallas_call | solution.py:113
  128.7 1.3 collective-permute-start.20
  130.3 1.8 collective-permute-start.18
  133.9 3.5 %collective-permute-done.19 = bf16[9,32,256]{2,1,0:T(8,128)(2,1)S(1)} collective-permute-done((bf16[9,32,256]{2,1,0:T(8,128)(2,1)S(1)}, bf16[9,32,256]{2,1,0:T(8,128)(2,1)S(1)}, u32[]{:S(2)}, u32[]{:S(2)}) %collective-permute-start.19) | collective-permute-done | bytes 147488 | tf_op jit(solution)/shard_map/ppermute | solution.py:798
  138.9 4.1 %collective-permute-start.22 = (bf16[18,16,256]{2,1,0:T(8,128)(2,1)S(1)}, bf16[18,16,256]{2,1,0:T(8,128)(2,1)S(1)}, u32[]{:S(2)}, u32[]{:S(2)}) collective-permute-start(bf16[18,16,256]{2,1,0:T(8,128)(2,1)S(1)} %select_convert_fusion.2), channel_id=1, source_target_pairs={{0,1},{1,0},{2,3},{3,2},{4,5},{5,4},{6,7},{7,6},{8,9},{9,8},{10,11... | collective-permute-start | bytes 442376 | tf_op jit(solution)/shard_map/ppermute | solution.py:798
  143.0 5.5 %collective-permute-done.22 = bf16[18,16,256]{2,1,0:T(8,128)(2,1)S(1)} collective-permute-done((bf16[18,16,256]{2,1,0:T(8,128)(2,1)S(1)}, bf16[18,16,256]{2,1,0:T(8,128)(2,1)S(1)}, u32[]{:S(2)}, u32[]{:S(2)}) %collective-permute-start.22) | collective-permute-done | bytes 147488 | tf_op jit(solution)/shard_map/ppermute | solution.py:798
  148.5 1.4 collective-permute-start.23
  150.0 2.5 %collective-permute-start.24 = (bf16[18,8,256]{2,1,0:T(8,128)(2,1)S(1)}, bf16[18,8,256]{2,1,0:T(8,128)(2,1)S(1)}, u32[]{:S(2)}, u32[]{:S(2)}) collective-permute-start(bf16[18,8,256]{2,1,0:T(8,128)(2,1)S(1)} %select_convert_fusion.5), channel_id=1, source_target_pairs={{0,2},{1,3},{2,0},{3,1},{4,6},{5,7},{6,4},{7,5},{8,10},{9,11},{10,... | collective-permute-start | bytes 221192 | tf_op jit(solution)/shard_map/ppermute | solution.py:798
  152.5 3.4 %collective-permute-done.24 = bf16[18,8,256]{2,1,0:T(8,128)(2,1)S(1)} collective-permute-done((bf16[18,8,256]{2,1,0:T(8,128)(2,1)S(1)}, bf16[18,8,256]{2,1,0:T(8,128)(2,1)S(1)}, u32[]{:S(2)}, u32[]{:S(2)}) %collective-permute-start.24) | collective-permute-done | bytes 73760 | tf_op jit(solution)/shard_map/ppermute | solution.py:798
  158.4 1.5 collective-permute-start.26
  160.0 2.3 %collective-permute-start.27 = (bf16[18,8,256]{2,1,0:T(8,128)(2,1)S(1)}, bf16[18,8,256]{2,1,0:T(8,128)(2,1)S(1)}, u32[]{:S(2)}, u32[]{:S(2)}) collective-permute-start(bf16[18,8,256]{2,1,0:T(8,128)(2,1)S(1)} %add_convert_fusion.1), channel_id=1, source_target_pairs={{0,2},{1,3},{2,0},{3,1},{4,6},{5,7},{6,4},{7,5},{8,10},{9,11},{10,... | collective-permute-start | bytes 221192 | tf_op jit(solution)/shard_map/ppermute | solution.py:798
  162.3 3.0 %collective-permute-done.27 = bf16[18,8,256]{2,1,0:T(8,128)(2,1)S(1)} collective-permute-done((bf16[18,8,256]{2,1,0:T(8,128)(2,1)S(1)}, bf16[18,8,256]{2,1,0:T(8,128)(2,1)S(1)}, u32[]{:S(2)}, u32[]{:S(2)}) %collective-permute-start.27) | collective-permute-done | bytes 73760 | tf_op jit(solution)/shard_map/ppermute | solution.py:798
  165.3 2.4 %collective-permute-done.25 = bf16[19,32,256]{2,1,0:T(8,128)(2,1)S(1)} collective-permute-done((bf16[19,32,256]{2,1,0:T(8,128)(2,1)S(1)}, bf16[19,32,256]{2,1,0:T(8,128)(2,1)S(1)}, u32[]{:S(2)}, u32[]{:S(2)}) %collective-permute-start.25) | collective-permute-done | bytes 311328 | tf_op jit(solution)/shard_map/ppermute | solution.py:798
  169.1 3.0 %collective-permute-start.28 = (bf16[18,16,256]{2,1,0:T(8,128)(2,1)S(1)}, bf16[18,16,256]{2,1,0:T(8,128)(2,1)S(1)}, u32[]{:S(2)}, u32[]{:S(2)}) collective-permute-start(bf16[18,16,256]{2,1,0:T(8,128)(2,1)S(1)} %pad_maximum_fusion.11), channel_id=1, source_target_pairs={{0,1},{1,0},{2,3},{3,2},{4,5},{5,4},{6,7},{7,6},{8,9},{9,8},{10,11... | collective-permute-start | bytes 442376 | tf_op jit(solution)/shard_map/ppermute | solution.py:798
  172.1 1.5 collective-permute-start.31
  173.6 1.6 collective-permute-done.28
  176.2 1.8 collective-permute-start.30
  178.0 2.6 %collective-permute-done.29 = bf16[9,32,256]{2,1,0:T(8,128)(2,1)S(1)} collective-permute-done((bf16[9,32,256]{2,1,0:T(8,128)(2,1)S(1)}, bf16[9,32,256]{2,1,0:T(8,128)(2,1)S(1)}, u32[]{:S(2)}, u32[]{:S(2)}) %collective-permute-start.29) | collective-permute-done | bytes 147488 | tf_op jit(solution)/shard_map/ppermute | solution.py:798
  180.5 3.5 %collective-permute-done.30 = bf16[9,32,256]{2,1,0:T(8,128)(2,1)S(1)} collective-permute-done((bf16[9,32,256]{2,1,0:T(8,128)(2,1)S(1)}, bf16[9,32,256]{2,1,0:T(8,128)(2,1)S(1)}, u32[]{:S(2)}, u32[]{:S(2)}) %collective-permute-start.30) | collective-permute-done | bytes 147488 | tf_op jit(solution)/shard_map/ppermute | solution.py:798
  186.6 2.0 collective-permute-start.33
  188.6 2.8 %shard_map.214 = (f32[18,256,512]{2,1,0:T(8,128)}, f32[1,256,512]{2,1,0:T(8,128)}) custom-call(s32[1]{0:T(128)} %bitcast.side_ref, bf16[19,256,256]{2,1,0:T(8,128)(2,1)S(1)} %pad_maximum_fusion.half_ref), custom_call_target="tpu_custom_call" | custom-call | tf_op jit(solution)/shard_map/pallas_call | solution.py:730
  191.4 3.4 %shard_map.215 = (f32[18,256,512]{2,1,0:T(8,128)}, f32[1,256,512]{2,1,0:T(8,128)}) custom-call(s32[1]{0:T(128)} %bitcast.15.side_ref, bf16[19,256,256]{2,1,0:T(8,128)(2,1)} %collective-permute-done.35.half_ref, f32[18,256,512]{2,1,0:T(8,128)} %get-tuple-element.181.refs_0_, ...), custom_call_target="tpu_custom_call", output_to_operand_aliasing={{0}: (2, {}), {1}: (3, {})} | custom-call | tf_op jit(solution)/shard_map/pallas_call | solution.py:730
  194.9 1.5 collective-permute-done.33
  198.7 2.1 %shard_map.216.refs_0_ = f32[9,256,512]{2,1,0:T(8,128)} custom-call(s32[1]{0:T(128)} %bitcast.side_ref, bf16[9,256,256]{2,1,0:T(8,128)(2,1)S(1)} %pad_maximum_fusion.1.half_ref), custom_call_target="tpu_custom_call" | custom-call | tf_op jit(solution)/shard_map/pallas_call | solution.py:730
  201.5 2.1 %shard_map.217 = f32[9,256,512]{2,1,0:T(8,128)} custom-call(s32[1]{0:T(128)} %bitcast.15.side_ref, bf16[9,256,256]{2,1,0:T(8,128)(2,1)S(1)} %collective-permute-done.36.half_ref, f32[9,256,512]{2,1,0:T(8,128)} %shard_map.216.refs_0_), custom_call_target="tpu_custom_call", output_to_operand_aliasing={{}: (2, {})} | custom-call | tf_op jit(solution)/shard_map/pallas_call | solution.py:730
  (138 shorter events, 30.2 us)
Async XLA Ops:
  3.5 17.7 %copy-start.1 = (bf16[2,16,32,256]{3,2,1,0:T(8,128)(2,1)S(1)}, bf16[2,16,32,256]{3,2,1,0:T(8,128)(2,1)}, u32[]{:S(2)}) copy-start(bf16[2,16,32,256]{3,2,1,0:T(8,128)(2,1)} %refs_0_.1) | copy-start | bytes 1572868
  3.5 17.7 %copy-start.5 = (bf16[256,512]{1,0:T(8,128)(2,1)S(1)}, bf16[256,512]{1,0:T(8,128)(2,1)}, u32[]{:S(2)}) copy-start(bf16[256,512]{1,0:T(8,128)(2,1)} %refs_4_.1) | copy-start | bytes 786436
  4.5 9.8 %collective-permute-start = (bf16[672,256]{1,0:T(8,128)(2,1)S(1)}, bf16[672,256]{1,0:T(8,128)(2,1)S(1)}, u32[]{:S(2)}, u32[]{:S(2)}) collective-permute-start(bf16[672,256]{1,0:T(8,128)(2,1)S(1)} %shard_map.203), channel_id=1, source_target_pairs={{0,16},{16,0},{1,17},{17,1},{2,18},{18,2},{3,19},{19,3},{4,20},{20... | collective-permute-start | bytes 1032200 | tf_op jit(solution)/shard_map/ppermute | solution.py:927
  5.1 2.8 %collective-permute-start.1 = (bf16[2,1,32,256]{3,2,1,0:T(8,128)(2,1)S(1)}, bf16[2,1,32,256]{3,2,1,0:T(8,128)(2,1)S(1)}, u32[]{:S(2)}, u32[]{:S(2)}) collective-permute-start(bf16[2,1,32,256]{3,2,1,0:T(8,128)(2,1)S(1)} %slice.57), channel_id=1, source_target_pairs={{0,16},{1,17},{2,18},{3,19},{4,20},{5,21},{6,22},{7,23},{8,24},{9,... | collective-permute-start | bytes 98312 | tf_op jit(solution)/shard_map/ppermute | solution.py:785
  7.9 6.4 %collective-permute-start.2 = (bf16[2,17,1,256]{3,2,1,0:T(2,128)(2,1)S(1)}, bf16[2,17,1,256]{3,2,1,0:T(2,128)(2,1)S(1)}, u32[]{:S(2)}, u32[]{:S(2)}) collective-permute-start(bf16[2,17,1,256]{3,2,1,0:T(2,128)(2,1)S(1)} %pad_maximum_fusion.12), channel_id=1, source_target_pairs={{0,4},{4,8},{8,12},{1,5},{5,9},{9,13},{2,6},{6,10},{10,14},{3,7},{... | collective-permute-start | bytes 52232 | tf_op jit(solution)/shard_map/ppermute | solution.py:785
  15.7 16.8 %collective-permute-start.3 = (bf16[480,256]{1,0:T(8,128)(2,1)S(1)}, bf16[480,256]{1,0:T(8,128)(2,1)S(1)}, u32[]{:S(2)}, u32[]{:S(2)}) collective-permute-start(bf16[480,256]{1,0:T(8,128)(2,1)S(1)} %get-tuple-element.104), channel_id=1, source_target_pairs={{0,4},{4,8},{8,12},{1,5},{5,9},{9,13},{2,6},{6,10},{10,14},{3,7},{... | collective-permute-start | bytes 737288 | tf_op jit(solution)/shard_map/ppermute | solution.py:785
  19.9 12.7 %collective-permute-start.4 = (bf16[480,256]{1,0:T(8,128)(2,1)S(1)}, bf16[480,256]{1,0:T(8,128)(2,1)S(1)}, u32[]{:S(2)}, u32[]{:S(2)}) collective-permute-start(bf16[480,256]{1,0:T(8,128)(2,1)S(1)} %get-tuple-element.105), channel_id=1, source_target_pairs={{4,0},{8,4},{12,8},{5,1},{9,5},{13,9},{6,2},{10,6},{14,10},{7,3},{... | collective-permute-start | bytes 737288 | tf_op jit(solution)/shard_map/ppermute | solution.py:785
  24.6 19.2 %all-to-all-start = ((f32[32,1,2176]{2,1,0:T(1,128)}), f32[32,1,2176]{2,1,0:T(1,128)S(1)}, u32[]{:S(2)}, u32[]{:S(2)}) async-start(f32[32,1,2176]{2,1,0:T(1,128)} %shard_map.206), calls=%async_computation | async-start | bytes 557056 | tf_op jit(solution)/shard_map/all_to_all | solution.py:789
  43.7 16.9 %copy-start.6 = (f32[512]{0:T(512)S(1)}, f32[512]{0:T(512)}, u32[]{:S(2)}) copy-start(f32[512]{0:T(512)} %param.17) | copy-start | bytes 6148
  43.7 16.9 %copy-start.7 = (f32[512]{0:T(512)S(1)}, f32[512]{0:T(512)}, u32[]{:S(2)}) copy-start(f32[512]{0:T(512)} %param.20) | copy-start | bytes 6148
  43.7 16.9 %copy-start.12 = (f32[512]{0:T(512)S(1)}, f32[512]{0:T(512)}, u32[]{:S(2)}) copy-start(f32[512]{0:T(512)} %param.18) | copy-start | bytes 6148
  43.8 16.9 %copy-start.13 = (f32[512]{0:T(512)S(1)}, f32[512]{0:T(512)}, u32[]{:S(2)}) copy-start(f32[512]{0:T(512)} %param.21) | copy-start | bytes 6148
  50.1 10.6 %collective-permute-start.5 = (bf16[624,1536]{1,0:T(8,128)(2,1)}, bf16[624,1536]{1,0:T(8,128)(2,1)S(1)}, u32[]{:S(2)}, u32[]{:S(2)}) collective-permute-start(bf16[624,1536]{1,0:T(8,128)(2,1)} %get-tuple-element.115.refs_3_), channel_id=1, source_target_pairs={{0,16},{16,0},{1,17},{17,1},{2,18},{18,2},{3,19},{19,3},{4,20},{20... | collective-permute-start | bytes 5750792 | tf_op jit(solution)/shard_map/ppermute | solution.py:798
  50.1 10.5 %all-to-all-start.1 = ((f32[32,1,1024]{2,1,0:T(1,128)}), f32[32,1,1024]{2,1,0:T(1,128)S(1)}, u32[]{:S(2)}, u32[]{:S(2)}) async-start(f32[32,1,1024]{2,1,0:T(1,128)} %get-tuple-element.114), calls=%async_computation.1 | async-start | bytes 262144 | tf_op jit(solution)/shard_map/all_to_all | solution.py:789
  52.9 35.4 %copy-start.10 = (s32[5]{0:T(128)}, s32[5]{0:T(128)S(1)}, u32[]{:S(2)}) copy-start(s32[5]{0:T(128)S(1)} %stack.32.refs_0_) | copy-start | bytes 64
  66.2 4.0 %collective-permute-start.6 = (f32[3,384,256]{2,1,0:T(8,128)}, f32[3,384,256]{2,1,0:T(8,128)S(1)}, u32[]{:S(2)}, u32[]{:S(2)}) collective-permute-start(f32[3,384,256]{2,1,0:T(8,128)} %get-tuple-element.121), channel_id=1, source_target_pairs={{0,16},{16,0},{1,17},{17,1},{2,18},{18,2},{3,19},{19,3},{4,20},{20... | collective-permute-start | bytes 3538952 | tf_op jit(solution)/shard_map/ppermute | solution.py:798
  66.3 4.5 %collective-permute-start.7 = (bf16[624,768]{1,0:T(8,128)(2,1)}, bf16[624,768]{1,0:T(8,128)(2,1)}, u32[]{:S(2)}, u32[]{:S(2)}) collective-permute-start(bf16[624,768]{1,0:T(8,128)(2,1)} %get-tuple-element.124.refs_5_.refs_3_), channel_id=1, source_target_pairs={{0,16},{16,0},{1,17},{17,1},{2,18},{18,2},{3,19},{19,3},{4,20},{20... | collective-permute-start | bytes 2875400 | tf_op jit(solution)/shard_map/ppermute | solution.py:798
  66.8 12.0 %all-to-all-start.2 = ((f32[32,1,1536]{2,1,0:T(1,128)}), f32[32,1,1536]{2,1,0:T(1,128)S(1)}, u32[]{:S(2)}, u32[]{:S(2)}) async-start(f32[32,1,1536]{2,1,0:T(1,128)} %get-tuple-element.125), calls=%async_computation.2 | async-start | bytes 393216 | tf_op jit(solution)/shard_map/all_to_all | solution.py:789
  70.3 8.6 %collective-permute-start.8 = (f32[624,128]{1,0:T(8,128)S(1)}, f32[624,128]{1,0:T(8,128)S(1)}, u32[]{:S(2)}, u32[]{:S(2)}) collective-permute-start(f32[624,128]{1,0:T(8,128)S(1)} %get-tuple-element.127.refs_5_.refs_10_.refs_12_.refs_14_), channel_id=1, source_target_pairs={{0,16},{16,0},{1,17},{17,1},{2,18},{18,2},{3,19},{19,3},{4,20},{20... | collective-permute-start | bytes 958472 | tf_op jit(solution)/shard_map/ppermute | solution.py:798
  87.2 15.6 %collective-permute-start.10 = (bf16[19,64,256]{2,1,0:T(8,128)(2,1)}, bf16[19,64,256]{2,1,0:T(8,128)(2,1)S(1)}, u32[]{:S(2)}, u32[]{:S(2)}) collective-permute-start(bf16[19,64,256]{2,1,0:T(8,128)(2,1)} %get-tuple-element.135), channel_id=1, source_target_pairs={{0,8},{4,12},{8,0},{12,4},{1,9},{5,13},{9,1},{13,5},{2,10},{6,14},... | collective-permute-start | bytes 1867784 | tf_op jit(solution)/shard_map/ppermute | solution.py:798
  88.2 15.2 %collective-permute-start.9 = (bf16[19,64,256]{2,1,0:T(8,128)(2,1)S(1)}, bf16[19,64,256]{2,1,0:T(8,128)(2,1)}, u32[]{:S(2)}, u32[]{:S(2)}) collective-permute-start(bf16[19,64,256]{2,1,0:T(8,128)(2,1)S(1)} %get-tuple-element.133), channel_id=1, source_target_pairs={{0,4},{4,0},{8,12},{12,8},{1,5},{5,1},{9,13},{13,9},{2,6},{6,2},{1... | collective-permute-start | bytes 1867784 | tf_op jit(solution)/shard_map/ppermute | solution.py:798
  88.3 21.1 %collective-permute-start.14 = (bf16[672,768]{1,0:T(8,128)(2,1)}, bf16[672,768]{1,0:T(8,128)(2,1)}, u32[]{:S(2)}, u32[]{:S(2)}) collective-permute-start(bf16[672,768]{1,0:T(8,128)(2,1)} %get-tuple-element.145.refs_5_), channel_id=1, source_target_pairs={{0,16},{16,0},{1,17},{17,1},{2,18},{18,2},{3,19},{19,3},{4,20},{20... | collective-permute-start | bytes 3096584 | tf_op jit(solution)/shard_map/ppermute | solution.py:798
  96.9 12.6 %collective-permute-start.13 = (f32[2,384,256]{2,1,0:T(8,128)}, f32[2,384,256]{2,1,0:T(8,128)}, u32[]{:S(2)}, u32[]{:S(2)}) collective-permute-start(f32[2,384,256]{2,1,0:T(8,128)} %get-tuple-element.144), channel_id=1, source_target_pairs={{0,16},{16,0},{1,17},{17,1},{2,18},{18,2},{3,19},{19,3},{4,20},{20... | collective-permute-start | bytes 2359304 | tf_op jit(solution)/shard_map/ppermute | solution.py:798
  97.5 12.0 %all-to-all-start.3 = ((f32[32,1,1024]{2,1,0:T(1,128)}), f32[32,1,1024]{2,1,0:T(1,128)S(1)}, u32[]{:S(2)}, u32[]{:S(2)}) async-start(f32[32,1,1024]{2,1,0:T(1,128)} %get-tuple-element.146), calls=%async_computation.3 | async-start | bytes 262144 | tf_op jit(solution)/shard_map/all_to_all | solution.py:789
  107.5 8.8 %collective-permute-start.11 = (bf16[19,32,256]{2,1,0:T(8,128)(2,1)}, bf16[19,32,256]{2,1,0:T(8,128)(2,1)S(1)}, u32[]{:S(2)}, u32[]{:S(2)}) collective-permute-start(bf16[19,32,256]{2,1,0:T(8,128)(2,1)} %get-tuple-element.141), channel_id=1, source_target_pairs={{0,8},{4,12},{8,0},{12,4},{1,9},{5,13},{9,1},{13,5},{2,10},{6,14},... | collective-permute-start | bytes 933896 | tf_op jit(solution)/shard_map/ppermute | solution.py:798
  108.5 8.2 %collective-permute-start.12 = (bf16[19,32,256]{2,1,0:T(8,128)(2,1)}, bf16[19,32,256]{2,1,0:T(8,128)(2,1)}, u32[]{:S(2)}, u32[]{:S(2)}) collective-permute-start(bf16[19,32,256]{2,1,0:T(8,128)(2,1)} %get-tuple-element.142), channel_id=1, source_target_pairs={{0,4},{4,0},{8,12},{12,8},{1,5},{5,1},{9,13},{13,9},{2,6},{6,2},{1... | collective-permute-start | bytes 933896 | tf_op jit(solution)/shard_map/ppermute | solution.py:798
  118.3 10.4 %collective-permute-start.15 = (bf16[38,16,256]{2,1,0:T(8,128)(2,1)S(1)}, bf16[38,16,256]{2,1,0:T(8,128)(2,1)S(1)}, u32[]{:S(2)}, u32[]{:S(2)}) collective-permute-start(bf16[38,16,256]{2,1,0:T(8,128)(2,1)S(1)} %select_convert_fusion), channel_id=1, source_target_pairs={{0,1},{1,0},{2,3},{3,2},{4,5},{5,4},{6,7},{7,6},{8,9},{9,8},{10,11... | collective-permute-start | bytes 933896 | tf_op jit(solution)/shard_map/ppermute | solution.py:798
  119.8 8.4 %collective-permute-start.16 = (bf16[9,64,256]{2,1,0:T(8,128)(2,1)S(1)}, bf16[9,64,256]{2,1,0:T(8,128)(2,1)S(1)}, u32[]{:S(2)}, u32[]{:S(2)}) collective-permute-start(bf16[9,64,256]{2,1,0:T(8,128)(2,1)S(1)} %get-tuple-element.154), channel_id=1, source_target_pairs={{0,4},{4,0},{8,12},{12,8},{1,5},{5,1},{9,13},{13,9},{2,6},{6,2},{1... | collective-permute-start | bytes 884744 | tf_op jit(solution)/shard_map/ppermute | solution.py:798
  121.3 7.4 %collective-permute-start.17 = (bf16[9,64,256]{2,1,0:T(8,128)(2,1)S(1)}, bf16[9,64,256]{2,1,0:T(8,128)(2,1)S(1)}, u32[]{:S(2)}, u32[]{:S(2)}) collective-permute-start(bf16[9,64,256]{2,1,0:T(8,128)(2,1)S(1)} %get-tuple-element.155), channel_id=1, source_target_pairs={{0,8},{4,12},{8,0},{12,4},{1,9},{5,13},{9,1},{13,5},{2,10},{6,14},... | collective-permute-start | bytes 884744 | tf_op jit(solution)/shard_map/ppermute | solution.py:798
  128.7 5.2 %collective-permute-start.20 = (bf16[9,32,256]{2,1,0:T(8,128)(2,1)S(1)}, bf16[9,32,256]{2,1,0:T(8,128)(2,1)S(1)}, u32[]{:S(2)}, u32[]{:S(2)}) collective-permute-start(bf16[9,32,256]{2,1,0:T(8,128)(2,1)S(1)} %select_convert_fusion.3), channel_id=1, source_target_pairs={{0,4},{4,0},{8,12},{12,8},{1,5},{5,1},{9,13},{13,9},{2,6},{6,2},{1... | collective-permute-start | bytes 442376 | tf_op jit(solution)/shard_map/ppermute | solution.py:798
  130.3 7.4 %collective-permute-start.18 = (bf16[38,8,256]{2,1,0:T(8,128)(2,1)S(1)}, bf16[38,8,256]{2,1,0:T(8,128)(2,1)S(1)}, u32[]{:S(2)}, u32[]{:S(2)}) collective-permute-start(bf16[38,8,256]{2,1,0:T(8,128)(2,1)S(1)} %select_convert_fusion.1), channel_id=1, source_target_pairs={{0,2},{1,3},{2,0},{3,1},{4,6},{5,7},{6,4},{7,5},{8,10},{9,11},{10,... | collective-permute-start | bytes 466952 | tf_op jit(solution)/shard_map/ppermute | solution.py:798
  132.2 5.2 %collective-permute-start.19 = (bf16[9,32,256]{2,1,0:T(8,128)(2,1)S(1)}, bf16[9,32,256]{2,1,0:T(8,128)(2,1)S(1)}, u32[]{:S(2)}, u32[]{:S(2)}) collective-permute-start(bf16[9,32,256]{2,1,0:T(8,128)(2,1)S(1)} %select_convert_fusion.4), channel_id=1, source_target_pairs={{0,8},{4,12},{8,0},{12,4},{1,9},{5,13},{9,1},{13,5},{2,10},{6,14},... | collective-permute-start | bytes 442376 | tf_op jit(solution)/shard_map/ppermute | solution.py:798
  137.9 10.6 %collective-permute-start.21 = (bf16[38,8,256]{2,1,0:T(8,128)(2,1)S(1)}, bf16[38,8,256]{2,1,0:T(8,128)(2,1)S(1)}, u32[]{:S(2)}, u32[]{:S(2)}) collective-permute-start(bf16[38,8,256]{2,1,0:T(8,128)(2,1)S(1)} %add_convert_fusion), channel_id=1, source_target_pairs={{0,2},{1,3},{2,0},{3,1},{4,6},{5,7},{6,4},{7,5},{8,10},{9,11},{10,... | collective-permute-start | bytes 466952 | tf_op jit(solution)/shard_map/ppermute | solution.py:798
  138.9 9.5 %collective-permute-start.22 = (bf16[18,16,256]{2,1,0:T(8,128)(2,1)S(1)}, bf16[18,16,256]{2,1,0:T(8,128)(2,1)S(1)}, u32[]{:S(2)}, u32[]{:S(2)}) collective-permute-start(bf16[18,16,256]{2,1,0:T(8,128)(2,1)S(1)} %select_convert_fusion.2), channel_id=1, source_target_pairs={{0,1},{1,0},{2,3},{3,2},{4,5},{5,4},{6,7},{7,6},{8,9},{9,8},{10,11... | collective-permute-start | bytes 442376 | tf_op jit(solution)/shard_map/ppermute | solution.py:798
  148.5 8.5 %collective-permute-start.23 = (bf16[38,16,256]{2,1,0:T(8,128)(2,1)S(1)}, bf16[38,16,256]{2,1,0:T(8,128)(2,1)S(1)}, u32[]{:S(2)}, u32[]{:S(2)}) collective-permute-start(bf16[38,16,256]{2,1,0:T(8,128)(2,1)S(1)} %pad_maximum_fusion.6), channel_id=1, source_target_pairs={{0,1},{1,0},{2,3},{3,2},{4,5},{5,4},{6,7},{7,6},{8,9},{9,8},{10,11... | collective-permute-start | bytes 933896 | tf_op jit(solution)/shard_map/ppermute | solution.py:798
  150.0 5.9 %collective-permute-start.24 = (bf16[18,8,256]{2,1,0:T(8,128)(2,1)S(1)}, bf16[18,8,256]{2,1,0:T(8,128)(2,1)S(1)}, u32[]{:S(2)}, u32[]{:S(2)}) collective-permute-start(bf16[18,8,256]{2,1,0:T(8,128)(2,1)S(1)} %select_convert_fusion.5), channel_id=1, source_target_pairs={{0,2},{1,3},{2,0},{3,1},{4,6},{5,7},{6,4},{7,5},{8,10},{9,11},{10,... | collective-permute-start | bytes 221192 | tf_op jit(solution)/shard_map/ppermute | solution.py:798
  157.3 10.3 %collective-permute-start.25 = (bf16[19,32,256]{2,1,0:T(8,128)(2,1)S(1)}, bf16[19,32,256]{2,1,0:T(8,128)(2,1)S(1)}, u32[]{:S(2)}, u32[]{:S(2)}) collective-permute-start(bf16[19,32,256]{2,1,0:T(8,128)(2,1)S(1)} %get-tuple-element.202), channel_id=1, source_target_pairs={{0,8},{4,12},{8,0},{12,4},{1,9},{5,13},{9,1},{13,5},{2,10},{6,14},... | collective-permute-start | bytes 933896 | tf_op jit(solution)/shard_map/ppermute | solution.py:798
  158.4 10.1 %collective-permute-start.26 = (bf16[19,32,256]{2,1,0:T(8,128)(2,1)S(1)}, bf16[19,32,256]{2,1,0:T(8,128)(2,1)S(1)}, u32[]{:S(2)}, u32[]{:S(2)}) collective-permute-start(bf16[19,32,256]{2,1,0:T(8,128)(2,1)S(1)} %get-tuple-element.201), channel_id=1, source_target_pairs={{0,4},{4,0},{8,12},{12,8},{1,5},{5,1},{9,13},{13,9},{2,6},{6,2},{1... | collective-permute-start | bytes 933896 | tf_op jit(solution)/shard_map/ppermute | solution.py:798
  160.0 5.3 %collective-permute-start.27 = (bf16[18,8,256]{2,1,0:T(8,128)(2,1)S(1)}, bf16[18,8,256]{2,1,0:T(8,128)(2,1)S(1)}, u32[]{:S(2)}, u32[]{:S(2)}) collective-permute-start(bf16[18,8,256]{2,1,0:T(8,128)(2,1)S(1)} %add_convert_fusion.1), channel_id=1, source_target_pairs={{0,2},{1,3},{2,0},{3,1},{4,6},{5,7},{6,4},{7,5},{8,10},{9,11},{10,... | collective-permute-start | bytes 221192 | tf_op jit(solution)/shard_map/ppermute | solution.py:798
  168.6 15.4 %collective-permute-start.32 = (bf16[19,64,256]{2,1,0:T(8,128)(2,1)S(1)}, bf16[19,64,256]{2,1,0:T(8,128)(2,1)S(1)}, u32[]{:S(2)}, u32[]{:S(2)}) collective-permute-start(bf16[19,64,256]{2,1,0:T(8,128)(2,1)S(1)} %pad_maximum_fusion.4), channel_id=1, source_target_pairs={{0,8},{4,12},{8,0},{12,4},{1,9},{5,13},{9,1},{13,5},{2,10},{6,14},... | collective-permute-start | bytes 1867784 | tf_op jit(solution)/shard_map/ppermute | solution.py:798
  169.1 6.1 %collective-permute-start.28 = (bf16[18,16,256]{2,1,0:T(8,128)(2,1)S(1)}, bf16[18,16,256]{2,1,0:T(8,128)(2,1)S(1)}, u32[]{:S(2)}, u32[]{:S(2)}) collective-permute-start(bf16[18,16,256]{2,1,0:T(8,128)(2,1)S(1)} %pad_maximum_fusion.11), channel_id=1, source_target_pairs={{0,1},{1,0},{2,3},{3,2},{4,5},{5,4},{6,7},{7,6},{8,9},{9,8},{10,11... | collective-permute-start | bytes 442376 | tf_op jit(solution)/shard_map/ppermute | solution.py:798
  172.1 11.9 %collective-permute-start.31 = (bf16[19,64,256]{2,1,0:T(8,128)(2,1)S(1)}, bf16[19,64,256]{2,1,0:T(8,128)(2,1)S(1)}, u32[]{:S(2)}, u32[]{:S(2)}) collective-permute-start(bf16[19,64,256]{2,1,0:T(8,128)(2,1)S(1)} %pad_maximum_fusion.3), channel_id=1, source_target_pairs={{0,4},{4,0},{8,12},{12,8},{1,5},{5,1},{9,13},{13,9},{2,6},{6,2},{1... | collective-permute-start | bytes 1867784 | tf_op jit(solution)/shard_map/ppermute | solution.py:798
  175.3 5.2 %collective-permute-start.29 = (bf16[9,32,256]{2,1,0:T(8,128)(2,1)S(1)}, bf16[9,32,256]{2,1,0:T(8,128)(2,1)S(1)}, u32[]{:S(2)}, u32[]{:S(2)}) collective-permute-start(bf16[9,32,256]{2,1,0:T(8,128)(2,1)S(1)} %get-tuple-element.216), channel_id=1, source_target_pairs={{0,8},{4,12},{8,0},{12,4},{1,9},{5,13},{9,1},{13,5},{2,10},{6,14},... | collective-permute-start | bytes 442376 | tf_op jit(solution)/shard_map/ppermute | solution.py:798
  176.2 7.9 %collective-permute-start.30 = (bf16[9,32,256]{2,1,0:T(8,128)(2,1)S(1)}, bf16[9,32,256]{2,1,0:T(8,128)(2,1)S(1)}, u32[]{:S(2)}, u32[]{:S(2)}) collective-permute-start(bf16[9,32,256]{2,1,0:T(8,128)(2,1)S(1)} %get-tuple-element.215), channel_id=1, source_target_pairs={{0,4},{4,0},{8,12},{12,8},{1,5},{5,1},{9,13},{13,9},{2,6},{6,2},{1... | collective-permute-start | bytes 442376 | tf_op jit(solution)/shard_map/ppermute | solution.py:798
  185.1 6.3 %collective-permute-start.35 = (bf16[19,256,256]{2,1,0:T(8,128)(2,1)S(1)}, bf16[19,256,256]{2,1,0:T(8,128)(2,1)}, u32[]{:S(2)}, u32[]{:S(2)}) collective-permute-start(bf16[19,256,256]{2,1,0:T(8,128)(2,1)S(1)} %pad_maximum_fusion.half_ref), channel_id=1, source_target_pairs={{0,16},{16,0},{1,17},{17,1},{2,18},{18,2},{3,19},{19,3},{4,20},{20... | collective-permute-start | bytes 7471112 | tf_op jit(solution)/shard_map/ppermute | solution.py:798
  185.3 9.6 %collective-permute-start.34 = (bf16[9,64,256]{2,1,0:T(8,128)(2,1)S(1)}, bf16[9,64,256]{2,1,0:T(8,128)(2,1)}, u32[]{:S(2)}, u32[]{:S(2)}) collective-permute-start(bf16[9,64,256]{2,1,0:T(8,128)(2,1)S(1)} %pad_maximum_fusion.9), channel_id=1, source_target_pairs={{0,8},{4,12},{8,0},{12,4},{1,9},{5,13},{9,1},{13,5},{2,10},{6,14},... | collective-permute-start | bytes 884744 | tf_op jit(solution)/shard_map/ppermute | solution.py:798
  186.6 9.7 %collective-permute-start.33 = (bf16[9,64,256]{2,1,0:T(8,128)(2,1)}, bf16[9,64,256]{2,1,0:T(8,128)(2,1)}, u32[]{:S(2)}, u32[]{:S(2)}) collective-permute-start(bf16[9,64,256]{2,1,0:T(8,128)(2,1)} %pad_maximum_fusion.8), channel_id=1, source_target_pairs={{0,4},{4,0},{8,12},{12,8},{1,5},{5,1},{9,13},{13,9},{2,6},{6,2},{1... | collective-permute-start | bytes 884744 | tf_op jit(solution)/shard_map/ppermute | solution.py:798
  198.6 2.9 %collective-permute-start.36 = (bf16[9,256,256]{2,1,0:T(8,128)(2,1)S(1)}, bf16[9,256,256]{2,1,0:T(8,128)(2,1)S(1)}, u32[]{:S(2)}, u32[]{:S(2)}) collective-permute-start(bf16[9,256,256]{2,1,0:T(8,128)(2,1)S(1)} %pad_maximum_fusion.1.half_ref), channel_id=1, source_target_pairs={{0,16},{16,0},{1,17},{17,1},{2,18},{18,2},{3,19},{19,3},{4,20},{20... | collective-permute-start | bytes 3538952 | tf_op jit(solution)/shard_map/ppermute | solution.py:798
  (15 other events, 96.9 us)

commit v9 on v8

--- a/solution.py
+++ b/solution.py
@@ -927,8 +927,7 @@
         top = bot = lax.ppermute(packed["down"], "rows", [(0, 1), (1, 0)])
     else:
         top, bot = shifted(packed[N.down], N.rows, 1), shifted(packed[N.up], N.rows, -1)
-    lft1 = shifted(jnp.concatenate([top1[:, :, -1:], inputs[:, :, -1:]], axis=1), N.cols, 1)
-    (top, bot), lft1 = lax.optimization_barrier(((top, bot), lft1))
+    (top, bot), top1 = lax.optimization_barrier(((top, bot), top1))
     lines = (rows_in + 2 * over) * groups, (rows + 2 * rim) * groups, (rows + 3) * groups
     n_strip = over * lines[0] + (rim + 1) // 2 * lines[1] + width // 128 * lines[2]
     n_strip = -(-n_strip // 16) * 16
@@ -945,8 +944,10 @@
         ),
         smem=(N.flags,),
     )
-    lft, rgt = shifted(strips[N.right], N.cols, 1), shifted(strips[N.left], N.cols, -1)
-    lft1, _ = lax.optimization_barrier((lft1, strips[N.right]))
+    edge = jnp.concatenate([top1[:, :, -1:], inputs[:, :, -1:]], axis=1)
+    edge, right, left = lax.optimization_barrier((edge, strips[N.right], strips[N.left]))
+    lft1, right, left = lax.optimization_barrier((shifted(edge, N.cols, 1), right, left))
+    lft, rgt = shifted(right, N.cols, 1), shifted(left, N.cols, -1)
     stats = call(
         stats_kernel,
         dict(x=inputs, top=top1, lft=lft1, own=own, w1=w1, wp=w_proj),

time: 205 us -> 205 us (level)
  no operation moved by 1% of the time
where the time goes in v9:
time: 205 us; the launch traced here: 204 us
  Pallas kernels  67.4 us (33%)
  starting transfers between devices  65.8 us (32%)
  waiting for transfers between devices  58.6 us (29%)
  other arithmetic  7.78 us (4%)
  local copies, waits for them, and re-layouts  2.63 us (1%)
    pallas_call x11, Pallas kernels, call(): pl.pallas_call(run, out_shape=list(outs.values()), in_specs=[spec(n) for...  57.1 us
    ppermute x32, starting transfers between devices, partner(): return lax.ppermute(value, axis, [(i, i ^ step) for i in range(count)])  36.3 us
    ppermute x32, waiting for transfers between devices, partner(): return lax.ppermute(value, axis, [(i, i ^ step) for i in range(count)])  34.9 us
    all_to_all x4, waiting for transfers between devices, gather_sum(): return lax.all_to_all(spread, axes, 0, 0)  21.2 us
    all_to_all x4, starting transfers between devices, gather_sum(): return lax.all_to_all(spread, axes, 0, 0)  16.7 us
    ppermute x4, starting transfers between devices, shifted(): lax.ppermute(value, axis, [(source, source + steps) for source in range(f...  12.3 us
    pallas_call x4, Pallas kernels, widen(): pl.pallas_call(body, out_shape=[shape((taps * per, n, 2 * m))] + [shape((...  10.3 us
  transfers between devices with their start and end apart: 41, of which 26 were waited for; matrix products, arithmetic and copies ran while one was open for 1% of the time, Pallas kernels for 21%

profile of v9, /device:TPU:0, one launch (start us, length us, event | category | flops | bytes accessed | tf_op | source)
XLA Modules:
  0.0 203.8 jit_solution(15079188550364402170)
XLA Ops:
  5.1 2.0 collective-permute-start.1
  9.2 4.8 %collective-permute-start.2 = (bf16[2,17,1,256]{3,2,1,0:T(2,128)(2,1)S(1)}, bf16[2,17,1,256]{3,2,1,0:T(2,128)(2,1)S(1)}, u32[]{:S(2)}, u32[]{:S(2)}) collective-permute-start(bf16[2,17,1,256]{3,2,1,0:T(2,128)(2,1)S(1)} %pad_maximum_fusion.12), channel_id=1, source_target_pairs={{0,4},{4,8},{8,12},{1,5},{5,9},{9,13},{2,6},{6,10},{10,14},{3,7},{... | collective-permute-start | bytes 52232 | tf_op jit(solution)/shard_map/ppermute | solution.py:785
  14.1 1.6 collective-permute-done.2.refs_2_
  15.7 4.2 %collective-permute-start.3 = (bf16[480,256]{1,0:T(8,128)(2,1)S(1)}, bf16[480,256]{1,0:T(8,128)(2,1)S(1)}, u32[]{:S(2)}, u32[]{:S(2)}) collective-permute-start(bf16[480,256]{1,0:T(8,128)(2,1)S(1)} %get-tuple-element.115), channel_id=1, source_target_pairs={{0,4},{4,8},{8,12},{1,5},{5,9},{9,13},{2,6},{6,10},{10,14},{3,7},{... | collective-permute-start | bytes 737288 | tf_op jit(solution)/shard_map/ppermute | solution.py:785
  21.2 3.3 %shard_map.206 = f32[32,1,2176]{2,1,0:T(1,128)} custom-call(bf16[2,16,32,256]{3,2,1,0:T(8,128)(2,1)S(1)} %copy-done.1, bf16[2,1,32,256]{3,2,1,0:T(8,128)(2,1)S(1)} %collective-permute-done.1.refs_1_, bf16[2,17,1,256]{3,2,1,0:T(2,128)(2,1)S(1)} %collective-permute-done.2.refs_2_, bf16[2,8,16,128]{3,2,1,0:T(8,128)(2,1)S(1)} %broadcast_in_dim.2.refs_3_, ...), custom_call_target="tpu_custom_call" | custom-call | tf_op jit(solution)/shard_map/pallas_call | solution.py:113
  24.6 7.9 %all-to-all-start = ((f32[32,1,2176]{2,1,0:T(1,128)}), f32[32,1,2176]{2,1,0:T(1,128)S(1)}, u32[]{:S(2)}, u32[]{:S(2)}) async-start(f32[32,1,2176]{2,1,0:T(1,128)} %shard_map.206), calls=%async_computation | async-start | bytes 557056 | tf_op jit(solution)/shard_map/all_to_all | solution.py:789
  32.6 5.7 %shard_map.205 = (f32[624,512]{1,0:T(8,128)}, f32[624,512]{1,0:T(8,128)}, bf16[624,768]{1,0:T(8,128)(2,1)}, bf16[672,768]{1,0:T(8,128)(2,1)}, f32[624,128]{1,0:T...) custom-call(s32[2]{0:T(128)S(1)} %add_convert_fusion.2.refs_0_, bf16[2,16,32,256]{3,2,1,0:T(8,128)(2,1)} %refs_0_.1, ...), custom_call_target="tpu_custom_call" | custom-call | flops 20000000000 | tf_op jit(solution)/shard_map/pallas_call | solution.py:113
  38.3 5.5 %all-to-all-done.refs_1_ = f32[32,1,2176]{2,1,0:T(1,128)S(1)} async-done(((f32[32,1,2176]{2,1,0:T(1,128)}), f32[32,1,2176]{2,1,0:T(1,128)S(1)}, u32[]{:S(2)}, u32[]{:S(2)}) %all-to-all-start) | async-done | bytes 278560 | tf_op jit(solution)/shard_map/all_to_all | solution.py:789
  43.8 6.3 %shard_map.207 = (bf16[624,1536]{1,0:T(8,128)(2,1)}, f32[528,512]{1,0:T(8,128)}, f32[32,1,1024]{2,1,0:T(1,128)}, f32[8,512]{1,0:T(8,128)S(1)}) custom-call(f32[624,512]{1,0:T(8,128)} %get-tuple-element.117.refs_0_.refs_3_, f32[32,1,2176]{2,1,0:T(1,128)S(1)} %all-to-all-done.refs_1_, f32[1,512]{1,0:T(1,128)S(1)} %bitcast.33, f32[1,512]{1,0:T(1,128)S(1)} %bitcast.31, ...), custom_call_target="tpu_custom_call" | custom-call | tf_op jit(solution)/shard_map/pallas_call | solution.py:113
  50.1 2.6 %all-to-all-start.1 = ((f32[32,1,1024]{2,1,0:T(1,128)}), f32[32,1,1024]{2,1,0:T(1,128)S(1)}, u32[]{:S(2)}, u32[]{:S(2)}) async-start(f32[32,1,1024]{2,1,0:T(1,128)} %get-tuple-element.124), calls=%async_computation.1 | async-start | bytes 262144 | tf_op jit(solution)/shard_map/all_to_all | solution.py:789
  52.9 7.7 %all-to-all-done.1.refs_4_ = f32[32,1,1024]{2,1,0:T(1,128)S(1)} async-done(((f32[32,1,1024]{2,1,0:T(1,128)}), f32[32,1,1024]{2,1,0:T(1,128)S(1)}, u32[]{:S(2)}, u32[]{:S(2)}) %all-to-all-start.1) | async-done | bytes 131104 | tf_op jit(solution)/shard_map/all_to_all | solution.py:789
  60.7 5.5 %shard_map.208 = (bf16[2,8,16,512]{3,2,1,0:T(8,128)(2,1)}, f32[528,512]{1,0:T(8,128)}, f32[32,1,1536]{2,1,0:T(1,128)}, f32[8,512]{1,0:T(8,128)S(1)}, f32[3,384,256]{2,1,0:T(8,128)}, /*index=5*/f32[3,384,256]{2,1,0:T(8,128)}) custom-call(s32[5]{0:T(128)S(1)} %stack.32.refs_0_, f32[528,512]{1,0:T(8,128)} %get-tuple-element.121.refs_1_.refs_2_, ...), custom_call_target="tpu_custom_call" | custom-call | tf_op jit(solution)/shard_map/pallas_call | solution.py:113
  66.8 2.8 %all-to-all-start.2 = ((f32[32,1,1536]{2,1,0:T(1,128)}), f32[32,1,1536]{2,1,0:T(1,128)S(1)}, u32[]{:S(2)}, u32[]{:S(2)}) async-start(f32[32,1,1536]{2,1,0:T(1,128)} %get-tuple-element.135), calls=%async_computation.2 | async-start | bytes 393216 | tf_op jit(solution)/shard_map/all_to_all | solution.py:789
  70.8 8.0 %all-to-all-done.2.refs_7_.refs_8_ = f32[32,1,1536]{2,1,0:T(1,128)S(1)} async-done(((f32[32,1,1536]{2,1,0:T(1,128)}), f32[32,1,1536]{2,1,0:T(1,128)S(1)}, u32[]{:S(2)}, u32[]{:S(2)}) %all-to-all-start.2) | async-done | bytes 196640 | tf_op jit(solution)/shard_map/all_to_all | solution.py:789
  78.8 8.4 %shard_map.209 = (bf16[19,64,256]{2,1,0:T(8,128)(2,1)S(1)}, f32[19,64,256]{2,1,0:T(8,128)}, bf16[19,64,256]{2,1,0:T(8,128)(2,1)}, f32[19,64,256]{2,1,0:T(8,128)}) custom-call(s32[5]{0:T(128)S(1)} %stack.32.refs_0_, f32[3,384,256]{2,1,0:T(8,128)} %get-tuple-element.130.refs_1_, f32[3,384,256]{2,1,0:T(8,128)} %copy-done.18, ...), custom_call_target="tpu_custom_call" | custom-call | tf_op jit(solution)/shard_map/pallas_call | solution.py:113
  88.3 8.6 %shard_map.211 = (f32[432,512]{1,0:T(8,128)}, f32[432,512]{1,0:T(8,128)}, f32[32,1,1024]{2,1,0:T(1,128)}, f32[2,384,256]{2,1,0:T(8,128)}, f32[2,384,256]{2,1,0:T...) custom-call(s32[5]{0:T(128)S(1)} %stack.32.refs_0_, ...), custom_call_target="tpu_custom_call" | custom-call | tf_op jit(solution)/shard_map/pallas_call | solution.py:113
  97.5 3.4 %all-to-all-start.3 = ((f32[32,1,1024]{2,1,0:T(1,128)}), f32[32,1,1024]{2,1,0:T(1,128)S(1)}, u32[]{:S(2)}, u32[]{:S(2)}) async-start(f32[32,1,1024]{2,1,0:T(1,128)} %get-tuple-element.156), calls=%async_computation.3 | async-start | bytes 262144 | tf_op jit(solution)/shard_map/all_to_all | solution.py:789
  100.9 1.9 collective-permute-done.10.refs_4_
  103.7 3.8 %shard_map.210 = (bf16[19,32,256]{2,1,0:T(8,128)(2,1)}, f32[19,32,256]{2,1,0:T(8,128)}, bf16[19,32,256]{2,1,0:T(8,128)(2,1)}, f32[19,32,256]{2,1,0:T(8,128)}) custom-call(s32[5]{0:T(128)} %copy-done.10, f32[19,64,256]{2,1,0:T(8,128)} %get-tuple-element.142.refs_1_, bf16[19,64,256]{2,1,0:T(8,128)(2,1)} %collective-permute-done.9.refs_2_, ...), custom_call_target="tpu_custom_call" | custom-call | flops 20000000000 | tf_op jit(solution)/shard_map/pallas_call | solution.py:113
  109.5 6.9 %shard_map.212 = (bf16[9,64,256]{2,1,0:T(8,128)(2,1)S(1)}, f32[9,64,256]{2,1,0:T(8,128)S(1)}, bf16[9,64,256]{2,1,0:T(8,128)(2,1)S(1)}, f32[9,64,256]{2,1,0:T(8,1...) custom-call(s32[5]{0:T(128)S(1)} %copy-done.11, f32[2,384,256]{2,1,0:T(8,128)} %get-tuple-element.153.refs_1_, ...), custom_call_target="tpu_custom_call" | custom-call | flops 20000000000 | tf_op jit(solution)/shard_map/pallas_call | solution.py:113
  116.7 1.4 convert_add_fusion.1
  118.3 1.5 collective-permute-start.15
  119.8 1.5 collective-permute-start.16
  121.9 6.4 %shard_map.213 = bf16[2,16,32,256]{3,2,1,0:T(8,128)(2,1)} custom-call(f32[432,512]{1,0:T(8,128)S(1)} %copy-done.14, f32[432,512]{1,0:T(8,128)} %get-tuple-element.167.refs_1_, bf16[384,512]{1,0:T(8,128)(2,1)S(1)} %get-tuple-element.168.refs_2_, bf16[3,768,512]{2,1,0:T(8,128)(2,1)} %bitcast.47, bf16[256,512]{1,0:T(8,128)(2,1)S(1)} %copy-done.5, ...), custom_call_target="tpu_custom_call" | custom-call | flops 10000000000 | tf_op jit(solution)/shard_map/pallas_call | solution.py:113
  128.7 1.3 collective-permute-start.20
  130.3 1.8 collective-permute-start.18
  134.0 3.5 %collective-permute-done.19 = bf16[9,32,256]{2,1,0:T(8,128)(2,1)S(1)} collective-permute-done((bf16[9,32,256]{2,1,0:T(8,128)(2,1)S(1)}, bf16[9,32,256]{2,1,0:T(8,128)(2,1)S(1)}, u32[]{:S(2)}, u32[]{:S(2)}) %collective-permute-start.19) | collective-permute-done | bytes 147488 | tf_op jit(solution)/shard_map/ppermute | solution.py:798
  138.9 4.1 %collective-permute-start.22 = (bf16[18,16,256]{2,1,0:T(8,128)(2,1)S(1)}, bf16[18,16,256]{2,1,0:T(8,128)(2,1)S(1)}, u32[]{:S(2)}, u32[]{:S(2)}) collective-permute-start(bf16[18,16,256]{2,1,0:T(8,128)(2,1)S(1)} %select_convert_fusion.2), channel_id=1, source_target_pairs={{0,1},{1,0},{2,3},{3,2},{4,5},{5,4},{6,7},{7,6},{8,9},{9,8},{10,11... | collective-permute-start | bytes 442376 | tf_op jit(solution)/shard_map/ppermute | solution.py:798
  143.0 5.5 %collective-permute-done.22 = bf16[18,16,256]{2,1,0:T(8,128)(2,1)S(1)} collective-permute-done((bf16[18,16,256]{2,1,0:T(8,128)(2,1)S(1)}, bf16[18,16,256]{2,1,0:T(8,128)(2,1)S(1)}, u32[]{:S(2)}, u32[]{:S(2)}) %collective-permute-start.22) | collective-permute-done | bytes 147488 | tf_op jit(solution)/shard_map/ppermute | solution.py:798
  148.5 1.4 collective-permute-start.23
  150.0 2.5 %collective-permute-start.24 = (bf16[18,8,256]{2,1,0:T(8,128)(2,1)S(1)}, bf16[18,8,256]{2,1,0:T(8,128)(2,1)S(1)}, u32[]{:S(2)}, u32[]{:S(2)}) collective-permute-start(bf16[18,8,256]{2,1,0:T(8,128)(2,1)S(1)} %select_convert_fusion.5), channel_id=1, source_target_pairs={{0,2},{1,3},{2,0},{3,1},{4,6},{5,7},{6,4},{7,5},{8,10},{9,11},{10,... | collective-permute-start | bytes 221192 | tf_op jit(solution)/shard_map/ppermute | solution.py:798
  152.5 3.4 %collective-permute-done.24 = bf16[18,8,256]{2,1,0:T(8,128)(2,1)S(1)} collective-permute-done((bf16[18,8,256]{2,1,0:T(8,128)(2,1)S(1)}, bf16[18,8,256]{2,1,0:T(8,128)(2,1)S(1)}, u32[]{:S(2)}, u32[]{:S(2)}) %collective-permute-start.24) | collective-permute-done | bytes 73760 | tf_op jit(solution)/shard_map/ppermute | solution.py:798
  158.4 1.5 collective-permute-start.26
  160.0 2.3 %collective-permute-start.27 = (bf16[18,8,256]{2,1,0:T(8,128)(2,1)S(1)}, bf16[18,8,256]{2,1,0:T(8,128)(2,1)S(1)}, u32[]{:S(2)}, u32[]{:S(2)}) collective-permute-start(bf16[18,8,256]{2,1,0:T(8,128)(2,1)S(1)} %add_convert_fusion.1), channel_id=1, source_target_pairs={{0,2},{1,3},{2,0},{3,1},{4,6},{5,7},{6,4},{7,5},{8,10},{9,11},{10,... | collective-permute-start | bytes 221192 | tf_op jit(solution)/shard_map/ppermute | solution.py:798
  162.3 3.0 %collective-permute-done.27 = bf16[18,8,256]{2,1,0:T(8,128)(2,1)S(1)} collective-permute-done((bf16[18,8,256]{2,1,0:T(8,128)(2,1)S(1)}, bf16[18,8,256]{2,1,0:T(8,128)(2,1)S(1)}, u32[]{:S(2)}, u32[]{:S(2)}) %collective-permute-start.27) | collective-permute-done | bytes 73760 | tf_op jit(solution)/shard_map/ppermute | solution.py:798
  165.3 2.4 %collective-permute-done.25 = bf16[19,32,256]{2,1,0:T(8,128)(2,1)S(1)} collective-permute-done((bf16[19,32,256]{2,1,0:T(8,128)(2,1)S(1)}, bf16[19,32,256]{2,1,0:T(8,128)(2,1)S(1)}, u32[]{:S(2)}, u32[]{:S(2)}) %collective-permute-start.25) | collective-permute-done | bytes 311328 | tf_op jit(solution)/shard_map/ppermute | solution.py:798
  169.1 3.0 %collective-permute-start.28 = (bf16[18,16,256]{2,1,0:T(8,128)(2,1)S(1)}, bf16[18,16,256]{2,1,0:T(8,128)(2,1)S(1)}, u32[]{:S(2)}, u32[]{:S(2)}) collective-permute-start(bf16[18,16,256]{2,1,0:T(8,128)(2,1)S(1)} %pad_maximum_fusion.11), channel_id=1, source_target_pairs={{0,1},{1,0},{2,3},{3,2},{4,5},{5,4},{6,7},{7,6},{8,9},{9,8},{10,11... | collective-permute-start | bytes 442376 | tf_op jit(solution)/shard_map/ppermute | solution.py:798
  172.1 1.5 collective-permute-start.31
  173.6 1.6 collective-permute-done.28
  176.2 1.8 collective-permute-start.30
  178.0 2.6 %collective-permute-done.29 = bf16[9,32,256]{2,1,0:T(8,128)(2,1)S(1)} collective-permute-done((bf16[9,32,256]{2,1,0:T(8,128)(2,1)S(1)}, bf16[9,32,256]{2,1,0:T(8,128)(2,1)S(1)}, u32[]{:S(2)}, u32[]{:S(2)}) %collective-permute-start.29) | collective-permute-done | bytes 147488 | tf_op jit(solution)/shard_map/ppermute | solution.py:798
  180.5 3.5 %collective-permute-done.30 = bf16[9,32,256]{2,1,0:T(8,128)(2,1)S(1)} collective-permute-done((bf16[9,32,256]{2,1,0:T(8,128)(2,1)S(1)}, bf16[9,32,256]{2,1,0:T(8,128)(2,1)S(1)}, u32[]{:S(2)}, u32[]{:S(2)}) %collective-permute-start.30) | collective-permute-done | bytes 147488 | tf_op jit(solution)/shard_map/ppermute | solution.py:798
  186.6 2.0 collective-permute-start.33
  188.6 2.8 %shard_map.214 = (f32[18,256,512]{2,1,0:T(8,128)}, f32[1,256,512]{2,1,0:T(8,128)}) custom-call(s32[1]{0:T(128)} %bitcast.side_ref, bf16[19,256,256]{2,1,0:T(8,128)(2,1)S(1)} %pad_maximum_fusion.half_ref), custom_call_target="tpu_custom_call" | custom-call | tf_op jit(solution)/shard_map/pallas_call | solution.py:730
  191.4 3.4 %shard_map.215 = (f32[18,256,512]{2,1,0:T(8,128)}, f32[1,256,512]{2,1,0:T(8,128)}) custom-call(s32[1]{0:T(128)} %bitcast.15.side_ref, bf16[19,256,256]{2,1,0:T(8,128)(2,1)} %collective-permute-done.35.half_ref, f32[18,256,512]{2,1,0:T(8,128)} %get-tuple-element.191.refs_0_, ...), custom_call_target="tpu_custom_call", output_to_operand_aliasing={{0}: (2, {}), {1}: (3, {})} | custom-call | tf_op jit(solution)/shard_map/pallas_call | solution.py:730
  194.9 1.5 collective-permute-done.33
  198.7 2.1 %shard_map.216.refs_0_ = f32[9,256,512]{2,1,0:T(8,128)} custom-call(s32[1]{0:T(128)} %bitcast.side_ref, bf16[9,256,256]{2,1,0:T(8,128)(2,1)S(1)} %pad_maximum_fusion.1.half_ref), custom_call_target="tpu_custom_call" | custom-call | tf_op jit(solution)/shard_map/pallas_call | solution.py:730
  201.5 2.1 %shard_map.217 = f32[9,256,512]{2,1,0:T(8,128)} custom-call(s32[1]{0:T(128)} %bitcast.15.side_ref, bf16[9,256,256]{2,1,0:T(8,128)(2,1)S(1)} %collective-permute-done.36.half_ref, f32[9,256,512]{2,1,0:T(8,128)} %shard_map.216.refs_0_), custom_call_target="tpu_custom_call", output_to_operand_aliasing={{}: (2, {})} | custom-call | tf_op jit(solution)/shard_map/pallas_call | solution.py:730
  (138 shorter events, 30.2 us)
Async XLA Ops:
  3.5 17.7 %copy-start.1 = (bf16[2,16,32,256]{3,2,1,0:T(8,128)(2,1)S(1)}, bf16[2,16,32,256]{3,2,1,0:T(8,128)(2,1)}, u32[]{:S(2)}) copy-start(bf16[2,16,32,256]{3,2,1,0:T(8,128)(2,1)} %refs_0_.1) | copy-start | bytes 1572868
  3.5 17.7 %copy-start.5 = (bf16[256,512]{1,0:T(8,128)(2,1)S(1)}, bf16[256,512]{1,0:T(8,128)(2,1)}, u32[]{:S(2)}) copy-start(bf16[256,512]{1,0:T(8,128)(2,1)} %refs_4_.1) | copy-start | bytes 786436
  4.5 3.3 %collective-permute-start = (bf16[672,256]{1,0:T(8,128)(2,1)S(1)}, bf16[672,256]{1,0:T(8,128)(2,1)S(1)}, u32[]{:S(2)}, u32[]{:S(2)}) collective-permute-start(bf16[672,256]{1,0:T(8,128)(2,1)S(1)} %shard_map.203), channel_id=1, source_target_pairs={{0,16},{16,0},{1,17},{17,1},{2,18},{18,2},{3,19},{19,3},{4,20},{20... | collective-permute-start | bytes 1032200 | tf_op jit(solution)/shard_map/ppermute | solution.py:927
  5.1 2.8 %collective-permute-start.1 = (bf16[2,1,32,256]{3,2,1,0:T(8,128)(2,1)S(1)}, bf16[2,1,32,256]{3,2,1,0:T(8,128)(2,1)S(1)}, u32[]{:S(2)}, u32[]{:S(2)}) collective-permute-start(bf16[2,1,32,256]{3,2,1,0:T(8,128)(2,1)S(1)} %slice.57), channel_id=1, source_target_pairs={{0,16},{1,17},{2,18},{3,19},{4,20},{5,21},{6,22},{7,23},{8,24},{9,... | collective-permute-start | bytes 98312 | tf_op jit(solution)/shard_map/ppermute | solution.py:785
  9.2 6.4 %collective-permute-start.2 = (bf16[2,17,1,256]{3,2,1,0:T(2,128)(2,1)S(1)}, bf16[2,17,1,256]{3,2,1,0:T(2,128)(2,1)S(1)}, u32[]{:S(2)}, u32[]{:S(2)}) collective-permute-start(bf16[2,17,1,256]{3,2,1,0:T(2,128)(2,1)S(1)} %pad_maximum_fusion.12), channel_id=1, source_target_pairs={{0,4},{4,8},{8,12},{1,5},{5,9},{9,13},{2,6},{6,10},{10,14},{3,7},{... | collective-permute-start | bytes 52232 | tf_op jit(solution)/shard_map/ppermute | solution.py:785
  15.7 16.8 %collective-permute-start.3 = (bf16[480,256]{1,0:T(8,128)(2,1)S(1)}, bf16[480,256]{1,0:T(8,128)(2,1)S(1)}, u32[]{:S(2)}, u32[]{:S(2)}) collective-permute-start(bf16[480,256]{1,0:T(8,128)(2,1)S(1)} %get-tuple-element.115), channel_id=1, source_target_pairs={{0,4},{4,8},{8,12},{1,5},{5,9},{9,13},{2,6},{6,10},{10,14},{3,7},{... | collective-permute-start | bytes 737288 | tf_op jit(solution)/shard_map/ppermute | solution.py:785
  19.9 12.7 %collective-permute-start.4 = (bf16[480,256]{1,0:T(8,128)(2,1)S(1)}, bf16[480,256]{1,0:T(8,128)(2,1)S(1)}, u32[]{:S(2)}, u32[]{:S(2)}) collective-permute-start(bf16[480,256]{1,0:T(8,128)(2,1)S(1)} %get-tuple-element.116), channel_id=1, source_target_pairs={{4,0},{8,4},{12,8},{5,1},{9,5},{13,9},{6,2},{10,6},{14,10},{7,3},{... | collective-permute-start | bytes 737288 | tf_op jit(solution)/shard_map/ppermute | solution.py:785
  24.6 19.2 %all-to-all-start = ((f32[32,1,2176]{2,1,0:T(1,128)}), f32[32,1,2176]{2,1,0:T(1,128)S(1)}, u32[]{:S(2)}, u32[]{:S(2)}) async-start(f32[32,1,2176]{2,1,0:T(1,128)} %shard_map.206), calls=%async_computation | async-start | bytes 557056 | tf_op jit(solution)/shard_map/all_to_all | solution.py:789
  43.7 16.9 %copy-start.6 = (f32[512]{0:T(512)S(1)}, f32[512]{0:T(512)}, u32[]{:S(2)}) copy-start(f32[512]{0:T(512)} %param.17) | copy-start | bytes 6148
  43.7 16.9 %copy-start.7 = (f32[512]{0:T(512)S(1)}, f32[512]{0:T(512)}, u32[]{:S(2)}) copy-start(f32[512]{0:T(512)} %param.20) | copy-start | bytes 6148
  43.7 16.9 %copy-start.12 = (f32[512]{0:T(512)S(1)}, f32[512]{0:T(512)}, u32[]{:S(2)}) copy-start(f32[512]{0:T(512)} %param.18) | copy-start | bytes 6148
  43.8 16.9 %copy-start.13 = (f32[512]{0:T(512)S(1)}, f32[512]{0:T(512)}, u32[]{:S(2)}) copy-start(f32[512]{0:T(512)} %param.21) | copy-start | bytes 6148
  50.1 10.6 %collective-permute-start.5 = (bf16[624,1536]{1,0:T(8,128)(2,1)}, bf16[624,1536]{1,0:T(8,128)(2,1)S(1)}, u32[]{:S(2)}, u32[]{:S(2)}) collective-permute-start(bf16[624,1536]{1,0:T(8,128)(2,1)} %get-tuple-element.125.refs_3_), channel_id=1, source_target_pairs={{0,16},{16,0},{1,17},{17,1},{2,18},{18,2},{3,19},{19,3},{4,20},{20... | collective-permute-start | bytes 5750792 | tf_op jit(solution)/shard_map/ppermute | solution.py:798
  50.1 10.5 %all-to-all-start.1 = ((f32[32,1,1024]{2,1,0:T(1,128)}), f32[32,1,1024]{2,1,0:T(1,128)S(1)}, u32[]{:S(2)}, u32[]{:S(2)}) async-start(f32[32,1,1024]{2,1,0:T(1,128)} %get-tuple-element.124), calls=%async_computation.1 | async-start | bytes 262144 | tf_op jit(solution)/shard_map/all_to_all | solution.py:789
  52.9 35.4 %copy-start.10 = (s32[5]{0:T(128)}, s32[5]{0:T(128)S(1)}, u32[]{:S(2)}) copy-start(s32[5]{0:T(128)S(1)} %stack.32.refs_0_) | copy-start | bytes 64
  66.2 4.0 %collective-permute-start.6 = (f32[3,384,256]{2,1,0:T(8,128)}, f32[3,384,256]{2,1,0:T(8,128)S(1)}, u32[]{:S(2)}, u32[]{:S(2)}) collective-permute-start(f32[3,384,256]{2,1,0:T(8,128)} %get-tuple-element.131), channel_id=1, source_target_pairs={{0,16},{16,0},{1,17},{17,1},{2,18},{18,2},{3,19},{19,3},{4,20},{20... | collective-permute-start | bytes 3538952 | tf_op jit(solution)/shard_map/ppermute | solution.py:798
  66.3 4.5 %collective-permute-start.7 = (bf16[624,768]{1,0:T(8,128)(2,1)}, bf16[624,768]{1,0:T(8,128)(2,1)}, u32[]{:S(2)}, u32[]{:S(2)}) collective-permute-start(bf16[624,768]{1,0:T(8,128)(2,1)} %get-tuple-element.134.refs_5_.refs_3_), channel_id=1, source_target_pairs={{0,16},{16,0},{1,17},{17,1},{2,18},{18,2},{3,19},{19,3},{4,20},{20... | collective-permute-start | bytes 2875400 | tf_op jit(solution)/shard_map/ppermute | solution.py:798
  66.8 12.0 %all-to-all-start.2 = ((f32[32,1,1536]{2,1,0:T(1,128)}), f32[32,1,1536]{2,1,0:T(1,128)S(1)}, u32[]{:S(2)}, u32[]{:S(2)}) async-start(f32[32,1,1536]{2,1,0:T(1,128)} %get-tuple-element.135), calls=%async_computation.2 | async-start | bytes 393216 | tf_op jit(solution)/shard_map/all_to_all | solution.py:789
  70.2 8.6 %collective-permute-start.8 = (f32[624,128]{1,0:T(8,128)S(1)}, f32[624,128]{1,0:T(8,128)S(1)}, u32[]{:S(2)}, u32[]{:S(2)}) collective-permute-start(f32[624,128]{1,0:T(8,128)S(1)} %get-tuple-element.137.refs_5_.refs_10_.refs_12_.refs_14_), channel_id=1, source_target_pairs={{0,16},{16,0},{1,17},{17,1},{2,18},{18,2},{3,19},{19,3},{4,20},{20... | collective-permute-start | bytes 958472 | tf_op jit(solution)/shard_map/ppermute | solution.py:798
  87.2 15.6 %collective-permute-start.10 = (bf16[19,64,256]{2,1,0:T(8,128)(2,1)}, bf16[19,64,256]{2,1,0:T(8,128)(2,1)S(1)}, u32[]{:S(2)}, u32[]{:S(2)}) collective-permute-start(bf16[19,64,256]{2,1,0:T(8,128)(2,1)} %get-tuple-element.145), channel_id=1, source_target_pairs={{0,8},{4,12},{8,0},{12,4},{1,9},{5,13},{9,1},{13,5},{2,10},{6,14},... | collective-permute-start | bytes 1867784 | tf_op jit(solution)/shard_map/ppermute | solution.py:798
  88.2 15.2 %collective-permute-start.9 = (bf16[19,64,256]{2,1,0:T(8,128)(2,1)S(1)}, bf16[19,64,256]{2,1,0:T(8,128)(2,1)}, u32[]{:S(2)}, u32[]{:S(2)}) collective-permute-start(bf16[19,64,256]{2,1,0:T(8,128)(2,1)S(1)} %get-tuple-element.143), channel_id=1, source_target_pairs={{0,4},{4,0},{8,12},{12,8},{1,5},{5,1},{9,13},{13,9},{2,6},{6,2},{1... | collective-permute-start | bytes 1867784 | tf_op jit(solution)/shard_map/ppermute | solution.py:798
  88.3 21.1 %collective-permute-start.14 = (bf16[672,768]{1,0:T(8,128)(2,1)}, bf16[672,768]{1,0:T(8,128)(2,1)}, u32[]{:S(2)}, u32[]{:S(2)}) collective-permute-start(bf16[672,768]{1,0:T(8,128)(2,1)} %get-tuple-element.155.refs_5_), channel_id=1, source_target_pairs={{0,16},{16,0},{1,17},{17,1},{2,18},{18,2},{3,19},{19,3},{4,20},{20... | collective-permute-start | bytes 3096584 | tf_op jit(solution)/shard_map/ppermute | solution.py:798
  96.9 12.5 %collective-permute-start.13 = (f32[2,384,256]{2,1,0:T(8,128)}, f32[2,384,256]{2,1,0:T(8,128)}, u32[]{:S(2)}, u32[]{:S(2)}) collective-permute-start(f32[2,384,256]{2,1,0:T(8,128)} %get-tuple-element.154), channel_id=1, source_target_pairs={{0,16},{16,0},{1,17},{17,1},{2,18},{18,2},{3,19},{19,3},{4,20},{20... | collective-permute-start | bytes 2359304 | tf_op jit(solution)/shard_map/ppermute | solution.py:798
  97.5 12.0 %all-to-all-start.3 = ((f32[32,1,1024]{2,1,0:T(1,128)}), f32[32,1,1024]{2,1,0:T(1,128)S(1)}, u32[]{:S(2)}, u32[]{:S(2)}) async-start(f32[32,1,1024]{2,1,0:T(1,128)} %get-tuple-element.156), calls=%async_computation.3 | async-start | bytes 262144 | tf_op jit(solution)/shard_map/all_to_all | solution.py:789
  107.5 8.8 %collective-permute-start.11 = (bf16[19,32,256]{2,1,0:T(8,128)(2,1)}, bf16[19,32,256]{2,1,0:T(8,128)(2,1)S(1)}, u32[]{:S(2)}, u32[]{:S(2)}) collective-permute-start(bf16[19,32,256]{2,1,0:T(8,128)(2,1)} %get-tuple-element.151), channel_id=1, source_target_pairs={{0,8},{4,12},{8,0},{12,4},{1,9},{5,13},{9,1},{13,5},{2,10},{6,14},... | collective-permute-start | bytes 933896 | tf_op jit(solution)/shard_map/ppermute | solution.py:798
  108.5 8.2 %collective-permute-start.12 = (bf16[19,32,256]{2,1,0:T(8,128)(2,1)}, bf16[19,32,256]{2,1,0:T(8,128)(2,1)}, u32[]{:S(2)}, u32[]{:S(2)}) collective-permute-start(bf16[19,32,256]{2,1,0:T(8,128)(2,1)} %get-tuple-element.152), channel_id=1, source_target_pairs={{0,4},{4,0},{8,12},{12,8},{1,5},{5,1},{9,13},{13,9},{2,6},{6,2},{1... | collective-permute-start | bytes 933896 | tf_op jit(solution)/shard_map/ppermute | solution.py:798
  118.3 10.4 %collective-permute-start.15 = (bf16[38,16,256]{2,1,0:T(8,128)(2,1)S(1)}, bf16[38,16,256]{2,1,0:T(8,128)(2,1)S(1)}, u32[]{:S(2)}, u32[]{:S(2)}) collective-permute-start(bf16[38,16,256]{2,1,0:T(8,128)(2,1)S(1)} %select_convert_fusion), channel_id=1, source_target_pairs={{0,1},{1,0},{2,3},{3,2},{4,5},{5,4},{6,7},{7,6},{8,9},{9,8},{10,11... | collective-permute-start | bytes 933896 | tf_op jit(solution)/shard_map/ppermute | solution.py:798
  119.8 8.4 %collective-permute-start.16 = (bf16[9,64,256]{2,1,0:T(8,128)(2,1)S(1)}, bf16[9,64,256]{2,1,0:T(8,128)(2,1)S(1)}, u32[]{:S(2)}, u32[]{:S(2)}) collective-permute-start(bf16[9,64,256]{2,1,0:T(8,128)(2,1)S(1)} %get-tuple-element.164), channel_id=1, source_target_pairs={{0,4},{4,0},{8,12},{12,8},{1,5},{5,1},{9,13},{13,9},{2,6},{6,2},{1... | collective-permute-start | bytes 884744 | tf_op jit(solution)/shard_map/ppermute | solution.py:798
  121.3 7.4 %collective-permute-start.17 = (bf16[9,64,256]{2,1,0:T(8,128)(2,1)S(1)}, bf16[9,64,256]{2,1,0:T(8,128)(2,1)S(1)}, u32[]{:S(2)}, u32[]{:S(2)}) collective-permute-start(bf16[9,64,256]{2,1,0:T(8,128)(2,1)S(1)} %get-tuple-element.165), channel_id=1, source_target_pairs={{0,8},{4,12},{8,0},{12,4},{1,9},{5,13},{9,1},{13,5},{2,10},{6,14},... | collective-permute-start | bytes 884744 | tf_op jit(solution)/shard_map/ppermute | solution.py:798
  128.7 5.2 %collective-permute-start.20 = (bf16[9,32,256]{2,1,0:T(8,128)(2,1)S(1)}, bf16[9,32,256]{2,1,0:T(8,128)(2,1)S(1)}, u32[]{:S(2)}, u32[]{:S(2)}) collective-permute-start(bf16[9,32,256]{2,1,0:T(8,128)(2,1)S(1)} %select_convert_fusion.3), channel_id=1, source_target_pairs={{0,4},{4,0},{8,12},{12,8},{1,5},{5,1},{9,13},{13,9},{2,6},{6,2},{1... | collective-permute-start | bytes 442376 | tf_op jit(solution)/shard_map/ppermute | solution.py:798
  130.3 7.4 %collective-permute-start.18 = (bf16[38,8,256]{2,1,0:T(8,128)(2,1)S(1)}, bf16[38,8,256]{2,1,0:T(8,128)(2,1)S(1)}, u32[]{:S(2)}, u32[]{:S(2)}) collective-permute-start(bf16[38,8,256]{2,1,0:T(8,128)(2,1)S(1)} %select_convert_fusion.1), channel_id=1, source_target_pairs={{0,2},{1,3},{2,0},{3,1},{4,6},{5,7},{6,4},{7,5},{8,10},{9,11},{10,... | collective-permute-start | bytes 466952 | tf_op jit(solution)/shard_map/ppermute | solution.py:798
  132.2 5.2 %collective-permute-start.19 = (bf16[9,32,256]{2,1,0:T(8,128)(2,1)S(1)}, bf16[9,32,256]{2,1,0:T(8,128)(2,1)S(1)}, u32[]{:S(2)}, u32[]{:S(2)}) collective-permute-start(bf16[9,32,256]{2,1,0:T(8,128)(2,1)S(1)} %select_convert_fusion.4), channel_id=1, source_target_pairs={{0,8},{4,12},{8,0},{12,4},{1,9},{5,13},{9,1},{13,5},{2,10},{6,14},... | collective-permute-start | bytes 442376 | tf_op jit(solution)/shard_map/ppermute | solution.py:798
  137.9 10.6 %collective-permute-start.21 = (bf16[38,8,256]{2,1,0:T(8,128)(2,1)S(1)}, bf16[38,8,256]{2,1,0:T(8,128)(2,1)S(1)}, u32[]{:S(2)}, u32[]{:S(2)}) collective-permute-start(bf16[38,8,256]{2,1,0:T(8,128)(2,1)S(1)} %add_convert_fusion), channel_id=1, source_target_pairs={{0,2},{1,3},{2,0},{3,1},{4,6},{5,7},{6,4},{7,5},{8,10},{9,11},{10,... | collective-permute-start | bytes 466952 | tf_op jit(solution)/shard_map/ppermute | solution.py:798
  138.9 9.5 %collective-permute-start.22 = (bf16[18,16,256]{2,1,0:T(8,128)(2,1)S(1)}, bf16[18,16,256]{2,1,0:T(8,128)(2,1)S(1)}, u32[]{:S(2)}, u32[]{:S(2)}) collective-permute-start(bf16[18,16,256]{2,1,0:T(8,128)(2,1)S(1)} %select_convert_fusion.2), channel_id=1, source_target_pairs={{0,1},{1,0},{2,3},{3,2},{4,5},{5,4},{6,7},{7,6},{8,9},{9,8},{10,11... | collective-permute-start | bytes 442376 | tf_op jit(solution)/shard_map/ppermute | solution.py:798
  148.5 8.5 %collective-permute-start.23 = (bf16[38,16,256]{2,1,0:T(8,128)(2,1)S(1)}, bf16[38,16,256]{2,1,0:T(8,128)(2,1)S(1)}, u32[]{:S(2)}, u32[]{:S(2)}) collective-permute-start(bf16[38,16,256]{2,1,0:T(8,128)(2,1)S(1)} %pad_maximum_fusion.6), channel_id=1, source_target_pairs={{0,1},{1,0},{2,3},{3,2},{4,5},{5,4},{6,7},{7,6},{8,9},{9,8},{10,11... | collective-permute-start | bytes 933896 | tf_op jit(solution)/shard_map/ppermute | solution.py:798
  150.0 5.9 %collective-permute-start.24 = (bf16[18,8,256]{2,1,0:T(8,128)(2,1)S(1)}, bf16[18,8,256]{2,1,0:T(8,128)(2,1)S(1)}, u32[]{:S(2)}, u32[]{:S(2)}) collective-permute-start(bf16[18,8,256]{2,1,0:T(8,128)(2,1)S(1)} %select_convert_fusion.5), channel_id=1, source_target_pairs={{0,2},{1,3},{2,0},{3,1},{4,6},{5,7},{6,4},{7,5},{8,10},{9,11},{10,... | collective-permute-start | bytes 221192 | tf_op jit(solution)/shard_map/ppermute | solution.py:798
  157.3 10.3 %collective-permute-start.25 = (bf16[19,32,256]{2,1,0:T(8,128)(2,1)S(1)}, bf16[19,32,256]{2,1,0:T(8,128)(2,1)S(1)}, u32[]{:S(2)}, u32[]{:S(2)}) collective-permute-start(bf16[19,32,256]{2,1,0:T(8,128)(2,1)S(1)} %get-tuple-element.212), channel_id=1, source_target_pairs={{0,8},{4,12},{8,0},{12,4},{1,9},{5,13},{9,1},{13,5},{2,10},{6,14},... | collective-permute-start | bytes 933896 | tf_op jit(solution)/shard_map/ppermute | solution.py:798
  158.4 10.1 %collective-permute-start.26 = (bf16[19,32,256]{2,1,0:T(8,128)(2,1)S(1)}, bf16[19,32,256]{2,1,0:T(8,128)(2,1)S(1)}, u32[]{:S(2)}, u32[]{:S(2)}) collective-permute-start(bf16[19,32,256]{2,1,0:T(8,128)(2,1)S(1)} %get-tuple-element.211), channel_id=1, source_target_pairs={{0,4},{4,0},{8,12},{12,8},{1,5},{5,1},{9,13},{13,9},{2,6},{6,2},{1... | collective-permute-start | bytes 933896 | tf_op jit(solution)/shard_map/ppermute | solution.py:798
  160.0 5.3 %collective-permute-start.27 = (bf16[18,8,256]{2,1,0:T(8,128)(2,1)S(1)}, bf16[18,8,256]{2,1,0:T(8,128)(2,1)S(1)}, u32[]{:S(2)}, u32[]{:S(2)}) collective-permute-start(bf16[18,8,256]{2,1,0:T(8,128)(2,1)S(1)} %add_convert_fusion.1), channel_id=1, source_target_pairs={{0,2},{1,3},{2,0},{3,1},{4,6},{5,7},{6,4},{7,5},{8,10},{9,11},{10,... | collective-permute-start | bytes 221192 | tf_op jit(solution)/shard_map/ppermute | solution.py:798
  168.6 15.4 %collective-permute-start.32 = (bf16[19,64,256]{2,1,0:T(8,128)(2,1)S(1)}, bf16[19,64,256]{2,1,0:T(8,128)(2,1)S(1)}, u32[]{:S(2)}, u32[]{:S(2)}) collective-permute-start(bf16[19,64,256]{2,1,0:T(8,128)(2,1)S(1)} %pad_maximum_fusion.4), channel_id=1, source_target_pairs={{0,8},{4,12},{8,0},{12,4},{1,9},{5,13},{9,1},{13,5},{2,10},{6,14},... | collective-permute-start | bytes 1867784 | tf_op jit(solution)/shard_map/ppermute | solution.py:798
  169.1 6.1 %collective-permute-start.28 = (bf16[18,16,256]{2,1,0:T(8,128)(2,1)S(1)}, bf16[18,16,256]{2,1,0:T(8,128)(2,1)S(1)}, u32[]{:S(2)}, u32[]{:S(2)}) collective-permute-start(bf16[18,16,256]{2,1,0:T(8,128)(2,1)S(1)} %pad_maximum_fusion.11), channel_id=1, source_target_pairs={{0,1},{1,0},{2,3},{3,2},{4,5},{5,4},{6,7},{7,6},{8,9},{9,8},{10,11... | collective-permute-start | bytes 442376 | tf_op jit(solution)/shard_map/ppermute | solution.py:798
  172.1 11.9 %collective-permute-start.31 = (bf16[19,64,256]{2,1,0:T(8,128)(2,1)S(1)}, bf16[19,64,256]{2,1,0:T(8,128)(2,1)S(1)}, u32[]{:S(2)}, u32[]{:S(2)}) collective-permute-start(bf16[19,64,256]{2,1,0:T(8,128)(2,1)S(1)} %pad_maximum_fusion.3), channel_id=1, source_target_pairs={{0,4},{4,0},{8,12},{12,8},{1,5},{5,1},{9,13},{13,9},{2,6},{6,2},{1... | collective-permute-start | bytes 1867784 | tf_op jit(solution)/shard_map/ppermute | solution.py:798
  175.3 5.2 %collective-permute-start.29 = (bf16[9,32,256]{2,1,0:T(8,128)(2,1)S(1)}, bf16[9,32,256]{2,1,0:T(8,128)(2,1)S(1)}, u32[]{:S(2)}, u32[]{:S(2)}) collective-permute-start(bf16[9,32,256]{2,1,0:T(8,128)(2,1)S(1)} %get-tuple-element.226), channel_id=1, source_target_pairs={{0,8},{4,12},{8,0},{12,4},{1,9},{5,13},{9,1},{13,5},{2,10},{6,14},... | collective-permute-start | bytes 442376 | tf_op jit(solution)/shard_map/ppermute | solution.py:798
  176.2 7.9 %collective-permute-start.30 = (bf16[9,32,256]{2,1,0:T(8,128)(2,1)S(1)}, bf16[9,32,256]{2,1,0:T(8,128)(2,1)S(1)}, u32[]{:S(2)}, u32[]{:S(2)}) collective-permute-start(bf16[9,32,256]{2,1,0:T(8,128)(2,1)S(1)} %get-tuple-element.225), channel_id=1, source_target_pairs={{0,4},{4,0},{8,12},{12,8},{1,5},{5,1},{9,13},{13,9},{2,6},{6,2},{1... | collective-permute-start | bytes 442376 | tf_op jit(solution)/shard_map/ppermute | solution.py:798
  185.1 6.3 %collective-permute-start.35 = (bf16[19,256,256]{2,1,0:T(8,128)(2,1)S(1)}, bf16[19,256,256]{2,1,0:T(8,128)(2,1)}, u32[]{:S(2)}, u32[]{:S(2)}) collective-permute-start(bf16[19,256,256]{2,1,0:T(8,128)(2,1)S(1)} %pad_maximum_fusion.half_ref), channel_id=1, source_target_pairs={{0,16},{16,0},{1,17},{17,1},{2,18},{18,2},{3,19},{19,3},{4,20},{20... | collective-permute-start | bytes 7471112 | tf_op jit(solution)/shard_map/ppermute | solution.py:798
  185.3 9.6 %collective-permute-start.34 = (bf16[9,64,256]{2,1,0:T(8,128)(2,1)S(1)}, bf16[9,64,256]{2,1,0:T(8,128)(2,1)}, u32[]{:S(2)}, u32[]{:S(2)}) collective-permute-start(bf16[9,64,256]{2,1,0:T(8,128)(2,1)S(1)} %pad_maximum_fusion.9), channel_id=1, source_target_pairs={{0,8},{4,12},{8,0},{12,4},{1,9},{5,13},{9,1},{13,5},{2,10},{6,14},... | collective-permute-start | bytes 884744 | tf_op jit(solution)/shard_map/ppermute | solution.py:798
  186.6 9.7 %collective-permute-start.33 = (bf16[9,64,256]{2,1,0:T(8,128)(2,1)}, bf16[9,64,256]{2,1,0:T(8,128)(2,1)}, u32[]{:S(2)}, u32[]{:S(2)}) collective-permute-start(bf16[9,64,256]{2,1,0:T(8,128)(2,1)} %pad_maximum_fusion.8), channel_id=1, source_target_pairs={{0,4},{4,0},{8,12},{12,8},{1,5},{5,1},{9,13},{13,9},{2,6},{6,2},{1... | collective-permute-start | bytes 884744 | tf_op jit(solution)/shard_map/ppermute | solution.py:798
  198.6 2.9 %collective-permute-start.36 = (bf16[9,256,256]{2,1,0:T(8,128)(2,1)S(1)}, bf16[9,256,256]{2,1,0:T(8,128)(2,1)S(1)}, u32[]{:S(2)}, u32[]{:S(2)}) collective-permute-start(bf16[9,256,256]{2,1,0:T(8,128)(2,1)S(1)} %pad_maximum_fusion.1.half_ref), channel_id=1, source_target_pairs={{0,16},{16,0},{1,17},{17,1},{2,18},{18,2},{3,19},{19,3},{4,20},{20... | collective-permute-start | bytes 3538952 | tf_op jit(solution)/shard_map/ppermute | solution.py:798
  (15 other events, 103.4 us)

commit v10 on v9

--- a/solution.py
+++ b/solution.py
@@ -818,6 +818,33 @@
     return jnp.concatenate([jnp.where(bit, other, value), jnp.where(bit, value, other)], axis=dim)
 
 
+def gathered(pieces, spots, cost=0):
+    taps, h, m = pieces[0].shape
+    count = len(pieces)
+
+    def body(spots_ref, *refs):
+        out, sems = refs[count:]
+        copies = []
+        for q in range(count):
+            rows = pl.ds(pl.multiple_of(spots_ref[q] * h, h), h)
+            copies.append(pltpu.make_async_copy(refs[q], out.at[:, rows], sems.at[q]))
+        for copy in copies:
+            copy.start()
+        for copy in copies:
+            copy.wait()
+
+    anywhere = pl.BlockSpec(memory_space=pl.ANY)
+    return pl.pallas_call(
+        body,
+        out_shape=shape((taps, count * h, m), pieces[0].dtype),
+        in_specs=[pl.BlockSpec(memory_space=pltpu.SMEM)] + [anywhere] * count,
+        out_specs=anywhere,
+        scratch_shapes=[pltpu.SemaphoreType.DMA((count,))],
+        compiler_params=pltpu.CompilerParams(vmem_limit_bytes=16 * 1024 * 1024),
+        cost_estimate=pl.CostEstimate(flops=cost, bytes_accessed=0, transcendentals=0),
+    )(spots, *pieces)
+
+
 class Tree:
     def __init__(self, parts, bits, plane, rest, core):
         self.bits, self.place = bits, {step: k for k, step in enumerate([core, *plane, *rest])}
@@ -866,9 +893,14 @@
             self.value = joined(self.value, self.got[0], *self.rest[k])
             self.value_a, self.value_b = self.value[: self.taps], self.value[self.taps :]
         elif kind == N.plane_join:
-            self.value_a = joined(self.value_a, self.got[0], *self.a[k])
-            self.value_b = joined(self.value_b, self.got[1], *self.b[k])
-            self.value = jnp.concatenate([self.value_a, self.value_b], axis=1)
+            if k == 0 and cost:
+                low, high = (self.bits[self.place[step]] for step in (self.a[0], self.b[0]))
+                spots = jnp.stack([low, 1 - low, 2 + high, 3 - high])
+                self.value = gathered([self.value_a, self.got[0], self.value_b, self.got[1]], spots, cost)
+            else:
+                self.value_a = joined(self.value_a, self.got[0], *self.a[k])
+                self.value_b = joined(self.value_b, self.got[1], *self.b[k])
+                self.value = jnp.concatenate([self.value_a, self.value_b], axis=1)
 
     def split_rest(self, total, k):
         if k < len(self.rest):
@@ -1163,7 +1195,7 @@
     grad_second = widen(tree2.got[0], 1 - side, 9, per, True, widen(tree2.value, side, 9, per, True))
     tree1.got, grad_second = lax.optimization_barrier((tree1.got, grad_second))
     grad_w2, grad_wp = grad_second
-    tree1.finish()
+    tree1.finish(1)
     tree1.start()
     (grad_w1,) = widen(tree1.got[0], 1 - side, 3, 3, False, widen(tree1.value, side, 3, 3, False))
 

time: 205 us -> 203 us (level)
  other arithmetic: 7.78 us -> 5.1 us
    select_n x10 -> x8, other arithmetic: 2.91 us -> 0.76 us  [joined(): jnp.where(bit, other, value)]
  transfers between devices with their start and end apart: 41 -> 41, of which waited for: 26 -> 27; matrix products, arithmetic and copies ran while one was open for 1% -> 0% of each run, Pallas kernels for 21% -> 21%
where the time goes in v10:
time: 203 us; the launch traced here: 202 us
  Pallas kernels  69 us (34%)
  starting transfers between devices  65.8 us (32%)
  waiting for transfers between devices  58.3 us (29%)
  other arithmetic  5.1 us (3%)
  local copies, waits for them, and re-layouts  2.62 us (1%)
    pallas_call x11, Pallas kernels, call(): pl.pallas_call(run, out_shape=list(outs.values()), in_specs=[spec(n) for...  57.1 us
    ppermute x32, starting transfers between devices, partner(): return lax.ppermute(value, axis, [(i, i ^ step) for i in range(count)])  36.3 us
    ppermute x32, waiting for transfers between devices, partner(): return lax.ppermute(value, axis, [(i, i ^ step) for i in range(count)])  34.7 us
    all_to_all x4, waiting for transfers between devices, gather_sum(): return lax.all_to_all(spread, axes, 0, 0)  21.2 us
    all_to_all x4, starting transfers between devices, gather_sum(): return lax.all_to_all(spread, axes, 0, 0)  16.6 us
    ppermute x4, starting transfers between devices, shifted(): lax.ppermute(value, axis, [(source, source + steps) for source in range(f...  12.3 us
    pallas_call x4, Pallas kernels, widen(): pl.pallas_call(body, out_shape=[shape((taps * per, n, 2 * m))] + [shape((...  10.3 us
  transfers between devices with their start and end apart: 41, of which 27 were waited for; matrix products, arithmetic and copies ran while one was open for 0% of the time, Pallas kernels for 21%

profile of v10, /device:TPU:0, one launch (start us, length us, event | category | flops | bytes accessed | tf_op | source)
XLA Modules:
  0.0 202.4 jit_solution(6157227639747345367)
XLA Ops:
  5.1 2.0 collective-permute-start.1
  9.2 4.8 %collective-permute-start.2 = (bf16[2,17,1,256]{3,2,1,0:T(2,128)(2,1)S(1)}, bf16[2,17,1,256]{3,2,1,0:T(2,128)(2,1)S(1)}, u32[]{:S(2)}, u32[]{:S(2)}) collective-permute-start(bf16[2,17,1,256]{3,2,1,0:T(2,128)(2,1)S(1)} %pad_maximum_fusion.11), channel_id=1, source_target_pairs={{0,4},{4,8},{8,12},{1,5},{5,9},{9,13},{2,6},{6,10},{10,14},{3,7},{... | collective-permute-start | bytes 52232 | tf_op jit(solution)/shard_map/ppermute | solution.py:785
  14.1 1.6 collective-permute-done.2.refs_2_
  15.7 4.2 %collective-permute-start.3 = (bf16[480,256]{1,0:T(8,128)(2,1)S(1)}, bf16[480,256]{1,0:T(8,128)(2,1)S(1)}, u32[]{:S(2)}, u32[]{:S(2)}) collective-permute-start(bf16[480,256]{1,0:T(8,128)(2,1)S(1)} %get-tuple-element.115), channel_id=1, source_target_pairs={{0,4},{4,8},{8,12},{1,5},{5,9},{9,13},{2,6},{6,10},{10,14},{3,7},{... | collective-permute-start | bytes 737288 | tf_op jit(solution)/shard_map/ppermute | solution.py:785
  21.2 3.3 %shard_map.206 = f32[32,1,2176]{2,1,0:T(1,128)} custom-call(bf16[2,16,32,256]{3,2,1,0:T(8,128)(2,1)S(1)} %copy-done.1, bf16[2,1,32,256]{3,2,1,0:T(8,128)(2,1)S(1)} %collective-permute-done.1.refs_1_, bf16[2,17,1,256]{3,2,1,0:T(2,128)(2,1)S(1)} %collective-permute-done.2.refs_2_, bf16[2,8,16,128]{3,2,1,0:T(8,128)(2,1)S(1)} %broadcast_in_dim.2.refs_3_, ...), custom_call_target="tpu_custom_call" | custom-call | tf_op jit(solution)/shard_map/pallas_call | solution.py:113
  24.6 7.9 %all-to-all-start = ((f32[32,1,2176]{2,1,0:T(1,128)}), f32[32,1,2176]{2,1,0:T(1,128)S(1)}, u32[]{:S(2)}, u32[]{:S(2)}) async-start(f32[32,1,2176]{2,1,0:T(1,128)} %shard_map.206), calls=%async_computation | async-start | bytes 557056 | tf_op jit(solution)/shard_map/all_to_all | solution.py:789
  32.6 5.7 %shard_map.205 = (f32[624,512]{1,0:T(8,128)}, f32[624,512]{1,0:T(8,128)}, bf16[624,768]{1,0:T(8,128)(2,1)}, bf16[672,768]{1,0:T(8,128)(2,1)}, f32[624,128]{1,0:T...) custom-call(s32[2]{0:T(128)S(1)} %add_convert_fusion.2.refs_0_, bf16[2,16,32,256]{3,2,1,0:T(8,128)(2,1)} %refs_0_.1, ...), custom_call_target="tpu_custom_call" | custom-call | flops 20000000000 | tf_op jit(solution)/shard_map/pallas_call | solution.py:113
  38.3 5.5 %all-to-all-done.refs_1_ = f32[32,1,2176]{2,1,0:T(1,128)S(1)} async-done(((f32[32,1,2176]{2,1,0:T(1,128)}), f32[32,1,2176]{2,1,0:T(1,128)S(1)}, u32[]{:S(2)}, u32[]{:S(2)}) %all-to-all-start) | async-done | bytes 278560 | tf_op jit(solution)/shard_map/all_to_all | solution.py:789
  43.8 6.3 %shard_map.207 = (bf16[624,1536]{1,0:T(8,128)(2,1)}, f32[528,512]{1,0:T(8,128)}, f32[32,1,1024]{2,1,0:T(1,128)}, f32[8,512]{1,0:T(8,128)S(1)}) custom-call(f32[624,512]{1,0:T(8,128)} %get-tuple-element.117.refs_0_.refs_3_, f32[32,1,2176]{2,1,0:T(1,128)S(1)} %all-to-all-done.refs_1_, f32[1,512]{1,0:T(1,128)S(1)} %bitcast.36, f32[1,512]{1,0:T(1,128)S(1)} %bitcast.34, ...), custom_call_target="tpu_custom_call" | custom-call | tf_op jit(solution)/shard_map/pallas_call | solution.py:113
  50.1 2.6 %all-to-all-start.1 = ((f32[32,1,1024]{2,1,0:T(1,128)}), f32[32,1,1024]{2,1,0:T(1,128)S(1)}, u32[]{:S(2)}, u32[]{:S(2)}) async-start(f32[32,1,1024]{2,1,0:T(1,128)} %get-tuple-element.124), calls=%async_computation.1 | async-start | bytes 262144 | tf_op jit(solution)/shard_map/all_to_all | solution.py:789
  52.9 7.7 %all-to-all-done.1.refs_4_ = f32[32,1,1024]{2,1,0:T(1,128)S(1)} async-done(((f32[32,1,1024]{2,1,0:T(1,128)}), f32[32,1,1024]{2,1,0:T(1,128)S(1)}, u32[]{:S(2)}, u32[]{:S(2)}) %all-to-all-start.1) | async-done | bytes 131104 | tf_op jit(solution)/shard_map/all_to_all | solution.py:789
  60.7 5.5 %shard_map.208 = (bf16[2,8,16,512]{3,2,1,0:T(8,128)(2,1)}, f32[528,512]{1,0:T(8,128)}, f32[32,1,1536]{2,1,0:T(1,128)}, f32[8,512]{1,0:T(8,128)S(1)}, f32[3,384,256]{2,1,0:T(8,128)}, /*index=5*/f32[3,384,256]{2,1,0:T(8,128)}) custom-call(s32[5]{0:T(128)S(1)} %stack.44.refs_0_, f32[528,512]{1,0:T(8,128)} %get-tuple-element.121.refs_1_.refs_2_, ...), custom_call_target="tpu_custom_call" | custom-call | tf_op jit(solution)/shard_map/pallas_call | solution.py:113
  66.8 2.8 %all-to-all-start.2 = ((f32[32,1,1536]{2,1,0:T(1,128)}), f32[32,1,1536]{2,1,0:T(1,128)S(1)}, u32[]{:S(2)}, u32[]{:S(2)}) async-start(f32[32,1,1536]{2,1,0:T(1,128)} %get-tuple-element.135), calls=%async_computation.2 | async-start | bytes 393216 | tf_op jit(solution)/shard_map/all_to_all | solution.py:789
  70.8 8.0 %all-to-all-done.2.refs_7_.refs_8_ = f32[32,1,1536]{2,1,0:T(1,128)S(1)} async-done(((f32[32,1,1536]{2,1,0:T(1,128)}), f32[32,1,1536]{2,1,0:T(1,128)S(1)}, u32[]{:S(2)}, u32[]{:S(2)}) %all-to-all-start.2) | async-done | bytes 196640 | tf_op jit(solution)/shard_map/all_to_all | solution.py:789
  78.8 8.4 %shard_map.209 = (bf16[19,64,256]{2,1,0:T(8,128)(2,1)S(1)}, f32[19,64,256]{2,1,0:T(8,128)}, bf16[19,64,256]{2,1,0:T(8,128)(2,1)}, f32[19,64,256]{2,1,0:T(8,128)}) custom-call(s32[5]{0:T(128)S(1)} %stack.44.refs_0_, f32[3,384,256]{2,1,0:T(8,128)} %get-tuple-element.130.refs_1_, f32[3,384,256]{2,1,0:T(8,128)} %copy-done.18, ...), custom_call_target="tpu_custom_call" | custom-call | tf_op jit(solution)/shard_map/pallas_call | solution.py:113
  88.3 8.6 %shard_map.211 = (f32[432,512]{1,0:T(8,128)}, f32[432,512]{1,0:T(8,128)}, f32[32,1,1024]{2,1,0:T(1,128)}, f32[2,384,256]{2,1,0:T(8,128)}, f32[2,384,256]{2,1,0:T...) custom-call(s32[5]{0:T(128)S(1)} %stack.44.refs_0_, ...), custom_call_target="tpu_custom_call" | custom-call | tf_op jit(solution)/shard_map/pallas_call | solution.py:113
  97.5 3.4 %all-to-all-start.3 = ((f32[32,1,1024]{2,1,0:T(1,128)}), f32[32,1,1024]{2,1,0:T(1,128)S(1)}, u32[]{:S(2)}, u32[]{:S(2)}) async-start(f32[32,1,1024]{2,1,0:T(1,128)} %get-tuple-element.156), calls=%async_computation.3 | async-start | bytes 262144 | tf_op jit(solution)/shard_map/all_to_all | solution.py:789
  100.9 1.9 collective-permute-done.10.refs_4_
  103.7 3.8 %shard_map.210 = (bf16[19,32,256]{2,1,0:T(8,128)(2,1)}, f32[19,32,256]{2,1,0:T(8,128)}, bf16[19,32,256]{2,1,0:T(8,128)(2,1)}, f32[19,32,256]{2,1,0:T(8,128)}) custom-call(s32[5]{0:T(128)} %copy-done.10, f32[19,64,256]{2,1,0:T(8,128)} %get-tuple-element.142.refs_1_, bf16[19,64,256]{2,1,0:T(8,128)(2,1)} %collective-permute-done.9.refs_2_, ...), custom_call_target="tpu_custom_call" | custom-call | flops 20000000000 | tf_op jit(solution)/shard_map/pallas_call | solution.py:113
  109.4 6.9 %shard_map.212 = (bf16[9,64,256]{2,1,0:T(8,128)(2,1)S(1)}, f32[9,64,256]{2,1,0:T(8,128)S(1)}, bf16[9,64,256]{2,1,0:T(8,128)(2,1)S(1)}, f32[9,64,256]{2,1,0:T(8,1...) custom-call(s32[5]{0:T(128)S(1)} %copy-done.11, f32[2,384,256]{2,1,0:T(8,128)} %get-tuple-element.153.refs_1_, ...), custom_call_target="tpu_custom_call" | custom-call | flops 20000000000 | tf_op jit(solution)/shard_map/pallas_call | solution.py:113
  116.7 1.5 convert_add_fusion.1
  118.4 1.5 collective-permute-start.15
  120.0 1.5 collective-permute-start.16
  122.0 6.4 %shard_map.213 = bf16[2,16,32,256]{3,2,1,0:T(8,128)(2,1)} custom-call(f32[432,512]{1,0:T(8,128)S(1)} %copy-done.14, f32[432,512]{1,0:T(8,128)} %get-tuple-element.167.refs_1_, bf16[384,512]{1,0:T(8,128)(2,1)S(1)} %get-tuple-element.168.refs_2_, bf16[3,768,512]{2,1,0:T(8,128)(2,1)} %bitcast.50, bf16[256,512]{1,0:T(8,128)(2,1)S(1)} %copy-done.5, ...), custom_call_target="tpu_custom_call" | custom-call | flops 10000000000 | tf_op jit(solution)/shard_map/pallas_call | solution.py:113
  128.9 1.3 collective-permute-start.20
  130.4 1.8 collective-permute-start.18
  134.1 3.5 %collective-permute-done.19 = bf16[9,32,256]{2,1,0:T(8,128)(2,1)S(1)} collective-permute-done((bf16[9,32,256]{2,1,0:T(8,128)(2,1)S(1)}, bf16[9,32,256]{2,1,0:T(8,128)(2,1)S(1)}, u32[]{:S(2)}, u32[]{:S(2)}) %collective-permute-start.19) | collective-permute-done | bytes 147488 | tf_op jit(solution)/shard_map/ppermute | solution.py:798
  139.1 4.1 %collective-permute-start.22 = (bf16[18,16,256]{2,1,0:T(8,128)(2,1)S(1)}, bf16[18,16,256]{2,1,0:T(8,128)(2,1)S(1)}, u32[]{:S(2)}, u32[]{:S(2)}) collective-permute-start(bf16[18,16,256]{2,1,0:T(8,128)(2,1)S(1)} %select_convert_fusion.2), channel_id=1, source_target_pairs={{0,1},{1,0},{2,3},{3,2},{4,5},{5,4},{6,7},{7,6},{8,9},{9,8},{10,11... | collective-permute-start | bytes 442376 | tf_op jit(solution)/shard_map/ppermute | solution.py:798
  143.1 5.5 %collective-permute-done.22 = bf16[18,16,256]{2,1,0:T(8,128)(2,1)S(1)} collective-permute-done((bf16[18,16,256]{2,1,0:T(8,128)(2,1)S(1)}, bf16[18,16,256]{2,1,0:T(8,128)(2,1)S(1)}, u32[]{:S(2)}, u32[]{:S(2)}) %collective-permute-start.22) | collective-permute-done | bytes 147488 | tf_op jit(solution)/shard_map/ppermute | solution.py:798
  148.7 1.4 collective-permute-start.23
  150.1 2.5 %collective-permute-start.24 = (bf16[18,8,256]{2,1,0:T(8,128)(2,1)S(1)}, bf16[18,8,256]{2,1,0:T(8,128)(2,1)S(1)}, u32[]{:S(2)}, u32[]{:S(2)}) collective-permute-start(bf16[18,8,256]{2,1,0:T(8,128)(2,1)S(1)} %select_convert_fusion.5), channel_id=1, source_target_pairs={{0,2},{1,3},{2,0},{3,1},{4,6},{5,7},{6,4},{7,5},{8,10},{9,11},{10,... | collective-permute-start | bytes 221192 | tf_op jit(solution)/shard_map/ppermute | solution.py:798
  152.6 3.4 %collective-permute-done.24 = bf16[18,8,256]{2,1,0:T(8,128)(2,1)S(1)} collective-permute-done((bf16[18,8,256]{2,1,0:T(8,128)(2,1)S(1)}, bf16[18,8,256]{2,1,0:T(8,128)(2,1)S(1)}, u32[]{:S(2)}, u32[]{:S(2)}) %collective-permute-start.24) | collective-permute-done | bytes 73760 | tf_op jit(solution)/shard_map/ppermute | solution.py:798
  158.5 1.5 collective-permute-start.26
  160.1 2.3 %collective-permute-start.27 = (bf16[18,8,256]{2,1,0:T(8,128)(2,1)S(1)}, bf16[18,8,256]{2,1,0:T(8,128)(2,1)S(1)}, u32[]{:S(2)}, u32[]{:S(2)}) collective-permute-start(bf16[18,8,256]{2,1,0:T(8,128)(2,1)S(1)} %add_convert_fusion.1), channel_id=1, source_target_pairs={{0,2},{1,3},{2,0},{3,1},{4,6},{5,7},{6,4},{7,5},{8,10},{9,11},{10,... | collective-permute-start | bytes 221192 | tf_op jit(solution)/shard_map/ppermute | solution.py:798
  162.4 3.0 %collective-permute-done.27 = bf16[18,8,256]{2,1,0:T(8,128)(2,1)S(1)} collective-permute-done((bf16[18,8,256]{2,1,0:T(8,128)(2,1)S(1)}, bf16[18,8,256]{2,1,0:T(8,128)(2,1)S(1)}, u32[]{:S(2)}, u32[]{:S(2)}) %collective-permute-start.27) | collective-permute-done | bytes 73760 | tf_op jit(solution)/shard_map/ppermute | solution.py:798
  165.4 2.4 %collective-permute-done.25 = bf16[19,32,256]{2,1,0:T(8,128)(2,1)S(1)} collective-permute-done((bf16[19,32,256]{2,1,0:T(8,128)(2,1)S(1)}, bf16[19,32,256]{2,1,0:T(8,128)(2,1)S(1)}, u32[]{:S(2)}, u32[]{:S(2)}) %collective-permute-start.25) | collective-permute-done | bytes 311328 | tf_op jit(solution)/shard_map/ppermute | solution.py:798
  169.3 3.0 %collective-permute-start.28 = (bf16[18,16,256]{2,1,0:T(8,128)(2,1)S(1)}, bf16[18,16,256]{2,1,0:T(8,128)(2,1)S(1)}, u32[]{:S(2)}, u32[]{:S(2)}) collective-permute-start(bf16[18,16,256]{2,1,0:T(8,128)(2,1)S(1)} %pad_maximum_fusion.10), channel_id=1, source_target_pairs={{0,1},{1,0},{2,3},{3,2},{4,5},{5,4},{6,7},{7,6},{8,9},{9,8},{10,11... | collective-permute-start | bytes 442376 | tf_op jit(solution)/shard_map/ppermute | solution.py:798
  172.3 1.5 collective-permute-start.31
  173.8 1.6 collective-permute-done.28
  176.3 1.8 collective-permute-start.30
  178.1 2.6 %collective-permute-done.29 = bf16[9,32,256]{2,1,0:T(8,128)(2,1)S(1)} collective-permute-done((bf16[9,32,256]{2,1,0:T(8,128)(2,1)S(1)}, bf16[9,32,256]{2,1,0:T(8,128)(2,1)S(1)}, u32[]{:S(2)}, u32[]{:S(2)}) %collective-permute-start.29) | collective-permute-done | bytes 147488 | tf_op jit(solution)/shard_map/ppermute | solution.py:798
  180.7 3.5 %collective-permute-done.30 = bf16[9,32,256]{2,1,0:T(8,128)(2,1)S(1)} collective-permute-done((bf16[9,32,256]{2,1,0:T(8,128)(2,1)S(1)}, bf16[9,32,256]{2,1,0:T(8,128)(2,1)S(1)}, u32[]{:S(2)}, u32[]{:S(2)}) %collective-permute-start.30) | collective-permute-done | bytes 147488 | tf_op jit(solution)/shard_map/ppermute | solution.py:798
  186.1 2.1 %collective-permute-start.33 = (bf16[9,64,256]{2,1,0:T(8,128)(2,1)S(1)}, bf16[9,64,256]{2,1,0:T(8,128)(2,1)}, u32[]{:S(2)}, u32[]{:S(2)}) collective-permute-start(bf16[9,64,256]{2,1,0:T(8,128)(2,1)S(1)} %pad_maximum_fusion.7.refs_0_), channel_id=1, source_target_pairs={{0,4},{4,0},{8,12},{12,8},{1,5},{5,1},{9,13},{13,9},{2,6},{6,2},{1... | collective-permute-start | bytes 884744 | tf_op jit(solution)/shard_map/ppermute | solution.py:798
  188.2 2.8 %shard_map.214 = (f32[18,256,512]{2,1,0:T(8,128)}, f32[1,256,512]{2,1,0:T(8,128)}) custom-call(s32[1]{0:T(128)} %bitcast.side_ref, bf16[19,256,256]{2,1,0:T(8,128)(2,1)S(1)} %pad_maximum_fusion.half_ref), custom_call_target="tpu_custom_call" | custom-call | tf_op jit(solution)/shard_map/pallas_call | solution.py:730
  191.0 3.4 %shard_map.215 = (f32[18,256,512]{2,1,0:T(8,128)}, f32[1,256,512]{2,1,0:T(8,128)}) custom-call(s32[1]{0:T(128)} %bitcast.15.side_ref, bf16[19,256,256]{2,1,0:T(8,128)(2,1)} %collective-permute-done.35.half_ref, f32[18,256,512]{2,1,0:T(8,128)} %get-tuple-element.191.refs_0_, ...), custom_call_target="tpu_custom_call", output_to_operand_aliasing={{0}: (2, {}), {1}: (3, {})} | custom-call | tf_op jit(solution)/shard_map/pallas_call | solution.py:730
  195.6 1.6 shard_map.216.half_ref
  197.3 2.1 %shard_map.217.refs_0_ = f32[9,256,512]{2,1,0:T(8,128)} custom-call(s32[1]{0:T(128)} %bitcast.side_ref, bf16[9,256,256]{2,1,0:T(8,128)(2,1)S(1)} %shard_map.216.half_ref), custom_call_target="tpu_custom_call" | custom-call | tf_op jit(solution)/shard_map/pallas_call | solution.py:730
  200.1 2.1 %shard_map.218 = f32[9,256,512]{2,1,0:T(8,128)} custom-call(s32[1]{0:T(128)} %bitcast.15.side_ref, bf16[9,256,256]{2,1,0:T(8,128)(2,1)S(1)} %collective-permute-done.36.half_ref, f32[9,256,512]{2,1,0:T(8,128)} %shard_map.217.refs_0_), custom_call_target="tpu_custom_call", output_to_operand_aliasing={{}: (2, {})} | custom-call | tf_op jit(solution)/shard_map/pallas_call | solution.py:730
  (135 shorter events, 28.6 us)
Async XLA Ops:
  3.5 17.7 %copy-start.1 = (bf16[2,16,32,256]{3,2,1,0:T(8,128)(2,1)S(1)}, bf16[2,16,32,256]{3,2,1,0:T(8,128)(2,1)}, u32[]{:S(2)}) copy-start(bf16[2,16,32,256]{3,2,1,0:T(8,128)(2,1)} %refs_0_.1) | copy-start | bytes 1572868
  3.5 17.7 %copy-start.5 = (bf16[256,512]{1,0:T(8,128)(2,1)S(1)}, bf16[256,512]{1,0:T(8,128)(2,1)}, u32[]{:S(2)}) copy-start(bf16[256,512]{1,0:T(8,128)(2,1)} %refs_4_.1) | copy-start | bytes 786436
  4.5 3.3 %collective-permute-start = (bf16[672,256]{1,0:T(8,128)(2,1)S(1)}, bf16[672,256]{1,0:T(8,128)(2,1)S(1)}, u32[]{:S(2)}, u32[]{:S(2)}) collective-permute-start(bf16[672,256]{1,0:T(8,128)(2,1)S(1)} %shard_map.203), channel_id=1, source_target_pairs={{0,16},{16,0},{1,17},{17,1},{2,18},{18,2},{3,19},{19,3},{4,20},{20... | collective-permute-start | bytes 1032200 | tf_op jit(solution)/shard_map/ppermute | solution.py:959
  5.1 2.8 %collective-permute-start.1 = (bf16[2,1,32,256]{3,2,1,0:T(8,128)(2,1)S(1)}, bf16[2,1,32,256]{3,2,1,0:T(8,128)(2,1)S(1)}, u32[]{:S(2)}, u32[]{:S(2)}) collective-permute-start(bf16[2,1,32,256]{3,2,1,0:T(8,128)(2,1)S(1)} %slice.57), channel_id=1, source_target_pairs={{0,16},{1,17},{2,18},{3,19},{4,20},{5,21},{6,22},{7,23},{8,24},{9,... | collective-permute-start | bytes 98312 | tf_op jit(solution)/shard_map/ppermute | solution.py:785
  9.2 6.4 %collective-permute-start.2 = (bf16[2,17,1,256]{3,2,1,0:T(2,128)(2,1)S(1)}, bf16[2,17,1,256]{3,2,1,0:T(2,128)(2,1)S(1)}, u32[]{:S(2)}, u32[]{:S(2)}) collective-permute-start(bf16[2,17,1,256]{3,2,1,0:T(2,128)(2,1)S(1)} %pad_maximum_fusion.11), channel_id=1, source_target_pairs={{0,4},{4,8},{8,12},{1,5},{5,9},{9,13},{2,6},{6,10},{10,14},{3,7},{... | collective-permute-start | bytes 52232 | tf_op jit(solution)/shard_map/ppermute | solution.py:785
  15.7 16.8 %collective-permute-start.3 = (bf16[480,256]{1,0:T(8,128)(2,1)S(1)}, bf16[480,256]{1,0:T(8,128)(2,1)S(1)}, u32[]{:S(2)}, u32[]{:S(2)}) collective-permute-start(bf16[480,256]{1,0:T(8,128)(2,1)S(1)} %get-tuple-element.115), channel_id=1, source_target_pairs={{0,4},{4,8},{8,12},{1,5},{5,9},{9,13},{2,6},{6,10},{10,14},{3,7},{... | collective-permute-start | bytes 737288 | tf_op jit(solution)/shard_map/ppermute | solution.py:785
  19.9 12.7 %collective-permute-start.4 = (bf16[480,256]{1,0:T(8,128)(2,1)S(1)}, bf16[480,256]{1,0:T(8,128)(2,1)S(1)}, u32[]{:S(2)}, u32[]{:S(2)}) collective-permute-start(bf16[480,256]{1,0:T(8,128)(2,1)S(1)} %get-tuple-element.116), channel_id=1, source_target_pairs={{4,0},{8,4},{12,8},{5,1},{9,5},{13,9},{6,2},{10,6},{14,10},{7,3},{... | collective-permute-start | bytes 737288 | tf_op jit(solution)/shard_map/ppermute | solution.py:785
  24.6 19.2 %all-to-all-start = ((f32[32,1,2176]{2,1,0:T(1,128)}), f32[32,1,2176]{2,1,0:T(1,128)S(1)}, u32[]{:S(2)}, u32[]{:S(2)}) async-start(f32[32,1,2176]{2,1,0:T(1,128)} %shard_map.206), calls=%async_computation | async-start | bytes 557056 | tf_op jit(solution)/shard_map/all_to_all | solution.py:789
  43.7 16.9 %copy-start.6 = (f32[512]{0:T(512)S(1)}, f32[512]{0:T(512)}, u32[]{:S(2)}) copy-start(f32[512]{0:T(512)} %param.17) | copy-start | bytes 6148
  43.7 16.9 %copy-start.7 = (f32[512]{0:T(512)S(1)}, f32[512]{0:T(512)}, u32[]{:S(2)}) copy-start(f32[512]{0:T(512)} %param.20) | copy-start | bytes 6148
  43.7 16.9 %copy-start.12 = (f32[512]{0:T(512)S(1)}, f32[512]{0:T(512)}, u32[]{:S(2)}) copy-start(f32[512]{0:T(512)} %param.18) | copy-start | bytes 6148
  43.8 16.9 %copy-start.13 = (f32[512]{0:T(512)S(1)}, f32[512]{0:T(512)}, u32[]{:S(2)}) copy-start(f32[512]{0:T(512)} %param.21) | copy-start | bytes 6148
  50.1 10.6 %collective-permute-start.5 = (bf16[624,1536]{1,0:T(8,128)(2,1)}, bf16[624,1536]{1,0:T(8,128)(2,1)S(1)}, u32[]{:S(2)}, u32[]{:S(2)}) collective-permute-start(bf16[624,1536]{1,0:T(8,128)(2,1)} %get-tuple-element.125.refs_3_), channel_id=1, source_target_pairs={{0,16},{16,0},{1,17},{17,1},{2,18},{18,2},{3,19},{19,3},{4,20},{20... | collective-permute-start | bytes 5750792 | tf_op jit(solution)/shard_map/ppermute | solution.py:798
  50.1 10.5 %all-to-all-start.1 = ((f32[32,1,1024]{2,1,0:T(1,128)}), f32[32,1,1024]{2,1,0:T(1,128)S(1)}, u32[]{:S(2)}, u32[]{:S(2)}) async-start(f32[32,1,1024]{2,1,0:T(1,128)} %get-tuple-element.124), calls=%async_computation.1 | async-start | bytes 262144 | tf_op jit(solution)/shard_map/all_to_all | solution.py:789
  52.9 35.4 %copy-start.10 = (s32[5]{0:T(128)}, s32[5]{0:T(128)S(1)}, u32[]{:S(2)}) copy-start(s32[5]{0:T(128)S(1)} %stack.44.refs_0_) | copy-start | bytes 64
  66.2 4.0 %collective-permute-start.6 = (f32[3,384,256]{2,1,0:T(8,128)}, f32[3,384,256]{2,1,0:T(8,128)S(1)}, u32[]{:S(2)}, u32[]{:S(2)}) collective-permute-start(f32[3,384,256]{2,1,0:T(8,128)} %get-tuple-element.131), channel_id=1, source_target_pairs={{0,16},{16,0},{1,17},{17,1},{2,18},{18,2},{3,19},{19,3},{4,20},{20... | collective-permute-start | bytes 3538952 | tf_op jit(solution)/shard_map/ppermute | solution.py:798
  66.3 4.5 %collective-permute-start.7 = (bf16[624,768]{1,0:T(8,128)(2,1)}, bf16[624,768]{1,0:T(8,128)(2,1)}, u32[]{:S(2)}, u32[]{:S(2)}) collective-permute-start(bf16[624,768]{1,0:T(8,128)(2,1)} %get-tuple-element.134.refs_5_.refs_3_), channel_id=1, source_target_pairs={{0,16},{16,0},{1,17},{17,1},{2,18},{18,2},{3,19},{19,3},{4,20},{20... | collective-permute-start | bytes 2875400 | tf_op jit(solution)/shard_map/ppermute | solution.py:798
  66.8 12.0 %all-to-all-start.2 = ((f32[32,1,1536]{2,1,0:T(1,128)}), f32[32,1,1536]{2,1,0:T(1,128)S(1)}, u32[]{:S(2)}, u32[]{:S(2)}) async-start(f32[32,1,1536]{2,1,0:T(1,128)} %get-tuple-element.135), calls=%async_computation.2 | async-start | bytes 393216 | tf_op jit(solution)/shard_map/all_to_all | solution.py:789
  70.2 8.6 %collective-permute-start.8 = (f32[624,128]{1,0:T(8,128)S(1)}, f32[624,128]{1,0:T(8,128)S(1)}, u32[]{:S(2)}, u32[]{:S(2)}) collective-permute-start(f32[624,128]{1,0:T(8,128)S(1)} %get-tuple-element.137.refs_5_.refs_10_.refs_12_.refs_14_), channel_id=1, source_target_pairs={{0,16},{16,0},{1,17},{17,1},{2,18},{18,2},{3,19},{19,3},{4,20},{20... | collective-permute-start | bytes 958472 | tf_op jit(solution)/shard_map/ppermute | solution.py:798
  87.2 15.6 %collective-permute-start.10 = (bf16[19,64,256]{2,1,0:T(8,128)(2,1)}, bf16[19,64,256]{2,1,0:T(8,128)(2,1)S(1)}, u32[]{:S(2)}, u32[]{:S(2)}) collective-permute-start(bf16[19,64,256]{2,1,0:T(8,128)(2,1)} %get-tuple-element.145), channel_id=1, source_target_pairs={{0,8},{4,12},{8,0},{12,4},{1,9},{5,13},{9,1},{13,5},{2,10},{6,14},... | collective-permute-start | bytes 1867784 | tf_op jit(solution)/shard_map/ppermute | solution.py:798
  88.2 15.2 %collective-permute-start.9 = (bf16[19,64,256]{2,1,0:T(8,128)(2,1)S(1)}, bf16[19,64,256]{2,1,0:T(8,128)(2,1)}, u32[]{:S(2)}, u32[]{:S(2)}) collective-permute-start(bf16[19,64,256]{2,1,0:T(8,128)(2,1)S(1)} %get-tuple-element.143), channel_id=1, source_target_pairs={{0,4},{4,0},{8,12},{12,8},{1,5},{5,1},{9,13},{13,9},{2,6},{6,2},{1... | collective-permute-start | bytes 1867784 | tf_op jit(solution)/shard_map/ppermute | solution.py:798
  88.3 21.1 %collective-permute-start.14 = (bf16[672,768]{1,0:T(8,128)(2,1)}, bf16[672,768]{1,0:T(8,128)(2,1)}, u32[]{:S(2)}, u32[]{:S(2)}) collective-permute-start(bf16[672,768]{1,0:T(8,128)(2,1)} %get-tuple-element.155.refs_5_), channel_id=1, source_target_pairs={{0,16},{16,0},{1,17},{17,1},{2,18},{18,2},{3,19},{19,3},{4,20},{20... | collective-permute-start | bytes 3096584 | tf_op jit(solution)/shard_map/ppermute | solution.py:798
  96.9 12.5 %collective-permute-start.13 = (f32[2,384,256]{2,1,0:T(8,128)}, f32[2,384,256]{2,1,0:T(8,128)}, u32[]{:S(2)}, u32[]{:S(2)}) collective-permute-start(f32[2,384,256]{2,1,0:T(8,128)} %get-tuple-element.154), channel_id=1, source_target_pairs={{0,16},{16,0},{1,17},{17,1},{2,18},{18,2},{3,19},{19,3},{4,20},{20... | collective-permute-start | bytes 2359304 | tf_op jit(solution)/shard_map/ppermute | solution.py:798
  97.5 12.0 %all-to-all-start.3 = ((f32[32,1,1024]{2,1,0:T(1,128)}), f32[32,1,1024]{2,1,0:T(1,128)S(1)}, u32[]{:S(2)}, u32[]{:S(2)}) async-start(f32[32,1,1024]{2,1,0:T(1,128)} %get-tuple-element.156), calls=%async_computation.3 | async-start | bytes 262144 | tf_op jit(solution)/shard_map/all_to_all | solution.py:789
  107.5 8.8 %collective-permute-start.11 = (bf16[19,32,256]{2,1,0:T(8,128)(2,1)}, bf16[19,32,256]{2,1,0:T(8,128)(2,1)S(1)}, u32[]{:S(2)}, u32[]{:S(2)}) collective-permute-start(bf16[19,32,256]{2,1,0:T(8,128)(2,1)} %get-tuple-element.151), channel_id=1, source_target_pairs={{0,8},{4,12},{8,0},{12,4},{1,9},{5,13},{9,1},{13,5},{2,10},{6,14},... | collective-permute-start | bytes 933896 | tf_op jit(solution)/shard_map/ppermute | solution.py:798
  108.5 8.2 %collective-permute-start.12 = (bf16[19,32,256]{2,1,0:T(8,128)(2,1)}, bf16[19,32,256]{2,1,0:T(8,128)(2,1)}, u32[]{:S(2)}, u32[]{:S(2)}) collective-permute-start(bf16[19,32,256]{2,1,0:T(8,128)(2,1)} %get-tuple-element.152), channel_id=1, source_target_pairs={{0,4},{4,0},{8,12},{12,8},{1,5},{5,1},{9,13},{13,9},{2,6},{6,2},{1... | collective-permute-start | bytes 933896 | tf_op jit(solution)/shard_map/ppermute | solution.py:798
  118.4 10.4 %collective-permute-start.15 = (bf16[38,16,256]{2,1,0:T(8,128)(2,1)S(1)}, bf16[38,16,256]{2,1,0:T(8,128)(2,1)S(1)}, u32[]{:S(2)}, u32[]{:S(2)}) collective-permute-start(bf16[38,16,256]{2,1,0:T(8,128)(2,1)S(1)} %select_convert_fusion), channel_id=1, source_target_pairs={{0,1},{1,0},{2,3},{3,2},{4,5},{5,4},{6,7},{7,6},{8,9},{9,8},{10,11... | collective-permute-start | bytes 933896 | tf_op jit(solution)/shard_map/ppermute | solution.py:798
  120.0 8.4 %collective-permute-start.16 = (bf16[9,64,256]{2,1,0:T(8,128)(2,1)S(1)}, bf16[9,64,256]{2,1,0:T(8,128)(2,1)S(1)}, u32[]{:S(2)}, u32[]{:S(2)}) collective-permute-start(bf16[9,64,256]{2,1,0:T(8,128)(2,1)S(1)} %get-tuple-element.164), channel_id=1, source_target_pairs={{0,4},{4,0},{8,12},{12,8},{1,5},{5,1},{9,13},{13,9},{2,6},{6,2},{1... | collective-permute-start | bytes 884744 | tf_op jit(solution)/shard_map/ppermute | solution.py:798
  121.4 7.4 %collective-permute-start.17 = (bf16[9,64,256]{2,1,0:T(8,128)(2,1)S(1)}, bf16[9,64,256]{2,1,0:T(8,128)(2,1)S(1)}, u32[]{:S(2)}, u32[]{:S(2)}) collective-permute-start(bf16[9,64,256]{2,1,0:T(8,128)(2,1)S(1)} %get-tuple-element.165), channel_id=1, source_target_pairs={{0,8},{4,12},{8,0},{12,4},{1,9},{5,13},{9,1},{13,5},{2,10},{6,14},... | collective-permute-start | bytes 884744 | tf_op jit(solution)/shard_map/ppermute | solution.py:798
  128.9 5.2 %collective-permute-start.20 = (bf16[9,32,256]{2,1,0:T(8,128)(2,1)S(1)}, bf16[9,32,256]{2,1,0:T(8,128)(2,1)S(1)}, u32[]{:S(2)}, u32[]{:S(2)}) collective-permute-start(bf16[9,32,256]{2,1,0:T(8,128)(2,1)S(1)} %select_convert_fusion.3), channel_id=1, source_target_pairs={{0,4},{4,0},{8,12},{12,8},{1,5},{5,1},{9,13},{13,9},{2,6},{6,2},{1... | collective-permute-start | bytes 442376 | tf_op jit(solution)/shard_map/ppermute | solution.py:798
  130.4 7.4 %collective-permute-start.18 = (bf16[38,8,256]{2,1,0:T(8,128)(2,1)S(1)}, bf16[38,8,256]{2,1,0:T(8,128)(2,1)S(1)}, u32[]{:S(2)}, u32[]{:S(2)}) collective-permute-start(bf16[38,8,256]{2,1,0:T(8,128)(2,1)S(1)} %select_convert_fusion.1), channel_id=1, source_target_pairs={{0,2},{1,3},{2,0},{3,1},{4,6},{5,7},{6,4},{7,5},{8,10},{9,11},{10,... | collective-permute-start | bytes 466952 | tf_op jit(solution)/shard_map/ppermute | solution.py:798
  132.3 5.2 %collective-permute-start.19 = (bf16[9,32,256]{2,1,0:T(8,128)(2,1)S(1)}, bf16[9,32,256]{2,1,0:T(8,128)(2,1)S(1)}, u32[]{:S(2)}, u32[]{:S(2)}) collective-permute-start(bf16[9,32,256]{2,1,0:T(8,128)(2,1)S(1)} %select_convert_fusion.4), channel_id=1, source_target_pairs={{0,8},{4,12},{8,0},{12,4},{1,9},{5,13},{9,1},{13,5},{2,10},{6,14},... | collective-permute-start | bytes 442376 | tf_op jit(solution)/shard_map/ppermute | solution.py:798
  138.0 10.6 %collective-permute-start.21 = (bf16[38,8,256]{2,1,0:T(8,128)(2,1)S(1)}, bf16[38,8,256]{2,1,0:T(8,128)(2,1)S(1)}, u32[]{:S(2)}, u32[]{:S(2)}) collective-permute-start(bf16[38,8,256]{2,1,0:T(8,128)(2,1)S(1)} %add_convert_fusion), channel_id=1, source_target_pairs={{0,2},{1,3},{2,0},{3,1},{4,6},{5,7},{6,4},{7,5},{8,10},{9,11},{10,... | collective-permute-start | bytes 466952 | tf_op jit(solution)/shard_map/ppermute | solution.py:798
  139.1 9.6 %collective-permute-start.22 = (bf16[18,16,256]{2,1,0:T(8,128)(2,1)S(1)}, bf16[18,16,256]{2,1,0:T(8,128)(2,1)S(1)}, u32[]{:S(2)}, u32[]{:S(2)}) collective-permute-start(bf16[18,16,256]{2,1,0:T(8,128)(2,1)S(1)} %select_convert_fusion.2), channel_id=1, source_target_pairs={{0,1},{1,0},{2,3},{3,2},{4,5},{5,4},{6,7},{7,6},{8,9},{9,8},{10,11... | collective-permute-start | bytes 442376 | tf_op jit(solution)/shard_map/ppermute | solution.py:798
  148.7 8.5 %collective-permute-start.23 = (bf16[38,16,256]{2,1,0:T(8,128)(2,1)S(1)}, bf16[38,16,256]{2,1,0:T(8,128)(2,1)S(1)}, u32[]{:S(2)}, u32[]{:S(2)}) collective-permute-start(bf16[38,16,256]{2,1,0:T(8,128)(2,1)S(1)} %pad_maximum_fusion.5), channel_id=1, source_target_pairs={{0,1},{1,0},{2,3},{3,2},{4,5},{5,4},{6,7},{7,6},{8,9},{9,8},{10,11... | collective-permute-start | bytes 933896 | tf_op jit(solution)/shard_map/ppermute | solution.py:798
  150.1 5.9 %collective-permute-start.24 = (bf16[18,8,256]{2,1,0:T(8,128)(2,1)S(1)}, bf16[18,8,256]{2,1,0:T(8,128)(2,1)S(1)}, u32[]{:S(2)}, u32[]{:S(2)}) collective-permute-start(bf16[18,8,256]{2,1,0:T(8,128)(2,1)S(1)} %select_convert_fusion.5), channel_id=1, source_target_pairs={{0,2},{1,3},{2,0},{3,1},{4,6},{5,7},{6,4},{7,5},{8,10},{9,11},{10,... | collective-permute-start | bytes 221192 | tf_op jit(solution)/shard_map/ppermute | solution.py:798
  157.5 10.3 %collective-permute-start.25 = (bf16[19,32,256]{2,1,0:T(8,128)(2,1)S(1)}, bf16[19,32,256]{2,1,0:T(8,128)(2,1)S(1)}, u32[]{:S(2)}, u32[]{:S(2)}) collective-permute-start(bf16[19,32,256]{2,1,0:T(8,128)(2,1)S(1)} %get-tuple-element.212), channel_id=1, source_target_pairs={{0,8},{4,12},{8,0},{12,4},{1,9},{5,13},{9,1},{13,5},{2,10},{6,14},... | collective-permute-start | bytes 933896 | tf_op jit(solution)/shard_map/ppermute | solution.py:798
  158.5 10.1 %collective-permute-start.26 = (bf16[19,32,256]{2,1,0:T(8,128)(2,1)S(1)}, bf16[19,32,256]{2,1,0:T(8,128)(2,1)S(1)}, u32[]{:S(2)}, u32[]{:S(2)}) collective-permute-start(bf16[19,32,256]{2,1,0:T(8,128)(2,1)S(1)} %get-tuple-element.211), channel_id=1, source_target_pairs={{0,4},{4,0},{8,12},{12,8},{1,5},{5,1},{9,13},{13,9},{2,6},{6,2},{1... | collective-permute-start | bytes 933896 | tf_op jit(solution)/shard_map/ppermute | solution.py:798
  160.1 5.3 %collective-permute-start.27 = (bf16[18,8,256]{2,1,0:T(8,128)(2,1)S(1)}, bf16[18,8,256]{2,1,0:T(8,128)(2,1)S(1)}, u32[]{:S(2)}, u32[]{:S(2)}) collective-permute-start(bf16[18,8,256]{2,1,0:T(8,128)(2,1)S(1)} %add_convert_fusion.1), channel_id=1, source_target_pairs={{0,2},{1,3},{2,0},{3,1},{4,6},{5,7},{6,4},{7,5},{8,10},{9,11},{10,... | collective-permute-start | bytes 221192 | tf_op jit(solution)/shard_map/ppermute | solution.py:798
  168.7 15.4 %collective-permute-start.32 = (bf16[19,64,256]{2,1,0:T(8,128)(2,1)S(1)}, bf16[19,64,256]{2,1,0:T(8,128)(2,1)S(1)}, u32[]{:S(2)}, u32[]{:S(2)}) collective-permute-start(bf16[19,64,256]{2,1,0:T(8,128)(2,1)S(1)} %pad_maximum_fusion.3), channel_id=1, source_target_pairs={{0,8},{4,12},{8,0},{12,4},{1,9},{5,13},{9,1},{13,5},{2,10},{6,14},... | collective-permute-start | bytes 1867784 | tf_op jit(solution)/shard_map/ppermute | solution.py:798
  169.3 6.1 %collective-permute-start.28 = (bf16[18,16,256]{2,1,0:T(8,128)(2,1)S(1)}, bf16[18,16,256]{2,1,0:T(8,128)(2,1)S(1)}, u32[]{:S(2)}, u32[]{:S(2)}) collective-permute-start(bf16[18,16,256]{2,1,0:T(8,128)(2,1)S(1)} %pad_maximum_fusion.10), channel_id=1, source_target_pairs={{0,1},{1,0},{2,3},{3,2},{4,5},{5,4},{6,7},{7,6},{8,9},{9,8},{10,11... | collective-permute-start | bytes 442376 | tf_op jit(solution)/shard_map/ppermute | solution.py:798
  172.3 11.9 %collective-permute-start.31 = (bf16[19,64,256]{2,1,0:T(8,128)(2,1)S(1)}, bf16[19,64,256]{2,1,0:T(8,128)(2,1)S(1)}, u32[]{:S(2)}, u32[]{:S(2)}) collective-permute-start(bf16[19,64,256]{2,1,0:T(8,128)(2,1)S(1)} %pad_maximum_fusion.2), channel_id=1, source_target_pairs={{0,4},{4,0},{8,12},{12,8},{1,5},{5,1},{9,13},{13,9},{2,6},{6,2},{1... | collective-permute-start | bytes 1867784 | tf_op jit(solution)/shard_map/ppermute | solution.py:798
  175.5 5.2 %collective-permute-start.29 = (bf16[9,32,256]{2,1,0:T(8,128)(2,1)S(1)}, bf16[9,32,256]{2,1,0:T(8,128)(2,1)S(1)}, u32[]{:S(2)}, u32[]{:S(2)}) collective-permute-start(bf16[9,32,256]{2,1,0:T(8,128)(2,1)S(1)} %get-tuple-element.222), channel_id=1, source_target_pairs={{0,8},{4,12},{8,0},{12,4},{1,9},{5,13},{9,1},{13,5},{2,10},{6,14},... | collective-permute-start | bytes 442376 | tf_op jit(solution)/shard_map/ppermute | solution.py:798
  176.3 7.9 %collective-permute-start.30 = (bf16[9,32,256]{2,1,0:T(8,128)(2,1)S(1)}, bf16[9,32,256]{2,1,0:T(8,128)(2,1)S(1)}, u32[]{:S(2)}, u32[]{:S(2)}) collective-permute-start(bf16[9,32,256]{2,1,0:T(8,128)(2,1)S(1)} %get-tuple-element.221), channel_id=1, source_target_pairs={{0,4},{4,0},{8,12},{12,8},{1,5},{5,1},{9,13},{13,9},{2,6},{6,2},{1... | collective-permute-start | bytes 442376 | tf_op jit(solution)/shard_map/ppermute | solution.py:798
  185.3 5.8 %collective-permute-start.35 = (bf16[19,256,256]{2,1,0:T(8,128)(2,1)S(1)}, bf16[19,256,256]{2,1,0:T(8,128)(2,1)}, u32[]{:S(2)}, u32[]{:S(2)}) collective-permute-start(bf16[19,256,256]{2,1,0:T(8,128)(2,1)S(1)} %pad_maximum_fusion.half_ref), channel_id=1, source_target_pairs={{0,16},{16,0},{1,17},{17,1},{2,18},{18,2},{3,19},{19,3},{4,20},{20... | collective-permute-start | bytes 7471112 | tf_op jit(solution)/shard_map/ppermute | solution.py:798
  185.4 9.5 %collective-permute-start.34 = (bf16[9,64,256]{2,1,0:T(8,128)(2,1)S(1)}, bf16[9,64,256]{2,1,0:T(8,128)(2,1)S(1)}, u32[]{:S(2)}, u32[]{:S(2)}) collective-permute-start(bf16[9,64,256]{2,1,0:T(8,128)(2,1)S(1)} %pad_maximum_fusion.8.refs_2_), channel_id=1, source_target_pairs={{0,8},{4,12},{8,0},{12,4},{1,9},{5,13},{9,1},{13,5},{2,10},{6,14},... | collective-permute-start | bytes 884744 | tf_op jit(solution)/shard_map/ppermute | solution.py:798
  186.1 9.6 %collective-permute-start.33 = (bf16[9,64,256]{2,1,0:T(8,128)(2,1)S(1)}, bf16[9,64,256]{2,1,0:T(8,128)(2,1)}, u32[]{:S(2)}, u32[]{:S(2)}) collective-permute-start(bf16[9,64,256]{2,1,0:T(8,128)(2,1)S(1)} %pad_maximum_fusion.7.refs_0_), channel_id=1, source_target_pairs={{0,4},{4,0},{8,12},{12,8},{1,5},{5,1},{9,13},{13,9},{2,6},{6,2},{1... | collective-permute-start | bytes 884744 | tf_op jit(solution)/shard_map/ppermute | solution.py:798
  197.2 2.9 %collective-permute-start.36 = (bf16[9,256,256]{2,1,0:T(8,128)(2,1)S(1)}, bf16[9,256,256]{2,1,0:T(8,128)(2,1)S(1)}, u32[]{:S(2)}, u32[]{:S(2)}) collective-permute-start(bf16[9,256,256]{2,1,0:T(8,128)(2,1)S(1)} %shard_map.216.half_ref), channel_id=1, source_target_pairs={{0,16},{16,0},{1,17},{17,1},{2,18},{18,2},{3,19},{19,3},{4,20},{20... | collective-permute-start | bytes 3538952 | tf_op jit(solution)/shard_map/ppermute | solution.py:798
  (14 other events, 94.2 us)

commit v11 on v10

--- a/solution.py
+++ b/solution.py
@@ -298,12 +298,12 @@
     z += matmul(r.xo[L : L + M, :], r.w1[2])
     zp = matmul(r.xe[:, cin : 2 * cin], r.wp[...])
     zm, zpm = z * wide(mask, width), zp * wide(mask, width)
-    row = jnp.concatenate(
-        [column_sum(zm), column_sum(zm * z), column_sum(zpm), column_sum(zpm * zp), column_sum(mask)], axis=1
-    )
+    row = jnp.concatenate([column_sum(zm), column_sum(zm * z), column_sum(mask)], axis=1)
     r.spread[...] = jnp.broadcast_to(row[None], r.spread.shape)
     copies.start(N.spread)
-    copies.wait(N.spread)
+    r.psum[...] = jnp.concatenate([column_sum(zpm), column_sum(zpm * zp)], axis=1)
+    copies.start(N.psum)
+    copies.wait(N.spread, N.psum)
 
 
 def first_kernel(r, copies):
@@ -387,10 +387,9 @@
 def second_kernel(r, copies):
     width = r.gain.shape[1]
     t = jnp.sum(r.tot1[...], axis=0)
-    n = wide(t[:, 4 * width :], width)
+    n = wide(t[:, 2 * width :], width)
     center, inv = moments(t[:, :width], t[:, width : 2 * width], n)
-    proj = moments(t[:, 2 * width : 3 * width], t[:, 3 * width : 4 * width], n)
-    r.mom1[...] = jnp.concatenate([center, inv, n, *proj, jnp.zeros((3, width), f32)], axis=0)
+    r.mom1[...] = jnp.concatenate([center, inv, n, jnp.zeros((5, width), f32)], axis=0)
     scale = inv * r.gain[...]
     M, Q = r.pre1.shape[0], r.pre2.shape[0]
     L = (M - Q) // 2
@@ -414,7 +413,7 @@
         copies.start((N.pre2, k))
         zm = z * wide(r.ownp[L + 1 + m0 : L + 1 + m0 + m, :], width)
         sums = [sums[0] + column_sum(zm), sums[1] + column_sum(zm * z)]
-    row = jnp.concatenate(sums, axis=1)
+    row = jnp.concatenate([*sums, r.psum[...]], axis=1)
     r.spread[...] = jnp.broadcast_to(row[None], r.spread.shape)
     copies.start(N.spread)
     copies.wait(N.h3, N.pre2, N.spread)
@@ -440,8 +439,8 @@
     L = groups * S
     n = r.mom1[2:3, :]
     t = jnp.sum(r.tot2[...], axis=0)
-    c2, i2 = moments(t[:, :width], t[:, width:], n)
-    cp, ip = r.mom1[3:4, :], r.mom1[4:5, :]
+    parts = [t[:, k * width : (k + 1) * width] for k in range(4)]
+    (c2, i2), (cp, ip) = moments(parts[0], parts[1], n), moments(parts[2], parts[3], n)
     r.mom2[...] = jnp.concatenate([c2, i2, cp, ip, jnp.zeros((4, width), f32)], axis=0)
     sums = [jnp.zeros((1, width), f32)] * 3
     both_shift = r.shift2[...] + r.shiftp[...]
@@ -983,14 +982,14 @@
     stats = call(
         stats_kernel,
         dict(x=inputs, top=top1, lft=lft1, own=own, w1=w1, wp=w_proj),
-        dict(spread=all_devices(4 * width + 128)),
+        dict(spread=all_devices(2 * width + 128), psum=vec(2)),
         dict(
             raw=pltpu.VMEM((cin // 128, (rows_in + 1) * groups, cols_in + 8, 128), f32),
             xe=pltpu.VMEM((rows * groups * cols, 3 * cin), bf16),
             xo=pltpu.VMEM(((rows + 1) * groups * cols, 3 * cin), bf16),
         ),
         far_in=(N.w1,),
-        far_out=(N.spread,),
+        far_out=(N.spread, N.psum),
     )
     tot1 = gather_sum(stats[N.spread])
 
@@ -1023,8 +1022,8 @@
 
     second = call(
         second_kernel,
-        dict(pre1=first[N.pre1], tot1=tot1, gain=g1, shift=b1, maskp=maskp, ownp=ownp, w2=w2),
-        dict(h3=shape((MP, 3 * width), bf16), pre2=shape((MQ, width)), spread=all_devices(2 * width), mom1=shape((8, width))),
+        dict(pre1=first[N.pre1], tot1=tot1, gain=g1, shift=b1, maskp=maskp, ownp=ownp, w2=w2, psum=stats[N.psum]),
+        dict(h3=shape((MP, 3 * width), bf16), pre2=shape((MQ, width)), spread=all_devices(4 * width), mom1=shape((8, width))),
         dict(hid=pltpu.VMEM((MP + 8, width), f32)),
         far_in=(N.pre1, N.w2),
         far_out=(N.h3, N.pre2, N.spread),

time: 203 us -> 204 us (level)
  no operation moved by 1% of the time
where the time goes in v11:
time: 204 us; the launch traced here: 203 us
  Pallas kernels  68.9 us (34%)
  starting transfers between devices  67 us (33%)
  waiting for transfers between devices  58.1 us (28%)
  other arithmetic  5.1 us (2%)
  local copies, waits for them, and re-layouts  2.61 us (1%)
    pallas_call x11, Pallas kernels, call(): pl.pallas_call(run, out_shape=list(outs.values()), in_specs=[spec(n) for...  57.1 us
    ppermute x32, starting transfers between devices, partner(): return lax.ppermute(value, axis, [(i, i ^ step) for i in range(count)])  36.3 us
    ppermute x32, waiting for transfers between devices, partner(): return lax.ppermute(value, axis, [(i, i ^ step) for i in range(count)])  34.6 us
    all_to_all x4, waiting for transfers between devices, gather_sum(): return lax.all_to_all(spread, axes, 0, 0)  20.9 us
    all_to_all x4, starting transfers between devices, gather_sum(): return lax.all_to_all(spread, axes, 0, 0)  17.8 us
    ppermute x4, starting transfers between devices, shifted(): lax.ppermute(value, axis, [(source, source + steps) for source in range(f...  12.3 us
    pallas_call x4, Pallas kernels, widen(): pl.pallas_call(body, out_shape=[shape((taps * per, n, 2 * m))] + [shape((...  10.3 us
  transfers between devices with their start and end apart: 41, of which 27 were waited for; matrix products, arithmetic and copies ran while one was open for 0% of the time, Pallas kernels for 21%

profile of v11, /device:TPU:0, one launch (start us, length us, event | category | flops | bytes accessed | tf_op | source)
XLA Modules:
  0.0 203.3 jit_solution(1178831475380916904)
XLA Ops:
  5.1 2.0 collective-permute-start.1
  9.2 4.8 %collective-permute-start.2 = (bf16[2,17,1,256]{3,2,1,0:T(2,128)(2,1)S(1)}, bf16[2,17,1,256]{3,2,1,0:T(2,128)(2,1)S(1)}, u32[]{:S(2)}, u32[]{:S(2)}) collective-permute-start(bf16[2,17,1,256]{3,2,1,0:T(2,128)(2,1)S(1)} %pad_maximum_fusion.11), channel_id=1, source_target_pairs={{0,4},{4,8},{8,12},{1,5},{5,9},{9,13},{2,6},{6,10},{10,14},{3,7},{... | collective-permute-start | bytes 52232 | tf_op jit(solution)/shard_map/ppermute | solution.py:784
  14.1 1.6 collective-permute-done.2.refs_2_
  15.7 4.2 %collective-permute-start.3 = (bf16[480,256]{1,0:T(8,128)(2,1)S(1)}, bf16[480,256]{1,0:T(8,128)(2,1)S(1)}, u32[]{:S(2)}, u32[]{:S(2)}) collective-permute-start(bf16[480,256]{1,0:T(8,128)(2,1)S(1)} %get-tuple-element.117), channel_id=1, source_target_pairs={{0,4},{4,8},{8,12},{1,5},{5,9},{9,13},{2,6},{6,10},{10,14},{3,7},{... | collective-permute-start | bytes 737288 | tf_op jit(solution)/shard_map/ppermute | solution.py:784
  21.2 3.2 %shard_map.206 = (f32[32,1,1152]{2,1,0:T(1,128)}, f32[1,1024]{1,0:T(1,128)S(1)}) custom-call(bf16[2,16,32,256]{3,2,1,0:T(8,128)(2,1)S(1)} %copy-done.1, bf16[2,1,32,256]{3,2,1,0:T(8,128)(2,1)S(1)} %collective-permute-done.1.refs_1_, bf16[2,17,1,256]{3,2,1,0:T(2,128)(2,1)S(1)} %collective-permute-done.2.refs_2_, ...), custom_call_target="tpu_custom_call" | custom-call | tf_op jit(solution)/shard_map/pallas_call | solution.py:113
  24.5 7.9 %all-to-all-start = ((f32[32,1,1152]{2,1,0:T(1,128)}), f32[32,1,1152]{2,1,0:T(1,128)S(1)}, u32[]{:S(2)}, u32[]{:S(2)}) async-start(f32[32,1,1152]{2,1,0:T(1,128)} %get-tuple-element.121), calls=%async_computation | async-start | bytes 294912 | tf_op jit(solution)/shard_map/all_to_all | solution.py:788
  32.6 5.7 %shard_map.205 = (f32[624,512]{1,0:T(8,128)}, f32[624,512]{1,0:T(8,128)}, bf16[624,768]{1,0:T(8,128)(2,1)}, bf16[672,768]{1,0:T(8,128)(2,1)}, f32[624,128]{1,0:T...) custom-call(s32[2]{0:T(128)S(1)} %add_convert_fusion.2.refs_0_, bf16[2,16,32,256]{3,2,1,0:T(8,128)(2,1)} %refs_0_.1, ...), custom_call_target="tpu_custom_call" | custom-call | flops 20000000000 | tf_op jit(solution)/shard_map/pallas_call | solution.py:113
  38.3 2.1 %all-to-all-done.refs_1_ = f32[32,1,1152]{2,1,0:T(1,128)S(1)} async-done(((f32[32,1,1152]{2,1,0:T(1,128)}), f32[32,1,1152]{2,1,0:T(1,128)S(1)}, u32[]{:S(2)}, u32[]{:S(2)}) %all-to-all-start) | async-done | bytes 147488 | tf_op jit(solution)/shard_map/all_to_all | solution.py:788
  40.4 6.3 %shard_map.207 = (bf16[624,1536]{1,0:T(8,128)(2,1)}, f32[528,512]{1,0:T(8,128)}, f32[32,1,2048]{2,1,0:T(1,128)}, f32[8,512]{1,0:T(8,128)S(1)}) custom-call(f32[624,512]{1,0:T(8,128)} %get-tuple-element.119.refs_0_.refs_3_, f32[32,1,1152]{2,1,0:T(1,128)S(1)} %all-to-all-done.refs_1_, f32[1,512]{1,0:T(1,128)S(1)} %bitcast.36, f32[1,512]{1,0:T(1,128)S(1)} %bitcast.34, ...), custom_call_target="tpu_custom_call" | custom-call | tf_op jit(solution)/shard_map/pallas_call | solution.py:113
  46.8 3.7 %all-to-all-start.1 = ((f32[32,1,2048]{2,1,0:T(1,128)}), f32[32,1,2048]{2,1,0:T(1,128)S(1)}, u32[]{:S(2)}, u32[]{:S(2)}) async-start(f32[32,1,2048]{2,1,0:T(1,128)} %get-tuple-element.128), calls=%async_computation.1 | async-start | bytes 524288 | tf_op jit(solution)/shard_map/all_to_all | solution.py:788
  50.8 10.8 %all-to-all-done.1.refs_4_ = f32[32,1,2048]{2,1,0:T(1,128)S(1)} async-done(((f32[32,1,2048]{2,1,0:T(1,128)}), f32[32,1,2048]{2,1,0:T(1,128)S(1)}, u32[]{:S(2)}, u32[]{:S(2)}) %all-to-all-start.1) | async-done | bytes 262176 | tf_op jit(solution)/shard_map/all_to_all | solution.py:788
  61.6 5.5 %shard_map.208 = (bf16[2,8,16,512]{3,2,1,0:T(8,128)(2,1)}, f32[528,512]{1,0:T(8,128)}, f32[32,1,1536]{2,1,0:T(1,128)}, f32[8,512]{1,0:T(8,128)S(1)}, f32[3,384,256]{2,1,0:T(8,128)}, /*index=5*/f32[3,384,256]{2,1,0:T(8,128)}) custom-call(s32[5]{0:T(128)S(1)} %stack.44.refs_0_, f32[528,512]{1,0:T(8,128)} %get-tuple-element.125.refs_1_.refs_2_, ...), custom_call_target="tpu_custom_call" | custom-call | tf_op jit(solution)/shard_map/pallas_call | solution.py:113
  67.7 2.8 %all-to-all-start.2 = ((f32[32,1,1536]{2,1,0:T(1,128)}), f32[32,1,1536]{2,1,0:T(1,128)S(1)}, u32[]{:S(2)}, u32[]{:S(2)}) async-start(f32[32,1,1536]{2,1,0:T(1,128)} %get-tuple-element.139), calls=%async_computation.2 | async-start | bytes 393216 | tf_op jit(solution)/shard_map/all_to_all | solution.py:788
  71.7 8.0 %all-to-all-done.2.refs_7_.refs_8_ = f32[32,1,1536]{2,1,0:T(1,128)S(1)} async-done(((f32[32,1,1536]{2,1,0:T(1,128)}), f32[32,1,1536]{2,1,0:T(1,128)S(1)}, u32[]{:S(2)}, u32[]{:S(2)}) %all-to-all-start.2) | async-done | bytes 196640 | tf_op jit(solution)/shard_map/all_to_all | solution.py:788
  79.7 8.4 %shard_map.209 = (bf16[19,64,256]{2,1,0:T(8,128)(2,1)S(1)}, f32[19,64,256]{2,1,0:T(8,128)}, bf16[19,64,256]{2,1,0:T(8,128)(2,1)}, f32[19,64,256]{2,1,0:T(8,128)}) custom-call(s32[5]{0:T(128)S(1)} %stack.44.refs_0_, f32[3,384,256]{2,1,0:T(8,128)} %get-tuple-element.134.refs_1_, f32[3,384,256]{2,1,0:T(8,128)} %copy-done.18, ...), custom_call_target="tpu_custom_call" | custom-call | tf_op jit(solution)/shard_map/pallas_call | solution.py:113
  89.2 8.6 %shard_map.211 = (f32[432,512]{1,0:T(8,128)}, f32[432,512]{1,0:T(8,128)}, f32[32,1,1024]{2,1,0:T(1,128)}, f32[2,384,256]{2,1,0:T(8,128)}, f32[2,384,256]{2,1,0:T...) custom-call(s32[5]{0:T(128)S(1)} %stack.44.refs_0_, ...), custom_call_target="tpu_custom_call" | custom-call | tf_op jit(solution)/shard_map/pallas_call | solution.py:113
  98.4 3.4 %all-to-all-start.3 = ((f32[32,1,1024]{2,1,0:T(1,128)}), f32[32,1,1024]{2,1,0:T(1,128)S(1)}, u32[]{:S(2)}, u32[]{:S(2)}) async-start(f32[32,1,1024]{2,1,0:T(1,128)} %get-tuple-element.160), calls=%async_computation.3 | async-start | bytes 262144 | tf_op jit(solution)/shard_map/all_to_all | solution.py:788
  101.8 1.9 collective-permute-done.10.refs_4_
  104.6 3.8 %shard_map.210 = (bf16[19,32,256]{2,1,0:T(8,128)(2,1)}, f32[19,32,256]{2,1,0:T(8,128)}, bf16[19,32,256]{2,1,0:T(8,128)(2,1)}, f32[19,32,256]{2,1,0:T(8,128)}) custom-call(s32[5]{0:T(128)} %copy-done.10, f32[19,64,256]{2,1,0:T(8,128)} %get-tuple-element.146.refs_1_, bf16[19,64,256]{2,1,0:T(8,128)(2,1)} %collective-permute-done.9.refs_2_, ...), custom_call_target="tpu_custom_call" | custom-call | flops 20000000000 | tf_op jit(solution)/shard_map/pallas_call | solution.py:113
  110.3 6.9 %shard_map.212 = (bf16[9,64,256]{2,1,0:T(8,128)(2,1)S(1)}, f32[9,64,256]{2,1,0:T(8,128)S(1)}, bf16[9,64,256]{2,1,0:T(8,128)(2,1)S(1)}, f32[9,64,256]{2,1,0:T(8,1...) custom-call(s32[5]{0:T(128)S(1)} %copy-done.11, f32[2,384,256]{2,1,0:T(8,128)} %get-tuple-element.157.refs_1_, ...), custom_call_target="tpu_custom_call" | custom-call | flops 20000000000 | tf_op jit(solution)/shard_map/pallas_call | solution.py:113
  117.6 1.5 convert_add_fusion.1
  119.3 1.5 collective-permute-start.15
  120.9 1.5 collective-permute-start.16
  122.9 6.4 %shard_map.213 = bf16[2,16,32,256]{3,2,1,0:T(8,128)(2,1)} custom-call(f32[432,512]{1,0:T(8,128)S(1)} %copy-done.14, f32[432,512]{1,0:T(8,128)} %get-tuple-element.171.refs_1_, bf16[384,512]{1,0:T(8,128)(2,1)S(1)} %get-tuple-element.172.refs_2_, bf16[3,768,512]{2,1,0:T(8,128)(2,1)} %bitcast.50, bf16[256,512]{1,0:T(8,128)(2,1)S(1)} %copy-done.5, ...), custom_call_target="tpu_custom_call" | custom-call | flops 10000000000 | tf_op jit(solution)/shard_map/pallas_call | solution.py:113
  129.8 1.3 collective-permute-start.20
  131.3 1.8 collective-permute-start.18
  135.0 3.5 %collective-permute-done.19 = bf16[9,32,256]{2,1,0:T(8,128)(2,1)S(1)} collective-permute-done((bf16[9,32,256]{2,1,0:T(8,128)(2,1)S(1)}, bf16[9,32,256]{2,1,0:T(8,128)(2,1)S(1)}, u32[]{:S(2)}, u32[]{:S(2)}) %collective-permute-start.19) | collective-permute-done | bytes 147488 | tf_op jit(solution)/shard_map/ppermute | solution.py:797
  140.0 4.1 %collective-permute-start.22 = (bf16[18,16,256]{2,1,0:T(8,128)(2,1)S(1)}, bf16[18,16,256]{2,1,0:T(8,128)(2,1)S(1)}, u32[]{:S(2)}, u32[]{:S(2)}) collective-permute-start(bf16[18,16,256]{2,1,0:T(8,128)(2,1)S(1)} %select_convert_fusion.2), channel_id=1, source_target_pairs={{0,1},{1,0},{2,3},{3,2},{4,5},{5,4},{6,7},{7,6},{8,9},{9,8},{10,11... | collective-permute-start | bytes 442376 | tf_op jit(solution)/shard_map/ppermute | solution.py:797
  144.0 5.5 %collective-permute-done.22 = bf16[18,16,256]{2,1,0:T(8,128)(2,1)S(1)} collective-permute-done((bf16[18,16,256]{2,1,0:T(8,128)(2,1)S(1)}, bf16[18,16,256]{2,1,0:T(8,128)(2,1)S(1)}, u32[]{:S(2)}, u32[]{:S(2)}) %collective-permute-start.22) | collective-permute-done | bytes 147488 | tf_op jit(solution)/shard_map/ppermute | solution.py:797
  149.6 1.4 collective-permute-start.23
  151.0 2.5 %collective-permute-start.24 = (bf16[18,8,256]{2,1,0:T(8,128)(2,1)S(1)}, bf16[18,8,256]{2,1,0:T(8,128)(2,1)S(1)}, u32[]{:S(2)}, u32[]{:S(2)}) collective-permute-start(bf16[18,8,256]{2,1,0:T(8,128)(2,1)S(1)} %select_convert_fusion.5), channel_id=1, source_target_pairs={{0,2},{1,3},{2,0},{3,1},{4,6},{5,7},{6,4},{7,5},{8,10},{9,11},{10,... | collective-permute-start | bytes 221192 | tf_op jit(solution)/shard_map/ppermute | solution.py:797
  153.5 3.4 %collective-permute-done.24 = bf16[18,8,256]{2,1,0:T(8,128)(2,1)S(1)} collective-permute-done((bf16[18,8,256]{2,1,0:T(8,128)(2,1)S(1)}, bf16[18,8,256]{2,1,0:T(8,128)(2,1)S(1)}, u32[]{:S(2)}, u32[]{:S(2)}) %collective-permute-start.24) | collective-permute-done | bytes 73760 | tf_op jit(solution)/shard_map/ppermute | solution.py:797
  159.4 1.6 collective-permute-start.26
  161.0 2.3 %collective-permute-start.27 = (bf16[18,8,256]{2,1,0:T(8,128)(2,1)S(1)}, bf16[18,8,256]{2,1,0:T(8,128)(2,1)S(1)}, u32[]{:S(2)}, u32[]{:S(2)}) collective-permute-start(bf16[18,8,256]{2,1,0:T(8,128)(2,1)S(1)} %add_convert_fusion.1), channel_id=1, source_target_pairs={{0,2},{1,3},{2,0},{3,1},{4,6},{5,7},{6,4},{7,5},{8,10},{9,11},{10,... | collective-permute-start | bytes 221192 | tf_op jit(solution)/shard_map/ppermute | solution.py:797
  163.3 3.0 %collective-permute-done.27 = bf16[18,8,256]{2,1,0:T(8,128)(2,1)S(1)} collective-permute-done((bf16[18,8,256]{2,1,0:T(8,128)(2,1)S(1)}, bf16[18,8,256]{2,1,0:T(8,128)(2,1)S(1)}, u32[]{:S(2)}, u32[]{:S(2)}) %collective-permute-start.27) | collective-permute-done | bytes 73760 | tf_op jit(solution)/shard_map/ppermute | solution.py:797
  166.3 2.4 %collective-permute-done.25 = bf16[19,32,256]{2,1,0:T(8,128)(2,1)S(1)} collective-permute-done((bf16[19,32,256]{2,1,0:T(8,128)(2,1)S(1)}, bf16[19,32,256]{2,1,0:T(8,128)(2,1)S(1)}, u32[]{:S(2)}, u32[]{:S(2)}) %collective-permute-start.25) | collective-permute-done | bytes 311328 | tf_op jit(solution)/shard_map/ppermute | solution.py:797
  170.2 3.0 %collective-permute-start.28 = (bf16[18,16,256]{2,1,0:T(8,128)(2,1)S(1)}, bf16[18,16,256]{2,1,0:T(8,128)(2,1)S(1)}, u32[]{:S(2)}, u32[]{:S(2)}) collective-permute-start(bf16[18,16,256]{2,1,0:T(8,128)(2,1)S(1)} %pad_maximum_fusion.10), channel_id=1, source_target_pairs={{0,1},{1,0},{2,3},{3,2},{4,5},{5,4},{6,7},{7,6},{8,9},{9,8},{10,11... | collective-permute-start | bytes 442376 | tf_op jit(solution)/shard_map/ppermute | solution.py:797
  173.2 1.5 collective-permute-start.31
  174.7 1.6 collective-permute-done.28
  177.2 1.8 collective-permute-start.30
  179.0 2.6 %collective-permute-done.29 = bf16[9,32,256]{2,1,0:T(8,128)(2,1)S(1)} collective-permute-done((bf16[9,32,256]{2,1,0:T(8,128)(2,1)S(1)}, bf16[9,32,256]{2,1,0:T(8,128)(2,1)S(1)}, u32[]{:S(2)}, u32[]{:S(2)}) %collective-permute-start.29) | collective-permute-done | bytes 147488 | tf_op jit(solution)/shard_map/ppermute | solution.py:797
  181.6 3.5 %collective-permute-done.30 = bf16[9,32,256]{2,1,0:T(8,128)(2,1)S(1)} collective-permute-done((bf16[9,32,256]{2,1,0:T(8,128)(2,1)S(1)}, bf16[9,32,256]{2,1,0:T(8,128)(2,1)S(1)}, u32[]{:S(2)}, u32[]{:S(2)}) %collective-permute-start.30) | collective-permute-done | bytes 147488 | tf_op jit(solution)/shard_map/ppermute | solution.py:797
  187.0 2.1 %collective-permute-start.33 = (bf16[9,64,256]{2,1,0:T(8,128)(2,1)S(1)}, bf16[9,64,256]{2,1,0:T(8,128)(2,1)}, u32[]{:S(2)}, u32[]{:S(2)}) collective-permute-start(bf16[9,64,256]{2,1,0:T(8,128)(2,1)S(1)} %pad_maximum_fusion.7.refs_0_), channel_id=1, source_target_pairs={{0,4},{4,0},{8,12},{12,8},{1,5},{5,1},{9,13},{13,9},{2,6},{6,2},{1... | collective-permute-start | bytes 884744 | tf_op jit(solution)/shard_map/ppermute | solution.py:797
  189.1 2.8 %shard_map.214 = (f32[18,256,512]{2,1,0:T(8,128)}, f32[1,256,512]{2,1,0:T(8,128)}) custom-call(s32[1]{0:T(128)} %bitcast.side_ref, bf16[19,256,256]{2,1,0:T(8,128)(2,1)S(1)} %pad_maximum_fusion.half_ref), custom_call_target="tpu_custom_call" | custom-call | tf_op jit(solution)/shard_map/pallas_call | solution.py:729
  191.9 3.4 %shard_map.215 = (f32[18,256,512]{2,1,0:T(8,128)}, f32[1,256,512]{2,1,0:T(8,128)}) custom-call(s32[1]{0:T(128)} %bitcast.15.side_ref, bf16[19,256,256]{2,1,0:T(8,128)(2,1)} %collective-permute-done.35.half_ref, f32[18,256,512]{2,1,0:T(8,128)} %get-tuple-element.195.refs_0_, ...), custom_call_target="tpu_custom_call", output_to_operand_aliasing={{0}: (2, {}), {1}: (3, {})} | custom-call | tf_op jit(solution)/shard_map/pallas_call | solution.py:729
  196.5 1.6 shard_map.216.half_ref
  198.2 2.1 %shard_map.217.refs_0_ = f32[9,256,512]{2,1,0:T(8,128)} custom-call(s32[1]{0:T(128)} %bitcast.side_ref, bf16[9,256,256]{2,1,0:T(8,128)(2,1)S(1)} %shard_map.216.half_ref), custom_call_target="tpu_custom_call" | custom-call | tf_op jit(solution)/shard_map/pallas_call | solution.py:729
  201.0 2.1 %shard_map.218 = f32[9,256,512]{2,1,0:T(8,128)} custom-call(s32[1]{0:T(128)} %bitcast.15.side_ref, bf16[9,256,256]{2,1,0:T(8,128)(2,1)S(1)} %collective-permute-done.36.half_ref, f32[9,256,512]{2,1,0:T(8,128)} %shard_map.217.refs_0_), custom_call_target="tpu_custom_call", output_to_operand_aliasing={{}: (2, {})} | custom-call | tf_op jit(solution)/shard_map/pallas_call | solution.py:729
  (135 shorter events, 28.7 us)
Async XLA Ops:
  3.5 17.7 %copy-start.1 = (bf16[2,16,32,256]{3,2,1,0:T(8,128)(2,1)S(1)}, bf16[2,16,32,256]{3,2,1,0:T(8,128)(2,1)}, u32[]{:S(2)}) copy-start(bf16[2,16,32,256]{3,2,1,0:T(8,128)(2,1)} %refs_0_.1) | copy-start | bytes 1572868
  3.5 17.7 %copy-start.5 = (bf16[256,512]{1,0:T(8,128)(2,1)S(1)}, bf16[256,512]{1,0:T(8,128)(2,1)}, u32[]{:S(2)}) copy-start(bf16[256,512]{1,0:T(8,128)(2,1)} %refs_4_.1) | copy-start | bytes 786436
  4.5 3.3 %collective-permute-start = (bf16[672,256]{1,0:T(8,128)(2,1)S(1)}, bf16[672,256]{1,0:T(8,128)(2,1)S(1)}, u32[]{:S(2)}, u32[]{:S(2)}) collective-permute-start(bf16[672,256]{1,0:T(8,128)(2,1)S(1)} %shard_map.203), channel_id=1, source_target_pairs={{0,16},{16,0},{1,17},{17,1},{2,18},{18,2},{3,19},{19,3},{4,20},{20... | collective-permute-start | bytes 1032200 | tf_op jit(solution)/shard_map/ppermute | solution.py:958
  5.1 2.8 %collective-permute-start.1 = (bf16[2,1,32,256]{3,2,1,0:T(8,128)(2,1)S(1)}, bf16[2,1,32,256]{3,2,1,0:T(8,128)(2,1)S(1)}, u32[]{:S(2)}, u32[]{:S(2)}) collective-permute-start(bf16[2,1,32,256]{3,2,1,0:T(8,128)(2,1)S(1)} %slice.57), channel_id=1, source_target_pairs={{0,16},{1,17},{2,18},{3,19},{4,20},{5,21},{6,22},{7,23},{8,24},{9,... | collective-permute-start | bytes 98312 | tf_op jit(solution)/shard_map/ppermute | solution.py:784
  9.2 6.4 %collective-permute-start.2 = (bf16[2,17,1,256]{3,2,1,0:T(2,128)(2,1)S(1)}, bf16[2,17,1,256]{3,2,1,0:T(2,128)(2,1)S(1)}, u32[]{:S(2)}, u32[]{:S(2)}) collective-permute-start(bf16[2,17,1,256]{3,2,1,0:T(2,128)(2,1)S(1)} %pad_maximum_fusion.11), channel_id=1, source_target_pairs={{0,4},{4,8},{8,12},{1,5},{5,9},{9,13},{2,6},{6,10},{10,14},{3,7},{... | collective-permute-start | bytes 52232 | tf_op jit(solution)/shard_map/ppermute | solution.py:784
  15.7 16.7 %collective-permute-start.3 = (bf16[480,256]{1,0:T(8,128)(2,1)S(1)}, bf16[480,256]{1,0:T(8,128)(2,1)S(1)}, u32[]{:S(2)}, u32[]{:S(2)}) collective-permute-start(bf16[480,256]{1,0:T(8,128)(2,1)S(1)} %get-tuple-element.117), channel_id=1, source_target_pairs={{0,4},{4,8},{8,12},{1,5},{5,9},{9,13},{2,6},{6,10},{10,14},{3,7},{... | collective-permute-start | bytes 737288 | tf_op jit(solution)/shard_map/ppermute | solution.py:784
  19.9 12.7 %collective-permute-start.4 = (bf16[480,256]{1,0:T(8,128)(2,1)S(1)}, bf16[480,256]{1,0:T(8,128)(2,1)S(1)}, u32[]{:S(2)}, u32[]{:S(2)}) collective-permute-start(bf16[480,256]{1,0:T(8,128)(2,1)S(1)} %get-tuple-element.118), channel_id=1, source_target_pairs={{4,0},{8,4},{12,8},{5,1},{9,5},{13,9},{6,2},{10,6},{14,10},{7,3},{... | collective-permute-start | bytes 737288 | tf_op jit(solution)/shard_map/ppermute | solution.py:784
  24.5 15.9 %all-to-all-start = ((f32[32,1,1152]{2,1,0:T(1,128)}), f32[32,1,1152]{2,1,0:T(1,128)S(1)}, u32[]{:S(2)}, u32[]{:S(2)}) async-start(f32[32,1,1152]{2,1,0:T(1,128)} %get-tuple-element.121), calls=%async_computation | async-start | bytes 294912 | tf_op jit(solution)/shard_map/all_to_all | solution.py:788
  40.4 21.2 %copy-start.6 = (f32[512]{0:T(512)S(1)}, f32[512]{0:T(512)}, u32[]{:S(2)}) copy-start(f32[512]{0:T(512)} %param.17) | copy-start | bytes 6148
  40.4 21.2 %copy-start.7 = (f32[512]{0:T(512)S(1)}, f32[512]{0:T(512)}, u32[]{:S(2)}) copy-start(f32[512]{0:T(512)} %param.20) | copy-start | bytes 6148
  40.4 21.2 %copy-start.12 = (f32[512]{0:T(512)S(1)}, f32[512]{0:T(512)}, u32[]{:S(2)}) copy-start(f32[512]{0:T(512)} %param.18) | copy-start | bytes 6148
  40.4 21.2 %copy-start.13 = (f32[512]{0:T(512)S(1)}, f32[512]{0:T(512)}, u32[]{:S(2)}) copy-start(f32[512]{0:T(512)} %param.21) | copy-start | bytes 6148
  46.8 14.8 %collective-permute-start.5 = (bf16[624,1536]{1,0:T(8,128)(2,1)}, bf16[624,1536]{1,0:T(8,128)(2,1)S(1)}, u32[]{:S(2)}, u32[]{:S(2)}) collective-permute-start(bf16[624,1536]{1,0:T(8,128)(2,1)} %get-tuple-element.129.refs_3_), channel_id=1, source_target_pairs={{0,16},{16,0},{1,17},{17,1},{2,18},{18,2},{3,19},{19,3},{4,20},{20... | collective-permute-start | bytes 5750792 | tf_op jit(solution)/shard_map/ppermute | solution.py:797
  46.8 14.7 %all-to-all-start.1 = ((f32[32,1,2048]{2,1,0:T(1,128)}), f32[32,1,2048]{2,1,0:T(1,128)S(1)}, u32[]{:S(2)}, u32[]{:S(2)}) async-start(f32[32,1,2048]{2,1,0:T(1,128)} %get-tuple-element.128), calls=%async_computation.1 | async-start | bytes 524288 | tf_op jit(solution)/shard_map/all_to_all | solution.py:788
  50.8 38.4 %copy-start.10 = (s32[5]{0:T(128)}, s32[5]{0:T(128)S(1)}, u32[]{:S(2)}) copy-start(s32[5]{0:T(128)S(1)} %stack.44.refs_0_) | copy-start | bytes 64
  67.1 4.0 %collective-permute-start.6 = (f32[3,384,256]{2,1,0:T(8,128)}, f32[3,384,256]{2,1,0:T(8,128)S(1)}, u32[]{:S(2)}, u32[]{:S(2)}) collective-permute-start(f32[3,384,256]{2,1,0:T(8,128)} %get-tuple-element.135), channel_id=1, source_target_pairs={{0,16},{16,0},{1,17},{17,1},{2,18},{18,2},{3,19},{19,3},{4,20},{20... | collective-permute-start | bytes 3538952 | tf_op jit(solution)/shard_map/ppermute | solution.py:797
  67.2 4.5 %collective-permute-start.7 = (bf16[624,768]{1,0:T(8,128)(2,1)}, bf16[624,768]{1,0:T(8,128)(2,1)}, u32[]{:S(2)}, u32[]{:S(2)}) collective-permute-start(bf16[624,768]{1,0:T(8,128)(2,1)} %get-tuple-element.138.refs_5_.refs_3_), channel_id=1, source_target_pairs={{0,16},{16,0},{1,17},{17,1},{2,18},{18,2},{3,19},{19,3},{4,20},{20... | collective-permute-start | bytes 2875400 | tf_op jit(solution)/shard_map/ppermute | solution.py:797
  67.7 12.0 %all-to-all-start.2 = ((f32[32,1,1536]{2,1,0:T(1,128)}), f32[32,1,1536]{2,1,0:T(1,128)S(1)}, u32[]{:S(2)}, u32[]{:S(2)}) async-start(f32[32,1,1536]{2,1,0:T(1,128)} %get-tuple-element.139), calls=%async_computation.2 | async-start | bytes 393216 | tf_op jit(solution)/shard_map/all_to_all | solution.py:788
  71.1 8.6 %collective-permute-start.8 = (f32[624,128]{1,0:T(8,128)S(1)}, f32[624,128]{1,0:T(8,128)S(1)}, u32[]{:S(2)}, u32[]{:S(2)}) collective-permute-start(f32[624,128]{1,0:T(8,128)S(1)} %get-tuple-element.141.refs_5_.refs_10_.refs_12_.refs_14_), channel_id=1, source_target_pairs={{0,16},{16,0},{1,17},{17,1},{2,18},{18,2},{3,19},{19,3},{4,20},{20... | collective-permute-start | bytes 958472 | tf_op jit(solution)/shard_map/ppermute | solution.py:797
  88.1 15.6 %collective-permute-start.10 = (bf16[19,64,256]{2,1,0:T(8,128)(2,1)}, bf16[19,64,256]{2,1,0:T(8,128)(2,1)S(1)}, u32[]{:S(2)}, u32[]{:S(2)}) collective-permute-start(bf16[19,64,256]{2,1,0:T(8,128)(2,1)} %get-tuple-element.149), channel_id=1, source_target_pairs={{0,8},{4,12},{8,0},{12,4},{1,9},{5,13},{9,1},{13,5},{2,10},{6,14},... | collective-permute-start | bytes 1867784 | tf_op jit(solution)/shard_map/ppermute | solution.py:797
  89.1 15.2 %collective-permute-start.9 = (bf16[19,64,256]{2,1,0:T(8,128)(2,1)S(1)}, bf16[19,64,256]{2,1,0:T(8,128)(2,1)}, u32[]{:S(2)}, u32[]{:S(2)}) collective-permute-start(bf16[19,64,256]{2,1,0:T(8,128)(2,1)S(1)} %get-tuple-element.147), channel_id=1, source_target_pairs={{0,4},{4,0},{8,12},{12,8},{1,5},{5,1},{9,13},{13,9},{2,6},{6,2},{1... | collective-permute-start | bytes 1867784 | tf_op jit(solution)/shard_map/ppermute | solution.py:797
  89.2 21.1 %collective-permute-start.14 = (bf16[672,768]{1,0:T(8,128)(2,1)}, bf16[672,768]{1,0:T(8,128)(2,1)}, u32[]{:S(2)}, u32[]{:S(2)}) collective-permute-start(bf16[672,768]{1,0:T(8,128)(2,1)} %get-tuple-element.159.refs_5_), channel_id=1, source_target_pairs={{0,16},{16,0},{1,17},{17,1},{2,18},{18,2},{3,19},{19,3},{4,20},{20... | collective-permute-start | bytes 3096584 | tf_op jit(solution)/shard_map/ppermute | solution.py:797
  97.8 12.5 %collective-permute-start.13 = (f32[2,384,256]{2,1,0:T(8,128)}, f32[2,384,256]{2,1,0:T(8,128)}, u32[]{:S(2)}, u32[]{:S(2)}) collective-permute-start(f32[2,384,256]{2,1,0:T(8,128)} %get-tuple-element.158), channel_id=1, source_target_pairs={{0,16},{16,0},{1,17},{17,1},{2,18},{18,2},{3,19},{19,3},{4,20},{20... | collective-permute-start | bytes 2359304 | tf_op jit(solution)/shard_map/ppermute | solution.py:797
  98.4 11.9 %all-to-all-start.3 = ((f32[32,1,1024]{2,1,0:T(1,128)}), f32[32,1,1024]{2,1,0:T(1,128)S(1)}, u32[]{:S(2)}, u32[]{:S(2)}) async-start(f32[32,1,1024]{2,1,0:T(1,128)} %get-tuple-element.160), calls=%async_computation.3 | async-start | bytes 262144 | tf_op jit(solution)/shard_map/all_to_all | solution.py:788
  108.4 8.8 %collective-permute-start.11 = (bf16[19,32,256]{2,1,0:T(8,128)(2,1)}, bf16[19,32,256]{2,1,0:T(8,128)(2,1)S(1)}, u32[]{:S(2)}, u32[]{:S(2)}) collective-permute-start(bf16[19,32,256]{2,1,0:T(8,128)(2,1)} %get-tuple-element.155), channel_id=1, source_target_pairs={{0,8},{4,12},{8,0},{12,4},{1,9},{5,13},{9,1},{13,5},{2,10},{6,14},... | collective-permute-start | bytes 933896 | tf_op jit(solution)/shard_map/ppermute | solution.py:797
  109.4 8.2 %collective-permute-start.12 = (bf16[19,32,256]{2,1,0:T(8,128)(2,1)}, bf16[19,32,256]{2,1,0:T(8,128)(2,1)}, u32[]{:S(2)}, u32[]{:S(2)}) collective-permute-start(bf16[19,32,256]{2,1,0:T(8,128)(2,1)} %get-tuple-element.156), channel_id=1, source_target_pairs={{0,4},{4,0},{8,12},{12,8},{1,5},{5,1},{9,13},{13,9},{2,6},{6,2},{1... | collective-permute-start | bytes 933896 | tf_op jit(solution)/shard_map/ppermute | solution.py:797
  119.3 10.4 %collective-permute-start.15 = (bf16[38,16,256]{2,1,0:T(8,128)(2,1)S(1)}, bf16[38,16,256]{2,1,0:T(8,128)(2,1)S(1)}, u32[]{:S(2)}, u32[]{:S(2)}) collective-permute-start(bf16[38,16,256]{2,1,0:T(8,128)(2,1)S(1)} %select_convert_fusion), channel_id=1, source_target_pairs={{0,1},{1,0},{2,3},{3,2},{4,5},{5,4},{6,7},{7,6},{8,9},{9,8},{10,11... | collective-permute-start | bytes 933896 | tf_op jit(solution)/shard_map/ppermute | solution.py:797
  120.9 8.4 %collective-permute-start.16 = (bf16[9,64,256]{2,1,0:T(8,128)(2,1)S(1)}, bf16[9,64,256]{2,1,0:T(8,128)(2,1)S(1)}, u32[]{:S(2)}, u32[]{:S(2)}) collective-permute-start(bf16[9,64,256]{2,1,0:T(8,128)(2,1)S(1)} %get-tuple-element.168), channel_id=1, source_target_pairs={{0,4},{4,0},{8,12},{12,8},{1,5},{5,1},{9,13},{13,9},{2,6},{6,2},{1... | collective-permute-start | bytes 884744 | tf_op jit(solution)/shard_map/ppermute | solution.py:797
  122.3 7.4 %collective-permute-start.17 = (bf16[9,64,256]{2,1,0:T(8,128)(2,1)S(1)}, bf16[9,64,256]{2,1,0:T(8,128)(2,1)S(1)}, u32[]{:S(2)}, u32[]{:S(2)}) collective-permute-start(bf16[9,64,256]{2,1,0:T(8,128)(2,1)S(1)} %get-tuple-element.169), channel_id=1, source_target_pairs={{0,8},{4,12},{8,0},{12,4},{1,9},{5,13},{9,1},{13,5},{2,10},{6,14},... | collective-permute-start | bytes 884744 | tf_op jit(solution)/shard_map/ppermute | solution.py:797
  129.8 5.2 %collective-permute-start.20 = (bf16[9,32,256]{2,1,0:T(8,128)(2,1)S(1)}, bf16[9,32,256]{2,1,0:T(8,128)(2,1)S(1)}, u32[]{:S(2)}, u32[]{:S(2)}) collective-permute-start(bf16[9,32,256]{2,1,0:T(8,128)(2,1)S(1)} %select_convert_fusion.3), channel_id=1, source_target_pairs={{0,4},{4,0},{8,12},{12,8},{1,5},{5,1},{9,13},{13,9},{2,6},{6,2},{1... | collective-permute-start | bytes 442376 | tf_op jit(solution)/shard_map/ppermute | solution.py:797
  131.3 7.4 %collective-permute-start.18 = (bf16[38,8,256]{2,1,0:T(8,128)(2,1)S(1)}, bf16[38,8,256]{2,1,0:T(8,128)(2,1)S(1)}, u32[]{:S(2)}, u32[]{:S(2)}) collective-permute-start(bf16[38,8,256]{2,1,0:T(8,128)(2,1)S(1)} %select_convert_fusion.1), channel_id=1, source_target_pairs={{0,2},{1,3},{2,0},{3,1},{4,6},{5,7},{6,4},{7,5},{8,10},{9,11},{10,... | collective-permute-start | bytes 466952 | tf_op jit(solution)/shard_map/ppermute | solution.py:797
  133.2 5.2 %collective-permute-start.19 = (bf16[9,32,256]{2,1,0:T(8,128)(2,1)S(1)}, bf16[9,32,256]{2,1,0:T(8,128)(2,1)S(1)}, u32[]{:S(2)}, u32[]{:S(2)}) collective-permute-start(bf16[9,32,256]{2,1,0:T(8,128)(2,1)S(1)} %select_convert_fusion.4), channel_id=1, source_target_pairs={{0,8},{4,12},{8,0},{12,4},{1,9},{5,13},{9,1},{13,5},{2,10},{6,14},... | collective-permute-start | bytes 442376 | tf_op jit(solution)/shard_map/ppermute | solution.py:797
  138.9 10.6 %collective-permute-start.21 = (bf16[38,8,256]{2,1,0:T(8,128)(2,1)S(1)}, bf16[38,8,256]{2,1,0:T(8,128)(2,1)S(1)}, u32[]{:S(2)}, u32[]{:S(2)}) collective-permute-start(bf16[38,8,256]{2,1,0:T(8,128)(2,1)S(1)} %add_convert_fusion), channel_id=1, source_target_pairs={{0,2},{1,3},{2,0},{3,1},{4,6},{5,7},{6,4},{7,5},{8,10},{9,11},{10,... | collective-permute-start | bytes 466952 | tf_op jit(solution)/shard_map/ppermute | solution.py:797
  140.0 9.5 %collective-permute-start.22 = (bf16[18,16,256]{2,1,0:T(8,128)(2,1)S(1)}, bf16[18,16,256]{2,1,0:T(8,128)(2,1)S(1)}, u32[]{:S(2)}, u32[]{:S(2)}) collective-permute-start(bf16[18,16,256]{2,1,0:T(8,128)(2,1)S(1)} %select_convert_fusion.2), channel_id=1, source_target_pairs={{0,1},{1,0},{2,3},{3,2},{4,5},{5,4},{6,7},{7,6},{8,9},{9,8},{10,11... | collective-permute-start | bytes 442376 | tf_op jit(solution)/shard_map/ppermute | solution.py:797
  149.6 8.5 %collective-permute-start.23 = (bf16[38,16,256]{2,1,0:T(8,128)(2,1)S(1)}, bf16[38,16,256]{2,1,0:T(8,128)(2,1)S(1)}, u32[]{:S(2)}, u32[]{:S(2)}) collective-permute-start(bf16[38,16,256]{2,1,0:T(8,128)(2,1)S(1)} %pad_maximum_fusion.5), channel_id=1, source_target_pairs={{0,1},{1,0},{2,3},{3,2},{4,5},{5,4},{6,7},{7,6},{8,9},{9,8},{10,11... | collective-permute-start | bytes 933896 | tf_op jit(solution)/shard_map/ppermute | solution.py:797
  151.0 5.9 %collective-permute-start.24 = (bf16[18,8,256]{2,1,0:T(8,128)(2,1)S(1)}, bf16[18,8,256]{2,1,0:T(8,128)(2,1)S(1)}, u32[]{:S(2)}, u32[]{:S(2)}) collective-permute-start(bf16[18,8,256]{2,1,0:T(8,128)(2,1)S(1)} %select_convert_fusion.5), channel_id=1, source_target_pairs={{0,2},{1,3},{2,0},{3,1},{4,6},{5,7},{6,4},{7,5},{8,10},{9,11},{10,... | collective-permute-start | bytes 221192 | tf_op jit(solution)/shard_map/ppermute | solution.py:797
  158.4 10.3 %collective-permute-start.25 = (bf16[19,32,256]{2,1,0:T(8,128)(2,1)S(1)}, bf16[19,32,256]{2,1,0:T(8,128)(2,1)S(1)}, u32[]{:S(2)}, u32[]{:S(2)}) collective-permute-start(bf16[19,32,256]{2,1,0:T(8,128)(2,1)S(1)} %get-tuple-element.216), channel_id=1, source_target_pairs={{0,8},{4,12},{8,0},{12,4},{1,9},{5,13},{9,1},{13,5},{2,10},{6,14},... | collective-permute-start | bytes 933896 | tf_op jit(solution)/shard_map/ppermute | solution.py:797
  159.4 10.1 %collective-permute-start.26 = (bf16[19,32,256]{2,1,0:T(8,128)(2,1)S(1)}, bf16[19,32,256]{2,1,0:T(8,128)(2,1)S(1)}, u32[]{:S(2)}, u32[]{:S(2)}) collective-permute-start(bf16[19,32,256]{2,1,0:T(8,128)(2,1)S(1)} %get-tuple-element.215), channel_id=1, source_target_pairs={{0,4},{4,0},{8,12},{12,8},{1,5},{5,1},{9,13},{13,9},{2,6},{6,2},{1... | collective-permute-start | bytes 933896 | tf_op jit(solution)/shard_map/ppermute | solution.py:797
  161.0 5.3 %collective-permute-start.27 = (bf16[18,8,256]{2,1,0:T(8,128)(2,1)S(1)}, bf16[18,8,256]{2,1,0:T(8,128)(2,1)S(1)}, u32[]{:S(2)}, u32[]{:S(2)}) collective-permute-start(bf16[18,8,256]{2,1,0:T(8,128)(2,1)S(1)} %add_convert_fusion.1), channel_id=1, source_target_pairs={{0,2},{1,3},{2,0},{3,1},{4,6},{5,7},{6,4},{7,5},{8,10},{9,11},{10,... | collective-permute-start | bytes 221192 | tf_op jit(solution)/shard_map/ppermute | solution.py:797
  169.6 15.4 %collective-permute-start.32 = (bf16[19,64,256]{2,1,0:T(8,128)(2,1)S(1)}, bf16[19,64,256]{2,1,0:T(8,128)(2,1)S(1)}, u32[]{:S(2)}, u32[]{:S(2)}) collective-permute-start(bf16[19,64,256]{2,1,0:T(8,128)(2,1)S(1)} %pad_maximum_fusion.3), channel_id=1, source_target_pairs={{0,8},{4,12},{8,0},{12,4},{1,9},{5,13},{9,1},{13,5},{2,10},{6,14},... | collective-permute-start | bytes 1867784 | tf_op jit(solution)/shard_map/ppermute | solution.py:797
  170.2 6.1 %collective-permute-start.28 = (bf16[18,16,256]{2,1,0:T(8,128)(2,1)S(1)}, bf16[18,16,256]{2,1,0:T(8,128)(2,1)S(1)}, u32[]{:S(2)}, u32[]{:S(2)}) collective-permute-start(bf16[18,16,256]{2,1,0:T(8,128)(2,1)S(1)} %pad_maximum_fusion.10), channel_id=1, source_target_pairs={{0,1},{1,0},{2,3},{3,2},{4,5},{5,4},{6,7},{7,6},{8,9},{9,8},{10,11... | collective-permute-start | bytes 442376 | tf_op jit(solution)/shard_map/ppermute | solution.py:797
  173.2 11.9 %collective-permute-start.31 = (bf16[19,64,256]{2,1,0:T(8,128)(2,1)S(1)}, bf16[19,64,256]{2,1,0:T(8,128)(2,1)S(1)}, u32[]{:S(2)}, u32[]{:S(2)}) collective-permute-start(bf16[19,64,256]{2,1,0:T(8,128)(2,1)S(1)} %pad_maximum_fusion.2), channel_id=1, source_target_pairs={{0,4},{4,0},{8,12},{12,8},{1,5},{5,1},{9,13},{13,9},{2,6},{6,2},{1... | collective-permute-start | bytes 1867784 | tf_op jit(solution)/shard_map/ppermute | solution.py:797
  176.4 5.2 %collective-permute-start.29 = (bf16[9,32,256]{2,1,0:T(8,128)(2,1)S(1)}, bf16[9,32,256]{2,1,0:T(8,128)(2,1)S(1)}, u32[]{:S(2)}, u32[]{:S(2)}) collective-permute-start(bf16[9,32,256]{2,1,0:T(8,128)(2,1)S(1)} %get-tuple-element.226), channel_id=1, source_target_pairs={{0,8},{4,12},{8,0},{12,4},{1,9},{5,13},{9,1},{13,5},{2,10},{6,14},... | collective-permute-start | bytes 442376 | tf_op jit(solution)/shard_map/ppermute | solution.py:797
  177.2 7.9 %collective-permute-start.30 = (bf16[9,32,256]{2,1,0:T(8,128)(2,1)S(1)}, bf16[9,32,256]{2,1,0:T(8,128)(2,1)S(1)}, u32[]{:S(2)}, u32[]{:S(2)}) collective-permute-start(bf16[9,32,256]{2,1,0:T(8,128)(2,1)S(1)} %get-tuple-element.225), channel_id=1, source_target_pairs={{0,4},{4,0},{8,12},{12,8},{1,5},{5,1},{9,13},{13,9},{2,6},{6,2},{1... | collective-permute-start | bytes 442376 | tf_op jit(solution)/shard_map/ppermute | solution.py:797
  186.2 5.8 %collective-permute-start.35 = (bf16[19,256,256]{2,1,0:T(8,128)(2,1)S(1)}, bf16[19,256,256]{2,1,0:T(8,128)(2,1)}, u32[]{:S(2)}, u32[]{:S(2)}) collective-permute-start(bf16[19,256,256]{2,1,0:T(8,128)(2,1)S(1)} %pad_maximum_fusion.half_ref), channel_id=1, source_target_pairs={{0,16},{16,0},{1,17},{17,1},{2,18},{18,2},{3,19},{19,3},{4,20},{20... | collective-permute-start | bytes 7471112 | tf_op jit(solution)/shard_map/ppermute | solution.py:797
  186.3 9.5 %collective-permute-start.34 = (bf16[9,64,256]{2,1,0:T(8,128)(2,1)S(1)}, bf16[9,64,256]{2,1,0:T(8,128)(2,1)S(1)}, u32[]{:S(2)}, u32[]{:S(2)}) collective-permute-start(bf16[9,64,256]{2,1,0:T(8,128)(2,1)S(1)} %pad_maximum_fusion.8.refs_2_), channel_id=1, source_target_pairs={{0,8},{4,12},{8,0},{12,4},{1,9},{5,13},{9,1},{13,5},{2,10},{6,14},... | collective-permute-start | bytes 884744 | tf_op jit(solution)/shard_map/ppermute | solution.py:797
  187.0 9.6 %collective-permute-start.33 = (bf16[9,64,256]{2,1,0:T(8,128)(2,1)S(1)}, bf16[9,64,256]{2,1,0:T(8,128)(2,1)}, u32[]{:S(2)}, u32[]{:S(2)}) collective-permute-start(bf16[9,64,256]{2,1,0:T(8,128)(2,1)S(1)} %pad_maximum_fusion.7.refs_0_), channel_id=1, source_target_pairs={{0,4},{4,0},{8,12},{12,8},{1,5},{5,1},{9,13},{13,9},{2,6},{6,2},{1... | collective-permute-start | bytes 884744 | tf_op jit(solution)/shard_map/ppermute | solution.py:797
  198.1 2.9 %collective-permute-start.36 = (bf16[9,256,256]{2,1,0:T(8,128)(2,1)S(1)}, bf16[9,256,256]{2,1,0:T(8,128)(2,1)S(1)}, u32[]{:S(2)}, u32[]{:S(2)}) collective-permute-start(bf16[9,256,256]{2,1,0:T(8,128)(2,1)S(1)} %shard_map.216.half_ref), channel_id=1, source_target_pairs={{0,16},{16,0},{1,17},{17,1},{2,18},{18,2},{3,19},{19,3},{4,20},{20... | collective-permute-start | bytes 3538952 | tf_op jit(solution)/shard_map/ppermute | solution.py:797
  (14 other events, 87.6 us)

commit v12 on v10

--- a/solution.py
+++ b/solution.py
@@ -1197,7 +1197,7 @@
     grad_w2, grad_wp = grad_second
     tree1.finish(1)
     tree1.start()
-    (grad_w1,) = widen(tree1.got[0], 1 - side, 3, 3, False, widen(tree1.value, side, 3, 3, False))
+    (grad_w1,) = widen(tree1.got[0], 1 - side, 9, 1, False, widen(tree1.value, side, 9, 1, False))
 
     return (
         third[N.out],

time: 203 us -> 204 us (level)
    pallas_call x4, Pallas kernels: 10.3 us -> 12.4 us  [widen(): pl.pallas_call(body, out_shape=[shape((taps * per, n, 2 * m))] + [shape((...]
  transfers between devices with their start and end apart: 41 -> 41, of which waited for: 27 -> 26; matrix products, arithmetic and copies ran while one was open for 0% -> 0% of each run, Pallas kernels for 21% -> 22%
where the time goes in v12:
time: 204 us
  Pallas kernels  71 us (35%)
  starting transfers between devices  65.8 us (32%)
  waiting for transfers between devices  57.6 us (28%)
  other arithmetic  5.1 us (2%)
  local copies, waits for them, and re-layouts  2.62 us (1%)
    pallas_call x11, Pallas kernels, call(): pl.pallas_call(run, out_shape=list(outs.values()), in_specs=[spec(n) for...  57.1 us
    ppermute x32, starting transfers between devices, partner(): return lax.ppermute(value, axis, [(i, i ^ step) for i in range(count)])  36.3 us
    ppermute x32, waiting for transfers between devices, partner(): return lax.ppermute(value, axis, [(i, i ^ step) for i in range(count)])  33.9 us
    all_to_all x4, waiting for transfers between devices, gather_sum(): return lax.all_to_all(spread, axes, 0, 0)  21.2 us
    all_to_all x4, starting transfers between devices, gather_sum(): return lax.all_to_all(spread, axes, 0, 0)  16.6 us
    pallas_call x4, Pallas kernels, widen(): pl.pallas_call(body, out_shape=[shape((taps * per, n, 2 * m))] + [shape((...  12.4 us
    ppermute x4, starting transfers between devices, shifted(): lax.ppermute(value, axis, [(source, source + steps) for source in range(f...  12.3 us
  transfers between devices with their start and end apart: 41, of which 26 were waited for; matrix products, arithmetic and copies ran while one was open for 0% of the time, Pallas kernels for 22%

profile of v12, /device:TPU:0, one launch (start us, length us, event | category | flops | bytes accessed | tf_op | source)
XLA Modules:
  0.0 203.7 jit_solution(11838884135739294296)
XLA Ops:
  5.1 2.0 collective-permute-start.1
  9.2 4.8 %collective-permute-start.2 = (bf16[2,17,1,256]{3,2,1,0:T(2,128)(2,1)S(1)}, bf16[2,17,1,256]{3,2,1,0:T(2,128)(2,1)S(1)}, u32[]{:S(2)}, u32[]{:S(2)}) collective-permute-start(bf16[2,17,1,256]{3,2,1,0:T(2,128)(2,1)S(1)} %pad_maximum_fusion.11), channel_id=1, source_target_pairs={{0,4},{4,8},{8,12},{1,5},{5,9},{9,13},{2,6},{6,10},{10,14},{3,7},{... | collective-permute-start | bytes 52232 | tf_op jit(solution)/shard_map/ppermute | solution.py:785
  14.1 1.6 collective-permute-done.2.refs_2_
  15.7 4.2 %collective-permute-start.3 = (bf16[480,256]{1,0:T(8,128)(2,1)S(1)}, bf16[480,256]{1,0:T(8,128)(2,1)S(1)}, u32[]{:S(2)}, u32[]{:S(2)}) collective-permute-start(bf16[480,256]{1,0:T(8,128)(2,1)S(1)} %get-tuple-element.115), channel_id=1, source_target_pairs={{0,4},{4,8},{8,12},{1,5},{5,9},{9,13},{2,6},{6,10},{10,14},{3,7},{... | collective-permute-start | bytes 737288 | tf_op jit(solution)/shard_map/ppermute | solution.py:785
  21.2 3.3 %shard_map.206 = f32[32,1,2176]{2,1,0:T(1,128)} custom-call(bf16[2,16,32,256]{3,2,1,0:T(8,128)(2,1)S(1)} %copy-done.1, bf16[2,1,32,256]{3,2,1,0:T(8,128)(2,1)S(1)} %collective-permute-done.1.refs_1_, bf16[2,17,1,256]{3,2,1,0:T(2,128)(2,1)S(1)} %collective-permute-done.2.refs_2_, bf16[2,8,16,128]{3,2,1,0:T(8,128)(2,1)S(1)} %broadcast_in_dim.2.refs_3_, ...), custom_call_target="tpu_custom_call" | custom-call | tf_op jit(solution)/shard_map/pallas_call | solution.py:113
  24.6 7.9 %all-to-all-start = ((f32[32,1,2176]{2,1,0:T(1,128)}), f32[32,1,2176]{2,1,0:T(1,128)S(1)}, u32[]{:S(2)}, u32[]{:S(2)}) async-start(f32[32,1,2176]{2,1,0:T(1,128)} %shard_map.206), calls=%async_computation | async-start | bytes 557056 | tf_op jit(solution)/shard_map/all_to_all | solution.py:789
  32.6 5.7 %shard_map.205 = (f32[624,512]{1,0:T(8,128)}, f32[624,512]{1,0:T(8,128)}, bf16[624,768]{1,0:T(8,128)(2,1)}, bf16[672,768]{1,0:T(8,128)(2,1)}, f32[624,128]{1,0:T...) custom-call(s32[2]{0:T(128)S(1)} %add_convert_fusion.2.refs_0_, bf16[2,16,32,256]{3,2,1,0:T(8,128)(2,1)} %refs_0_.1, ...), custom_call_target="tpu_custom_call" | custom-call | flops 20000000000 | tf_op jit(solution)/shard_map/pallas_call | solution.py:113
  38.3 5.5 %all-to-all-done.refs_1_ = f32[32,1,2176]{2,1,0:T(1,128)S(1)} async-done(((f32[32,1,2176]{2,1,0:T(1,128)}), f32[32,1,2176]{2,1,0:T(1,128)S(1)}, u32[]{:S(2)}, u32[]{:S(2)}) %all-to-all-start) | async-done | bytes 278560 | tf_op jit(solution)/shard_map/all_to_all | solution.py:789
  43.8 6.3 %shard_map.207 = (bf16[624,1536]{1,0:T(8,128)(2,1)}, f32[528,512]{1,0:T(8,128)}, f32[32,1,1024]{2,1,0:T(1,128)}, f32[8,512]{1,0:T(8,128)S(1)}) custom-call(f32[624,512]{1,0:T(8,128)} %get-tuple-element.117.refs_0_.refs_3_, f32[32,1,2176]{2,1,0:T(1,128)S(1)} %all-to-all-done.refs_1_, f32[1,512]{1,0:T(1,128)S(1)} %bitcast.36, f32[1,512]{1,0:T(1,128)S(1)} %bitcast.34, ...), custom_call_target="tpu_custom_call" | custom-call | tf_op jit(solution)/shard_map/pallas_call | solution.py:113
  50.1 2.6 %all-to-all-start.1 = ((f32[32,1,1024]{2,1,0:T(1,128)}), f32[32,1,1024]{2,1,0:T(1,128)S(1)}, u32[]{:S(2)}, u32[]{:S(2)}) async-start(f32[32,1,1024]{2,1,0:T(1,128)} %get-tuple-element.124), calls=%async_computation.1 | async-start | bytes 262144 | tf_op jit(solution)/shard_map/all_to_all | solution.py:789
  52.9 7.7 %all-to-all-done.1.refs_4_ = f32[32,1,1024]{2,1,0:T(1,128)S(1)} async-done(((f32[32,1,1024]{2,1,0:T(1,128)}), f32[32,1,1024]{2,1,0:T(1,128)S(1)}, u32[]{:S(2)}, u32[]{:S(2)}) %all-to-all-start.1) | async-done | bytes 131104 | tf_op jit(solution)/shard_map/all_to_all | solution.py:789
  60.7 5.5 %shard_map.208 = (bf16[2,8,16,512]{3,2,1,0:T(8,128)(2,1)}, f32[528,512]{1,0:T(8,128)}, f32[32,1,1536]{2,1,0:T(1,128)}, f32[8,512]{1,0:T(8,128)S(1)}, f32[3,384,256]{2,1,0:T(8,128)}, /*index=5*/f32[3,384,256]{2,1,0:T(8,128)}) custom-call(s32[5]{0:T(128)S(1)} %stack.44.refs_0_, f32[528,512]{1,0:T(8,128)} %get-tuple-element.121.refs_1_.refs_2_, ...), custom_call_target="tpu_custom_call" | custom-call | tf_op jit(solution)/shard_map/pallas_call | solution.py:113
  66.8 2.8 %all-to-all-start.2 = ((f32[32,1,1536]{2,1,0:T(1,128)}), f32[32,1,1536]{2,1,0:T(1,128)S(1)}, u32[]{:S(2)}, u32[]{:S(2)}) async-start(f32[32,1,1536]{2,1,0:T(1,128)} %get-tuple-element.135), calls=%async_computation.2 | async-start | bytes 393216 | tf_op jit(solution)/shard_map/all_to_all | solution.py:789
  70.8 8.0 %all-to-all-done.2.refs_7_.refs_8_ = f32[32,1,1536]{2,1,0:T(1,128)S(1)} async-done(((f32[32,1,1536]{2,1,0:T(1,128)}), f32[32,1,1536]{2,1,0:T(1,128)S(1)}, u32[]{:S(2)}, u32[]{:S(2)}) %all-to-all-start.2) | async-done | bytes 196640 | tf_op jit(solution)/shard_map/all_to_all | solution.py:789
  78.8 8.4 %shard_map.209 = (bf16[19,64,256]{2,1,0:T(8,128)(2,1)S(1)}, f32[19,64,256]{2,1,0:T(8,128)}, bf16[19,64,256]{2,1,0:T(8,128)(2,1)}, f32[19,64,256]{2,1,0:T(8,128)}) custom-call(s32[5]{0:T(128)S(1)} %stack.44.refs_0_, f32[3,384,256]{2,1,0:T(8,128)} %get-tuple-element.130.refs_1_, f32[3,384,256]{2,1,0:T(8,128)} %copy-done.18, ...), custom_call_target="tpu_custom_call" | custom-call | tf_op jit(solution)/shard_map/pallas_call | solution.py:113
  88.3 8.6 %shard_map.211 = (f32[432,512]{1,0:T(8,128)}, f32[432,512]{1,0:T(8,128)}, f32[32,1,1024]{2,1,0:T(1,128)}, f32[2,384,256]{2,1,0:T(8,128)}, f32[2,384,256]{2,1,0:T...) custom-call(s32[5]{0:T(128)S(1)} %stack.44.refs_0_, ...), custom_call_target="tpu_custom_call" | custom-call | tf_op jit(solution)/shard_map/pallas_call | solution.py:113
  97.5 3.4 %all-to-all-start.3 = ((f32[32,1,1024]{2,1,0:T(1,128)}), f32[32,1,1024]{2,1,0:T(1,128)S(1)}, u32[]{:S(2)}, u32[]{:S(2)}) async-start(f32[32,1,1024]{2,1,0:T(1,128)} %get-tuple-element.156), calls=%async_computation.3 | async-start | bytes 262144 | tf_op jit(solution)/shard_map/all_to_all | solution.py:789
  100.9 1.9 collective-permute-done.10.refs_4_
  103.7 3.8 %shard_map.210 = (bf16[19,32,256]{2,1,0:T(8,128)(2,1)}, f32[19,32,256]{2,1,0:T(8,128)}, bf16[19,32,256]{2,1,0:T(8,128)(2,1)}, f32[19,32,256]{2,1,0:T(8,128)}) custom-call(s32[5]{0:T(128)} %copy-done.10, f32[19,64,256]{2,1,0:T(8,128)} %get-tuple-element.142.refs_1_, bf16[19,64,256]{2,1,0:T(8,128)(2,1)} %collective-permute-done.9.refs_2_, ...), custom_call_target="tpu_custom_call" | custom-call | flops 20000000000 | tf_op jit(solution)/shard_map/pallas_call | solution.py:113
  109.4 6.9 %shard_map.212 = (bf16[9,64,256]{2,1,0:T(8,128)(2,1)S(1)}, f32[9,64,256]{2,1,0:T(8,128)S(1)}, bf16[9,64,256]{2,1,0:T(8,128)(2,1)S(1)}, f32[9,64,256]{2,1,0:T(8,1...) custom-call(s32[5]{0:T(128)S(1)} %copy-done.11, f32[2,384,256]{2,1,0:T(8,128)} %get-tuple-element.153.refs_1_, ...), custom_call_target="tpu_custom_call" | custom-call | flops 20000000000 | tf_op jit(solution)/shard_map/pallas_call | solution.py:113
  116.7 1.5 convert_add_fusion.1
  118.4 1.5 collective-permute-start.15
  120.0 1.5 collective-permute-start.16
  122.0 6.4 %shard_map.213 = bf16[2,16,32,256]{3,2,1,0:T(8,128)(2,1)} custom-call(f32[432,512]{1,0:T(8,128)S(1)} %copy-done.14, f32[432,512]{1,0:T(8,128)} %get-tuple-element.167.refs_1_, bf16[384,512]{1,0:T(8,128)(2,1)S(1)} %get-tuple-element.168.refs_2_, bf16[3,768,512]{2,1,0:T(8,128)(2,1)} %bitcast.50, bf16[256,512]{1,0:T(8,128)(2,1)S(1)} %copy-done.5, ...), custom_call_target="tpu_custom_call" | custom-call | flops 10000000000 | tf_op jit(solution)/shard_map/pallas_call | solution.py:113
  128.9 1.3 collective-permute-start.20
  130.4 1.8 collective-permute-start.18
  134.1 3.5 %collective-permute-done.19 = bf16[9,32,256]{2,1,0:T(8,128)(2,1)S(1)} collective-permute-done((bf16[9,32,256]{2,1,0:T(8,128)(2,1)S(1)}, bf16[9,32,256]{2,1,0:T(8,128)(2,1)S(1)}, u32[]{:S(2)}, u32[]{:S(2)}) %collective-permute-start.19) | collective-permute-done | bytes 147488 | tf_op jit(solution)/shard_map/ppermute | solution.py:798
  139.1 4.1 %collective-permute-start.22 = (bf16[18,16,256]{2,1,0:T(8,128)(2,1)S(1)}, bf16[18,16,256]{2,1,0:T(8,128)(2,1)S(1)}, u32[]{:S(2)}, u32[]{:S(2)}) collective-permute-start(bf16[18,16,256]{2,1,0:T(8,128)(2,1)S(1)} %select_convert_fusion.2), channel_id=1, source_target_pairs={{0,1},{1,0},{2,3},{3,2},{4,5},{5,4},{6,7},{7,6},{8,9},{9,8},{10,11... | collective-permute-start | bytes 442376 | tf_op jit(solution)/shard_map/ppermute | solution.py:798
  143.1 5.5 %collective-permute-done.22 = bf16[18,16,256]{2,1,0:T(8,128)(2,1)S(1)} collective-permute-done((bf16[18,16,256]{2,1,0:T(8,128)(2,1)S(1)}, bf16[18,16,256]{2,1,0:T(8,128)(2,1)S(1)}, u32[]{:S(2)}, u32[]{:S(2)}) %collective-permute-start.22) | collective-permute-done | bytes 147488 | tf_op jit(solution)/shard_map/ppermute | solution.py:798
  148.7 1.4 collective-permute-start.23
  150.1 2.5 %collective-permute-start.24 = (bf16[18,8,256]{2,1,0:T(8,128)(2,1)S(1)}, bf16[18,8,256]{2,1,0:T(8,128)(2,1)S(1)}, u32[]{:S(2)}, u32[]{:S(2)}) collective-permute-start(bf16[18,8,256]{2,1,0:T(8,128)(2,1)S(1)} %select_convert_fusion.5), channel_id=1, source_target_pairs={{0,2},{1,3},{2,0},{3,1},{4,6},{5,7},{6,4},{7,5},{8,10},{9,11},{10,... | collective-permute-start | bytes 221192 | tf_op jit(solution)/shard_map/ppermute | solution.py:798
  152.6 3.4 %collective-permute-done.24 = bf16[18,8,256]{2,1,0:T(8,128)(2,1)S(1)} collective-permute-done((bf16[18,8,256]{2,1,0:T(8,128)(2,1)S(1)}, bf16[18,8,256]{2,1,0:T(8,128)(2,1)S(1)}, u32[]{:S(2)}, u32[]{:S(2)}) %collective-permute-start.24) | collective-permute-done | bytes 73760 | tf_op jit(solution)/shard_map/ppermute | solution.py:798
  158.5 1.5 collective-permute-start.26
  160.1 2.3 %collective-permute-start.27 = (bf16[18,8,256]{2,1,0:T(8,128)(2,1)S(1)}, bf16[18,8,256]{2,1,0:T(8,128)(2,1)S(1)}, u32[]{:S(2)}, u32[]{:S(2)}) collective-permute-start(bf16[18,8,256]{2,1,0:T(8,128)(2,1)S(1)} %add_convert_fusion.1), channel_id=1, source_target_pairs={{0,2},{1,3},{2,0},{3,1},{4,6},{5,7},{6,4},{7,5},{8,10},{9,11},{10,... | collective-permute-start | bytes 221192 | tf_op jit(solution)/shard_map/ppermute | solution.py:798
  162.4 3.0 %collective-permute-done.27 = bf16[18,8,256]{2,1,0:T(8,128)(2,1)S(1)} collective-permute-done((bf16[18,8,256]{2,1,0:T(8,128)(2,1)S(1)}, bf16[18,8,256]{2,1,0:T(8,128)(2,1)S(1)}, u32[]{:S(2)}, u32[]{:S(2)}) %collective-permute-start.27) | collective-permute-done | bytes 73760 | tf_op jit(solution)/shard_map/ppermute | solution.py:798
  165.4 2.4 %collective-permute-done.25 = bf16[19,32,256]{2,1,0:T(8,128)(2,1)S(1)} collective-permute-done((bf16[19,32,256]{2,1,0:T(8,128)(2,1)S(1)}, bf16[19,32,256]{2,1,0:T(8,128)(2,1)S(1)}, u32[]{:S(2)}, u32[]{:S(2)}) %collective-permute-start.25) | collective-permute-done | bytes 311328 | tf_op jit(solution)/shard_map/ppermute | solution.py:798
  169.3 3.0 %collective-permute-start.28 = (bf16[18,16,256]{2,1,0:T(8,128)(2,1)S(1)}, bf16[18,16,256]{2,1,0:T(8,128)(2,1)S(1)}, u32[]{:S(2)}, u32[]{:S(2)}) collective-permute-start(bf16[18,16,256]{2,1,0:T(8,128)(2,1)S(1)} %pad_maximum_fusion.10), channel_id=1, source_target_pairs={{0,1},{1,0},{2,3},{3,2},{4,5},{5,4},{6,7},{7,6},{8,9},{9,8},{10,11... | collective-permute-start | bytes 442376 | tf_op jit(solution)/shard_map/ppermute | solution.py:798
  172.3 1.5 collective-permute-start.31
  173.8 1.6 collective-permute-done.28
  176.3 1.8 collective-permute-start.30
  178.1 2.6 %collective-permute-done.29 = bf16[9,32,256]{2,1,0:T(8,128)(2,1)S(1)} collective-permute-done((bf16[9,32,256]{2,1,0:T(8,128)(2,1)S(1)}, bf16[9,32,256]{2,1,0:T(8,128)(2,1)S(1)}, u32[]{:S(2)}, u32[]{:S(2)}) %collective-permute-start.29) | collective-permute-done | bytes 147488 | tf_op jit(solution)/shard_map/ppermute | solution.py:798
  180.7 3.5 %collective-permute-done.30 = bf16[9,32,256]{2,1,0:T(8,128)(2,1)S(1)} collective-permute-done((bf16[9,32,256]{2,1,0:T(8,128)(2,1)S(1)}, bf16[9,32,256]{2,1,0:T(8,128)(2,1)S(1)}, u32[]{:S(2)}, u32[]{:S(2)}) %collective-permute-start.30) | collective-permute-done | bytes 147488 | tf_op jit(solution)/shard_map/ppermute | solution.py:798
  186.1 2.1 %collective-permute-start.33 = (bf16[9,64,256]{2,1,0:T(8,128)(2,1)S(1)}, bf16[9,64,256]{2,1,0:T(8,128)(2,1)}, u32[]{:S(2)}, u32[]{:S(2)}) collective-permute-start(bf16[9,64,256]{2,1,0:T(8,128)(2,1)S(1)} %pad_maximum_fusion.7.refs_0_), channel_id=1, source_target_pairs={{0,4},{4,0},{8,12},{12,8},{1,5},{5,1},{9,13},{13,9},{2,6},{6,2},{1... | collective-permute-start | bytes 884744 | tf_op jit(solution)/shard_map/ppermute | solution.py:798
  188.2 2.8 %shard_map.214 = (f32[18,256,512]{2,1,0:T(8,128)}, f32[1,256,512]{2,1,0:T(8,128)}) custom-call(s32[1]{0:T(128)} %bitcast.side_ref, bf16[19,256,256]{2,1,0:T(8,128)(2,1)S(1)} %pad_maximum_fusion.half_ref), custom_call_target="tpu_custom_call" | custom-call | tf_op jit(solution)/shard_map/pallas_call | solution.py:730
  191.0 3.4 %shard_map.215 = (f32[18,256,512]{2,1,0:T(8,128)}, f32[1,256,512]{2,1,0:T(8,128)}) custom-call(s32[1]{0:T(128)} %bitcast.15.side_ref, bf16[19,256,256]{2,1,0:T(8,128)(2,1)} %collective-permute-done.35.half_ref, f32[18,256,512]{2,1,0:T(8,128)} %get-tuple-element.191.refs_0_, ...), custom_call_target="tpu_custom_call", output_to_operand_aliasing={{0}: (2, {}), {1}: (3, {})} | custom-call | tf_op jit(solution)/shard_map/pallas_call | solution.py:730
  195.6 1.6 shard_map.216.half_ref
  197.3 3.1 %shard_map.217.refs_0_ = f32[9,256,512]{2,1,0:T(8,128)} custom-call(s32[1]{0:T(128)} %bitcast.side_ref, bf16[9,256,256]{2,1,0:T(8,128)(2,1)S(1)} %shard_map.216.half_ref), custom_call_target="tpu_custom_call" | custom-call | tf_op jit(solution)/shard_map/pallas_call | solution.py:730
  200.4 3.1 %shard_map.218 = f32[9,256,512]{2,1,0:T(8,128)} custom-call(s32[1]{0:T(128)} %bitcast.15.side_ref, bf16[9,256,256]{2,1,0:T(8,128)(2,1)S(1)} %collective-permute-done.36.half_ref, f32[9,256,512]{2,1,0:T(8,128)} %shard_map.217.refs_0_), custom_call_target="tpu_custom_call", output_to_operand_aliasing={{}: (2, {})} | custom-call | tf_op jit(solution)/shard_map/pallas_call | solution.py:730
  (135 shorter events, 27.8 us)
Async XLA Ops:
  3.5 17.7 %copy-start.1 = (bf16[2,16,32,256]{3,2,1,0:T(8,128)(2,1)S(1)}, bf16[2,16,32,256]{3,2,1,0:T(8,128)(2,1)}, u32[]{:S(2)}) copy-start(bf16[2,16,32,256]{3,2,1,0:T(8,128)(2,1)} %refs_0_.1) | copy-start | bytes 1572868
  3.5 17.7 %copy-start.5 = (bf16[256,512]{1,0:T(8,128)(2,1)S(1)}, bf16[256,512]{1,0:T(8,128)(2,1)}, u32[]{:S(2)}) copy-start(bf16[256,512]{1,0:T(8,128)(2,1)} %refs_4_.1) | copy-start | bytes 786436
  4.5 3.3 %collective-permute-start = (bf16[672,256]{1,0:T(8,128)(2,1)S(1)}, bf16[672,256]{1,0:T(8,128)(2,1)S(1)}, u32[]{:S(2)}, u32[]{:S(2)}) collective-permute-start(bf16[672,256]{1,0:T(8,128)(2,1)S(1)} %shard_map.203), channel_id=1, source_target_pairs={{0,16},{16,0},{1,17},{17,1},{2,18},{18,2},{3,19},{19,3},{4,20},{20... | collective-permute-start | bytes 1032200 | tf_op jit(solution)/shard_map/ppermute | solution.py:959
  5.1 2.8 %collective-permute-start.1 = (bf16[2,1,32,256]{3,2,1,0:T(8,128)(2,1)S(1)}, bf16[2,1,32,256]{3,2,1,0:T(8,128)(2,1)S(1)}, u32[]{:S(2)}, u32[]{:S(2)}) collective-permute-start(bf16[2,1,32,256]{3,2,1,0:T(8,128)(2,1)S(1)} %slice.57), channel_id=1, source_target_pairs={{0,16},{1,17},{2,18},{3,19},{4,20},{5,21},{6,22},{7,23},{8,24},{9,... | collective-permute-start | bytes 98312 | tf_op jit(solution)/shard_map/ppermute | solution.py:785
  9.2 6.4 %collective-permute-start.2 = (bf16[2,17,1,256]{3,2,1,0:T(2,128)(2,1)S(1)}, bf16[2,17,1,256]{3,2,1,0:T(2,128)(2,1)S(1)}, u32[]{:S(2)}, u32[]{:S(2)}) collective-permute-start(bf16[2,17,1,256]{3,2,1,0:T(2,128)(2,1)S(1)} %pad_maximum_fusion.11), channel_id=1, source_target_pairs={{0,4},{4,8},{8,12},{1,5},{5,9},{9,13},{2,6},{6,10},{10,14},{3,7},{... | collective-permute-start | bytes 52232 | tf_op jit(solution)/shard_map/ppermute | solution.py:785
  15.7 16.8 %collective-permute-start.3 = (bf16[480,256]{1,0:T(8,128)(2,1)S(1)}, bf16[480,256]{1,0:T(8,128)(2,1)S(1)}, u32[]{:S(2)}, u32[]{:S(2)}) collective-permute-start(bf16[480,256]{1,0:T(8,128)(2,1)S(1)} %get-tuple-element.115), channel_id=1, source_target_pairs={{0,4},{4,8},{8,12},{1,5},{5,9},{9,13},{2,6},{6,10},{10,14},{3,7},{... | collective-permute-start | bytes 737288 | tf_op jit(solution)/shard_map/ppermute | solution.py:785
  19.9 12.7 %collective-permute-start.4 = (bf16[480,256]{1,0:T(8,128)(2,1)S(1)}, bf16[480,256]{1,0:T(8,128)(2,1)S(1)}, u32[]{:S(2)}, u32[]{:S(2)}) collective-permute-start(bf16[480,256]{1,0:T(8,128)(2,1)S(1)} %get-tuple-element.116), channel_id=1, source_target_pairs={{4,0},{8,4},{12,8},{5,1},{9,5},{13,9},{6,2},{10,6},{14,10},{7,3},{... | collective-permute-start | bytes 737288 | tf_op jit(solution)/shard_map/ppermute | solution.py:785
  24.6 19.2 %all-to-all-start = ((f32[32,1,2176]{2,1,0:T(1,128)}), f32[32,1,2176]{2,1,0:T(1,128)S(1)}, u32[]{:S(2)}, u32[]{:S(2)}) async-start(f32[32,1,2176]{2,1,0:T(1,128)} %shard_map.206), calls=%async_computation | async-start | bytes 557056 | tf_op jit(solution)/shard_map/all_to_all | solution.py:789
  43.7 16.9 %copy-start.6 = (f32[512]{0:T(512)S(1)}, f32[512]{0:T(512)}, u32[]{:S(2)}) copy-start(f32[512]{0:T(512)} %param.17) | copy-start | bytes 6148
  43.7 16.9 %copy-start.7 = (f32[512]{0:T(512)S(1)}, f32[512]{0:T(512)}, u32[]{:S(2)}) copy-start(f32[512]{0:T(512)} %param.20) | copy-start | bytes 6148
  43.7 16.9 %copy-start.12 = (f32[512]{0:T(512)S(1)}, f32[512]{0:T(512)}, u32[]{:S(2)}) copy-start(f32[512]{0:T(512)} %param.18) | copy-start | bytes 6148
  43.8 16.9 %copy-start.13 = (f32[512]{0:T(512)S(1)}, f32[512]{0:T(512)}, u32[]{:S(2)}) copy-start(f32[512]{0:T(512)} %param.21) | copy-start | bytes 6148
  50.1 10.6 %collective-permute-start.5 = (bf16[624,1536]{1,0:T(8,128)(2,1)}, bf16[624,1536]{1,0:T(8,128)(2,1)S(1)}, u32[]{:S(2)}, u32[]{:S(2)}) collective-permute-start(bf16[624,1536]{1,0:T(8,128)(2,1)} %get-tuple-element.125.refs_3_), channel_id=1, source_target_pairs={{0,16},{16,0},{1,17},{17,1},{2,18},{18,2},{3,19},{19,3},{4,20},{20... | collective-permute-start | bytes 5750792 | tf_op jit(solution)/shard_map/ppermute | solution.py:798
  50.1 10.5 %all-to-all-start.1 = ((f32[32,1,1024]{2,1,0:T(1,128)}), f32[32,1,1024]{2,1,0:T(1,128)S(1)}, u32[]{:S(2)}, u32[]{:S(2)}) async-start(f32[32,1,1024]{2,1,0:T(1,128)} %get-tuple-element.124), calls=%async_computation.1 | async-start | bytes 262144 | tf_op jit(solution)/shard_map/all_to_all | solution.py:789
  52.9 35.4 %copy-start.10 = (s32[5]{0:T(128)}, s32[5]{0:T(128)S(1)}, u32[]{:S(2)}) copy-start(s32[5]{0:T(128)S(1)} %stack.44.refs_0_) | copy-start | bytes 64
  66.2 4.0 %collective-permute-start.6 = (f32[3,384,256]{2,1,0:T(8,128)}, f32[3,384,256]{2,1,0:T(8,128)S(1)}, u32[]{:S(2)}, u32[]{:S(2)}) collective-permute-start(f32[3,384,256]{2,1,0:T(8,128)} %get-tuple-element.131), channel_id=1, source_target_pairs={{0,16},{16,0},{1,17},{17,1},{2,18},{18,2},{3,19},{19,3},{4,20},{20... | collective-permute-start | bytes 3538952 | tf_op jit(solution)/shard_map/ppermute | solution.py:798
  66.3 4.5 %collective-permute-start.7 = (bf16[624,768]{1,0:T(8,128)(2,1)}, bf16[624,768]{1,0:T(8,128)(2,1)}, u32[]{:S(2)}, u32[]{:S(2)}) collective-permute-start(bf16[624,768]{1,0:T(8,128)(2,1)} %get-tuple-element.134.refs_5_.refs_3_), channel_id=1, source_target_pairs={{0,16},{16,0},{1,17},{17,1},{2,18},{18,2},{3,19},{19,3},{4,20},{20... | collective-permute-start | bytes 2875400 | tf_op jit(solution)/shard_map/ppermute | solution.py:798
  66.8 12.0 %all-to-all-start.2 = ((f32[32,1,1536]{2,1,0:T(1,128)}), f32[32,1,1536]{2,1,0:T(1,128)S(1)}, u32[]{:S(2)}, u32[]{:S(2)}) async-start(f32[32,1,1536]{2,1,0:T(1,128)} %get-tuple-element.135), calls=%async_computation.2 | async-start | bytes 393216 | tf_op jit(solution)/shard_map/all_to_all | solution.py:789
  70.2 8.6 %collective-permute-start.8 = (f32[624,128]{1,0:T(8,128)S(1)}, f32[624,128]{1,0:T(8,128)S(1)}, u32[]{:S(2)}, u32[]{:S(2)}) collective-permute-start(f32[624,128]{1,0:T(8,128)S(1)} %get-tuple-element.137.refs_5_.refs_10_.refs_12_.refs_14_), channel_id=1, source_target_pairs={{0,16},{16,0},{1,17},{17,1},{2,18},{18,2},{3,19},{19,3},{4,20},{20... | collective-permute-start | bytes 958472 | tf_op jit(solution)/shard_map/ppermute | solution.py:798
  87.2 15.6 %collective-permute-start.10 = (bf16[19,64,256]{2,1,0:T(8,128)(2,1)}, bf16[19,64,256]{2,1,0:T(8,128)(2,1)S(1)}, u32[]{:S(2)}, u32[]{:S(2)}) collective-permute-start(bf16[19,64,256]{2,1,0:T(8,128)(2,1)} %get-tuple-element.145), channel_id=1, source_target_pairs={{0,8},{4,12},{8,0},{12,4},{1,9},{5,13},{9,1},{13,5},{2,10},{6,14},... | collective-permute-start | bytes 1867784 | tf_op jit(solution)/shard_map/ppermute | solution.py:798
  88.2 15.2 %collective-permute-start.9 = (bf16[19,64,256]{2,1,0:T(8,128)(2,1)S(1)}, bf16[19,64,256]{2,1,0:T(8,128)(2,1)}, u32[]{:S(2)}, u32[]{:S(2)}) collective-permute-start(bf16[19,64,256]{2,1,0:T(8,128)(2,1)S(1)} %get-tuple-element.143), channel_id=1, source_target_pairs={{0,4},{4,0},{8,12},{12,8},{1,5},{5,1},{9,13},{13,9},{2,6},{6,2},{1... | collective-permute-start | bytes 1867784 | tf_op jit(solution)/shard_map/ppermute | solution.py:798
  88.3 21.1 %collective-permute-start.14 = (bf16[672,768]{1,0:T(8,128)(2,1)}, bf16[672,768]{1,0:T(8,128)(2,1)}, u32[]{:S(2)}, u32[]{:S(2)}) collective-permute-start(bf16[672,768]{1,0:T(8,128)(2,1)} %get-tuple-element.155.refs_5_), channel_id=1, source_target_pairs={{0,16},{16,0},{1,17},{17,1},{2,18},{18,2},{3,19},{19,3},{4,20},{20... | collective-permute-start | bytes 3096584 | tf_op jit(solution)/shard_map/ppermute | solution.py:798
  96.9 12.5 %collective-permute-start.13 = (f32[2,384,256]{2,1,0:T(8,128)}, f32[2,384,256]{2,1,0:T(8,128)}, u32[]{:S(2)}, u32[]{:S(2)}) collective-permute-start(f32[2,384,256]{2,1,0:T(8,128)} %get-tuple-element.154), channel_id=1, source_target_pairs={{0,16},{16,0},{1,17},{17,1},{2,18},{18,2},{3,19},{19,3},{4,20},{20... | collective-permute-start | bytes 2359304 | tf_op jit(solution)/shard_map/ppermute | solution.py:798
  97.5 12.0 %all-to-all-start.3 = ((f32[32,1,1024]{2,1,0:T(1,128)}), f32[32,1,1024]{2,1,0:T(1,128)S(1)}, u32[]{:S(2)}, u32[]{:S(2)}) async-start(f32[32,1,1024]{2,1,0:T(1,128)} %get-tuple-element.156), calls=%async_computation.3 | async-start | bytes 262144 | tf_op jit(solution)/shard_map/all_to_all | solution.py:789
  107.5 8.8 %collective-permute-start.11 = (bf16[19,32,256]{2,1,0:T(8,128)(2,1)}, bf16[19,32,256]{2,1,0:T(8,128)(2,1)S(1)}, u32[]{:S(2)}, u32[]{:S(2)}) collective-permute-start(bf16[19,32,256]{2,1,0:T(8,128)(2,1)} %get-tuple-element.151), channel_id=1, source_target_pairs={{0,8},{4,12},{8,0},{12,4},{1,9},{5,13},{9,1},{13,5},{2,10},{6,14},... | collective-permute-start | bytes 933896 | tf_op jit(solution)/shard_map/ppermute | solution.py:798
  108.5 8.2 %collective-permute-start.12 = (bf16[19,32,256]{2,1,0:T(8,128)(2,1)}, bf16[19,32,256]{2,1,0:T(8,128)(2,1)}, u32[]{:S(2)}, u32[]{:S(2)}) collective-permute-start(bf16[19,32,256]{2,1,0:T(8,128)(2,1)} %get-tuple-element.152), channel_id=1, source_target_pairs={{0,4},{4,0},{8,12},{12,8},{1,5},{5,1},{9,13},{13,9},{2,6},{6,2},{1... | collective-permute-start | bytes 933896 | tf_op jit(solution)/shard_map/ppermute | solution.py:798
  118.4 10.4 %collective-permute-start.15 = (bf16[38,16,256]{2,1,0:T(8,128)(2,1)S(1)}, bf16[38,16,256]{2,1,0:T(8,128)(2,1)S(1)}, u32[]{:S(2)}, u32[]{:S(2)}) collective-permute-start(bf16[38,16,256]{2,1,0:T(8,128)(2,1)S(1)} %select_convert_fusion), channel_id=1, source_target_pairs={{0,1},{1,0},{2,3},{3,2},{4,5},{5,4},{6,7},{7,6},{8,9},{9,8},{10,11... | collective-permute-start | bytes 933896 | tf_op jit(solution)/shard_map/ppermute | solution.py:798
  120.0 8.4 %collective-permute-start.16 = (bf16[9,64,256]{2,1,0:T(8,128)(2,1)S(1)}, bf16[9,64,256]{2,1,0:T(8,128)(2,1)S(1)}, u32[]{:S(2)}, u32[]{:S(2)}) collective-permute-start(bf16[9,64,256]{2,1,0:T(8,128)(2,1)S(1)} %get-tuple-element.164), channel_id=1, source_target_pairs={{0,4},{4,0},{8,12},{12,8},{1,5},{5,1},{9,13},{13,9},{2,6},{6,2},{1... | collective-permute-start | bytes 884744 | tf_op jit(solution)/shard_map/ppermute | solution.py:798
  121.4 7.4 %collective-permute-start.17 = (bf16[9,64,256]{2,1,0:T(8,128)(2,1)S(1)}, bf16[9,64,256]{2,1,0:T(8,128)(2,1)S(1)}, u32[]{:S(2)}, u32[]{:S(2)}) collective-permute-start(bf16[9,64,256]{2,1,0:T(8,128)(2,1)S(1)} %get-tuple-element.165), channel_id=1, source_target_pairs={{0,8},{4,12},{8,0},{12,4},{1,9},{5,13},{9,1},{13,5},{2,10},{6,14},... | collective-permute-start | bytes 884744 | tf_op jit(solution)/shard_map/ppermute | solution.py:798
  128.9 5.2 %collective-permute-start.20 = (bf16[9,32,256]{2,1,0:T(8,128)(2,1)S(1)}, bf16[9,32,256]{2,1,0:T(8,128)(2,1)S(1)}, u32[]{:S(2)}, u32[]{:S(2)}) collective-permute-start(bf16[9,32,256]{2,1,0:T(8,128)(2,1)S(1)} %select_convert_fusion.3), channel_id=1, source_target_pairs={{0,4},{4,0},{8,12},{12,8},{1,5},{5,1},{9,13},{13,9},{2,6},{6,2},{1... | collective-permute-start | bytes 442376 | tf_op jit(solution)/shard_map/ppermute | solution.py:798
  130.4 7.4 %collective-permute-start.18 = (bf16[38,8,256]{2,1,0:T(8,128)(2,1)S(1)}, bf16[38,8,256]{2,1,0:T(8,128)(2,1)S(1)}, u32[]{:S(2)}, u32[]{:S(2)}) collective-permute-start(bf16[38,8,256]{2,1,0:T(8,128)(2,1)S(1)} %select_convert_fusion.1), channel_id=1, source_target_pairs={{0,2},{1,3},{2,0},{3,1},{4,6},{5,7},{6,4},{7,5},{8,10},{9,11},{10,... | collective-permute-start | bytes 466952 | tf_op jit(solution)/shard_map/ppermute | solution.py:798
  132.3 5.2 %collective-permute-start.19 = (bf16[9,32,256]{2,1,0:T(8,128)(2,1)S(1)}, bf16[9,32,256]{2,1,0:T(8,128)(2,1)S(1)}, u32[]{:S(2)}, u32[]{:S(2)}) collective-permute-start(bf16[9,32,256]{2,1,0:T(8,128)(2,1)S(1)} %select_convert_fusion.4), channel_id=1, source_target_pairs={{0,8},{4,12},{8,0},{12,4},{1,9},{5,13},{9,1},{13,5},{2,10},{6,14},... | collective-permute-start | bytes 442376 | tf_op jit(solution)/shard_map/ppermute | solution.py:798
  138.0 10.6 %collective-permute-start.21 = (bf16[38,8,256]{2,1,0:T(8,128)(2,1)S(1)}, bf16[38,8,256]{2,1,0:T(8,128)(2,1)S(1)}, u32[]{:S(2)}, u32[]{:S(2)}) collective-permute-start(bf16[38,8,256]{2,1,0:T(8,128)(2,1)S(1)} %add_convert_fusion), channel_id=1, source_target_pairs={{0,2},{1,3},{2,0},{3,1},{4,6},{5,7},{6,4},{7,5},{8,10},{9,11},{10,... | collective-permute-start | bytes 466952 | tf_op jit(solution)/shard_map/ppermute | solution.py:798
  139.1 9.6 %collective-permute-start.22 = (bf16[18,16,256]{2,1,0:T(8,128)(2,1)S(1)}, bf16[18,16,256]{2,1,0:T(8,128)(2,1)S(1)}, u32[]{:S(2)}, u32[]{:S(2)}) collective-permute-start(bf16[18,16,256]{2,1,0:T(8,128)(2,1)S(1)} %select_convert_fusion.2), channel_id=1, source_target_pairs={{0,1},{1,0},{2,3},{3,2},{4,5},{5,4},{6,7},{7,6},{8,9},{9,8},{10,11... | collective-permute-start | bytes 442376 | tf_op jit(solution)/shard_map/ppermute | solution.py:798
  148.7 8.5 %collective-permute-start.23 = (bf16[38,16,256]{2,1,0:T(8,128)(2,1)S(1)}, bf16[38,16,256]{2,1,0:T(8,128)(2,1)S(1)}, u32[]{:S(2)}, u32[]{:S(2)}) collective-permute-start(bf16[38,16,256]{2,1,0:T(8,128)(2,1)S(1)} %pad_maximum_fusion.5), channel_id=1, source_target_pairs={{0,1},{1,0},{2,3},{3,2},{4,5},{5,4},{6,7},{7,6},{8,9},{9,8},{10,11... | collective-permute-start | bytes 933896 | tf_op jit(solution)/shard_map/ppermute | solution.py:798
  150.1 5.9 %collective-permute-start.24 = (bf16[18,8,256]{2,1,0:T(8,128)(2,1)S(1)}, bf16[18,8,256]{2,1,0:T(8,128)(2,1)S(1)}, u32[]{:S(2)}, u32[]{:S(2)}) collective-permute-start(bf16[18,8,256]{2,1,0:T(8,128)(2,1)S(1)} %select_convert_fusion.5), channel_id=1, source_target_pairs={{0,2},{1,3},{2,0},{3,1},{4,6},{5,7},{6,4},{7,5},{8,10},{9,11},{10,... | collective-permute-start | bytes 221192 | tf_op jit(solution)/shard_map/ppermute | solution.py:798
  157.5 10.3 %collective-permute-start.25 = (bf16[19,32,256]{2,1,0:T(8,128)(2,1)S(1)}, bf16[19,32,256]{2,1,0:T(8,128)(2,1)S(1)}, u32[]{:S(2)}, u32[]{:S(2)}) collective-permute-start(bf16[19,32,256]{2,1,0:T(8,128)(2,1)S(1)} %get-tuple-element.212), channel_id=1, source_target_pairs={{0,8},{4,12},{8,0},{12,4},{1,9},{5,13},{9,1},{13,5},{2,10},{6,14},... | collective-permute-start | bytes 933896 | tf_op jit(solution)/shard_map/ppermute | solution.py:798
  158.5 10.1 %collective-permute-start.26 = (bf16[19,32,256]{2,1,0:T(8,128)(2,1)S(1)}, bf16[19,32,256]{2,1,0:T(8,128)(2,1)S(1)}, u32[]{:S(2)}, u32[]{:S(2)}) collective-permute-start(bf16[19,32,256]{2,1,0:T(8,128)(2,1)S(1)} %get-tuple-element.211), channel_id=1, source_target_pairs={{0,4},{4,0},{8,12},{12,8},{1,5},{5,1},{9,13},{13,9},{2,6},{6,2},{1... | collective-permute-start | bytes 933896 | tf_op jit(solution)/shard_map/ppermute | solution.py:798
  160.1 5.3 %collective-permute-start.27 = (bf16[18,8,256]{2,1,0:T(8,128)(2,1)S(1)}, bf16[18,8,256]{2,1,0:T(8,128)(2,1)S(1)}, u32[]{:S(2)}, u32[]{:S(2)}) collective-permute-start(bf16[18,8,256]{2,1,0:T(8,128)(2,1)S(1)} %add_convert_fusion.1), channel_id=1, source_target_pairs={{0,2},{1,3},{2,0},{3,1},{4,6},{5,7},{6,4},{7,5},{8,10},{9,11},{10,... | collective-permute-start | bytes 221192 | tf_op jit(solution)/shard_map/ppermute | solution.py:798
  168.7 15.4 %collective-permute-start.32 = (bf16[19,64,256]{2,1,0:T(8,128)(2,1)S(1)}, bf16[19,64,256]{2,1,0:T(8,128)(2,1)S(1)}, u32[]{:S(2)}, u32[]{:S(2)}) collective-permute-start(bf16[19,64,256]{2,1,0:T(8,128)(2,1)S(1)} %pad_maximum_fusion.3), channel_id=1, source_target_pairs={{0,8},{4,12},{8,0},{12,4},{1,9},{5,13},{9,1},{13,5},{2,10},{6,14},... | collective-permute-start | bytes 1867784 | tf_op jit(solution)/shard_map/ppermute | solution.py:798
  169.3 6.1 %collective-permute-start.28 = (bf16[18,16,256]{2,1,0:T(8,128)(2,1)S(1)}, bf16[18,16,256]{2,1,0:T(8,128)(2,1)S(1)}, u32[]{:S(2)}, u32[]{:S(2)}) collective-permute-start(bf16[18,16,256]{2,1,0:T(8,128)(2,1)S(1)} %pad_maximum_fusion.10), channel_id=1, source_target_pairs={{0,1},{1,0},{2,3},{3,2},{4,5},{5,4},{6,7},{7,6},{8,9},{9,8},{10,11... | collective-permute-start | bytes 442376 | tf_op jit(solution)/shard_map/ppermute | solution.py:798
  172.3 11.9 %collective-permute-start.31 = (bf16[19,64,256]{2,1,0:T(8,128)(2,1)S(1)}, bf16[19,64,256]{2,1,0:T(8,128)(2,1)S(1)}, u32[]{:S(2)}, u32[]{:S(2)}) collective-permute-start(bf16[19,64,256]{2,1,0:T(8,128)(2,1)S(1)} %pad_maximum_fusion.2), channel_id=1, source_target_pairs={{0,4},{4,0},{8,12},{12,8},{1,5},{5,1},{9,13},{13,9},{2,6},{6,2},{1... | collective-permute-start | bytes 1867784 | tf_op jit(solution)/shard_map/ppermute | solution.py:798
  175.5 5.2 %collective-permute-start.29 = (bf16[9,32,256]{2,1,0:T(8,128)(2,1)S(1)}, bf16[9,32,256]{2,1,0:T(8,128)(2,1)S(1)}, u32[]{:S(2)}, u32[]{:S(2)}) collective-permute-start(bf16[9,32,256]{2,1,0:T(8,128)(2,1)S(1)} %get-tuple-element.222), channel_id=1, source_target_pairs={{0,8},{4,12},{8,0},{12,4},{1,9},{5,13},{9,1},{13,5},{2,10},{6,14},... | collective-permute-start | bytes 442376 | tf_op jit(solution)/shard_map/ppermute | solution.py:798
  176.3 7.9 %collective-permute-start.30 = (bf16[9,32,256]{2,1,0:T(8,128)(2,1)S(1)}, bf16[9,32,256]{2,1,0:T(8,128)(2,1)S(1)}, u32[]{:S(2)}, u32[]{:S(2)}) collective-permute-start(bf16[9,32,256]{2,1,0:T(8,128)(2,1)S(1)} %get-tuple-element.221), channel_id=1, source_target_pairs={{0,4},{4,0},{8,12},{12,8},{1,5},{5,1},{9,13},{13,9},{2,6},{6,2},{1... | collective-permute-start | bytes 442376 | tf_op jit(solution)/shard_map/ppermute | solution.py:798
  185.3 5.8 %collective-permute-start.35 = (bf16[19,256,256]{2,1,0:T(8,128)(2,1)S(1)}, bf16[19,256,256]{2,1,0:T(8,128)(2,1)}, u32[]{:S(2)}, u32[]{:S(2)}) collective-permute-start(bf16[19,256,256]{2,1,0:T(8,128)(2,1)S(1)} %pad_maximum_fusion.half_ref), channel_id=1, source_target_pairs={{0,16},{16,0},{1,17},{17,1},{2,18},{18,2},{3,19},{19,3},{4,20},{20... | collective-permute-start | bytes 7471112 | tf_op jit(solution)/shard_map/ppermute | solution.py:798
  185.4 9.5 %collective-permute-start.34 = (bf16[9,64,256]{2,1,0:T(8,128)(2,1)S(1)}, bf16[9,64,256]{2,1,0:T(8,128)(2,1)S(1)}, u32[]{:S(2)}, u32[]{:S(2)}) collective-permute-start(bf16[9,64,256]{2,1,0:T(8,128)(2,1)S(1)} %pad_maximum_fusion.8.refs_2_), channel_id=1, source_target_pairs={{0,8},{4,12},{8,0},{12,4},{1,9},{5,13},{9,1},{13,5},{2,10},{6,14},... | collective-permute-start | bytes 884744 | tf_op jit(solution)/shard_map/ppermute | solution.py:798
  186.1 9.6 %collective-permute-start.33 = (bf16[9,64,256]{2,1,0:T(8,128)(2,1)S(1)}, bf16[9,64,256]{2,1,0:T(8,128)(2,1)}, u32[]{:S(2)}, u32[]{:S(2)}) collective-permute-start(bf16[9,64,256]{2,1,0:T(8,128)(2,1)S(1)} %pad_maximum_fusion.7.refs_0_), channel_id=1, source_target_pairs={{0,4},{4,0},{8,12},{12,8},{1,5},{5,1},{9,13},{13,9},{2,6},{6,2},{1... | collective-permute-start | bytes 884744 | tf_op jit(solution)/shard_map/ppermute | solution.py:798
  197.2 3.2 %collective-permute-start.36 = (bf16[9,256,256]{2,1,0:T(8,128)(2,1)S(1)}, bf16[9,256,256]{2,1,0:T(8,128)(2,1)S(1)}, u32[]{:S(2)}, u32[]{:S(2)}) collective-permute-start(bf16[9,256,256]{2,1,0:T(8,128)(2,1)S(1)} %shard_map.216.half_ref), channel_id=1, source_target_pairs={{0,16},{16,0},{1,17},{17,1},{2,18},{18,2},{3,19},{19,3},{4,20},{20... | collective-permute-start | bytes 3538952 | tf_op jit(solution)/shard_map/ppermute | solution.py:798
  (14 other events, 94.2 us)

commit v13 on v12

--- a/solution.py
+++ b/solution.py
@@ -1197,7 +1197,7 @@
     grad_w2, grad_wp = grad_second
     tree1.finish(1)
     tree1.start()
-    (grad_w1,) = widen(tree1.got[0], 1 - side, 9, 1, False, widen(tree1.value, side, 9, 1, False))
+    (grad_w1,) = widen(tree1.got[0], 1 - side, 1, 9, False, widen(tree1.value, side, 1, 9, False))
 
     return (
         third[N.out],

time: 204 us -> 203 us (level)
  Pallas kernels: 71 us -> 68.5 us
    pallas_call x4, Pallas kernels: 12.4 us -> 9.82 us  [widen(): pl.pallas_call(body, out_shape=[shape((taps * per, n, 2 * m))] + [shape((...]
  transfers between devices with their start and end apart: 41 -> 41, of which waited for: 26 -> 27; matrix products, arithmetic and copies ran while one was open for 0% -> 0% of each run, Pallas kernels for 22% -> 21%
where the time goes in v13:
time: 203 us; the launch traced here: 202 us
  Pallas kernels  68.5 us (34%)
  starting transfers between devices  65.8 us (32%)
  waiting for transfers between devices  58.6 us (29%)
  other arithmetic  5.1 us (3%)
  local copies, waits for them, and re-layouts  2.62 us (1%)
    pallas_call x11, Pallas kernels, call(): pl.pallas_call(run, out_shape=list(outs.values()), in_specs=[spec(n) for...  57.1 us
    ppermute x32, starting transfers between devices, partner(): return lax.ppermute(value, axis, [(i, i ^ step) for i in range(count)])  36.3 us
    ppermute x32, waiting for transfers between devices, partner(): return lax.ppermute(value, axis, [(i, i ^ step) for i in range(count)])  34.9 us
    all_to_all x4, waiting for transfers between devices, gather_sum(): return lax.all_to_all(spread, axes, 0, 0)  21.2 us
    all_to_all x4, starting transfers between devices, gather_sum(): return lax.all_to_all(spread, axes, 0, 0)  16.6 us
    ppermute x4, starting transfers between devices, shifted(): lax.ppermute(value, axis, [(source, source + steps) for source in range(f...  12.3 us
    pallas_call x4, Pallas kernels, widen(): pl.pallas_call(body, out_shape=[shape((taps * per, n, 2 * m))] + [shape((...  9.82 us
  transfers between devices with their start and end apart: 41, of which 27 were waited for; matrix products, arithmetic and copies ran while one was open for 0% of the time, Pallas kernels for 21%

profile of v13, /device:TPU:0, one launch (start us, length us, event | category | flops | bytes accessed | tf_op | source)
XLA Modules:
  0.0 202.1 jit_solution(5308701873193743761)
XLA Ops:
  5.1 2.0 collective-permute-start.1
  9.2 4.8 %collective-permute-start.2 = (bf16[2,17,1,256]{3,2,1,0:T(2,128)(2,1)S(1)}, bf16[2,17,1,256]{3,2,1,0:T(2,128)(2,1)S(1)}, u32[]{:S(2)}, u32[]{:S(2)}) collective-permute-start(bf16[2,17,1,256]{3,2,1,0:T(2,128)(2,1)S(1)} %pad_maximum_fusion.11), channel_id=1, source_target_pairs={{0,4},{4,8},{8,12},{1,5},{5,9},{9,13},{2,6},{6,10},{10,14},{3,7},{... | collective-permute-start | bytes 52232 | tf_op jit(solution)/shard_map/ppermute | solution.py:785
  14.1 1.6 collective-permute-done.2.refs_2_
  15.7 4.2 %collective-permute-start.3 = (bf16[480,256]{1,0:T(8,128)(2,1)S(1)}, bf16[480,256]{1,0:T(8,128)(2,1)S(1)}, u32[]{:S(2)}, u32[]{:S(2)}) collective-permute-start(bf16[480,256]{1,0:T(8,128)(2,1)S(1)} %get-tuple-element.115), channel_id=1, source_target_pairs={{0,4},{4,8},{8,12},{1,5},{5,9},{9,13},{2,6},{6,10},{10,14},{3,7},{... | collective-permute-start | bytes 737288 | tf_op jit(solution)/shard_map/ppermute | solution.py:785
  21.2 3.3 %shard_map.206 = f32[32,1,2176]{2,1,0:T(1,128)} custom-call(bf16[2,16,32,256]{3,2,1,0:T(8,128)(2,1)S(1)} %copy-done.1, bf16[2,1,32,256]{3,2,1,0:T(8,128)(2,1)S(1)} %collective-permute-done.1.refs_1_, bf16[2,17,1,256]{3,2,1,0:T(2,128)(2,1)S(1)} %collective-permute-done.2.refs_2_, bf16[2,8,16,128]{3,2,1,0:T(8,128)(2,1)S(1)} %broadcast_in_dim.2.refs_3_, ...), custom_call_target="tpu_custom_call" | custom-call | tf_op jit(solution)/shard_map/pallas_call | solution.py:113
  24.6 7.9 %all-to-all-start = ((f32[32,1,2176]{2,1,0:T(1,128)}), f32[32,1,2176]{2,1,0:T(1,128)S(1)}, u32[]{:S(2)}, u32[]{:S(2)}) async-start(f32[32,1,2176]{2,1,0:T(1,128)} %shard_map.206), calls=%async_computation | async-start | bytes 557056 | tf_op jit(solution)/shard_map/all_to_all | solution.py:789
  32.6 5.7 %shard_map.205 = (f32[624,512]{1,0:T(8,128)}, f32[624,512]{1,0:T(8,128)}, bf16[624,768]{1,0:T(8,128)(2,1)}, bf16[672,768]{1,0:T(8,128)(2,1)}, f32[624,128]{1,0:T...) custom-call(s32[2]{0:T(128)S(1)} %add_convert_fusion.2.refs_0_, bf16[2,16,32,256]{3,2,1,0:T(8,128)(2,1)} %refs_0_.1, ...), custom_call_target="tpu_custom_call" | custom-call | flops 20000000000 | tf_op jit(solution)/shard_map/pallas_call | solution.py:113
  38.3 5.5 %all-to-all-done.refs_1_ = f32[32,1,2176]{2,1,0:T(1,128)S(1)} async-done(((f32[32,1,2176]{2,1,0:T(1,128)}), f32[32,1,2176]{2,1,0:T(1,128)S(1)}, u32[]{:S(2)}, u32[]{:S(2)}) %all-to-all-start) | async-done | bytes 278560 | tf_op jit(solution)/shard_map/all_to_all | solution.py:789
  43.8 6.3 %shard_map.207 = (bf16[624,1536]{1,0:T(8,128)(2,1)}, f32[528,512]{1,0:T(8,128)}, f32[32,1,1024]{2,1,0:T(1,128)}, f32[8,512]{1,0:T(8,128)S(1)}) custom-call(f32[624,512]{1,0:T(8,128)} %get-tuple-element.117.refs_0_.refs_3_, f32[32,1,2176]{2,1,0:T(1,128)S(1)} %all-to-all-done.refs_1_, f32[1,512]{1,0:T(1,128)S(1)} %bitcast.36, f32[1,512]{1,0:T(1,128)S(1)} %bitcast.34, ...), custom_call_target="tpu_custom_call" | custom-call | tf_op jit(solution)/shard_map/pallas_call | solution.py:113
  50.1 2.6 %all-to-all-start.1 = ((f32[32,1,1024]{2,1,0:T(1,128)}), f32[32,1,1024]{2,1,0:T(1,128)S(1)}, u32[]{:S(2)}, u32[]{:S(2)}) async-start(f32[32,1,1024]{2,1,0:T(1,128)} %get-tuple-element.124), calls=%async_computation.1 | async-start | bytes 262144 | tf_op jit(solution)/shard_map/all_to_all | solution.py:789
  52.9 7.7 %all-to-all-done.1.refs_4_ = f32[32,1,1024]{2,1,0:T(1,128)S(1)} async-done(((f32[32,1,1024]{2,1,0:T(1,128)}), f32[32,1,1024]{2,1,0:T(1,128)S(1)}, u32[]{:S(2)}, u32[]{:S(2)}) %all-to-all-start.1) | async-done | bytes 131104 | tf_op jit(solution)/shard_map/all_to_all | solution.py:789
  60.7 5.5 %shard_map.208 = (bf16[2,8,16,512]{3,2,1,0:T(8,128)(2,1)}, f32[528,512]{1,0:T(8,128)}, f32[32,1,1536]{2,1,0:T(1,128)}, f32[8,512]{1,0:T(8,128)S(1)}, f32[3,384,256]{2,1,0:T(8,128)}, /*index=5*/f32[3,384,256]{2,1,0:T(8,128)}) custom-call(s32[5]{0:T(128)S(1)} %stack.44.refs_0_, f32[528,512]{1,0:T(8,128)} %get-tuple-element.121.refs_1_.refs_2_, ...), custom_call_target="tpu_custom_call" | custom-call | tf_op jit(solution)/shard_map/pallas_call | solution.py:113
  66.8 2.8 %all-to-all-start.2 = ((f32[32,1,1536]{2,1,0:T(1,128)}), f32[32,1,1536]{2,1,0:T(1,128)S(1)}, u32[]{:S(2)}, u32[]{:S(2)}) async-start(f32[32,1,1536]{2,1,0:T(1,128)} %get-tuple-element.135), calls=%async_computation.2 | async-start | bytes 393216 | tf_op jit(solution)/shard_map/all_to_all | solution.py:789
  70.8 8.0 %all-to-all-done.2.refs_7_.refs_8_ = f32[32,1,1536]{2,1,0:T(1,128)S(1)} async-done(((f32[32,1,1536]{2,1,0:T(1,128)}), f32[32,1,1536]{2,1,0:T(1,128)S(1)}, u32[]{:S(2)}, u32[]{:S(2)}) %all-to-all-start.2) | async-done | bytes 196640 | tf_op jit(solution)/shard_map/all_to_all | solution.py:789
  78.8 8.4 %shard_map.209 = (bf16[19,64,256]{2,1,0:T(8,128)(2,1)S(1)}, f32[19,64,256]{2,1,0:T(8,128)}, bf16[19,64,256]{2,1,0:T(8,128)(2,1)}, f32[19,64,256]{2,1,0:T(8,128)}) custom-call(s32[5]{0:T(128)S(1)} %stack.44.refs_0_, f32[3,384,256]{2,1,0:T(8,128)} %get-tuple-element.130.refs_1_, f32[3,384,256]{2,1,0:T(8,128)} %copy-done.18, ...), custom_call_target="tpu_custom_call" | custom-call | tf_op jit(solution)/shard_map/pallas_call | solution.py:113
  88.3 8.6 %shard_map.211 = (f32[432,512]{1,0:T(8,128)}, f32[432,512]{1,0:T(8,128)}, f32[32,1,1024]{2,1,0:T(1,128)}, f32[2,384,256]{2,1,0:T(8,128)}, f32[2,384,256]{2,1,0:T...) custom-call(s32[5]{0:T(128)S(1)} %stack.44.refs_0_, ...), custom_call_target="tpu_custom_call" | custom-call | tf_op jit(solution)/shard_map/pallas_call | solution.py:113
  97.5 3.4 %all-to-all-start.3 = ((f32[32,1,1024]{2,1,0:T(1,128)}), f32[32,1,1024]{2,1,0:T(1,128)S(1)}, u32[]{:S(2)}, u32[]{:S(2)}) async-start(f32[32,1,1024]{2,1,0:T(1,128)} %get-tuple-element.156), calls=%async_computation.3 | async-start | bytes 262144 | tf_op jit(solution)/shard_map/all_to_all | solution.py:789
  100.9 1.9 collective-permute-done.10.refs_4_
  103.7 3.8 %shard_map.210 = (bf16[19,32,256]{2,1,0:T(8,128)(2,1)}, f32[19,32,256]{2,1,0:T(8,128)}, bf16[19,32,256]{2,1,0:T(8,128)(2,1)}, f32[19,32,256]{2,1,0:T(8,128)}) custom-call(s32[5]{0:T(128)} %copy-done.10, f32[19,64,256]{2,1,0:T(8,128)} %get-tuple-element.142.refs_1_, bf16[19,64,256]{2,1,0:T(8,128)(2,1)} %collective-permute-done.9.refs_2_, ...), custom_call_target="tpu_custom_call" | custom-call | flops 20000000000 | tf_op jit(solution)/shard_map/pallas_call | solution.py:113
  109.4 6.9 %shard_map.212 = (bf16[9,64,256]{2,1,0:T(8,128)(2,1)S(1)}, f32[9,64,256]{2,1,0:T(8,128)S(1)}, bf16[9,64,256]{2,1,0:T(8,128)(2,1)S(1)}, f32[9,64,256]{2,1,0:T(8,1...) custom-call(s32[5]{0:T(128)S(1)} %copy-done.11, f32[2,384,256]{2,1,0:T(8,128)} %get-tuple-element.153.refs_1_, ...), custom_call_target="tpu_custom_call" | custom-call | flops 20000000000 | tf_op jit(solution)/shard_map/pallas_call | solution.py:113
  116.7 1.5 convert_add_fusion.1
  118.4 1.5 collective-permute-start.15
  120.0 1.5 collective-permute-start.16
  122.0 6.4 %shard_map.213 = bf16[2,16,32,256]{3,2,1,0:T(8,128)(2,1)} custom-call(f32[432,512]{1,0:T(8,128)S(1)} %copy-done.14, f32[432,512]{1,0:T(8,128)} %get-tuple-element.167.refs_1_, bf16[384,512]{1,0:T(8,128)(2,1)S(1)} %get-tuple-element.168.refs_2_, bf16[3,768,512]{2,1,0:T(8,128)(2,1)} %bitcast.50, bf16[256,512]{1,0:T(8,128)(2,1)S(1)} %copy-done.5, ...), custom_call_target="tpu_custom_call" | custom-call | flops 10000000000 | tf_op jit(solution)/shard_map/pallas_call | solution.py:113
  128.9 1.3 collective-permute-start.20
  130.4 1.8 collective-permute-start.18
  134.1 3.5 %collective-permute-done.19 = bf16[9,32,256]{2,1,0:T(8,128)(2,1)S(1)} collective-permute-done((bf16[9,32,256]{2,1,0:T(8,128)(2,1)S(1)}, bf16[9,32,256]{2,1,0:T(8,128)(2,1)S(1)}, u32[]{:S(2)}, u32[]{:S(2)}) %collective-permute-start.19) | collective-permute-done | bytes 147488 | tf_op jit(solution)/shard_map/ppermute | solution.py:798
  139.1 4.1 %collective-permute-start.22 = (bf16[18,16,256]{2,1,0:T(8,128)(2,1)S(1)}, bf16[18,16,256]{2,1,0:T(8,128)(2,1)S(1)}, u32[]{:S(2)}, u32[]{:S(2)}) collective-permute-start(bf16[18,16,256]{2,1,0:T(8,128)(2,1)S(1)} %select_convert_fusion.2), channel_id=1, source_target_pairs={{0,1},{1,0},{2,3},{3,2},{4,5},{5,4},{6,7},{7,6},{8,9},{9,8},{10,11... | collective-permute-start | bytes 442376 | tf_op jit(solution)/shard_map/ppermute | solution.py:798
  143.1 5.5 %collective-permute-done.22 = bf16[18,16,256]{2,1,0:T(8,128)(2,1)S(1)} collective-permute-done((bf16[18,16,256]{2,1,0:T(8,128)(2,1)S(1)}, bf16[18,16,256]{2,1,0:T(8,128)(2,1)S(1)}, u32[]{:S(2)}, u32[]{:S(2)}) %collective-permute-start.22) | collective-permute-done | bytes 147488 | tf_op jit(solution)/shard_map/ppermute | solution.py:798
  148.7 1.4 collective-permute-start.23
  150.1 2.5 %collective-permute-start.24 = (bf16[18,8,256]{2,1,0:T(8,128)(2,1)S(1)}, bf16[18,8,256]{2,1,0:T(8,128)(2,1)S(1)}, u32[]{:S(2)}, u32[]{:S(2)}) collective-permute-start(bf16[18,8,256]{2,1,0:T(8,128)(2,1)S(1)} %select_convert_fusion.5), channel_id=1, source_target_pairs={{0,2},{1,3},{2,0},{3,1},{4,6},{5,7},{6,4},{7,5},{8,10},{9,11},{10,... | collective-permute-start | bytes 221192 | tf_op jit(solution)/shard_map/ppermute | solution.py:798
  152.6 3.4 %collective-permute-done.24 = bf16[18,8,256]{2,1,0:T(8,128)(2,1)S(1)} collective-permute-done((bf16[18,8,256]{2,1,0:T(8,128)(2,1)S(1)}, bf16[18,8,256]{2,1,0:T(8,128)(2,1)S(1)}, u32[]{:S(2)}, u32[]{:S(2)}) %collective-permute-start.24) | collective-permute-done | bytes 73760 | tf_op jit(solution)/shard_map/ppermute | solution.py:798
  158.5 1.5 collective-permute-start.26
  160.1 2.3 %collective-permute-start.27 = (bf16[18,8,256]{2,1,0:T(8,128)(2,1)S(1)}, bf16[18,8,256]{2,1,0:T(8,128)(2,1)S(1)}, u32[]{:S(2)}, u32[]{:S(2)}) collective-permute-start(bf16[18,8,256]{2,1,0:T(8,128)(2,1)S(1)} %add_convert_fusion.1), channel_id=1, source_target_pairs={{0,2},{1,3},{2,0},{3,1},{4,6},{5,7},{6,4},{7,5},{8,10},{9,11},{10,... | collective-permute-start | bytes 221192 | tf_op jit(solution)/shard_map/ppermute | solution.py:798
  162.4 3.0 %collective-permute-done.27 = bf16[18,8,256]{2,1,0:T(8,128)(2,1)S(1)} collective-permute-done((bf16[18,8,256]{2,1,0:T(8,128)(2,1)S(1)}, bf16[18,8,256]{2,1,0:T(8,128)(2,1)S(1)}, u32[]{:S(2)}, u32[]{:S(2)}) %collective-permute-start.27) | collective-permute-done | bytes 73760 | tf_op jit(solution)/shard_map/ppermute | solution.py:798
  165.4 2.4 %collective-permute-done.25 = bf16[19,32,256]{2,1,0:T(8,128)(2,1)S(1)} collective-permute-done((bf16[19,32,256]{2,1,0:T(8,128)(2,1)S(1)}, bf16[19,32,256]{2,1,0:T(8,128)(2,1)S(1)}, u32[]{:S(2)}, u32[]{:S(2)}) %collective-permute-start.25) | collective-permute-done | bytes 311328 | tf_op jit(solution)/shard_map/ppermute | solution.py:798
  169.3 3.0 %collective-permute-start.28 = (bf16[18,16,256]{2,1,0:T(8,128)(2,1)S(1)}, bf16[18,16,256]{2,1,0:T(8,128)(2,1)S(1)}, u32[]{:S(2)}, u32[]{:S(2)}) collective-permute-start(bf16[18,16,256]{2,1,0:T(8,128)(2,1)S(1)} %pad_maximum_fusion.10), channel_id=1, source_target_pairs={{0,1},{1,0},{2,3},{3,2},{4,5},{5,4},{6,7},{7,6},{8,9},{9,8},{10,11... | collective-permute-start | bytes 442376 | tf_op jit(solution)/shard_map/ppermute | solution.py:798
  172.3 1.5 collective-permute-start.31
  173.8 1.6 collective-permute-done.28
  176.3 1.8 collective-permute-start.30
  178.1 2.6 %collective-permute-done.29 = bf16[9,32,256]{2,1,0:T(8,128)(2,1)S(1)} collective-permute-done((bf16[9,32,256]{2,1,0:T(8,128)(2,1)S(1)}, bf16[9,32,256]{2,1,0:T(8,128)(2,1)S(1)}, u32[]{:S(2)}, u32[]{:S(2)}) %collective-permute-start.29) | collective-permute-done | bytes 147488 | tf_op jit(solution)/shard_map/ppermute | solution.py:798
  180.7 3.5 %collective-permute-done.30 = bf16[9,32,256]{2,1,0:T(8,128)(2,1)S(1)} collective-permute-done((bf16[9,32,256]{2,1,0:T(8,128)(2,1)S(1)}, bf16[9,32,256]{2,1,0:T(8,128)(2,1)S(1)}, u32[]{:S(2)}, u32[]{:S(2)}) %collective-permute-start.30) | collective-permute-done | bytes 147488 | tf_op jit(solution)/shard_map/ppermute | solution.py:798
  186.1 2.1 %collective-permute-start.33 = (bf16[9,64,256]{2,1,0:T(8,128)(2,1)S(1)}, bf16[9,64,256]{2,1,0:T(8,128)(2,1)}, u32[]{:S(2)}, u32[]{:S(2)}) collective-permute-start(bf16[9,64,256]{2,1,0:T(8,128)(2,1)S(1)} %pad_maximum_fusion.7.refs_0_), channel_id=1, source_target_pairs={{0,4},{4,0},{8,12},{12,8},{1,5},{5,1},{9,13},{13,9},{2,6},{6,2},{1... | collective-permute-start | bytes 884744 | tf_op jit(solution)/shard_map/ppermute | solution.py:798
  188.2 2.8 %shard_map.214 = (f32[18,256,512]{2,1,0:T(8,128)}, f32[1,256,512]{2,1,0:T(8,128)}) custom-call(s32[1]{0:T(128)} %bitcast.side_ref, bf16[19,256,256]{2,1,0:T(8,128)(2,1)S(1)} %pad_maximum_fusion.half_ref), custom_call_target="tpu_custom_call" | custom-call | tf_op jit(solution)/shard_map/pallas_call | solution.py:730
  191.0 3.4 %shard_map.215 = (f32[18,256,512]{2,1,0:T(8,128)}, f32[1,256,512]{2,1,0:T(8,128)}) custom-call(s32[1]{0:T(128)} %bitcast.15.side_ref, bf16[19,256,256]{2,1,0:T(8,128)(2,1)} %collective-permute-done.35.half_ref, f32[18,256,512]{2,1,0:T(8,128)} %get-tuple-element.191.refs_0_, ...), custom_call_target="tpu_custom_call", output_to_operand_aliasing={{0}: (2, {}), {1}: (3, {})} | custom-call | tf_op jit(solution)/shard_map/pallas_call | solution.py:730
  195.6 1.6 shard_map.216.half_ref
  197.3 1.8 shard_map.217.refs_0_
  200.1 1.8 shard_map.218
  (135 shorter events, 28.8 us)
Async XLA Ops:
  3.5 17.7 %copy-start.1 = (bf16[2,16,32,256]{3,2,1,0:T(8,128)(2,1)S(1)}, bf16[2,16,32,256]{3,2,1,0:T(8,128)(2,1)}, u32[]{:S(2)}) copy-start(bf16[2,16,32,256]{3,2,1,0:T(8,128)(2,1)} %refs_0_.1) | copy-start | bytes 1572868
  3.5 17.7 %copy-start.5 = (bf16[256,512]{1,0:T(8,128)(2,1)S(1)}, bf16[256,512]{1,0:T(8,128)(2,1)}, u32[]{:S(2)}) copy-start(bf16[256,512]{1,0:T(8,128)(2,1)} %refs_4_.1) | copy-start | bytes 786436
  4.5 3.3 %collective-permute-start = (bf16[672,256]{1,0:T(8,128)(2,1)S(1)}, bf16[672,256]{1,0:T(8,128)(2,1)S(1)}, u32[]{:S(2)}, u32[]{:S(2)}) collective-permute-start(bf16[672,256]{1,0:T(8,128)(2,1)S(1)} %shard_map.203), channel_id=1, source_target_pairs={{0,16},{16,0},{1,17},{17,1},{2,18},{18,2},{3,19},{19,3},{4,20},{20... | collective-permute-start | bytes 1032200 | tf_op jit(solution)/shard_map/ppermute | solution.py:959
  5.1 2.8 %collective-permute-start.1 = (bf16[2,1,32,256]{3,2,1,0:T(8,128)(2,1)S(1)}, bf16[2,1,32,256]{3,2,1,0:T(8,128)(2,1)S(1)}, u32[]{:S(2)}, u32[]{:S(2)}) collective-permute-start(bf16[2,1,32,256]{3,2,1,0:T(8,128)(2,1)S(1)} %slice.57), channel_id=1, source_target_pairs={{0,16},{1,17},{2,18},{3,19},{4,20},{5,21},{6,22},{7,23},{8,24},{9,... | collective-permute-start | bytes 98312 | tf_op jit(solution)/shard_map/ppermute | solution.py:785
  9.2 6.4 %collective-permute-start.2 = (bf16[2,17,1,256]{3,2,1,0:T(2,128)(2,1)S(1)}, bf16[2,17,1,256]{3,2,1,0:T(2,128)(2,1)S(1)}, u32[]{:S(2)}, u32[]{:S(2)}) collective-permute-start(bf16[2,17,1,256]{3,2,1,0:T(2,128)(2,1)S(1)} %pad_maximum_fusion.11), channel_id=1, source_target_pairs={{0,4},{4,8},{8,12},{1,5},{5,9},{9,13},{2,6},{6,10},{10,14},{3,7},{... | collective-permute-start | bytes 52232 | tf_op jit(solution)/shard_map/ppermute | solution.py:785
  15.7 16.8 %collective-permute-start.3 = (bf16[480,256]{1,0:T(8,128)(2,1)S(1)}, bf16[480,256]{1,0:T(8,128)(2,1)S(1)}, u32[]{:S(2)}, u32[]{:S(2)}) collective-permute-start(bf16[480,256]{1,0:T(8,128)(2,1)S(1)} %get-tuple-element.115), channel_id=1, source_target_pairs={{0,4},{4,8},{8,12},{1,5},{5,9},{9,13},{2,6},{6,10},{10,14},{3,7},{... | collective-permute-start | bytes 737288 | tf_op jit(solution)/shard_map/ppermute | solution.py:785
  19.9 12.7 %collective-permute-start.4 = (bf16[480,256]{1,0:T(8,128)(2,1)S(1)}, bf16[480,256]{1,0:T(8,128)(2,1)S(1)}, u32[]{:S(2)}, u32[]{:S(2)}) collective-permute-start(bf16[480,256]{1,0:T(8,128)(2,1)S(1)} %get-tuple-element.116), channel_id=1, source_target_pairs={{4,0},{8,4},{12,8},{5,1},{9,5},{13,9},{6,2},{10,6},{14,10},{7,3},{... | collective-permute-start | bytes 737288 | tf_op jit(solution)/shard_map/ppermute | solution.py:785
  24.6 19.2 %all-to-all-start = ((f32[32,1,2176]{2,1,0:T(1,128)}), f32[32,1,2176]{2,1,0:T(1,128)S(1)}, u32[]{:S(2)}, u32[]{:S(2)}) async-start(f32[32,1,2176]{2,1,0:T(1,128)} %shard_map.206), calls=%async_computation | async-start | bytes 557056 | tf_op jit(solution)/shard_map/all_to_all | solution.py:789
  43.7 16.9 %copy-start.6 = (f32[512]{0:T(512)S(1)}, f32[512]{0:T(512)}, u32[]{:S(2)}) copy-start(f32[512]{0:T(512)} %param.17) | copy-start | bytes 6148
  43.7 16.9 %copy-start.7 = (f32[512]{0:T(512)S(1)}, f32[512]{0:T(512)}, u32[]{:S(2)}) copy-start(f32[512]{0:T(512)} %param.20) | copy-start | bytes 6148
  43.7 16.9 %copy-start.12 = (f32[512]{0:T(512)S(1)}, f32[512]{0:T(512)}, u32[]{:S(2)}) copy-start(f32[512]{0:T(512)} %param.18) | copy-start | bytes 6148
  43.8 16.9 %copy-start.13 = (f32[512]{0:T(512)S(1)}, f32[512]{0:T(512)}, u32[]{:S(2)}) copy-start(f32[512]{0:T(512)} %param.21) | copy-start | bytes 6148
  50.1 10.6 %collective-permute-start.5 = (bf16[624,1536]{1,0:T(8,128)(2,1)}, bf16[624,1536]{1,0:T(8,128)(2,1)S(1)}, u32[]{:S(2)}, u32[]{:S(2)}) collective-permute-start(bf16[624,1536]{1,0:T(8,128)(2,1)} %get-tuple-element.125.refs_3_), channel_id=1, source_target_pairs={{0,16},{16,0},{1,17},{17,1},{2,18},{18,2},{3,19},{19,3},{4,20},{20... | collective-permute-start | bytes 5750792 | tf_op jit(solution)/shard_map/ppermute | solution.py:798
  50.1 10.5 %all-to-all-start.1 = ((f32[32,1,1024]{2,1,0:T(1,128)}), f32[32,1,1024]{2,1,0:T(1,128)S(1)}, u32[]{:S(2)}, u32[]{:S(2)}) async-start(f32[32,1,1024]{2,1,0:T(1,128)} %get-tuple-element.124), calls=%async_computation.1 | async-start | bytes 262144 | tf_op jit(solution)/shard_map/all_to_all | solution.py:789
  52.9 35.4 %copy-start.10 = (s32[5]{0:T(128)}, s32[5]{0:T(128)S(1)}, u32[]{:S(2)}) copy-start(s32[5]{0:T(128)S(1)} %stack.44.refs_0_) | copy-start | bytes 64
  66.2 4.0 %collective-permute-start.6 = (f32[3,384,256]{2,1,0:T(8,128)}, f32[3,384,256]{2,1,0:T(8,128)S(1)}, u32[]{:S(2)}, u32[]{:S(2)}) collective-permute-start(f32[3,384,256]{2,1,0:T(8,128)} %get-tuple-element.131), channel_id=1, source_target_pairs={{0,16},{16,0},{1,17},{17,1},{2,18},{18,2},{3,19},{19,3},{4,20},{20... | collective-permute-start | bytes 3538952 | tf_op jit(solution)/shard_map/ppermute | solution.py:798
  66.3 4.5 %collective-permute-start.7 = (bf16[624,768]{1,0:T(8,128)(2,1)}, bf16[624,768]{1,0:T(8,128)(2,1)}, u32[]{:S(2)}, u32[]{:S(2)}) collective-permute-start(bf16[624,768]{1,0:T(8,128)(2,1)} %get-tuple-element.134.refs_5_.refs_3_), channel_id=1, source_target_pairs={{0,16},{16,0},{1,17},{17,1},{2,18},{18,2},{3,19},{19,3},{4,20},{20... | collective-permute-start | bytes 2875400 | tf_op jit(solution)/shard_map/ppermute | solution.py:798
  66.8 12.0 %all-to-all-start.2 = ((f32[32,1,1536]{2,1,0:T(1,128)}), f32[32,1,1536]{2,1,0:T(1,128)S(1)}, u32[]{:S(2)}, u32[]{:S(2)}) async-start(f32[32,1,1536]{2,1,0:T(1,128)} %get-tuple-element.135), calls=%async_computation.2 | async-start | bytes 393216 | tf_op jit(solution)/shard_map/all_to_all | solution.py:789
  70.2 8.6 %collective-permute-start.8 = (f32[624,128]{1,0:T(8,128)S(1)}, f32[624,128]{1,0:T(8,128)S(1)}, u32[]{:S(2)}, u32[]{:S(2)}) collective-permute-start(f32[624,128]{1,0:T(8,128)S(1)} %get-tuple-element.137.refs_5_.refs_10_.refs_12_.refs_14_), channel_id=1, source_target_pairs={{0,16},{16,0},{1,17},{17,1},{2,18},{18,2},{3,19},{19,3},{4,20},{20... | collective-permute-start | bytes 958472 | tf_op jit(solution)/shard_map/ppermute | solution.py:798
  87.2 15.6 %collective-permute-start.10 = (bf16[19,64,256]{2,1,0:T(8,128)(2,1)}, bf16[19,64,256]{2,1,0:T(8,128)(2,1)S(1)}, u32[]{:S(2)}, u32[]{:S(2)}) collective-permute-start(bf16[19,64,256]{2,1,0:T(8,128)(2,1)} %get-tuple-element.145), channel_id=1, source_target_pairs={{0,8},{4,12},{8,0},{12,4},{1,9},{5,13},{9,1},{13,5},{2,10},{6,14},... | collective-permute-start | bytes 1867784 | tf_op jit(solution)/shard_map/ppermute | solution.py:798
  88.2 15.2 %collective-permute-start.9 = (bf16[19,64,256]{2,1,0:T(8,128)(2,1)S(1)}, bf16[19,64,256]{2,1,0:T(8,128)(2,1)}, u32[]{:S(2)}, u32[]{:S(2)}) collective-permute-start(bf16[19,64,256]{2,1,0:T(8,128)(2,1)S(1)} %get-tuple-element.143), channel_id=1, source_target_pairs={{0,4},{4,0},{8,12},{12,8},{1,5},{5,1},{9,13},{13,9},{2,6},{6,2},{1... | collective-permute-start | bytes 1867784 | tf_op jit(solution)/shard_map/ppermute | solution.py:798
  88.3 21.1 %collective-permute-start.14 = (bf16[672,768]{1,0:T(8,128)(2,1)}, bf16[672,768]{1,0:T(8,128)(2,1)}, u32[]{:S(2)}, u32[]{:S(2)}) collective-permute-start(bf16[672,768]{1,0:T(8,128)(2,1)} %get-tuple-element.155.refs_5_), channel_id=1, source_target_pairs={{0,16},{16,0},{1,17},{17,1},{2,18},{18,2},{3,19},{19,3},{4,20},{20... | collective-permute-start | bytes 3096584 | tf_op jit(solution)/shard_map/ppermute | solution.py:798
  96.9 12.5 %collective-permute-start.13 = (f32[2,384,256]{2,1,0:T(8,128)}, f32[2,384,256]{2,1,0:T(8,128)}, u32[]{:S(2)}, u32[]{:S(2)}) collective-permute-start(f32[2,384,256]{2,1,0:T(8,128)} %get-tuple-element.154), channel_id=1, source_target_pairs={{0,16},{16,0},{1,17},{17,1},{2,18},{18,2},{3,19},{19,3},{4,20},{20... | collective-permute-start | bytes 2359304 | tf_op jit(solution)/shard_map/ppermute | solution.py:798
  97.5 12.0 %all-to-all-start.3 = ((f32[32,1,1024]{2,1,0:T(1,128)}), f32[32,1,1024]{2,1,0:T(1,128)S(1)}, u32[]{:S(2)}, u32[]{:S(2)}) async-start(f32[32,1,1024]{2,1,0:T(1,128)} %get-tuple-element.156), calls=%async_computation.3 | async-start | bytes 262144 | tf_op jit(solution)/shard_map/all_to_all | solution.py:789
  107.5 8.8 %collective-permute-start.11 = (bf16[19,32,256]{2,1,0:T(8,128)(2,1)}, bf16[19,32,256]{2,1,0:T(8,128)(2,1)S(1)}, u32[]{:S(2)}, u32[]{:S(2)}) collective-permute-start(bf16[19,32,256]{2,1,0:T(8,128)(2,1)} %get-tuple-element.151), channel_id=1, source_target_pairs={{0,8},{4,12},{8,0},{12,4},{1,9},{5,13},{9,1},{13,5},{2,10},{6,14},... | collective-permute-start | bytes 933896 | tf_op jit(solution)/shard_map/ppermute | solution.py:798
  108.5 8.2 %collective-permute-start.12 = (bf16[19,32,256]{2,1,0:T(8,128)(2,1)}, bf16[19,32,256]{2,1,0:T(8,128)(2,1)}, u32[]{:S(2)}, u32[]{:S(2)}) collective-permute-start(bf16[19,32,256]{2,1,0:T(8,128)(2,1)} %get-tuple-element.152), channel_id=1, source_target_pairs={{0,4},{4,0},{8,12},{12,8},{1,5},{5,1},{9,13},{13,9},{2,6},{6,2},{1... | collective-permute-start | bytes 933896 | tf_op jit(solution)/shard_map/ppermute | solution.py:798
  118.4 10.4 %collective-permute-start.15 = (bf16[38,16,256]{2,1,0:T(8,128)(2,1)S(1)}, bf16[38,16,256]{2,1,0:T(8,128)(2,1)S(1)}, u32[]{:S(2)}, u32[]{:S(2)}) collective-permute-start(bf16[38,16,256]{2,1,0:T(8,128)(2,1)S(1)} %select_convert_fusion), channel_id=1, source_target_pairs={{0,1},{1,0},{2,3},{3,2},{4,5},{5,4},{6,7},{7,6},{8,9},{9,8},{10,11... | collective-permute-start | bytes 933896 | tf_op jit(solution)/shard_map/ppermute | solution.py:798
  120.0 8.4 %collective-permute-start.16 = (bf16[9,64,256]{2,1,0:T(8,128)(2,1)S(1)}, bf16[9,64,256]{2,1,0:T(8,128)(2,1)S(1)}, u32[]{:S(2)}, u32[]{:S(2)}) collective-permute-start(bf16[9,64,256]{2,1,0:T(8,128)(2,1)S(1)} %get-tuple-element.164), channel_id=1, source_target_pairs={{0,4},{4,0},{8,12},{12,8},{1,5},{5,1},{9,13},{13,9},{2,6},{6,2},{1... | collective-permute-start | bytes 884744 | tf_op jit(solution)/shard_map/ppermute | solution.py:798
  121.4 7.4 %collective-permute-start.17 = (bf16[9,64,256]{2,1,0:T(8,128)(2,1)S(1)}, bf16[9,64,256]{2,1,0:T(8,128)(2,1)S(1)}, u32[]{:S(2)}, u32[]{:S(2)}) collective-permute-start(bf16[9,64,256]{2,1,0:T(8,128)(2,1)S(1)} %get-tuple-element.165), channel_id=1, source_target_pairs={{0,8},{4,12},{8,0},{12,4},{1,9},{5,13},{9,1},{13,5},{2,10},{6,14},... | collective-permute-start | bytes 884744 | tf_op jit(solution)/shard_map/ppermute | solution.py:798
  128.9 5.2 %collective-permute-start.20 = (bf16[9,32,256]{2,1,0:T(8,128)(2,1)S(1)}, bf16[9,32,256]{2,1,0:T(8,128)(2,1)S(1)}, u32[]{:S(2)}, u32[]{:S(2)}) collective-permute-start(bf16[9,32,256]{2,1,0:T(8,128)(2,1)S(1)} %select_convert_fusion.3), channel_id=1, source_target_pairs={{0,4},{4,0},{8,12},{12,8},{1,5},{5,1},{9,13},{13,9},{2,6},{6,2},{1... | collective-permute-start | bytes 442376 | tf_op jit(solution)/shard_map/ppermute | solution.py:798
  130.4 7.4 %collective-permute-start.18 = (bf16[38,8,256]{2,1,0:T(8,128)(2,1)S(1)}, bf16[38,8,256]{2,1,0:T(8,128)(2,1)S(1)}, u32[]{:S(2)}, u32[]{:S(2)}) collective-permute-start(bf16[38,8,256]{2,1,0:T(8,128)(2,1)S(1)} %select_convert_fusion.1), channel_id=1, source_target_pairs={{0,2},{1,3},{2,0},{3,1},{4,6},{5,7},{6,4},{7,5},{8,10},{9,11},{10,... | collective-permute-start | bytes 466952 | tf_op jit(solution)/shard_map/ppermute | solution.py:798
  132.3 5.2 %collective-permute-start.19 = (bf16[9,32,256]{2,1,0:T(8,128)(2,1)S(1)}, bf16[9,32,256]{2,1,0:T(8,128)(2,1)S(1)}, u32[]{:S(2)}, u32[]{:S(2)}) collective-permute-start(bf16[9,32,256]{2,1,0:T(8,128)(2,1)S(1)} %select_convert_fusion.4), channel_id=1, source_target_pairs={{0,8},{4,12},{8,0},{12,4},{1,9},{5,13},{9,1},{13,5},{2,10},{6,14},... | collective-permute-start | bytes 442376 | tf_op jit(solution)/shard_map/ppermute | solution.py:798
  138.0 10.6 %collective-permute-start.21 = (bf16[38,8,256]{2,1,0:T(8,128)(2,1)S(1)}, bf16[38,8,256]{2,1,0:T(8,128)(2,1)S(1)}, u32[]{:S(2)}, u32[]{:S(2)}) collective-permute-start(bf16[38,8,256]{2,1,0:T(8,128)(2,1)S(1)} %add_convert_fusion), channel_id=1, source_target_pairs={{0,2},{1,3},{2,0},{3,1},{4,6},{5,7},{6,4},{7,5},{8,10},{9,11},{10,... | collective-permute-start | bytes 466952 | tf_op jit(solution)/shard_map/ppermute | solution.py:798
  139.1 9.6 %collective-permute-start.22 = (bf16[18,16,256]{2,1,0:T(8,128)(2,1)S(1)}, bf16[18,16,256]{2,1,0:T(8,128)(2,1)S(1)}, u32[]{:S(2)}, u32[]{:S(2)}) collective-permute-start(bf16[18,16,256]{2,1,0:T(8,128)(2,1)S(1)} %select_convert_fusion.2), channel_id=1, source_target_pairs={{0,1},{1,0},{2,3},{3,2},{4,5},{5,4},{6,7},{7,6},{8,9},{9,8},{10,11... | collective-permute-start | bytes 442376 | tf_op jit(solution)/shard_map/ppermute | solution.py:798
  148.7 8.5 %collective-permute-start.23 = (bf16[38,16,256]{2,1,0:T(8,128)(2,1)S(1)}, bf16[38,16,256]{2,1,0:T(8,128)(2,1)S(1)}, u32[]{:S(2)}, u32[]{:S(2)}) collective-permute-start(bf16[38,16,256]{2,1,0:T(8,128)(2,1)S(1)} %pad_maximum_fusion.5), channel_id=1, source_target_pairs={{0,1},{1,0},{2,3},{3,2},{4,5},{5,4},{6,7},{7,6},{8,9},{9,8},{10,11... | collective-permute-start | bytes 933896 | tf_op jit(solution)/shard_map/ppermute | solution.py:798
  150.1 5.9 %collective-permute-start.24 = (bf16[18,8,256]{2,1,0:T(8,128)(2,1)S(1)}, bf16[18,8,256]{2,1,0:T(8,128)(2,1)S(1)}, u32[]{:S(2)}, u32[]{:S(2)}) collective-permute-start(bf16[18,8,256]{2,1,0:T(8,128)(2,1)S(1)} %select_convert_fusion.5), channel_id=1, source_target_pairs={{0,2},{1,3},{2,0},{3,1},{4,6},{5,7},{6,4},{7,5},{8,10},{9,11},{10,... | collective-permute-start | bytes 221192 | tf_op jit(solution)/shard_map/ppermute | solution.py:798
  157.5 10.3 %collective-permute-start.25 = (bf16[19,32,256]{2,1,0:T(8,128)(2,1)S(1)}, bf16[19,32,256]{2,1,0:T(8,128)(2,1)S(1)}, u32[]{:S(2)}, u32[]{:S(2)}) collective-permute-start(bf16[19,32,256]{2,1,0:T(8,128)(2,1)S(1)} %get-tuple-element.212), channel_id=1, source_target_pairs={{0,8},{4,12},{8,0},{12,4},{1,9},{5,13},{9,1},{13,5},{2,10},{6,14},... | collective-permute-start | bytes 933896 | tf_op jit(solution)/shard_map/ppermute | solution.py:798
  158.5 10.1 %collective-permute-start.26 = (bf16[19,32,256]{2,1,0:T(8,128)(2,1)S(1)}, bf16[19,32,256]{2,1,0:T(8,128)(2,1)S(1)}, u32[]{:S(2)}, u32[]{:S(2)}) collective-permute-start(bf16[19,32,256]{2,1,0:T(8,128)(2,1)S(1)} %get-tuple-element.211), channel_id=1, source_target_pairs={{0,4},{4,0},{8,12},{12,8},{1,5},{5,1},{9,13},{13,9},{2,6},{6,2},{1... | collective-permute-start | bytes 933896 | tf_op jit(solution)/shard_map/ppermute | solution.py:798
  160.1 5.3 %collective-permute-start.27 = (bf16[18,8,256]{2,1,0:T(8,128)(2,1)S(1)}, bf16[18,8,256]{2,1,0:T(8,128)(2,1)S(1)}, u32[]{:S(2)}, u32[]{:S(2)}) collective-permute-start(bf16[18,8,256]{2,1,0:T(8,128)(2,1)S(1)} %add_convert_fusion.1), channel_id=1, source_target_pairs={{0,2},{1,3},{2,0},{3,1},{4,6},{5,7},{6,4},{7,5},{8,10},{9,11},{10,... | collective-permute-start | bytes 221192 | tf_op jit(solution)/shard_map/ppermute | solution.py:798
  168.7 15.4 %collective-permute-start.32 = (bf16[19,64,256]{2,1,0:T(8,128)(2,1)S(1)}, bf16[19,64,256]{2,1,0:T(8,128)(2,1)S(1)}, u32[]{:S(2)}, u32[]{:S(2)}) collective-permute-start(bf16[19,64,256]{2,1,0:T(8,128)(2,1)S(1)} %pad_maximum_fusion.3), channel_id=1, source_target_pairs={{0,8},{4,12},{8,0},{12,4},{1,9},{5,13},{9,1},{13,5},{2,10},{6,14},... | collective-permute-start | bytes 1867784 | tf_op jit(solution)/shard_map/ppermute | solution.py:798
  169.3 6.1 %collective-permute-start.28 = (bf16[18,16,256]{2,1,0:T(8,128)(2,1)S(1)}, bf16[18,16,256]{2,1,0:T(8,128)(2,1)S(1)}, u32[]{:S(2)}, u32[]{:S(2)}) collective-permute-start(bf16[18,16,256]{2,1,0:T(8,128)(2,1)S(1)} %pad_maximum_fusion.10), channel_id=1, source_target_pairs={{0,1},{1,0},{2,3},{3,2},{4,5},{5,4},{6,7},{7,6},{8,9},{9,8},{10,11... | collective-permute-start | bytes 442376 | tf_op jit(solution)/shard_map/ppermute | solution.py:798
  172.3 11.9 %collective-permute-start.31 = (bf16[19,64,256]{2,1,0:T(8,128)(2,1)S(1)}, bf16[19,64,256]{2,1,0:T(8,128)(2,1)S(1)}, u32[]{:S(2)}, u32[]{:S(2)}) collective-permute-start(bf16[19,64,256]{2,1,0:T(8,128)(2,1)S(1)} %pad_maximum_fusion.2), channel_id=1, source_target_pairs={{0,4},{4,0},{8,12},{12,8},{1,5},{5,1},{9,13},{13,9},{2,6},{6,2},{1... | collective-permute-start | bytes 1867784 | tf_op jit(solution)/shard_map/ppermute | solution.py:798
  175.5 5.2 %collective-permute-start.29 = (bf16[9,32,256]{2,1,0:T(8,128)(2,1)S(1)}, bf16[9,32,256]{2,1,0:T(8,128)(2,1)S(1)}, u32[]{:S(2)}, u32[]{:S(2)}) collective-permute-start(bf16[9,32,256]{2,1,0:T(8,128)(2,1)S(1)} %get-tuple-element.222), channel_id=1, source_target_pairs={{0,8},{4,12},{8,0},{12,4},{1,9},{5,13},{9,1},{13,5},{2,10},{6,14},... | collective-permute-start | bytes 442376 | tf_op jit(solution)/shard_map/ppermute | solution.py:798
  176.3 7.9 %collective-permute-start.30 = (bf16[9,32,256]{2,1,0:T(8,128)(2,1)S(1)}, bf16[9,32,256]{2,1,0:T(8,128)(2,1)S(1)}, u32[]{:S(2)}, u32[]{:S(2)}) collective-permute-start(bf16[9,32,256]{2,1,0:T(8,128)(2,1)S(1)} %get-tuple-element.221), channel_id=1, source_target_pairs={{0,4},{4,0},{8,12},{12,8},{1,5},{5,1},{9,13},{13,9},{2,6},{6,2},{1... | collective-permute-start | bytes 442376 | tf_op jit(solution)/shard_map/ppermute | solution.py:798
  185.3 5.8 %collective-permute-start.35 = (bf16[19,256,256]{2,1,0:T(8,128)(2,1)S(1)}, bf16[19,256,256]{2,1,0:T(8,128)(2,1)}, u32[]{:S(2)}, u32[]{:S(2)}) collective-permute-start(bf16[19,256,256]{2,1,0:T(8,128)(2,1)S(1)} %pad_maximum_fusion.half_ref), channel_id=1, source_target_pairs={{0,16},{16,0},{1,17},{17,1},{2,18},{18,2},{3,19},{19,3},{4,20},{20... | collective-permute-start | bytes 7471112 | tf_op jit(solution)/shard_map/ppermute | solution.py:798
  185.4 9.5 %collective-permute-start.34 = (bf16[9,64,256]{2,1,0:T(8,128)(2,1)S(1)}, bf16[9,64,256]{2,1,0:T(8,128)(2,1)S(1)}, u32[]{:S(2)}, u32[]{:S(2)}) collective-permute-start(bf16[9,64,256]{2,1,0:T(8,128)(2,1)S(1)} %pad_maximum_fusion.8.refs_2_), channel_id=1, source_target_pairs={{0,8},{4,12},{8,0},{12,4},{1,9},{5,13},{9,1},{13,5},{2,10},{6,14},... | collective-permute-start | bytes 884744 | tf_op jit(solution)/shard_map/ppermute | solution.py:798
  186.1 9.6 %collective-permute-start.33 = (bf16[9,64,256]{2,1,0:T(8,128)(2,1)S(1)}, bf16[9,64,256]{2,1,0:T(8,128)(2,1)}, u32[]{:S(2)}, u32[]{:S(2)}) collective-permute-start(bf16[9,64,256]{2,1,0:T(8,128)(2,1)S(1)} %pad_maximum_fusion.7.refs_0_), channel_id=1, source_target_pairs={{0,4},{4,0},{8,12},{12,8},{1,5},{5,1},{9,13},{13,9},{2,6},{6,2},{1... | collective-permute-start | bytes 884744 | tf_op jit(solution)/shard_map/ppermute | solution.py:798
  197.2 2.9 %collective-permute-start.36 = (bf16[9,256,256]{2,1,0:T(8,128)(2,1)S(1)}, bf16[9,256,256]{2,1,0:T(8,128)(2,1)S(1)}, u32[]{:S(2)}, u32[]{:S(2)}) collective-permute-start(bf16[9,256,256]{2,1,0:T(8,128)(2,1)S(1)} %shard_map.216.half_ref), channel_id=1, source_target_pairs={{0,16},{16,0},{1,17},{17,1},{2,18},{18,2},{3,19},{19,3},{4,20},{20... | collective-permute-start | bytes 3538952 | tf_op jit(solution)/shard_map/ppermute | solution.py:798
  (14 other events, 94.2 us)
